TPU v7x, 32 devices: a whole 2x2x4 slice. The times are simulated.
32 devices in a mesh: section: 4 (over y, x), dp: 8 (over z, core).
Axes of the slice: x: 2, y: 2, z: 4, core: 2. Of those that a mesh axis runs over, the one named last changes fastest.
Arguments:
- images: bfloat16 [4, 8, 8, 24, 512], P(None, 'dp')
- image_group: int32 [4, 8], P(None, 'dp'), may hold values from 0 to 2, as said below
- group_size: int32 [3, 2], replicated, may hold values from 4 to 24, as said below
- conv_weight: bfloat16 [4, 512, 3, 3, 512], P('section'), may hold values from -0.09375 to 0.09375
- bn_gain: float32 [4, 512], P('section'), may hold values from 0.1 to 1.9
- bn_bias: float32 [4, 512], P('section'), may hold values from -3 to 3
- cotangent: bfloat16 [4, 8, 8, 24, 512], P(None, 'dp'), may hold values from -6 to 6
Outputs:
- activations: bfloat16 [4, 8, 8, 24, 512], P('section', 'dp')
- input_grad: bfloat16 [4, 8, 8, 24, 512], P('section', 'dp')
- weight_grad: float32 [4, 512, 3, 3, 512], P('section', 'dp')
- gain_grad: float32 [4, 512], P('section', 'dp')
- bias_grad: float32 [4, 512], P('section', 'dp')
Inputs may be any that keep to these rules, and one draw needn't show every extreme that they name: `image_group`: in every micro-batch some image is of group 0. `group_size`: row g holds the height and the width of group g; group 0 fills the canvas, 8 by 24; heights are at least 4 and widths at least 12.
All inputs are finite; a program needn't handle non-finite values.
Results may differ from a plain program's by a relative error of at most 0.04.
Values may be sent and summed in bfloat16 or wider, within the bound.
No kernel may reach another device: no remote copies, remote signals or barrier semaphores. Data moves between devices by JAX's collectives and lax.ppermute only.
A program may use at most 256 MiB of HBM per device.

v0:
```python
import math
from functools import partial

import jax
import jax.numpy as jnp
import numpy as np
from jax import lax
from jax.experimental import pallas as pl
from jax.experimental.pallas import tpu as pltpu
from jax.sharding import PartitionSpec as P

CONVS = 2


eps = 1e-05


def from_behind(x, axis, by):
    peers = lax.axis_size(axis)
    pairs = [(i, i + by) for i in range(peers) if 0 <= i + by < peers]
    return lax.ppermute(x, axis, pairs)


def canvas_mask(image_group, group_size, canvas_rows, canvas_cols):
    groups_n = group_size.shape[0]
    onehot = image_group[..., None] == jnp.arange(groups_n, dtype=jnp.int32)
    height = jnp.sum(jnp.where(onehot, group_size[:, 0], 0), axis=-1)
    breadth = jnp.sum(jnp.where(onehot, group_size[:, 1], 0), axis=-1)
    inside_rows = jnp.arange(canvas_rows, dtype=jnp.int32)[:, None] < height[..., None, None]
    inside_cols = jnp.arange(canvas_cols, dtype=jnp.int32)[None, :] < breadth[..., None, None]
    return (inside_rows & inside_cols).astype(jnp.float32)[..., None]


def window_pool(hidden):
    frames, height, breadth, channels = hidden.shape
    blocks = hidden.reshape(frames, height // 2, 2, breadth // 2, 2, channels)
    window_max = jnp.max(blocks, axis=(2, 4), keepdims=True)
    raised = jnp.exp(blocks - window_max)
    weights = raised / jnp.sum(raised, axis=(2, 4), keepdims=True)
    pooled = jnp.sum(weights * blocks, axis=(2, 4), keepdims=True)
    return (weights * pooled).reshape(frames, height, breadth, channels)


def activate(pre_act, inside, pooling):
    hidden = jax.nn.silu(pre_act) * inside
    return jnp.where(pooling, window_pool(hidden) * inside, hidden)


def conv_forward(layer_in, weight):
    return lax.conv_general_dilated(
        layer_in,
        weight,
        (1, 1),
        "SAME",
        dimension_numbers=("NHWC", "IHWO", "NHWC"),
        preferred_element_type=jnp.float32,
    )


def conv_data_back(grad_pre, weight):
    flipped = weight[:, ::-1, ::-1, :]
    return lax.conv_general_dilated(
        grad_pre,
        flipped,
        (1, 1),
        "SAME",
        dimension_numbers=("NHWC", "OHWI", "NHWC"),
        preferred_element_type=jnp.float32,
    )


def weight_back(layer_in, grad_pre):
    height = layer_in.shape[1]
    breadth = layer_in.shape[2]
    padded = jnp.pad(layer_in, ((0, 0), (1, 1), (1, 1), (0, 0)))
    pieces = []
    for tap_row in range(3):
        for tap_col in range(3):
            window = padded[:, tap_row : tap_row + height, tap_col : tap_col + breadth, :]
            pieces.append(
                jnp.einsum("nhwi,nhwo->io", window, grad_pre, preferred_element_type=jnp.float32)
            )
    return jnp.stack(pieces, axis=1).reshape(layer_in.shape[3], 3, 3, grad_pre.shape[3])


def layer_forward(layer_in, weight, gain_row, bias_row, inside, pooling):
    pre_norm = conv_forward(layer_in, weight)
    sums = lax.psum(
        (
            jnp.sum(pre_norm * inside, axis=(0, 1, 2)),
            jnp.sum(pre_norm * pre_norm * inside, axis=(0, 1, 2)),
            jnp.sum(inside),
        ),
        "dp",
    )
    pixel_total = sums[2]
    mean_val = sums[0] / pixel_total
    scale_inv = lax.rsqrt(sums[1] / pixel_total - mean_val * mean_val + eps)
    pre_act = (pre_norm - mean_val) * scale_inv * gain_row + bias_row
    hidden = activate(pre_act, inside, pooling)
    return (pre_norm, mean_val, scale_inv, pixel_total, hidden)


def layer_backward(
    grad_out,
    layer_in,
    pre_norm,
    mean_val,
    scale_inv,
    pixel_total,
    weight,
    gain_row,
    bias_row,
    inside,
    pooling,
):
    normed = (pre_norm - mean_val) * scale_inv
    pre_act = normed * gain_row + bias_row
    hidden_out, pullback = jax.vjp(partial(activate, inside=inside, pooling=pooling), pre_act)
    grad_act = pullback(grad_out)[0]
    sums = lax.psum(
        (jnp.sum(grad_act, axis=(0, 1, 2)), jnp.sum(grad_act * normed, axis=(0, 1, 2))), "dp"
    )
    shift_term = sums[0] / pixel_total
    slope_term = sums[1] / pixel_total
    grad_pre = (
        inside * scale_inv * gain_row * (grad_act - shift_term - normed * slope_term)
    ).astype(jnp.bfloat16)
    weight_term = weight_back(layer_in, grad_pre)
    grad_in = conv_data_back(grad_pre, weight).astype(jnp.bfloat16)
    return (grad_in, weight_term, sums[1], sums[0])


def pipeline_shards(images, image_group, group_size, conv_weight, bn_gain, bn_bias, cotangent):
    section_index = lax.axis_index("section")
    sections = lax.axis_size("section")
    micro_total = images.shape[0]
    channels = conv_weight.shape[1]
    inside_all = canvas_mask(image_group, group_size, images.shape[2], images.shape[3])
    ticks = micro_total + sections - 1
    weight = conv_weight[0]
    gain_row = bn_gain[0]
    bias_row = bn_bias[0]
    pool_here = section_index == CONVS - 1
    received = jnp.zeros(images.shape[1:], jnp.bfloat16)
    kept_in, kept_pre, kept_mean, kept_scale, kept_total, finished = ([], [], [], [], [], [])
    for tick in range(ticks):
        micro_pos = jnp.clip(tick - section_index, 0, micro_total - 1)
        inside = inside_all[micro_pos]
        fresh = (images[micro_pos].astype(jnp.float32) * inside).astype(jnp.bfloat16)
        layer_in = jnp.where(section_index == 0, fresh, received)
        pre_norm, mean_val, scale_inv, pixel_total, hidden = layer_forward(
            layer_in, weight, gain_row, bias_row, inside, pool_here
        )
        sent = hidden.astype(jnp.bfloat16)
        if tick < ticks - 1:
            received = from_behind(sent, "section", 1)
        kept_in.append(layer_in)
        kept_pre.append(pre_norm)
        kept_mean.append(mean_val)
        kept_scale.append(scale_inv)
        kept_total.append(pixel_total)
        finished.append(sent)
    stack_in = jnp.stack(kept_in)
    stack_pre = jnp.stack(kept_pre)
    stack_mean = jnp.stack(kept_mean)
    stack_scale = jnp.stack(kept_scale)
    stack_total = jnp.stack(kept_total)
    returned = jnp.zeros(images.shape[1:], jnp.bfloat16)
    weight_sum = jnp.zeros(conv_weight.shape[1:], jnp.float32)
    gain_sum = jnp.zeros((channels,), jnp.float32)
    bias_sum = jnp.zeros((channels,), jnp.float32)
    input_list = []
    for tick in range(ticks):
        micro_raw = tick - (sections - 1 - section_index)
        valid = ((micro_raw >= 0) & (micro_raw < micro_total)).astype(jnp.float32)
        micro_pos = jnp.clip(micro_raw, 0, micro_total - 1)
        forward_tick = jnp.clip(micro_pos + section_index, 0, ticks - 1)
        inside = inside_all[micro_pos]
        grad_out = jnp.where(
            section_index == sections - 1,
            cotangent[micro_pos].astype(jnp.float32),
            returned.astype(jnp.float32),
        )
        grad_in, weight_term, gain_term, bias_term = layer_backward(
            grad_out,
            stack_in[forward_tick],
            stack_pre[forward_tick],
            stack_mean[forward_tick],
            stack_scale[forward_tick],
            stack_total[forward_tick],
            weight,
            gain_row,
            bias_row,
            inside,
            pool_here,
        )
        weight_sum = weight_sum + valid * weight_term
        gain_sum = gain_sum + valid * gain_term
        bias_sum = bias_sum + valid * bias_term
        if tick < ticks - 1:
            returned = from_behind(grad_in, "section", -1)
        input_list.append((grad_in.astype(jnp.float32) * inside).astype(jnp.bfloat16))
    out_stack = jnp.stack(finished[sections - 1 :], axis=0)
    grad_stack = jnp.stack(input_list[sections - 1 :], axis=0)
    out_back, grad_back = (
        lax.all_to_all(out_stack, "section", split_axis=0, concat_axis=1, tiled=True),
        lax.all_to_all(grad_stack, "section", split_axis=0, concat_axis=1, tiled=True),
    )
    activations = out_back[:, sections - 1 : sections]
    input_grad = grad_back[:, 0:1]
    weight_grad = lax.psum_scatter(weight_sum[None], "dp", scatter_dimension=1, tiled=True)
    share = channels // lax.axis_size("dp")
    gain_grad = lax.dynamic_slice_in_dim(gain_sum, lax.axis_index("dp") * share, share)[None]
    bias_grad = lax.dynamic_slice_in_dim(bias_sum, lax.axis_index("dp") * share, share)[None]
    return (activations, input_grad, weight_grad, gain_grad, bias_grad)


AXES = ("section", "dp")
TAPS = 9
VMEM_LIMIT = 24 * 1024 * 1024
META_ROWS = 16
LANES = 128
ROW_AT, COL_AT, FRAME_AT = 6, 7, 8
NT = (((1,), (1,)), ((), ()))


def place():
    dp_index = lax.axis_index("dp")
    return lax.axis_index("section"), dp_index // 2, dp_index % 2


def peer_order():
    return [(k, j) for j in range(2) for k in range(4)]


def slice_at(section, core, k, j):
    return (core ^ j) * lax.axis_size("section") + (section ^ k)


def send(x, target):
    sections = lax.axis_size("section")
    dps = lax.axis_size("dp")
    pairs = []
    for s in range(sections):
        for d in range(dps):
            ts, tz, tc = target(s, d // 2, d % 2)
            pairs.append((s * dps + d, ts * dps + tz * 2 + tc))
    return lax.ppermute(x, AXES, pairs)


def to_section(x, k):
    return send(x, lambda s, z, c: (s ^ k, z, c))


def to_plane(x, k):
    return send(x, lambda s, z, c: (s, z ^ k, c))


def to_core(x):
    return send(x, lambda s, z, c: (s, z, c ^ 1))


def spread(blocks, move, *beside):
    moved = lax.optimization_barrier(([move(blocks[k], k) for k in (1, 2, 3)], beside))[0]
    return [blocks[0]] + moved


def with_core(blocks):
    return blocks + [to_core(x) for x in blocks]


def after(x, *first):
    return lax.optimization_barrier((x, first))[0]


def grid_facts(frames, rows, cols):
    at = np.arange(frames * rows * cols)
    col = at % cols
    row = (at // cols) % rows
    facts = [row > 0, row < rows - 1, col > 0, col < cols - 1, col % 2 == 0, row % 2 == 0, row, col]
    facts = facts + [at // (rows * cols) == frame for frame in range(frames)]
    return jnp.asarray(np.stack(facts).astype(np.float32))


def shift(x, by):
    length = x.shape[1]
    return pltpu.roll(x, (-by) % length, 1) if by % length else x


def row_ok(facts, d):
    return facts[0:1, :] if d < 0 else facts[1:2, :]


def col_ok(facts, d):
    return facts[2:3, :] if d < 0 else facts[3:4, :]


def sum_taps(taps_ref, facts, cols):
    ch = taps_ref.shape[0] // TAPS
    total = None
    for dx in (-1, 0, 1):
        column = None
        for dy in (-1, 0, 1):
            tap = (dy + 1) * 3 + dx + 1
            piece = taps_ref[tap * ch : (tap + 1) * ch, :]
            if dy:
                piece = shift(piece, dy * cols) * row_ok(facts, dy)
            column = piece if column is None else column + piece
        if dx:
            column = shift(column, dx) * col_ok(facts, dx)
        total = column if total is None else total + column
    return total


def spread_taps(grad, moved_ref, base, facts, cols):
    ch = grad.shape[0]
    for dx in (-1, 0, 1):
        column = shift(grad, -dx) * col_ok(facts, -dx) if dx else grad
        for dy in (-1, 0, 1):
            piece = shift(column, -dy * cols) * row_ok(facts, -dy) if dy else column
            at = base + ((dy + 1) * 3 + dx + 1) * ch
            moved_ref[at : at + ch, :] = piece.astype(jnp.bfloat16)


def corner_sum(x, cols):
    x = x + shift(x, 1)
    return x + shift(x, cols)


def from_corner(x, facts, cols):
    x = jnp.where(facts[4:5, :] > 0.5, x, shift(x, -1))
    return jnp.where(facts[5:6, :] > 0.5, x, shift(x, -cols))


def lane_sum(x):
    return jnp.sum(x, axis=1, keepdims=True)


def normalise(pre, inside):
    count = lane_sum(inside)
    mean = lane_sum(pre * inside) / count
    square = lane_sum(pre * pre * inside) / count
    scale = lax.rsqrt(square - mean * mean + eps)
    return (pre - mean) * scale, scale


def hidden_of(normed, gain, bias, inside, facts, cols, pooling):
    pre_act = normed * gain + bias
    hidden = pre_act * jax.nn.sigmoid(pre_act) * inside
    if pooling:
        raised = jnp.exp(hidden)
        total = corner_sum(raised, cols)
        pooled = corner_sum(raised * hidden, cols) / total
        hidden = raised * from_corner(pooled / total, facts, cols) * inside
    return hidden


def norm_back(grad, normed, scale, gain, bias, inside, facts, cols, pooling):
    pre_act = normed * gain + bias
    gate = jax.nn.sigmoid(pre_act)
    if pooling:
        hidden = pre_act * gate * inside
        raised = jnp.exp(hidden)
        out = grad * inside
        total = 1.0 / corner_sum(raised, cols)
        pooled = corner_sum(raised * hidden, cols) * total
        d_pooled = corner_sum(raised * out, cols) * total
        by_out = from_corner(pooled * total, facts, cols)
        by_hidden = from_corner(d_pooled * total, facts, cols)
        rest = from_corner(d_pooled * total * (1.0 - 2.0 * pooled), facts, cols)
        grad = raised * (out * by_out + hidden * by_hidden + rest)
    grad_act = grad * inside * gate * (1.0 + pre_act * (1.0 - gate))
    count = lane_sum(inside)
    shift_sum = lane_sum(grad_act)
    slope_sum = lane_sum(grad_act * normed)
    grad_pre = inside * (scale * gain) * (grad_act - shift_sum / count - normed * (slope_sum / count))
    return grad_pre.astype(jnp.bfloat16), shift_sum, slope_sum


def assemble(blocks, full_ref):
    section, _, core = place()
    ch = blocks[0].shape[0]
    for (k, j), block in zip(peer_order(), blocks):
        at = pl.multiple_of(slice_at(section, core, k, j) * ch, ch)
        full_ref[pl.ds(at, ch), :] = block[...]


def assemble_frames(blocks, full_ref, rows, lanes):
    _, plane, core = place()
    size = rows.stop - rows.start
    for (k, j), block in zip(peer_order(), blocks):
        frame = (plane ^ k) * 2 + (core ^ j)
        full_ref[pl.ds(pl.multiple_of(frame * size, size), size), :] = block[rows, lanes]


def start_all(copies):
    for copy in copies:
        copy.start()
    return copies


def wait_all(copies):
    for copy in copies:
        copy.wait()


def tap_products(weight, full_ref, taps_ref, by_cells):
    length = taps_ref.shape[1]
    step = 512 if length % 512 == 0 else length
    for at in range(0, length, step):
        if by_cells:
            taps_ref[:, at : at + step] = lax.dot_general(
                weight, full_ref[at : at + step, :], NT, preferred_element_type=jnp.float32
            )
        else:
            taps_ref[:, at : at + step] = jnp.dot(
                weight, full_ref[:, at : at + step], preferred_element_type=jnp.float32
            )


def pick_layer(layer, sources, start, target, sem):
    section, _, _ = place()
    rows = pl.ds(start, target.shape[0])
    for k, source in enumerate(sources):

        @pl.when((section ^ layer) == k)
        def _():
            pltpu.make_async_copy(source.at[rows], target, sem).start()

    return pltpu.make_async_copy(sources[0].at[rows], target, sem)


def affine(meta, ch):
    parts = meta[:, :LANES].astype(jnp.float32).T[:ch]
    return (
        parts[:, 0:1] + parts[:, 1:2] + parts[:, 2:3],
        parts[:, 3:4] + parts[:, 4:5] + parts[:, 5:6],
    )


def plane_inside(metas, facts):
    frames = metas.shape[0] // META_ROWS
    extents = []
    for line in (0, 1):
        total = None
        for f in range(frames):
            at = f * META_ROWS + line
            extent = metas[at : at + 1, 0:1].astype(jnp.float32) * facts[FRAME_AT + f : FRAME_AT + f + 1, :]
            total = extent if total is None else total + extent
        extents.append(total)
    on = (facts[ROW_AT : ROW_AT + 1, :] < extents[0]) & (facts[COL_AT : COL_AT + 1, :] < extents[1])
    return jnp.where(on, 1.0, 0.0)


def frames_kernel(dims, group_table, size_table, images, cots, *refs):
    payloads, (image_in, cot_in, groups, sizes, sems) = refs[:4], refs[4:]
    copies = start_all(
        [
            pltpu.make_async_copy(group_table, groups, sems.at[0]),
            pltpu.make_async_copy(size_table, sizes, sems.at[1]),
            pltpu.make_async_copy(images, image_in, sems.at[2]),
            pltpu.make_async_copy(cots, cot_in, sems.at[3]),
        ]
    )
    section, plane, _ = place()
    rows, cols = dims
    cells = rows * cols
    at = lax.broadcasted_iota(jnp.int32, (cells, LANES), 0).astype(jnp.float32)
    row = jnp.floor((at + 0.5) * (1.0 / cols))
    col = at - row * cols
    channels = images.shape[2]
    half = channels // 2
    wait_all(copies)
    for k in range(4):
        micro = plane ^ k
        group = groups[0, micro]
        height = sizes[0, 0]
        breadth = sizes[1, 0]
        for g in range(1, sizes.shape[1]):
            height = jnp.where(group == g, sizes[0, g], height)
            breadth = jnp.where(group == g, sizes[1, g], breadth)
        height = height.astype(jnp.float32)
        breadth = breadth.astype(jnp.float32)
        on = jnp.where((row < height) & (col < breadth), 1.0, 0.0)
        image = image_in[micro]
        for c in range(0, channels, LANES):
            piece = image[:, c : c + LANES].astype(jnp.float32) * on
            payloads[k][:cells, c : c + LANES] = piece.astype(jnp.bfloat16)
        line = lax.broadcasted_iota(jnp.int32, (META_ROWS, channels + LANES), 0)
        payloads[k][cells:, :] = jnp.where(line == 0, height, breadth).astype(jnp.bfloat16)
        tile = section // 2 * LANES
        low = cot_in[micro, :, pl.ds(pl.multiple_of(tile, LANES), LANES)].astype(jnp.float32)
        high = cot_in[micro, :, pl.ds(pl.multiple_of(half + tile, LANES), LANES)].astype(jnp.float32)
        odd = section % 2 == 1
        low = jnp.where(odd, pltpu.roll(low, LANES // 2, 1), low)
        high = jnp.where(odd, high, pltpu.roll(high, LANES // 2, 1))
        lane = lax.broadcasted_iota(jnp.int32, (cells, LANES), 1)
        both = jnp.where(lane < LANES // 2, low, high).astype(jnp.bfloat16)
        payloads[k][:cells, channels:] = both


def pack_kernel(gain, bias, weight, *refs):
    outs, (own, columns, turned, tables, sems) = refs[:4], refs[4:]
    section, _, core = place()
    width = columns.shape[2]
    ch = width // 4
    start = pl.multiple_of(core * width, width)
    copies = start_all(
        [
            pltpu.make_async_copy(weight.at[tap, :, pl.ds(start, width)], columns.at[tap], sems.at[tap])
            for tap in range(TAPS)
        ]
    )
    table_copies = start_all(
        [
            pltpu.make_async_copy(gain, tables.at[0], sems.at[TAPS]),
            pltpu.make_async_copy(bias, tables.at[1], sems.at[TAPS + 1]),
        ]
    )
    wait_all(table_copies)
    targets = [own, *outs[1:]]
    for k, out in enumerate(targets):
        lines = []
        tile = pl.multiple_of(start + (section ^ k) // 2 * LANES, LANES)
        odd = (section ^ k) % 2 == 1
        for m in range(2):
            line = tables[m, :, pl.ds(tile, LANES)]
            line = jnp.where(odd, pltpu.roll(line, ch, 1), line)
            for _ in range(3):
                part = line.astype(jnp.bfloat16).astype(jnp.float32)
                lines.append(part)
                line = line - part
        lines.append(jnp.zeros((META_ROWS - len(lines), LANES), jnp.float32))
        out[TAPS * ch :, :] = jnp.zeros((META_ROWS, out.shape[1]), jnp.bfloat16)
        out[TAPS * ch :, :LANES] = jnp.concatenate(lines, axis=0).astype(jnp.bfloat16)
    for tap in range(TAPS):
        copies[tap].wait()
        turned[...] = columns[tap].T
        for k, out in enumerate(targets):
            rows = pl.ds(pl.multiple_of((section ^ k) * ch, ch), ch)
            out[tap * ch : (tap + 1) * ch, :] = turned[rows, :]
    own_copy = pltpu.make_async_copy(own, outs[0], sems.at[TAPS])
    own_copy.start()
    own_copy.wait()


def pick_kernel(layer, *refs):
    sources, (out, sem) = refs[:4], refs[4:]
    pick_layer(layer, sources, 0, out, sem.at[0]).wait()


def forward_kernel(dims, layer, first, pooling, *refs):
    blocks, weights, rest = refs[:8], refs[8 : 12 if first else 9], refs[12 if first else 9 :]
    rows, cols = dims
    cells = rows * cols
    if first:
        facts, pick, hidden, kept, full_out, inside_out, cot_out, full, taps, stage, weight, metas, *rest = rest
        cot_full, cot, sems = rest
        copy = pick_layer(layer, weights, 0, weight, sems.at[2])
    else:
        inside, facts, hidden, kept, full_out, full, taps, stage, sems = rest
        (weight,) = weights
    facts_now = facts[...]
    if first:
        channels = full.shape[1]
        assemble_frames(blocks, full, slice(0, cells), slice(0, channels))
    else:
        assemble(blocks, full)
    full_copy = pltpu.make_async_copy(full, full_out, sems.at[0])
    full_copy.start()
    if first:
        assemble_frames(blocks, metas, slice(cells, cells + META_ROWS), slice(0, channels))
        assemble_frames(blocks, cot_full, slice(0, cells), slice(channels, channels + LANES))
        inside_now = plane_inside(metas, facts_now)
        inside_out[...] = inside_now
        copy.wait()
    else:
        inside_now = inside[...]
    ch = hidden.shape[0]
    tap_products(weight[: TAPS * ch, :], full, taps, first)
    if first:
        cot[...] = lax.dot_general(
            pick[...], cot_full[...], NT, preferred_element_type=jnp.float32
        ).astype(jnp.bfloat16)
        cot_copy = pltpu.make_async_copy(cot, cot_out, sems.at[3])
        cot_copy.start()
    pre = sum_taps(taps, facts_now, cols)
    normed, scale = normalise(pre, inside_now)
    length = normed.shape[1]
    stage[:, :length] = normed
    stage[:, length:] = jnp.broadcast_to(scale, (ch, LANES))
    kept_copy = pltpu.make_async_copy(stage, kept, sems.at[1])
    kept_copy.start()
    gain, bias = affine(weight[TAPS * ch :, :], ch)
    hidden[...] = hidden_of(normed, gain, bias, inside_now, facts_now, cols, pooling).astype(jnp.bfloat16)
    if first:
        cot_copy.wait()
    full_copy.wait()
    kept_copy.wait()


def turn_kernel(dims, layer, pooling, *refs):
    blocks, (weight, cot_in, inside, facts) = refs[:8], refs[8:12]
    hidden_out, full_out, grad_pre, sums, full, taps, cot, hidden, sems = refs[12:]
    cols = dims[1]
    cot_copy = pltpu.make_async_copy(cot_in, cot, sems.at[0])
    cot_copy.start()
    assemble(blocks, full)
    full_copy = pltpu.make_async_copy(full, full_out, sems.at[1])
    full_copy.start()
    ch = grad_pre.shape[0]
    tap_products(weight[: TAPS * ch, :], full, taps, False)
    facts_now, inside_now = facts[...], inside[...]
    pre = sum_taps(taps, facts_now, cols)
    normed, scale = normalise(pre, inside_now)
    gain, bias = affine(weight[TAPS * ch :, :], ch)
    hidden[...] = hidden_of(normed, gain, bias, inside_now, facts_now, cols, pooling).astype(jnp.bfloat16)
    hidden_copy = pltpu.make_async_copy(hidden, hidden_out, sems.at[2])
    hidden_copy.start()
    cot_copy.wait()
    grad_pre[...], shift_sum, slope_sum = norm_back(
        cot[...].astype(jnp.float32), normed, scale, gain, bias, inside_now, facts_now, cols, pooling
    )
    keep_sums(sums, shift_sum, slope_sum)
    full_copy.wait()
    hidden_copy.wait()


def keep_sums(sums, shift_sum, slope_sum):
    ch = shift_sum.shape[0]
    sums[:, :LANES] = jnp.broadcast_to(shift_sum, (ch, LANES))
    sums[:, LANES:] = jnp.broadcast_to(slope_sum, (ch, LANES))


def add_blocks(blocks):
    total = blocks[0][...].astype(jnp.float32)
    for block in blocks[1:]:
        total = total + block[...].astype(jnp.float32)
    return total


def fetch_kernel(layer, kept, *refs):
    sources, (kept_out, meta_out, sems) = refs[:4], refs[4:]
    copy = pltpu.make_async_copy(kept, kept_out, sems.at[0])
    copy.start()
    start = sources[0].shape[0] - META_ROWS
    pick_layer(layer, sources, start, meta_out, sems.at[1]).wait()
    copy.wait()


def norm_back_kernel(dims, pooling, *refs):
    blocks, (kept, meta, inside, facts, grad_pre, sums) = refs[:4], refs[4:]
    ch, length = grad_pre.shape
    grad = add_blocks(blocks).astype(jnp.bfloat16).astype(jnp.float32)
    gain, bias = affine(meta[...], ch)
    grad_pre[...], shift_sum, slope_sum = norm_back(
        grad,
        kept[:, :length],
        kept[:, length : length + 1],
        gain,
        bias,
        inside[...],
        facts[...],
        dims[1],
        pooling,
    )
    keep_sums(sums, shift_sum, slope_sum)


def conv_back_kernel(dims, layer, own, other, own_weights, other_weights, facts, *refs):
    outs, (moved, weights, sems) = refs[:4], refs[4:]
    ch = own.shape[0]
    rows = pl.ds(layer * 4 * ch, 4 * ch)
    copies = start_all(
        [
            pltpu.make_async_copy(own_weights.at[rows], weights.at[0], sems.at[0]),
            pltpu.make_async_copy(other_weights.at[rows], weights.at[1], sems.at[1]),
        ]
    )
    facts_now = facts[...]
    spread_taps(own[...].astype(jnp.float32), moved.at[0], 0, facts_now, dims[1])
    spread_taps(other[...].astype(jnp.float32), moved.at[1], 0, facts_now, dims[1])
    wait_all(copies)
    value = jnp.dot(weights[0], moved[0], preferred_element_type=jnp.float32)
    value = value + jnp.dot(weights[1], moved[1], preferred_element_type=jnp.float32)
    for k, out in enumerate(outs):
        out[...] = value[k * ch : (k + 1) * ch, :].astype(jnp.bfloat16)


def turn_weights_kernel(layers, *refs):
    sources, outs, (full, turned, stage, sems) = refs[:4], refs[4:6], refs[6:]
    section, _, core = place()
    rows, channels = full.shape[1:]
    half = channels // 2
    ch = half // 4
    copies = [pick_layer(n, sources, 0, full.at[n], sems.at[n]) for n in range(layers)]
    for n in range(layers):
        copies[n].wait()
        turned[...] = full[n].T
        for j in range(2):
            for k in range(4):
                at = pl.multiple_of((core ^ j) * half + (section ^ k) * ch, ch)
                stage[j, n * half + k * ch : n * half + (k + 1) * ch, :] = turned[pl.ds(at, ch), :]
    wait_all(
        start_all([pltpu.make_async_copy(stage.at[j], outs[j], sems.at[j]) for j in range(2)])
    )


def weight_kernel(dims, first, full_in, grad_pre, sums, facts, *refs):
    outs, (full, moved, sems) = refs[:-3], refs[-3:]
    copy = pltpu.make_async_copy(full_in, full, sems.at[0])
    copy.start()
    cols = dims[1]
    ch = grad_pre.shape[0]
    spread_taps(grad_pre[...].astype(jnp.float32), moved, 0, facts[...], cols)
    copy.wait()
    if first:
        value = jnp.dot(moved[...], full[...], preferred_element_type=jnp.float32)
    else:
        value = lax.dot_general(moved[...], full[...], NT, preferred_element_type=jnp.float32)
    width = outs[0].shape[1]
    lines = []
    for at in (0, LANES):
        turned = sums[:, at : at + LANES].T
        lines.append(jnp.concatenate([turned, jnp.zeros((LANES, width - ch), jnp.float32)], axis=1)[0:1])
    sums_block = jnp.concatenate(lines + [jnp.zeros((META_ROWS - 2, width), jnp.float32)], axis=0)
    if len(outs) == 1:
        size = outs[0].shape[0] // 4
        targets = [outs[0].at[pl.ds(n * size, size)] for n in range(4)]
        for n, target in enumerate(targets):
            target[: TAPS * ch, :] = value[:, n * width : (n + 1) * width].astype(jnp.bfloat16)
            target[TAPS * ch :, :] = sums_block.astype(jnp.bfloat16)
    else:
        _, plane, _ = place()
        for n in range(4):
            piece = value[:, n * width : (n + 1) * width].astype(jnp.bfloat16)
            for k, target in enumerate(outs):

                @pl.when((plane ^ k) == n)
                def _():
                    target[: TAPS * ch, :] = piece

        for target in outs:
            target[TAPS * ch :, :] = sums_block.astype(jnp.bfloat16)


def input_kernel(*refs):
    blocks, (hidden, inside), pieces, (full, sems) = refs[:4], refs[4:6], refs[6:10], refs[10:]
    section, _, _ = place()
    ch = hidden.shape[0]
    copy = pltpu.make_async_copy(hidden, full.at[pl.ds(0, ch)], sems.at[0])
    copy.start()
    full[ch:, :] = (add_blocks(blocks) * inside[...]).astype(jnp.bfloat16)
    copy.wait()
    width = pieces[0].shape[1]
    for k, piece in enumerate(pieces):
        piece[...] = full[:, pl.ds(pl.multiple_of((section ^ k) * width, width), width)]


def maps_out_kernel(*refs):
    blocks, outs, (full,) = refs[:8], refs[8:10], refs[10:]
    _, plane, core = place()
    ch = blocks[0].shape[0] // 2
    cells = outs[0].shape[0]
    for n, out in enumerate(outs):
        for (k, j), block in zip(peer_order(), blocks):
            at = pl.multiple_of(slice_at(plane, core, k, j) * ch, ch)
            full[pl.ds(at, ch), :] = block[n * ch : (n + 1) * ch, :]
        both = full[...].astype(jnp.float32)
        mine = jnp.where(core == 0, both[:, :cells], both[:, cells:])
        out[...] = mine.T.astype(out.dtype)


def grads_out_kernel(*refs):
    blocks, (weight_out, shift_out, slope_out), (full, turned) = refs[:8], refs[8:11], refs[11:]
    section, plane, core = place()
    taps, rows, channels = weight_out.shape
    for tap in range(taps):
        for (k, j), block in zip(peer_order(), blocks):
            at = pl.multiple_of(slice_at(section, core, k, j) * rows, rows)
            full[pl.ds(at, rows), :] = block[tap * rows : (tap + 1) * rows, :].astype(jnp.float32)
        turned[...] = full[...].T
        weight_out[tap] = turned[pl.ds(pl.multiple_of(core * rows, rows), rows), :]
    shift_row = jnp.zeros((1, rows), jnp.float32)
    slope_row = jnp.zeros((1, rows), jnp.float32)
    slot = plane * 2 + core
    for (k, j), block in zip(peer_order(), blocks):
        tail = block[taps * rows :, :].astype(jnp.float32)
        mine = slice_at(section, core, k, j) == slot
        shift_row = shift_row + jnp.where(mine, tail[0:1, :rows], 0.0)
        slope_row = slope_row + jnp.where(mine, tail[1:2, :rows], 0.0)
    shift_out[...] = shift_row
    slope_out[...] = slope_row


def call(kernel, outs, scratch, args, name, held=(), held_outs=(), loose=(), last=False, flops=0, copies=None):
    shapes = [
        (jax.ShapeDtypeStruct if last else pltpu.HBM if n in held_outs else pltpu.VMEM)(shape, dtype)
        for n, (shape, dtype) in enumerate(outs)
    ]
    moved = sum(a.size * a.dtype.itemsize for a in args)
    moved += sum(math.prod(shape) * jnp.dtype(dtype).itemsize for shape, dtype in outs)
    spaces = [pltpu.HBM if n in held else pltpu.VMEM for n in range(len(args))]
    out_spaces = [pltpu.HBM if n in held_outs else pltpu.VMEM for n in range(len(outs))]
    args = [
        a if n in loose else pltpu.with_memory_space_constraint(a, space)
        for n, (a, space) in enumerate(zip(args, spaces))
    ]
    scratch_shapes = [
        pltpu.SMEM(shape, dtype) if dtype == jnp.int32 else pltpu.VMEM(shape, dtype) for shape, dtype in scratch
    ]
    if copies is not None:
        scratch_shapes.append(pltpu.SemaphoreType.DMA((copies,)))
    return pl.pallas_call(
        kernel,
        out_shape=shapes,
        in_specs=[pl.BlockSpec(memory_space=space) for space in spaces],
        out_specs=[pl.BlockSpec(memory_space=space) for space in out_spaces],
        scratch_shapes=scratch_shapes,
        compiler_params=pltpu.CompilerParams(vmem_limit_bytes=VMEM_LIMIT),
        cost_estimate=pl.CostEstimate(flops=flops, bytes_accessed=moved, transcendentals=0),
        name=name,
    )(*args)


def plane_shards(images, image_group, group_size, conv_weight, bn_gain, bn_bias, cotangent):
    section, _, core = place()
    micro_total, _, rows, cols, channels = images.shape
    layers = lax.axis_size("section")
    last = layers - 1
    cells = rows * cols
    frames = 2 * micro_total
    length = frames * cells
    ch = channels // 8
    dims = (rows, cols)
    bf16, f32 = jnp.bfloat16, jnp.float32
    facts = grid_facts(frames, rows, cols)
    conv_flops = 2 * TAPS * ch * channels * length
    slice_rows = TAPS * ch + META_ROWS

    full_map = ((channels, length), bf16)
    full_frames = ((length, channels), bf16)
    tap_scratch = ((TAPS * ch, length), f32)
    weight_slice = ((slice_rows, channels), bf16)
    map_out = ((ch, length), bf16)
    sums_out = ((ch, 2 * LANES), f32)
    kept_out = ((ch, length + LANES), f32)

    taps_first = conv_weight[0].transpose(1, 2, 0, 3).reshape(TAPS, channels, channels)
    packed = call(
        pack_kernel,
        [weight_slice] * 4,
        [
            weight_slice,
            ((TAPS, channels, 4 * ch), bf16),
            ((4 * ch, channels), bf16),
            ((2, 1, channels), f32),
        ],
        [bn_gain, bn_bias, taps_first],
        "weight_pack",
        held=range(3),
        held_outs=(0,),
        copies=TAPS + 2,
    )
    slices = spread(packed, to_section)

    payload = ((cells + META_ROWS, channels + LANES), bf16)
    sent = call(
        partial(frames_kernel, dims),
        [payload] * 4,
        [((micro_total, cells, channels), bf16)] * 2
        + [(image_group.shape[::-1], jnp.int32), (group_size.shape[::-1], jnp.int32)],
        [
            image_group.T,
            group_size.T,
            after(images.reshape(micro_total, cells, channels), packed),
            cotangent.reshape(micro_total, cells, channels),
        ],
        "frames",
        held=range(4),
        copies=4,
    )
    frames_in = with_core(spread(sent, to_plane))

    half = (core * ch + np.arange(ch))[:, None] == np.arange(2 * ch)[None, :]
    hidden, normed, full, inside, cot = call(
        partial(forward_kernel, dims, 0, True, CONVS == 1),
        [map_out, kept_out, full_frames, ((1, length), f32), map_out],
        [
            full_frames,
            tap_scratch,
            kept_out,
            weight_slice,
            ((frames * META_ROWS, channels), bf16),
            ((length, LANES), bf16),
            map_out,
        ],
        [*frames_in, *slices, facts, half.astype(bf16)],
        "forward",
        held=range(8, 12),
        held_outs=(1, 2, 4),
        loose=(12, 13),
        flops=conv_flops,
        copies=4,
    )
    kept, fulls = [normed], [full]
    for layer in range(1, layers):
        (weight,) = call(
            partial(pick_kernel, layer),
            [weight_slice],
            [],
            after(slices, hidden),
            "pick",
            held=range(4),
            copies=1,
        )
        beside = [weight]
        if layer == 1:
            turned = call(
                partial(turn_weights_kernel, layers),
                [((layers * 4 * ch, TAPS * ch), bf16)] * 2,
                [
                    ((layers, TAPS * ch, channels), bf16),
                    ((channels, TAPS * ch), bf16),
                    ((2, layers * 4 * ch, TAPS * ch), bf16),
                ],
                after(slices, hidden),
                "turn_weights",
                held=range(4),
                held_outs=(0, 1),
                copies=layers,
            )
            beside.append(turned)
        if layer == 2:
            turned = [turned[0], to_core(after(turned[1], hidden))]
        blocks = with_core(spread([hidden] * 4, to_section, beside))
        if layer < last:
            hidden, normed, full = call(
                partial(forward_kernel, dims, layer, False, layer == CONVS - 1),
                [map_out, kept_out, full_map],
                [full_map, tap_scratch, kept_out],
                [*blocks, weight, inside, facts],
                "forward",
                held_outs=(1, 2),
                loose=(9, 10),
                flops=conv_flops,
                copies=2,
            )
            kept.append(normed)
        else:
            activation, full, grad_pre, sums = call(
                partial(turn_kernel, dims, last, last == CONVS - 1),
                [map_out, full_map, map_out, sums_out],
                [full_map, tap_scratch, map_out, map_out],
                [*blocks, weight, cot, inside, facts],
                "turn",
                held=(9,),
                held_outs=(0, 1),
                loose=(10, 11),
                flops=conv_flops,
                copies=3,
            )
        fulls.append(full)

    shares = [None] * layers
    same_core = [[2 * z + c for z in range(layers)] for c in range(2)]
    for layer in range(last, -1, -1):
        first = layer == 0
        pieces = call(
            partial(weight_kernel, dims, first),
            [((slice_rows, 2 * ch), bf16)] * 4 if first else [((4 * slice_rows, 2 * ch), bf16)],
            [full_frames if first else full_map, ((TAPS * ch, length), bf16)],
            [fulls[layer], grad_pre, sums, facts],
            "weight_share",
            held=(0,),
            loose=(2, 3),
            flops=conv_flops,
            copies=1,
        )
        if first:
            moved = spread(pieces, to_plane)
            shares[layer] = sum(x.astype(f32) for x in moved).astype(bf16)
        else:
            shares[layer] = lax.psum_scatter(
                pieces[0], "dp", scatter_dimension=0, tiled=True, axis_index_groups=same_core
            )
        own, other = after((grad_pre, to_core(grad_pre)), pieces)
        parts = call(
            partial(conv_back_kernel, dims, layer),
            [map_out] * 4,
            [((2, TAPS * ch, length), bf16), ((2, 4 * ch, TAPS * ch), bf16)],
            [own, other, *turned, facts],
            "conv_back",
            held=(2, 3),
            loose=(4,),
            flops=conv_flops,
            copies=2,
        )
        if layer:
            held = call(
                partial(fetch_kernel, layer - 1),
                [kept_out, ((META_ROWS, channels), bf16)],
                [],
                [after(kept[layer - 1], parts), *slices],
                "fetch",
                held=range(5),
                copies=2,
            )
            blocks = spread(parts, to_section, held)
            grad_pre, sums = call(
                partial(norm_back_kernel, dims, layer - 1 == CONVS - 1),
                [map_out, sums_out],
                [],
                [*blocks, *held, inside, facts],
                "norm_back",
                loose=(6, 7),
            )
    blocks = spread(parts, to_section)
    maps = call(
        input_kernel,
        [((2 * ch, 2 * cells), bf16)] * 4,
        [((2 * ch, length), bf16)],
        [*blocks, activation, inside],
        "input",
        held=(4,),
        loose=(5,),
        copies=1,
    )
    maps = lax.optimization_barrier(
        [send(x, lambda s, z, c, k=k: (z, s ^ k, c)) for k, x in enumerate(maps)]
    )
    activations, input_grad = call(
        maps_out_kernel,
        [((cells, channels), bf16)] * 2,
        [((channels, 2 * cells), bf16)],
        with_core(maps),
        "maps_out",
        last=True,
    )

    chosen = [lax.select_n(section ^ k, *shares) for k in range(4)]
    weight_grad, bias_grad, gain_grad = call(
        grads_out_kernel,
        [((TAPS, ch, channels), f32), ((1, ch), f32), ((1, ch), f32)],
        [((channels, 2 * ch), f32), ((2 * ch, channels), f32)],
        with_core(spread(chosen, to_section)),
        "grads_out",
        last=True,
    )
    weight_grad = weight_grad.reshape(3, 3, ch, channels).transpose(2, 0, 1, 3)[None]
    return (
        activations.reshape(1, 1, rows, cols, channels),
        input_grad.reshape(1, 1, rows, cols, channels),
        weight_grad,
        gain_grad,
        bias_grad,
    )


def fits_plane_plan(images, conv_weight, sections, dps):
    micro_total, images_total, rows, cols, channels = images.shape
    return (
        sections == 4
        and dps == 2 * sections
        and micro_total == sections
        and conv_weight.shape[0] == sections
        and images_total == dps
        and rows % 2 == 0
        and cols % 2 == 0
        and (rows * cols) % 64 == 0
        and channels == 512
    )


def solution(mesh):
    in_specs = (
        P(None, "dp", None, None, None),
        P(None, "dp"),
        P(),
        P("section", None, None, None, None),
        P("section", None),
        P("section", None),
        P(None, "dp", None, None, None),
    )
    out_specs = (
        P("section", "dp", None, None, None),
        P("section", "dp", None, None, None),
        P("section", "dp", None, None, None),
        P("section", "dp"),
        P("section", "dp"),
    )
    sections, dps = mesh.shape["section"], mesh.shape["dp"]

    def program(images, image_group, group_size, conv_weight, bn_gain, bn_bias, cotangent):
        plan = plane_shards if fits_plane_plan(images, conv_weight, sections, dps) else pipeline_shards
        sharded = jax.shard_map(plan, mesh=mesh, in_specs=in_specs, out_specs=out_specs, check_vma=False)
        return sharded(images, image_group, group_size, conv_weight, bn_gain, bn_bias, cotangent)

    return program
```

profile of v0, /device:TPU:0, one launch (start us, length us, event | category | flops | bytes accessed | tf_op | source)
XLA Modules:
  0.0 233.2 jit_solution(10628468011481590740)
XLA Ops:
  7.2 3.7 %weight_pack.1 = (bf16[592,512]{1,0:T(8,128)(2,1)}, bf16[592,512]{1,0:T(8,128)(2,1)S(1)}, bf16[592,512]{1,0:T(8,128)(2,1)S(1)}, bf16[592,512]{1,0:T(8,128)(2,1)S(1)}) custom-call(f32[1,512]{1,0:T(1,128)} %gain.1, f32[1,512]{1,0:T(1,128)} %bias.1, bf16[9,512,512]{2,1,0:T(8,128)(2,1)} %bitcast.16), custom_call_target="tpu_custom_call" | custom-call | bytes 7147520 | tf_op jit(solution)/shard_map/weight_pack/pallas_call | solution.py:815
  10.9 3.0 %collective-permute-start.7 = (bf16[592,512]{1,0:T(8,128)(2,1)S(1)}, bf16[592,512]{1,0:T(8,128)(2,1)}, u32[]{:S(2)}, u32[]{:S(2)}) collective-permute-start(bf16[592,512]{1,0:T(8,128)(2,1)S(1)} %get-tuple-element.134), channel_id=1, source_target_pairs={{0,8},{1,9},{2,10},{3,11},{4,12},{5,13},{6,14},{7,15},{8,0},{9,1},... | collective-permute-start | bytes 1818632 | tf_op jit(solution)/shard_map/ppermute | solution.py:249
  14.0 1.5 collective-permute-start.8
  15.5 1.8 frames.1
  17.3 1.6 collective-permute-start
  19.4 2.6 %collective-permute-start.1 = (bf16[208,640]{1,0:T(8,128)(2,1)S(1)}, bf16[208,640]{1,0:T(8,128)(2,1)S(1)}, u32[]{:S(2)}, u32[]{:S(2)}) collective-permute-start(bf16[208,640]{1,0:T(8,128)(2,1)S(1)} %get-tuple-element.140), channel_id=1, source_target_pairs={{0,4},{1,5},{2,6},{3,7},{4,0},{5,1},{6,2},{7,3},{8,12},{9,13},{10,... | collective-permute-start | bytes 798728 | tf_op jit(solution)/shard_map/ppermute | solution.py:249
  22.0 8.4 %collective-permute-done.refs_1_ = bf16[208,640]{1,0:T(8,128)(2,1)S(1)} collective-permute-done((bf16[208,640]{1,0:T(8,128)(2,1)S(1)}, bf16[208,640]{1,0:T(8,128)(2,1)S(1)}, u32[]{:S(2)}, u32[]{:S(2)}) %collective-permute-start) | collective-permute-done | bytes 266272 | tf_op jit(solution)/shard_map/ppermute | solution.py:249
  30.4 2.5 %collective-permute-start.2 = (bf16[208,640]{1,0:T(8,128)(2,1)S(1)}, bf16[208,640]{1,0:T(8,128)(2,1)S(1)}, u32[]{:S(2)}, u32[]{:S(2)}) collective-permute-start(bf16[208,640]{1,0:T(8,128)(2,1)S(1)} %get-tuple-element.141), channel_id=1, source_target_pairs={{0,6},{1,7},{2,4},{3,5},{4,2},{5,3},{6,0},{7,1},{8,14},{9,15},{10,... | collective-permute-start | bytes 798728 | tf_op jit(solution)/shard_map/ppermute | solution.py:249
  32.9 6.2 %collective-permute-done.1.refs_2_ = bf16[208,640]{1,0:T(8,128)(2,1)S(1)} collective-permute-done((bf16[208,640]{1,0:T(8,128)(2,1)S(1)}, bf16[208,640]{1,0:T(8,128)(2,1)S(1)}, u32[]{:S(2)}, u32[]{:S(2)}) %collective-permute-start.1) | collective-permute-done | bytes 266272 | tf_op jit(solution)/shard_map/ppermute | solution.py:249
  39.6 2.6 %collective-permute-done.8.refs_10_.refs_2_ = bf16[592,512]{1,0:T(8,128)(2,1)} collective-permute-done((bf16[592,512]{1,0:T(8,128)(2,1)S(1)}, bf16[592,512]{1,0:T(8,128)(2,1)}, u32[]{:S(2)}, u32[]{:S(2)}) %collective-permute-start.8) | collective-permute-done | bytes 606240 | tf_op jit(solution)/shard_map/ppermute | solution.py:249
  42.4 1.4 collective-permute-done.6.refs_7_
  43.8 3.8 %forward.3 = (bf16[64,1536]{1,0:T(8,128)(2,1)S(1)}, f32[64,1664]{1,0:T(8,128)}, bf16[1536,512]{1,0:T(8,128)(2,1)}, f32[1,1536]{1,0:T(1,128)S(1)}, bf16[64,1536]{1,0:T(8,128)(2,1)}) custom-call(bf16[208,640]{1,0:T(8,128)(2,1)S(1)} %get-tuple-element.138.refs_0_, bf16[208,640]{1,0:T(8,128)(2,1)S(1)} %collective-permute-done.refs_1_, ...), custom_call_target="tpu_custom_call" | custom-call | flops 905969664 | bytes 7067648 | tf_op jit(solution)/shard_map/forward/pallas_call | solution.py:815
  47.6 2.2 collective-permute-start.12
  49.8 1.3 collective-permute-start.10
  52.2 3.7 %turn_weights.1 = (bf16[1024,576]{1,0:T(8,128)(2,1)}, bf16[1024,576]{1,0:T(8,128)(2,1)}) custom-call(bf16[592,512]{1,0:T(8,128)(2,1)} %get-tuple-element.168.refs_8_.refs_0_, bf16[592,512]{1,0:T(8,128)(2,1)} %collective-permute-done.7.refs_9_.refs_1_, bf16[592,512]{1,0:T(8,128)(2,1)} %collective-permute-done.8.refs_10_.refs_2_, ...), custom_call_target="tpu_custom_call" | custom-call | bytes 4784128 | tf_op jit(solution)/shard_map/turn_weights/pallas_call | solution.py:815
  56.3 3.4 %collective-permute-done.11.refs_2_ = bf16[64,1536]{1,0:T(8,128)(2,1)S(1)} collective-permute-done((bf16[64,1536]{1,0:T(8,128)(2,1)S(1)}, bf16[64,1536]{1,0:T(8,128)(2,1)S(1)}, u32[]{:S(2)}, u32[]{:S(2)}) %collective-permute-start.11) | collective-permute-done | bytes 196640 | tf_op jit(solution)/shard_map/ppermute | solution.py:249
  61.8 3.1 %forward.4 = (bf16[64,1536]{1,0:T(8,128)(2,1)S(1)}, f32[64,1664]{1,0:T(8,128)}, bf16[512,1536]{1,0:T(8,128)(2,1)}) custom-call(bf16[64,1536]{1,0:T(8,128)(2,1)S(1)} %get-tuple-element.148.refs_0_, bf16[64,1536]{1,0:T(8,128)(2,1)S(1)} %collective-permute-done.10.refs_1_, bf16[64,1536]{1,0:T(8,128)(2,1)S(1)} %collective-permute-done.11.refs_2_, ...), custom_call_target="tpu_custom_call" | custom-call | flops 905969664 | bytes 4478976 | tf_op jit(solution)/shard_map/forward/pallas_call | solution.py:815
  64.9 1.7 collective-permute-start.19
  69.5 4.1 %collective-permute-done.19.refs_3_ = bf16[64,1536]{1,0:T(8,128)(2,1)S(1)} collective-permute-done((bf16[64,1536]{1,0:T(8,128)(2,1)S(1)}, bf16[64,1536]{1,0:T(8,128)(2,1)S(1)}, u32[]{:S(2)}, u32[]{:S(2)}) %collective-permute-start.19) | collective-permute-done | bytes 196640 | tf_op jit(solution)/shard_map/ppermute | solution.py:249
  73.6 3.5 %collective-permute-done.18.refs_2_ = bf16[64,1536]{1,0:T(8,128)(2,1)S(1)} collective-permute-done((bf16[64,1536]{1,0:T(8,128)(2,1)S(1)}, bf16[64,1536]{1,0:T(8,128)(2,1)S(1)}, u32[]{:S(2)}, u32[]{:S(2)}) %collective-permute-start.18) | collective-permute-done | bytes 196640 | tf_op jit(solution)/shard_map/ppermute | solution.py:249
  79.1 2.4 %forward.5 = (bf16[64,1536]{1,0:T(8,128)(2,1)S(1)}, f32[64,1664]{1,0:T(8,128)}, bf16[512,1536]{1,0:T(8,128)(2,1)}) custom-call(bf16[64,1536]{1,0:T(8,128)(2,1)S(1)} %get-tuple-element.159.refs_0_, bf16[64,1536]{1,0:T(8,128)(2,1)S(1)} %collective-permute-done.17.refs_1_, bf16[64,1536]{1,0:T(8,128)(2,1)S(1)} %collective-permute-done.18.refs_2_, ...), custom_call_target="tpu_custom_call" | custom-call | flops 905969664 | bytes 4478976 | tf_op jit(solution)/shard_map/forward/pallas_call | solution.py:815
  81.5 1.7 collective-permute-start.26
  86.2 4.1 %collective-permute-done.26.refs_3_ = bf16[64,1536]{1,0:T(8,128)(2,1)S(1)} collective-permute-done((bf16[64,1536]{1,0:T(8,128)(2,1)S(1)}, bf16[64,1536]{1,0:T(8,128)(2,1)S(1)}, u32[]{:S(2)}, u32[]{:S(2)}) %collective-permute-start.26) | collective-permute-done | bytes 196640 | tf_op jit(solution)/shard_map/ppermute | solution.py:249
  90.3 3.5 %collective-permute-done.25.refs_2_ = bf16[64,1536]{1,0:T(8,128)(2,1)S(1)} collective-permute-done((bf16[64,1536]{1,0:T(8,128)(2,1)S(1)}, bf16[64,1536]{1,0:T(8,128)(2,1)S(1)}, u32[]{:S(2)}, u32[]{:S(2)}) %collective-permute-start.25) | collective-permute-done | bytes 196640 | tf_op jit(solution)/shard_map/ppermute | solution.py:249
  94.3 2.4 %copy.15 = bf16[1024,576]{0,1:T(8,128)(2,1)} copy(bf16[1024,576]{1,0:T(8,128)(2,1)} %get-tuple-element.181) | data formatting | bytes 2359296 | tf_op jit(solution)/shard_map/optimization_barrier | solution.py:274
  97.2 2.4 %turn.1 = (bf16[64,1536]{1,0:T(8,128)(2,1)}, bf16[512,1536]{1,0:T(8,128)(2,1)}, bf16[64,1536]{1,0:T(8,128)(2,1)S(1)}, f32[64,256]{1,0:T(8,128)S(1)}) custom-call(bf16[64,1536]{1,0:T(8,128)(2,1)S(1)} %get-tuple-element.167.refs_0_, bf16[64,1536]{1,0:T(8,128)(2,1)S(1)} %collective-permute-done.24.refs_1_, ...), custom_call_target="tpu_custom_call" | custom-call | flops 905969664 | bytes 4511744 | tf_op jit(solution)/shard_map/turn/pallas_call | solution.py:815
  99.6 3.4 %weight_share.4 = bf16[2368,128]{1,0:T(8,128)(2,1)} custom-call(bf16[512,1536]{1,0:T(8,128)(2,1)} %get-tuple-element.177.full_in, bf16[64,1536]{1,0:T(8,128)(2,1)S(1)} %get-tuple-element.179.grad_pre.own, f32[64,256]{1,0:T(8,128)S(1)} %get-tuple-element.178.sums, f32[16,1536]{1,0:T(8,128)S(1)} %copy-done), custom_call_target="tpu_custom_call" | custom-call | flops 905969664 | bytes 2539520 | tf_op jit(solution)/shard_map/weight_share/pallas_call | solution.py:815
  103.1 1.4 collective-permute-done.31.other
  104.6 2.4 %copy.16.other_weights = bf16[1024,576]{1,0:T(8,128)(2,1)} copy(bf16[1024,576]{0,1:T(8,128)(2,1)} %collective-permute-done.32) | data formatting | bytes 2359296 | tf_op jit(solution)/shard_map/ppermute | solution.py:249
  107.0 3.8 %conv_back.4 = (bf16[64,1536]{1,0:T(8,128)(2,1)S(1)}, bf16[64,1536]{1,0:T(8,128)(2,1)S(1)}, bf16[64,1536]{1,0:T(8,128)(2,1)S(1)}, bf16[64,1536]{1,0:T(8,128)(2,1)S(1)}) custom-call(bf16[64,1536]{1,0:T(8,128)(2,1)S(1)} %get-tuple-element.179.grad_pre.own, bf16[64,1536]{1,0:T(8,128)(2,1)S(1)} %collective-permute-done.31.other, ...), custom_call_target="tpu_custom_call" | custom-call | flops 905969664 | bytes 3637248 | tf_op jit(solution)/shard_map/conv_back/pallas_call | solution.py:815
  110.8 1.2 collective-permute-start.33
  113.1 1.3 collective-permute-start.35
  115.3 3.2 %collective-permute-done.33.refs_1_ = bf16[64,1536]{1,0:T(8,128)(2,1)S(1)} collective-permute-done((bf16[64,1536]{1,0:T(8,128)(2,1)S(1)}, bf16[64,1536]{1,0:T(8,128)(2,1)S(1)}, u32[]{:S(2)}, u32[]{:S(2)}) %collective-permute-start.33) | collective-permute-done | bytes 196640 | tf_op jit(solution)/shard_map/ppermute | solution.py:249
  118.6 4.3 %collective-permute-done.34.refs_2_ = bf16[64,1536]{1,0:T(8,128)(2,1)S(1)} collective-permute-done((bf16[64,1536]{1,0:T(8,128)(2,1)S(1)}, bf16[64,1536]{1,0:T(8,128)(2,1)S(1)}, u32[]{:S(2)}, u32[]{:S(2)}) %collective-permute-start.34) | collective-permute-done | bytes 196640 | tf_op jit(solution)/shard_map/ppermute | solution.py:249
  123.4 3.4 %weight_share.5 = bf16[2368,128]{1,0:T(8,128)(2,1)} custom-call(bf16[512,1536]{1,0:T(8,128)(2,1)} %get-tuple-element.194.full_in, bf16[64,1536]{1,0:T(8,128)(2,1)S(1)} %get-tuple-element.196.grad_pre.own, f32[64,256]{1,0:T(8,128)S(1)} %get-tuple-element.195.sums, f32[16,1536]{1,0:T(8,128)S(1)} %copy-done), custom_call_target="tpu_custom_call" | custom-call | flops 905969664 | bytes 2539520 | tf_op jit(solution)/shard_map/weight_share/pallas_call | solution.py:815
  127.1 1.4 collective-permute-done.36.other
  128.6 3.8 %conv_back.5 = (bf16[64,1536]{1,0:T(8,128)(2,1)S(1)}, bf16[64,1536]{1,0:T(8,128)(2,1)S(1)}, bf16[64,1536]{1,0:T(8,128)(2,1)S(1)}, bf16[64,1536]{1,0:T(8,128)(2,1)S(1)}) custom-call(bf16[64,1536]{1,0:T(8,128)(2,1)S(1)} %get-tuple-element.196.grad_pre.own, bf16[64,1536]{1,0:T(8,128)(2,1)S(1)} %collective-permute-done.36.other, ...), custom_call_target="tpu_custom_call" | custom-call | flops 905969664 | bytes 3637248 | tf_op jit(solution)/shard_map/conv_back/pallas_call | solution.py:815
  134.4 1.5 collective-permute-start.39
  137.0 3.2 %collective-permute-done.37.refs_1_ = bf16[64,1536]{1,0:T(8,128)(2,1)S(1)} collective-permute-done((bf16[64,1536]{1,0:T(8,128)(2,1)S(1)}, bf16[64,1536]{1,0:T(8,128)(2,1)S(1)}, u32[]{:S(2)}, u32[]{:S(2)}) %collective-permute-start.37) | collective-permute-done | bytes 196640 | tf_op jit(solution)/shard_map/ppermute | solution.py:249
  140.8 3.4 %collective-permute-done.39.refs_3_ = bf16[64,1536]{1,0:T(8,128)(2,1)S(1)} collective-permute-done((bf16[64,1536]{1,0:T(8,128)(2,1)S(1)}, bf16[64,1536]{1,0:T(8,128)(2,1)S(1)}, u32[]{:S(2)}, u32[]{:S(2)}) %collective-permute-start.39) | collective-permute-done | bytes 196640 | tf_op jit(solution)/shard_map/ppermute | solution.py:249
  144.2 2.0 norm_back.4
  146.2 3.4 %weight_share.6 = bf16[2368,128]{1,0:T(8,128)(2,1)} custom-call(bf16[512,1536]{1,0:T(8,128)(2,1)} %get-tuple-element.210.full_in, bf16[64,1536]{1,0:T(8,128)(2,1)S(1)} %get-tuple-element.212.grad_pre.own, f32[64,256]{1,0:T(8,128)S(1)} %get-tuple-element.211.sums, f32[16,1536]{1,0:T(8,128)S(1)} %copy-done), custom_call_target="tpu_custom_call" | custom-call | flops 905969664 | bytes 2539520 | tf_op jit(solution)/shard_map/weight_share/pallas_call | solution.py:815
  149.7 1.4 collective-permute-done.40.other
  151.1 3.8 %conv_back.6 = (bf16[64,1536]{1,0:T(8,128)(2,1)S(1)}, bf16[64,1536]{1,0:T(8,128)(2,1)S(1)}, bf16[64,1536]{1,0:T(8,128)(2,1)S(1)}, bf16[64,1536]{1,0:T(8,128)(2,1)S(1)}) custom-call(bf16[64,1536]{1,0:T(8,128)(2,1)S(1)} %get-tuple-element.212.grad_pre.own, bf16[64,1536]{1,0:T(8,128)(2,1)S(1)} %collective-permute-done.40.other, ...), custom_call_target="tpu_custom_call" | custom-call | flops 905969664 | bytes 3637248 | tf_op jit(solution)/shard_map/conv_back/pallas_call | solution.py:815
  154.9 1.2 collective-permute-start.41
  157.3 1.2 collective-permute-start.43
  159.5 3.2 %collective-permute-done.41.refs_1_ = bf16[64,1536]{1,0:T(8,128)(2,1)S(1)} collective-permute-done((bf16[64,1536]{1,0:T(8,128)(2,1)S(1)}, bf16[64,1536]{1,0:T(8,128)(2,1)S(1)}, u32[]{:S(2)}, u32[]{:S(2)}) %collective-permute-start.41) | collective-permute-done | bytes 196640 | tf_op jit(solution)/shard_map/ppermute | solution.py:249
  162.7 4.3 %collective-permute-done.42.refs_2_ = bf16[64,1536]{1,0:T(8,128)(2,1)S(1)} collective-permute-done((bf16[64,1536]{1,0:T(8,128)(2,1)S(1)}, bf16[64,1536]{1,0:T(8,128)(2,1)S(1)}, u32[]{:S(2)}, u32[]{:S(2)}) %collective-permute-start.42) | collective-permute-done | bytes 196640 | tf_op jit(solution)/shard_map/ppermute | solution.py:249
  167.7 3.5 %weight_share.7 = (bf16[592,128]{1,0:T(8,128)(2,1)S(1)}, bf16[592,128]{1,0:T(8,128)(2,1)S(1)}, bf16[592,128]{1,0:T(8,128)(2,1)S(1)}, bf16[592,128]{1,0:T(8,128)(2,1)S(1)}) custom-call(bf16[1536,512]{1,0:T(8,128)(2,1)} %get-tuple-element.226.full_in, bf16[64,1536]{1,0:T(8,128)(2,1)S(1)} %get-tuple-element.232.grad_pre.own, ...), custom_call_target="tpu_custom_call" | custom-call | flops 905969664 | bytes 2539520 | tf_op jit(solution)/shard_map/weight_share/pallas_call | solution.py:815
  171.1 4.0 %collective-permute-start.56 = (bf16[592,128]{1,0:T(8,128)(2,1)S(1)}, bf16[592,128]{1,0:T(8,128)(2,1)S(1)}, u32[]{:S(2)}, u32[]{:S(2)}) collective-permute-start(bf16[592,128]{1,0:T(8,128)(2,1)S(1)} %get-tuple-element.229), channel_id=1, source_target_pairs={{0,2},{1,3},{2,0},{3,1},{4,6},{5,7},{6,4},{7,5},{8,10},{9,11},{10,... | collective-permute-start | bytes 454664 | tf_op jit(solution)/shard_map/ppermute | solution.py:249
  175.2 3.8 %conv_back.7 = (bf16[64,1536]{1,0:T(8,128)(2,1)S(1)}, bf16[64,1536]{1,0:T(8,128)(2,1)S(1)}, bf16[64,1536]{1,0:T(8,128)(2,1)S(1)}, bf16[64,1536]{1,0:T(8,128)(2,1)S(1)}) custom-call(bf16[64,1536]{1,0:T(8,128)(2,1)S(1)} %get-tuple-element.232.grad_pre.own, bf16[64,1536]{1,0:T(8,128)(2,1)S(1)} %collective-permute-done.44.other, ...), custom_call_target="tpu_custom_call" | custom-call | flops 905969664 | bytes 3637248 | tf_op jit(solution)/shard_map/conv_back/pallas_call | solution.py:815
  179.5 1.4 collective-permute-start.46
  180.9 1.5 collective-permute-start.47
  183.5 1.4 collective-permute-start.58
  185.0 10.0 %collective-permute-done.57 = bf16[592,128]{1,0:T(8,128)(2,1)S(1)} collective-permute-done((bf16[592,128]{1,0:T(8,128)(2,1)S(1)}, bf16[592,128]{1,0:T(8,128)(2,1)S(1)}, u32[]{:S(2)}, u32[]{:S(2)}) %collective-permute-start.57) | collective-permute-done | bytes 151584 | tf_op jit(solution)/shard_map/ppermute | solution.py:249
  196.7 5.0 %collective-permute-start.49 = (bf16[128,384]{1,0:T(8,128)(2,1)S(1)}, bf16[128,384]{1,0:T(8,128)(2,1)S(1)}, u32[]{:S(2)}, u32[]{:S(2)}) collective-permute-start(bf16[128,384]{1,0:T(8,128)(2,1)S(1)} %get-tuple-element.243), channel_id=1, source_target_pairs={{0,2},{1,3},{2,10},{3,11},{4,18},{5,19},{6,26},{7,27},{8,0},{9,1},... | collective-permute-start | bytes 294920 | tf_op jit(solution)/shard_map/ppermute | solution.py:249
  201.7 3.8 %collective-permute-start.50 = (bf16[128,384]{1,0:T(8,128)(2,1)S(1)}, bf16[128,384]{1,0:T(8,128)(2,1)S(1)}, u32[]{:S(2)}, u32[]{:S(2)}) collective-permute-start(bf16[128,384]{1,0:T(8,128)(2,1)S(1)} %get-tuple-element.244), channel_id=1, source_target_pairs={{0,4},{1,5},{2,12},{3,13},{4,20},{5,21},{6,28},{7,29},{8,6},{9,7},... | collective-permute-start | bytes 294920 | tf_op jit(solution)/shard_map/ppermute | solution.py:249
  205.6 1.3 select_select_fusion
  206.9 3.9 %collective-permute-start.60 = (bf16[592,128]{1,0:T(8,128)(2,1)S(1)}, bf16[592,128]{1,0:T(8,128)(2,1)S(1)}, u32[]{:S(2)}, u32[]{:S(2)}) collective-permute-start(bf16[592,128]{1,0:T(8,128)(2,1)S(1)} %get-tuple-element.263), channel_id=1, source_target_pairs={{0,16},{1,17},{2,18},{3,19},{4,20},{5,21},{6,22},{7,23},{8,24},{9,... | collective-permute-start | bytes 454664 | tf_op jit(solution)/shard_map/ppermute | solution.py:249
  210.8 1.6 collective-permute-start.61
  212.9 2.0 collective-permute-done.60.refs_2_
  214.9 1.8 collective-permute-done.59.refs_1_
  216.7 4.8 %collective-permute-done.61.refs_3_ = bf16[592,128]{1,0:T(8,128)(2,1)S(1)} collective-permute-done((bf16[592,128]{1,0:T(8,128)(2,1)S(1)}, bf16[592,128]{1,0:T(8,128)(2,1)S(1)}, u32[]{:S(2)}, u32[]{:S(2)}) %collective-permute-start.61) | collective-permute-done | bytes 151584 | tf_op jit(solution)/shard_map/ppermute | solution.py:249
  224.8 1.9 grads_out.1
  (118 shorter events, 30.3 us)
Async XLA Ops:
  7.2 198.3 %reduce-scatter.8.cloned.1.call-start = ((), (), s32[]{:S(2)}) async-start(), calls=%async_computation.5 | async-start | bytes 757760 | tf_op jit(solution)/shard_map/reduce_scatter | solution.py:985
  10.9 28.6 %collective-permute-start.7 = (bf16[592,512]{1,0:T(8,128)(2,1)S(1)}, bf16[592,512]{1,0:T(8,128)(2,1)}, u32[]{:S(2)}, u32[]{:S(2)}) collective-permute-start(bf16[592,512]{1,0:T(8,128)(2,1)S(1)} %get-tuple-element.134), channel_id=1, source_target_pairs={{0,8},{1,9},{2,10},{3,11},{4,12},{5,13},{6,14},{7,15},{8,0},{9,1},... | collective-permute-start | bytes 1818632 | tf_op jit(solution)/shard_map/ppermute | solution.py:249
  14.0 28.3 %collective-permute-start.8 = (bf16[592,512]{1,0:T(8,128)(2,1)S(1)}, bf16[592,512]{1,0:T(8,128)(2,1)}, u32[]{:S(2)}, u32[]{:S(2)}) collective-permute-start(bf16[592,512]{1,0:T(8,128)(2,1)S(1)} %get-tuple-element.135), channel_id=1, source_target_pairs={{0,16},{1,17},{2,18},{3,19},{4,20},{5,21},{6,22},{7,23},{8,24},{9,... | collective-permute-start | bytes 1818632 | tf_op jit(solution)/shard_map/ppermute | solution.py:249
  17.3 13.1 %collective-permute-start = (bf16[208,640]{1,0:T(8,128)(2,1)S(1)}, bf16[208,640]{1,0:T(8,128)(2,1)S(1)}, u32[]{:S(2)}, u32[]{:S(2)}) collective-permute-start(bf16[208,640]{1,0:T(8,128)(2,1)S(1)} %get-tuple-element.139), channel_id=1, source_target_pairs={{0,2},{1,3},{2,0},{3,1},{4,6},{5,7},{6,4},{7,5},{8,10},{9,11},{10,... | collective-permute-start | bytes 798728 | tf_op jit(solution)/shard_map/ppermute | solution.py:249
  18.9 23.4 %collective-permute-start.9 = (bf16[592,512]{1,0:T(8,128)(2,1)S(1)}, bf16[592,512]{1,0:T(8,128)(2,1)}, u32[]{:S(2)}, u32[]{:S(2)}) collective-permute-start(bf16[592,512]{1,0:T(8,128)(2,1)S(1)} %get-tuple-element.136), channel_id=1, source_target_pairs={{0,24},{1,25},{2,26},{3,27},{4,28},{5,29},{6,30},{7,31},{8,16},{9,... | collective-permute-start | bytes 1818632 | tf_op jit(solution)/shard_map/ppermute | solution.py:249
  19.4 19.6 %collective-permute-start.1 = (bf16[208,640]{1,0:T(8,128)(2,1)S(1)}, bf16[208,640]{1,0:T(8,128)(2,1)S(1)}, u32[]{:S(2)}, u32[]{:S(2)}) collective-permute-start(bf16[208,640]{1,0:T(8,128)(2,1)S(1)} %get-tuple-element.140), channel_id=1, source_target_pairs={{0,4},{1,5},{2,6},{3,7},{4,0},{5,1},{6,2},{7,3},{8,12},{9,13},{10,... | collective-permute-start | bytes 798728 | tf_op jit(solution)/shard_map/ppermute | solution.py:249
  30.4 8.6 %collective-permute-start.2 = (bf16[208,640]{1,0:T(8,128)(2,1)S(1)}, bf16[208,640]{1,0:T(8,128)(2,1)S(1)}, u32[]{:S(2)}, u32[]{:S(2)}) collective-permute-start(bf16[208,640]{1,0:T(8,128)(2,1)S(1)} %get-tuple-element.141), channel_id=1, source_target_pairs={{0,6},{1,7},{2,4},{3,5},{4,2},{5,3},{6,0},{7,1},{8,14},{9,15},{10,... | collective-permute-start | bytes 798728 | tf_op jit(solution)/shard_map/ppermute | solution.py:249
  39.0 3.3 %collective-permute-start.3 = (bf16[208,640]{1,0:T(8,128)(2,1)S(1)}, bf16[208,640]{1,0:T(8,128)(2,1)S(1)}, u32[]{:S(2)}, u32[]{:S(2)}) collective-permute-start(bf16[208,640]{1,0:T(8,128)(2,1)S(1)} %get-tuple-element.138.refs_0_), channel_id=1, source_target_pairs={{0,1},{1,0},{2,3},{3,2},{4,5},{5,4},{6,7},{7,6},{8,9},{9,8},{10,11... | collective-permute-start | bytes 798728 | tf_op jit(solution)/shard_map/ppermute | solution.py:249
  39.0 3.3 %collective-permute-start.4 = (bf16[208,640]{1,0:T(8,128)(2,1)S(1)}, bf16[208,640]{1,0:T(8,128)(2,1)S(1)}, u32[]{:S(2)}, u32[]{:S(2)}) collective-permute-start(bf16[208,640]{1,0:T(8,128)(2,1)S(1)} %collective-permute-done.refs_1_), channel_id=1, source_target_pairs={{0,1},{1,0},{2,3},{3,2},{4,5},{5,4},{6,7},{7,6},{8,9},{9,8},{10,11... | collective-permute-start | bytes 798728 | tf_op jit(solution)/shard_map/ppermute | solution.py:249
  39.6 2.8 %collective-permute-start.5 = (bf16[208,640]{1,0:T(8,128)(2,1)S(1)}, bf16[208,640]{1,0:T(8,128)(2,1)S(1)}, u32[]{:S(2)}, u32[]{:S(2)}) collective-permute-start(bf16[208,640]{1,0:T(8,128)(2,1)S(1)} %collective-permute-done.1.refs_2_), channel_id=1, source_target_pairs={{0,1},{1,0},{2,3},{3,2},{4,5},{5,4},{6,7},{7,6},{8,9},{9,8},{10,11... | collective-permute-start | bytes 798728 | tf_op jit(solution)/shard_map/ppermute | solution.py:249
  42.3 1.5 collective-permute-start.6
  47.6 8.8 %collective-permute-start.12 = (bf16[64,1536]{1,0:T(8,128)(2,1)S(1)}, bf16[64,1536]{1,0:T(8,128)(2,1)S(1)}, u32[]{:S(2)}, u32[]{:S(2)}) collective-permute-start(bf16[64,1536]{1,0:T(8,128)(2,1)S(1)} %get-tuple-element.148.refs_0_), channel_id=1, source_target_pairs={{0,24},{1,25},{2,26},{3,27},{4,28},{5,29},{6,30},{7,31},{8,16},{9,... | collective-permute-start | bytes 589832 | tf_op jit(solution)/shard_map/ppermute | solution.py:249
  49.7 10.0 %collective-permute-start.11 = (bf16[64,1536]{1,0:T(8,128)(2,1)S(1)}, bf16[64,1536]{1,0:T(8,128)(2,1)S(1)}, u32[]{:S(2)}, u32[]{:S(2)}) collective-permute-start(bf16[64,1536]{1,0:T(8,128)(2,1)S(1)} %get-tuple-element.148.refs_0_), channel_id=1, source_target_pairs={{0,16},{1,17},{2,18},{3,19},{4,20},{5,21},{6,22},{7,23},{8,24},{9,... | collective-permute-start | bytes 589832 | tf_op jit(solution)/shard_map/ppermute | solution.py:249
  49.8 10.0 %collective-permute-start.10 = (bf16[64,1536]{1,0:T(8,128)(2,1)S(1)}, bf16[64,1536]{1,0:T(8,128)(2,1)S(1)}, u32[]{:S(2)}, u32[]{:S(2)}) collective-permute-start(bf16[64,1536]{1,0:T(8,128)(2,1)S(1)} %get-tuple-element.148.refs_0_), channel_id=1, source_target_pairs={{0,8},{1,9},{2,10},{3,11},{4,12},{5,13},{6,14},{7,15},{8,0},{9,1},... | collective-permute-start | bytes 589832 | tf_op jit(solution)/shard_map/ppermute | solution.py:249
  51.1 9.2 %collective-permute-start.13 = (bf16[64,1536]{1,0:T(8,128)(2,1)S(1)}, bf16[64,1536]{1,0:T(8,128)(2,1)S(1)}, u32[]{:S(2)}, u32[]{:S(2)}) collective-permute-start(bf16[64,1536]{1,0:T(8,128)(2,1)S(1)} %get-tuple-element.148.refs_0_), channel_id=1, source_target_pairs={{0,1},{1,0},{2,3},{3,2},{4,5},{5,4},{6,7},{7,6},{8,9},{9,8},{10,11... | collective-permute-start | bytes 589832 | tf_op jit(solution)/shard_map/ppermute | solution.py:249
  59.8 1.7 collective-permute-start.15
  64.9 8.7 %collective-permute-start.19 = (bf16[64,1536]{1,0:T(8,128)(2,1)S(1)}, bf16[64,1536]{1,0:T(8,128)(2,1)S(1)}, u32[]{:S(2)}, u32[]{:S(2)}) collective-permute-start(bf16[64,1536]{1,0:T(8,128)(2,1)S(1)} %get-tuple-element.159.refs_0_), channel_id=1, source_target_pairs={{0,24},{1,25},{2,26},{3,27},{4,28},{5,29},{6,30},{7,31},{8,16},{9,... | collective-permute-start | bytes 589832 | tf_op jit(solution)/shard_map/ppermute | solution.py:249
  66.6 10.5 %collective-permute-start.18 = (bf16[64,1536]{1,0:T(8,128)(2,1)S(1)}, bf16[64,1536]{1,0:T(8,128)(2,1)S(1)}, u32[]{:S(2)}, u32[]{:S(2)}) collective-permute-start(bf16[64,1536]{1,0:T(8,128)(2,1)S(1)} %get-tuple-element.159.refs_0_), channel_id=1, source_target_pairs={{0,16},{1,17},{2,18},{3,19},{4,20},{5,21},{6,22},{7,23},{8,24},{9,... | collective-permute-start | bytes 589832 | tf_op jit(solution)/shard_map/ppermute | solution.py:249
  67.6 9.5 %collective-permute-start.17 = (bf16[64,1536]{1,0:T(8,128)(2,1)S(1)}, bf16[64,1536]{1,0:T(8,128)(2,1)S(1)}, u32[]{:S(2)}, u32[]{:S(2)}) collective-permute-start(bf16[64,1536]{1,0:T(8,128)(2,1)S(1)} %get-tuple-element.159.refs_0_), channel_id=1, source_target_pairs={{0,8},{1,9},{2,10},{3,11},{4,12},{5,13},{6,14},{7,15},{8,0},{9,1},... | collective-permute-start | bytes 589832 | tf_op jit(solution)/shard_map/ppermute | solution.py:249
  68.4 9.2 %collective-permute-start.20 = (bf16[64,1536]{1,0:T(8,128)(2,1)S(1)}, bf16[64,1536]{1,0:T(8,128)(2,1)S(1)}, u32[]{:S(2)}, u32[]{:S(2)}) collective-permute-start(bf16[64,1536]{1,0:T(8,128)(2,1)S(1)} %get-tuple-element.159.refs_0_), channel_id=1, source_target_pairs={{0,1},{1,0},{2,3},{3,2},{4,5},{5,4},{6,7},{7,6},{8,9},{9,8},{10,11... | collective-permute-start | bytes 589832 | tf_op jit(solution)/shard_map/ppermute | solution.py:249
  77.1 1.7 collective-permute-start.22
  81.5 8.7 %collective-permute-start.26 = (bf16[64,1536]{1,0:T(8,128)(2,1)S(1)}, bf16[64,1536]{1,0:T(8,128)(2,1)S(1)}, u32[]{:S(2)}, u32[]{:S(2)}) collective-permute-start(bf16[64,1536]{1,0:T(8,128)(2,1)S(1)} %get-tuple-element.167.refs_0_), channel_id=1, source_target_pairs={{0,24},{1,25},{2,26},{3,27},{4,28},{5,29},{6,30},{7,31},{8,16},{9,... | collective-permute-start | bytes 589832 | tf_op jit(solution)/shard_map/ppermute | solution.py:249
  83.3 10.5 %collective-permute-start.25 = (bf16[64,1536]{1,0:T(8,128)(2,1)S(1)}, bf16[64,1536]{1,0:T(8,128)(2,1)S(1)}, u32[]{:S(2)}, u32[]{:S(2)}) collective-permute-start(bf16[64,1536]{1,0:T(8,128)(2,1)S(1)} %get-tuple-element.167.refs_0_), channel_id=1, source_target_pairs={{0,16},{1,17},{2,18},{3,19},{4,20},{5,21},{6,22},{7,23},{8,24},{9,... | collective-permute-start | bytes 589832 | tf_op jit(solution)/shard_map/ppermute | solution.py:249
  84.2 9.5 %collective-permute-start.24 = (bf16[64,1536]{1,0:T(8,128)(2,1)S(1)}, bf16[64,1536]{1,0:T(8,128)(2,1)S(1)}, u32[]{:S(2)}, u32[]{:S(2)}) collective-permute-start(bf16[64,1536]{1,0:T(8,128)(2,1)S(1)} %get-tuple-element.167.refs_0_), channel_id=1, source_target_pairs={{0,8},{1,9},{2,10},{3,11},{4,12},{5,13},{6,14},{7,15},{8,0},{9,1},... | collective-permute-start | bytes 589832 | tf_op jit(solution)/shard_map/ppermute | solution.py:249
  85.1 12.1 %collective-permute-start.27 = (bf16[64,1536]{1,0:T(8,128)(2,1)S(1)}, bf16[64,1536]{1,0:T(8,128)(2,1)S(1)}, u32[]{:S(2)}, u32[]{:S(2)}) collective-permute-start(bf16[64,1536]{1,0:T(8,128)(2,1)S(1)} %get-tuple-element.167.refs_0_), channel_id=1, source_target_pairs={{0,1},{1,0},{2,3},{3,2},{4,5},{5,4},{6,7},{7,6},{8,9},{9,8},{10,11... | collective-permute-start | bytes 589832 | tf_op jit(solution)/shard_map/ppermute | solution.py:249
  93.8 3.4 %collective-permute-start.28 = (bf16[64,1536]{1,0:T(8,128)(2,1)S(1)}, bf16[64,1536]{1,0:T(8,128)(2,1)S(1)}, u32[]{:S(2)}, u32[]{:S(2)}) collective-permute-start(bf16[64,1536]{1,0:T(8,128)(2,1)S(1)} %collective-permute-done.24.refs_1_), channel_id=1, source_target_pairs={{0,1},{1,0},{2,3},{3,2},{4,5},{5,4},{6,7},{7,6},{8,9},{9,8},{10,11... | collective-permute-start | bytes 589832 | tf_op jit(solution)/shard_map/ppermute | solution.py:249
  93.8 3.4 %collective-permute-start.29 = (bf16[64,1536]{1,0:T(8,128)(2,1)S(1)}, bf16[64,1536]{1,0:T(8,128)(2,1)S(1)}, u32[]{:S(2)}, u32[]{:S(2)}) collective-permute-start(bf16[64,1536]{1,0:T(8,128)(2,1)S(1)} %collective-permute-done.25.refs_2_), channel_id=1, source_target_pairs={{0,1},{1,0},{2,3},{3,2},{4,5},{5,4},{6,7},{7,6},{8,9},{9,8},{10,11... | collective-permute-start | bytes 589832 | tf_op jit(solution)/shard_map/ppermute | solution.py:249
  94.3 2.9 %collective-permute-start.30 = (bf16[64,1536]{1,0:T(8,128)(2,1)S(1)}, bf16[64,1536]{1,0:T(8,128)(2,1)S(1)}, u32[]{:S(2)}, u32[]{:S(2)}) collective-permute-start(bf16[64,1536]{1,0:T(8,128)(2,1)S(1)} %collective-permute-done.26.refs_3_), channel_id=1, source_target_pairs={{0,1},{1,0},{2,3},{3,2},{4,5},{5,4},{6,7},{7,6},{8,9},{9,8},{10,11... | collective-permute-start | bytes 589832 | tf_op jit(solution)/shard_map/ppermute | solution.py:249
  96.7 7.9 %collective-permute-start.32 = (bf16[1024,576]{0,1:T(8,128)(2,1)}, bf16[1024,576]{0,1:T(8,128)(2,1)}, u32[]{:S(2)}, u32[]{:S(2)}) collective-permute-start(bf16[1024,576]{0,1:T(8,128)(2,1)} %copy.15), channel_id=1, source_target_pairs={{0,1},{1,0},{2,3},{3,2},{4,5},{5,4},{6,7},{7,6},{8,9},{9,8},{10,11... | collective-permute-start | bytes 3538952 | tf_op jit(solution)/shard_map/ppermute | solution.py:249
  103.0 102.5 %reduce-scatter.6.cloned.1.call-start = ((), (), s32[]{:S(2)}) async-start(), calls=%async_computation.4 | async-start | bytes 757760 | tf_op jit(solution)/shard_map/reduce_scatter | solution.py:985
  103.0 1.5 collective-permute-start.31
  110.8 7.8 %collective-permute-start.33 = (bf16[64,1536]{1,0:T(8,128)(2,1)S(1)}, bf16[64,1536]{1,0:T(8,128)(2,1)S(1)}, u32[]{:S(2)}, u32[]{:S(2)}) collective-permute-start(bf16[64,1536]{1,0:T(8,128)(2,1)S(1)} %get-tuple-element.183), channel_id=1, source_target_pairs={{0,8},{1,9},{2,10},{3,11},{4,12},{5,13},{6,14},{7,15},{8,0},{9,1},... | collective-permute-start | bytes 589832 | tf_op jit(solution)/shard_map/ppermute | solution.py:249
  112.0 10.9 %collective-permute-start.34 = (bf16[64,1536]{1,0:T(8,128)(2,1)S(1)}, bf16[64,1536]{1,0:T(8,128)(2,1)S(1)}, u32[]{:S(2)}, u32[]{:S(2)}) collective-permute-start(bf16[64,1536]{1,0:T(8,128)(2,1)S(1)} %get-tuple-element.184), channel_id=1, source_target_pairs={{0,16},{1,17},{2,18},{3,19},{4,20},{5,21},{6,22},{7,23},{8,24},{9,... | collective-permute-start | bytes 589832 | tf_op jit(solution)/shard_map/ppermute | solution.py:249
  113.1 9.8 %collective-permute-start.35 = (bf16[64,1536]{1,0:T(8,128)(2,1)S(1)}, bf16[64,1536]{1,0:T(8,128)(2,1)S(1)}, u32[]{:S(2)}, u32[]{:S(2)}) collective-permute-start(bf16[64,1536]{1,0:T(8,128)(2,1)S(1)} %get-tuple-element.185), channel_id=1, source_target_pairs={{0,24},{1,25},{2,26},{3,27},{4,28},{5,29},{6,30},{7,31},{8,16},{9,... | collective-permute-start | bytes 589832 | tf_op jit(solution)/shard_map/ppermute | solution.py:249
  126.8 78.8 %reduce-scatter.4.cloned.1.call-start = ((), (), s32[]{:S(2)}) async-start(), calls=%async_computation.3 | async-start | bytes 757760 | tf_op jit(solution)/shard_map/reduce_scatter | solution.py:985
  127.1 1.5 collective-permute-start.36
  132.4 7.8 %collective-permute-start.37 = (bf16[64,1536]{1,0:T(8,128)(2,1)S(1)}, bf16[64,1536]{1,0:T(8,128)(2,1)S(1)}, u32[]{:S(2)}, u32[]{:S(2)}) collective-permute-start(bf16[64,1536]{1,0:T(8,128)(2,1)S(1)} %get-tuple-element.199), channel_id=1, source_target_pairs={{0,8},{1,9},{2,10},{3,11},{4,12},{5,13},{6,14},{7,15},{8,0},{9,1},... | collective-permute-start | bytes 589832 | tf_op jit(solution)/shard_map/ppermute | solution.py:249
  133.3 7.5 %collective-permute-start.38 = (bf16[64,1536]{1,0:T(8,128)(2,1)S(1)}, bf16[64,1536]{1,0:T(8,128)(2,1)S(1)}, u32[]{:S(2)}, u32[]{:S(2)}) collective-permute-start(bf16[64,1536]{1,0:T(8,128)(2,1)S(1)} %get-tuple-element.200), channel_id=1, source_target_pairs={{0,16},{1,17},{2,18},{3,19},{4,20},{5,21},{6,22},{7,23},{8,24},{9,... | collective-permute-start | bytes 589832 | tf_op jit(solution)/shard_map/ppermute | solution.py:249
  134.4 9.7 %collective-permute-start.39 = (bf16[64,1536]{1,0:T(8,128)(2,1)S(1)}, bf16[64,1536]{1,0:T(8,128)(2,1)S(1)}, u32[]{:S(2)}, u32[]{:S(2)}) collective-permute-start(bf16[64,1536]{1,0:T(8,128)(2,1)S(1)} %get-tuple-element.201), channel_id=1, source_target_pairs={{0,24},{1,25},{2,26},{3,27},{4,28},{5,29},{6,30},{7,31},{8,16},{9,... | collective-permute-start | bytes 589832 | tf_op jit(solution)/shard_map/ppermute | solution.py:249
  149.6 1.5 collective-permute-start.40
  154.9 7.8 %collective-permute-start.41 = (bf16[64,1536]{1,0:T(8,128)(2,1)S(1)}, bf16[64,1536]{1,0:T(8,128)(2,1)S(1)}, u32[]{:S(2)}, u32[]{:S(2)}) collective-permute-start(bf16[64,1536]{1,0:T(8,128)(2,1)S(1)} %get-tuple-element.215), channel_id=1, source_target_pairs={{0,8},{1,9},{2,10},{3,11},{4,12},{5,13},{6,14},{7,15},{8,0},{9,1},... | collective-permute-start | bytes 589832 | tf_op jit(solution)/shard_map/ppermute | solution.py:249
  156.2 10.9 %collective-permute-start.42 = (bf16[64,1536]{1,0:T(8,128)(2,1)S(1)}, bf16[64,1536]{1,0:T(8,128)(2,1)S(1)}, u32[]{:S(2)}, u32[]{:S(2)}) collective-permute-start(bf16[64,1536]{1,0:T(8,128)(2,1)S(1)} %get-tuple-element.216), channel_id=1, source_target_pairs={{0,16},{1,17},{2,18},{3,19},{4,20},{5,21},{6,22},{7,23},{8,24},{9,... | collective-permute-start | bytes 589832 | tf_op jit(solution)/shard_map/ppermute | solution.py:249
  157.3 9.8 %collective-permute-start.43 = (bf16[64,1536]{1,0:T(8,128)(2,1)S(1)}, bf16[64,1536]{1,0:T(8,128)(2,1)S(1)}, u32[]{:S(2)}, u32[]{:S(2)}) collective-permute-start(bf16[64,1536]{1,0:T(8,128)(2,1)S(1)} %get-tuple-element.217), channel_id=1, source_target_pairs={{0,24},{1,25},{2,26},{3,27},{4,28},{5,29},{6,30},{7,31},{8,16},{9,... | collective-permute-start | bytes 589832 | tf_op jit(solution)/shard_map/ppermute | solution.py:249
  167.6 7.6 %collective-permute-start.44 = (bf16[64,1536]{1,0:T(8,128)(2,1)S(1)}, bf16[64,1536]{1,0:T(8,128)(2,1)S(1)}, u32[]{:S(2)}, u32[]{:S(2)}) collective-permute-start(bf16[64,1536]{1,0:T(8,128)(2,1)S(1)} %get-tuple-element.232.grad_pre.own), channel_id=1, source_target_pairs={{0,1},{1,0},{2,3},{3,2},{4,5},{5,4},{6,7},{7,6},{8,9},{9,8},{10,11... | collective-permute-start | bytes 589832 | tf_op jit(solution)/shard_map/ppermute | solution.py:249
  171.1 12.4 %collective-permute-start.56 = (bf16[592,128]{1,0:T(8,128)(2,1)S(1)}, bf16[592,128]{1,0:T(8,128)(2,1)S(1)}, u32[]{:S(2)}, u32[]{:S(2)}) collective-permute-start(bf16[592,128]{1,0:T(8,128)(2,1)S(1)} %get-tuple-element.229), channel_id=1, source_target_pairs={{0,2},{1,3},{2,0},{3,1},{4,6},{5,7},{6,4},{7,5},{8,10},{9,11},{10,... | collective-permute-start | bytes 454664 | tf_op jit(solution)/shard_map/ppermute | solution.py:249
  178.9 16.1 %collective-permute-start.45 = (bf16[64,1536]{1,0:T(8,128)(2,1)S(1)}, bf16[64,1536]{1,0:T(8,128)(2,1)S(1)}, u32[]{:S(2)}, u32[]{:S(2)}) collective-permute-start(bf16[64,1536]{1,0:T(8,128)(2,1)S(1)} %get-tuple-element.235), channel_id=1, source_target_pairs={{0,8},{1,9},{2,10},{3,11},{4,12},{5,13},{6,14},{7,15},{8,0},{9,1},... | collective-permute-start | bytes 589832 | tf_op jit(solution)/shard_map/ppermute | solution.py:249
  179.5 15.5 %collective-permute-start.46 = (bf16[64,1536]{1,0:T(8,128)(2,1)S(1)}, bf16[64,1536]{1,0:T(8,128)(2,1)S(1)}, u32[]{:S(2)}, u32[]{:S(2)}) collective-permute-start(bf16[64,1536]{1,0:T(8,128)(2,1)S(1)} %get-tuple-element.236), channel_id=1, source_target_pairs={{0,16},{1,17},{2,18},{3,19},{4,20},{5,21},{6,22},{7,23},{8,24},{9,... | collective-permute-start | bytes 589832 | tf_op jit(solution)/shard_map/ppermute | solution.py:249
  180.9 14.1 %collective-permute-start.47 = (bf16[64,1536]{1,0:T(8,128)(2,1)S(1)}, bf16[64,1536]{1,0:T(8,128)(2,1)S(1)}, u32[]{:S(2)}, u32[]{:S(2)}) collective-permute-start(bf16[64,1536]{1,0:T(8,128)(2,1)S(1)} %get-tuple-element.237), channel_id=1, source_target_pairs={{0,24},{1,25},{2,26},{3,27},{4,28},{5,29},{6,30},{7,31},{8,16},{9,... | collective-permute-start | bytes 589832 | tf_op jit(solution)/shard_map/ppermute | solution.py:249
  182.5 12.5 %collective-permute-start.57 = (bf16[592,128]{1,0:T(8,128)(2,1)S(1)}, bf16[592,128]{1,0:T(8,128)(2,1)S(1)}, u32[]{:S(2)}, u32[]{:S(2)}) collective-permute-start(bf16[592,128]{1,0:T(8,128)(2,1)S(1)} %get-tuple-element.230), channel_id=1, source_target_pairs={{0,4},{1,5},{2,6},{3,7},{4,0},{5,1},{6,2},{7,3},{8,12},{9,13},{10,... | collective-permute-start | bytes 454664 | tf_op jit(solution)/shard_map/ppermute | solution.py:249
  183.5 11.5 %collective-permute-start.58 = (bf16[592,128]{1,0:T(8,128)(2,1)S(1)}, bf16[592,128]{1,0:T(8,128)(2,1)S(1)}, u32[]{:S(2)}, u32[]{:S(2)}) collective-permute-start(bf16[592,128]{1,0:T(8,128)(2,1)S(1)} %get-tuple-element.231), channel_id=1, source_target_pairs={{0,6},{1,7},{2,4},{3,5},{4,2},{5,3},{6,0},{7,1},{8,14},{9,15},{10,... | collective-permute-start | bytes 454664 | tf_op jit(solution)/shard_map/ppermute | solution.py:249
  196.0 14.8 %collective-permute-start.48 = (bf16[128,384]{1,0:T(8,128)(2,1)S(1)}, bf16[128,384]{1,0:T(8,128)(2,1)S(1)}, u32[]{:S(2)}, u32[]{:S(2)}) collective-permute-start(bf16[128,384]{1,0:T(8,128)(2,1)S(1)} %get-tuple-element.242), channel_id=1, source_target_pairs={{0,0},{1,1},{2,8},{3,9},{4,16},{5,17},{6,24},{7,25},{8,2},{9,3},{1... | collective-permute-start | bytes 294920 | tf_op jit(solution)/shard_map/ppermute | solution.py:249
  196.7 14.1 %collective-permute-start.49 = (bf16[128,384]{1,0:T(8,128)(2,1)S(1)}, bf16[128,384]{1,0:T(8,128)(2,1)S(1)}, u32[]{:S(2)}, u32[]{:S(2)}) collective-permute-start(bf16[128,384]{1,0:T(8,128)(2,1)S(1)} %get-tuple-element.243), channel_id=1, source_target_pairs={{0,2},{1,3},{2,10},{3,11},{4,18},{5,19},{6,26},{7,27},{8,0},{9,1},... | collective-permute-start | bytes 294920 | tf_op jit(solution)/shard_map/ppermute | solution.py:249
  201.7 10.7 %collective-permute-start.50 = (bf16[128,384]{1,0:T(8,128)(2,1)S(1)}, bf16[128,384]{1,0:T(8,128)(2,1)S(1)}, u32[]{:S(2)}, u32[]{:S(2)}) collective-permute-start(bf16[128,384]{1,0:T(8,128)(2,1)S(1)} %get-tuple-element.244), channel_id=1, source_target_pairs={{0,4},{1,5},{2,12},{3,13},{4,20},{5,21},{6,28},{7,29},{8,6},{9,7},... | collective-permute-start | bytes 294920 | tf_op jit(solution)/shard_map/ppermute | solution.py:249
  205.5 6.9 %collective-permute-start.51 = (bf16[128,384]{1,0:T(8,128)(2,1)S(1)}, bf16[128,384]{1,0:T(8,128)(2,1)S(1)}, u32[]{:S(2)}, u32[]{:S(2)}) collective-permute-start(bf16[128,384]{1,0:T(8,128)(2,1)S(1)} %get-tuple-element.245), channel_id=1, source_target_pairs={{0,6},{1,7},{2,14},{3,15},{4,22},{5,23},{6,30},{7,31},{8,4},{9,5},... | collective-permute-start | bytes 294920 | tf_op jit(solution)/shard_map/ppermute | solution.py:249
  206.9 8.0 %collective-permute-start.60 = (bf16[592,128]{1,0:T(8,128)(2,1)S(1)}, bf16[592,128]{1,0:T(8,128)(2,1)S(1)}, u32[]{:S(2)}, u32[]{:S(2)}) collective-permute-start(bf16[592,128]{1,0:T(8,128)(2,1)S(1)} %get-tuple-element.263), channel_id=1, source_target_pairs={{0,16},{1,17},{2,18},{3,19},{4,20},{5,21},{6,22},{7,23},{8,24},{9,... | collective-permute-start | bytes 454664 | tf_op jit(solution)/shard_map/ppermute | solution.py:249
  210.8 5.9 %collective-permute-start.59 = (bf16[592,128]{1,0:T(8,128)(2,1)S(1)}, bf16[592,128]{1,0:T(8,128)(2,1)S(1)}, u32[]{:S(2)}, u32[]{:S(2)}) collective-permute-start(bf16[592,128]{1,0:T(8,128)(2,1)S(1)} %get-tuple-element.264), channel_id=1, source_target_pairs={{0,8},{1,9},{2,10},{3,11},{4,12},{5,13},{6,14},{7,15},{8,0},{9,1},... | collective-permute-start | bytes 454664 | tf_op jit(solution)/shard_map/ppermute | solution.py:249
  210.8 10.7 %collective-permute-start.61 = (bf16[592,128]{1,0:T(8,128)(2,1)S(1)}, bf16[592,128]{1,0:T(8,128)(2,1)S(1)}, u32[]{:S(2)}, u32[]{:S(2)}) collective-permute-start(bf16[592,128]{1,0:T(8,128)(2,1)S(1)} %get-tuple-element.261), channel_id=1, source_target_pairs={{0,24},{1,25},{2,26},{3,27},{4,28},{5,29},{6,30},{7,31},{8,16},{9,... | collective-permute-start | bytes 454664 | tf_op jit(solution)/shard_map/ppermute | solution.py:249
  212.4 9.2 %collective-permute-start.52 = (bf16[128,384]{1,0:T(8,128)(2,1)S(1)}, bf16[128,384]{1,0:T(8,128)(2,1)S(1)}, u32[]{:S(2)}, u32[]{:S(2)}) collective-permute-start(bf16[128,384]{1,0:T(8,128)(2,1)S(1)} %collective-permute-done.48.refs_0_), channel_id=1, source_target_pairs={{0,1},{1,0},{2,3},{3,2},{4,5},{5,4},{6,7},{7,6},{8,9},{9,8},{10,11... | collective-permute-start | bytes 294920 | tf_op jit(solution)/shard_map/ppermute | solution.py:249
  212.4 9.7 %collective-permute-start.53 = (bf16[128,384]{1,0:T(8,128)(2,1)S(1)}, bf16[128,384]{1,0:T(8,128)(2,1)S(1)}, u32[]{:S(2)}, u32[]{:S(2)}) collective-permute-start(bf16[128,384]{1,0:T(8,128)(2,1)S(1)} %collective-permute-done.49.refs_1_), channel_id=1, source_target_pairs={{0,1},{1,0},{2,3},{3,2},{4,5},{5,4},{6,7},{7,6},{8,9},{9,8},{10,11... | collective-permute-start | bytes 294920 | tf_op jit(solution)/shard_map/ppermute | solution.py:249
  214.9 7.3 %collective-permute-start.54 = (bf16[128,384]{1,0:T(8,128)(2,1)S(1)}, bf16[128,384]{1,0:T(8,128)(2,1)S(1)}, u32[]{:S(2)}, u32[]{:S(2)}) collective-permute-start(bf16[128,384]{1,0:T(8,128)(2,1)S(1)} %collective-permute-done.50.refs_2_), channel_id=1, source_target_pairs={{0,1},{1,0},{2,3},{3,2},{4,5},{5,4},{6,7},{7,6},{8,9},{9,8},{10,11... | collective-permute-start | bytes 294920 | tf_op jit(solution)/shard_map/ppermute | solution.py:249
  216.7 8.0 %collective-permute-start.62 = (bf16[592,128]{1,0:T(8,128)(2,1)S(1)}, bf16[592,128]{1,0:T(8,128)(2,1)S(1)}, u32[]{:S(2)}, u32[]{:S(2)}) collective-permute-start(bf16[592,128]{1,0:T(8,128)(2,1)S(1)} %get-tuple-element.265.refs_0_), channel_id=1, source_target_pairs={{0,1},{1,0},{2,3},{3,2},{4,5},{5,4},{6,7},{7,6},{8,9},{9,8},{10,11... | collective-permute-start | bytes 454664 | tf_op jit(solution)/shard_map/ppermute | solution.py:249
  221.6 3.2 %collective-permute-start.63 = (bf16[592,128]{1,0:T(8,128)(2,1)S(1)}, bf16[592,128]{1,0:T(8,128)(2,1)S(1)}, u32[]{:S(2)}, u32[]{:S(2)}) collective-permute-start(bf16[592,128]{1,0:T(8,128)(2,1)S(1)} %collective-permute-done.59.refs_1_), channel_id=1, source_target_pairs={{0,1},{1,0},{2,3},{3,2},{4,5},{5,4},{6,7},{7,6},{8,9},{9,8},{10,11... | collective-permute-start | bytes 454664 | tf_op jit(solution)/shard_map/ppermute | solution.py:249
  221.6 3.2 %collective-permute-start.64 = (bf16[592,128]{1,0:T(8,128)(2,1)S(1)}, bf16[592,128]{1,0:T(8,128)(2,1)S(1)}, u32[]{:S(2)}, u32[]{:S(2)}) collective-permute-start(bf16[592,128]{1,0:T(8,128)(2,1)S(1)} %collective-permute-done.60.refs_2_), channel_id=1, source_target_pairs={{0,1},{1,0},{2,3},{3,2},{4,5},{5,4},{6,7},{7,6},{8,9},{9,8},{10,11... | collective-permute-start | bytes 454664 | tf_op jit(solution)/shard_map/ppermute | solution.py:249
  222.1 2.7 %collective-permute-start.65 = (bf16[592,128]{1,0:T(8,128)(2,1)S(1)}, bf16[592,128]{1,0:T(8,128)(2,1)S(1)}, u32[]{:S(2)}, u32[]{:S(2)}) collective-permute-start(bf16[592,128]{1,0:T(8,128)(2,1)S(1)} %collective-permute-done.61.refs_3_), channel_id=1, source_target_pairs={{0,1},{1,0},{2,3},{3,2},{4,5},{5,4},{6,7},{7,6},{8,9},{9,8},{10,11... | collective-permute-start | bytes 454664 | tf_op jit(solution)/shard_map/ppermute | solution.py:249
  (9 other events, 44.2 us)
Sparse Core Ops, SparseCore 0:
  103.1 23.5 reduce-scatter.7
  129.6 20.9 reduce-scatter.5
  152.9 20.6 reduce-scatter.3
where the time goes:
time: 234 us; the launch traced here: 233 us
  waiting for transfers between devices  87 us (37%)
  Pallas kernels  63 us (27%)
  starting transfers between devices  62.8 us (27%)
  between operations  14.2 us (6%)
  local copies, waits for them, and re-layouts  4.79 us (2%)
    ppermute x66, waiting for transfers between devices, send(): return lax.ppermute(x, AXES, pairs)  86.9 us
    pallas_call x27, Pallas kernels, call(): pl.pallas_call(kernel, out_shape=shapes, in_specs=[pl.BlockSpec(memory_sp...  63 us
    ppermute x66, starting transfers between devices, send(): return lax.ppermute(x, AXES, pairs)  62.5 us
  transfers between devices with their start and end apart: 69, of which 32 were waited for; matrix products, arithmetic and copies ran while one was open for 3% of the time, Pallas kernels for 21%

commit v1 on v0

--- a/solution.py
+++ b/solution.py
@@ -315,12 +315,13 @@
 
 def spread_taps(grad, moved_ref, base, facts, cols):
     ch = grad.shape[0]
+    facts = facts[:4, :].astype(grad.dtype)
     for dx in (-1, 0, 1):
         column = shift(grad, -dx) * col_ok(facts, -dx) if dx else grad
         for dy in (-1, 0, 1):
             piece = shift(column, -dy * cols) * row_ok(facts, -dy) if dy else column
             at = base + ((dy + 1) * 3 + dx + 1) * ch
-            moved_ref[at : at + ch, :] = piece.astype(jnp.bfloat16)
+            moved_ref[at : at + ch, :] = piece
 
 
 def corner_sum(x, cols):
@@ -546,8 +547,13 @@
 
 
 def pick_kernel(layer, *refs):
-    sources, (out, sem) = refs[:4], refs[4:]
-    pick_layer(layer, sources, 0, out, sem.at[0]).wait()
+    sources, others, out, targets, sems = refs[:4], refs[4:-2], refs[-2], (), refs[-1]
+    if len(others) > 0:
+        others, out, targets = refs[4:5], refs[5], refs[6:7]
+    copies = [pick_layer(layer, sources, 0, out, sems.at[0])]
+    for other, target in zip(others, targets):
+        copies += start_all([pltpu.make_async_copy(other, target, sems.at[1])])
+    wait_all(copies)
 
 
 def forward_kernel(dims, layer, first, pooling, *refs):
@@ -668,24 +674,93 @@
     keep_sums(sums, shift_sum, slope_sum)
 
 
-def conv_back_kernel(dims, layer, own, other, own_weights, other_weights, facts, *refs):
-    outs, (moved, weights, sems) = refs[:4], refs[4:]
+def weight_product(moved, full, first):
+    if first:
+        return jnp.dot(moved, full, preferred_element_type=jnp.float32)
+    return lax.dot_general(moved, full, NT, preferred_element_type=jnp.float32)
+
+
+def sums_rows(sums, ch, width):
+    lines = []
+    for at in (0, LANES):
+        turned = sums[:, at : at + LANES].T
+        lines.append(jnp.concatenate([turned, jnp.zeros((LANES, width - ch), jnp.float32)], axis=1)[0:1])
+    lines.append(jnp.zeros((META_ROWS - 2, width), jnp.float32))
+    return jnp.concatenate(lines, axis=0).astype(jnp.bfloat16)
+
+
+def store_share(value, sums, pieces):
+    rows = value.shape[0]
+    width = pieces[0].shape[1]
+    for n, piece in enumerate(pieces):
+        piece[:rows, :] = value[:, n * width : (n + 1) * width].astype(jnp.bfloat16)
+        piece[rows:, :] = sums_rows(sums, rows // TAPS, width)
+
+
+def conv_back_kernel(dims, layer, own, other, own_weights, other_weights, full_in, sums, facts, *refs):
+    outs, shares, (product, moved, weights, full, sems) = refs[:4], refs[4:-5], refs[-5:]
     ch = own.shape[0]
+    size = moved.shape[0] // 2
     rows = pl.ds(layer * 4 * ch, 4 * ch)
     copies = start_all(
         [
-            pltpu.make_async_copy(own_weights.at[rows], weights.at[0], sems.at[0]),
-            pltpu.make_async_copy(other_weights.at[rows], weights.at[1], sems.at[1]),
+            pltpu.make_async_copy(own_weights.at[rows], weights.at[:, pl.ds(0, size)], sems.at[0]),
+            pltpu.make_async_copy(other_weights.at[rows], weights.at[:, pl.ds(size, size)], sems.at[1]),
         ]
     )
+    full_copy = pltpu.make_async_copy(full_in, full, sems.at[2])
+    full_copy.start()
     facts_now = facts[...]
-    spread_taps(own[...].astype(jnp.float32), moved.at[0], 0, facts_now, dims[1])
-    spread_taps(other[...].astype(jnp.float32), moved.at[1], 0, facts_now, dims[1])
+    spread_taps(own[...], moved, 0, facts_now, dims[1])
+    full_copy.wait()
+    value = weight_product(moved[: TAPS * ch, :], full[...], layer == 0)
+    if len(shares) == 1:
+        piece = product.shape[0] // 4
+        store_share(value, sums, [product.at[pl.ds(n * piece, piece)] for n in range(4)])
+        share_copy = pltpu.make_async_copy(product, shares[0], sems.at[3])
+        share_copy.start()
+    else:
+        _, plane, _ = place()
+        width = shares[0].shape[1]
+        product[...] = value.astype(jnp.bfloat16)
+        for k, share in enumerate(shares):
+            at = pl.multiple_of((plane ^ k) * width, width)
+            share[: TAPS * ch, :] = product[:, pl.ds(at, width)]
+            share[TAPS * ch :, :] = sums_rows(sums, ch, width)
+    spread_taps(other[...], moved, size, facts_now, dims[1])
+    for n in range(2):
+        moved[n * size + TAPS * ch : (n + 1) * size, :] = jnp.zeros(
+            (size - TAPS * ch, moved.shape[1]), jnp.bfloat16
+        )
     wait_all(copies)
-    value = jnp.dot(weights[0], moved[0], preferred_element_type=jnp.float32)
-    value = value + jnp.dot(weights[1], moved[1], preferred_element_type=jnp.float32)
+    value = jnp.dot(weights[...], moved[...], preferred_element_type=jnp.float32)
     for k, out in enumerate(outs):
         out[...] = value[k * ch : (k + 1) * ch, :].astype(jnp.bfloat16)
+    if len(shares) == 1:
+        share_copy.wait()
+
+
+def choose_kernel(*refs):
+    blocks, others, outs, sem = refs[:4], refs[4:-5], refs[-5:-1], refs[-1]
+    section, _, _ = place()
+    for layer, other in enumerate(others, 1):
+        for k, out in enumerate(outs):
+
+            @pl.when((section ^ k) == layer)
+            def _():
+                pltpu.make_async_copy(other, out, sem.at[k]).start()
+
+    value = add_blocks(blocks).astype(jnp.bfloat16)
+    for k, out in enumerate(outs):
+        copy = pltpu.make_async_copy(others[0], out, sem.at[k])
+
+        @pl.when((section ^ k) == 0)
+        def _():
+            out[...] = value
+
+        @pl.when((section ^ k) != 0)
+        def _():
+            copy.wait()
 
 
 def turn_weights_kernel(layers, *refs):
@@ -695,54 +770,17 @@
     half = channels // 2
     ch = half // 4
     copies = [pick_layer(n, sources, 0, full.at[n], sems.at[n]) for n in range(layers)]
+    stage[:, :, rows:] = jnp.zeros((*stage.shape[:2], stage.shape[2] - rows), jnp.bfloat16)
     for n in range(layers):
         copies[n].wait()
         turned[...] = full[n].T
         for j in range(2):
             for k in range(4):
                 at = pl.multiple_of((core ^ j) * half + (section ^ k) * ch, ch)
-                stage[j, n * half + k * ch : n * half + (k + 1) * ch, :] = turned[pl.ds(at, ch), :]
+                stage[j, n * half + k * ch : n * half + (k + 1) * ch, :rows] = turned[pl.ds(at, ch), :]
     wait_all(
         start_all([pltpu.make_async_copy(stage.at[j], outs[j], sems.at[j]) for j in range(2)])
     )
-
-
-def weight_kernel(dims, first, full_in, grad_pre, sums, facts, *refs):
-    outs, (full, moved, sems) = refs[:-3], refs[-3:]
-    copy = pltpu.make_async_copy(full_in, full, sems.at[0])
-    copy.start()
-    cols = dims[1]
-    ch = grad_pre.shape[0]
-    spread_taps(grad_pre[...].astype(jnp.float32), moved, 0, facts[...], cols)
-    copy.wait()
-    if first:
-        value = jnp.dot(moved[...], full[...], preferred_element_type=jnp.float32)
-    else:
-        value = lax.dot_general(moved[...], full[...], NT, preferred_element_type=jnp.float32)
-    width = outs[0].shape[1]
-    lines = []
-    for at in (0, LANES):
-        turned = sums[:, at : at + LANES].T
-        lines.append(jnp.concatenate([turned, jnp.zeros((LANES, width - ch), jnp.float32)], axis=1)[0:1])
-    sums_block = jnp.concatenate(lines + [jnp.zeros((META_ROWS - 2, width), jnp.float32)], axis=0)
-    if len(outs) == 1:
-        size = outs[0].shape[0] // 4
-        targets = [outs[0].at[pl.ds(n * size, size)] for n in range(4)]
-        for n, target in enumerate(targets):
-            target[: TAPS * ch, :] = value[:, n * width : (n + 1) * width].astype(jnp.bfloat16)
-            target[TAPS * ch :, :] = sums_block.astype(jnp.bfloat16)
-    else:
-        _, plane, _ = place()
-        for n in range(4):
-            piece = value[:, n * width : (n + 1) * width].astype(jnp.bfloat16)
-            for k, target in enumerate(outs):
-
-                @pl.when((plane ^ k) == n)
-                def _():
-                    target[: TAPS * ch, :] = piece
-
-        for target in outs:
-            target[TAPS * ch :, :] = sums_block.astype(jnp.bfloat16)
 
 
 def input_kernel(*refs):
@@ -825,7 +863,7 @@
 
 
 def plane_shards(images, image_group, group_size, conv_weight, bn_gain, bn_bias, cotangent):
-    section, _, core = place()
+    _, _, core = place()
     micro_total, _, rows, cols, channels = images.shape
     layers = lax.axis_size("section")
     last = layers - 1
@@ -838,6 +876,7 @@
     facts = grid_facts(frames, rows, cols)
     conv_flops = 2 * TAPS * ch * channels * length
     slice_rows = TAPS * ch + META_ROWS
+    tap_rows = -(-TAPS * ch // LANES) * LANES
 
     full_map = ((channels, length), bf16)
     full_frames = ((length, channels), bf16)
@@ -846,6 +885,8 @@
     map_out = ((ch, length), bf16)
     sums_out = ((ch, 2 * LANES), f32)
     kept_out = ((ch, length + LANES), f32)
+    share_out = ((4 * slice_rows, 2 * ch), bf16)
+    share_piece = ((slice_rows, 2 * ch), bf16)
 
     taps_first = conv_weight[0].transpose(1, 2, 0, 3).reshape(TAPS, channels, channels)
     packed = call(
@@ -906,24 +947,29 @@
     )
     kept, fulls = [normed], [full]
     for layer in range(1, layers):
-        (weight,) = call(
+        stored = [turned[1]] if layer == last else []
+        weight, *stored = call(
             partial(pick_kernel, layer),
-            [weight_slice],
+            [weight_slice] + [((layers * 4 * ch, tap_rows), bf16)] * len(stored),
             [],
-            after(slices, hidden),
+            [*after(slices, hidden), *after(stored, hidden)],
             "pick",
             held=range(4),
-            copies=1,
+            held_outs=(1,),
+            loose=(4,),
+            copies=2,
         )
+        if stored:
+            turned[1] = stored[0]
         beside = [weight]
         if layer == 1:
             turned = call(
                 partial(turn_weights_kernel, layers),
-                [((layers * 4 * ch, TAPS * ch), bf16)] * 2,
+                [((layers * 4 * ch, tap_rows), bf16)] * 2,
                 [
                     ((layers, TAPS * ch, channels), bf16),
                     ((channels, TAPS * ch), bf16),
-                    ((2, layers * 4 * ch, TAPS * ch), bf16),
+                    ((2, layers * 4 * ch, tap_rows), bf16),
                 ],
                 after(slices, hidden),
                 "turn_weights",
@@ -934,7 +980,9 @@
             beside.append(turned)
         if layer == 2:
             turned = [turned[0], to_core(after(turned[1], hidden))]
-        blocks = with_core(spread([hidden] * 4, to_section, beside))
+        blocks = [hidden] + [to_section(hidden, k) for k in (1, 2, 3)]
+        blocks[3] = after(blocks[3], *beside)
+        blocks = with_core(blocks)
         if layer < last:
             hidden, normed, full = call(
                 partial(forward_kernel, dims, layer, False, layer == CONVS - 1),
@@ -966,37 +1014,30 @@
     shares = [None] * layers
     same_core = [[2 * z + c for z in range(layers)] for c in range(2)]
     for layer in range(last, -1, -1):
-        first = layer == 0
-        pieces = call(
-            partial(weight_kernel, dims, first),
-            [((slice_rows, 2 * ch), bf16)] * 4 if first else [((4 * slice_rows, 2 * ch), bf16)],
-            [full_frames if first else full_map, ((TAPS * ch, length), bf16)],
-            [fulls[layer], grad_pre, sums, facts],
-            "weight_share",
-            held=(0,),
-            loose=(2, 3),
-            flops=conv_flops,
-            copies=1,
+        scattered = layer > 0
+        result = call(
+            partial(conv_back_kernel, dims, layer),
+            [map_out] * 4 + ([share_out] if scattered else [share_piece] * 4),
+            [
+                share_out if scattered else ((TAPS * ch, channels), bf16),
+                ((2 * tap_rows, length), bf16),
+                ((4 * ch, 2 * tap_rows), bf16),
+                full_map if layer else full_frames,
+            ],
+            [grad_pre, to_core(grad_pre), *turned, fulls[layer], sums, facts],
+            "conv_back",
+            held=(2, 3, 4),
+            held_outs=(4,) if scattered else (),
+            loose=(5, 6),
+            copies=4,
         )
-        if first:
-            moved = spread(pieces, to_plane)
-            shares[layer] = sum(x.astype(f32) for x in moved).astype(bf16)
+        parts = result[:4]
+        if scattered:
+            shares[layer] = lax.psum_scatter(
+                result[4], "dp", scatter_dimension=0, tiled=True, axis_index_groups=same_core
+            )
         else:
-            shares[layer] = lax.psum_scatter(
-                pieces[0], "dp", scatter_dimension=0, tiled=True, axis_index_groups=same_core
-            )
-        own, other = after((grad_pre, to_core(grad_pre)), pieces)
-        parts = call(
-            partial(conv_back_kernel, dims, layer),
-            [map_out] * 4,
-            [((2, TAPS * ch, length), bf16), ((2, 4 * ch, TAPS * ch), bf16)],
-            [own, other, *turned, facts],
-            "conv_back",
-            held=(2, 3),
-            loose=(4,),
-            flops=conv_flops,
-            copies=2,
-        )
+            shares[layer] = spread(result[4:], to_plane)
         if layer:
             held = call(
                 partial(fetch_kernel, layer - 1),
@@ -1039,7 +1080,16 @@
         last=True,
     )
 
-    chosen = [lax.select_n(section ^ k, *shares) for k in range(4)]
+    ready = shares[1:]
+    chosen = call(
+        choose_kernel,
+        [share_piece] * 4,
+        [],
+        [*shares[0], *ready],
+        "choose",
+        held=range(4, 4 + len(ready)),
+        copies=4,
+    )
     weight_grad, bias_grad, gain_grad = call(
         grads_out_kernel,
         [((TAPS, ch, channels), f32), ((1, ch), f32), ((1, ch), f32)],

time: 234 us -> 215 us (0.919)
  Pallas kernels: 63 us -> 51.9 us
  local copies, waits for them, and re-layouts: 4.79 us -> 0.01 us
  waiting for transfers between devices: 87 us -> 83.6 us
    pallas_call x27 -> x24, Pallas kernels: 63 us -> 51.9 us  [call(): pl.pallas_call(kernel, out_shape=shapes, in_specs=[pl.BlockSpec(memory_sp...]
    ppermute x66, waiting for transfers between devices: 86.9 us -> 83.5 us  [send(): return lax.ppermute(x, AXES, pairs)]
    ppermute x1 -> x0, local copies, waits for them, and re-layouts: 2.4 us -> none  [send(): return lax.ppermute(x, AXES, pairs)]
    optimization_barrier x1 -> x0, local copies, waits for them, and re-layouts: 2.37 us -> none  [after(): return lax.optimization_barrier((x, first))[0]]
  transfers between devices with their start and end apart: 69 -> 69, of which waited for: 32 -> 37; matrix products, arithmetic and copies ran while one was open for 3% -> 0% of each run, Pallas kernels for 21% -> 15%
where the time goes in v1:
time: 215 us; the launch traced here: 214 us
  waiting for transfers between devices  83.6 us (39%)
  starting transfers between devices  64.5 us (30%)
  Pallas kernels  51.9 us (24%)
  between operations  14.1 us (7%)
    ppermute x66, waiting for transfers between devices, send(): return lax.ppermute(x, AXES, pairs)  83.5 us
    ppermute x66, starting transfers between devices, send(): return lax.ppermute(x, AXES, pairs)  64.3 us
    pallas_call x24, Pallas kernels, call(): pl.pallas_call(kernel, out_shape=shapes, in_specs=[pl.BlockSpec(memory_sp...  51.9 us
  transfers between devices with their start and end apart: 69, of which 37 were waited for; matrix products, arithmetic and copies ran while one was open for 0% of the time, Pallas kernels for 15%

profile of v1, /device:TPU:0, one launch (start us, length us, event | category | flops | bytes accessed | tf_op | source)
XLA Modules:
  0.0 214.1 jit_solution(16812656551427497062)
XLA Ops:
  7.2 3.7 %weight_pack.1 = (bf16[592,512]{1,0:T(8,128)(2,1)}, bf16[592,512]{1,0:T(8,128)(2,1)S(1)}, bf16[592,512]{1,0:T(8,128)(2,1)S(1)}, bf16[592,512]{1,0:T(8,128)(2,1)S(1)}) custom-call(f32[1,512]{1,0:T(1,128)} %gain.1, f32[1,512]{1,0:T(1,128)} %bias.1, bf16[9,512,512]{2,1,0:T(8,128)(2,1)} %bitcast.16), custom_call_target="tpu_custom_call" | custom-call | bytes 7147520 | tf_op jit(solution)/shard_map/weight_pack/pallas_call | solution.py:853
  10.9 3.0 %collective-permute-start.7 = (bf16[592,512]{1,0:T(8,128)(2,1)S(1)}, bf16[592,512]{1,0:T(8,128)(2,1)}, u32[]{:S(2)}, u32[]{:S(2)}) collective-permute-start(bf16[592,512]{1,0:T(8,128)(2,1)S(1)} %get-tuple-element.130), channel_id=1, source_target_pairs={{0,8},{1,9},{2,10},{3,11},{4,12},{5,13},{6,14},{7,15},{8,0},{9,1},... | collective-permute-start | bytes 1818632 | tf_op jit(solution)/shard_map/ppermute | solution.py:249
  14.0 1.5 collective-permute-start.8
  15.5 1.8 frames.1
  17.3 1.6 collective-permute-start
  19.4 2.6 %collective-permute-start.1 = (bf16[208,640]{1,0:T(8,128)(2,1)S(1)}, bf16[208,640]{1,0:T(8,128)(2,1)S(1)}, u32[]{:S(2)}, u32[]{:S(2)}) collective-permute-start(bf16[208,640]{1,0:T(8,128)(2,1)S(1)} %get-tuple-element.136), channel_id=1, source_target_pairs={{0,4},{1,5},{2,6},{3,7},{4,0},{5,1},{6,2},{7,3},{8,12},{9,13},{10,... | collective-permute-start | bytes 798728 | tf_op jit(solution)/shard_map/ppermute | solution.py:249
  22.0 8.4 %collective-permute-done.refs_1_ = bf16[208,640]{1,0:T(8,128)(2,1)S(1)} collective-permute-done((bf16[208,640]{1,0:T(8,128)(2,1)S(1)}, bf16[208,640]{1,0:T(8,128)(2,1)S(1)}, u32[]{:S(2)}, u32[]{:S(2)}) %collective-permute-start) | collective-permute-done | bytes 266272 | tf_op jit(solution)/shard_map/ppermute | solution.py:249
  30.4 2.5 %collective-permute-start.2 = (bf16[208,640]{1,0:T(8,128)(2,1)S(1)}, bf16[208,640]{1,0:T(8,128)(2,1)S(1)}, u32[]{:S(2)}, u32[]{:S(2)}) collective-permute-start(bf16[208,640]{1,0:T(8,128)(2,1)S(1)} %get-tuple-element.137), channel_id=1, source_target_pairs={{0,6},{1,7},{2,4},{3,5},{4,2},{5,3},{6,0},{7,1},{8,14},{9,15},{10,... | collective-permute-start | bytes 798728 | tf_op jit(solution)/shard_map/ppermute | solution.py:249
  32.8 6.2 %collective-permute-done.1.refs_2_ = bf16[208,640]{1,0:T(8,128)(2,1)S(1)} collective-permute-done((bf16[208,640]{1,0:T(8,128)(2,1)S(1)}, bf16[208,640]{1,0:T(8,128)(2,1)S(1)}, u32[]{:S(2)}, u32[]{:S(2)}) %collective-permute-start.1) | collective-permute-done | bytes 266272 | tf_op jit(solution)/shard_map/ppermute | solution.py:249
  39.6 2.6 %collective-permute-done.8.refs_10_.refs_2_ = bf16[592,512]{1,0:T(8,128)(2,1)} collective-permute-done((bf16[592,512]{1,0:T(8,128)(2,1)S(1)}, bf16[592,512]{1,0:T(8,128)(2,1)}, u32[]{:S(2)}, u32[]{:S(2)}) %collective-permute-start.8) | collective-permute-done | bytes 606240 | tf_op jit(solution)/shard_map/ppermute | solution.py:249
  42.4 1.4 collective-permute-done.6.refs_7_
  43.8 3.8 %forward.3 = (bf16[64,1536]{1,0:T(8,128)(2,1)S(1)}, f32[64,1664]{1,0:T(8,128)}, bf16[1536,512]{1,0:T(8,128)(2,1)}, f32[1,1536]{1,0:T(1,128)S(1)}, bf16[64,1536]{1,0:T(8,128)(2,1)}) custom-call(bf16[208,640]{1,0:T(8,128)(2,1)S(1)} %get-tuple-element.134.refs_0_, bf16[208,640]{1,0:T(8,128)(2,1)S(1)} %collective-permute-done.refs_1_, ...), custom_call_target="tpu_custom_call" | custom-call | flops 905969664 | bytes 7067648 | tf_op jit(solution)/shard_map/forward/pallas_call | solution.py:853
  47.6 2.2 %collective-permute-start.12 = (bf16[64,1536]{1,0:T(8,128)(2,1)S(1)}, bf16[64,1536]{1,0:T(8,128)(2,1)S(1)}, u32[]{:S(2)}, u32[]{:S(2)}) collective-permute-start(bf16[64,1536]{1,0:T(8,128)(2,1)S(1)} %get-tuple-element.144.refs_0_), channel_id=1, source_target_pairs={{0,24},{1,25},{2,26},{3,27},{4,28},{5,29},{6,30},{7,31},{8,16},{9,... | collective-permute-start | bytes 589832 | tf_op jit(solution)/shard_map/ppermute | solution.py:249
  49.8 1.3 collective-permute-start.10
  52.2 3.8 %turn_weights.1 = (bf16[1024,640]{1,0:T(8,128)(2,1)}, bf16[1024,640]{1,0:T(8,128)(2,1)}) custom-call(bf16[592,512]{1,0:T(8,128)(2,1)} %get-tuple-element.160.refs_8_.refs_0_, bf16[592,512]{1,0:T(8,128)(2,1)} %collective-permute-done.7.refs_9_.refs_1_, bf16[592,512]{1,0:T(8,128)(2,1)} %collective-permute-done.8.refs_10_.refs_2_, ...), custom_call_target="tpu_custom_call" | custom-call | bytes 5046272 | tf_op jit(solution)/shard_map/turn_weights/pallas_call | solution.py:853
  56.3 3.4 %collective-permute-done.11.refs_2_ = bf16[64,1536]{1,0:T(8,128)(2,1)S(1)} collective-permute-done((bf16[64,1536]{1,0:T(8,128)(2,1)S(1)}, bf16[64,1536]{1,0:T(8,128)(2,1)S(1)}, u32[]{:S(2)}, u32[]{:S(2)}) %collective-permute-start.11) | collective-permute-done | bytes 196640 | tf_op jit(solution)/shard_map/ppermute | solution.py:249
  61.7 3.1 %forward.4 = (bf16[64,1536]{1,0:T(8,128)(2,1)S(1)}, f32[64,1664]{1,0:T(8,128)}, bf16[512,1536]{1,0:T(8,128)(2,1)}) custom-call(bf16[64,1536]{1,0:T(8,128)(2,1)S(1)} %get-tuple-element.144.refs_0_, bf16[64,1536]{1,0:T(8,128)(2,1)S(1)} %collective-permute-done.10.refs_1_, bf16[64,1536]{1,0:T(8,128)(2,1)S(1)} %collective-permute-done.11.refs_2_, ...), custom_call_target="tpu_custom_call" | custom-call | flops 905969664 | bytes 4478976 | tf_op jit(solution)/shard_map/forward/pallas_call | solution.py:853
  65.1 1.7 collective-permute-start.19
  69.7 4.1 %collective-permute-done.19.refs_3_ = bf16[64,1536]{1,0:T(8,128)(2,1)S(1)} collective-permute-done((bf16[64,1536]{1,0:T(8,128)(2,1)S(1)}, bf16[64,1536]{1,0:T(8,128)(2,1)S(1)}, u32[]{:S(2)}, u32[]{:S(2)}) %collective-permute-start.19) | collective-permute-done | bytes 196640 | tf_op jit(solution)/shard_map/ppermute | solution.py:249
  73.8 3.5 %collective-permute-done.18.refs_2_ = bf16[64,1536]{1,0:T(8,128)(2,1)S(1)} collective-permute-done((bf16[64,1536]{1,0:T(8,128)(2,1)S(1)}, bf16[64,1536]{1,0:T(8,128)(2,1)S(1)}, u32[]{:S(2)}, u32[]{:S(2)}) %collective-permute-start.18) | collective-permute-done | bytes 196640 | tf_op jit(solution)/shard_map/ppermute | solution.py:249
  79.3 2.4 %forward.5 = (bf16[64,1536]{1,0:T(8,128)(2,1)S(1)}, f32[64,1664]{1,0:T(8,128)}, bf16[512,1536]{1,0:T(8,128)(2,1)}) custom-call(bf16[64,1536]{1,0:T(8,128)(2,1)S(1)} %get-tuple-element.153.refs_0_, bf16[64,1536]{1,0:T(8,128)(2,1)S(1)} %collective-permute-done.17.refs_1_, bf16[64,1536]{1,0:T(8,128)(2,1)S(1)} %collective-permute-done.18.refs_2_, ...), custom_call_target="tpu_custom_call" | custom-call | flops 905969664 | bytes 4478976 | tf_op jit(solution)/shard_map/forward/pallas_call | solution.py:853
  81.7 1.3 collective-permute-start.25
  84.1 1.2 collective-permute-start.26
  85.3 3.5 %collective-permute-done.25.refs_2_ = bf16[64,1536]{1,0:T(8,128)(2,1)S(1)} collective-permute-done((bf16[64,1536]{1,0:T(8,128)(2,1)S(1)}, bf16[64,1536]{1,0:T(8,128)(2,1)S(1)}, u32[]{:S(2)}, u32[]{:S(2)}) %collective-permute-start.25) | collective-permute-done | bytes 196640 | tf_op jit(solution)/shard_map/ppermute | solution.py:249
  88.8 1.9 collective-permute-done.24.refs_1_
  90.8 1.5 pick.5
  92.3 2.0 collective-permute-done.26.refs_3_
  94.2 1.4 collective-permute-done.31.refs_7_
  95.7 2.4 %turn.1 = (bf16[64,1536]{1,0:T(8,128)(2,1)}, bf16[512,1536]{1,0:T(8,128)(2,1)}, bf16[64,1536]{1,0:T(8,128)(2,1)S(1)}, f32[64,256]{1,0:T(8,128)S(1)}) custom-call(bf16[64,1536]{1,0:T(8,128)(2,1)S(1)} %get-tuple-element.159.refs_0_, bf16[64,1536]{1,0:T(8,128)(2,1)S(1)} %collective-permute-done.24.refs_1_, ...), custom_call_target="tpu_custom_call" | custom-call | flops 905969664 | bytes 4511744 | tf_op jit(solution)/shard_map/turn/pallas_call | solution.py:853
  98.3 1.3 collective-permute-done.32.other
  99.6 4.0 %conv_back.4 = (bf16[64,1536]{1,0:T(8,128)(2,1)S(1)}, bf16[64,1536]{1,0:T(8,128)(2,1)S(1)}, bf16[64,1536]{1,0:T(8,128)(2,1)S(1)}, bf16[64,1536]{1,0:T(8,128)(2,1)S(1)}, bf16[2368,128]{1,0:T(8,128)(2,1)}) custom-call(bf16[64,1536]{1,0:T(8,128)(2,1)S(1)} %get-tuple-element.169.own, bf16[64,1536]{1,0:T(8,128)(2,1)S(1)} %collective-permute-done.32.other, ...), custom_call_target="tpu_custom_call" | custom-call | bytes 6144000 | tf_op jit(solution)/shard_map/conv_back/pallas_call | solution.py:853
  104.6 1.4 collective-permute-start.34
  106.0 1.2 collective-permute-start.35
  108.2 3.2 %collective-permute-done.33.refs_1_ = bf16[64,1536]{1,0:T(8,128)(2,1)S(1)} collective-permute-done((bf16[64,1536]{1,0:T(8,128)(2,1)S(1)}, bf16[64,1536]{1,0:T(8,128)(2,1)S(1)}, u32[]{:S(2)}, u32[]{:S(2)}) %collective-permute-start.33) | collective-permute-done | bytes 196640 | tf_op jit(solution)/shard_map/ppermute | solution.py:249
  111.4 3.0 %collective-permute-done.34.refs_2_ = bf16[64,1536]{1,0:T(8,128)(2,1)S(1)} collective-permute-done((bf16[64,1536]{1,0:T(8,128)(2,1)S(1)}, bf16[64,1536]{1,0:T(8,128)(2,1)S(1)}, u32[]{:S(2)}, u32[]{:S(2)}) %collective-permute-start.34) | collective-permute-done | bytes 196640 | tf_op jit(solution)/shard_map/ppermute | solution.py:249
  116.1 1.4 collective-permute-done.36.other
  117.6 4.0 %conv_back.5 = (bf16[64,1536]{1,0:T(8,128)(2,1)S(1)}, bf16[64,1536]{1,0:T(8,128)(2,1)S(1)}, bf16[64,1536]{1,0:T(8,128)(2,1)S(1)}, bf16[64,1536]{1,0:T(8,128)(2,1)S(1)}, bf16[2368,128]{1,0:T(8,128)(2,1)}) custom-call(bf16[64,1536]{1,0:T(8,128)(2,1)S(1)} %get-tuple-element.184.own, bf16[64,1536]{1,0:T(8,128)(2,1)S(1)} %collective-permute-done.36.other, ...), custom_call_target="tpu_custom_call" | custom-call | bytes 6144000 | tf_op jit(solution)/shard_map/conv_back/pallas_call | solution.py:853
  122.8 1.2 collective-permute-start.38
  124.0 1.2 collective-permute-start.39
  126.2 3.2 %collective-permute-done.37.refs_1_ = bf16[64,1536]{1,0:T(8,128)(2,1)S(1)} collective-permute-done((bf16[64,1536]{1,0:T(8,128)(2,1)S(1)}, bf16[64,1536]{1,0:T(8,128)(2,1)S(1)}, u32[]{:S(2)}, u32[]{:S(2)}) %collective-permute-start.37) | collective-permute-done | bytes 196640 | tf_op jit(solution)/shard_map/ppermute | solution.py:249
  129.4 2.9 %collective-permute-done.38.refs_2_ = bf16[64,1536]{1,0:T(8,128)(2,1)S(1)} collective-permute-done((bf16[64,1536]{1,0:T(8,128)(2,1)S(1)}, bf16[64,1536]{1,0:T(8,128)(2,1)S(1)}, u32[]{:S(2)}, u32[]{:S(2)}) %collective-permute-start.38) | collective-permute-done | bytes 196640 | tf_op jit(solution)/shard_map/ppermute | solution.py:249
  132.4 1.3 collective-permute-done.39.refs_3_
  133.6 2.1 norm_back.4
  135.8 1.4 collective-permute-done.40.other
  137.2 4.0 %conv_back.6 = (bf16[64,1536]{1,0:T(8,128)(2,1)S(1)}, bf16[64,1536]{1,0:T(8,128)(2,1)S(1)}, bf16[64,1536]{1,0:T(8,128)(2,1)S(1)}, bf16[64,1536]{1,0:T(8,128)(2,1)S(1)}, bf16[2368,128]{1,0:T(8,128)(2,1)}) custom-call(bf16[64,1536]{1,0:T(8,128)(2,1)S(1)} %get-tuple-element.198.own, bf16[64,1536]{1,0:T(8,128)(2,1)S(1)} %collective-permute-done.40.other, ...), custom_call_target="tpu_custom_call" | custom-call | bytes 6144000 | tf_op jit(solution)/shard_map/conv_back/pallas_call | solution.py:853
  142.3 1.3 collective-permute-start.42
  143.6 1.2 collective-permute-start.43
  145.8 3.2 %collective-permute-done.41.refs_1_ = bf16[64,1536]{1,0:T(8,128)(2,1)S(1)} collective-permute-done((bf16[64,1536]{1,0:T(8,128)(2,1)S(1)}, bf16[64,1536]{1,0:T(8,128)(2,1)S(1)}, u32[]{:S(2)}, u32[]{:S(2)}) %collective-permute-start.41) | collective-permute-done | bytes 196640 | tf_op jit(solution)/shard_map/ppermute | solution.py:249
  149.1 3.0 %collective-permute-done.42.refs_2_ = bf16[64,1536]{1,0:T(8,128)(2,1)S(1)} collective-permute-done((bf16[64,1536]{1,0:T(8,128)(2,1)S(1)}, bf16[64,1536]{1,0:T(8,128)(2,1)S(1)}, u32[]{:S(2)}, u32[]{:S(2)}) %collective-permute-start.42) | collective-permute-done | bytes 196640 | tf_op jit(solution)/shard_map/ppermute | solution.py:249
  153.8 1.4 collective-permute-done.44.other
  155.2 4.0 %conv_back.7 = (bf16[64,1536]{1,0:T(8,128)(2,1)S(1)}, bf16[64,1536]{1,0:T(8,128)(2,1)S(1)}, bf16[64,1536]{1,0:T(8,128)(2,1)S(1)}, bf16[64,1536]{1,0:T(8,128)(2,1...) custom-call(bf16[64,1536]{1,0:T(8,128)(2,1)S(1)} %get-tuple-element., ...), custom_call_target="tpu_custom_call" | custom-call | bytes 6144000 | tf_op jit(solution)/shard_map/conv_back/pallas_call | solution.py:853
  160.4 1.2 collective-permute-start.46
  161.6 1.2 collective-permute-start.47
  162.8 4.2 %collective-permute-start.56 = (bf16[592,128]{1,0:T(8,128)(2,1)S(1)}, bf16[592,128]{1,0:T(8,128)(2,1)S(1)}, u32[]{:S(2)}, u32[]{:S(2)}) collective-permute-start(bf16[592,128]{1,0:T(8,128)(2,1)S(1)} %get-tuple-element.234), channel_id=1, source_target_pairs={{0,2},{1,3},{2,0},{3,1},{4,6},{5,7},{6,4},{7,5},{8,10},{9,11},{10,... | collective-permute-start | bytes 454664 | tf_op jit(solution)/shard_map/ppermute | solution.py:249
  168.0 2.1 collective-permute-start.58
  170.1 1.2 collective-permute-done.47.refs_3_
  172.9 4.9 %collective-permute-start.49 = (bf16[128,384]{1,0:T(8,128)(2,1)S(1)}, bf16[128,384]{1,0:T(8,128)(2,1)S(1)}, u32[]{:S(2)}, u32[]{:S(2)}) collective-permute-start(bf16[128,384]{1,0:T(8,128)(2,1)S(1)} %get-tuple-element.224), channel_id=1, source_target_pairs={{0,2},{1,3},{2,10},{3,11},{4,18},{5,19},{6,26},{7,27},{8,0},{9,1},... | collective-permute-start | bytes 294920 | tf_op jit(solution)/shard_map/ppermute | solution.py:249
  177.8 8.1 %collective-permute-done.57.refs_2_ = bf16[592,128]{1,0:T(8,128)(2,1)S(1)} collective-permute-done((bf16[592,128]{1,0:T(8,128)(2,1)S(1)}, bf16[592,128]{1,0:T(8,128)(2,1)S(1)}, u32[]{:S(2)}, u32[]{:S(2)}) %collective-permute-start.57) | collective-permute-done | bytes 151584 | tf_op jit(solution)/shard_map/ppermute | solution.py:249
  185.9 2.8 %collective-permute-start.50 = (bf16[128,384]{1,0:T(8,128)(2,1)S(1)}, bf16[128,384]{1,0:T(8,128)(2,1)S(1)}, u32[]{:S(2)}, u32[]{:S(2)}) collective-permute-start(bf16[128,384]{1,0:T(8,128)(2,1)S(1)} %get-tuple-element.225), channel_id=1, source_target_pairs={{0,4},{1,5},{2,12},{3,13},{4,20},{5,21},{6,28},{7,29},{8,6},{9,7},... | collective-permute-start | bytes 294920 | tf_op jit(solution)/shard_map/ppermute | solution.py:249
  188.7 4.7 %collective-permute-start.51 = (bf16[128,384]{1,0:T(8,128)(2,1)S(1)}, bf16[128,384]{1,0:T(8,128)(2,1)S(1)}, u32[]{:S(2)}, u32[]{:S(2)}) collective-permute-start(bf16[128,384]{1,0:T(8,128)(2,1)S(1)} %get-tuple-element.226), channel_id=1, source_target_pairs={{0,6},{1,7},{2,14},{3,15},{4,22},{5,23},{6,30},{7,31},{8,4},{9,5},... | collective-permute-start | bytes 294920 | tf_op jit(solution)/shard_map/ppermute | solution.py:249
  194.7 3.4 %collective-permute-start.61 = (bf16[592,128]{1,0:T(8,128)(2,1)S(1)}, bf16[592,128]{1,0:T(8,128)(2,1)S(1)}, u32[]{:S(2)}, u32[]{:S(2)}) collective-permute-start(bf16[592,128]{1,0:T(8,128)(2,1)S(1)} %get-tuple-element.246), channel_id=1, source_target_pairs={{0,24},{1,25},{2,26},{3,27},{4,28},{5,29},{6,30},{7,31},{8,16},{9,... | collective-permute-start | bytes 454664 | tf_op jit(solution)/shard_map/ppermute | solution.py:249
  199.8 2.5 %collective-permute-done.60.refs_2_ = bf16[592,128]{1,0:T(8,128)(2,1)S(1)} collective-permute-done((bf16[592,128]{1,0:T(8,128)(2,1)S(1)}, bf16[592,128]{1,0:T(8,128)(2,1)S(1)}, u32[]{:S(2)}, u32[]{:S(2)}) %collective-permute-start.60) | collective-permute-done | bytes 151584 | tf_op jit(solution)/shard_map/ppermute | solution.py:249
  203.4 1.2 collective-permute-done.55.refs_7_
  205.8 1.9 grads_out.1
  (107 shorter events, 29.9 us)
Async XLA Ops:
  7.2 186.2 %reduce-scatter.8.cloned.1.call-start = ((), (), s32[]{:S(2)}) async-start(), calls=%async_computation.5 | async-start | bytes 757760 | tf_op jit(solution)/shard_map/reduce_scatter | solution.py:1036
  10.9 28.6 %collective-permute-start.7 = (bf16[592,512]{1,0:T(8,128)(2,1)S(1)}, bf16[592,512]{1,0:T(8,128)(2,1)}, u32[]{:S(2)}, u32[]{:S(2)}) collective-permute-start(bf16[592,512]{1,0:T(8,128)(2,1)S(1)} %get-tuple-element.130), channel_id=1, source_target_pairs={{0,8},{1,9},{2,10},{3,11},{4,12},{5,13},{6,14},{7,15},{8,0},{9,1},... | collective-permute-start | bytes 1818632 | tf_op jit(solution)/shard_map/ppermute | solution.py:249
  14.0 28.3 %collective-permute-start.8 = (bf16[592,512]{1,0:T(8,128)(2,1)S(1)}, bf16[592,512]{1,0:T(8,128)(2,1)}, u32[]{:S(2)}, u32[]{:S(2)}) collective-permute-start(bf16[592,512]{1,0:T(8,128)(2,1)S(1)} %get-tuple-element.131), channel_id=1, source_target_pairs={{0,16},{1,17},{2,18},{3,19},{4,20},{5,21},{6,22},{7,23},{8,24},{9,... | collective-permute-start | bytes 1818632 | tf_op jit(solution)/shard_map/ppermute | solution.py:249
  17.3 13.1 %collective-permute-start = (bf16[208,640]{1,0:T(8,128)(2,1)S(1)}, bf16[208,640]{1,0:T(8,128)(2,1)S(1)}, u32[]{:S(2)}, u32[]{:S(2)}) collective-permute-start(bf16[208,640]{1,0:T(8,128)(2,1)S(1)} %get-tuple-element.135), channel_id=1, source_target_pairs={{0,2},{1,3},{2,0},{3,1},{4,6},{5,7},{6,4},{7,5},{8,10},{9,11},{10,... | collective-permute-start | bytes 798728 | tf_op jit(solution)/shard_map/ppermute | solution.py:249
  18.9 23.4 %collective-permute-start.9 = (bf16[592,512]{1,0:T(8,128)(2,1)S(1)}, bf16[592,512]{1,0:T(8,128)(2,1)}, u32[]{:S(2)}, u32[]{:S(2)}) collective-permute-start(bf16[592,512]{1,0:T(8,128)(2,1)S(1)} %get-tuple-element.132), channel_id=1, source_target_pairs={{0,24},{1,25},{2,26},{3,27},{4,28},{5,29},{6,30},{7,31},{8,16},{9,... | collective-permute-start | bytes 1818632 | tf_op jit(solution)/shard_map/ppermute | solution.py:249
  19.4 19.6 %collective-permute-start.1 = (bf16[208,640]{1,0:T(8,128)(2,1)S(1)}, bf16[208,640]{1,0:T(8,128)(2,1)S(1)}, u32[]{:S(2)}, u32[]{:S(2)}) collective-permute-start(bf16[208,640]{1,0:T(8,128)(2,1)S(1)} %get-tuple-element.136), channel_id=1, source_target_pairs={{0,4},{1,5},{2,6},{3,7},{4,0},{5,1},{6,2},{7,3},{8,12},{9,13},{10,... | collective-permute-start | bytes 798728 | tf_op jit(solution)/shard_map/ppermute | solution.py:249
  30.4 8.6 %collective-permute-start.2 = (bf16[208,640]{1,0:T(8,128)(2,1)S(1)}, bf16[208,640]{1,0:T(8,128)(2,1)S(1)}, u32[]{:S(2)}, u32[]{:S(2)}) collective-permute-start(bf16[208,640]{1,0:T(8,128)(2,1)S(1)} %get-tuple-element.137), channel_id=1, source_target_pairs={{0,6},{1,7},{2,4},{3,5},{4,2},{5,3},{6,0},{7,1},{8,14},{9,15},{10,... | collective-permute-start | bytes 798728 | tf_op jit(solution)/shard_map/ppermute | solution.py:249
  39.0 3.3 %collective-permute-start.3 = (bf16[208,640]{1,0:T(8,128)(2,1)S(1)}, bf16[208,640]{1,0:T(8,128)(2,1)S(1)}, u32[]{:S(2)}, u32[]{:S(2)}) collective-permute-start(bf16[208,640]{1,0:T(8,128)(2,1)S(1)} %get-tuple-element.134.refs_0_), channel_id=1, source_target_pairs={{0,1},{1,0},{2,3},{3,2},{4,5},{5,4},{6,7},{7,6},{8,9},{9,8},{10,11... | collective-permute-start | bytes 798728 | tf_op jit(solution)/shard_map/ppermute | solution.py:249
  39.0 3.3 %collective-permute-start.4 = (bf16[208,640]{1,0:T(8,128)(2,1)S(1)}, bf16[208,640]{1,0:T(8,128)(2,1)S(1)}, u32[]{:S(2)}, u32[]{:S(2)}) collective-permute-start(bf16[208,640]{1,0:T(8,128)(2,1)S(1)} %collective-permute-done.refs_1_), channel_id=1, source_target_pairs={{0,1},{1,0},{2,3},{3,2},{4,5},{5,4},{6,7},{7,6},{8,9},{9,8},{10,11... | collective-permute-start | bytes 798728 | tf_op jit(solution)/shard_map/ppermute | solution.py:249
  39.5 2.8 %collective-permute-start.5 = (bf16[208,640]{1,0:T(8,128)(2,1)S(1)}, bf16[208,640]{1,0:T(8,128)(2,1)S(1)}, u32[]{:S(2)}, u32[]{:S(2)}) collective-permute-start(bf16[208,640]{1,0:T(8,128)(2,1)S(1)} %collective-permute-done.1.refs_2_), channel_id=1, source_target_pairs={{0,1},{1,0},{2,3},{3,2},{4,5},{5,4},{6,7},{7,6},{8,9},{9,8},{10,11... | collective-permute-start | bytes 798728 | tf_op jit(solution)/shard_map/ppermute | solution.py:249
  42.2 1.5 collective-permute-start.6
  47.6 8.8 %collective-permute-start.12 = (bf16[64,1536]{1,0:T(8,128)(2,1)S(1)}, bf16[64,1536]{1,0:T(8,128)(2,1)S(1)}, u32[]{:S(2)}, u32[]{:S(2)}) collective-permute-start(bf16[64,1536]{1,0:T(8,128)(2,1)S(1)} %get-tuple-element.144.refs_0_), channel_id=1, source_target_pairs={{0,24},{1,25},{2,26},{3,27},{4,28},{5,29},{6,30},{7,31},{8,16},{9,... | collective-permute-start | bytes 589832 | tf_op jit(solution)/shard_map/ppermute | solution.py:249
  49.7 10.0 %collective-permute-start.11 = (bf16[64,1536]{1,0:T(8,128)(2,1)S(1)}, bf16[64,1536]{1,0:T(8,128)(2,1)S(1)}, u32[]{:S(2)}, u32[]{:S(2)}) collective-permute-start(bf16[64,1536]{1,0:T(8,128)(2,1)S(1)} %get-tuple-element.144.refs_0_), channel_id=1, source_target_pairs={{0,16},{1,17},{2,18},{3,19},{4,20},{5,21},{6,22},{7,23},{8,24},{9,... | collective-permute-start | bytes 589832 | tf_op jit(solution)/shard_map/ppermute | solution.py:249
  49.8 10.0 %collective-permute-start.10 = (bf16[64,1536]{1,0:T(8,128)(2,1)S(1)}, bf16[64,1536]{1,0:T(8,128)(2,1)S(1)}, u32[]{:S(2)}, u32[]{:S(2)}) collective-permute-start(bf16[64,1536]{1,0:T(8,128)(2,1)S(1)} %get-tuple-element.144.refs_0_), channel_id=1, source_target_pairs={{0,8},{1,9},{2,10},{3,11},{4,12},{5,13},{6,14},{7,15},{8,0},{9,1},... | collective-permute-start | bytes 589832 | tf_op jit(solution)/shard_map/ppermute | solution.py:249
  51.1 9.2 %collective-permute-start.13 = (bf16[64,1536]{1,0:T(8,128)(2,1)S(1)}, bf16[64,1536]{1,0:T(8,128)(2,1)S(1)}, u32[]{:S(2)}, u32[]{:S(2)}) collective-permute-start(bf16[64,1536]{1,0:T(8,128)(2,1)S(1)} %get-tuple-element.144.refs_0_), channel_id=1, source_target_pairs={{0,1},{1,0},{2,3},{3,2},{4,5},{5,4},{6,7},{7,6},{8,9},{9,8},{10,11... | collective-permute-start | bytes 589832 | tf_op jit(solution)/shard_map/ppermute | solution.py:249
  59.8 1.6 collective-permute-start.14
  60.2 1.5 collective-permute-start.16
  64.8 26.0 %collective-permute-start.27 = (bf16[1024,640]{1,0:T(8,128)(2,1)S(1)}, bf16[1024,640]{1,0:T(8,128)(2,1)S(1)}, u32[]{:S(2)}, u32[]{:S(2)}) collective-permute-start(bf16[1024,640]{1,0:T(8,128)(2,1)S(1)} %copy-done.1), channel_id=1, source_target_pairs={{0,1},{1,0},{2,3},{3,2},{4,5},{5,4},{6,7},{7,6},{8,9},{9,8},{10,11... | collective-permute-start | bytes 3932168 | tf_op jit(solution)/shard_map/ppermute | solution.py:249
  65.1 8.7 %collective-permute-start.19 = (bf16[64,1536]{1,0:T(8,128)(2,1)S(1)}, bf16[64,1536]{1,0:T(8,128)(2,1)S(1)}, u32[]{:S(2)}, u32[]{:S(2)}) collective-permute-start(bf16[64,1536]{1,0:T(8,128)(2,1)S(1)} %get-tuple-element.153.refs_0_), channel_id=1, source_target_pairs={{0,24},{1,25},{2,26},{3,27},{4,28},{5,29},{6,30},{7,31},{8,16},{9,... | collective-permute-start | bytes 589832 | tf_op jit(solution)/shard_map/ppermute | solution.py:249
  66.8 10.4 %collective-permute-start.18 = (bf16[64,1536]{1,0:T(8,128)(2,1)S(1)}, bf16[64,1536]{1,0:T(8,128)(2,1)S(1)}, u32[]{:S(2)}, u32[]{:S(2)}) collective-permute-start(bf16[64,1536]{1,0:T(8,128)(2,1)S(1)} %get-tuple-element.153.refs_0_), channel_id=1, source_target_pairs={{0,16},{1,17},{2,18},{3,19},{4,20},{5,21},{6,22},{7,23},{8,24},{9,... | collective-permute-start | bytes 589832 | tf_op jit(solution)/shard_map/ppermute | solution.py:249
  67.5 9.8 %collective-permute-start.17 = (bf16[64,1536]{1,0:T(8,128)(2,1)S(1)}, bf16[64,1536]{1,0:T(8,128)(2,1)S(1)}, u32[]{:S(2)}, u32[]{:S(2)}) collective-permute-start(bf16[64,1536]{1,0:T(8,128)(2,1)S(1)} %get-tuple-element.153.refs_0_), channel_id=1, source_target_pairs={{0,8},{1,9},{2,10},{3,11},{4,12},{5,13},{6,14},{7,15},{8,0},{9,1},... | collective-permute-start | bytes 589832 | tf_op jit(solution)/shard_map/ppermute | solution.py:249
  68.6 9.2 %collective-permute-start.20 = (bf16[64,1536]{1,0:T(8,128)(2,1)S(1)}, bf16[64,1536]{1,0:T(8,128)(2,1)S(1)}, u32[]{:S(2)}, u32[]{:S(2)}) collective-permute-start(bf16[64,1536]{1,0:T(8,128)(2,1)S(1)} %get-tuple-element.153.refs_0_), channel_id=1, source_target_pairs={{0,1},{1,0},{2,3},{3,2},{4,5},{5,4},{6,7},{7,6},{8,9},{9,8},{10,11... | collective-permute-start | bytes 589832 | tf_op jit(solution)/shard_map/ppermute | solution.py:249
  77.3 1.7 collective-permute-start.21
  81.7 7.1 %collective-permute-start.25 = (bf16[64,1536]{1,0:T(8,128)(2,1)S(1)}, bf16[64,1536]{1,0:T(8,128)(2,1)S(1)}, u32[]{:S(2)}, u32[]{:S(2)}) collective-permute-start(bf16[64,1536]{1,0:T(8,128)(2,1)S(1)} %get-tuple-element.159.refs_0_), channel_id=1, source_target_pairs={{0,16},{1,17},{2,18},{3,19},{4,20},{5,21},{6,22},{7,23},{8,24},{9,... | collective-permute-start | bytes 589832 | tf_op jit(solution)/shard_map/ppermute | solution.py:249
  83.0 7.8 %collective-permute-start.24 = (bf16[64,1536]{1,0:T(8,128)(2,1)S(1)}, bf16[64,1536]{1,0:T(8,128)(2,1)S(1)}, u32[]{:S(2)}, u32[]{:S(2)}) collective-permute-start(bf16[64,1536]{1,0:T(8,128)(2,1)S(1)} %get-tuple-element.159.refs_0_), channel_id=1, source_target_pairs={{0,8},{1,9},{2,10},{3,11},{4,12},{5,13},{6,14},{7,15},{8,0},{9,1},... | collective-permute-start | bytes 589832 | tf_op jit(solution)/shard_map/ppermute | solution.py:249
  84.1 10.1 %collective-permute-start.26 = (bf16[64,1536]{1,0:T(8,128)(2,1)S(1)}, bf16[64,1536]{1,0:T(8,128)(2,1)S(1)}, u32[]{:S(2)}, u32[]{:S(2)}) collective-permute-start(bf16[64,1536]{1,0:T(8,128)(2,1)S(1)} %get-tuple-element.159.refs_0_), channel_id=1, source_target_pairs={{0,24},{1,25},{2,26},{3,27},{4,28},{5,29},{6,30},{7,31},{8,16},{9,... | collective-permute-start | bytes 589832 | tf_op jit(solution)/shard_map/ppermute | solution.py:249
  85.3 9.0 %collective-permute-start.28 = (bf16[64,1536]{1,0:T(8,128)(2,1)S(1)}, bf16[64,1536]{1,0:T(8,128)(2,1)S(1)}, u32[]{:S(2)}, u32[]{:S(2)}) collective-permute-start(bf16[64,1536]{1,0:T(8,128)(2,1)S(1)} %get-tuple-element.159.refs_0_), channel_id=1, source_target_pairs={{0,1},{1,0},{2,3},{3,2},{4,5},{5,4},{6,7},{7,6},{8,9},{9,8},{10,11... | collective-permute-start | bytes 589832 | tf_op jit(solution)/shard_map/ppermute | solution.py:249
  88.8 5.4 %collective-permute-start.30 = (bf16[64,1536]{1,0:T(8,128)(2,1)S(1)}, bf16[64,1536]{1,0:T(8,128)(2,1)S(1)}, u32[]{:S(2)}, u32[]{:S(2)}) collective-permute-start(bf16[64,1536]{1,0:T(8,128)(2,1)S(1)} %collective-permute-done.25.refs_2_), channel_id=1, source_target_pairs={{0,1},{1,0},{2,3},{3,2},{4,5},{5,4},{6,7},{7,6},{8,9},{9,8},{10,11... | collective-permute-start | bytes 589832 | tf_op jit(solution)/shard_map/ppermute | solution.py:249
  90.8 3.5 %collective-permute-start.29 = (bf16[64,1536]{1,0:T(8,128)(2,1)S(1)}, bf16[64,1536]{1,0:T(8,128)(2,1)S(1)}, u32[]{:S(2)}, u32[]{:S(2)}) collective-permute-start(bf16[64,1536]{1,0:T(8,128)(2,1)S(1)} %collective-permute-done.24.refs_1_), channel_id=1, source_target_pairs={{0,1},{1,0},{2,3},{3,2},{4,5},{5,4},{6,7},{7,6},{8,9},{9,8},{10,11... | collective-permute-start | bytes 589832 | tf_op jit(solution)/shard_map/ppermute | solution.py:249
  98.0 1.5 collective-permute-start.32
  103.6 89.8 %reduce-scatter.6.cloned.1.call-start = ((), (), s32[]{:S(2)}) async-start(), calls=%async_computation.4 | async-start | bytes 757760 | tf_op jit(solution)/shard_map/reduce_scatter | solution.py:1036
  103.6 7.8 %collective-permute-start.33 = (bf16[64,1536]{1,0:T(8,128)(2,1)S(1)}, bf16[64,1536]{1,0:T(8,128)(2,1)S(1)}, u32[]{:S(2)}, u32[]{:S(2)}) collective-permute-start(bf16[64,1536]{1,0:T(8,128)(2,1)S(1)} %get-tuple-element.174), channel_id=1, source_target_pairs={{0,8},{1,9},{2,10},{3,11},{4,12},{5,13},{6,14},{7,15},{8,0},{9,1},... | collective-permute-start | bytes 589832 | tf_op jit(solution)/shard_map/ppermute | solution.py:249
  104.6 9.8 %collective-permute-start.34 = (bf16[64,1536]{1,0:T(8,128)(2,1)S(1)}, bf16[64,1536]{1,0:T(8,128)(2,1)S(1)}, u32[]{:S(2)}, u32[]{:S(2)}) collective-permute-start(bf16[64,1536]{1,0:T(8,128)(2,1)S(1)} %get-tuple-element.175), channel_id=1, source_target_pairs={{0,16},{1,17},{2,18},{3,19},{4,20},{5,21},{6,22},{7,23},{8,24},{9,... | collective-permute-start | bytes 589832 | tf_op jit(solution)/shard_map/ppermute | solution.py:249
  106.0 9.5 %collective-permute-start.35 = (bf16[64,1536]{1,0:T(8,128)(2,1)S(1)}, bf16[64,1536]{1,0:T(8,128)(2,1)S(1)}, u32[]{:S(2)}, u32[]{:S(2)}) collective-permute-start(bf16[64,1536]{1,0:T(8,128)(2,1)S(1)} %get-tuple-element.176), channel_id=1, source_target_pairs={{0,24},{1,25},{2,26},{3,27},{4,28},{5,29},{6,30},{7,31},{8,16},{9,... | collective-permute-start | bytes 589832 | tf_op jit(solution)/shard_map/ppermute | solution.py:249
  116.1 1.5 collective-permute-start.36
  121.6 71.8 %reduce-scatter.4.cloned.1.call-start = ((), (), s32[]{:S(2)}) async-start(), calls=%async_computation.3 | async-start | bytes 757760 | tf_op jit(solution)/shard_map/reduce_scatter | solution.py:1036
  121.6 7.8 %collective-permute-start.37 = (bf16[64,1536]{1,0:T(8,128)(2,1)S(1)}, bf16[64,1536]{1,0:T(8,128)(2,1)S(1)}, u32[]{:S(2)}, u32[]{:S(2)}) collective-permute-start(bf16[64,1536]{1,0:T(8,128)(2,1)S(1)} %get-tuple-element.188), channel_id=1, source_target_pairs={{0,8},{1,9},{2,10},{3,11},{4,12},{5,13},{6,14},{7,15},{8,0},{9,1},... | collective-permute-start | bytes 589832 | tf_op jit(solution)/shard_map/ppermute | solution.py:249
  122.8 9.6 %collective-permute-start.38 = (bf16[64,1536]{1,0:T(8,128)(2,1)S(1)}, bf16[64,1536]{1,0:T(8,128)(2,1)S(1)}, u32[]{:S(2)}, u32[]{:S(2)}) collective-permute-start(bf16[64,1536]{1,0:T(8,128)(2,1)S(1)} %get-tuple-element.189), channel_id=1, source_target_pairs={{0,16},{1,17},{2,18},{3,19},{4,20},{5,21},{6,22},{7,23},{8,24},{9,... | collective-permute-start | bytes 589832 | tf_op jit(solution)/shard_map/ppermute | solution.py:249
  124.0 9.7 %collective-permute-start.39 = (bf16[64,1536]{1,0:T(8,128)(2,1)S(1)}, bf16[64,1536]{1,0:T(8,128)(2,1)S(1)}, u32[]{:S(2)}, u32[]{:S(2)}) collective-permute-start(bf16[64,1536]{1,0:T(8,128)(2,1)S(1)} %get-tuple-element.190), channel_id=1, source_target_pairs={{0,24},{1,25},{2,26},{3,27},{4,28},{5,29},{6,30},{7,31},{8,16},{9,... | collective-permute-start | bytes 589832 | tf_op jit(solution)/shard_map/ppermute | solution.py:249
  135.7 1.5 collective-permute-start.40
  141.2 7.8 %collective-permute-start.41 = (bf16[64,1536]{1,0:T(8,128)(2,1)S(1)}, bf16[64,1536]{1,0:T(8,128)(2,1)S(1)}, u32[]{:S(2)}, u32[]{:S(2)}) collective-permute-start(bf16[64,1536]{1,0:T(8,128)(2,1)S(1)} %get-tuple-element.202), channel_id=1, source_target_pairs={{0,8},{1,9},{2,10},{3,11},{4,12},{5,13},{6,14},{7,15},{8,0},{9,1},... | collective-permute-start | bytes 589832 | tf_op jit(solution)/shard_map/ppermute | solution.py:249
  142.3 9.8 %collective-permute-start.42 = (bf16[64,1536]{1,0:T(8,128)(2,1)S(1)}, bf16[64,1536]{1,0:T(8,128)(2,1)S(1)}, u32[]{:S(2)}, u32[]{:S(2)}) collective-permute-start(bf16[64,1536]{1,0:T(8,128)(2,1)S(1)} %get-tuple-element.203), channel_id=1, source_target_pairs={{0,16},{1,17},{2,18},{3,19},{4,20},{5,21},{6,22},{7,23},{8,24},{9,... | collective-permute-start | bytes 589832 | tf_op jit(solution)/shard_map/ppermute | solution.py:249
  143.6 9.5 %collective-permute-start.43 = (bf16[64,1536]{1,0:T(8,128)(2,1)S(1)}, bf16[64,1536]{1,0:T(8,128)(2,1)S(1)}, u32[]{:S(2)}, u32[]{:S(2)}) collective-permute-start(bf16[64,1536]{1,0:T(8,128)(2,1)S(1)} %get-tuple-element.204), channel_id=1, source_target_pairs={{0,24},{1,25},{2,26},{3,27},{4,28},{5,29},{6,30},{7,31},{8,16},{9,... | collective-permute-start | bytes 589832 | tf_op jit(solution)/shard_map/ppermute | solution.py:249
  153.7 1.5 collective-permute-start.44
  159.2 8.7 %collective-permute-start.45 = (bf16[64,1536]{1,0:T(8,128)(2,1)S(1)}, bf16[64,1536]{1,0:T(8,128)(2,1)S(1)}, u32[]{:S(2)}, u32[]{:S(2)}) collective-permute-start(bf16[64,1536]{1,0:T(8,128)(2,1)S(1)} %get-tuple-element.216), channel_id=1, source_target_pairs={{0,8},{1,9},{2,10},{3,11},{4,12},{5,13},{6,14},{7,15},{8,0},{9,1},... | collective-permute-start | bytes 589832 | tf_op jit(solution)/shard_map/ppermute | solution.py:249
  160.4 9.7 %collective-permute-start.46 = (bf16[64,1536]{1,0:T(8,128)(2,1)S(1)}, bf16[64,1536]{1,0:T(8,128)(2,1)S(1)}, u32[]{:S(2)}, u32[]{:S(2)}) collective-permute-start(bf16[64,1536]{1,0:T(8,128)(2,1)S(1)} %get-tuple-element.217), channel_id=1, source_target_pairs={{0,16},{1,17},{2,18},{3,19},{4,20},{5,21},{6,22},{7,23},{8,24},{9,... | collective-permute-start | bytes 589832 | tf_op jit(solution)/shard_map/ppermute | solution.py:249
  161.6 9.7 %collective-permute-start.47 = (bf16[64,1536]{1,0:T(8,128)(2,1)S(1)}, bf16[64,1536]{1,0:T(8,128)(2,1)S(1)}, u32[]{:S(2)}, u32[]{:S(2)}) collective-permute-start(bf16[64,1536]{1,0:T(8,128)(2,1)S(1)} %get-tuple-element.218), channel_id=1, source_target_pairs={{0,24},{1,25},{2,26},{3,27},{4,28},{5,29},{6,30},{7,31},{8,16},{9,... | collective-permute-start | bytes 589832 | tf_op jit(solution)/shard_map/ppermute | solution.py:249
  162.8 15.0 %collective-permute-start.56 = (bf16[592,128]{1,0:T(8,128)(2,1)S(1)}, bf16[592,128]{1,0:T(8,128)(2,1)S(1)}, u32[]{:S(2)}, u32[]{:S(2)}) collective-permute-start(bf16[592,128]{1,0:T(8,128)(2,1)S(1)} %get-tuple-element.234), channel_id=1, source_target_pairs={{0,2},{1,3},{2,0},{3,1},{4,6},{5,7},{6,4},{7,5},{8,10},{9,11},{10,... | collective-permute-start | bytes 454664 | tf_op jit(solution)/shard_map/ppermute | solution.py:249
  167.0 18.9 %collective-permute-start.57 = (bf16[592,128]{1,0:T(8,128)(2,1)S(1)}, bf16[592,128]{1,0:T(8,128)(2,1)S(1)}, u32[]{:S(2)}, u32[]{:S(2)}) collective-permute-start(bf16[592,128]{1,0:T(8,128)(2,1)S(1)} %get-tuple-element.235), channel_id=1, source_target_pairs={{0,4},{1,5},{2,6},{3,7},{4,0},{5,1},{6,2},{7,3},{8,12},{9,13},{10,... | collective-permute-start | bytes 454664 | tf_op jit(solution)/shard_map/ppermute | solution.py:249
  168.0 17.9 %collective-permute-start.58 = (bf16[592,128]{1,0:T(8,128)(2,1)S(1)}, bf16[592,128]{1,0:T(8,128)(2,1)S(1)}, u32[]{:S(2)}, u32[]{:S(2)}) collective-permute-start(bf16[592,128]{1,0:T(8,128)(2,1)S(1)} %get-tuple-element.236), channel_id=1, source_target_pairs={{0,6},{1,7},{2,4},{3,5},{4,2},{5,3},{6,0},{7,1},{8,14},{9,15},{10,... | collective-permute-start | bytes 454664 | tf_op jit(solution)/shard_map/ppermute | solution.py:249
  172.2 22.4 %collective-permute-start.48 = (bf16[128,384]{1,0:T(8,128)(2,1)S(1)}, bf16[128,384]{1,0:T(8,128)(2,1)S(1)}, u32[]{:S(2)}, u32[]{:S(2)}) collective-permute-start(bf16[128,384]{1,0:T(8,128)(2,1)S(1)} %get-tuple-element.223), channel_id=1, source_target_pairs={{0,0},{1,1},{2,8},{3,9},{4,16},{5,17},{6,24},{7,25},{8,2},{9,3},{1... | collective-permute-start | bytes 294920 | tf_op jit(solution)/shard_map/ppermute | solution.py:249
  172.9 21.8 %collective-permute-start.49 = (bf16[128,384]{1,0:T(8,128)(2,1)S(1)}, bf16[128,384]{1,0:T(8,128)(2,1)S(1)}, u32[]{:S(2)}, u32[]{:S(2)}) collective-permute-start(bf16[128,384]{1,0:T(8,128)(2,1)S(1)} %get-tuple-element.224), channel_id=1, source_target_pairs={{0,2},{1,3},{2,10},{3,11},{4,18},{5,19},{6,26},{7,27},{8,0},{9,1},... | collective-permute-start | bytes 294920 | tf_op jit(solution)/shard_map/ppermute | solution.py:249
  185.9 12.2 %collective-permute-start.50 = (bf16[128,384]{1,0:T(8,128)(2,1)S(1)}, bf16[128,384]{1,0:T(8,128)(2,1)S(1)}, u32[]{:S(2)}, u32[]{:S(2)}) collective-permute-start(bf16[128,384]{1,0:T(8,128)(2,1)S(1)} %get-tuple-element.225), channel_id=1, source_target_pairs={{0,4},{1,5},{2,12},{3,13},{4,20},{5,21},{6,28},{7,29},{8,6},{9,7},... | collective-permute-start | bytes 294920 | tf_op jit(solution)/shard_map/ppermute | solution.py:249
  188.7 9.4 %collective-permute-start.51 = (bf16[128,384]{1,0:T(8,128)(2,1)S(1)}, bf16[128,384]{1,0:T(8,128)(2,1)S(1)}, u32[]{:S(2)}, u32[]{:S(2)}) collective-permute-start(bf16[128,384]{1,0:T(8,128)(2,1)S(1)} %get-tuple-element.226), channel_id=1, source_target_pairs={{0,6},{1,7},{2,14},{3,15},{4,22},{5,23},{6,30},{7,31},{8,4},{9,5},... | collective-permute-start | bytes 294920 | tf_op jit(solution)/shard_map/ppermute | solution.py:249
  194.5 5.3 %collective-permute-start.59 = (bf16[592,128]{1,0:T(8,128)(2,1)S(1)}, bf16[592,128]{1,0:T(8,128)(2,1)S(1)}, u32[]{:S(2)}, u32[]{:S(2)}) collective-permute-start(bf16[592,128]{1,0:T(8,128)(2,1)S(1)} %get-tuple-element.244), channel_id=1, source_target_pairs={{0,8},{1,9},{2,10},{3,11},{4,12},{5,13},{6,14},{7,15},{8,0},{9,1},... | collective-permute-start | bytes 454664 | tf_op jit(solution)/shard_map/ppermute | solution.py:249
  194.6 7.6 %collective-permute-start.60 = (bf16[592,128]{1,0:T(8,128)(2,1)S(1)}, bf16[592,128]{1,0:T(8,128)(2,1)S(1)}, u32[]{:S(2)}, u32[]{:S(2)}) collective-permute-start(bf16[592,128]{1,0:T(8,128)(2,1)S(1)} %get-tuple-element.245), channel_id=1, source_target_pairs={{0,16},{1,17},{2,18},{3,19},{4,20},{5,21},{6,22},{7,23},{8,24},{9,... | collective-permute-start | bytes 454664 | tf_op jit(solution)/shard_map/ppermute | solution.py:249
  194.7 7.6 %collective-permute-start.61 = (bf16[592,128]{1,0:T(8,128)(2,1)S(1)}, bf16[592,128]{1,0:T(8,128)(2,1)S(1)}, u32[]{:S(2)}, u32[]{:S(2)}) collective-permute-start(bf16[592,128]{1,0:T(8,128)(2,1)S(1)} %get-tuple-element.246), channel_id=1, source_target_pairs={{0,24},{1,25},{2,26},{3,27},{4,28},{5,29},{6,30},{7,31},{8,16},{9,... | collective-permute-start | bytes 454664 | tf_op jit(solution)/shard_map/ppermute | solution.py:249
  198.1 4.7 %collective-permute-start.52 = (bf16[128,384]{1,0:T(8,128)(2,1)S(1)}, bf16[128,384]{1,0:T(8,128)(2,1)S(1)}, u32[]{:S(2)}, u32[]{:S(2)}) collective-permute-start(bf16[128,384]{1,0:T(8,128)(2,1)S(1)} %collective-permute-done.48.refs_0_), channel_id=1, source_target_pairs={{0,1},{1,0},{2,3},{3,2},{4,5},{5,4},{6,7},{7,6},{8,9},{9,8},{10,11... | collective-permute-start | bytes 294920 | tf_op jit(solution)/shard_map/ppermute | solution.py:249
  198.1 4.7 %collective-permute-start.53 = (bf16[128,384]{1,0:T(8,128)(2,1)S(1)}, bf16[128,384]{1,0:T(8,128)(2,1)S(1)}, u32[]{:S(2)}, u32[]{:S(2)}) collective-permute-start(bf16[128,384]{1,0:T(8,128)(2,1)S(1)} %collective-permute-done.49.refs_1_), channel_id=1, source_target_pairs={{0,1},{1,0},{2,3},{3,2},{4,5},{5,4},{6,7},{7,6},{8,9},{9,8},{10,11... | collective-permute-start | bytes 294920 | tf_op jit(solution)/shard_map/ppermute | solution.py:249
  199.8 3.5 %collective-permute-start.54 = (bf16[128,384]{1,0:T(8,128)(2,1)S(1)}, bf16[128,384]{1,0:T(8,128)(2,1)S(1)}, u32[]{:S(2)}, u32[]{:S(2)}) collective-permute-start(bf16[128,384]{1,0:T(8,128)(2,1)S(1)} %collective-permute-done.50.refs_2_), channel_id=1, source_target_pairs={{0,1},{1,0},{2,3},{3,2},{4,5},{5,4},{6,7},{7,6},{8,9},{9,8},{10,11... | collective-permute-start | bytes 294920 | tf_op jit(solution)/shard_map/ppermute | solution.py:249
  202.2 3.5 %collective-permute-start.62 = (bf16[592,128]{1,0:T(8,128)(2,1)S(1)}, bf16[592,128]{1,0:T(8,128)(2,1)S(1)}, u32[]{:S(2)}, u32[]{:S(2)}) collective-permute-start(bf16[592,128]{1,0:T(8,128)(2,1)S(1)} %get-tuple-element.243.refs_0_), channel_id=1, source_target_pairs={{0,1},{1,0},{2,3},{3,2},{4,5},{5,4},{6,7},{7,6},{8,9},{9,8},{10,11... | collective-permute-start | bytes 454664 | tf_op jit(solution)/shard_map/ppermute | solution.py:249
  202.3 3.5 %collective-permute-start.63 = (bf16[592,128]{1,0:T(8,128)(2,1)S(1)}, bf16[592,128]{1,0:T(8,128)(2,1)S(1)}, u32[]{:S(2)}, u32[]{:S(2)}) collective-permute-start(bf16[592,128]{1,0:T(8,128)(2,1)S(1)} %collective-permute-done.59.refs_1_), channel_id=1, source_target_pairs={{0,1},{1,0},{2,3},{3,2},{4,5},{5,4},{6,7},{7,6},{8,9},{9,8},{10,11... | collective-permute-start | bytes 454664 | tf_op jit(solution)/shard_map/ppermute | solution.py:249
  202.8 3.0 %collective-permute-start.64 = (bf16[592,128]{1,0:T(8,128)(2,1)S(1)}, bf16[592,128]{1,0:T(8,128)(2,1)S(1)}, u32[]{:S(2)}, u32[]{:S(2)}) collective-permute-start(bf16[592,128]{1,0:T(8,128)(2,1)S(1)} %collective-permute-done.60.refs_2_), channel_id=1, source_target_pairs={{0,1},{1,0},{2,3},{3,2},{4,5},{5,4},{6,7},{7,6},{8,9},{9,8},{10,11... | collective-permute-start | bytes 454664 | tf_op jit(solution)/shard_map/ppermute | solution.py:249
  202.8 2.9 %collective-permute-start.65 = (bf16[592,128]{1,0:T(8,128)(2,1)S(1)}, bf16[592,128]{1,0:T(8,128)(2,1)S(1)}, u32[]{:S(2)}, u32[]{:S(2)}) collective-permute-start(bf16[592,128]{1,0:T(8,128)(2,1)S(1)} %collective-permute-done.61.refs_3_), channel_id=1, source_target_pairs={{0,1},{1,0},{2,3},{3,2},{4,5},{5,4},{6,7},{7,6},{8,9},{9,8},{10,11... | collective-permute-start | bytes 454664 | tf_op jit(solution)/shard_map/ppermute | solution.py:249
  (7 other events, 43.1 us)
Sparse Core Ops, SparseCore 0:
  103.7 23.5 reduce-scatter.7
  129.6 20.6 reduce-scatter.5
  152.6 22.6 reduce-scatter.3

commit v2 on v1

--- a/solution.py
+++ b/solution.py
@@ -10,6 +10,7 @@
 from jax.sharding import PartitionSpec as P
 
 CONVS = 2
+BACK_FLOPS = 6000000000
 
 
 eps = 1e-05
@@ -535,15 +536,19 @@
         lines.append(jnp.zeros((META_ROWS - len(lines), LANES), jnp.float32))
         out[TAPS * ch :, :] = jnp.zeros((META_ROWS, out.shape[1]), jnp.bfloat16)
         out[TAPS * ch :, :LANES] = jnp.concatenate(lines, axis=0).astype(jnp.bfloat16)
+    tail = pl.ds(TAPS * ch, META_ROWS)
+    own_copies = start_all([pltpu.make_async_copy(own.at[tail], outs[0].at[tail], sems.at[2 * TAPS + 2])])
     for tap in range(TAPS):
         copies[tap].wait()
         turned[...] = columns[tap].T
         for k, out in enumerate(targets):
             rows = pl.ds(pl.multiple_of((section ^ k) * ch, ch), ch)
             out[tap * ch : (tap + 1) * ch, :] = turned[rows, :]
-    own_copy = pltpu.make_async_copy(own, outs[0], sems.at[TAPS])
-    own_copy.start()
-    own_copy.wait()
+        piece = pl.ds(tap * ch, ch)
+        own_copies += start_all(
+            [pltpu.make_async_copy(own.at[piece], outs[0].at[piece], sems.at[TAPS + 2 + tap])]
+        )
+    wait_all(own_copies)
 
 
 def pick_kernel(layer, *refs):
@@ -697,8 +702,14 @@
         piece[rows:, :] = sums_rows(sums, rows // TAPS, width)
 
 
+def form_share(layer, moved, full, sums, product):
+    piece = product.shape[0] // 4
+    value = weight_product(moved[: piece - META_ROWS, :], full[...], layer == 0)
+    store_share(value, sums, [product.at[pl.ds(n * piece, piece)] for n in range(4)])
+
+
 def conv_back_kernel(dims, layer, own, other, own_weights, other_weights, full_in, sums, facts, *refs):
-    outs, shares, (product, moved, weights, full, sems) = refs[:4], refs[4:-5], refs[-5:]
+    *outs, share, product, full, moved, weights, sems = refs
     ch = own.shape[0]
     size = moved.shape[0] // 2
     rows = pl.ds(layer * 4 * ch, 4 * ch)
@@ -713,20 +724,9 @@
     facts_now = facts[...]
     spread_taps(own[...], moved, 0, facts_now, dims[1])
     full_copy.wait()
-    value = weight_product(moved[: TAPS * ch, :], full[...], layer == 0)
-    if len(shares) == 1:
-        piece = product.shape[0] // 4
-        store_share(value, sums, [product.at[pl.ds(n * piece, piece)] for n in range(4)])
-        share_copy = pltpu.make_async_copy(product, shares[0], sems.at[3])
-        share_copy.start()
-    else:
-        _, plane, _ = place()
-        width = shares[0].shape[1]
-        product[...] = value.astype(jnp.bfloat16)
-        for k, share in enumerate(shares):
-            at = pl.multiple_of((plane ^ k) * width, width)
-            share[: TAPS * ch, :] = product[:, pl.ds(at, width)]
-            share[TAPS * ch :, :] = sums_rows(sums, ch, width)
+    form_share(layer, moved, full, sums, product)
+    share_copy = pltpu.make_async_copy(product, share, sems.at[3])
+    share_copy.start()
     spread_taps(other[...], moved, size, facts_now, dims[1])
     for n in range(2):
         moved[n * size + TAPS * ch : (n + 1) * size, :] = jnp.zeros(
@@ -736,31 +736,25 @@
     value = jnp.dot(weights[...], moved[...], preferred_element_type=jnp.float32)
     for k, out in enumerate(outs):
         out[...] = value[k * ch : (k + 1) * ch, :].astype(jnp.bfloat16)
-    if len(shares) == 1:
-        share_copy.wait()
+    share_copy.wait()
 
 
 def choose_kernel(*refs):
-    blocks, others, outs, sem = refs[:4], refs[4:-5], refs[-5:-1], refs[-1]
+    shares, outs, (blocks, sems) = refs[:-6], refs[-6:-2], refs[-2:]
     section, _, _ = place()
-    for layer, other in enumerate(others, 1):
+    rows = outs[0].shape[0]
+    copies = start_all(
+        [pltpu.make_async_copy(share, blocks.at[layer], sems.at[layer]) for layer, share in enumerate(shares)]
+    )
+    for layer, copy in enumerate(copies):
+        copy.wait()
+        value = add_blocks([blocks.at[layer, pl.ds(n * rows, rows)] for n in range(blocks.shape[1] // rows)])
+        value = value.astype(jnp.bfloat16)
         for k, out in enumerate(outs):
 
             @pl.when((section ^ k) == layer)
             def _():
-                pltpu.make_async_copy(other, out, sem.at[k]).start()
-
-    value = add_blocks(blocks).astype(jnp.bfloat16)
-    for k, out in enumerate(outs):
-        copy = pltpu.make_async_copy(others[0], out, sem.at[k])
-
-        @pl.when((section ^ k) == 0)
-        def _():
-            out[...] = value
-
-        @pl.when((section ^ k) != 0)
-        def _():
-            copy.wait()
+                out[...] = value
 
 
 def turn_weights_kernel(layers, *refs):
@@ -784,42 +778,53 @@
 
 
 def input_kernel(*refs):
-    blocks, (hidden, inside), pieces, (full, sems) = refs[:4], refs[4:6], refs[6:10], refs[10:]
-    section, _, _ = place()
+    blocks, (hidden, inside, keep, give, full, sems) = refs[:4], refs[4:]
+    section, _, core = place()
     ch = hidden.shape[0]
     copy = pltpu.make_async_copy(hidden, full.at[pl.ds(0, ch)], sems.at[0])
     copy.start()
     full[ch:, :] = (add_blocks(blocks) * inside[...]).astype(jnp.bfloat16)
     copy.wait()
-    width = pieces[0].shape[1]
-    for k, piece in enumerate(pieces):
-        piece[...] = full[:, pl.ds(pl.multiple_of((section ^ k) * width, width), width)]
+    rows = 2 * ch
+    width = keep.shape[1]
+    for j, out in enumerate((keep, give)):
+        for n in range(2):
+            at = pl.multiple_of((section ^ (2 * (core ^ j) + n)) * width, width)
+            out[n * rows : (n + 1) * rows, :] = full[:, pl.ds(at, width)]
+
+
+def pair_kernel(keep, got, *outs):
+    rows = keep.shape[0] // 2
+    for n, out in enumerate(outs):
+        out[:rows, :] = keep[n * rows : (n + 1) * rows, :]
+        out[rows:, :] = got[n * rows : (n + 1) * rows, :]
 
 
 def maps_out_kernel(*refs):
-    blocks, outs, (full,) = refs[:8], refs[8:10], refs[10:]
+    blocks, pick, outs, full = refs[:4], refs[4], refs[5:7], refs[7]
     _, plane, core = place()
-    ch = blocks[0].shape[0] // 2
-    cells = outs[0].shape[0]
-    for n, out in enumerate(outs):
-        for (k, j), block in zip(peer_order(), blocks):
-            at = pl.multiple_of(slice_at(plane, core, k, j) * ch, ch)
-            full[pl.ds(at, ch), :] = block[n * ch : (n + 1) * ch, :]
-        both = full[...].astype(jnp.float32)
-        mine = jnp.where(core == 0, both[:, :cells], both[:, cells:])
-        out[...] = mine.T.astype(out.dtype)
+    ch = blocks[0].shape[0] // 4
+    for m, out in enumerate(outs):
+        for j in range(2):
+            for n in range(2):
+                for h in range(2):
+                    slot = slice_at(plane ^ (2 * (core ^ j) + n), core ^ j, 0, h)
+                    at = pl.multiple_of(slot * ch, ch)
+                    start = (2 * h + m) * ch
+                    full[pl.ds(at, ch), :] = blocks[2 * j + n][start : start + ch, :]
+        mine = lax.dot_general(pick[...], full[...], NT, preferred_element_type=jnp.float32)
+        out[...] = mine.astype(out.dtype)
 
 
 def grads_out_kernel(*refs):
-    blocks, (weight_out, shift_out, slope_out), (full, turned) = refs[:8], refs[8:11], refs[11:]
+    blocks, pick, (weight_out, shift_out, slope_out), (full,) = refs[:8], refs[8], refs[9:12], refs[12:]
     section, plane, core = place()
     taps, rows, channels = weight_out.shape
     for tap in range(taps):
         for (k, j), block in zip(peer_order(), blocks):
             at = pl.multiple_of(slice_at(section, core, k, j) * rows, rows)
-            full[pl.ds(at, rows), :] = block[tap * rows : (tap + 1) * rows, :].astype(jnp.float32)
-        turned[...] = full[...].T
-        weight_out[tap] = turned[pl.ds(pl.multiple_of(core * rows, rows), rows), :]
+            full[tap, pl.ds(at, rows), :] = block[tap * rows : (tap + 1) * rows, :]
+        weight_out[tap] = lax.dot_general(pick[...], full[tap], NT, preferred_element_type=jnp.float32)
     shift_row = jnp.zeros((1, rows), jnp.float32)
     slope_row = jnp.zeros((1, rows), jnp.float32)
     slot = plane * 2 + core
@@ -902,7 +907,7 @@
         "weight_pack",
         held=range(3),
         held_outs=(0,),
-        copies=TAPS + 2,
+        copies=2 * TAPS + 3,
     )
     slices = spread(packed, to_section)
 
@@ -1014,30 +1019,26 @@
     shares = [None] * layers
     same_core = [[2 * z + c for z in range(layers)] for c in range(2)]
     for layer in range(last, -1, -1):
-        scattered = layer > 0
-        result = call(
+        *parts, share = call(
             partial(conv_back_kernel, dims, layer),
-            [map_out] * 4 + ([share_out] if scattered else [share_piece] * 4),
+            [map_out] * 4 + [share_out],
             [
-                share_out if scattered else ((TAPS * ch, channels), bf16),
+                share_out,
+                full_map if layer else full_frames,
                 ((2 * tap_rows, length), bf16),
                 ((4 * ch, 2 * tap_rows), bf16),
-                full_map if layer else full_frames,
             ],
             [grad_pre, to_core(grad_pre), *turned, fulls[layer], sums, facts],
             "conv_back",
             held=(2, 3, 4),
-            held_outs=(4,) if scattered else (),
+            held_outs=(4,),
             loose=(5, 6),
+            flops=BACK_FLOPS,
             copies=4,
         )
-        parts = result[:4]
-        if scattered:
-            shares[layer] = lax.psum_scatter(
-                result[4], "dp", scatter_dimension=0, tiled=True, axis_index_groups=same_core
-            )
-        else:
-            shares[layer] = spread(result[4:], to_plane)
+        if layer < last:
+            share = after(share, shares[layer + 1])
+        shares[layer] = lax.all_to_all(share, "dp", 0, 0, tiled=True, axis_index_groups=same_core)
         if layer:
             held = call(
                 partial(fetch_kernel, layer - 1),
@@ -1058,9 +1059,9 @@
                 loose=(6, 7),
             )
     blocks = spread(parts, to_section)
-    maps = call(
+    keep, give = call(
         input_kernel,
-        [((2 * ch, 2 * cells), bf16)] * 4,
+        [((4 * ch, 2 * cells), bf16)] * 2,
         [((2 * ch, length), bf16)],
         [*blocks, activation, inside],
         "input",
@@ -1068,34 +1069,36 @@
         loose=(5,),
         copies=1,
     )
-    maps = lax.optimization_barrier(
-        [send(x, lambda s, z, c, k=k: (z, s ^ k, c)) for k, x in enumerate(maps)]
-    )
+    maps = call(pair_kernel, [((4 * ch, 2 * cells), bf16)] * 2, [], [keep, to_core(give)], "pair")
+    maps = [send(x, lambda s, z, c, n=n: (z, s ^ (2 * c + n), c)) for n, x in enumerate(maps)]
+    chosen = call(
+        choose_kernel,
+        [share_piece] * 4,
+        [((layers, 4 * slice_rows, 2 * ch), bf16)],
+        shares,
+        "choose",
+        held=range(layers),
+        copies=layers,
+    )
+    pick = (core * cells + np.arange(cells))[:, None] == np.arange(2 * cells)[None, :]
     activations, input_grad = call(
         maps_out_kernel,
         [((cells, channels), bf16)] * 2,
         [((channels, 2 * cells), bf16)],
-        with_core(maps),
+        [*with_core(after(maps, chosen)), pick.astype(bf16)],
         "maps_out",
+        loose=(4,),
         last=True,
     )
 
-    ready = shares[1:]
-    chosen = call(
-        choose_kernel,
-        [share_piece] * 4,
-        [],
-        [*shares[0], *ready],
-        "choose",
-        held=range(4, 4 + len(ready)),
-        copies=4,
-    )
+    pick = (core * ch + np.arange(ch))[:, None] == np.arange(2 * ch)[None, :]
     weight_grad, bias_grad, gain_grad = call(
         grads_out_kernel,
         [((TAPS, ch, channels), f32), ((1, ch), f32), ((1, ch), f32)],
-        [((channels, 2 * ch), f32), ((2 * ch, channels), f32)],
-        with_core(spread(chosen, to_section)),
+        [((TAPS, channels, 2 * ch), bf16)],
+        [*with_core(after(spread(chosen, to_section), activations, input_grad)), pick.astype(bf16)],
         "grads_out",
+        loose=(8,),
         last=True,
     )
     weight_grad = weight_grad.reshape(3, 3, ch, channels).transpose(2, 0, 1, 3)[None]

time: 215 us -> 204 us (0.949)
  between operations: 14.1 us -> 1.11 us
  starting transfers between devices: 64.5 us -> 68.2 us
  waiting for transfers between devices: 83.6 us -> 80.7 us
    ppermute x66 -> x60, waiting for transfers between devices: 83.5 us -> 64.6 us  [send(): return lax.ppermute(x, AXES, pairs)]
    all_to_all x0 -> x4, starting transfers between devices: none -> 16.9 us  [plane_shards(): lax.all_to_all(share, 'dp', 0, 0, tiled=True, axis_index_groups=same_core)]
    all_to_all x0 -> x4, waiting for transfers between devices: none -> 16.1 us  [plane_shards(): lax.all_to_all(share, 'dp', 0, 0, tiled=True, axis_index_groups=same_core)]
    ppermute x66 -> x60, starting transfers between devices: 64.3 us -> 51.3 us  [send(): return lax.ppermute(x, AXES, pairs)]
    pallas_call x24 -> x25, Pallas kernels: 51.9 us -> 52.2 us  [call(): pl.pallas_call(kernel, out_shape=shapes, in_specs=[pl.BlockSpec(memory_sp...]
  transfers between devices with their start and end apart: 69 -> 64, of which waited for: 37 -> 34; matrix products, arithmetic and copies ran while one was open for 0% -> 0% of each run, Pallas kernels for 15% -> 16%
where the time goes in v2:
time: 204 us; the launch traced here: 203 us
  waiting for transfers between devices  80.7 us (40%)
  starting transfers between devices  68.2 us (33%)
  Pallas kernels  52.2 us (26%)
    ppermute x60, waiting for transfers between devices, send(): return lax.ppermute(x, AXES, pairs)  64.6 us
    pallas_call x25, Pallas kernels, call(): pl.pallas_call(kernel, out_shape=shapes, in_specs=[pl.BlockSpec(memory_sp...  52.2 us
    ppermute x60, starting transfers between devices, send(): return lax.ppermute(x, AXES, pairs)  51.3 us
    all_to_all x4, starting transfers between devices, plane_shards(): lax.all_to_all(share, 'dp', 0, 0, tiled=True, axis_index_groups=same_core)  16.9 us
    all_to_all x4, waiting for transfers between devices, plane_shards(): lax.all_to_all(share, 'dp', 0, 0, tiled=True, axis_index_groups=same_core)  16.1 us
  transfers between devices with their start and end apart: 64, of which 34 were waited for; matrix products, arithmetic and copies ran while one was open for 0% of the time, Pallas kernels for 16%

profile of v2, /device:TPU:0, one launch (start us, length us, event | category | flops | bytes accessed | tf_op | source)
XLA Modules:
  0.0 203.3 jit_solution(7138020640311064358)
XLA Ops:
  0.6 3.6 %weight_pack.1 = (bf16[592,512]{1,0:T(8,128)(2,1)}, bf16[592,512]{1,0:T(8,128)(2,1)S(1)}, bf16[592,512]{1,0:T(8,128)(2,1)S(1)}, bf16[592,512]{1,0:T(8,128)(2,1)S(1)}) custom-call(f32[1,512]{1,0:T(1,128)} %gain.1, f32[1,512]{1,0:T(1,128)} %bias.1, bf16[9,512,512]{2,1,0:T(8,128)(2,1)} %bitcast.24), custom_call_target="tpu_custom_call" | custom-call | bytes 7147520 | tf_op jit(solution)/shard_map/weight_pack/pallas_call | solution.py:858
  4.2 3.0 %collective-permute-start.7 = (bf16[592,512]{1,0:T(8,128)(2,1)S(1)}, bf16[592,512]{1,0:T(8,128)(2,1)}, u32[]{:S(2)}, u32[]{:S(2)}) collective-permute-start(bf16[592,512]{1,0:T(8,128)(2,1)S(1)} %get-tuple-element.129), channel_id=1, source_target_pairs={{0,8},{1,9},{2,10},{3,11},{4,12},{5,13},{6,14},{7,15},{8,0},{9,1},... | collective-permute-start | bytes 1818632 | tf_op jit(solution)/shard_map/ppermute | solution.py:250
  7.3 1.5 collective-permute-start.8
  8.8 1.8 frames.1
  10.6 1.6 collective-permute-start
  12.7 2.6 %collective-permute-start.1 = (bf16[208,640]{1,0:T(8,128)(2,1)S(1)}, bf16[208,640]{1,0:T(8,128)(2,1)S(1)}, u32[]{:S(2)}, u32[]{:S(2)}) collective-permute-start(bf16[208,640]{1,0:T(8,128)(2,1)S(1)} %get-tuple-element.135), channel_id=1, source_target_pairs={{0,4},{1,5},{2,6},{3,7},{4,0},{5,1},{6,2},{7,3},{8,12},{9,13},{10,... | collective-permute-start | bytes 798728 | tf_op jit(solution)/shard_map/ppermute | solution.py:250
  15.3 8.4 %collective-permute-done.refs_1_ = bf16[208,640]{1,0:T(8,128)(2,1)S(1)} collective-permute-done((bf16[208,640]{1,0:T(8,128)(2,1)S(1)}, bf16[208,640]{1,0:T(8,128)(2,1)S(1)}, u32[]{:S(2)}, u32[]{:S(2)}) %collective-permute-start) | collective-permute-done | bytes 266272 | tf_op jit(solution)/shard_map/ppermute | solution.py:250
  23.7 2.5 %collective-permute-start.2 = (bf16[208,640]{1,0:T(8,128)(2,1)S(1)}, bf16[208,640]{1,0:T(8,128)(2,1)S(1)}, u32[]{:S(2)}, u32[]{:S(2)}) collective-permute-start(bf16[208,640]{1,0:T(8,128)(2,1)S(1)} %get-tuple-element.136), channel_id=1, source_target_pairs={{0,6},{1,7},{2,4},{3,5},{4,2},{5,3},{6,0},{7,1},{8,14},{9,15},{10,... | collective-permute-start | bytes 798728 | tf_op jit(solution)/shard_map/ppermute | solution.py:250
  26.2 6.2 %collective-permute-done.1.refs_2_ = bf16[208,640]{1,0:T(8,128)(2,1)S(1)} collective-permute-done((bf16[208,640]{1,0:T(8,128)(2,1)S(1)}, bf16[208,640]{1,0:T(8,128)(2,1)S(1)}, u32[]{:S(2)}, u32[]{:S(2)}) %collective-permute-start.1) | collective-permute-done | bytes 266272 | tf_op jit(solution)/shard_map/ppermute | solution.py:250
  32.9 2.6 %collective-permute-done.8.refs_10_.refs_2_ = bf16[592,512]{1,0:T(8,128)(2,1)} collective-permute-done((bf16[592,512]{1,0:T(8,128)(2,1)S(1)}, bf16[592,512]{1,0:T(8,128)(2,1)}, u32[]{:S(2)}, u32[]{:S(2)}) %collective-permute-start.8) | collective-permute-done | bytes 606240 | tf_op jit(solution)/shard_map/ppermute | solution.py:250
  35.7 1.4 collective-permute-done.6.refs_7_
  37.1 3.8 %forward.3 = (bf16[64,1536]{1,0:T(8,128)(2,1)S(1)}, f32[64,1664]{1,0:T(8,128)}, bf16[1536,512]{1,0:T(8,128)(2,1)}, f32[1,1536]{1,0:T(1,128)S(1)}, bf16[64,1536]{1,0:T(8,128)(2,1)}) custom-call(bf16[208,640]{1,0:T(8,128)(2,1)S(1)} %get-tuple-element.133.refs_0_, bf16[208,640]{1,0:T(8,128)(2,1)S(1)} %collective-permute-done.refs_1_, ...), custom_call_target="tpu_custom_call" | custom-call | flops 905969664 | bytes 7067648 | tf_op jit(solution)/shard_map/forward/pallas_call | solution.py:858
  40.9 2.2 %collective-permute-start.12 = (bf16[64,1536]{1,0:T(8,128)(2,1)S(1)}, bf16[64,1536]{1,0:T(8,128)(2,1)S(1)}, u32[]{:S(2)}, u32[]{:S(2)}) collective-permute-start(bf16[64,1536]{1,0:T(8,128)(2,1)S(1)} %get-tuple-element.143.refs_0_), channel_id=1, source_target_pairs={{0,24},{1,25},{2,26},{3,27},{4,28},{5,29},{6,30},{7,31},{8,16},{9,... | collective-permute-start | bytes 589832 | tf_op jit(solution)/shard_map/ppermute | solution.py:250
  44.4 3.8 %turn_weights.1 = (bf16[1024,640]{1,0:T(8,128)(2,1)}, bf16[1024,640]{1,0:T(8,128)(2,1)}) custom-call(bf16[592,512]{1,0:T(8,128)(2,1)} %get-tuple-element.159.refs_8_.refs_0_, bf16[592,512]{1,0:T(8,128)(2,1)} %collective-permute-done.7.refs_9_.refs_1_, bf16[592,512]{1,0:T(8,128)(2,1)} %collective-permute-done.8.refs_10_.refs_2_, ...), custom_call_target="tpu_custom_call" | custom-call | bytes 5046272 | tf_op jit(solution)/shard_map/turn_weights/pallas_call | solution.py:858
  48.3 1.1 pick.3.refs_8_
  50.0 3.1 %collective-permute-done.10.refs_1_ = bf16[64,1536]{1,0:T(8,128)(2,1)S(1)} collective-permute-done((bf16[64,1536]{1,0:T(8,128)(2,1)S(1)}, bf16[64,1536]{1,0:T(8,128)(2,1)S(1)}, u32[]{:S(2)}, u32[]{:S(2)}) %collective-permute-start.10) | collective-permute-done | bytes 196640 | tf_op jit(solution)/shard_map/ppermute | solution.py:250
  54.8 3.1 %forward.4 = (bf16[64,1536]{1,0:T(8,128)(2,1)S(1)}, f32[64,1664]{1,0:T(8,128)}, bf16[512,1536]{1,0:T(8,128)(2,1)}) custom-call(bf16[64,1536]{1,0:T(8,128)(2,1)S(1)} %get-tuple-element.143.refs_0_, bf16[64,1536]{1,0:T(8,128)(2,1)S(1)} %collective-permute-done.10.refs_1_, bf16[64,1536]{1,0:T(8,128)(2,1)S(1)} %collective-permute-done.11.refs_2_, ...), custom_call_target="tpu_custom_call" | custom-call | flops 905969664 | bytes 4478976 | tf_op jit(solution)/shard_map/forward/pallas_call | solution.py:858
  58.2 1.7 collective-permute-start.19
  61.7 1.1 pick.4.refs_8_
  62.8 4.1 %collective-permute-done.19.refs_3_ = bf16[64,1536]{1,0:T(8,128)(2,1)S(1)} collective-permute-done((bf16[64,1536]{1,0:T(8,128)(2,1)S(1)}, bf16[64,1536]{1,0:T(8,128)(2,1)S(1)}, u32[]{:S(2)}, u32[]{:S(2)}) %collective-permute-start.19) | collective-permute-done | bytes 196640 | tf_op jit(solution)/shard_map/ppermute | solution.py:250
  66.9 3.2 %collective-permute-done.17.refs_1_ = bf16[64,1536]{1,0:T(8,128)(2,1)S(1)} collective-permute-done((bf16[64,1536]{1,0:T(8,128)(2,1)S(1)}, bf16[64,1536]{1,0:T(8,128)(2,1)S(1)}, u32[]{:S(2)}, u32[]{:S(2)}) %collective-permute-start.17) | collective-permute-done | bytes 196640 | tf_op jit(solution)/shard_map/ppermute | solution.py:250
  71.8 2.4 %forward.5 = (bf16[64,1536]{1,0:T(8,128)(2,1)S(1)}, f32[64,1664]{1,0:T(8,128)}, bf16[512,1536]{1,0:T(8,128)(2,1)}) custom-call(bf16[64,1536]{1,0:T(8,128)(2,1)S(1)} %get-tuple-element.152.refs_0_, bf16[64,1536]{1,0:T(8,128)(2,1)S(1)} %collective-permute-done.17.refs_1_, bf16[64,1536]{1,0:T(8,128)(2,1)S(1)} %collective-permute-done.18.refs_2_, ...), custom_call_target="tpu_custom_call" | custom-call | flops 905969664 | bytes 4478976 | tf_op jit(solution)/shard_map/forward/pallas_call | solution.py:858
  74.3 1.2 collective-permute-start.24
  75.5 1.1 collective-permute-start.25
  76.6 1.2 collective-permute-start.26
  77.8 4.2 %collective-permute-done.24.refs_1_ = bf16[64,1536]{1,0:T(8,128)(2,1)S(1)} collective-permute-done((bf16[64,1536]{1,0:T(8,128)(2,1)S(1)}, bf16[64,1536]{1,0:T(8,128)(2,1)S(1)}, u32[]{:S(2)}, u32[]{:S(2)}) %collective-permute-start.24) | collective-permute-done | bytes 196640 | tf_op jit(solution)/shard_map/ppermute | solution.py:250
  82.1 4.4 %collective-permute-done.25.refs_2_ = bf16[64,1536]{1,0:T(8,128)(2,1)S(1)} collective-permute-done((bf16[64,1536]{1,0:T(8,128)(2,1)S(1)}, bf16[64,1536]{1,0:T(8,128)(2,1)S(1)}, u32[]{:S(2)}, u32[]{:S(2)}) %collective-permute-start.25) | collective-permute-done | bytes 196640 | tf_op jit(solution)/shard_map/ppermute | solution.py:250
  86.5 1.5 pick.5
  89.6 2.4 %turn.1 = (bf16[64,1536]{1,0:T(8,128)(2,1)}, bf16[512,1536]{1,0:T(8,128)(2,1)}, bf16[64,1536]{1,0:T(8,128)(2,1)S(1)}, f32[64,256]{1,0:T(8,128)S(1)}) custom-call(bf16[64,1536]{1,0:T(8,128)(2,1)S(1)} %get-tuple-element.158.refs_0_, bf16[64,1536]{1,0:T(8,128)(2,1)S(1)} %collective-permute-done.24.refs_1_, ...), custom_call_target="tpu_custom_call" | custom-call | flops 905969664 | bytes 4511744 | tf_op jit(solution)/shard_map/turn/pallas_call | solution.py:858
  92.5 1.1 collective-permute-done.32.other
  93.5 4.0 %conv_back.4 = (bf16[64,1536]{1,0:T(8,128)(2,1)S(1)}, bf16[64,1536]{1,0:T(8,128)(2,1)S(1)}, bf16[64,1536]{1,0:T(8,128)(2,1)S(1)}, bf16[64,1536]{1,0:T(8,128)(2,1)S(1)}, bf16[2368,128]{1,0:T(8,128)(2,1)}) custom-call(bf16[64,1536]{1,0:T(8,128)(2,1)S(1)} %get-tuple-element.168.own, bf16[64,1536]{1,0:T(8,128)(2,1)S(1)} %collective-permute-done.32.other, ...), custom_call_target="tpu_custom_call" | custom-call | flops 6000000000 | bytes 6144000 | tf_op jit(solution)/shard_map/conv_back/pallas_call | solution.py:858
  97.6 1.9 collective-permute-start.34
  99.5 1.6 collective-permute-start.35
  101.1 6.2 %all-to-all-start = ((bf16[4,592,128]{2,1,0:T(8,128)(2,1)}), bf16[4,592,128]{2,1,0:T(8,128)(2,1)S(1)}, u32[]{:S(2)}, u32[]{:S(2)}) async-start(bf16[4,592,128]{2,1,0:T(8,128)(2,1)} %bitcast.33), calls=%async_computation | async-start | bytes 1212416 | tf_op jit(solution)/shard_map/all_to_all | solution.py:1041
  108.4 1.1 collective-permute-done.35.refs_3_
  110.1 1.4 collective-permute-done.36.other
  111.5 4.0 %conv_back.5 = (bf16[64,1536]{1,0:T(8,128)(2,1)S(1)}, bf16[64,1536]{1,0:T(8,128)(2,1)S(1)}, bf16[64,1536]{1,0:T(8,128)(2,1)S(1)}, bf16[64,1536]{1,0:T(8,128)(2,1)S(1)}, bf16[2368,128]{1,0:T(8,128)(2,1)}) custom-call(bf16[64,1536]{1,0:T(8,128)(2,1)S(1)} %get-tuple-element.183.own, bf16[64,1536]{1,0:T(8,128)(2,1)S(1)} %collective-permute-done.36.other, ...), custom_call_target="tpu_custom_call" | custom-call | flops 6000000000 | bytes 6144000 | tf_op jit(solution)/shard_map/conv_back/pallas_call | solution.py:858
  115.5 1.4 collective-permute-start.37
  117.9 1.2 collective-permute-start.39
  119.0 4.2 %all-to-all-done = bf16[4,592,128]{2,1,0:T(8,128)(2,1)S(1)} async-done(((bf16[4,592,128]{2,1,0:T(8,128)(2,1)}), bf16[4,592,128]{2,1,0:T(8,128)(2,1)S(1)}, u32[]{:S(2)}, u32[]{:S(2)}) %all-to-all-start) | async-done | bytes 606240 | tf_op jit(solution)/shard_map/all_to_all | solution.py:1041
  123.2 3.5 %all-to-all-start.1 = ((bf16[4,592,128]{2,1,0:T(8,128)(2,1)}), bf16[4,592,128]{2,1,0:T(8,128)(2,1)S(1)}, u32[]{:S(2)}, u32[]{:S(2)}) async-start(bf16[4,592,128]{2,1,0:T(8,128)(2,1)} %bitcast.31), calls=%async_computation.1 | async-start | bytes 1212416 | tf_op jit(solution)/shard_map/all_to_all | solution.py:1041
  127.8 2.1 %norm_back.4 = (bf16[64,1536]{1,0:T(8,128)(2,1)S(1)}, f32[64,256]{1,0:T(8,128)S(1)}) custom-call(bf16[64,1536]{1,0:T(8,128)(2,1)S(1)} %get-tuple-element.186.refs_0_, bf16[64,1536]{1,0:T(8,128)(2,1)S(1)} %collective-permute-done.37.refs_1_, bf16[64,1536]{1,0:T(8,128)(2,1)S(1)} %collective-permute-done.38.refs_2_, ...), custom_call_target="tpu_custom_call" | custom-call | bytes 1595392 | tf_op jit(solution)/shard_map/norm_back/pallas_call | solution.py:858
  130.0 1.4 collective-permute-done.40.other
  131.4 4.0 %conv_back.6 = (bf16[64,1536]{1,0:T(8,128)(2,1)S(1)}, bf16[64,1536]{1,0:T(8,128)(2,1)S(1)}, bf16[64,1536]{1,0:T(8,128)(2,1)S(1)}, bf16[64,1536]{1,0:T(8,128)(2,1)S(1)}, bf16[2368,128]{1,0:T(8,128)(2,1)}) custom-call(bf16[64,1536]{1,0:T(8,128)(2,1)S(1)} %get-tuple-element.197.own, bf16[64,1536]{1,0:T(8,128)(2,1)S(1)} %collective-permute-done.40.other, ...), custom_call_target="tpu_custom_call" | custom-call | flops 6000000000 | bytes 6144000 | tf_op jit(solution)/shard_map/conv_back/pallas_call | solution.py:858
  136.1 1.1 collective-permute-start.42
  137.2 1.7 collective-permute-start.43
  138.9 3.5 %all-to-all-done.1 = bf16[4,592,128]{2,1,0:T(8,128)(2,1)S(1)} async-done(((bf16[4,592,128]{2,1,0:T(8,128)(2,1)}), bf16[4,592,128]{2,1,0:T(8,128)(2,1)S(1)}, u32[]{:S(2)}, u32[]{:S(2)}) %all-to-all-start.1) | async-done | bytes 606240 | tf_op jit(solution)/shard_map/all_to_all | solution.py:1041
  142.4 3.7 %all-to-all-start.2 = ((bf16[4,592,128]{2,1,0:T(8,128)(2,1)}), bf16[4,592,128]{2,1,0:T(8,128)(2,1)S(1)}, u32[]{:S(2)}, u32[]{:S(2)}) async-start(bf16[4,592,128]{2,1,0:T(8,128)(2,1)} %bitcast.34), calls=%async_computation.2 | async-start | bytes 1212416 | tf_op jit(solution)/shard_map/all_to_all | solution.py:1041
  147.9 1.4 collective-permute-done.44.other
  149.3 3.9 %conv_back.7 = (bf16[64,1536]{1,0:T(8,128)(2,1)S(1)}, bf16[64,1536]{1,0:T(8,128)(2,1)S(1)}, bf16[64,1536]{1,0:T(8,128)(2,1)S(1)}, bf16[64,1536]{1,0:T(8,128)(2,1)S(1)}, bf16[2368,128]{1,0:T(8,128)(2,1)}) custom-call(bf16[64,1536]{1,0:T(8,128)(2,1)S(1)} %get-tuple-element.211.own, bf16[64,1536]{1,0:T(8,128)(2,1)S(1)} %collective-permute-done.44.other, ...), custom_call_target="tpu_custom_call" | custom-call | flops 6000000000 | bytes 6144000 | tf_op jit(solution)/shard_map/conv_back/pallas_call | solution.py:858
  153.2 8.4 %all-to-all-done.2 = bf16[4,592,128]{2,1,0:T(8,128)(2,1)S(1)} async-done(((bf16[4,592,128]{2,1,0:T(8,128)(2,1)}), bf16[4,592,128]{2,1,0:T(8,128)(2,1)S(1)}, u32[]{:S(2)}, u32[]{:S(2)}) %all-to-all-start.2) | async-done | bytes 606240 | tf_op jit(solution)/shard_map/all_to_all | solution.py:1041
  161.6 3.5 %all-to-all-start.3 = ((bf16[4,592,128]{2,1,0:T(8,128)(2,1)}), bf16[4,592,128]{2,1,0:T(8,128)(2,1)S(1)}, u32[]{:S(2)}, u32[]{:S(2)}) async-start(bf16[4,592,128]{2,1,0:T(8,128)(2,1)} %bitcast.32), calls=%async_computation.3 | async-start | bytes 1212416 | tf_op jit(solution)/shard_map/all_to_all | solution.py:1041
  166.6 2.1 %collective-permute-start.47 = (bf16[64,1536]{1,0:T(8,128)(2,1)S(1)}, bf16[64,1536]{1,0:T(8,128)(2,1)S(1)}, u32[]{:S(2)}, u32[]{:S(2)}) collective-permute-start(bf16[64,1536]{1,0:T(8,128)(2,1)S(1)} %get-tuple-element.217), channel_id=1, source_target_pairs={{0,24},{1,25},{2,26},{3,27},{4,28},{5,29},{6,30},{7,31},{8,16},{9,... | collective-permute-start | bytes 589832 | tf_op jit(solution)/shard_map/ppermute | solution.py:250
  168.7 4.3 %collective-permute-done.45.refs_1_ = bf16[64,1536]{1,0:T(8,128)(2,1)S(1)} collective-permute-done((bf16[64,1536]{1,0:T(8,128)(2,1)S(1)}, bf16[64,1536]{1,0:T(8,128)(2,1)S(1)}, u32[]{:S(2)}, u32[]{:S(2)}) %collective-permute-start.45) | collective-permute-done | bytes 196640 | tf_op jit(solution)/shard_map/ppermute | solution.py:250
  173.0 2.7 %collective-permute-done.47.refs_3_ = bf16[64,1536]{1,0:T(8,128)(2,1)S(1)} collective-permute-done((bf16[64,1536]{1,0:T(8,128)(2,1)S(1)}, bf16[64,1536]{1,0:T(8,128)(2,1)S(1)}, u32[]{:S(2)}, u32[]{:S(2)}) %collective-permute-start.47) | collective-permute-done | bytes 196640 | tf_op jit(solution)/shard_map/ppermute | solution.py:250
  176.8 1.4 collective-permute-done.48.got
  178.9 4.0 %collective-permute-start.50 = (bf16[256,384]{1,0:T(8,128)(2,1)S(1)}, bf16[256,384]{1,0:T(8,128)(2,1)S(1)}, u32[]{:S(2)}, u32[]{:S(2)}) collective-permute-start(bf16[256,384]{1,0:T(8,128)(2,1)S(1)} %get-tuple-element.225), channel_id=1, source_target_pairs={{0,2},{1,7},{2,10},{3,15},{4,18},{5,23},{6,26},{7,31},{8,0},{9,5},... | collective-permute-start | bytes 589832 | tf_op jit(solution)/shard_map/ppermute | solution.py:250
  183.8 1.8 choose.1
  186.0 3.4 %collective-permute-start.54 = (bf16[592,128]{1,0:T(8,128)(2,1)S(1)}, bf16[592,128]{1,0:T(8,128)(2,1)S(1)}, u32[]{:S(2)}, u32[]{:S(2)}) collective-permute-start(bf16[592,128]{1,0:T(8,128)(2,1)S(1)} %get-tuple-element.235), channel_id=1, source_target_pairs={{0,16},{1,17},{2,18},{3,19},{4,20},{5,21},{6,22},{7,23},{8,24},{9,... | collective-permute-start | bytes 454664 | tf_op jit(solution)/shard_map/ppermute | solution.py:250
  189.4 1.4 collective-permute-start.55
  191.5 1.4 collective-permute-done.53.refs_1_
  193.9 4.5 %collective-permute-done.55.refs_3_ = bf16[592,128]{1,0:T(8,128)(2,1)S(1)} collective-permute-done((bf16[592,128]{1,0:T(8,128)(2,1)S(1)}, bf16[592,128]{1,0:T(8,128)(2,1)S(1)}, u32[]{:S(2)}, u32[]{:S(2)}) %collective-permute-start.55) | collective-permute-done | bytes 151584 | tf_op jit(solution)/shard_map/ppermute | solution.py:250
  198.4 1.2 maps_out.1
  201.7 1.6 grads_out.1
  (105 shorter events, 25.2 us)
Async XLA Ops:
  4.2 28.6 %collective-permute-start.7 = (bf16[592,512]{1,0:T(8,128)(2,1)S(1)}, bf16[592,512]{1,0:T(8,128)(2,1)}, u32[]{:S(2)}, u32[]{:S(2)}) collective-permute-start(bf16[592,512]{1,0:T(8,128)(2,1)S(1)} %get-tuple-element.129), channel_id=1, source_target_pairs={{0,8},{1,9},{2,10},{3,11},{4,12},{5,13},{6,14},{7,15},{8,0},{9,1},... | collective-permute-start | bytes 1818632 | tf_op jit(solution)/shard_map/ppermute | solution.py:250
  7.3 28.3 %collective-permute-start.8 = (bf16[592,512]{1,0:T(8,128)(2,1)S(1)}, bf16[592,512]{1,0:T(8,128)(2,1)}, u32[]{:S(2)}, u32[]{:S(2)}) collective-permute-start(bf16[592,512]{1,0:T(8,128)(2,1)S(1)} %get-tuple-element.130), channel_id=1, source_target_pairs={{0,16},{1,17},{2,18},{3,19},{4,20},{5,21},{6,22},{7,23},{8,24},{9,... | collective-permute-start | bytes 1818632 | tf_op jit(solution)/shard_map/ppermute | solution.py:250
  10.6 13.1 %collective-permute-start = (bf16[208,640]{1,0:T(8,128)(2,1)S(1)}, bf16[208,640]{1,0:T(8,128)(2,1)S(1)}, u32[]{:S(2)}, u32[]{:S(2)}) collective-permute-start(bf16[208,640]{1,0:T(8,128)(2,1)S(1)} %get-tuple-element.134), channel_id=1, source_target_pairs={{0,2},{1,3},{2,0},{3,1},{4,6},{5,7},{6,4},{7,5},{8,10},{9,11},{10,... | collective-permute-start | bytes 798728 | tf_op jit(solution)/shard_map/ppermute | solution.py:250
  12.2 23.4 %collective-permute-start.9 = (bf16[592,512]{1,0:T(8,128)(2,1)S(1)}, bf16[592,512]{1,0:T(8,128)(2,1)}, u32[]{:S(2)}, u32[]{:S(2)}) collective-permute-start(bf16[592,512]{1,0:T(8,128)(2,1)S(1)} %get-tuple-element.131), channel_id=1, source_target_pairs={{0,24},{1,25},{2,26},{3,27},{4,28},{5,29},{6,30},{7,31},{8,16},{9,... | collective-permute-start | bytes 1818632 | tf_op jit(solution)/shard_map/ppermute | solution.py:250
  12.7 19.6 %collective-permute-start.1 = (bf16[208,640]{1,0:T(8,128)(2,1)S(1)}, bf16[208,640]{1,0:T(8,128)(2,1)S(1)}, u32[]{:S(2)}, u32[]{:S(2)}) collective-permute-start(bf16[208,640]{1,0:T(8,128)(2,1)S(1)} %get-tuple-element.135), channel_id=1, source_target_pairs={{0,4},{1,5},{2,6},{3,7},{4,0},{5,1},{6,2},{7,3},{8,12},{9,13},{10,... | collective-permute-start | bytes 798728 | tf_op jit(solution)/shard_map/ppermute | solution.py:250
  23.7 8.6 %collective-permute-start.2 = (bf16[208,640]{1,0:T(8,128)(2,1)S(1)}, bf16[208,640]{1,0:T(8,128)(2,1)S(1)}, u32[]{:S(2)}, u32[]{:S(2)}) collective-permute-start(bf16[208,640]{1,0:T(8,128)(2,1)S(1)} %get-tuple-element.136), channel_id=1, source_target_pairs={{0,6},{1,7},{2,4},{3,5},{4,2},{5,3},{6,0},{7,1},{8,14},{9,15},{10,... | collective-permute-start | bytes 798728 | tf_op jit(solution)/shard_map/ppermute | solution.py:250
  32.3 3.3 %collective-permute-start.3 = (bf16[208,640]{1,0:T(8,128)(2,1)S(1)}, bf16[208,640]{1,0:T(8,128)(2,1)S(1)}, u32[]{:S(2)}, u32[]{:S(2)}) collective-permute-start(bf16[208,640]{1,0:T(8,128)(2,1)S(1)} %get-tuple-element.133.refs_0_), channel_id=1, source_target_pairs={{0,1},{1,0},{2,3},{3,2},{4,5},{5,4},{6,7},{7,6},{8,9},{9,8},{10,11... | collective-permute-start | bytes 798728 | tf_op jit(solution)/shard_map/ppermute | solution.py:250
  32.3 3.3 %collective-permute-start.4 = (bf16[208,640]{1,0:T(8,128)(2,1)S(1)}, bf16[208,640]{1,0:T(8,128)(2,1)S(1)}, u32[]{:S(2)}, u32[]{:S(2)}) collective-permute-start(bf16[208,640]{1,0:T(8,128)(2,1)S(1)} %collective-permute-done.refs_1_), channel_id=1, source_target_pairs={{0,1},{1,0},{2,3},{3,2},{4,5},{5,4},{6,7},{7,6},{8,9},{9,8},{10,11... | collective-permute-start | bytes 798728 | tf_op jit(solution)/shard_map/ppermute | solution.py:250
  32.8 2.8 %collective-permute-start.5 = (bf16[208,640]{1,0:T(8,128)(2,1)S(1)}, bf16[208,640]{1,0:T(8,128)(2,1)S(1)}, u32[]{:S(2)}, u32[]{:S(2)}) collective-permute-start(bf16[208,640]{1,0:T(8,128)(2,1)S(1)} %collective-permute-done.1.refs_2_), channel_id=1, source_target_pairs={{0,1},{1,0},{2,3},{3,2},{4,5},{5,4},{6,7},{7,6},{8,9},{9,8},{10,11... | collective-permute-start | bytes 798728 | tf_op jit(solution)/shard_map/ppermute | solution.py:250
  35.6 1.5 collective-permute-start.6
  40.9 8.8 %collective-permute-start.12 = (bf16[64,1536]{1,0:T(8,128)(2,1)S(1)}, bf16[64,1536]{1,0:T(8,128)(2,1)S(1)}, u32[]{:S(2)}, u32[]{:S(2)}) collective-permute-start(bf16[64,1536]{1,0:T(8,128)(2,1)S(1)} %get-tuple-element.143.refs_0_), channel_id=1, source_target_pairs={{0,24},{1,25},{2,26},{3,27},{4,28},{5,29},{6,30},{7,31},{8,16},{9,... | collective-permute-start | bytes 589832 | tf_op jit(solution)/shard_map/ppermute | solution.py:250
  43.0 10.0 %collective-permute-start.10 = (bf16[64,1536]{1,0:T(8,128)(2,1)S(1)}, bf16[64,1536]{1,0:T(8,128)(2,1)S(1)}, u32[]{:S(2)}, u32[]{:S(2)}) collective-permute-start(bf16[64,1536]{1,0:T(8,128)(2,1)S(1)} %get-tuple-element.143.refs_0_), channel_id=1, source_target_pairs={{0,8},{1,9},{2,10},{3,11},{4,12},{5,13},{6,14},{7,15},{8,0},{9,1},... | collective-permute-start | bytes 589832 | tf_op jit(solution)/shard_map/ppermute | solution.py:250
  43.9 9.2 %collective-permute-start.11 = (bf16[64,1536]{1,0:T(8,128)(2,1)S(1)}, bf16[64,1536]{1,0:T(8,128)(2,1)S(1)}, u32[]{:S(2)}, u32[]{:S(2)}) collective-permute-start(bf16[64,1536]{1,0:T(8,128)(2,1)S(1)} %get-tuple-element.143.refs_0_), channel_id=1, source_target_pairs={{0,16},{1,17},{2,18},{3,19},{4,20},{5,21},{6,22},{7,23},{8,24},{9,... | collective-permute-start | bytes 589832 | tf_op jit(solution)/shard_map/ppermute | solution.py:250
  49.4 4.2 %collective-permute-start.13 = (bf16[64,1536]{1,0:T(8,128)(2,1)S(1)}, bf16[64,1536]{1,0:T(8,128)(2,1)S(1)}, u32[]{:S(2)}, u32[]{:S(2)}) collective-permute-start(bf16[64,1536]{1,0:T(8,128)(2,1)S(1)} %get-tuple-element.143.refs_0_), channel_id=1, source_target_pairs={{0,1},{1,0},{2,3},{3,2},{4,5},{5,4},{6,7},{7,6},{8,9},{9,8},{10,11... | collective-permute-start | bytes 589832 | tf_op jit(solution)/shard_map/ppermute | solution.py:250
  49.6 4.0 %collective-permute-start.16 = (bf16[64,1536]{1,0:T(8,128)(2,1)S(1)}, bf16[64,1536]{1,0:T(8,128)(2,1)S(1)}, u32[]{:S(2)}, u32[]{:S(2)}) collective-permute-start(bf16[64,1536]{1,0:T(8,128)(2,1)S(1)} %collective-permute-done.12.refs_3_), channel_id=1, source_target_pairs={{0,1},{1,0},{2,3},{3,2},{4,5},{5,4},{6,7},{7,6},{8,9},{9,8},{10,11... | collective-permute-start | bytes 589832 | tf_op jit(solution)/shard_map/ppermute | solution.py:250
  53.1 1.4 collective-permute-start.14
  53.1 1.7 collective-permute-start.15
  57.9 28.6 %collective-permute-start.27 = (bf16[1024,640]{1,0:T(8,128)(2,1)S(1)}, bf16[1024,640]{1,0:T(8,128)(2,1)S(1)}, u32[]{:S(2)}, u32[]{:S(2)}) collective-permute-start(bf16[1024,640]{1,0:T(8,128)(2,1)S(1)} %copy-done.5), channel_id=1, source_target_pairs={{0,1},{1,0},{2,3},{3,2},{4,5},{5,4},{6,7},{7,6},{8,9},{9,8},{10,11... | collective-permute-start | bytes 3932168 | tf_op jit(solution)/shard_map/ppermute | solution.py:250
  58.2 8.7 %collective-permute-start.19 = (bf16[64,1536]{1,0:T(8,128)(2,1)S(1)}, bf16[64,1536]{1,0:T(8,128)(2,1)S(1)}, u32[]{:S(2)}, u32[]{:S(2)}) collective-permute-start(bf16[64,1536]{1,0:T(8,128)(2,1)S(1)} %get-tuple-element.152.refs_0_), channel_id=1, source_target_pairs={{0,24},{1,25},{2,26},{3,27},{4,28},{5,29},{6,30},{7,31},{8,16},{9,... | collective-permute-start | bytes 589832 | tf_op jit(solution)/shard_map/ppermute | solution.py:250
  59.8 10.3 %collective-permute-start.17 = (bf16[64,1536]{1,0:T(8,128)(2,1)S(1)}, bf16[64,1536]{1,0:T(8,128)(2,1)S(1)}, u32[]{:S(2)}, u32[]{:S(2)}) collective-permute-start(bf16[64,1536]{1,0:T(8,128)(2,1)S(1)} %get-tuple-element.152.refs_0_), channel_id=1, source_target_pairs={{0,8},{1,9},{2,10},{3,11},{4,12},{5,13},{6,14},{7,15},{8,0},{9,1},... | collective-permute-start | bytes 589832 | tf_op jit(solution)/shard_map/ppermute | solution.py:250
  60.7 9.7 %collective-permute-start.18 = (bf16[64,1536]{1,0:T(8,128)(2,1)S(1)}, bf16[64,1536]{1,0:T(8,128)(2,1)S(1)}, u32[]{:S(2)}, u32[]{:S(2)}) collective-permute-start(bf16[64,1536]{1,0:T(8,128)(2,1)S(1)} %get-tuple-element.152.refs_0_), channel_id=1, source_target_pairs={{0,16},{1,17},{2,18},{3,19},{4,20},{5,21},{6,22},{7,23},{8,24},{9,... | collective-permute-start | bytes 589832 | tf_op jit(solution)/shard_map/ppermute | solution.py:250
  61.7 8.9 %collective-permute-start.20 = (bf16[64,1536]{1,0:T(8,128)(2,1)S(1)}, bf16[64,1536]{1,0:T(8,128)(2,1)S(1)}, u32[]{:S(2)}, u32[]{:S(2)}) collective-permute-start(bf16[64,1536]{1,0:T(8,128)(2,1)S(1)} %get-tuple-element.152.refs_0_), channel_id=1, source_target_pairs={{0,1},{1,0},{2,3},{3,2},{4,5},{5,4},{6,7},{7,6},{8,9},{9,8},{10,11... | collective-permute-start | bytes 589832 | tf_op jit(solution)/shard_map/ppermute | solution.py:250
  66.9 3.8 %collective-permute-start.23 = (bf16[64,1536]{1,0:T(8,128)(2,1)S(1)}, bf16[64,1536]{1,0:T(8,128)(2,1)S(1)}, u32[]{:S(2)}, u32[]{:S(2)}) collective-permute-start(bf16[64,1536]{1,0:T(8,128)(2,1)S(1)} %collective-permute-done.19.refs_3_), channel_id=1, source_target_pairs={{0,1},{1,0},{2,3},{3,2},{4,5},{5,4},{6,7},{7,6},{8,9},{9,8},{10,11... | collective-permute-start | bytes 589832 | tf_op jit(solution)/shard_map/ppermute | solution.py:250
  70.1 1.4 collective-permute-start.21
  70.4 1.4 collective-permute-start.22
  74.3 7.8 %collective-permute-start.24 = (bf16[64,1536]{1,0:T(8,128)(2,1)S(1)}, bf16[64,1536]{1,0:T(8,128)(2,1)S(1)}, u32[]{:S(2)}, u32[]{:S(2)}) collective-permute-start(bf16[64,1536]{1,0:T(8,128)(2,1)S(1)} %get-tuple-element.158.refs_0_), channel_id=1, source_target_pairs={{0,8},{1,9},{2,10},{3,11},{4,12},{5,13},{6,14},{7,15},{8,0},{9,1},... | collective-permute-start | bytes 589832 | tf_op jit(solution)/shard_map/ppermute | solution.py:250
  75.5 11.0 %collective-permute-start.25 = (bf16[64,1536]{1,0:T(8,128)(2,1)S(1)}, bf16[64,1536]{1,0:T(8,128)(2,1)S(1)}, u32[]{:S(2)}, u32[]{:S(2)}) collective-permute-start(bf16[64,1536]{1,0:T(8,128)(2,1)S(1)} %get-tuple-element.158.refs_0_), channel_id=1, source_target_pairs={{0,16},{1,17},{2,18},{3,19},{4,20},{5,21},{6,22},{7,23},{8,24},{9,... | collective-permute-start | bytes 589832 | tf_op jit(solution)/shard_map/ppermute | solution.py:250
  76.6 11.3 %collective-permute-start.26 = (bf16[64,1536]{1,0:T(8,128)(2,1)S(1)}, bf16[64,1536]{1,0:T(8,128)(2,1)S(1)}, u32[]{:S(2)}, u32[]{:S(2)}) collective-permute-start(bf16[64,1536]{1,0:T(8,128)(2,1)S(1)} %get-tuple-element.158.refs_0_), channel_id=1, source_target_pairs={{0,24},{1,25},{2,26},{3,27},{4,28},{5,29},{6,30},{7,31},{8,16},{9,... | collective-permute-start | bytes 589832 | tf_op jit(solution)/shard_map/ppermute | solution.py:250
  77.8 10.7 %collective-permute-start.28 = (bf16[64,1536]{1,0:T(8,128)(2,1)S(1)}, bf16[64,1536]{1,0:T(8,128)(2,1)S(1)}, u32[]{:S(2)}, u32[]{:S(2)}) collective-permute-start(bf16[64,1536]{1,0:T(8,128)(2,1)S(1)} %get-tuple-element.158.refs_0_), channel_id=1, source_target_pairs={{0,1},{1,0},{2,3},{3,2},{4,5},{5,4},{6,7},{7,6},{8,9},{9,8},{10,11... | collective-permute-start | bytes 589832 | tf_op jit(solution)/shard_map/ppermute | solution.py:250
  82.1 6.5 %collective-permute-start.29 = (bf16[64,1536]{1,0:T(8,128)(2,1)S(1)}, bf16[64,1536]{1,0:T(8,128)(2,1)S(1)}, u32[]{:S(2)}, u32[]{:S(2)}) collective-permute-start(bf16[64,1536]{1,0:T(8,128)(2,1)S(1)} %collective-permute-done.24.refs_1_), channel_id=1, source_target_pairs={{0,1},{1,0},{2,3},{3,2},{4,5},{5,4},{6,7},{7,6},{8,9},{9,8},{10,11... | collective-permute-start | bytes 589832 | tf_op jit(solution)/shard_map/ppermute | solution.py:250
  86.5 2.1 %collective-permute-start.30 = (bf16[64,1536]{1,0:T(8,128)(2,1)S(1)}, bf16[64,1536]{1,0:T(8,128)(2,1)S(1)}, u32[]{:S(2)}, u32[]{:S(2)}) collective-permute-start(bf16[64,1536]{1,0:T(8,128)(2,1)S(1)} %collective-permute-done.25.refs_2_), channel_id=1, source_target_pairs={{0,1},{1,0},{2,3},{3,2},{4,5},{5,4},{6,7},{7,6},{8,9},{9,8},{10,11... | collective-permute-start | bytes 589832 | tf_op jit(solution)/shard_map/ppermute | solution.py:250
  88.0 1.6 collective-permute-start.31
  92.0 1.5 collective-permute-start.32
  97.5 10.8 %collective-permute-start.33 = (bf16[64,1536]{1,0:T(8,128)(2,1)S(1)}, bf16[64,1536]{1,0:T(8,128)(2,1)S(1)}, u32[]{:S(2)}, u32[]{:S(2)}) collective-permute-start(bf16[64,1536]{1,0:T(8,128)(2,1)S(1)} %get-tuple-element.173), channel_id=1, source_target_pairs={{0,8},{1,9},{2,10},{3,11},{4,12},{5,13},{6,14},{7,15},{8,0},{9,1},... | collective-permute-start | bytes 589832 | tf_op jit(solution)/shard_map/ppermute | solution.py:250
  97.6 10.8 %collective-permute-start.34 = (bf16[64,1536]{1,0:T(8,128)(2,1)S(1)}, bf16[64,1536]{1,0:T(8,128)(2,1)S(1)}, u32[]{:S(2)}, u32[]{:S(2)}) collective-permute-start(bf16[64,1536]{1,0:T(8,128)(2,1)S(1)} %get-tuple-element.174), channel_id=1, source_target_pairs={{0,16},{1,17},{2,18},{3,19},{4,20},{5,21},{6,22},{7,23},{8,24},{9,... | collective-permute-start | bytes 589832 | tf_op jit(solution)/shard_map/ppermute | solution.py:250
  99.5 10.0 %collective-permute-start.35 = (bf16[64,1536]{1,0:T(8,128)(2,1)S(1)}, bf16[64,1536]{1,0:T(8,128)(2,1)S(1)}, u32[]{:S(2)}, u32[]{:S(2)}) collective-permute-start(bf16[64,1536]{1,0:T(8,128)(2,1)S(1)} %get-tuple-element.175), channel_id=1, source_target_pairs={{0,24},{1,25},{2,26},{3,27},{4,28},{5,29},{6,30},{7,31},{8,16},{9,... | collective-permute-start | bytes 589832 | tf_op jit(solution)/shard_map/ppermute | solution.py:250
  101.1 22.2 %all-to-all-start = ((bf16[4,592,128]{2,1,0:T(8,128)(2,1)}), bf16[4,592,128]{2,1,0:T(8,128)(2,1)S(1)}, u32[]{:S(2)}, u32[]{:S(2)}) async-start(bf16[4,592,128]{2,1,0:T(8,128)(2,1)} %bitcast.33), calls=%async_computation | async-start | bytes 1212416 | tf_op jit(solution)/shard_map/all_to_all | solution.py:1041
  110.0 1.5 collective-permute-start.36
  115.5 12.3 %collective-permute-start.37 = (bf16[64,1536]{1,0:T(8,128)(2,1)S(1)}, bf16[64,1536]{1,0:T(8,128)(2,1)S(1)}, u32[]{:S(2)}, u32[]{:S(2)}) collective-permute-start(bf16[64,1536]{1,0:T(8,128)(2,1)S(1)} %get-tuple-element.187), channel_id=1, source_target_pairs={{0,8},{1,9},{2,10},{3,11},{4,12},{5,13},{6,14},{7,15},{8,0},{9,1},... | collective-permute-start | bytes 589832 | tf_op jit(solution)/shard_map/ppermute | solution.py:250
  116.8 11.0 %collective-permute-start.38 = (bf16[64,1536]{1,0:T(8,128)(2,1)S(1)}, bf16[64,1536]{1,0:T(8,128)(2,1)S(1)}, u32[]{:S(2)}, u32[]{:S(2)}) collective-permute-start(bf16[64,1536]{1,0:T(8,128)(2,1)S(1)} %get-tuple-element.188), channel_id=1, source_target_pairs={{0,16},{1,17},{2,18},{3,19},{4,20},{5,21},{6,22},{7,23},{8,24},{9,... | collective-permute-start | bytes 589832 | tf_op jit(solution)/shard_map/ppermute | solution.py:250
  117.9 9.9 %collective-permute-start.39 = (bf16[64,1536]{1,0:T(8,128)(2,1)S(1)}, bf16[64,1536]{1,0:T(8,128)(2,1)S(1)}, u32[]{:S(2)}, u32[]{:S(2)}) collective-permute-start(bf16[64,1536]{1,0:T(8,128)(2,1)S(1)} %get-tuple-element.189), channel_id=1, source_target_pairs={{0,24},{1,25},{2,26},{3,27},{4,28},{5,29},{6,30},{7,31},{8,16},{9,... | collective-permute-start | bytes 589832 | tf_op jit(solution)/shard_map/ppermute | solution.py:250
  123.2 19.2 %all-to-all-start.1 = ((bf16[4,592,128]{2,1,0:T(8,128)(2,1)}), bf16[4,592,128]{2,1,0:T(8,128)(2,1)S(1)}, u32[]{:S(2)}, u32[]{:S(2)}) async-start(bf16[4,592,128]{2,1,0:T(8,128)(2,1)} %bitcast.31), calls=%async_computation.1 | async-start | bytes 1212416 | tf_op jit(solution)/shard_map/all_to_all | solution.py:1041
  129.9 1.5 collective-permute-start.40
  135.4 11.8 %collective-permute-start.41 = (bf16[64,1536]{1,0:T(8,128)(2,1)S(1)}, bf16[64,1536]{1,0:T(8,128)(2,1)S(1)}, u32[]{:S(2)}, u32[]{:S(2)}) collective-permute-start(bf16[64,1536]{1,0:T(8,128)(2,1)S(1)} %get-tuple-element.201), channel_id=1, source_target_pairs={{0,8},{1,9},{2,10},{3,11},{4,12},{5,13},{6,14},{7,15},{8,0},{9,1},... | collective-permute-start | bytes 589832 | tf_op jit(solution)/shard_map/ppermute | solution.py:250
  136.1 11.1 %collective-permute-start.42 = (bf16[64,1536]{1,0:T(8,128)(2,1)S(1)}, bf16[64,1536]{1,0:T(8,128)(2,1)S(1)}, u32[]{:S(2)}, u32[]{:S(2)}) collective-permute-start(bf16[64,1536]{1,0:T(8,128)(2,1)S(1)} %get-tuple-element.202), channel_id=1, source_target_pairs={{0,16},{1,17},{2,18},{3,19},{4,20},{5,21},{6,22},{7,23},{8,24},{9,... | collective-permute-start | bytes 589832 | tf_op jit(solution)/shard_map/ppermute | solution.py:250
  137.2 10.0 %collective-permute-start.43 = (bf16[64,1536]{1,0:T(8,128)(2,1)S(1)}, bf16[64,1536]{1,0:T(8,128)(2,1)S(1)}, u32[]{:S(2)}, u32[]{:S(2)}) collective-permute-start(bf16[64,1536]{1,0:T(8,128)(2,1)S(1)} %get-tuple-element.203), channel_id=1, source_target_pairs={{0,24},{1,25},{2,26},{3,27},{4,28},{5,29},{6,30},{7,31},{8,16},{9,... | collective-permute-start | bytes 589832 | tf_op jit(solution)/shard_map/ppermute | solution.py:250
  142.4 19.2 %all-to-all-start.2 = ((bf16[4,592,128]{2,1,0:T(8,128)(2,1)}), bf16[4,592,128]{2,1,0:T(8,128)(2,1)S(1)}, u32[]{:S(2)}, u32[]{:S(2)}) async-start(bf16[4,592,128]{2,1,0:T(8,128)(2,1)} %bitcast.34), calls=%async_computation.2 | async-start | bytes 1212416 | tf_op jit(solution)/shard_map/all_to_all | solution.py:1041
  147.8 1.5 collective-permute-start.44
  161.6 21.3 %all-to-all-start.3 = ((bf16[4,592,128]{2,1,0:T(8,128)(2,1)}), bf16[4,592,128]{2,1,0:T(8,128)(2,1)S(1)}, u32[]{:S(2)}, u32[]{:S(2)}) async-start(bf16[4,592,128]{2,1,0:T(8,128)(2,1)} %bitcast.32), calls=%async_computation.3 | async-start | bytes 1212416 | tf_op jit(solution)/shard_map/all_to_all | solution.py:1041
  165.1 7.9 %collective-permute-start.45 = (bf16[64,1536]{1,0:T(8,128)(2,1)S(1)}, bf16[64,1536]{1,0:T(8,128)(2,1)S(1)}, u32[]{:S(2)}, u32[]{:S(2)}) collective-permute-start(bf16[64,1536]{1,0:T(8,128)(2,1)S(1)} %get-tuple-element.215), channel_id=1, source_target_pairs={{0,8},{1,9},{2,10},{3,11},{4,12},{5,13},{6,14},{7,15},{8,0},{9,1},... | collective-permute-start | bytes 589832 | tf_op jit(solution)/shard_map/ppermute | solution.py:250
  165.5 7.5 %collective-permute-start.46 = (bf16[64,1536]{1,0:T(8,128)(2,1)S(1)}, bf16[64,1536]{1,0:T(8,128)(2,1)S(1)}, u32[]{:S(2)}, u32[]{:S(2)}) collective-permute-start(bf16[64,1536]{1,0:T(8,128)(2,1)S(1)} %get-tuple-element.216), channel_id=1, source_target_pairs={{0,16},{1,17},{2,18},{3,19},{4,20},{5,21},{6,22},{7,23},{8,24},{9,... | collective-permute-start | bytes 589832 | tf_op jit(solution)/shard_map/ppermute | solution.py:250
  166.6 9.1 %collective-permute-start.47 = (bf16[64,1536]{1,0:T(8,128)(2,1)S(1)}, bf16[64,1536]{1,0:T(8,128)(2,1)S(1)}, u32[]{:S(2)}, u32[]{:S(2)}) collective-permute-start(bf16[64,1536]{1,0:T(8,128)(2,1)S(1)} %get-tuple-element.217), channel_id=1, source_target_pairs={{0,24},{1,25},{2,26},{3,27},{4,28},{5,29},{6,30},{7,31},{8,16},{9,... | collective-permute-start | bytes 589832 | tf_op jit(solution)/shard_map/ppermute | solution.py:250
  176.7 1.5 collective-permute-start.48
  178.2 12.6 %collective-permute-start.49 = (bf16[256,384]{1,0:T(8,128)(2,1)S(1)}, bf16[256,384]{1,0:T(8,128)(2,1)S(1)}, u32[]{:S(2)}, u32[]{:S(2)}) collective-permute-start(bf16[256,384]{1,0:T(8,128)(2,1)S(1)} %get-tuple-element.224), channel_id=1, source_target_pairs={{0,0},{1,5},{2,8},{3,13},{4,16},{5,21},{6,24},{7,29},{8,2},{9,7},{... | collective-permute-start | bytes 589832 | tf_op jit(solution)/shard_map/ppermute | solution.py:250
  178.9 11.9 %collective-permute-start.50 = (bf16[256,384]{1,0:T(8,128)(2,1)S(1)}, bf16[256,384]{1,0:T(8,128)(2,1)S(1)}, u32[]{:S(2)}, u32[]{:S(2)}) collective-permute-start(bf16[256,384]{1,0:T(8,128)(2,1)S(1)} %get-tuple-element.225), channel_id=1, source_target_pairs={{0,2},{1,7},{2,10},{3,15},{4,18},{5,23},{6,26},{7,31},{8,0},{9,5},... | collective-permute-start | bytes 589832 | tf_op jit(solution)/shard_map/ppermute | solution.py:250
  185.6 7.3 %collective-permute-start.53 = (bf16[592,128]{1,0:T(8,128)(2,1)S(1)}, bf16[592,128]{1,0:T(8,128)(2,1)S(1)}, u32[]{:S(2)}, u32[]{:S(2)}) collective-permute-start(bf16[592,128]{1,0:T(8,128)(2,1)S(1)} %get-tuple-element.234), channel_id=1, source_target_pairs={{0,8},{1,9},{2,10},{3,11},{4,12},{5,13},{6,14},{7,15},{8,0},{9,1},... | collective-permute-start | bytes 454664 | tf_op jit(solution)/shard_map/ppermute | solution.py:250
  186.0 7.9 %collective-permute-start.54 = (bf16[592,128]{1,0:T(8,128)(2,1)S(1)}, bf16[592,128]{1,0:T(8,128)(2,1)S(1)}, u32[]{:S(2)}, u32[]{:S(2)}) collective-permute-start(bf16[592,128]{1,0:T(8,128)(2,1)S(1)} %get-tuple-element.235), channel_id=1, source_target_pairs={{0,16},{1,17},{2,18},{3,19},{4,20},{5,21},{6,22},{7,23},{8,24},{9,... | collective-permute-start | bytes 454664 | tf_op jit(solution)/shard_map/ppermute | solution.py:250
  189.4 8.9 %collective-permute-start.55 = (bf16[592,128]{1,0:T(8,128)(2,1)S(1)}, bf16[592,128]{1,0:T(8,128)(2,1)S(1)}, u32[]{:S(2)}, u32[]{:S(2)}) collective-permute-start(bf16[592,128]{1,0:T(8,128)(2,1)S(1)} %get-tuple-element.236), channel_id=1, source_target_pairs={{0,24},{1,25},{2,26},{3,27},{4,28},{5,29},{6,30},{7,31},{8,16},{9,... | collective-permute-start | bytes 454664 | tf_op jit(solution)/shard_map/ppermute | solution.py:250
  190.8 7.5 %collective-permute-start.51 = (bf16[256,384]{1,0:T(8,128)(2,1)S(1)}, bf16[256,384]{1,0:T(8,128)(2,1)S(1)}, u32[]{:S(2)}, u32[]{:S(2)}) collective-permute-start(bf16[256,384]{1,0:T(8,128)(2,1)S(1)} %collective-permute-done.49.refs_0_), channel_id=1, source_target_pairs={{0,1},{1,0},{2,3},{3,2},{4,5},{5,4},{6,7},{7,6},{8,9},{9,8},{10,11... | collective-permute-start | bytes 589832 | tf_op jit(solution)/shard_map/ppermute | solution.py:250
  190.8 7.5 %collective-permute-start.52 = (bf16[256,384]{1,0:T(8,128)(2,1)S(1)}, bf16[256,384]{1,0:T(8,128)(2,1)S(1)}, u32[]{:S(2)}, u32[]{:S(2)}) collective-permute-start(bf16[256,384]{1,0:T(8,128)(2,1)S(1)} %collective-permute-done.50.refs_1_), channel_id=1, source_target_pairs={{0,1},{1,0},{2,3},{3,2},{4,5},{5,4},{6,7},{7,6},{8,9},{9,8},{10,11... | collective-permute-start | bytes 589832 | tf_op jit(solution)/shard_map/ppermute | solution.py:250
  199.6 1.4 collective-permute-start.56
  199.6 1.6 collective-permute-start.57
  200.1 1.4 collective-permute-start.58
  200.1 1.6 collective-permute-start.59
  (6 other events, 67.4 us)

commit v3 on v2

--- a/solution.py
+++ b/solution.py
@@ -11,6 +11,7 @@
 
 CONVS = 2
 BACK_FLOPS = 6000000000
+INPUT_FLOPS = 4000000000
 
 
 eps = 1e-05
@@ -739,22 +740,36 @@
     share_copy.wait()
 
 
+def fold_kernel(*refs):
+    count = (len(refs) - 2) // 2
+    shares, outs, (blocks, sems) = refs[:count], refs[count:-2], refs[-2:]
+    rows = outs[0].shape[0]
+    copies = start_all(
+        [pltpu.make_async_copy(share, blocks.at[n], sems.at[n]) for n, share in enumerate(shares)]
+    )
+    for n, copy in enumerate(copies):
+        copy.wait()
+        value = add_blocks([blocks.at[n, pl.ds(m * rows, rows)] for m in range(blocks.shape[1] // rows)])
+        outs[n][...] = value.astype(jnp.bfloat16)
+
+
 def choose_kernel(*refs):
-    shares, outs, (blocks, sems) = refs[:-6], refs[-6:-2], refs[-2:]
+    last, others, outs = refs[0], refs[1:-4], refs[-4:]
     section, _, _ = place()
     rows = outs[0].shape[0]
-    copies = start_all(
-        [pltpu.make_async_copy(share, blocks.at[layer], sems.at[layer]) for layer, share in enumerate(shares)]
-    )
-    for layer, copy in enumerate(copies):
-        copy.wait()
-        value = add_blocks([blocks.at[layer, pl.ds(n * rows, rows)] for n in range(blocks.shape[1] // rows)])
-        value = value.astype(jnp.bfloat16)
-        for k, out in enumerate(outs):
+    value = add_blocks([last.at[pl.ds(n * rows, rows)] for n in range(last.shape[0] // rows)])
+    value = value.astype(jnp.bfloat16)
+    for k, out in enumerate(outs):
+
+        @pl.when((section ^ k) == 0)
+        def _():
+            out[...] = value
+
+        for layer, other in enumerate(others, 1):
 
             @pl.when((section ^ k) == layer)
             def _():
-                out[...] = value
+                out[...] = other[...]
 
 
 def turn_weights_kernel(layers, *refs):
@@ -1065,20 +1080,29 @@
         [((2 * ch, length), bf16)],
         [*blocks, activation, inside],
         "input",
+        flops=INPUT_FLOPS,
         held=(4,),
         loose=(5,),
         copies=1,
     )
     maps = call(pair_kernel, [((4 * ch, 2 * cells), bf16)] * 2, [], [keep, to_core(give)], "pair")
     maps = [send(x, lambda s, z, c, n=n: (z, s ^ (2 * c + n), c)) for n, x in enumerate(maps)]
+    folded = call(
+        fold_kernel,
+        [share_piece] * last,
+        [((last, 4 * slice_rows, 2 * ch), bf16)],
+        shares[1:],
+        "fold",
+        held=range(last),
+        copies=last,
+    )
     chosen = call(
         choose_kernel,
         [share_piece] * 4,
-        [((layers, 4 * slice_rows, 2 * ch), bf16)],
-        shares,
+        [],
+        [shares[0], *folded],
         "choose",
-        held=range(layers),
-        copies=layers,
+        loose=(0,),
     )
     pick = (core * cells + np.arange(cells))[:, None] == np.arange(2 * cells)[None, :]
     activations, input_grad = call(

time: 204 us -> 201 us (0.985)
    ppermute x60, waiting for transfers between devices: 64.6 us -> 56.4 us  [send(): return lax.ppermute(x, AXES, pairs)]
    all_to_all x4, waiting for transfers between devices: 16.1 us -> 22.4 us  [plane_shards(): lax.all_to_all(share, 'dp', 0, 0, tiled=True, axis_index_groups=same_core)]
    pallas_call x25 -> x26, Pallas kernels: 52.2 us -> 52.1 us  [call(): pl.pallas_call(kernel, out_shape=shapes, in_specs=[pl.BlockSpec(memory_sp...]
where the time goes in v3:
time: 201 us; the launch traced here: 200 us
  waiting for transfers between devices  78.8 us (39%)
  starting transfers between devices  67.7 us (34%)
  Pallas kernels  52.1 us (26%)
    ppermute x60, waiting for transfers between devices, send(): return lax.ppermute(x, AXES, pairs)  56.4 us
    pallas_call x26, Pallas kernels, call(): pl.pallas_call(kernel, out_shape=shapes, in_specs=[pl.BlockSpec(memory_sp...  52.1 us
    ppermute x60, starting transfers between devices, send(): return lax.ppermute(x, AXES, pairs)  50.8 us
    all_to_all x4, waiting for transfers between devices, plane_shards(): lax.all_to_all(share, 'dp', 0, 0, tiled=True, axis_index_groups=same_core)  22.4 us
    all_to_all x4, starting transfers between devices, plane_shards(): lax.all_to_all(share, 'dp', 0, 0, tiled=True, axis_index_groups=same_core)  16.9 us
  transfers between devices with their start and end apart: 64, of which 34 were waited for; matrix products, arithmetic and copies ran while one was open for 0% of the time, Pallas kernels for 16%

profile of v3, /device:TPU:0, one launch (start us, length us, event | category | flops | bytes accessed | tf_op | source)
XLA Modules:
  0.0 199.8 jit_solution(18431480210253944921)
XLA Ops:
  0.6 3.6 %weight_pack.1 = (bf16[592,512]{1,0:T(8,128)(2,1)}, bf16[592,512]{1,0:T(8,128)(2,1)S(1)}, bf16[592,512]{1,0:T(8,128)(2,1)S(1)}, bf16[592,512]{1,0:T(8,128)(2,1)S(1)}) custom-call(f32[1,512]{1,0:T(1,128)} %gain.1, f32[1,512]{1,0:T(1,128)} %bias.1, bf16[9,512,512]{2,1,0:T(8,128)(2,1)} %bitcast.25), custom_call_target="tpu_custom_call" | custom-call | bytes 7147520 | tf_op jit(solution)/shard_map/weight_pack/pallas_call | solution.py:873
  4.2 3.0 %collective-permute-start.7 = (bf16[592,512]{1,0:T(8,128)(2,1)S(1)}, bf16[592,512]{1,0:T(8,128)(2,1)}, u32[]{:S(2)}, u32[]{:S(2)}) collective-permute-start(bf16[592,512]{1,0:T(8,128)(2,1)S(1)} %get-tuple-element.132), channel_id=1, source_target_pairs={{0,8},{1,9},{2,10},{3,11},{4,12},{5,13},{6,14},{7,15},{8,0},{9,1},... | collective-permute-start | bytes 1818632 | tf_op jit(solution)/shard_map/ppermute | solution.py:251
  7.3 1.5 collective-permute-start.8
  8.8 1.8 frames.1
  10.6 1.6 collective-permute-start
  12.7 2.6 %collective-permute-start.1 = (bf16[208,640]{1,0:T(8,128)(2,1)S(1)}, bf16[208,640]{1,0:T(8,128)(2,1)S(1)}, u32[]{:S(2)}, u32[]{:S(2)}) collective-permute-start(bf16[208,640]{1,0:T(8,128)(2,1)S(1)} %get-tuple-element.138), channel_id=1, source_target_pairs={{0,4},{1,5},{2,6},{3,7},{4,0},{5,1},{6,2},{7,3},{8,12},{9,13},{10,... | collective-permute-start | bytes 798728 | tf_op jit(solution)/shard_map/ppermute | solution.py:251
  15.3 8.4 %collective-permute-done.refs_1_ = bf16[208,640]{1,0:T(8,128)(2,1)S(1)} collective-permute-done((bf16[208,640]{1,0:T(8,128)(2,1)S(1)}, bf16[208,640]{1,0:T(8,128)(2,1)S(1)}, u32[]{:S(2)}, u32[]{:S(2)}) %collective-permute-start) | collective-permute-done | bytes 266272 | tf_op jit(solution)/shard_map/ppermute | solution.py:251
  23.7 2.5 %collective-permute-start.2 = (bf16[208,640]{1,0:T(8,128)(2,1)S(1)}, bf16[208,640]{1,0:T(8,128)(2,1)S(1)}, u32[]{:S(2)}, u32[]{:S(2)}) collective-permute-start(bf16[208,640]{1,0:T(8,128)(2,1)S(1)} %get-tuple-element.139), channel_id=1, source_target_pairs={{0,6},{1,7},{2,4},{3,5},{4,2},{5,3},{6,0},{7,1},{8,14},{9,15},{10,... | collective-permute-start | bytes 798728 | tf_op jit(solution)/shard_map/ppermute | solution.py:251
  26.2 6.2 %collective-permute-done.1.refs_2_ = bf16[208,640]{1,0:T(8,128)(2,1)S(1)} collective-permute-done((bf16[208,640]{1,0:T(8,128)(2,1)S(1)}, bf16[208,640]{1,0:T(8,128)(2,1)S(1)}, u32[]{:S(2)}, u32[]{:S(2)}) %collective-permute-start.1) | collective-permute-done | bytes 266272 | tf_op jit(solution)/shard_map/ppermute | solution.py:251
  32.9 2.6 %collective-permute-done.8.refs_10_.refs_2_ = bf16[592,512]{1,0:T(8,128)(2,1)} collective-permute-done((bf16[592,512]{1,0:T(8,128)(2,1)S(1)}, bf16[592,512]{1,0:T(8,128)(2,1)}, u32[]{:S(2)}, u32[]{:S(2)}) %collective-permute-start.8) | collective-permute-done | bytes 606240 | tf_op jit(solution)/shard_map/ppermute | solution.py:251
  35.7 1.4 collective-permute-done.6.refs_7_
  37.1 3.8 %forward.3 = (bf16[64,1536]{1,0:T(8,128)(2,1)S(1)}, f32[64,1664]{1,0:T(8,128)}, bf16[1536,512]{1,0:T(8,128)(2,1)}, f32[1,1536]{1,0:T(1,128)S(1)}, bf16[64,1536]{1,0:T(8,128)(2,1)}) custom-call(bf16[208,640]{1,0:T(8,128)(2,1)S(1)} %get-tuple-element.136.refs_0_, bf16[208,640]{1,0:T(8,128)(2,1)S(1)} %collective-permute-done.refs_1_, ...), custom_call_target="tpu_custom_call" | custom-call | flops 905969664 | bytes 7067648 | tf_op jit(solution)/shard_map/forward/pallas_call | solution.py:873
  40.9 2.2 %collective-permute-start.12 = (bf16[64,1536]{1,0:T(8,128)(2,1)S(1)}, bf16[64,1536]{1,0:T(8,128)(2,1)S(1)}, u32[]{:S(2)}, u32[]{:S(2)}) collective-permute-start(bf16[64,1536]{1,0:T(8,128)(2,1)S(1)} %get-tuple-element.146.refs_0_), channel_id=1, source_target_pairs={{0,24},{1,25},{2,26},{3,27},{4,28},{5,29},{6,30},{7,31},{8,16},{9,... | collective-permute-start | bytes 589832 | tf_op jit(solution)/shard_map/ppermute | solution.py:251
  44.4 3.8 %turn_weights.1 = (bf16[1024,640]{1,0:T(8,128)(2,1)}, bf16[1024,640]{1,0:T(8,128)(2,1)}) custom-call(bf16[592,512]{1,0:T(8,128)(2,1)} %get-tuple-element.162.refs_8_.refs_0_, bf16[592,512]{1,0:T(8,128)(2,1)} %collective-permute-done.7.refs_9_.refs_1_, bf16[592,512]{1,0:T(8,128)(2,1)} %collective-permute-done.8.refs_10_.refs_2_, ...), custom_call_target="tpu_custom_call" | custom-call | bytes 5046272 | tf_op jit(solution)/shard_map/turn_weights/pallas_call | solution.py:873
  48.3 1.1 pick.3.refs_8_
  50.0 3.1 %collective-permute-done.10.refs_1_ = bf16[64,1536]{1,0:T(8,128)(2,1)S(1)} collective-permute-done((bf16[64,1536]{1,0:T(8,128)(2,1)S(1)}, bf16[64,1536]{1,0:T(8,128)(2,1)S(1)}, u32[]{:S(2)}, u32[]{:S(2)}) %collective-permute-start.10) | collective-permute-done | bytes 196640 | tf_op jit(solution)/shard_map/ppermute | solution.py:251
  54.8 3.1 %forward.4 = (bf16[64,1536]{1,0:T(8,128)(2,1)S(1)}, f32[64,1664]{1,0:T(8,128)}, bf16[512,1536]{1,0:T(8,128)(2,1)}) custom-call(bf16[64,1536]{1,0:T(8,128)(2,1)S(1)} %get-tuple-element.146.refs_0_, bf16[64,1536]{1,0:T(8,128)(2,1)S(1)} %collective-permute-done.10.refs_1_, bf16[64,1536]{1,0:T(8,128)(2,1)S(1)} %collective-permute-done.11.refs_2_, ...), custom_call_target="tpu_custom_call" | custom-call | flops 905969664 | bytes 4478976 | tf_op jit(solution)/shard_map/forward/pallas_call | solution.py:873
  58.2 1.7 collective-permute-start.19
  61.7 1.1 pick.4.refs_8_
  62.8 4.1 %collective-permute-done.19.refs_3_ = bf16[64,1536]{1,0:T(8,128)(2,1)S(1)} collective-permute-done((bf16[64,1536]{1,0:T(8,128)(2,1)S(1)}, bf16[64,1536]{1,0:T(8,128)(2,1)S(1)}, u32[]{:S(2)}, u32[]{:S(2)}) %collective-permute-start.19) | collective-permute-done | bytes 196640 | tf_op jit(solution)/shard_map/ppermute | solution.py:251
  66.9 3.2 %collective-permute-done.17.refs_1_ = bf16[64,1536]{1,0:T(8,128)(2,1)S(1)} collective-permute-done((bf16[64,1536]{1,0:T(8,128)(2,1)S(1)}, bf16[64,1536]{1,0:T(8,128)(2,1)S(1)}, u32[]{:S(2)}, u32[]{:S(2)}) %collective-permute-start.17) | collective-permute-done | bytes 196640 | tf_op jit(solution)/shard_map/ppermute | solution.py:251
  71.8 2.4 %forward.5 = (bf16[64,1536]{1,0:T(8,128)(2,1)S(1)}, f32[64,1664]{1,0:T(8,128)}, bf16[512,1536]{1,0:T(8,128)(2,1)}) custom-call(bf16[64,1536]{1,0:T(8,128)(2,1)S(1)} %get-tuple-element.155.refs_0_, bf16[64,1536]{1,0:T(8,128)(2,1)S(1)} %collective-permute-done.17.refs_1_, bf16[64,1536]{1,0:T(8,128)(2,1)S(1)} %collective-permute-done.18.refs_2_, ...), custom_call_target="tpu_custom_call" | custom-call | flops 905969664 | bytes 4478976 | tf_op jit(solution)/shard_map/forward/pallas_call | solution.py:873
  74.3 1.2 collective-permute-start.24
  75.5 1.1 collective-permute-start.25
  76.6 1.2 collective-permute-start.26
  77.8 4.2 %collective-permute-done.24.refs_1_ = bf16[64,1536]{1,0:T(8,128)(2,1)S(1)} collective-permute-done((bf16[64,1536]{1,0:T(8,128)(2,1)S(1)}, bf16[64,1536]{1,0:T(8,128)(2,1)S(1)}, u32[]{:S(2)}, u32[]{:S(2)}) %collective-permute-start.24) | collective-permute-done | bytes 196640 | tf_op jit(solution)/shard_map/ppermute | solution.py:251
  82.1 4.4 %collective-permute-done.25.refs_2_ = bf16[64,1536]{1,0:T(8,128)(2,1)S(1)} collective-permute-done((bf16[64,1536]{1,0:T(8,128)(2,1)S(1)}, bf16[64,1536]{1,0:T(8,128)(2,1)S(1)}, u32[]{:S(2)}, u32[]{:S(2)}) %collective-permute-start.25) | collective-permute-done | bytes 196640 | tf_op jit(solution)/shard_map/ppermute | solution.py:251
  86.5 1.5 pick.5
  88.6 1.1 collective-permute-done.31.refs_7_
  89.6 2.4 %turn.1 = (bf16[64,1536]{1,0:T(8,128)(2,1)}, bf16[512,1536]{1,0:T(8,128)(2,1)}, bf16[64,1536]{1,0:T(8,128)(2,1)S(1)}, f32[64,256]{1,0:T(8,128)S(1)}) custom-call(bf16[64,1536]{1,0:T(8,128)(2,1)S(1)} %get-tuple-element.161.refs_0_, bf16[64,1536]{1,0:T(8,128)(2,1)S(1)} %collective-permute-done.24.refs_1_, ...), custom_call_target="tpu_custom_call" | custom-call | flops 905969664 | bytes 4511744 | tf_op jit(solution)/shard_map/turn/pallas_call | solution.py:873
  92.4 1.1 collective-permute-done.32.other
  93.5 4.0 %conv_back.4 = (bf16[64,1536]{1,0:T(8,128)(2,1)S(1)}, bf16[64,1536]{1,0:T(8,128)(2,1)S(1)}, bf16[64,1536]{1,0:T(8,128)(2,1)S(1)}, bf16[64,1536]{1,0:T(8,128)(2,1)S(1)}, bf16[2368,128]{1,0:T(8,128)(2,1)}) custom-call(bf16[64,1536]{1,0:T(8,128)(2,1)S(1)} %get-tuple-element.171.own, bf16[64,1536]{1,0:T(8,128)(2,1)S(1)} %collective-permute-done.32.other, ...), custom_call_target="tpu_custom_call" | custom-call | flops 6000000000 | bytes 6144000 | tf_op jit(solution)/shard_map/conv_back/pallas_call | solution.py:873
  99.5 1.6 collective-permute-start.35
  101.1 6.2 %all-to-all-start = ((bf16[4,592,128]{2,1,0:T(8,128)(2,1)}), bf16[4,592,128]{2,1,0:T(8,128)(2,1)S(1)}, u32[]{:S(2)}, u32[]{:S(2)}) async-start(bf16[4,592,128]{2,1,0:T(8,128)(2,1)} %bitcast.34), calls=%async_computation | async-start | bytes 1212416 | tf_op jit(solution)/shard_map/all_to_all | solution.py:1056
  108.3 1.2 collective-permute-done.34.refs_2_
  110.2 1.4 collective-permute-done.36.other
  111.6 4.0 %conv_back.5 = (bf16[64,1536]{1,0:T(8,128)(2,1)S(1)}, bf16[64,1536]{1,0:T(8,128)(2,1)S(1)}, bf16[64,1536]{1,0:T(8,128)(2,1)S(1)}, bf16[64,1536]{1,0:T(8,128)(2,1)S(1)}, bf16[2368,128]{1,0:T(8,128)(2,1)}) custom-call(bf16[64,1536]{1,0:T(8,128)(2,1)S(1)} %get-tuple-element.186.own, bf16[64,1536]{1,0:T(8,128)(2,1)S(1)} %collective-permute-done.36.other, ...), custom_call_target="tpu_custom_call" | custom-call | flops 6000000000 | bytes 6144000 | tf_op jit(solution)/shard_map/conv_back/pallas_call | solution.py:873
  115.6 1.2 collective-permute-start.37
  117.8 1.3 collective-permute-start.39
  119.1 4.1 %all-to-all-done = bf16[4,592,128]{2,1,0:T(8,128)(2,1)S(1)} async-done(((bf16[4,592,128]{2,1,0:T(8,128)(2,1)}), bf16[4,592,128]{2,1,0:T(8,128)(2,1)S(1)}, u32[]{:S(2)}, u32[]{:S(2)}) %all-to-all-start) | async-done | bytes 606240 | tf_op jit(solution)/shard_map/all_to_all | solution.py:1056
  123.2 3.5 %all-to-all-start.1 = ((bf16[4,592,128]{2,1,0:T(8,128)(2,1)}), bf16[4,592,128]{2,1,0:T(8,128)(2,1)S(1)}, u32[]{:S(2)}, u32[]{:S(2)}) async-start(bf16[4,592,128]{2,1,0:T(8,128)(2,1)} %bitcast.33), calls=%async_computation.1 | async-start | bytes 1212416 | tf_op jit(solution)/shard_map/all_to_all | solution.py:1056
  127.8 2.0 %norm_back.4 = (bf16[64,1536]{1,0:T(8,128)(2,1)S(1)}, f32[64,256]{1,0:T(8,128)S(1)}) custom-call(bf16[64,1536]{1,0:T(8,128)(2,1)S(1)} %get-tuple-element.189.refs_0_, bf16[64,1536]{1,0:T(8,128)(2,1)S(1)} %collective-permute-done.37.refs_1_, bf16[64,1536]{1,0:T(8,128)(2,1)S(1)} %collective-permute-done.38.refs_2_, ...), custom_call_target="tpu_custom_call" | custom-call | bytes 1595392 | tf_op jit(solution)/shard_map/norm_back/pallas_call | solution.py:873
  129.9 1.4 collective-permute-done.40.other
  131.4 4.0 %conv_back.6 = (bf16[64,1536]{1,0:T(8,128)(2,1)S(1)}, bf16[64,1536]{1,0:T(8,128)(2,1)S(1)}, bf16[64,1536]{1,0:T(8,128)(2,1)S(1)}, bf16[64,1536]{1,0:T(8,128)(2,1)S(1)}, bf16[2368,128]{1,0:T(8,128)(2,1)}) custom-call(bf16[64,1536]{1,0:T(8,128)(2,1)S(1)} %get-tuple-element.200.own, bf16[64,1536]{1,0:T(8,128)(2,1)S(1)} %collective-permute-done.40.other, ...), custom_call_target="tpu_custom_call" | custom-call | flops 6000000000 | bytes 6144000 | tf_op jit(solution)/shard_map/conv_back/pallas_call | solution.py:873
  137.2 1.7 collective-permute-start.43
  138.9 3.5 %all-to-all-done.1 = bf16[4,592,128]{2,1,0:T(8,128)(2,1)S(1)} async-done(((bf16[4,592,128]{2,1,0:T(8,128)(2,1)}), bf16[4,592,128]{2,1,0:T(8,128)(2,1)S(1)}, u32[]{:S(2)}, u32[]{:S(2)}) %all-to-all-start.1) | async-done | bytes 606240 | tf_op jit(solution)/shard_map/all_to_all | solution.py:1056
  142.4 3.7 %all-to-all-start.2 = ((bf16[4,592,128]{2,1,0:T(8,128)(2,1)}), bf16[4,592,128]{2,1,0:T(8,128)(2,1)S(1)}, u32[]{:S(2)}, u32[]{:S(2)}) async-start(bf16[4,592,128]{2,1,0:T(8,128)(2,1)} %bitcast.31), calls=%async_computation.2 | async-start | bytes 1212416 | tf_op jit(solution)/shard_map/all_to_all | solution.py:1056
  147.8 1.4 collective-permute-done.44.other
  149.3 3.9 %conv_back.7 = (bf16[64,1536]{1,0:T(8,128)(2,1)S(1)}, bf16[64,1536]{1,0:T(8,128)(2,1)S(1)}, bf16[64,1536]{1,0:T(8,128)(2,1)S(1)}, bf16[64,1536]{1,0:T(8,128)(2,1)S(1)}, bf16[2368,128]{1,0:T(8,128)(2,1)}) custom-call(bf16[64,1536]{1,0:T(8,128)(2,1)S(1)} %get-tuple-element.214.own, bf16[64,1536]{1,0:T(8,128)(2,1)S(1)} %collective-permute-done.44.other, ...), custom_call_target="tpu_custom_call" | custom-call | flops 6000000000 | bytes 6144000 | tf_op jit(solution)/shard_map/conv_back/pallas_call | solution.py:873
  153.2 1.2 collective-permute-start.45
  155.4 1.3 collective-permute-start.47
  156.7 4.9 %all-to-all-done.2 = bf16[4,592,128]{2,1,0:T(8,128)(2,1)S(1)} async-done(((bf16[4,592,128]{2,1,0:T(8,128)(2,1)}), bf16[4,592,128]{2,1,0:T(8,128)(2,1)S(1)}, u32[]{:S(2)}, u32[]{:S(2)}) %all-to-all-start.2) | async-done | bytes 606240 | tf_op jit(solution)/shard_map/all_to_all | solution.py:1056
  161.6 3.5 %all-to-all-start.3 = ((bf16[4,592,128]{2,1,0:T(8,128)(2,1)}), bf16[4,592,128]{2,1,0:T(8,128)(2,1)S(1)}, u32[]{:S(2)}, u32[]{:S(2)}) async-start(bf16[4,592,128]{2,1,0:T(8,128)(2,1)} %bitcast.32), calls=%async_computation.3 | async-start | bytes 1212416 | tf_op jit(solution)/shard_map/all_to_all | solution.py:1056
  166.3 1.4 collective-permute-done.48.got
  168.5 5.1 %collective-permute-start.50 = (bf16[256,384]{1,0:T(8,128)(2,1)S(1)}, bf16[256,384]{1,0:T(8,128)(2,1)S(1)}, u32[]{:S(2)}, u32[]{:S(2)}) collective-permute-start(bf16[256,384]{1,0:T(8,128)(2,1)S(1)} %get-tuple-element.228), channel_id=1, source_target_pairs={{0,2},{1,7},{2,10},{3,15},{4,18},{5,23},{6,26},{7,31},{8,0},{9,5},... | collective-permute-start | bytes 589832 | tf_op jit(solution)/shard_map/ppermute | solution.py:251
  173.6 1.5 fold.1
  175.1 9.9 %all-to-all-done.3 = bf16[4,592,128]{2,1,0:T(8,128)(2,1)S(1)} async-done(((bf16[4,592,128]{2,1,0:T(8,128)(2,1)}), bf16[4,592,128]{2,1,0:T(8,128)(2,1)S(1)}, u32[]{:S(2)}, u32[]{:S(2)}) %all-to-all-start.3) | async-done | bytes 606240 | tf_op jit(solution)/shard_map/all_to_all | solution.py:1056
  185.2 1.5 collective-permute-start.53
  186.7 1.1 collective-permute-start.54
  187.8 1.1 collective-permute-start.55
  189.5 3.0 %collective-permute-done.53.refs_1_ = bf16[592,128]{1,0:T(8,128)(2,1)S(1)} collective-permute-done((bf16[592,128]{1,0:T(8,128)(2,1)S(1)}, bf16[592,128]{1,0:T(8,128)(2,1)S(1)}, u32[]{:S(2)}, u32[]{:S(2)}) %collective-permute-start.53) | collective-permute-done | bytes 151584 | tf_op jit(solution)/shard_map/ppermute | solution.py:251
  192.5 2.2 %collective-permute-done.54.refs_2_ = bf16[592,128]{1,0:T(8,128)(2,1)S(1)} collective-permute-done((bf16[592,128]{1,0:T(8,128)(2,1)S(1)}, bf16[592,128]{1,0:T(8,128)(2,1)S(1)}, u32[]{:S(2)}, u32[]{:S(2)}) %collective-permute-start.54) | collective-permute-done | bytes 151584 | tf_op jit(solution)/shard_map/ppermute | solution.py:251
  195.0 1.2 maps_out.1
  198.2 1.6 grads_out.1
  (104 shorter events, 25.1 us)
Async XLA Ops:
  4.2 28.6 %collective-permute-start.7 = (bf16[592,512]{1,0:T(8,128)(2,1)S(1)}, bf16[592,512]{1,0:T(8,128)(2,1)}, u32[]{:S(2)}, u32[]{:S(2)}) collective-permute-start(bf16[592,512]{1,0:T(8,128)(2,1)S(1)} %get-tuple-element.132), channel_id=1, source_target_pairs={{0,8},{1,9},{2,10},{3,11},{4,12},{5,13},{6,14},{7,15},{8,0},{9,1},... | collective-permute-start | bytes 1818632 | tf_op jit(solution)/shard_map/ppermute | solution.py:251
  7.3 28.3 %collective-permute-start.8 = (bf16[592,512]{1,0:T(8,128)(2,1)S(1)}, bf16[592,512]{1,0:T(8,128)(2,1)}, u32[]{:S(2)}, u32[]{:S(2)}) collective-permute-start(bf16[592,512]{1,0:T(8,128)(2,1)S(1)} %get-tuple-element.133), channel_id=1, source_target_pairs={{0,16},{1,17},{2,18},{3,19},{4,20},{5,21},{6,22},{7,23},{8,24},{9,... | collective-permute-start | bytes 1818632 | tf_op jit(solution)/shard_map/ppermute | solution.py:251
  10.6 13.1 %collective-permute-start = (bf16[208,640]{1,0:T(8,128)(2,1)S(1)}, bf16[208,640]{1,0:T(8,128)(2,1)S(1)}, u32[]{:S(2)}, u32[]{:S(2)}) collective-permute-start(bf16[208,640]{1,0:T(8,128)(2,1)S(1)} %get-tuple-element.137), channel_id=1, source_target_pairs={{0,2},{1,3},{2,0},{3,1},{4,6},{5,7},{6,4},{7,5},{8,10},{9,11},{10,... | collective-permute-start | bytes 798728 | tf_op jit(solution)/shard_map/ppermute | solution.py:251
  12.2 23.4 %collective-permute-start.9 = (bf16[592,512]{1,0:T(8,128)(2,1)S(1)}, bf16[592,512]{1,0:T(8,128)(2,1)}, u32[]{:S(2)}, u32[]{:S(2)}) collective-permute-start(bf16[592,512]{1,0:T(8,128)(2,1)S(1)} %get-tuple-element.134), channel_id=1, source_target_pairs={{0,24},{1,25},{2,26},{3,27},{4,28},{5,29},{6,30},{7,31},{8,16},{9,... | collective-permute-start | bytes 1818632 | tf_op jit(solution)/shard_map/ppermute | solution.py:251
  12.7 19.6 %collective-permute-start.1 = (bf16[208,640]{1,0:T(8,128)(2,1)S(1)}, bf16[208,640]{1,0:T(8,128)(2,1)S(1)}, u32[]{:S(2)}, u32[]{:S(2)}) collective-permute-start(bf16[208,640]{1,0:T(8,128)(2,1)S(1)} %get-tuple-element.138), channel_id=1, source_target_pairs={{0,4},{1,5},{2,6},{3,7},{4,0},{5,1},{6,2},{7,3},{8,12},{9,13},{10,... | collective-permute-start | bytes 798728 | tf_op jit(solution)/shard_map/ppermute | solution.py:251
  23.7 8.6 %collective-permute-start.2 = (bf16[208,640]{1,0:T(8,128)(2,1)S(1)}, bf16[208,640]{1,0:T(8,128)(2,1)S(1)}, u32[]{:S(2)}, u32[]{:S(2)}) collective-permute-start(bf16[208,640]{1,0:T(8,128)(2,1)S(1)} %get-tuple-element.139), channel_id=1, source_target_pairs={{0,6},{1,7},{2,4},{3,5},{4,2},{5,3},{6,0},{7,1},{8,14},{9,15},{10,... | collective-permute-start | bytes 798728 | tf_op jit(solution)/shard_map/ppermute | solution.py:251
  32.3 3.3 %collective-permute-start.3 = (bf16[208,640]{1,0:T(8,128)(2,1)S(1)}, bf16[208,640]{1,0:T(8,128)(2,1)S(1)}, u32[]{:S(2)}, u32[]{:S(2)}) collective-permute-start(bf16[208,640]{1,0:T(8,128)(2,1)S(1)} %get-tuple-element.136.refs_0_), channel_id=1, source_target_pairs={{0,1},{1,0},{2,3},{3,2},{4,5},{5,4},{6,7},{7,6},{8,9},{9,8},{10,11... | collective-permute-start | bytes 798728 | tf_op jit(solution)/shard_map/ppermute | solution.py:251
  32.3 3.3 %collective-permute-start.4 = (bf16[208,640]{1,0:T(8,128)(2,1)S(1)}, bf16[208,640]{1,0:T(8,128)(2,1)S(1)}, u32[]{:S(2)}, u32[]{:S(2)}) collective-permute-start(bf16[208,640]{1,0:T(8,128)(2,1)S(1)} %collective-permute-done.refs_1_), channel_id=1, source_target_pairs={{0,1},{1,0},{2,3},{3,2},{4,5},{5,4},{6,7},{7,6},{8,9},{9,8},{10,11... | collective-permute-start | bytes 798728 | tf_op jit(solution)/shard_map/ppermute | solution.py:251
  32.8 2.8 %collective-permute-start.5 = (bf16[208,640]{1,0:T(8,128)(2,1)S(1)}, bf16[208,640]{1,0:T(8,128)(2,1)S(1)}, u32[]{:S(2)}, u32[]{:S(2)}) collective-permute-start(bf16[208,640]{1,0:T(8,128)(2,1)S(1)} %collective-permute-done.1.refs_2_), channel_id=1, source_target_pairs={{0,1},{1,0},{2,3},{3,2},{4,5},{5,4},{6,7},{7,6},{8,9},{9,8},{10,11... | collective-permute-start | bytes 798728 | tf_op jit(solution)/shard_map/ppermute | solution.py:251
  35.6 1.5 collective-permute-start.6
  40.9 8.8 %collective-permute-start.12 = (bf16[64,1536]{1,0:T(8,128)(2,1)S(1)}, bf16[64,1536]{1,0:T(8,128)(2,1)S(1)}, u32[]{:S(2)}, u32[]{:S(2)}) collective-permute-start(bf16[64,1536]{1,0:T(8,128)(2,1)S(1)} %get-tuple-element.146.refs_0_), channel_id=1, source_target_pairs={{0,24},{1,25},{2,26},{3,27},{4,28},{5,29},{6,30},{7,31},{8,16},{9,... | collective-permute-start | bytes 589832 | tf_op jit(solution)/shard_map/ppermute | solution.py:251
  43.0 10.0 %collective-permute-start.10 = (bf16[64,1536]{1,0:T(8,128)(2,1)S(1)}, bf16[64,1536]{1,0:T(8,128)(2,1)S(1)}, u32[]{:S(2)}, u32[]{:S(2)}) collective-permute-start(bf16[64,1536]{1,0:T(8,128)(2,1)S(1)} %get-tuple-element.146.refs_0_), channel_id=1, source_target_pairs={{0,8},{1,9},{2,10},{3,11},{4,12},{5,13},{6,14},{7,15},{8,0},{9,1},... | collective-permute-start | bytes 589832 | tf_op jit(solution)/shard_map/ppermute | solution.py:251
  43.9 9.2 %collective-permute-start.11 = (bf16[64,1536]{1,0:T(8,128)(2,1)S(1)}, bf16[64,1536]{1,0:T(8,128)(2,1)S(1)}, u32[]{:S(2)}, u32[]{:S(2)}) collective-permute-start(bf16[64,1536]{1,0:T(8,128)(2,1)S(1)} %get-tuple-element.146.refs_0_), channel_id=1, source_target_pairs={{0,16},{1,17},{2,18},{3,19},{4,20},{5,21},{6,22},{7,23},{8,24},{9,... | collective-permute-start | bytes 589832 | tf_op jit(solution)/shard_map/ppermute | solution.py:251
  49.4 4.2 %collective-permute-start.13 = (bf16[64,1536]{1,0:T(8,128)(2,1)S(1)}, bf16[64,1536]{1,0:T(8,128)(2,1)S(1)}, u32[]{:S(2)}, u32[]{:S(2)}) collective-permute-start(bf16[64,1536]{1,0:T(8,128)(2,1)S(1)} %get-tuple-element.146.refs_0_), channel_id=1, source_target_pairs={{0,1},{1,0},{2,3},{3,2},{4,5},{5,4},{6,7},{7,6},{8,9},{9,8},{10,11... | collective-permute-start | bytes 589832 | tf_op jit(solution)/shard_map/ppermute | solution.py:251
  49.6 4.0 %collective-permute-start.16 = (bf16[64,1536]{1,0:T(8,128)(2,1)S(1)}, bf16[64,1536]{1,0:T(8,128)(2,1)S(1)}, u32[]{:S(2)}, u32[]{:S(2)}) collective-permute-start(bf16[64,1536]{1,0:T(8,128)(2,1)S(1)} %collective-permute-done.12.refs_3_), channel_id=1, source_target_pairs={{0,1},{1,0},{2,3},{3,2},{4,5},{5,4},{6,7},{7,6},{8,9},{9,8},{10,11... | collective-permute-start | bytes 589832 | tf_op jit(solution)/shard_map/ppermute | solution.py:251
  53.1 1.4 collective-permute-start.14
  53.1 1.7 collective-permute-start.15
  57.9 28.6 %collective-permute-start.27 = (bf16[1024,640]{1,0:T(8,128)(2,1)S(1)}, bf16[1024,640]{1,0:T(8,128)(2,1)S(1)}, u32[]{:S(2)}, u32[]{:S(2)}) collective-permute-start(bf16[1024,640]{1,0:T(8,128)(2,1)S(1)} %copy-done.4), channel_id=1, source_target_pairs={{0,1},{1,0},{2,3},{3,2},{4,5},{5,4},{6,7},{7,6},{8,9},{9,8},{10,11... | collective-permute-start | bytes 3932168 | tf_op jit(solution)/shard_map/ppermute | solution.py:251
  58.2 8.7 %collective-permute-start.19 = (bf16[64,1536]{1,0:T(8,128)(2,1)S(1)}, bf16[64,1536]{1,0:T(8,128)(2,1)S(1)}, u32[]{:S(2)}, u32[]{:S(2)}) collective-permute-start(bf16[64,1536]{1,0:T(8,128)(2,1)S(1)} %get-tuple-element.155.refs_0_), channel_id=1, source_target_pairs={{0,24},{1,25},{2,26},{3,27},{4,28},{5,29},{6,30},{7,31},{8,16},{9,... | collective-permute-start | bytes 589832 | tf_op jit(solution)/shard_map/ppermute | solution.py:251
  59.8 10.3 %collective-permute-start.17 = (bf16[64,1536]{1,0:T(8,128)(2,1)S(1)}, bf16[64,1536]{1,0:T(8,128)(2,1)S(1)}, u32[]{:S(2)}, u32[]{:S(2)}) collective-permute-start(bf16[64,1536]{1,0:T(8,128)(2,1)S(1)} %get-tuple-element.155.refs_0_), channel_id=1, source_target_pairs={{0,8},{1,9},{2,10},{3,11},{4,12},{5,13},{6,14},{7,15},{8,0},{9,1},... | collective-permute-start | bytes 589832 | tf_op jit(solution)/shard_map/ppermute | solution.py:251
  60.7 9.7 %collective-permute-start.18 = (bf16[64,1536]{1,0:T(8,128)(2,1)S(1)}, bf16[64,1536]{1,0:T(8,128)(2,1)S(1)}, u32[]{:S(2)}, u32[]{:S(2)}) collective-permute-start(bf16[64,1536]{1,0:T(8,128)(2,1)S(1)} %get-tuple-element.155.refs_0_), channel_id=1, source_target_pairs={{0,16},{1,17},{2,18},{3,19},{4,20},{5,21},{6,22},{7,23},{8,24},{9,... | collective-permute-start | bytes 589832 | tf_op jit(solution)/shard_map/ppermute | solution.py:251
  61.7 8.9 %collective-permute-start.20 = (bf16[64,1536]{1,0:T(8,128)(2,1)S(1)}, bf16[64,1536]{1,0:T(8,128)(2,1)S(1)}, u32[]{:S(2)}, u32[]{:S(2)}) collective-permute-start(bf16[64,1536]{1,0:T(8,128)(2,1)S(1)} %get-tuple-element.155.refs_0_), channel_id=1, source_target_pairs={{0,1},{1,0},{2,3},{3,2},{4,5},{5,4},{6,7},{7,6},{8,9},{9,8},{10,11... | collective-permute-start | bytes 589832 | tf_op jit(solution)/shard_map/ppermute | solution.py:251
  66.9 3.8 %collective-permute-start.23 = (bf16[64,1536]{1,0:T(8,128)(2,1)S(1)}, bf16[64,1536]{1,0:T(8,128)(2,1)S(1)}, u32[]{:S(2)}, u32[]{:S(2)}) collective-permute-start(bf16[64,1536]{1,0:T(8,128)(2,1)S(1)} %collective-permute-done.19.refs_3_), channel_id=1, source_target_pairs={{0,1},{1,0},{2,3},{3,2},{4,5},{5,4},{6,7},{7,6},{8,9},{9,8},{10,11... | collective-permute-start | bytes 589832 | tf_op jit(solution)/shard_map/ppermute | solution.py:251
  70.1 1.4 collective-permute-start.21
  70.4 1.4 collective-permute-start.22
  74.3 7.8 %collective-permute-start.24 = (bf16[64,1536]{1,0:T(8,128)(2,1)S(1)}, bf16[64,1536]{1,0:T(8,128)(2,1)S(1)}, u32[]{:S(2)}, u32[]{:S(2)}) collective-permute-start(bf16[64,1536]{1,0:T(8,128)(2,1)S(1)} %get-tuple-element.161.refs_0_), channel_id=1, source_target_pairs={{0,8},{1,9},{2,10},{3,11},{4,12},{5,13},{6,14},{7,15},{8,0},{9,1},... | collective-permute-start | bytes 589832 | tf_op jit(solution)/shard_map/ppermute | solution.py:251
  75.5 11.0 %collective-permute-start.25 = (bf16[64,1536]{1,0:T(8,128)(2,1)S(1)}, bf16[64,1536]{1,0:T(8,128)(2,1)S(1)}, u32[]{:S(2)}, u32[]{:S(2)}) collective-permute-start(bf16[64,1536]{1,0:T(8,128)(2,1)S(1)} %get-tuple-element.161.refs_0_), channel_id=1, source_target_pairs={{0,16},{1,17},{2,18},{3,19},{4,20},{5,21},{6,22},{7,23},{8,24},{9,... | collective-permute-start | bytes 589832 | tf_op jit(solution)/shard_map/ppermute | solution.py:251
  76.6 11.3 %collective-permute-start.26 = (bf16[64,1536]{1,0:T(8,128)(2,1)S(1)}, bf16[64,1536]{1,0:T(8,128)(2,1)S(1)}, u32[]{:S(2)}, u32[]{:S(2)}) collective-permute-start(bf16[64,1536]{1,0:T(8,128)(2,1)S(1)} %get-tuple-element.161.refs_0_), channel_id=1, source_target_pairs={{0,24},{1,25},{2,26},{3,27},{4,28},{5,29},{6,30},{7,31},{8,16},{9,... | collective-permute-start | bytes 589832 | tf_op jit(solution)/shard_map/ppermute | solution.py:251
  77.8 10.7 %collective-permute-start.28 = (bf16[64,1536]{1,0:T(8,128)(2,1)S(1)}, bf16[64,1536]{1,0:T(8,128)(2,1)S(1)}, u32[]{:S(2)}, u32[]{:S(2)}) collective-permute-start(bf16[64,1536]{1,0:T(8,128)(2,1)S(1)} %get-tuple-element.161.refs_0_), channel_id=1, source_target_pairs={{0,1},{1,0},{2,3},{3,2},{4,5},{5,4},{6,7},{7,6},{8,9},{9,8},{10,11... | collective-permute-start | bytes 589832 | tf_op jit(solution)/shard_map/ppermute | solution.py:251
  82.1 6.5 %collective-permute-start.29 = (bf16[64,1536]{1,0:T(8,128)(2,1)S(1)}, bf16[64,1536]{1,0:T(8,128)(2,1)S(1)}, u32[]{:S(2)}, u32[]{:S(2)}) collective-permute-start(bf16[64,1536]{1,0:T(8,128)(2,1)S(1)} %collective-permute-done.24.refs_1_), channel_id=1, source_target_pairs={{0,1},{1,0},{2,3},{3,2},{4,5},{5,4},{6,7},{7,6},{8,9},{9,8},{10,11... | collective-permute-start | bytes 589832 | tf_op jit(solution)/shard_map/ppermute | solution.py:251
  86.5 2.1 %collective-permute-start.30 = (bf16[64,1536]{1,0:T(8,128)(2,1)S(1)}, bf16[64,1536]{1,0:T(8,128)(2,1)S(1)}, u32[]{:S(2)}, u32[]{:S(2)}) collective-permute-start(bf16[64,1536]{1,0:T(8,128)(2,1)S(1)} %collective-permute-done.25.refs_2_), channel_id=1, source_target_pairs={{0,1},{1,0},{2,3},{3,2},{4,5},{5,4},{6,7},{7,6},{8,9},{9,8},{10,11... | collective-permute-start | bytes 589832 | tf_op jit(solution)/shard_map/ppermute | solution.py:251
  88.0 1.6 collective-permute-start.31
  92.0 1.5 collective-permute-start.32
  97.5 10.8 %collective-permute-start.33 = (bf16[64,1536]{1,0:T(8,128)(2,1)S(1)}, bf16[64,1536]{1,0:T(8,128)(2,1)S(1)}, u32[]{:S(2)}, u32[]{:S(2)}) collective-permute-start(bf16[64,1536]{1,0:T(8,128)(2,1)S(1)} %get-tuple-element.176), channel_id=1, source_target_pairs={{0,8},{1,9},{2,10},{3,11},{4,12},{5,13},{6,14},{7,15},{8,0},{9,1},... | collective-permute-start | bytes 589832 | tf_op jit(solution)/shard_map/ppermute | solution.py:251
  98.4 11.1 %collective-permute-start.34 = (bf16[64,1536]{1,0:T(8,128)(2,1)S(1)}, bf16[64,1536]{1,0:T(8,128)(2,1)S(1)}, u32[]{:S(2)}, u32[]{:S(2)}) collective-permute-start(bf16[64,1536]{1,0:T(8,128)(2,1)S(1)} %get-tuple-element.177), channel_id=1, source_target_pairs={{0,16},{1,17},{2,18},{3,19},{4,20},{5,21},{6,22},{7,23},{8,24},{9,... | collective-permute-start | bytes 589832 | tf_op jit(solution)/shard_map/ppermute | solution.py:251
  99.5 10.0 %collective-permute-start.35 = (bf16[64,1536]{1,0:T(8,128)(2,1)S(1)}, bf16[64,1536]{1,0:T(8,128)(2,1)S(1)}, u32[]{:S(2)}, u32[]{:S(2)}) collective-permute-start(bf16[64,1536]{1,0:T(8,128)(2,1)S(1)} %get-tuple-element.178), channel_id=1, source_target_pairs={{0,24},{1,25},{2,26},{3,27},{4,28},{5,29},{6,30},{7,31},{8,16},{9,... | collective-permute-start | bytes 589832 | tf_op jit(solution)/shard_map/ppermute | solution.py:251
  101.1 22.2 %all-to-all-start = ((bf16[4,592,128]{2,1,0:T(8,128)(2,1)}), bf16[4,592,128]{2,1,0:T(8,128)(2,1)S(1)}, u32[]{:S(2)}, u32[]{:S(2)}) async-start(bf16[4,592,128]{2,1,0:T(8,128)(2,1)} %bitcast.34), calls=%async_computation | async-start | bytes 1212416 | tf_op jit(solution)/shard_map/all_to_all | solution.py:1056
  110.1 1.5 collective-permute-start.36
  115.6 12.2 %collective-permute-start.37 = (bf16[64,1536]{1,0:T(8,128)(2,1)S(1)}, bf16[64,1536]{1,0:T(8,128)(2,1)S(1)}, u32[]{:S(2)}, u32[]{:S(2)}) collective-permute-start(bf16[64,1536]{1,0:T(8,128)(2,1)S(1)} %get-tuple-element.190), channel_id=1, source_target_pairs={{0,8},{1,9},{2,10},{3,11},{4,12},{5,13},{6,14},{7,15},{8,0},{9,1},... | collective-permute-start | bytes 589832 | tf_op jit(solution)/shard_map/ppermute | solution.py:251
  116.8 11.0 %collective-permute-start.38 = (bf16[64,1536]{1,0:T(8,128)(2,1)S(1)}, bf16[64,1536]{1,0:T(8,128)(2,1)S(1)}, u32[]{:S(2)}, u32[]{:S(2)}) collective-permute-start(bf16[64,1536]{1,0:T(8,128)(2,1)S(1)} %get-tuple-element.191), channel_id=1, source_target_pairs={{0,16},{1,17},{2,18},{3,19},{4,20},{5,21},{6,22},{7,23},{8,24},{9,... | collective-permute-start | bytes 589832 | tf_op jit(solution)/shard_map/ppermute | solution.py:251
  117.8 9.9 %collective-permute-start.39 = (bf16[64,1536]{1,0:T(8,128)(2,1)S(1)}, bf16[64,1536]{1,0:T(8,128)(2,1)S(1)}, u32[]{:S(2)}, u32[]{:S(2)}) collective-permute-start(bf16[64,1536]{1,0:T(8,128)(2,1)S(1)} %get-tuple-element.192), channel_id=1, source_target_pairs={{0,24},{1,25},{2,26},{3,27},{4,28},{5,29},{6,30},{7,31},{8,16},{9,... | collective-permute-start | bytes 589832 | tf_op jit(solution)/shard_map/ppermute | solution.py:251
  123.2 19.2 %all-to-all-start.1 = ((bf16[4,592,128]{2,1,0:T(8,128)(2,1)}), bf16[4,592,128]{2,1,0:T(8,128)(2,1)S(1)}, u32[]{:S(2)}, u32[]{:S(2)}) async-start(bf16[4,592,128]{2,1,0:T(8,128)(2,1)} %bitcast.33), calls=%async_computation.1 | async-start | bytes 1212416 | tf_op jit(solution)/shard_map/all_to_all | solution.py:1056
  129.8 1.5 collective-permute-start.40
  135.3 11.8 %collective-permute-start.41 = (bf16[64,1536]{1,0:T(8,128)(2,1)S(1)}, bf16[64,1536]{1,0:T(8,128)(2,1)S(1)}, u32[]{:S(2)}, u32[]{:S(2)}) collective-permute-start(bf16[64,1536]{1,0:T(8,128)(2,1)S(1)} %get-tuple-element.204), channel_id=1, source_target_pairs={{0,8},{1,9},{2,10},{3,11},{4,12},{5,13},{6,14},{7,15},{8,0},{9,1},... | collective-permute-start | bytes 589832 | tf_op jit(solution)/shard_map/ppermute | solution.py:251
  136.1 11.1 %collective-permute-start.42 = (bf16[64,1536]{1,0:T(8,128)(2,1)S(1)}, bf16[64,1536]{1,0:T(8,128)(2,1)S(1)}, u32[]{:S(2)}, u32[]{:S(2)}) collective-permute-start(bf16[64,1536]{1,0:T(8,128)(2,1)S(1)} %get-tuple-element.205), channel_id=1, source_target_pairs={{0,16},{1,17},{2,18},{3,19},{4,20},{5,21},{6,22},{7,23},{8,24},{9,... | collective-permute-start | bytes 589832 | tf_op jit(solution)/shard_map/ppermute | solution.py:251
  137.2 10.0 %collective-permute-start.43 = (bf16[64,1536]{1,0:T(8,128)(2,1)S(1)}, bf16[64,1536]{1,0:T(8,128)(2,1)S(1)}, u32[]{:S(2)}, u32[]{:S(2)}) collective-permute-start(bf16[64,1536]{1,0:T(8,128)(2,1)S(1)} %get-tuple-element.206), channel_id=1, source_target_pairs={{0,24},{1,25},{2,26},{3,27},{4,28},{5,29},{6,30},{7,31},{8,16},{9,... | collective-permute-start | bytes 589832 | tf_op jit(solution)/shard_map/ppermute | solution.py:251
  142.4 19.2 %all-to-all-start.2 = ((bf16[4,592,128]{2,1,0:T(8,128)(2,1)}), bf16[4,592,128]{2,1,0:T(8,128)(2,1)S(1)}, u32[]{:S(2)}, u32[]{:S(2)}) async-start(bf16[4,592,128]{2,1,0:T(8,128)(2,1)} %bitcast.31), calls=%async_computation.2 | async-start | bytes 1212416 | tf_op jit(solution)/shard_map/all_to_all | solution.py:1056
  147.7 1.5 collective-permute-start.44
  153.2 11.9 %collective-permute-start.45 = (bf16[64,1536]{1,0:T(8,128)(2,1)S(1)}, bf16[64,1536]{1,0:T(8,128)(2,1)S(1)}, u32[]{:S(2)}, u32[]{:S(2)}) collective-permute-start(bf16[64,1536]{1,0:T(8,128)(2,1)S(1)} %get-tuple-element.218), channel_id=1, source_target_pairs={{0,8},{1,9},{2,10},{3,11},{4,12},{5,13},{6,14},{7,15},{8,0},{9,1},... | collective-permute-start | bytes 589832 | tf_op jit(solution)/shard_map/ppermute | solution.py:251
  154.4 10.9 %collective-permute-start.46 = (bf16[64,1536]{1,0:T(8,128)(2,1)S(1)}, bf16[64,1536]{1,0:T(8,128)(2,1)S(1)}, u32[]{:S(2)}, u32[]{:S(2)}) collective-permute-start(bf16[64,1536]{1,0:T(8,128)(2,1)S(1)} %get-tuple-element.219), channel_id=1, source_target_pairs={{0,16},{1,17},{2,18},{3,19},{4,20},{5,21},{6,22},{7,23},{8,24},{9,... | collective-permute-start | bytes 589832 | tf_op jit(solution)/shard_map/ppermute | solution.py:251
  155.4 9.8 %collective-permute-start.47 = (bf16[64,1536]{1,0:T(8,128)(2,1)S(1)}, bf16[64,1536]{1,0:T(8,128)(2,1)S(1)}, u32[]{:S(2)}, u32[]{:S(2)}) collective-permute-start(bf16[64,1536]{1,0:T(8,128)(2,1)S(1)} %get-tuple-element.220), channel_id=1, source_target_pairs={{0,24},{1,25},{2,26},{3,27},{4,28},{5,29},{6,30},{7,31},{8,16},{9,... | collective-permute-start | bytes 589832 | tf_op jit(solution)/shard_map/ppermute | solution.py:251
  161.6 23.4 %all-to-all-start.3 = ((bf16[4,592,128]{2,1,0:T(8,128)(2,1)}), bf16[4,592,128]{2,1,0:T(8,128)(2,1)S(1)}, u32[]{:S(2)}, u32[]{:S(2)}) async-start(bf16[4,592,128]{2,1,0:T(8,128)(2,1)} %bitcast.32), calls=%async_computation.3 | async-start | bytes 1212416 | tf_op jit(solution)/shard_map/all_to_all | solution.py:1056
  166.2 1.5 collective-permute-start.48
  167.8 21.1 %collective-permute-start.49 = (bf16[256,384]{1,0:T(8,128)(2,1)S(1)}, bf16[256,384]{1,0:T(8,128)(2,1)S(1)}, u32[]{:S(2)}, u32[]{:S(2)}) collective-permute-start(bf16[256,384]{1,0:T(8,128)(2,1)S(1)} %get-tuple-element.227), channel_id=1, source_target_pairs={{0,0},{1,5},{2,8},{3,13},{4,16},{5,21},{6,24},{7,29},{8,2},{9,7},{... | collective-permute-start | bytes 589832 | tf_op jit(solution)/shard_map/ppermute | solution.py:251
  168.5 20.4 %collective-permute-start.50 = (bf16[256,384]{1,0:T(8,128)(2,1)S(1)}, bf16[256,384]{1,0:T(8,128)(2,1)S(1)}, u32[]{:S(2)}, u32[]{:S(2)}) collective-permute-start(bf16[256,384]{1,0:T(8,128)(2,1)S(1)} %get-tuple-element.228), channel_id=1, source_target_pairs={{0,2},{1,7},{2,10},{3,15},{4,18},{5,23},{6,26},{7,31},{8,0},{9,5},... | collective-permute-start | bytes 589832 | tf_op jit(solution)/shard_map/ppermute | solution.py:251
  185.2 7.3 %collective-permute-start.53 = (bf16[592,128]{1,0:T(8,128)(2,1)S(1)}, bf16[592,128]{1,0:T(8,128)(2,1)S(1)}, u32[]{:S(2)}, u32[]{:S(2)}) collective-permute-start(bf16[592,128]{1,0:T(8,128)(2,1)S(1)} %get-tuple-element.240), channel_id=1, source_target_pairs={{0,8},{1,9},{2,10},{3,11},{4,12},{5,13},{6,14},{7,15},{8,0},{9,1},... | collective-permute-start | bytes 454664 | tf_op jit(solution)/shard_map/ppermute | solution.py:251
  186.7 8.0 %collective-permute-start.54 = (bf16[592,128]{1,0:T(8,128)(2,1)S(1)}, bf16[592,128]{1,0:T(8,128)(2,1)S(1)}, u32[]{:S(2)}, u32[]{:S(2)}) collective-permute-start(bf16[592,128]{1,0:T(8,128)(2,1)S(1)} %get-tuple-element.241), channel_id=1, source_target_pairs={{0,16},{1,17},{2,18},{3,19},{4,20},{5,21},{6,22},{7,23},{8,24},{9,... | collective-permute-start | bytes 454664 | tf_op jit(solution)/shard_map/ppermute | solution.py:251
  187.8 7.2 %collective-permute-start.55 = (bf16[592,128]{1,0:T(8,128)(2,1)S(1)}, bf16[592,128]{1,0:T(8,128)(2,1)S(1)}, u32[]{:S(2)}, u32[]{:S(2)}) collective-permute-start(bf16[592,128]{1,0:T(8,128)(2,1)S(1)} %get-tuple-element.242), channel_id=1, source_target_pairs={{0,24},{1,25},{2,26},{3,27},{4,28},{5,29},{6,30},{7,31},{8,16},{9,... | collective-permute-start | bytes 454664 | tf_op jit(solution)/shard_map/ppermute | solution.py:251
  188.9 6.1 %collective-permute-start.51 = (bf16[256,384]{1,0:T(8,128)(2,1)S(1)}, bf16[256,384]{1,0:T(8,128)(2,1)S(1)}, u32[]{:S(2)}, u32[]{:S(2)}) collective-permute-start(bf16[256,384]{1,0:T(8,128)(2,1)S(1)} %collective-permute-done.49.refs_0_), channel_id=1, source_target_pairs={{0,1},{1,0},{2,3},{3,2},{4,5},{5,4},{6,7},{7,6},{8,9},{9,8},{10,11... | collective-permute-start | bytes 589832 | tf_op jit(solution)/shard_map/ppermute | solution.py:251
  188.9 6.1 %collective-permute-start.52 = (bf16[256,384]{1,0:T(8,128)(2,1)S(1)}, bf16[256,384]{1,0:T(8,128)(2,1)S(1)}, u32[]{:S(2)}, u32[]{:S(2)}) collective-permute-start(bf16[256,384]{1,0:T(8,128)(2,1)S(1)} %collective-permute-done.50.refs_1_), channel_id=1, source_target_pairs={{0,1},{1,0},{2,3},{3,2},{4,5},{5,4},{6,7},{7,6},{8,9},{9,8},{10,11... | collective-permute-start | bytes 589832 | tf_op jit(solution)/shard_map/ppermute | solution.py:251
  196.1 1.4 collective-permute-start.56
  196.1 1.6 collective-permute-start.57
  196.6 1.4 collective-permute-start.58
  196.7 1.6 collective-permute-start.59
  (5 other events, 49.9 us)

commit v4 on v3

--- a/solution.py
+++ b/solution.py
@@ -10,7 +10,9 @@
 from jax.sharding import PartitionSpec as P
 
 CONVS = 2
-BACK_FLOPS = 6000000000
+BACK_FLOPS = (6 * 10**9, 6 * 10**9, 6 * 10**9, 0)
+PICK_FLOPS = 4 * 10**9
+COT_LAYER = 2
 INPUT_FLOPS = 4000000000
 
 
@@ -456,24 +458,23 @@
     return jnp.where(on, 1.0, 0.0)
 
 
-def frames_kernel(dims, group_table, size_table, images, cots, *refs):
-    payloads, (image_in, cot_in, groups, sizes, sems) = refs[:4], refs[4:]
+def frames_kernel(dims, group_table, size_table, images, *refs):
+    payloads, (image_in, groups, sizes, sems) = refs[:4], refs[4:]
     copies = start_all(
         [
             pltpu.make_async_copy(group_table, groups, sems.at[0]),
             pltpu.make_async_copy(size_table, sizes, sems.at[1]),
             pltpu.make_async_copy(images, image_in, sems.at[2]),
-            pltpu.make_async_copy(cots, cot_in, sems.at[3]),
         ]
     )
-    section, plane, _ = place()
+    _, plane, _ = place()
     rows, cols = dims
     cells = rows * cols
     at = lax.broadcasted_iota(jnp.int32, (cells, LANES), 0).astype(jnp.float32)
     row = jnp.floor((at + 0.5) * (1.0 / cols))
     col = at - row * cols
     channels = images.shape[2]
-    half = channels // 2
+    line = lax.broadcasted_iota(jnp.int32, (META_ROWS, channels), 0)
     wait_all(copies)
     for k in range(4):
         micro = plane ^ k
@@ -490,17 +491,38 @@
         for c in range(0, channels, LANES):
             piece = image[:, c : c + LANES].astype(jnp.float32) * on
             payloads[k][:cells, c : c + LANES] = piece.astype(jnp.bfloat16)
-        line = lax.broadcasted_iota(jnp.int32, (META_ROWS, channels + LANES), 0)
         payloads[k][cells:, :] = jnp.where(line == 0, height, breadth).astype(jnp.bfloat16)
-        tile = section // 2 * LANES
+
+
+def cot_slice_kernel(cots, out, cot_in, sems):
+    copy = pltpu.make_async_copy(cots, cot_in, sems.at[0])
+    copy.start()
+    section, _, _ = place()
+    micros, cells, channels = cots.shape
+    half = channels // 2
+    tile = section // 2 * LANES
+    odd = section % 2 == 1
+    lane = lax.broadcasted_iota(jnp.int32, (cells, LANES), 1)
+    copy.wait()
+    for micro in range(micros):
         low = cot_in[micro, :, pl.ds(pl.multiple_of(tile, LANES), LANES)].astype(jnp.float32)
         high = cot_in[micro, :, pl.ds(pl.multiple_of(half + tile, LANES), LANES)].astype(jnp.float32)
-        odd = section % 2 == 1
         low = jnp.where(odd, pltpu.roll(low, LANES // 2, 1), low)
         high = jnp.where(odd, high, pltpu.roll(high, LANES // 2, 1))
-        lane = lax.broadcasted_iota(jnp.int32, (cells, LANES), 1)
         both = jnp.where(lane < LANES // 2, low, high).astype(jnp.bfloat16)
-        payloads[k][:cells, channels:] = both
+        out[micro * cells : (micro + 1) * cells, :] = both
+
+
+def cot_kernel(own, other, pick, out, full):
+    _, _, core = place()
+    cells = full.shape[0] // 8
+    for n in range(4):
+        for j, block in enumerate((own, other)):
+            at = pl.multiple_of((2 * n + (core ^ j)) * cells, cells)
+            full[pl.ds(at, cells), :] = block[n * cells : (n + 1) * cells, :]
+    out[...] = lax.dot_general(pick[...], full[...], NT, preferred_element_type=jnp.float32).astype(
+        jnp.bfloat16
+    )
 
 
 def pack_kernel(gain, bias, weight, *refs):
@@ -521,8 +543,19 @@
             pltpu.make_async_copy(bias, tables.at[1], sems.at[TAPS + 1]),
         ]
     )
+    targets = [own, *outs[1:]]
+    own_copies = []
+    for tap in range(TAPS):
+        copies[tap].wait()
+        turned[tap % 2] = columns[tap].T
+        for k, out in enumerate(targets):
+            rows = pl.ds(pl.multiple_of((section ^ k) * ch, ch), ch)
+            out[tap * ch : (tap + 1) * ch, :] = turned[tap % 2, rows, :]
+        piece = pl.ds(tap * ch, ch)
+        own_copies += start_all(
+            [pltpu.make_async_copy(own.at[piece], outs[0].at[piece], sems.at[TAPS + 2 + tap])]
+        )
     wait_all(table_copies)
-    targets = [own, *outs[1:]]
     for k, out in enumerate(targets):
         lines = []
         tile = pl.multiple_of(start + (section ^ k) // 2 * LANES, LANES)
@@ -538,41 +571,28 @@
         out[TAPS * ch :, :] = jnp.zeros((META_ROWS, out.shape[1]), jnp.bfloat16)
         out[TAPS * ch :, :LANES] = jnp.concatenate(lines, axis=0).astype(jnp.bfloat16)
     tail = pl.ds(TAPS * ch, META_ROWS)
-    own_copies = start_all([pltpu.make_async_copy(own.at[tail], outs[0].at[tail], sems.at[2 * TAPS + 2])])
-    for tap in range(TAPS):
-        copies[tap].wait()
-        turned[...] = columns[tap].T
-        for k, out in enumerate(targets):
-            rows = pl.ds(pl.multiple_of((section ^ k) * ch, ch), ch)
-            out[tap * ch : (tap + 1) * ch, :] = turned[rows, :]
-        piece = pl.ds(tap * ch, ch)
-        own_copies += start_all(
-            [pltpu.make_async_copy(own.at[piece], outs[0].at[piece], sems.at[TAPS + 2 + tap])]
-        )
+    own_copies += start_all([pltpu.make_async_copy(own.at[tail], outs[0].at[tail], sems.at[2 * TAPS + 2])])
     wait_all(own_copies)
 
 
 def pick_kernel(layer, *refs):
-    sources, others, out, targets, sems = refs[:4], refs[4:-2], refs[-2], (), refs[-1]
-    if len(others) > 0:
-        others, out, targets = refs[4:5], refs[5], refs[6:7]
-    copies = [pick_layer(layer, sources, 0, out, sems.at[0])]
-    for other, target in zip(others, targets):
-        copies += start_all([pltpu.make_async_copy(other, target, sems.at[1])])
-    wait_all(copies)
-
-
-def forward_kernel(dims, layer, first, pooling, *refs):
-    blocks, weights, rest = refs[:8], refs[8 : 12 if first else 9], refs[12 if first else 9 :]
+    sources, (out, sems) = refs[:4], refs[4:]
+    pick_layer(layer, sources, 0, out, sems.at[0]).wait()
+
+
+def forward_kernel(dims, layer, first, picks, pooling, *refs):
+    blocks, weights, rest = refs[:8], refs[8 : 12 if picks else 9], refs[12 if picks else 9 :]
     rows, cols = dims
     cells = rows * cols
     if first:
-        facts, pick, hidden, kept, full_out, inside_out, cot_out, full, taps, stage, weight, metas, *rest = rest
-        cot_full, cot, sems = rest
-        copy = pick_layer(layer, weights, 0, weight, sems.at[2])
+        facts, hidden, kept, full_out, inside_out, full, taps, stage, weight, metas, sems = rest
+    elif picks:
+        inside, facts, hidden, kept, full_out, full, taps, stage, weight, sems = rest
     else:
         inside, facts, hidden, kept, full_out, full, taps, stage, sems = rest
         (weight,) = weights
+    if picks:
+        copy = pick_layer(layer, weights, 0, weight, sems.at[2])
     facts_now = facts[...]
     if first:
         channels = full.shape[1]
@@ -583,20 +603,14 @@
     full_copy.start()
     if first:
         assemble_frames(blocks, metas, slice(cells, cells + META_ROWS), slice(0, channels))
-        assemble_frames(blocks, cot_full, slice(0, cells), slice(channels, channels + LANES))
         inside_now = plane_inside(metas, facts_now)
         inside_out[...] = inside_now
-        copy.wait()
     else:
         inside_now = inside[...]
+    if picks:
+        copy.wait()
     ch = hidden.shape[0]
     tap_products(weight[: TAPS * ch, :], full, taps, first)
-    if first:
-        cot[...] = lax.dot_general(
-            pick[...], cot_full[...], NT, preferred_element_type=jnp.float32
-        ).astype(jnp.bfloat16)
-        cot_copy = pltpu.make_async_copy(cot, cot_out, sems.at[3])
-        cot_copy.start()
     pre = sum_taps(taps, facts_now, cols)
     normed, scale = normalise(pre, inside_now)
     length = normed.shape[1]
@@ -606,18 +620,14 @@
     kept_copy.start()
     gain, bias = affine(weight[TAPS * ch :, :], ch)
     hidden[...] = hidden_of(normed, gain, bias, inside_now, facts_now, cols, pooling).astype(jnp.bfloat16)
-    if first:
-        cot_copy.wait()
     full_copy.wait()
     kept_copy.wait()
 
 
 def turn_kernel(dims, layer, pooling, *refs):
     blocks, (weight, cot_in, inside, facts) = refs[:8], refs[8:12]
-    hidden_out, full_out, grad_pre, sums, full, taps, cot, hidden, sems = refs[12:]
+    hidden_out, full_out, grad_pre, sums, full, taps, hidden, sems = refs[12:]
     cols = dims[1]
-    cot_copy = pltpu.make_async_copy(cot_in, cot, sems.at[0])
-    cot_copy.start()
     assemble(blocks, full)
     full_copy = pltpu.make_async_copy(full, full_out, sems.at[1])
     full_copy.start()
@@ -630,9 +640,8 @@
     hidden[...] = hidden_of(normed, gain, bias, inside_now, facts_now, cols, pooling).astype(jnp.bfloat16)
     hidden_copy = pltpu.make_async_copy(hidden, hidden_out, sems.at[2])
     hidden_copy.start()
-    cot_copy.wait()
     grad_pre[...], shift_sum, slope_sum = norm_back(
-        cot[...].astype(jnp.float32), normed, scale, gain, bias, inside_now, facts_now, cols, pooling
+        cot_in[...].astype(jnp.float32), normed, scale, gain, bias, inside_now, facts_now, cols, pooling
     )
     keep_sums(sums, shift_sum, slope_sum)
     full_copy.wait()
@@ -698,9 +707,10 @@
 def store_share(value, sums, pieces):
     rows = value.shape[0]
     width = pieces[0].shape[1]
+    below = sums_rows(sums, rows // TAPS, width)
     for n, piece in enumerate(pieces):
         piece[:rows, :] = value[:, n * width : (n + 1) * width].astype(jnp.bfloat16)
-        piece[rows:, :] = sums_rows(sums, rows // TAPS, width)
+        piece[rows:, :] = below
 
 
 def form_share(layer, moved, full, sums, product):
@@ -815,8 +825,7 @@
         out[rows:, :] = got[n * rows : (n + 1) * rows, :]
 
 
-def maps_out_kernel(*refs):
-    blocks, pick, outs, full = refs[:4], refs[4], refs[5:7], refs[7]
+def store_maps(blocks, pick, outs, full):
     _, plane, core = place()
     ch = blocks[0].shape[0] // 4
     for m, out in enumerate(outs):
@@ -826,13 +835,15 @@
                     slot = slice_at(plane ^ (2 * (core ^ j) + n), core ^ j, 0, h)
                     at = pl.multiple_of(slot * ch, ch)
                     start = (2 * h + m) * ch
-                    full[pl.ds(at, ch), :] = blocks[2 * j + n][start : start + ch, :]
-        mine = lax.dot_general(pick[...], full[...], NT, preferred_element_type=jnp.float32)
+                    full[m, pl.ds(at, ch), :] = blocks[2 * j + n][start : start + ch, :]
+        mine = lax.dot_general(pick[...], full[m], NT, preferred_element_type=jnp.float32)
         out[...] = mine.astype(out.dtype)
 
 
-def grads_out_kernel(*refs):
-    blocks, pick, (weight_out, shift_out, slope_out), (full,) = refs[:8], refs[8], refs[9:12], refs[12:]
+def outputs_kernel(*refs):
+    blocks, pick, map_blocks, map_pick, refs = refs[:8], refs[8], refs[9:13], refs[13], refs[14:]
+    (weight_out, shift_out, slope_out), map_outs, (full, maps_full) = refs[:3], refs[3:5], refs[5:]
+    store_maps(map_blocks, map_pick, map_outs, maps_full)
     section, plane, core = place()
     taps, rows, channels = weight_out.shape
     for tap in range(taps):
@@ -852,17 +863,19 @@
     slope_out[...] = slope_row
 
 
-def call(kernel, outs, scratch, args, name, held=(), held_outs=(), loose=(), last=False, flops=0, copies=None):
+def call(
+    kernel, outs, scratch, args, name, held=(), free=(), held_outs=(), loose=(), last=False, flops=0, copies=None
+):
     shapes = [
         (jax.ShapeDtypeStruct if last else pltpu.HBM if n in held_outs else pltpu.VMEM)(shape, dtype)
         for n, (shape, dtype) in enumerate(outs)
     ]
     moved = sum(a.size * a.dtype.itemsize for a in args)
     moved += sum(math.prod(shape) * jnp.dtype(dtype).itemsize for shape, dtype in outs)
-    spaces = [pltpu.HBM if n in held else pltpu.VMEM for n in range(len(args))]
+    spaces = [pl.ANY if n in free else pltpu.HBM if n in held else pltpu.VMEM for n in range(len(args))]
     out_spaces = [pltpu.HBM if n in held_outs else pltpu.VMEM for n in range(len(outs))]
     args = [
-        a if n in loose else pltpu.with_memory_space_constraint(a, space)
+        a if n in loose or n in free else pltpu.with_memory_space_constraint(a, space)
         for n, (a, space) in enumerate(zip(args, spaces))
     ]
     scratch_shapes = [
@@ -915,7 +928,7 @@
         [
             weight_slice,
             ((TAPS, channels, 4 * ch), bf16),
-            ((4 * ch, channels), bf16),
+            ((2, 4 * ch, channels), bf16),
             ((2, 1, channels), f32),
         ],
         [bn_gain, bn_bias, taps_first],
@@ -926,62 +939,56 @@
     )
     slices = spread(packed, to_section)
 
-    payload = ((cells + META_ROWS, channels + LANES), bf16)
+    payload = ((cells + META_ROWS, channels), bf16)
     sent = call(
         partial(frames_kernel, dims),
         [payload] * 4,
-        [((micro_total, cells, channels), bf16)] * 2
-        + [(image_group.shape[::-1], jnp.int32), (group_size.shape[::-1], jnp.int32)],
         [
-            image_group.T,
-            group_size.T,
-            after(images.reshape(micro_total, cells, channels), packed),
-            cotangent.reshape(micro_total, cells, channels),
+            ((micro_total, cells, channels), bf16),
+            (image_group.shape[::-1], jnp.int32),
+            (group_size.shape[::-1], jnp.int32),
         ],
+        [image_group.T, group_size.T, after(images.reshape(micro_total, cells, channels), packed)],
         "frames",
-        held=range(4),
-        copies=4,
+        held=range(3),
+        copies=3,
     )
     frames_in = with_core(spread(sent, to_plane))
 
     half = (core * ch + np.arange(ch))[:, None] == np.arange(2 * ch)[None, :]
-    hidden, normed, full, inside, cot = call(
-        partial(forward_kernel, dims, 0, True, CONVS == 1),
-        [map_out, kept_out, full_frames, ((1, length), f32), map_out],
+    hidden, normed, full, inside = call(
+        partial(forward_kernel, dims, 0, True, True, CONVS == 1),
+        [map_out, kept_out, full_frames, ((1, length), f32)],
         [
             full_frames,
             tap_scratch,
             kept_out,
             weight_slice,
             ((frames * META_ROWS, channels), bf16),
-            ((length, LANES), bf16),
-            map_out,
         ],
-        [*frames_in, *slices, facts, half.astype(bf16)],
+        [*frames_in, *slices, facts],
         "forward",
         held=range(8, 12),
-        held_outs=(1, 2, 4),
-        loose=(12, 13),
+        held_outs=(1, 2),
+        loose=(12,),
         flops=conv_flops,
         copies=4,
     )
     kept, fulls = [normed], [full]
+    same_core = [[2 * z + c for z in range(layers)] for c in range(2)]
     for layer in range(1, layers):
-        stored = [turned[1]] if layer == last else []
-        weight, *stored = call(
+        picks = layer == COT_LAYER
+        weights = slices if picks else call(
             partial(pick_kernel, layer),
-            [weight_slice] + [((layers * 4 * ch, tap_rows), bf16)] * len(stored),
+            [weight_slice],
             [],
-            [*after(slices, hidden), *after(stored, hidden)],
+            after(slices, hidden),
             "pick",
+            flops=PICK_FLOPS,
             held=range(4),
-            held_outs=(1,),
-            loose=(4,),
-            copies=2,
+            copies=1,
         )
-        if stored:
-            turned[1] = stored[0]
-        beside = [weight]
+        beside = [] if picks else [*weights]
         if layer == 1:
             turned = call(
                 partial(turn_weights_kernel, layers),
@@ -998,32 +1005,57 @@
                 copies=layers,
             )
             beside.append(turned)
+        if layer == COT_LAYER - 1:
+            (cot_slots,) = call(
+                cot_slice_kernel,
+                [((micro_total * cells, LANES), bf16)],
+                [((micro_total, cells, channels), bf16)],
+                [after(cotangent.reshape(micro_total, cells, channels), hidden)],
+                "cot_slices",
+                held=(0,),
+                copies=1,
+            )
+            beside.append(cot_slots)
+        if layer == COT_LAYER:
+            cot_slots = after(cot_slots, hidden)
+            cots = lax.all_to_all(cot_slots, "dp", 0, 0, tiled=True, axis_index_groups=same_core)
         if layer == 2:
             turned = [turned[0], to_core(after(turned[1], hidden))]
+        if layer == last:
+            cots = after(cots, hidden)
+            (cot,) = call(
+                cot_kernel,
+                [map_out],
+                [((length, LANES), bf16)],
+                [cots, to_core(cots), half.astype(bf16)],
+                "cotangent",
+                loose=(0, 1, 2),
+            )
+            beside.append(cot)
         blocks = [hidden] + [to_section(hidden, k) for k in (1, 2, 3)]
         blocks[3] = after(blocks[3], *beside)
         blocks = with_core(blocks)
         if layer < last:
             hidden, normed, full = call(
-                partial(forward_kernel, dims, layer, False, layer == CONVS - 1),
+                partial(forward_kernel, dims, layer, False, picks, layer == CONVS - 1),
                 [map_out, kept_out, full_map],
-                [full_map, tap_scratch, kept_out],
-                [*blocks, weight, inside, facts],
+                [full_map, tap_scratch, kept_out] + [weight_slice] * picks,
+                [*blocks, *weights, inside, facts],
                 "forward",
+                held=range(8, 12) if picks else (),
                 held_outs=(1, 2),
-                loose=(9, 10),
+                loose=(12, 13) if picks else (9, 10),
                 flops=conv_flops,
-                copies=2,
+                copies=3,
             )
             kept.append(normed)
         else:
             activation, full, grad_pre, sums = call(
                 partial(turn_kernel, dims, last, last == CONVS - 1),
                 [map_out, full_map, map_out, sums_out],
-                [full_map, tap_scratch, map_out, map_out],
-                [*blocks, weight, cot, inside, facts],
+                [full_map, tap_scratch, map_out],
+                [*blocks, *weights, cot, inside, facts],
                 "turn",
-                held=(9,),
                 held_outs=(0, 1),
                 loose=(10, 11),
                 flops=conv_flops,
@@ -1032,7 +1064,6 @@
         fulls.append(full)
 
     shares = [None] * layers
-    same_core = [[2 * z + c for z in range(layers)] for c in range(2)]
     for layer in range(last, -1, -1):
         *parts, share = call(
             partial(conv_back_kernel, dims, layer),
@@ -1045,10 +1076,11 @@
             ],
             [grad_pre, to_core(grad_pre), *turned, fulls[layer], sums, facts],
             "conv_back",
-            held=(2, 3, 4),
+            held=(2, 4),
+            free=(3,),
             held_outs=(4,),
             loose=(5, 6),
-            flops=BACK_FLOPS,
+            flops=BACK_FLOPS[layer],
             copies=4,
         )
         if layer < last:
@@ -1105,24 +1137,20 @@
         loose=(0,),
     )
     pick = (core * cells + np.arange(cells))[:, None] == np.arange(2 * cells)[None, :]
-    activations, input_grad = call(
-        maps_out_kernel,
-        [((cells, channels), bf16)] * 2,
-        [((channels, 2 * cells), bf16)],
-        [*with_core(after(maps, chosen)), pick.astype(bf16)],
-        "maps_out",
-        loose=(4,),
-        last=True,
-    )
-
+    map_pick = pick.astype(bf16)
     pick = (core * ch + np.arange(ch))[:, None] == np.arange(2 * ch)[None, :]
-    weight_grad, bias_grad, gain_grad = call(
-        grads_out_kernel,
-        [((TAPS, ch, channels), f32), ((1, ch), f32), ((1, ch), f32)],
-        [((TAPS, channels, 2 * ch), bf16)],
-        [*with_core(after(spread(chosen, to_section), activations, input_grad)), pick.astype(bf16)],
-        "grads_out",
-        loose=(8,),
+    weight_grad, bias_grad, gain_grad, activations, input_grad = call(
+        outputs_kernel,
+        [((TAPS, ch, channels), f32), ((1, ch), f32), ((1, ch), f32)] + [((cells, channels), bf16)] * 2,
+        [((TAPS, channels, 2 * ch), bf16), ((2, channels, 2 * cells), bf16)],
+        [
+            *with_core([chosen[0]] + [to_section(chosen[k], k) for k in (1, 2, 3)]),
+            pick.astype(bf16),
+            *with_core(after(maps, chosen)),
+            map_pick,
+        ],
+        "outputs",
+        loose=(8, 13),
         last=True,
     )
     weight_grad = weight_grad.reshape(3, 3, ch, channels).transpose(2, 0, 1, 3)[None]

time: 201 us -> 198 us (0.985)
  waiting for transfers between devices: 78.8 us -> 73.6 us
  starting transfers between devices: 67.7 us -> 70.1 us
    ppermute x60 -> x61, waiting for transfers between devices: 56.4 us -> 50.1 us  [send(): return lax.ppermute(x, AXES, pairs)]
    all_to_all x0 -> x1, starting transfers between devices: none -> 4.87 us  [plane_shards(): lax.all_to_all(cot_slots, 'dp', 0, 0, tiled=True, axis_index_groups=same_...]
    ppermute x60 -> x61, starting transfers between devices: 50.8 us -> 48.4 us  [send(): return lax.ppermute(x, AXES, pairs)]
  transfers between devices with their start and end apart: 64 -> 66, of which waited for: 34 -> 35; matrix products, arithmetic and copies ran while one was open for 0% -> 0% of each run, Pallas kernels for 16% -> 18%
where the time goes in v4:
time: 198 us; the launch traced here: 197 us
  waiting for transfers between devices  73.6 us (37%)
  starting transfers between devices  70.1 us (35%)
  Pallas kernels  52 us (26%)
    pallas_call x26, Pallas kernels, call(): pl.pallas_call(kernel, out_shape=shapes, in_specs=[pl.BlockSpec(memory_sp...  52 us
    ppermute x61, waiting for transfers between devices, send(): return lax.ppermute(x, AXES, pairs)  50.1 us
    ppermute x61, starting transfers between devices, send(): return lax.ppermute(x, AXES, pairs)  48.4 us
    all_to_all x4, waiting for transfers between devices, plane_shards(): lax.all_to_all(share, 'dp', 0, 0, tiled=True, axis_index_groups=same_core)  23.5 us
    all_to_all x4, starting transfers between devices, plane_shards(): lax.all_to_all(share, 'dp', 0, 0, tiled=True, axis_index_groups=same_core)  16.9 us
    all_to_all x1, starting transfers between devices, plane_shards(): lax.all_to_all(cot_slots, 'dp', 0, 0, tiled=True, axis_index_groups=same_...  4.87 us
  transfers between devices with their start and end apart: 66, of which 35 were waited for; matrix products, arithmetic and copies ran while one was open for 0% of the time, Pallas kernels for 18%

profile of v4, /device:TPU:0, one launch (start us, length us, event | category | flops | bytes accessed | tf_op | source)
XLA Modules:
  0.0 197.1 jit_solution(16090404760888389964)
XLA Ops:
  0.6 3.2 %weight_pack.1 = (bf16[592,512]{1,0:T(8,128)(2,1)}, bf16[592,512]{1,0:T(8,128)(2,1)S(1)}, bf16[592,512]{1,0:T(8,128)(2,1)S(1)}, bf16[592,512]{1,0:T(8,128)(2,1)S(1)}) custom-call(f32[1,512]{1,0:T(1,128)} %gain.1, f32[1,512]{1,0:T(1,128)} %bias.1, bf16[9,512,512]{2,1,0:T(8,128)(2,1)} %bitcast.29), custom_call_target="tpu_custom_call" | custom-call | bytes 7147520 | tf_op jit(solution)/shard_map/weight_pack/pallas_call | solution.py:886
  3.8 3.0 %collective-permute-start.7 = (bf16[592,512]{1,0:T(8,128)(2,1)S(1)}, bf16[592,512]{1,0:T(8,128)(2,1)S(1)}, u32[]{:S(2)}, u32[]{:S(2)}) collective-permute-start(bf16[592,512]{1,0:T(8,128)(2,1)S(1)} %get-tuple-element.119), channel_id=1, source_target_pairs={{0,8},{1,9},{2,10},{3,11},{4,12},{5,13},{6,14},{7,15},{8,0},{9,1},... | collective-permute-start | bytes 1818632 | tf_op jit(solution)/shard_map/ppermute | solution.py:253
  6.9 1.5 collective-permute-start.8
  8.4 1.4 frames.1
  9.7 1.6 collective-permute-start
  11.8 2.6 %collective-permute-start.1 = (bf16[208,512]{1,0:T(8,128)(2,1)S(1)}, bf16[208,512]{1,0:T(8,128)(2,1)S(1)}, u32[]{:S(2)}, u32[]{:S(2)}) collective-permute-start(bf16[208,512]{1,0:T(8,128)(2,1)S(1)} %get-tuple-element.125), channel_id=1, source_target_pairs={{0,4},{1,5},{2,6},{3,7},{4,0},{5,1},{6,2},{7,3},{8,12},{9,13},{10,... | collective-permute-start | bytes 638984 | tf_op jit(solution)/shard_map/ppermute | solution.py:253
  14.4 6.1 %collective-permute-done.refs_1_ = bf16[208,512]{1,0:T(8,128)(2,1)S(1)} collective-permute-done((bf16[208,512]{1,0:T(8,128)(2,1)S(1)}, bf16[208,512]{1,0:T(8,128)(2,1)S(1)}, u32[]{:S(2)}, u32[]{:S(2)}) %collective-permute-start) | collective-permute-done | bytes 213024 | tf_op jit(solution)/shard_map/ppermute | solution.py:253
  20.5 2.5 %collective-permute-start.2 = (bf16[208,512]{1,0:T(8,128)(2,1)S(1)}, bf16[208,512]{1,0:T(8,128)(2,1)S(1)}, u32[]{:S(2)}, u32[]{:S(2)}) collective-permute-start(bf16[208,512]{1,0:T(8,128)(2,1)S(1)} %get-tuple-element.126), channel_id=1, source_target_pairs={{0,6},{1,7},{2,4},{3,5},{4,2},{5,3},{6,0},{7,1},{8,14},{9,15},{10,... | collective-permute-start | bytes 638984 | tf_op jit(solution)/shard_map/ppermute | solution.py:253
  23.0 2.8 %collective-permute-done.1.refs_2_ = bf16[208,512]{1,0:T(8,128)(2,1)S(1)} collective-permute-done((bf16[208,512]{1,0:T(8,128)(2,1)S(1)}, bf16[208,512]{1,0:T(8,128)(2,1)S(1)}, u32[]{:S(2)}, u32[]{:S(2)}) %collective-permute-start.1) | collective-permute-done | bytes 213024 | tf_op jit(solution)/shard_map/ppermute | solution.py:253
  25.7 2.5 %collective-permute-done.2.refs_3_ = bf16[208,512]{1,0:T(8,128)(2,1)S(1)} collective-permute-done((bf16[208,512]{1,0:T(8,128)(2,1)S(1)}, bf16[208,512]{1,0:T(8,128)(2,1)S(1)}, u32[]{:S(2)}, u32[]{:S(2)}) %collective-permute-start.2) | collective-permute-done | bytes 213024 | tf_op jit(solution)/shard_map/ppermute | solution.py:253
  28.8 6.2 %collective-permute-done.8.refs_10_.refs_2_ = bf16[592,512]{1,0:T(8,128)(2,1)S(1)} collective-permute-done((bf16[592,512]{1,0:T(8,128)(2,1)S(1)}, bf16[592,512]{1,0:T(8,128)(2,1)S(1)}, u32[]{:S(2)}, u32[]{:S(2)}) %collective-permute-start.8) | collective-permute-done | bytes 606240 | tf_op jit(solution)/shard_map/ppermute | solution.py:253
  35.0 1.4 collective-permute-done.6.refs_7_
  36.5 3.6 %forward.3 = (bf16[64,1536]{1,0:T(8,128)(2,1)S(1)}, f32[64,1664]{1,0:T(8,128)}, bf16[1536,512]{1,0:T(8,128)(2,1)}, f32[1,1536]{1,0:T(1,128)S(1)}) custom-call(bf16[208,512]{1,0:T(8,128)(2,1)S(1)} %get-tuple-element.123.refs_0_, bf16[208,512]{1,0:T(8,128)(2,1)S(1)} %collective-permute-done.refs_1_, bf16[208,512]{1,0:T(8,128)(2,1)S(1)} %collective-permute-done.1.refs_2_, ...), custom_call_target="tpu_custom_call" | custom-call | flops 905969664 | bytes 6428672 | tf_op jit(solution)/shard_map/forward/pallas_call | solution.py:886
  40.1 1.5 collective-permute-start.12
  41.6 1.5 collective-permute-start.10
  43.7 2.0 %cot_slices.1 = bf16[768,128]{1,0:T(8,128)(2,1)} custom-call(bf16[4,192,512]{2,1,0:T(8,128)(2,1)} %bitcast.31), custom_call_target="tpu_custom_call" | custom-call | bytes 983040 | tf_op jit(solution)/shard_map/cot_slices/pallas_call | solution.py:886
  45.7 3.8 %turn_weights.1 = (bf16[1024,640]{1,0:T(8,128)(2,1)}, bf16[1024,640]{1,0:T(8,128)(2,1)}) custom-call(bf16[592,512]{1,0:T(8,128)(2,1)} %get-tuple-element.145.refs_8_.refs_0_, bf16[592,512]{1,0:T(8,128)(2,1)} %copy-done.1, bf16[592,512]{1,0:T(8,128)(2,1)} %copy-done.2, bf16[592,512]{1,0:T(8,128)(2,1)} %copy-done.3), custom_call_target="tpu_custom_call" | custom-call | bytes 5046272 | tf_op jit(solution)/shard_map/turn_weights/pallas_call | solution.py:886
  49.5 1.1 pick.2.refs_8_
  51.1 1.2 collective-permute-done.10.refs_1_
  54.0 3.1 %forward.4 = (bf16[64,1536]{1,0:T(8,128)(2,1)S(1)}, f32[64,1664]{1,0:T(8,128)}, bf16[512,1536]{1,0:T(8,128)(2,1)}) custom-call(bf16[64,1536]{1,0:T(8,128)(2,1)S(1)} %get-tuple-element.133.refs_0_, bf16[64,1536]{1,0:T(8,128)(2,1)S(1)} %collective-permute-done.10.refs_1_, bf16[64,1536]{1,0:T(8,128)(2,1)S(1)} %collective-permute-done.11.refs_2_, ...), custom_call_target="tpu_custom_call" | custom-call | flops 905969664 | bytes 4478976 | tf_op jit(solution)/shard_map/forward/pallas_call | solution.py:886
  57.1 1.1 collective-permute-start.19
  58.3 1.5 collective-permute-start.17
  61.2 4.9 %all-to-all-start = ((bf16[4,192,128]{2,1,0:T(8,128)(2,1)}), bf16[4,192,128]{2,1,0:T(8,128)(2,1)S(1)}, u32[]{:S(2)}, u32[]{:S(2)}) async-start(bf16[4,192,128]{2,1,0:T(8,128)(2,1)} %bitcast.7), calls=%async_computation | async-start | bytes 393216 | tf_op jit(solution)/shard_map/all_to_all | solution.py:1021
  66.1 2.9 %collective-permute-done.17.refs_1_ = bf16[64,1536]{1,0:T(8,128)(2,1)S(1)} collective-permute-done((bf16[64,1536]{1,0:T(8,128)(2,1)S(1)}, bf16[64,1536]{1,0:T(8,128)(2,1)S(1)}, u32[]{:S(2)}, u32[]{:S(2)}) %collective-permute-start.17) | collective-permute-done | bytes 196640 | tf_op jit(solution)/shard_map/ppermute | solution.py:253
  70.8 3.6 %forward.5 = (bf16[64,1536]{1,0:T(8,128)(2,1)S(1)}, f32[64,1664]{1,0:T(8,128)}, bf16[512,1536]{1,0:T(8,128)(2,1)}) custom-call(bf16[64,1536]{1,0:T(8,128)(2,1)S(1)} %get-tuple-element.143.refs_0_, bf16[64,1536]{1,0:T(8,128)(2,1)S(1)} %collective-permute-done.17.refs_1_, bf16[64,1536]{1,0:T(8,128)(2,1)S(1)} %collective-permute-done.18.refs_2_, ...), custom_call_target="tpu_custom_call" | custom-call | flops 905969664 | bytes 6297600 | tf_op jit(solution)/shard_map/forward/pallas_call | solution.py:886
  74.4 1.1 collective-permute-start.26
  75.4 1.5 collective-permute-start.24
  77.9 1.1 pick.3.refs_8_
  79.9 3.2 %collective-permute-done.26.refs_3_ = bf16[64,1536]{1,0:T(8,128)(2,1)S(1)} collective-permute-done((bf16[64,1536]{1,0:T(8,128)(2,1)S(1)}, bf16[64,1536]{1,0:T(8,128)(2,1)S(1)}, u32[]{:S(2)}, u32[]{:S(2)}) %collective-permute-start.26) | collective-permute-done | bytes 196640 | tf_op jit(solution)/shard_map/ppermute | solution.py:253
  83.1 3.0 %collective-permute-done.24.refs_1_ = bf16[64,1536]{1,0:T(8,128)(2,1)S(1)} collective-permute-done((bf16[64,1536]{1,0:T(8,128)(2,1)S(1)}, bf16[64,1536]{1,0:T(8,128)(2,1)S(1)}, u32[]{:S(2)}, u32[]{:S(2)}) %collective-permute-start.24) | collective-permute-done | bytes 196640 | tf_op jit(solution)/shard_map/ppermute | solution.py:253
  87.9 2.7 %turn.1 = (bf16[64,1536]{1,0:T(8,128)(2,1)}, bf16[512,1536]{1,0:T(8,128)(2,1)}, bf16[64,1536]{1,0:T(8,128)(2,1)S(1)}, f32[64,256]{1,0:T(8,128)S(1)}) custom-call(bf16[64,1536]{1,0:T(8,128)(2,1)S(1)} %get-tuple-element.144.refs_0_, bf16[64,1536]{1,0:T(8,128)(2,1)S(1)} %collective-permute-done.24.refs_1_, ...), custom_call_target="tpu_custom_call" | custom-call | flops 905969664 | bytes 4511744 | tf_op jit(solution)/shard_map/turn/pallas_call | solution.py:886
  90.9 1.3 collective-permute-done.32.other
  92.2 3.9 %conv_back.4 = (bf16[64,1536]{1,0:T(8,128)(2,1)S(1)}, bf16[64,1536]{1,0:T(8,128)(2,1)S(1)}, bf16[64,1536]{1,0:T(8,128)(2,1)S(1)}, bf16[64,1536]{1,0:T(8,128)(2,1)S(1)}, bf16[2368,128]{1,0:T(8,128)(2,1)}) custom-call(bf16[64,1536]{1,0:T(8,128)(2,1)S(1)} %get-tuple-element.152.own, bf16[64,1536]{1,0:T(8,128)(2,1)S(1)} %collective-permute-done.32.other, ...), custom_call_target="tpu_custom_call" | custom-call | bytes 6144000 | tf_op jit(solution)/shard_map/conv_back/pallas_call | solution.py:886
  96.6 1.0 collective-permute-start.35
  97.7 1.9 collective-permute-start.36
  99.6 4.9 %all-to-all-start.1 = ((bf16[4,592,128]{2,1,0:T(8,128)(2,1)}), bf16[4,592,128]{2,1,0:T(8,128)(2,1)}, u32[]{:S(2)}, u32[]{:S(2)}) async-start(bf16[4,592,128]{2,1,0:T(8,128)(2,1)} %bitcast.35), calls=%async_computation.1 | async-start | bytes 1212416 | tf_op jit(solution)/shard_map/all_to_all | solution.py:1088
  105.5 2.2 %collective-permute-done.36.refs_3_ = bf16[64,1536]{1,0:T(8,128)(2,1)S(1)} collective-permute-done((bf16[64,1536]{1,0:T(8,128)(2,1)S(1)}, bf16[64,1536]{1,0:T(8,128)(2,1)S(1)}, u32[]{:S(2)}, u32[]{:S(2)}) %collective-permute-start.36) | collective-permute-done | bytes 196640 | tf_op jit(solution)/shard_map/ppermute | solution.py:253
  108.4 1.4 collective-permute-done.37.other
  109.8 3.9 %conv_back.5 = (bf16[64,1536]{1,0:T(8,128)(2,1)S(1)}, bf16[64,1536]{1,0:T(8,128)(2,1)S(1)}, bf16[64,1536]{1,0:T(8,128)(2,1)S(1)}, bf16[64,1536]{1,0:T(8,128)(2,1)S(1)}, bf16[2368,128]{1,0:T(8,128)(2,1)}) custom-call(bf16[64,1536]{1,0:T(8,128)(2,1)S(1)} %get-tuple-element.167.own, bf16[64,1536]{1,0:T(8,128)(2,1)S(1)} %collective-permute-done.37.other, ...), custom_call_target="tpu_custom_call" | custom-call | flops 6000000000 | bytes 6144000 | tf_op jit(solution)/shard_map/conv_back/pallas_call | solution.py:886
  113.7 1.3 collective-permute-start.38
  115.0 1.0 collective-permute-start.39
  116.1 1.2 collective-permute-start.40
  117.2 3.1 %all-to-all-done.1 = bf16[4,592,128]{2,1,0:T(8,128)(2,1)} async-done(((bf16[4,592,128]{2,1,0:T(8,128)(2,1)}), bf16[4,592,128]{2,1,0:T(8,128)(2,1)}, u32[]{:S(2)}, u32[]{:S(2)}) %all-to-all-start.1) | async-done | bytes 606240 | tf_op jit(solution)/shard_map/all_to_all | solution.py:1088
  120.3 4.4 %all-to-all-start.2 = ((bf16[4,592,128]{2,1,0:T(8,128)(2,1)}), bf16[4,592,128]{2,1,0:T(8,128)(2,1)}, u32[]{:S(2)}, u32[]{:S(2)}) async-start(bf16[4,592,128]{2,1,0:T(8,128)(2,1)} %bitcast.33), calls=%async_computation.2 | async-start | bytes 1212416 | tf_op jit(solution)/shard_map/all_to_all | solution.py:1088
  125.9 2.0 %norm_back.4 = (bf16[64,1536]{1,0:T(8,128)(2,1)S(1)}, f32[64,256]{1,0:T(8,128)S(1)}) custom-call(bf16[64,1536]{1,0:T(8,128)(2,1)S(1)} %get-tuple-element.170.refs_0_, bf16[64,1536]{1,0:T(8,128)(2,1)S(1)} %collective-permute-done.38.refs_1_, bf16[64,1536]{1,0:T(8,128)(2,1)S(1)} %collective-permute-done.39.refs_2_, ...), custom_call_target="tpu_custom_call" | custom-call | bytes 1595392 | tf_op jit(solution)/shard_map/norm_back/pallas_call | solution.py:886
  128.0 1.4 collective-permute-done.41.other
  129.5 3.9 %conv_back.6 = (bf16[64,1536]{1,0:T(8,128)(2,1)S(1)}, bf16[64,1536]{1,0:T(8,128)(2,1)S(1)}, bf16[64,1536]{1,0:T(8,128)(2,1)S(1)}, bf16[64,1536]{1,0:T(8,128)(2,1)S(1)}, bf16[2368,128]{1,0:T(8,128)(2,1)}) custom-call(bf16[64,1536]{1,0:T(8,128)(2,1)S(1)} %get-tuple-element.181.own, bf16[64,1536]{1,0:T(8,128)(2,1)S(1)} %collective-permute-done.41.other, ...), custom_call_target="tpu_custom_call" | custom-call | flops 6000000000 | bytes 6144000 | tf_op jit(solution)/shard_map/conv_back/pallas_call | solution.py:886
  135.1 1.8 collective-permute-start.44
  136.9 3.4 %all-to-all-done.2 = bf16[4,592,128]{2,1,0:T(8,128)(2,1)} async-done(((bf16[4,592,128]{2,1,0:T(8,128)(2,1)}), bf16[4,592,128]{2,1,0:T(8,128)(2,1)}, u32[]{:S(2)}, u32[]{:S(2)}) %all-to-all-start.2) | async-done | bytes 606240 | tf_op jit(solution)/shard_map/all_to_all | solution.py:1088
  140.3 4.2 %all-to-all-start.3 = ((bf16[4,592,128]{2,1,0:T(8,128)(2,1)}), bf16[4,592,128]{2,1,0:T(8,128)(2,1)}, u32[]{:S(2)}, u32[]{:S(2)}) async-start(bf16[4,592,128]{2,1,0:T(8,128)(2,1)} %bitcast.32), calls=%async_computation.3 | async-start | bytes 1212416 | tf_op jit(solution)/shard_map/all_to_all | solution.py:1088
  146.1 1.4 collective-permute-done.45.other
  147.6 3.8 %conv_back.7 = (bf16[64,1536]{1,0:T(8,128)(2,1)S(1)}, bf16[64,1536]{1,0:T(8,128)(2,1)S(1)}, bf16[64,1536]{1,0:T(8,128)(2,1)S(1)}, bf16[64,1536]{1,0:T(8,128)(2,1)S(1)}, bf16[2368,128]{1,0:T(8,128)(2,1)}) custom-call(bf16[64,1536]{1,0:T(8,128)(2,1)S(1)} %get-tuple-element.195.own, bf16[64,1536]{1,0:T(8,128)(2,1)S(1)} %collective-permute-done.45.other, ...), custom_call_target="tpu_custom_call" | custom-call | flops 6000000000 | bytes 6144000 | tf_op jit(solution)/shard_map/conv_back/pallas_call | solution.py:886
  153.3 1.7 collective-permute-start.55
  155.0 5.3 %all-to-all-done.3 = bf16[4,592,128]{2,1,0:T(8,128)(2,1)} async-done(((bf16[4,592,128]{2,1,0:T(8,128)(2,1)}), bf16[4,592,128]{2,1,0:T(8,128)(2,1)}, u32[]{:S(2)}, u32[]{:S(2)}) %all-to-all-start.3) | async-done | bytes 606240 | tf_op jit(solution)/shard_map/all_to_all | solution.py:1088
  160.2 3.5 %all-to-all-start.4 = ((bf16[4,592,128]{2,1,0:T(8,128)(2,1)}), bf16[4,592,128]{2,1,0:T(8,128)(2,1)S(1)}, u32[]{:S(2)}, u32[]{:S(2)}) async-start(bf16[4,592,128]{2,1,0:T(8,128)(2,1)} %bitcast.34), calls=%async_computation.4 | async-start | bytes 1212416 | tf_op jit(solution)/shard_map/all_to_all | solution.py:1088
  164.8 1.4 collective-permute-done.56.got
  167.0 3.4 %collective-permute-start.58 = (bf16[256,384]{1,0:T(8,128)(2,1)S(1)}, bf16[256,384]{1,0:T(8,128)(2,1)S(1)}, u32[]{:S(2)}, u32[]{:S(2)}) collective-permute-start(bf16[256,384]{1,0:T(8,128)(2,1)S(1)} %get-tuple-element.223), channel_id=1, source_target_pairs={{0,2},{1,7},{2,10},{3,15},{4,18},{5,23},{6,26},{7,31},{8,0},{9,5},... | collective-permute-start | bytes 589832 | tf_op jit(solution)/shard_map/ppermute | solution.py:253
  170.3 1.5 fold.1
  171.9 11.8 %all-to-all-done.4 = bf16[4,592,128]{2,1,0:T(8,128)(2,1)S(1)} async-done(((bf16[4,592,128]{2,1,0:T(8,128)(2,1)}), bf16[4,592,128]{2,1,0:T(8,128)(2,1)S(1)}, u32[]{:S(2)}, u32[]{:S(2)}) %all-to-all-start.4) | async-done | bytes 606240 | tf_op jit(solution)/shard_map/all_to_all | solution.py:1088
  183.9 1.5 collective-permute-start.46
  185.4 1.1 collective-permute-start.47
  188.0 3.1 %collective-permute-done.46.refs_1_ = bf16[592,128]{1,0:T(8,128)(2,1)S(1)} collective-permute-done((bf16[592,128]{1,0:T(8,128)(2,1)S(1)}, bf16[592,128]{1,0:T(8,128)(2,1)S(1)}, u32[]{:S(2)}, u32[]{:S(2)}) %collective-permute-start.46) | collective-permute-done | bytes 151584 | tf_op jit(solution)/shard_map/ppermute | solution.py:253
  191.2 2.2 %collective-permute-done.47.refs_2_ = bf16[592,128]{1,0:T(8,128)(2,1)S(1)} collective-permute-done((bf16[592,128]{1,0:T(8,128)(2,1)S(1)}, bf16[592,128]{1,0:T(8,128)(2,1)S(1)}, u32[]{:S(2)}, u32[]{:S(2)}) %collective-permute-start.47) | collective-permute-done | bytes 151584 | tf_op jit(solution)/shard_map/ppermute | solution.py:253
  195.2 1.9 outputs.1
  (106 shorter events, 25.0 us)
Async XLA Ops:
  3.8 24.5 %collective-permute-start.7 = (bf16[592,512]{1,0:T(8,128)(2,1)S(1)}, bf16[592,512]{1,0:T(8,128)(2,1)S(1)}, u32[]{:S(2)}, u32[]{:S(2)}) collective-permute-start(bf16[592,512]{1,0:T(8,128)(2,1)S(1)} %get-tuple-element.119), channel_id=1, source_target_pairs={{0,8},{1,9},{2,10},{3,11},{4,12},{5,13},{6,14},{7,15},{8,0},{9,1},... | collective-permute-start | bytes 1818632 | tf_op jit(solution)/shard_map/ppermute | solution.py:253
  6.9 28.1 %collective-permute-start.8 = (bf16[592,512]{1,0:T(8,128)(2,1)S(1)}, bf16[592,512]{1,0:T(8,128)(2,1)S(1)}, u32[]{:S(2)}, u32[]{:S(2)}) collective-permute-start(bf16[592,512]{1,0:T(8,128)(2,1)S(1)} %get-tuple-element.120), channel_id=1, source_target_pairs={{0,16},{1,17},{2,18},{3,19},{4,20},{5,21},{6,22},{7,23},{8,24},{9,... | collective-permute-start | bytes 1818632 | tf_op jit(solution)/shard_map/ppermute | solution.py:253
  9.7 10.8 %collective-permute-start = (bf16[208,512]{1,0:T(8,128)(2,1)S(1)}, bf16[208,512]{1,0:T(8,128)(2,1)S(1)}, u32[]{:S(2)}, u32[]{:S(2)}) collective-permute-start(bf16[208,512]{1,0:T(8,128)(2,1)S(1)} %get-tuple-element.124), channel_id=1, source_target_pairs={{0,2},{1,3},{2,0},{3,1},{4,6},{5,7},{6,4},{7,5},{8,10},{9,11},{10,... | collective-permute-start | bytes 638984 | tf_op jit(solution)/shard_map/ppermute | solution.py:253
  11.4 23.6 %collective-permute-start.9 = (bf16[592,512]{1,0:T(8,128)(2,1)S(1)}, bf16[592,512]{1,0:T(8,128)(2,1)S(1)}, u32[]{:S(2)}, u32[]{:S(2)}) collective-permute-start(bf16[592,512]{1,0:T(8,128)(2,1)S(1)} %get-tuple-element.121), channel_id=1, source_target_pairs={{0,24},{1,25},{2,26},{3,27},{4,28},{5,29},{6,30},{7,31},{8,16},{9,... | collective-permute-start | bytes 1818632 | tf_op jit(solution)/shard_map/ppermute | solution.py:253
  11.8 13.9 %collective-permute-start.1 = (bf16[208,512]{1,0:T(8,128)(2,1)S(1)}, bf16[208,512]{1,0:T(8,128)(2,1)S(1)}, u32[]{:S(2)}, u32[]{:S(2)}) collective-permute-start(bf16[208,512]{1,0:T(8,128)(2,1)S(1)} %get-tuple-element.125), channel_id=1, source_target_pairs={{0,4},{1,5},{2,6},{3,7},{4,0},{5,1},{6,2},{7,3},{8,12},{9,13},{10,... | collective-permute-start | bytes 638984 | tf_op jit(solution)/shard_map/ppermute | solution.py:253
  20.5 7.8 %collective-permute-start.2 = (bf16[208,512]{1,0:T(8,128)(2,1)S(1)}, bf16[208,512]{1,0:T(8,128)(2,1)S(1)}, u32[]{:S(2)}, u32[]{:S(2)}) collective-permute-start(bf16[208,512]{1,0:T(8,128)(2,1)S(1)} %get-tuple-element.126), channel_id=1, source_target_pairs={{0,6},{1,7},{2,4},{3,5},{4,2},{5,3},{6,0},{7,1},{8,14},{9,15},{10,... | collective-permute-start | bytes 638984 | tf_op jit(solution)/shard_map/ppermute | solution.py:253
  25.7 9.3 %collective-permute-start.3 = (bf16[208,512]{1,0:T(8,128)(2,1)S(1)}, bf16[208,512]{1,0:T(8,128)(2,1)S(1)}, u32[]{:S(2)}, u32[]{:S(2)}) collective-permute-start(bf16[208,512]{1,0:T(8,128)(2,1)S(1)} %get-tuple-element.123.refs_0_), channel_id=1, source_target_pairs={{0,1},{1,0},{2,3},{3,2},{4,5},{5,4},{6,7},{7,6},{8,9},{9,8},{10,11... | collective-permute-start | bytes 638984 | tf_op jit(solution)/shard_map/ppermute | solution.py:253
  28.3 6.8 %collective-permute-start.4 = (bf16[208,512]{1,0:T(8,128)(2,1)S(1)}, bf16[208,512]{1,0:T(8,128)(2,1)S(1)}, u32[]{:S(2)}, u32[]{:S(2)}) collective-permute-start(bf16[208,512]{1,0:T(8,128)(2,1)S(1)} %collective-permute-done.refs_1_), channel_id=1, source_target_pairs={{0,1},{1,0},{2,3},{3,2},{4,5},{5,4},{6,7},{7,6},{8,9},{9,8},{10,11... | collective-permute-start | bytes 638984 | tf_op jit(solution)/shard_map/ppermute | solution.py:253
  28.3 6.8 %collective-permute-start.5 = (bf16[208,512]{1,0:T(8,128)(2,1)S(1)}, bf16[208,512]{1,0:T(8,128)(2,1)S(1)}, u32[]{:S(2)}, u32[]{:S(2)}) collective-permute-start(bf16[208,512]{1,0:T(8,128)(2,1)S(1)} %collective-permute-done.1.refs_2_), channel_id=1, source_target_pairs={{0,1},{1,0},{2,3},{3,2},{4,5},{5,4},{6,7},{7,6},{8,9},{9,8},{10,11... | collective-permute-start | bytes 638984 | tf_op jit(solution)/shard_map/ppermute | solution.py:253
  35.0 1.5 collective-permute-start.6
  40.1 10.4 %collective-permute-start.12 = (bf16[64,1536]{1,0:T(8,128)(2,1)S(1)}, bf16[64,1536]{1,0:T(8,128)(2,1)S(1)}, u32[]{:S(2)}, u32[]{:S(2)}) collective-permute-start(bf16[64,1536]{1,0:T(8,128)(2,1)S(1)} %get-tuple-element.133.refs_0_), channel_id=1, source_target_pairs={{0,24},{1,25},{2,26},{3,27},{4,28},{5,29},{6,30},{7,31},{8,16},{9,... | collective-permute-start | bytes 589832 | tf_op jit(solution)/shard_map/ppermute | solution.py:253
  41.6 10.7 %collective-permute-start.10 = (bf16[64,1536]{1,0:T(8,128)(2,1)S(1)}, bf16[64,1536]{1,0:T(8,128)(2,1)S(1)}, u32[]{:S(2)}, u32[]{:S(2)}) collective-permute-start(bf16[64,1536]{1,0:T(8,128)(2,1)S(1)} %get-tuple-element.133.refs_0_), channel_id=1, source_target_pairs={{0,8},{1,9},{2,10},{3,11},{4,12},{5,13},{6,14},{7,15},{8,0},{9,1},... | collective-permute-start | bytes 589832 | tf_op jit(solution)/shard_map/ppermute | solution.py:253
  43.1 9.2 %collective-permute-start.11 = (bf16[64,1536]{1,0:T(8,128)(2,1)S(1)}, bf16[64,1536]{1,0:T(8,128)(2,1)S(1)}, u32[]{:S(2)}, u32[]{:S(2)}) collective-permute-start(bf16[64,1536]{1,0:T(8,128)(2,1)S(1)} %get-tuple-element.133.refs_0_), channel_id=1, source_target_pairs={{0,16},{1,17},{2,18},{3,19},{4,20},{5,21},{6,22},{7,23},{8,24},{9,... | collective-permute-start | bytes 589832 | tf_op jit(solution)/shard_map/ppermute | solution.py:253
  43.7 9.2 %collective-permute-start.13 = (bf16[64,1536]{1,0:T(8,128)(2,1)S(1)}, bf16[64,1536]{1,0:T(8,128)(2,1)S(1)}, u32[]{:S(2)}, u32[]{:S(2)}) collective-permute-start(bf16[64,1536]{1,0:T(8,128)(2,1)S(1)} %get-tuple-element.133.refs_0_), channel_id=1, source_target_pairs={{0,1},{1,0},{2,3},{3,2},{4,5},{5,4},{6,7},{7,6},{8,9},{9,8},{10,11... | collective-permute-start | bytes 589832 | tf_op jit(solution)/shard_map/ppermute | solution.py:253
  50.6 2.3 %collective-permute-start.16 = (bf16[64,1536]{1,0:T(8,128)(2,1)S(1)}, bf16[64,1536]{1,0:T(8,128)(2,1)S(1)}, u32[]{:S(2)}, u32[]{:S(2)}) collective-permute-start(bf16[64,1536]{1,0:T(8,128)(2,1)S(1)} %collective-permute-done.12.refs_3_), channel_id=1, source_target_pairs={{0,1},{1,0},{2,3},{3,2},{4,5},{5,4},{6,7},{7,6},{8,9},{9,8},{10,11... | collective-permute-start | bytes 589832 | tf_op jit(solution)/shard_map/ppermute | solution.py:253
  52.3 1.4 collective-permute-start.14
  52.3 1.7 collective-permute-start.15
  57.1 8.9 %collective-permute-start.19 = (bf16[64,1536]{1,0:T(8,128)(2,1)S(1)}, bf16[64,1536]{1,0:T(8,128)(2,1)S(1)}, u32[]{:S(2)}, u32[]{:S(2)}) collective-permute-start(bf16[64,1536]{1,0:T(8,128)(2,1)S(1)} %get-tuple-element.143.refs_0_), channel_id=1, source_target_pairs={{0,24},{1,25},{2,26},{3,27},{4,28},{5,29},{6,30},{7,31},{8,16},{9,... | collective-permute-start | bytes 589832 | tf_op jit(solution)/shard_map/ppermute | solution.py:253
  58.3 10.7 %collective-permute-start.17 = (bf16[64,1536]{1,0:T(8,128)(2,1)S(1)}, bf16[64,1536]{1,0:T(8,128)(2,1)S(1)}, u32[]{:S(2)}, u32[]{:S(2)}) collective-permute-start(bf16[64,1536]{1,0:T(8,128)(2,1)S(1)} %get-tuple-element.143.refs_0_), channel_id=1, source_target_pairs={{0,8},{1,9},{2,10},{3,11},{4,12},{5,13},{6,14},{7,15},{8,0},{9,1},... | collective-permute-start | bytes 589832 | tf_op jit(solution)/shard_map/ppermute | solution.py:253
  59.8 9.6 %collective-permute-start.18 = (bf16[64,1536]{1,0:T(8,128)(2,1)S(1)}, bf16[64,1536]{1,0:T(8,128)(2,1)S(1)}, u32[]{:S(2)}, u32[]{:S(2)}) collective-permute-start(bf16[64,1536]{1,0:T(8,128)(2,1)S(1)} %get-tuple-element.143.refs_0_), channel_id=1, source_target_pairs={{0,16},{1,17},{2,18},{3,19},{4,20},{5,21},{6,22},{7,23},{8,24},{9,... | collective-permute-start | bytes 589832 | tf_op jit(solution)/shard_map/ppermute | solution.py:253
  60.7 31.5 %collective-permute-start.33 = (bf16[1024,640]{1,0:T(8,128)(2,1)}, bf16[1024,640]{1,0:T(8,128)(2,1)S(1)}, u32[]{:S(2)}, u32[]{:S(2)}) collective-permute-start(bf16[1024,640]{1,0:T(8,128)(2,1)} %get-tuple-element.153), channel_id=1, source_target_pairs={{0,1},{1,0},{2,3},{3,2},{4,5},{5,4},{6,7},{7,6},{8,9},{9,8},{10,11... | collective-permute-start | bytes 3932168 | tf_op jit(solution)/shard_map/ppermute | solution.py:253
  60.7 8.9 %collective-permute-start.20 = (bf16[64,1536]{1,0:T(8,128)(2,1)S(1)}, bf16[64,1536]{1,0:T(8,128)(2,1)S(1)}, u32[]{:S(2)}, u32[]{:S(2)}) collective-permute-start(bf16[64,1536]{1,0:T(8,128)(2,1)S(1)} %get-tuple-element.143.refs_0_), channel_id=1, source_target_pairs={{0,1},{1,0},{2,3},{3,2},{4,5},{5,4},{6,7},{7,6},{8,9},{9,8},{10,11... | collective-permute-start | bytes 589832 | tf_op jit(solution)/shard_map/ppermute | solution.py:253
  61.2 16.7 %all-to-all-start = ((bf16[4,192,128]{2,1,0:T(8,128)(2,1)}), bf16[4,192,128]{2,1,0:T(8,128)(2,1)S(1)}, u32[]{:S(2)}, u32[]{:S(2)}) async-start(bf16[4,192,128]{2,1,0:T(8,128)(2,1)} %bitcast.7), calls=%async_computation | async-start | bytes 393216 | tf_op jit(solution)/shard_map/all_to_all | solution.py:1021
  66.1 4.7 %collective-permute-start.23 = (bf16[64,1536]{1,0:T(8,128)(2,1)S(1)}, bf16[64,1536]{1,0:T(8,128)(2,1)S(1)}, u32[]{:S(2)}, u32[]{:S(2)}) collective-permute-start(bf16[64,1536]{1,0:T(8,128)(2,1)S(1)} %collective-permute-done.19.refs_3_), channel_id=1, source_target_pairs={{0,1},{1,0},{2,3},{3,2},{4,5},{5,4},{6,7},{7,6},{8,9},{9,8},{10,11... | collective-permute-start | bytes 589832 | tf_op jit(solution)/shard_map/ppermute | solution.py:253
  69.0 1.4 collective-permute-start.21
  69.3 1.4 collective-permute-start.22
  74.4 8.8 %collective-permute-start.26 = (bf16[64,1536]{1,0:T(8,128)(2,1)S(1)}, bf16[64,1536]{1,0:T(8,128)(2,1)S(1)}, u32[]{:S(2)}, u32[]{:S(2)}) collective-permute-start(bf16[64,1536]{1,0:T(8,128)(2,1)S(1)} %get-tuple-element.144.refs_0_), channel_id=1, source_target_pairs={{0,24},{1,25},{2,26},{3,27},{4,28},{5,29},{6,30},{7,31},{8,16},{9,... | collective-permute-start | bytes 589832 | tf_op jit(solution)/shard_map/ppermute | solution.py:253
  75.4 10.7 %collective-permute-start.24 = (bf16[64,1536]{1,0:T(8,128)(2,1)S(1)}, bf16[64,1536]{1,0:T(8,128)(2,1)S(1)}, u32[]{:S(2)}, u32[]{:S(2)}) collective-permute-start(bf16[64,1536]{1,0:T(8,128)(2,1)S(1)} %get-tuple-element.144.refs_0_), channel_id=1, source_target_pairs={{0,8},{1,9},{2,10},{3,11},{4,12},{5,13},{6,14},{7,15},{8,0},{9,1},... | collective-permute-start | bytes 589832 | tf_op jit(solution)/shard_map/ppermute | solution.py:253
  76.9 9.6 %collective-permute-start.25 = (bf16[64,1536]{1,0:T(8,128)(2,1)S(1)}, bf16[64,1536]{1,0:T(8,128)(2,1)S(1)}, u32[]{:S(2)}, u32[]{:S(2)}) collective-permute-start(bf16[64,1536]{1,0:T(8,128)(2,1)S(1)} %get-tuple-element.144.refs_0_), channel_id=1, source_target_pairs={{0,16},{1,17},{2,18},{3,19},{4,20},{5,21},{6,22},{7,23},{8,24},{9,... | collective-permute-start | bytes 589832 | tf_op jit(solution)/shard_map/ppermute | solution.py:253
  77.9 1.4 collective-permute-start.27
  79.4 7.3 %collective-permute-start.28 = (bf16[64,1536]{1,0:T(8,128)(2,1)S(1)}, bf16[64,1536]{1,0:T(8,128)(2,1)S(1)}, u32[]{:S(2)}, u32[]{:S(2)}) collective-permute-start(bf16[64,1536]{1,0:T(8,128)(2,1)S(1)} %get-tuple-element.144.refs_0_), channel_id=1, source_target_pairs={{0,1},{1,0},{2,3},{3,2},{4,5},{5,4},{6,7},{7,6},{8,9},{9,8},{10,11... | collective-permute-start | bytes 589832 | tf_op jit(solution)/shard_map/ppermute | solution.py:253
  83.1 3.5 %collective-permute-start.31 = (bf16[64,1536]{1,0:T(8,128)(2,1)S(1)}, bf16[64,1536]{1,0:T(8,128)(2,1)S(1)}, u32[]{:S(2)}, u32[]{:S(2)}) collective-permute-start(bf16[64,1536]{1,0:T(8,128)(2,1)S(1)} %collective-permute-done.26.refs_3_), channel_id=1, source_target_pairs={{0,1},{1,0},{2,3},{3,2},{4,5},{5,4},{6,7},{7,6},{8,9},{9,8},{10,11... | collective-permute-start | bytes 589832 | tf_op jit(solution)/shard_map/ppermute | solution.py:253
  86.1 1.4 collective-permute-start.29
  86.5 1.4 collective-permute-start.30
  90.7 1.5 collective-permute-start.32
  96.1 9.5 %collective-permute-start.34 = (bf16[64,1536]{1,0:T(8,128)(2,1)S(1)}, bf16[64,1536]{1,0:T(8,128)(2,1)S(1)}, u32[]{:S(2)}, u32[]{:S(2)}) collective-permute-start(bf16[64,1536]{1,0:T(8,128)(2,1)S(1)} %get-tuple-element.157), channel_id=1, source_target_pairs={{0,8},{1,9},{2,10},{3,11},{4,12},{5,13},{6,14},{7,15},{8,0},{9,1},... | collective-permute-start | bytes 589832 | tf_op jit(solution)/shard_map/ppermute | solution.py:253
  96.6 8.9 %collective-permute-start.35 = (bf16[64,1536]{1,0:T(8,128)(2,1)S(1)}, bf16[64,1536]{1,0:T(8,128)(2,1)S(1)}, u32[]{:S(2)}, u32[]{:S(2)}) collective-permute-start(bf16[64,1536]{1,0:T(8,128)(2,1)S(1)} %get-tuple-element.158), channel_id=1, source_target_pairs={{0,16},{1,17},{2,18},{3,19},{4,20},{5,21},{6,22},{7,23},{8,24},{9,... | collective-permute-start | bytes 589832 | tf_op jit(solution)/shard_map/ppermute | solution.py:253
  97.7 10.1 %collective-permute-start.36 = (bf16[64,1536]{1,0:T(8,128)(2,1)S(1)}, bf16[64,1536]{1,0:T(8,128)(2,1)S(1)}, u32[]{:S(2)}, u32[]{:S(2)}) collective-permute-start(bf16[64,1536]{1,0:T(8,128)(2,1)S(1)} %get-tuple-element.159), channel_id=1, source_target_pairs={{0,24},{1,25},{2,26},{3,27},{4,28},{5,29},{6,30},{7,31},{8,16},{9,... | collective-permute-start | bytes 589832 | tf_op jit(solution)/shard_map/ppermute | solution.py:253
  99.6 20.7 %all-to-all-start.1 = ((bf16[4,592,128]{2,1,0:T(8,128)(2,1)}), bf16[4,592,128]{2,1,0:T(8,128)(2,1)}, u32[]{:S(2)}, u32[]{:S(2)}) async-start(bf16[4,592,128]{2,1,0:T(8,128)(2,1)} %bitcast.35), calls=%async_computation.1 | async-start | bytes 1212416 | tf_op jit(solution)/shard_map/all_to_all | solution.py:1088
  108.3 1.5 collective-permute-start.37
  113.7 12.1 %collective-permute-start.38 = (bf16[64,1536]{1,0:T(8,128)(2,1)S(1)}, bf16[64,1536]{1,0:T(8,128)(2,1)S(1)}, u32[]{:S(2)}, u32[]{:S(2)}) collective-permute-start(bf16[64,1536]{1,0:T(8,128)(2,1)S(1)} %get-tuple-element.171), channel_id=1, source_target_pairs={{0,8},{1,9},{2,10},{3,11},{4,12},{5,13},{6,14},{7,15},{8,0},{9,1},... | collective-permute-start | bytes 589832 | tf_op jit(solution)/shard_map/ppermute | solution.py:253
  115.0 10.9 %collective-permute-start.39 = (bf16[64,1536]{1,0:T(8,128)(2,1)S(1)}, bf16[64,1536]{1,0:T(8,128)(2,1)S(1)}, u32[]{:S(2)}, u32[]{:S(2)}) collective-permute-start(bf16[64,1536]{1,0:T(8,128)(2,1)S(1)} %get-tuple-element.172), channel_id=1, source_target_pairs={{0,16},{1,17},{2,18},{3,19},{4,20},{5,21},{6,22},{7,23},{8,24},{9,... | collective-permute-start | bytes 589832 | tf_op jit(solution)/shard_map/ppermute | solution.py:253
  116.1 9.8 %collective-permute-start.40 = (bf16[64,1536]{1,0:T(8,128)(2,1)S(1)}, bf16[64,1536]{1,0:T(8,128)(2,1)S(1)}, u32[]{:S(2)}, u32[]{:S(2)}) collective-permute-start(bf16[64,1536]{1,0:T(8,128)(2,1)S(1)} %get-tuple-element.173), channel_id=1, source_target_pairs={{0,24},{1,25},{2,26},{3,27},{4,28},{5,29},{6,30},{7,31},{8,16},{9,... | collective-permute-start | bytes 589832 | tf_op jit(solution)/shard_map/ppermute | solution.py:253
  120.3 20.0 %all-to-all-start.2 = ((bf16[4,592,128]{2,1,0:T(8,128)(2,1)}), bf16[4,592,128]{2,1,0:T(8,128)(2,1)}, u32[]{:S(2)}, u32[]{:S(2)}) async-start(bf16[4,592,128]{2,1,0:T(8,128)(2,1)} %bitcast.33), calls=%async_computation.2 | async-start | bytes 1212416 | tf_op jit(solution)/shard_map/all_to_all | solution.py:1088
  128.0 1.5 collective-permute-start.41
  133.3 12.1 %collective-permute-start.42 = (bf16[64,1536]{1,0:T(8,128)(2,1)S(1)}, bf16[64,1536]{1,0:T(8,128)(2,1)S(1)}, u32[]{:S(2)}, u32[]{:S(2)}) collective-permute-start(bf16[64,1536]{1,0:T(8,128)(2,1)S(1)} %get-tuple-element.185), channel_id=1, source_target_pairs={{0,8},{1,9},{2,10},{3,11},{4,12},{5,13},{6,14},{7,15},{8,0},{9,1},... | collective-permute-start | bytes 589832 | tf_op jit(solution)/shard_map/ppermute | solution.py:253
  134.1 11.4 %collective-permute-start.43 = (bf16[64,1536]{1,0:T(8,128)(2,1)S(1)}, bf16[64,1536]{1,0:T(8,128)(2,1)S(1)}, u32[]{:S(2)}, u32[]{:S(2)}) collective-permute-start(bf16[64,1536]{1,0:T(8,128)(2,1)S(1)} %get-tuple-element.186), channel_id=1, source_target_pairs={{0,16},{1,17},{2,18},{3,19},{4,20},{5,21},{6,22},{7,23},{8,24},{9,... | collective-permute-start | bytes 589832 | tf_op jit(solution)/shard_map/ppermute | solution.py:253
  135.1 10.4 %collective-permute-start.44 = (bf16[64,1536]{1,0:T(8,128)(2,1)S(1)}, bf16[64,1536]{1,0:T(8,128)(2,1)S(1)}, u32[]{:S(2)}, u32[]{:S(2)}) collective-permute-start(bf16[64,1536]{1,0:T(8,128)(2,1)S(1)} %get-tuple-element.187), channel_id=1, source_target_pairs={{0,24},{1,25},{2,26},{3,27},{4,28},{5,29},{6,30},{7,31},{8,16},{9,... | collective-permute-start | bytes 589832 | tf_op jit(solution)/shard_map/ppermute | solution.py:253
  140.3 20.0 %all-to-all-start.3 = ((bf16[4,592,128]{2,1,0:T(8,128)(2,1)}), bf16[4,592,128]{2,1,0:T(8,128)(2,1)}, u32[]{:S(2)}, u32[]{:S(2)}) async-start(bf16[4,592,128]{2,1,0:T(8,128)(2,1)} %bitcast.32), calls=%async_computation.3 | async-start | bytes 1212416 | tf_op jit(solution)/shard_map/all_to_all | solution.py:1088
  146.1 1.5 collective-permute-start.45
  151.4 12.3 %collective-permute-start.53 = (bf16[64,1536]{1,0:T(8,128)(2,1)S(1)}, bf16[64,1536]{1,0:T(8,128)(2,1)S(1)}, u32[]{:S(2)}, u32[]{:S(2)}) collective-permute-start(bf16[64,1536]{1,0:T(8,128)(2,1)S(1)} %get-tuple-element.213), channel_id=1, source_target_pairs={{0,8},{1,9},{2,10},{3,11},{4,12},{5,13},{6,14},{7,15},{8,0},{9,1},... | collective-permute-start | bytes 589832 | tf_op jit(solution)/shard_map/ppermute | solution.py:253
  152.3 11.5 %collective-permute-start.54 = (bf16[64,1536]{1,0:T(8,128)(2,1)S(1)}, bf16[64,1536]{1,0:T(8,128)(2,1)S(1)}, u32[]{:S(2)}, u32[]{:S(2)}) collective-permute-start(bf16[64,1536]{1,0:T(8,128)(2,1)S(1)} %get-tuple-element.214), channel_id=1, source_target_pairs={{0,16},{1,17},{2,18},{3,19},{4,20},{5,21},{6,22},{7,23},{8,24},{9,... | collective-permute-start | bytes 589832 | tf_op jit(solution)/shard_map/ppermute | solution.py:253
  153.3 10.5 %collective-permute-start.55 = (bf16[64,1536]{1,0:T(8,128)(2,1)S(1)}, bf16[64,1536]{1,0:T(8,128)(2,1)S(1)}, u32[]{:S(2)}, u32[]{:S(2)}) collective-permute-start(bf16[64,1536]{1,0:T(8,128)(2,1)S(1)} %get-tuple-element.215), channel_id=1, source_target_pairs={{0,24},{1,25},{2,26},{3,27},{4,28},{5,29},{6,30},{7,31},{8,16},{9,... | collective-permute-start | bytes 589832 | tf_op jit(solution)/shard_map/ppermute | solution.py:253
  160.2 23.4 %all-to-all-start.4 = ((bf16[4,592,128]{2,1,0:T(8,128)(2,1)}), bf16[4,592,128]{2,1,0:T(8,128)(2,1)S(1)}, u32[]{:S(2)}, u32[]{:S(2)}) async-start(bf16[4,592,128]{2,1,0:T(8,128)(2,1)} %bitcast.34), calls=%async_computation.4 | async-start | bytes 1212416 | tf_op jit(solution)/shard_map/all_to_all | solution.py:1088
  164.7 1.5 collective-permute-start.56
  166.3 21.2 %collective-permute-start.57 = (bf16[256,384]{1,0:T(8,128)(2,1)S(1)}, bf16[256,384]{1,0:T(8,128)(2,1)S(1)}, u32[]{:S(2)}, u32[]{:S(2)}) collective-permute-start(bf16[256,384]{1,0:T(8,128)(2,1)S(1)} %get-tuple-element.222), channel_id=1, source_target_pairs={{0,0},{1,5},{2,8},{3,13},{4,16},{5,21},{6,24},{7,29},{8,2},{9,7},{... | collective-permute-start | bytes 589832 | tf_op jit(solution)/shard_map/ppermute | solution.py:253
  167.0 20.5 %collective-permute-start.58 = (bf16[256,384]{1,0:T(8,128)(2,1)S(1)}, bf16[256,384]{1,0:T(8,128)(2,1)S(1)}, u32[]{:S(2)}, u32[]{:S(2)}) collective-permute-start(bf16[256,384]{1,0:T(8,128)(2,1)S(1)} %get-tuple-element.223), channel_id=1, source_target_pairs={{0,2},{1,7},{2,10},{3,15},{4,18},{5,23},{6,26},{7,31},{8,0},{9,5},... | collective-permute-start | bytes 589832 | tf_op jit(solution)/shard_map/ppermute | solution.py:253
  183.9 7.3 %collective-permute-start.46 = (bf16[592,128]{1,0:T(8,128)(2,1)S(1)}, bf16[592,128]{1,0:T(8,128)(2,1)S(1)}, u32[]{:S(2)}, u32[]{:S(2)}) collective-permute-start(bf16[592,128]{1,0:T(8,128)(2,1)S(1)} %get-tuple-element.209), channel_id=1, source_target_pairs={{0,8},{1,9},{2,10},{3,11},{4,12},{5,13},{6,14},{7,15},{8,0},{9,1},... | collective-permute-start | bytes 454664 | tf_op jit(solution)/shard_map/ppermute | solution.py:253
  185.4 7.9 %collective-permute-start.47 = (bf16[592,128]{1,0:T(8,128)(2,1)S(1)}, bf16[592,128]{1,0:T(8,128)(2,1)S(1)}, u32[]{:S(2)}, u32[]{:S(2)}) collective-permute-start(bf16[592,128]{1,0:T(8,128)(2,1)S(1)} %get-tuple-element.210), channel_id=1, source_target_pairs={{0,16},{1,17},{2,18},{3,19},{4,20},{5,21},{6,22},{7,23},{8,24},{9,... | collective-permute-start | bytes 454664 | tf_op jit(solution)/shard_map/ppermute | solution.py:253
  186.5 7.1 %collective-permute-start.48 = (bf16[592,128]{1,0:T(8,128)(2,1)S(1)}, bf16[592,128]{1,0:T(8,128)(2,1)S(1)}, u32[]{:S(2)}, u32[]{:S(2)}) collective-permute-start(bf16[592,128]{1,0:T(8,128)(2,1)S(1)} %get-tuple-element.211), channel_id=1, source_target_pairs={{0,24},{1,25},{2,26},{3,27},{4,28},{5,29},{6,30},{7,31},{8,16},{9,... | collective-permute-start | bytes 454664 | tf_op jit(solution)/shard_map/ppermute | solution.py:253
  187.5 6.4 %collective-permute-start.49 = (bf16[592,128]{1,0:T(8,128)(2,1)S(1)}, bf16[592,128]{1,0:T(8,128)(2,1)S(1)}, u32[]{:S(2)}, u32[]{:S(2)}) collective-permute-start(bf16[592,128]{1,0:T(8,128)(2,1)S(1)} %get-tuple-element.208.refs_0_), channel_id=1, source_target_pairs={{0,1},{1,0},{2,3},{3,2},{4,5},{5,4},{6,7},{7,6},{8,9},{9,8},{10,11... | collective-permute-start | bytes 454664 | tf_op jit(solution)/shard_map/ppermute | solution.py:253
  187.5 6.7 %collective-permute-start.59 = (bf16[256,384]{1,0:T(8,128)(2,1)S(1)}, bf16[256,384]{1,0:T(8,128)(2,1)S(1)}, u32[]{:S(2)}, u32[]{:S(2)}) collective-permute-start(bf16[256,384]{1,0:T(8,128)(2,1)S(1)} %collective-permute-done.57.refs_9_), channel_id=1, source_target_pairs={{0,1},{1,0},{2,3},{3,2},{4,5},{5,4},{6,7},{7,6},{8,9},{9,8},{10,11... | collective-permute-start | bytes 589832 | tf_op jit(solution)/shard_map/ppermute | solution.py:253
  191.2 3.1 %collective-permute-start.60 = (bf16[256,384]{1,0:T(8,128)(2,1)S(1)}, bf16[256,384]{1,0:T(8,128)(2,1)S(1)}, u32[]{:S(2)}, u32[]{:S(2)}) collective-permute-start(bf16[256,384]{1,0:T(8,128)(2,1)S(1)} %collective-permute-done.58.refs_10_), channel_id=1, source_target_pairs={{0,1},{1,0},{2,3},{3,2},{4,5},{5,4},{6,7},{7,6},{8,9},{9,8},{10,11... | collective-permute-start | bytes 589832 | tf_op jit(solution)/shard_map/ppermute | solution.py:253
  193.9 1.4 collective-permute-start.52
  (6 other events, 49.7 us)

commit v5 on v4

--- a/solution.py
+++ b/solution.py
@@ -436,6 +436,15 @@
     return pltpu.make_async_copy(sources[0].at[rows], target, sem)
 
 
+def take_layer(layer, sources, target):
+    section, _, _ = place()
+    for k, source in enumerate(sources):
+
+        @pl.when((section ^ layer) == k)
+        def _():
+            target[...] = source[...]
+
+
 def affine(meta, ch):
     parts = meta[:, :LANES].astype(jnp.float32).T[:ch]
     return (
@@ -526,7 +535,7 @@
 
 
 def pack_kernel(gain, bias, weight, *refs):
-    outs, (own, columns, turned, tables, sems) = refs[:4], refs[4:]
+    outs, (columns, turned, tables, sems) = refs[:4], refs[4:]
     section, _, core = place()
     width = columns.shape[2]
     ch = width // 4
@@ -543,20 +552,14 @@
             pltpu.make_async_copy(bias, tables.at[1], sems.at[TAPS + 1]),
         ]
     )
-    targets = [own, *outs[1:]]
-    own_copies = []
     for tap in range(TAPS):
         copies[tap].wait()
         turned[tap % 2] = columns[tap].T
-        for k, out in enumerate(targets):
+        for k, out in enumerate(outs):
             rows = pl.ds(pl.multiple_of((section ^ k) * ch, ch), ch)
             out[tap * ch : (tap + 1) * ch, :] = turned[tap % 2, rows, :]
-        piece = pl.ds(tap * ch, ch)
-        own_copies += start_all(
-            [pltpu.make_async_copy(own.at[piece], outs[0].at[piece], sems.at[TAPS + 2 + tap])]
-        )
     wait_all(table_copies)
-    for k, out in enumerate(targets):
+    for k, out in enumerate(outs):
         lines = []
         tile = pl.multiple_of(start + (section ^ k) // 2 * LANES, LANES)
         odd = (section ^ k) % 2 == 1
@@ -570,9 +573,6 @@
         lines.append(jnp.zeros((META_ROWS - len(lines), LANES), jnp.float32))
         out[TAPS * ch :, :] = jnp.zeros((META_ROWS, out.shape[1]), jnp.bfloat16)
         out[TAPS * ch :, :LANES] = jnp.concatenate(lines, axis=0).astype(jnp.bfloat16)
-    tail = pl.ds(TAPS * ch, META_ROWS)
-    own_copies += start_all([pltpu.make_async_copy(own.at[tail], outs[0].at[tail], sems.at[2 * TAPS + 2])])
-    wait_all(own_copies)
 
 
 def pick_kernel(layer, *refs):
@@ -591,7 +591,9 @@
     else:
         inside, facts, hidden, kept, full_out, full, taps, stage, sems = rest
         (weight,) = weights
-    if picks:
+    if first:
+        take_layer(layer, weights, weight)
+    elif picks:
         copy = pick_layer(layer, weights, 0, weight, sems.at[2])
     facts_now = facts[...]
     if first:
@@ -607,7 +609,7 @@
         inside_out[...] = inside_now
     else:
         inside_now = inside[...]
-    if picks:
+    if picks and not first:
         copy.wait()
     ch = hidden.shape[0]
     tap_products(weight[: TAPS * ch, :], full, taps, first)
@@ -926,7 +928,6 @@
         pack_kernel,
         [weight_slice] * 4,
         [
-            weight_slice,
             ((TAPS, channels, 4 * ch), bf16),
             ((2, 4 * ch, channels), bf16),
             ((2, 1, channels), f32),
@@ -934,8 +935,7 @@
         [bn_gain, bn_bias, taps_first],
         "weight_pack",
         held=range(3),
-        held_outs=(0,),
-        copies=2 * TAPS + 3,
+        copies=TAPS + 2,
     )
     slices = spread(packed, to_section)
 
@@ -968,9 +968,8 @@
         ],
         [*frames_in, *slices, facts],
         "forward",
-        held=range(8, 12),
         held_outs=(1, 2),
-        loose=(12,),
+        loose=(8, 9, 10, 11, 12),
         flops=conv_flops,
         copies=4,
     )

time: 198 us -> 196 us (0.990)
  transfers between devices with their start and end apart: 66 -> 66, of which waited for: 35 -> 35; matrix products, arithmetic and copies ran while one was open for 0% -> 0% of each run, Pallas kernels for 18% -> 19%
where the time goes in v5:
time: 196 us; the launch traced here: 195 us
  waiting for transfers between devices  73.6 us (38%)
  starting transfers between devices  70.1 us (36%)
  Pallas kernels  50.3 us (26%)
    pallas_call x26, Pallas kernels, call(): pl.pallas_call(kernel, out_shape=shapes, in_specs=[pl.BlockSpec(memory_sp...  50.3 us
    ppermute x61, waiting for transfers between devices, send(): return lax.ppermute(x, AXES, pairs)  50.1 us
    ppermute x61, starting transfers between devices, send(): return lax.ppermute(x, AXES, pairs)  48.4 us
    all_to_all x4, waiting for transfers between devices, plane_shards(): lax.all_to_all(share, 'dp', 0, 0, tiled=True, axis_index_groups=same_core)  23.5 us
    all_to_all x4, starting transfers between devices, plane_shards(): lax.all_to_all(share, 'dp', 0, 0, tiled=True, axis_index_groups=same_core)  16.9 us
    all_to_all x1, starting transfers between devices, plane_shards(): lax.all_to_all(cot_slots, 'dp', 0, 0, tiled=True, axis_index_groups=same_...  4.87 us
  transfers between devices with their start and end apart: 66, of which 35 were waited for; matrix products, arithmetic and copies ran while one was open for 0% of the time, Pallas kernels for 19%

profile of v5, /device:TPU:0, one launch (start us, length us, event | category | flops | bytes accessed | tf_op | source)
XLA Modules:
  0.0 195.4 jit_solution(12656327172304759529)
XLA Ops:
  0.6 2.5 %weight_pack.1 = (bf16[592,512]{1,0:T(8,128)(2,1)S(1)}, bf16[592,512]{1,0:T(8,128)(2,1)S(1)}, bf16[592,512]{1,0:T(8,128)(2,1)S(1)}, bf16[592,512]{1,0:T(8,128)(2,1)S(1)}) custom-call(f32[1,512]{1,0:T(1,128)} %gain.1, f32[1,512]{1,0:T(1,128)} %bias.1, bf16[9,512,512]{2,1,0:T(8,128)(2,1)} %bitcast.29), custom_call_target="tpu_custom_call" | custom-call | bytes 7147520 | tf_op jit(solution)/shard_map/weight_pack/pallas_call | solution.py:888
  3.1 3.0 %collective-permute-start.7 = (bf16[592,512]{1,0:T(8,128)(2,1)S(1)}, bf16[592,512]{1,0:T(8,128)(2,1)S(1)}, u32[]{:S(2)}, u32[]{:S(2)}) collective-permute-start(bf16[592,512]{1,0:T(8,128)(2,1)S(1)} %get-tuple-element.119), channel_id=1, source_target_pairs={{0,8},{1,9},{2,10},{3,11},{4,12},{5,13},{6,14},{7,15},{8,0},{9,1},... | collective-permute-start | bytes 1818632 | tf_op jit(solution)/shard_map/ppermute | solution.py:253
  6.2 1.5 collective-permute-start.8
  7.7 1.4 frames.1
  9.1 1.6 collective-permute-start
  11.2 2.6 %collective-permute-start.1 = (bf16[208,512]{1,0:T(8,128)(2,1)S(1)}, bf16[208,512]{1,0:T(8,128)(2,1)S(1)}, u32[]{:S(2)}, u32[]{:S(2)}) collective-permute-start(bf16[208,512]{1,0:T(8,128)(2,1)S(1)} %get-tuple-element.125), channel_id=1, source_target_pairs={{0,4},{1,5},{2,6},{3,7},{4,0},{5,1},{6,2},{7,3},{8,12},{9,13},{10,... | collective-permute-start | bytes 638984 | tf_op jit(solution)/shard_map/ppermute | solution.py:253
  13.8 6.1 %collective-permute-done.refs_1_ = bf16[208,512]{1,0:T(8,128)(2,1)S(1)} collective-permute-done((bf16[208,512]{1,0:T(8,128)(2,1)S(1)}, bf16[208,512]{1,0:T(8,128)(2,1)S(1)}, u32[]{:S(2)}, u32[]{:S(2)}) %collective-permute-start) | collective-permute-done | bytes 213024 | tf_op jit(solution)/shard_map/ppermute | solution.py:253
  19.8 2.5 %collective-permute-start.2 = (bf16[208,512]{1,0:T(8,128)(2,1)S(1)}, bf16[208,512]{1,0:T(8,128)(2,1)S(1)}, u32[]{:S(2)}, u32[]{:S(2)}) collective-permute-start(bf16[208,512]{1,0:T(8,128)(2,1)S(1)} %get-tuple-element.126), channel_id=1, source_target_pairs={{0,6},{1,7},{2,4},{3,5},{4,2},{5,3},{6,0},{7,1},{8,14},{9,15},{10,... | collective-permute-start | bytes 638984 | tf_op jit(solution)/shard_map/ppermute | solution.py:253
  22.3 2.8 %collective-permute-done.1.refs_2_ = bf16[208,512]{1,0:T(8,128)(2,1)S(1)} collective-permute-done((bf16[208,512]{1,0:T(8,128)(2,1)S(1)}, bf16[208,512]{1,0:T(8,128)(2,1)S(1)}, u32[]{:S(2)}, u32[]{:S(2)}) %collective-permute-start.1) | collective-permute-done | bytes 213024 | tf_op jit(solution)/shard_map/ppermute | solution.py:253
  25.1 2.5 %collective-permute-done.2.refs_3_ = bf16[208,512]{1,0:T(8,128)(2,1)S(1)} collective-permute-done((bf16[208,512]{1,0:T(8,128)(2,1)S(1)}, bf16[208,512]{1,0:T(8,128)(2,1)S(1)}, u32[]{:S(2)}, u32[]{:S(2)}) %collective-permute-start.2) | collective-permute-done | bytes 213024 | tf_op jit(solution)/shard_map/ppermute | solution.py:253
  28.1 6.2 %collective-permute-done.8.refs_10_.refs_2_ = bf16[592,512]{1,0:T(8,128)(2,1)S(1)} collective-permute-done((bf16[592,512]{1,0:T(8,128)(2,1)S(1)}, bf16[592,512]{1,0:T(8,128)(2,1)S(1)}, u32[]{:S(2)}, u32[]{:S(2)}) %collective-permute-start.8) | collective-permute-done | bytes 606240 | tf_op jit(solution)/shard_map/ppermute | solution.py:253
  34.4 1.4 collective-permute-done.6.refs_7_
  35.8 2.5 %forward.3 = (bf16[64,1536]{1,0:T(8,128)(2,1)S(1)}, f32[64,1664]{1,0:T(8,128)}, bf16[1536,512]{1,0:T(8,128)(2,1)}, f32[1,1536]{1,0:T(1,128)S(1)}) custom-call(bf16[208,512]{1,0:T(8,128)(2,1)S(1)} %get-tuple-element.123.refs_0_, bf16[208,512]{1,0:T(8,128)(2,1)S(1)} %collective-permute-done.refs_1_, bf16[208,512]{1,0:T(8,128)(2,1)S(1)} %collective-permute-done.1.refs_2_, ...), custom_call_target="tpu_custom_call" | custom-call | flops 905969664 | bytes 6428672 | tf_op jit(solution)/shard_map/forward/pallas_call | solution.py:888
  38.4 1.5 collective-permute-start.12
  39.9 1.5 collective-permute-start.10
  41.9 2.0 %cot_slices.1 = bf16[768,128]{1,0:T(8,128)(2,1)} custom-call(bf16[4,192,512]{2,1,0:T(8,128)(2,1)} %bitcast.31), custom_call_target="tpu_custom_call" | custom-call | bytes 983040 | tf_op jit(solution)/shard_map/cot_slices/pallas_call | solution.py:888
  43.9 3.8 %turn_weights.1 = (bf16[1024,640]{1,0:T(8,128)(2,1)}, bf16[1024,640]{1,0:T(8,128)(2,1)}) custom-call(bf16[592,512]{1,0:T(8,128)(2,1)} %copy-done, bf16[592,512]{1,0:T(8,128)(2,1)} %copy-done.1, bf16[592,512]{1,0:T(8,128)(2,1)} %copy-done.2, bf16[592,512]{1,0:T(8,128)(2,1)} %copy-done.3), custom_call_target="tpu_custom_call" | custom-call | bytes 5046272 | tf_op jit(solution)/shard_map/turn_weights/pallas_call | solution.py:888
  47.7 1.1 pick.2.refs_8_
  49.4 1.2 collective-permute-done.10.refs_1_
  52.3 3.1 %forward.4 = (bf16[64,1536]{1,0:T(8,128)(2,1)S(1)}, f32[64,1664]{1,0:T(8,128)}, bf16[512,1536]{1,0:T(8,128)(2,1)}) custom-call(bf16[64,1536]{1,0:T(8,128)(2,1)S(1)} %get-tuple-element.133.refs_0_, bf16[64,1536]{1,0:T(8,128)(2,1)S(1)} %collective-permute-done.10.refs_1_, bf16[64,1536]{1,0:T(8,128)(2,1)S(1)} %collective-permute-done.11.refs_2_, ...), custom_call_target="tpu_custom_call" | custom-call | flops 905969664 | bytes 4478976 | tf_op jit(solution)/shard_map/forward/pallas_call | solution.py:888
  55.4 1.2 collective-permute-start.19
  56.5 1.5 collective-permute-start.17
  59.4 4.9 %all-to-all-start = ((bf16[4,192,128]{2,1,0:T(8,128)(2,1)}), bf16[4,192,128]{2,1,0:T(8,128)(2,1)S(1)}, u32[]{:S(2)}, u32[]{:S(2)}) async-start(bf16[4,192,128]{2,1,0:T(8,128)(2,1)} %bitcast.7), calls=%async_computation | async-start | bytes 393216 | tf_op jit(solution)/shard_map/all_to_all | solution.py:1020
  64.3 2.9 %collective-permute-done.17.refs_1_ = bf16[64,1536]{1,0:T(8,128)(2,1)S(1)} collective-permute-done((bf16[64,1536]{1,0:T(8,128)(2,1)S(1)}, bf16[64,1536]{1,0:T(8,128)(2,1)S(1)}, u32[]{:S(2)}, u32[]{:S(2)}) %collective-permute-start.17) | collective-permute-done | bytes 196640 | tf_op jit(solution)/shard_map/ppermute | solution.py:253
  69.0 3.6 %forward.5 = (bf16[64,1536]{1,0:T(8,128)(2,1)S(1)}, f32[64,1664]{1,0:T(8,128)}, bf16[512,1536]{1,0:T(8,128)(2,1)}) custom-call(bf16[64,1536]{1,0:T(8,128)(2,1)S(1)} %get-tuple-element.143.refs_0_, bf16[64,1536]{1,0:T(8,128)(2,1)S(1)} %collective-permute-done.17.refs_1_, bf16[64,1536]{1,0:T(8,128)(2,1)S(1)} %collective-permute-done.18.refs_2_, ...), custom_call_target="tpu_custom_call" | custom-call | flops 905969664 | bytes 6297600 | tf_op jit(solution)/shard_map/forward/pallas_call | solution.py:888
  72.6 1.1 collective-permute-start.26
  73.7 1.5 collective-permute-start.24
  76.2 1.1 pick.3.refs_8_
  78.2 3.2 %collective-permute-done.26.refs_3_ = bf16[64,1536]{1,0:T(8,128)(2,1)S(1)} collective-permute-done((bf16[64,1536]{1,0:T(8,128)(2,1)S(1)}, bf16[64,1536]{1,0:T(8,128)(2,1)S(1)}, u32[]{:S(2)}, u32[]{:S(2)}) %collective-permute-start.26) | collective-permute-done | bytes 196640 | tf_op jit(solution)/shard_map/ppermute | solution.py:253
  81.4 3.0 %collective-permute-done.24.refs_1_ = bf16[64,1536]{1,0:T(8,128)(2,1)S(1)} collective-permute-done((bf16[64,1536]{1,0:T(8,128)(2,1)S(1)}, bf16[64,1536]{1,0:T(8,128)(2,1)S(1)}, u32[]{:S(2)}, u32[]{:S(2)}) %collective-permute-start.24) | collective-permute-done | bytes 196640 | tf_op jit(solution)/shard_map/ppermute | solution.py:253
  86.2 2.7 %turn.1 = (bf16[64,1536]{1,0:T(8,128)(2,1)}, bf16[512,1536]{1,0:T(8,128)(2,1)}, bf16[64,1536]{1,0:T(8,128)(2,1)S(1)}, f32[64,256]{1,0:T(8,128)S(1)}) custom-call(bf16[64,1536]{1,0:T(8,128)(2,1)S(1)} %get-tuple-element.144.refs_0_, bf16[64,1536]{1,0:T(8,128)(2,1)S(1)} %collective-permute-done.24.refs_1_, ...), custom_call_target="tpu_custom_call" | custom-call | flops 905969664 | bytes 4511744 | tf_op jit(solution)/shard_map/turn/pallas_call | solution.py:888
  89.2 1.3 collective-permute-done.32.other
  90.5 3.9 %conv_back.4 = (bf16[64,1536]{1,0:T(8,128)(2,1)S(1)}, bf16[64,1536]{1,0:T(8,128)(2,1)S(1)}, bf16[64,1536]{1,0:T(8,128)(2,1)S(1)}, bf16[64,1536]{1,0:T(8,128)(2,1)S(1)}, bf16[2368,128]{1,0:T(8,128)(2,1)}) custom-call(bf16[64,1536]{1,0:T(8,128)(2,1)S(1)} %get-tuple-element.152.own, bf16[64,1536]{1,0:T(8,128)(2,1)S(1)} %collective-permute-done.32.other, ...), custom_call_target="tpu_custom_call" | custom-call | bytes 6144000 | tf_op jit(solution)/shard_map/conv_back/pallas_call | solution.py:888
  94.9 1.1 collective-permute-start.35
  96.0 1.9 collective-permute-start.36
  97.9 4.9 %all-to-all-start.1 = ((bf16[4,592,128]{2,1,0:T(8,128)(2,1)}), bf16[4,592,128]{2,1,0:T(8,128)(2,1)}, u32[]{:S(2)}, u32[]{:S(2)}) async-start(bf16[4,592,128]{2,1,0:T(8,128)(2,1)} %bitcast.35), calls=%async_computation.1 | async-start | bytes 1212416 | tf_op jit(solution)/shard_map/all_to_all | solution.py:1087
  103.8 2.2 %collective-permute-done.36.refs_3_ = bf16[64,1536]{1,0:T(8,128)(2,1)S(1)} collective-permute-done((bf16[64,1536]{1,0:T(8,128)(2,1)S(1)}, bf16[64,1536]{1,0:T(8,128)(2,1)S(1)}, u32[]{:S(2)}, u32[]{:S(2)}) %collective-permute-start.36) | collective-permute-done | bytes 196640 | tf_op jit(solution)/shard_map/ppermute | solution.py:253
  106.6 1.4 collective-permute-done.37.other
  108.1 3.9 %conv_back.5 = (bf16[64,1536]{1,0:T(8,128)(2,1)S(1)}, bf16[64,1536]{1,0:T(8,128)(2,1)S(1)}, bf16[64,1536]{1,0:T(8,128)(2,1)S(1)}, bf16[64,1536]{1,0:T(8,128)(2,1)S(1)}, bf16[2368,128]{1,0:T(8,128)(2,1)}) custom-call(bf16[64,1536]{1,0:T(8,128)(2,1)S(1)} %get-tuple-element.167.own, bf16[64,1536]{1,0:T(8,128)(2,1)S(1)} %collective-permute-done.37.other, ...), custom_call_target="tpu_custom_call" | custom-call | flops 6000000000 | bytes 6144000 | tf_op jit(solution)/shard_map/conv_back/pallas_call | solution.py:888
  111.9 1.4 collective-permute-start.38
  114.3 1.2 collective-permute-start.40
  115.5 3.1 %all-to-all-done.1 = bf16[4,592,128]{2,1,0:T(8,128)(2,1)} async-done(((bf16[4,592,128]{2,1,0:T(8,128)(2,1)}), bf16[4,592,128]{2,1,0:T(8,128)(2,1)}, u32[]{:S(2)}, u32[]{:S(2)}) %all-to-all-start.1) | async-done | bytes 606240 | tf_op jit(solution)/shard_map/all_to_all | solution.py:1087
  118.6 4.4 %all-to-all-start.2 = ((bf16[4,592,128]{2,1,0:T(8,128)(2,1)}), bf16[4,592,128]{2,1,0:T(8,128)(2,1)}, u32[]{:S(2)}, u32[]{:S(2)}) async-start(bf16[4,592,128]{2,1,0:T(8,128)(2,1)} %bitcast.33), calls=%async_computation.2 | async-start | bytes 1212416 | tf_op jit(solution)/shard_map/all_to_all | solution.py:1087
  124.2 2.0 %norm_back.4 = (bf16[64,1536]{1,0:T(8,128)(2,1)S(1)}, f32[64,256]{1,0:T(8,128)S(1)}) custom-call(bf16[64,1536]{1,0:T(8,128)(2,1)S(1)} %get-tuple-element.170.refs_0_, bf16[64,1536]{1,0:T(8,128)(2,1)S(1)} %collective-permute-done.38.refs_1_, bf16[64,1536]{1,0:T(8,128)(2,1)S(1)} %collective-permute-done.39.refs_2_, ...), custom_call_target="tpu_custom_call" | custom-call | bytes 1595392 | tf_op jit(solution)/shard_map/norm_back/pallas_call | solution.py:888
  126.3 1.4 collective-permute-done.41.other
  127.7 3.9 %conv_back.6 = (bf16[64,1536]{1,0:T(8,128)(2,1)S(1)}, bf16[64,1536]{1,0:T(8,128)(2,1)S(1)}, bf16[64,1536]{1,0:T(8,128)(2,1)S(1)}, bf16[64,1536]{1,0:T(8,128)(2,1)S(1)}, bf16[2368,128]{1,0:T(8,128)(2,1)}) custom-call(bf16[64,1536]{1,0:T(8,128)(2,1)S(1)} %get-tuple-element.181.own, bf16[64,1536]{1,0:T(8,128)(2,1)S(1)} %collective-permute-done.41.other, ...), custom_call_target="tpu_custom_call" | custom-call | flops 6000000000 | bytes 6144000 | tf_op jit(solution)/shard_map/conv_back/pallas_call | solution.py:888
  133.4 1.8 collective-permute-start.44
  135.2 3.4 %all-to-all-done.2 = bf16[4,592,128]{2,1,0:T(8,128)(2,1)} async-done(((bf16[4,592,128]{2,1,0:T(8,128)(2,1)}), bf16[4,592,128]{2,1,0:T(8,128)(2,1)}, u32[]{:S(2)}, u32[]{:S(2)}) %all-to-all-start.2) | async-done | bytes 606240 | tf_op jit(solution)/shard_map/all_to_all | solution.py:1087
  138.5 4.2 %all-to-all-start.3 = ((bf16[4,592,128]{2,1,0:T(8,128)(2,1)}), bf16[4,592,128]{2,1,0:T(8,128)(2,1)}, u32[]{:S(2)}, u32[]{:S(2)}) async-start(bf16[4,592,128]{2,1,0:T(8,128)(2,1)} %bitcast.32), calls=%async_computation.3 | async-start | bytes 1212416 | tf_op jit(solution)/shard_map/all_to_all | solution.py:1087
  144.4 1.4 collective-permute-done.45.other
  145.8 3.8 %conv_back.7 = (bf16[64,1536]{1,0:T(8,128)(2,1)S(1)}, bf16[64,1536]{1,0:T(8,128)(2,1)S(1)}, bf16[64,1536]{1,0:T(8,128)(2,1)S(1)}, bf16[64,1536]{1,0:T(8,128)(2,1)S(1)}, bf16[2368,128]{1,0:T(8,128)(2,1)}) custom-call(bf16[64,1536]{1,0:T(8,128)(2,1)S(1)} %get-tuple-element.195.own, bf16[64,1536]{1,0:T(8,128)(2,1)S(1)} %collective-permute-done.45.other, ...), custom_call_target="tpu_custom_call" | custom-call | flops 6000000000 | bytes 6144000 | tf_op jit(solution)/shard_map/conv_back/pallas_call | solution.py:888
  150.5 1.0 collective-permute-start.54
  151.6 1.6 collective-permute-start.55
  153.2 5.3 %all-to-all-done.3 = bf16[4,592,128]{2,1,0:T(8,128)(2,1)} async-done(((bf16[4,592,128]{2,1,0:T(8,128)(2,1)}), bf16[4,592,128]{2,1,0:T(8,128)(2,1)}, u32[]{:S(2)}, u32[]{:S(2)}) %all-to-all-start.3) | async-done | bytes 606240 | tf_op jit(solution)/shard_map/all_to_all | solution.py:1087
  158.5 3.5 %all-to-all-start.4 = ((bf16[4,592,128]{2,1,0:T(8,128)(2,1)}), bf16[4,592,128]{2,1,0:T(8,128)(2,1)S(1)}, u32[]{:S(2)}, u32[]{:S(2)}) async-start(bf16[4,592,128]{2,1,0:T(8,128)(2,1)} %bitcast.34), calls=%async_computation.4 | async-start | bytes 1212416 | tf_op jit(solution)/shard_map/all_to_all | solution.py:1087
  163.1 1.4 collective-permute-done.56.got
  165.2 3.4 %collective-permute-start.58 = (bf16[256,384]{1,0:T(8,128)(2,1)S(1)}, bf16[256,384]{1,0:T(8,128)(2,1)S(1)}, u32[]{:S(2)}, u32[]{:S(2)}) collective-permute-start(bf16[256,384]{1,0:T(8,128)(2,1)S(1)} %get-tuple-element.223), channel_id=1, source_target_pairs={{0,2},{1,7},{2,10},{3,15},{4,18},{5,23},{6,26},{7,31},{8,0},{9,5},... | collective-permute-start | bytes 589832 | tf_op jit(solution)/shard_map/ppermute | solution.py:253
  168.6 1.5 fold.1
  170.1 11.8 %all-to-all-done.4 = bf16[4,592,128]{2,1,0:T(8,128)(2,1)S(1)} async-done(((bf16[4,592,128]{2,1,0:T(8,128)(2,1)}), bf16[4,592,128]{2,1,0:T(8,128)(2,1)S(1)}, u32[]{:S(2)}, u32[]{:S(2)}) %all-to-all-start.4) | async-done | bytes 606240 | tf_op jit(solution)/shard_map/all_to_all | solution.py:1087
  182.1 1.5 collective-permute-start.46
  183.7 1.1 collective-permute-start.47
  186.3 3.1 %collective-permute-done.46.refs_1_ = bf16[592,128]{1,0:T(8,128)(2,1)S(1)} collective-permute-done((bf16[592,128]{1,0:T(8,128)(2,1)S(1)}, bf16[592,128]{1,0:T(8,128)(2,1)S(1)}, u32[]{:S(2)}, u32[]{:S(2)}) %collective-permute-start.46) | collective-permute-done | bytes 151584 | tf_op jit(solution)/shard_map/ppermute | solution.py:253
  189.4 2.2 %collective-permute-done.47.refs_2_ = bf16[592,128]{1,0:T(8,128)(2,1)S(1)} collective-permute-done((bf16[592,128]{1,0:T(8,128)(2,1)S(1)}, bf16[592,128]{1,0:T(8,128)(2,1)S(1)}, u32[]{:S(2)}, u32[]{:S(2)}) %collective-permute-start.47) | collective-permute-done | bytes 151584 | tf_op jit(solution)/shard_map/ppermute | solution.py:253
  193.5 1.9 outputs.1
  (108 shorter events, 25.0 us)
Async XLA Ops:
  3.1 24.4 %collective-permute-start.7 = (bf16[592,512]{1,0:T(8,128)(2,1)S(1)}, bf16[592,512]{1,0:T(8,128)(2,1)S(1)}, u32[]{:S(2)}, u32[]{:S(2)}) collective-permute-start(bf16[592,512]{1,0:T(8,128)(2,1)S(1)} %get-tuple-element.119), channel_id=1, source_target_pairs={{0,8},{1,9},{2,10},{3,11},{4,12},{5,13},{6,14},{7,15},{8,0},{9,1},... | collective-permute-start | bytes 1818632 | tf_op jit(solution)/shard_map/ppermute | solution.py:253
  6.2 28.1 %collective-permute-start.8 = (bf16[592,512]{1,0:T(8,128)(2,1)S(1)}, bf16[592,512]{1,0:T(8,128)(2,1)S(1)}, u32[]{:S(2)}, u32[]{:S(2)}) collective-permute-start(bf16[592,512]{1,0:T(8,128)(2,1)S(1)} %get-tuple-element.120), channel_id=1, source_target_pairs={{0,16},{1,17},{2,18},{3,19},{4,20},{5,21},{6,22},{7,23},{8,24},{9,... | collective-permute-start | bytes 1818632 | tf_op jit(solution)/shard_map/ppermute | solution.py:253
  9.1 10.8 %collective-permute-start = (bf16[208,512]{1,0:T(8,128)(2,1)S(1)}, bf16[208,512]{1,0:T(8,128)(2,1)S(1)}, u32[]{:S(2)}, u32[]{:S(2)}) collective-permute-start(bf16[208,512]{1,0:T(8,128)(2,1)S(1)} %get-tuple-element.124), channel_id=1, source_target_pairs={{0,2},{1,3},{2,0},{3,1},{4,6},{5,7},{6,4},{7,5},{8,10},{9,11},{10,... | collective-permute-start | bytes 638984 | tf_op jit(solution)/shard_map/ppermute | solution.py:253
  10.7 23.6 %collective-permute-start.9 = (bf16[592,512]{1,0:T(8,128)(2,1)S(1)}, bf16[592,512]{1,0:T(8,128)(2,1)S(1)}, u32[]{:S(2)}, u32[]{:S(2)}) collective-permute-start(bf16[592,512]{1,0:T(8,128)(2,1)S(1)} %get-tuple-element.121), channel_id=1, source_target_pairs={{0,24},{1,25},{2,26},{3,27},{4,28},{5,29},{6,30},{7,31},{8,16},{9,... | collective-permute-start | bytes 1818632 | tf_op jit(solution)/shard_map/ppermute | solution.py:253
  11.2 13.9 %collective-permute-start.1 = (bf16[208,512]{1,0:T(8,128)(2,1)S(1)}, bf16[208,512]{1,0:T(8,128)(2,1)S(1)}, u32[]{:S(2)}, u32[]{:S(2)}) collective-permute-start(bf16[208,512]{1,0:T(8,128)(2,1)S(1)} %get-tuple-element.125), channel_id=1, source_target_pairs={{0,4},{1,5},{2,6},{3,7},{4,0},{5,1},{6,2},{7,3},{8,12},{9,13},{10,... | collective-permute-start | bytes 638984 | tf_op jit(solution)/shard_map/ppermute | solution.py:253
  19.8 7.8 %collective-permute-start.2 = (bf16[208,512]{1,0:T(8,128)(2,1)S(1)}, bf16[208,512]{1,0:T(8,128)(2,1)S(1)}, u32[]{:S(2)}, u32[]{:S(2)}) collective-permute-start(bf16[208,512]{1,0:T(8,128)(2,1)S(1)} %get-tuple-element.126), channel_id=1, source_target_pairs={{0,6},{1,7},{2,4},{3,5},{4,2},{5,3},{6,0},{7,1},{8,14},{9,15},{10,... | collective-permute-start | bytes 638984 | tf_op jit(solution)/shard_map/ppermute | solution.py:253
  25.1 9.2 %collective-permute-start.3 = (bf16[208,512]{1,0:T(8,128)(2,1)S(1)}, bf16[208,512]{1,0:T(8,128)(2,1)S(1)}, u32[]{:S(2)}, u32[]{:S(2)}) collective-permute-start(bf16[208,512]{1,0:T(8,128)(2,1)S(1)} %get-tuple-element.123.refs_0_), channel_id=1, source_target_pairs={{0,1},{1,0},{2,3},{3,2},{4,5},{5,4},{6,7},{7,6},{8,9},{9,8},{10,11... | collective-permute-start | bytes 638984 | tf_op jit(solution)/shard_map/ppermute | solution.py:253
  27.6 6.8 %collective-permute-start.4 = (bf16[208,512]{1,0:T(8,128)(2,1)S(1)}, bf16[208,512]{1,0:T(8,128)(2,1)S(1)}, u32[]{:S(2)}, u32[]{:S(2)}) collective-permute-start(bf16[208,512]{1,0:T(8,128)(2,1)S(1)} %collective-permute-done.refs_1_), channel_id=1, source_target_pairs={{0,1},{1,0},{2,3},{3,2},{4,5},{5,4},{6,7},{7,6},{8,9},{9,8},{10,11... | collective-permute-start | bytes 638984 | tf_op jit(solution)/shard_map/ppermute | solution.py:253
  27.6 6.8 %collective-permute-start.5 = (bf16[208,512]{1,0:T(8,128)(2,1)S(1)}, bf16[208,512]{1,0:T(8,128)(2,1)S(1)}, u32[]{:S(2)}, u32[]{:S(2)}) collective-permute-start(bf16[208,512]{1,0:T(8,128)(2,1)S(1)} %collective-permute-done.1.refs_2_), channel_id=1, source_target_pairs={{0,1},{1,0},{2,3},{3,2},{4,5},{5,4},{6,7},{7,6},{8,9},{9,8},{10,11... | collective-permute-start | bytes 638984 | tf_op jit(solution)/shard_map/ppermute | solution.py:253
  34.3 1.5 collective-permute-start.6
  38.4 10.4 %collective-permute-start.12 = (bf16[64,1536]{1,0:T(8,128)(2,1)S(1)}, bf16[64,1536]{1,0:T(8,128)(2,1)S(1)}, u32[]{:S(2)}, u32[]{:S(2)}) collective-permute-start(bf16[64,1536]{1,0:T(8,128)(2,1)S(1)} %get-tuple-element.133.refs_0_), channel_id=1, source_target_pairs={{0,24},{1,25},{2,26},{3,27},{4,28},{5,29},{6,30},{7,31},{8,16},{9,... | collective-permute-start | bytes 589832 | tf_op jit(solution)/shard_map/ppermute | solution.py:253
  39.9 10.7 %collective-permute-start.10 = (bf16[64,1536]{1,0:T(8,128)(2,1)S(1)}, bf16[64,1536]{1,0:T(8,128)(2,1)S(1)}, u32[]{:S(2)}, u32[]{:S(2)}) collective-permute-start(bf16[64,1536]{1,0:T(8,128)(2,1)S(1)} %get-tuple-element.133.refs_0_), channel_id=1, source_target_pairs={{0,8},{1,9},{2,10},{3,11},{4,12},{5,13},{6,14},{7,15},{8,0},{9,1},... | collective-permute-start | bytes 589832 | tf_op jit(solution)/shard_map/ppermute | solution.py:253
  41.4 9.2 %collective-permute-start.11 = (bf16[64,1536]{1,0:T(8,128)(2,1)S(1)}, bf16[64,1536]{1,0:T(8,128)(2,1)S(1)}, u32[]{:S(2)}, u32[]{:S(2)}) collective-permute-start(bf16[64,1536]{1,0:T(8,128)(2,1)S(1)} %get-tuple-element.133.refs_0_), channel_id=1, source_target_pairs={{0,16},{1,17},{2,18},{3,19},{4,20},{5,21},{6,22},{7,23},{8,24},{9,... | collective-permute-start | bytes 589832 | tf_op jit(solution)/shard_map/ppermute | solution.py:253
  41.9 9.2 %collective-permute-start.13 = (bf16[64,1536]{1,0:T(8,128)(2,1)S(1)}, bf16[64,1536]{1,0:T(8,128)(2,1)S(1)}, u32[]{:S(2)}, u32[]{:S(2)}) collective-permute-start(bf16[64,1536]{1,0:T(8,128)(2,1)S(1)} %get-tuple-element.133.refs_0_), channel_id=1, source_target_pairs={{0,1},{1,0},{2,3},{3,2},{4,5},{5,4},{6,7},{7,6},{8,9},{9,8},{10,11... | collective-permute-start | bytes 589832 | tf_op jit(solution)/shard_map/ppermute | solution.py:253
  48.8 2.3 %collective-permute-start.16 = (bf16[64,1536]{1,0:T(8,128)(2,1)S(1)}, bf16[64,1536]{1,0:T(8,128)(2,1)S(1)}, u32[]{:S(2)}, u32[]{:S(2)}) collective-permute-start(bf16[64,1536]{1,0:T(8,128)(2,1)S(1)} %collective-permute-done.12.refs_3_), channel_id=1, source_target_pairs={{0,1},{1,0},{2,3},{3,2},{4,5},{5,4},{6,7},{7,6},{8,9},{9,8},{10,11... | collective-permute-start | bytes 589832 | tf_op jit(solution)/shard_map/ppermute | solution.py:253
  50.6 1.4 collective-permute-start.14
  50.6 1.7 collective-permute-start.15
  55.4 8.9 %collective-permute-start.19 = (bf16[64,1536]{1,0:T(8,128)(2,1)S(1)}, bf16[64,1536]{1,0:T(8,128)(2,1)S(1)}, u32[]{:S(2)}, u32[]{:S(2)}) collective-permute-start(bf16[64,1536]{1,0:T(8,128)(2,1)S(1)} %get-tuple-element.143.refs_0_), channel_id=1, source_target_pairs={{0,24},{1,25},{2,26},{3,27},{4,28},{5,29},{6,30},{7,31},{8,16},{9,... | collective-permute-start | bytes 589832 | tf_op jit(solution)/shard_map/ppermute | solution.py:253
  56.5 10.7 %collective-permute-start.17 = (bf16[64,1536]{1,0:T(8,128)(2,1)S(1)}, bf16[64,1536]{1,0:T(8,128)(2,1)S(1)}, u32[]{:S(2)}, u32[]{:S(2)}) collective-permute-start(bf16[64,1536]{1,0:T(8,128)(2,1)S(1)} %get-tuple-element.143.refs_0_), channel_id=1, source_target_pairs={{0,8},{1,9},{2,10},{3,11},{4,12},{5,13},{6,14},{7,15},{8,0},{9,1},... | collective-permute-start | bytes 589832 | tf_op jit(solution)/shard_map/ppermute | solution.py:253
  58.0 9.6 %collective-permute-start.18 = (bf16[64,1536]{1,0:T(8,128)(2,1)S(1)}, bf16[64,1536]{1,0:T(8,128)(2,1)S(1)}, u32[]{:S(2)}, u32[]{:S(2)}) collective-permute-start(bf16[64,1536]{1,0:T(8,128)(2,1)S(1)} %get-tuple-element.143.refs_0_), channel_id=1, source_target_pairs={{0,16},{1,17},{2,18},{3,19},{4,20},{5,21},{6,22},{7,23},{8,24},{9,... | collective-permute-start | bytes 589832 | tf_op jit(solution)/shard_map/ppermute | solution.py:253
  58.9 31.5 %collective-permute-start.33 = (bf16[1024,640]{1,0:T(8,128)(2,1)}, bf16[1024,640]{1,0:T(8,128)(2,1)S(1)}, u32[]{:S(2)}, u32[]{:S(2)}) collective-permute-start(bf16[1024,640]{1,0:T(8,128)(2,1)} %get-tuple-element.153), channel_id=1, source_target_pairs={{0,1},{1,0},{2,3},{3,2},{4,5},{5,4},{6,7},{7,6},{8,9},{9,8},{10,11... | collective-permute-start | bytes 3932168 | tf_op jit(solution)/shard_map/ppermute | solution.py:253
  58.9 8.9 %collective-permute-start.20 = (bf16[64,1536]{1,0:T(8,128)(2,1)S(1)}, bf16[64,1536]{1,0:T(8,128)(2,1)S(1)}, u32[]{:S(2)}, u32[]{:S(2)}) collective-permute-start(bf16[64,1536]{1,0:T(8,128)(2,1)S(1)} %get-tuple-element.143.refs_0_), channel_id=1, source_target_pairs={{0,1},{1,0},{2,3},{3,2},{4,5},{5,4},{6,7},{7,6},{8,9},{9,8},{10,11... | collective-permute-start | bytes 589832 | tf_op jit(solution)/shard_map/ppermute | solution.py:253
  59.4 16.8 %all-to-all-start = ((bf16[4,192,128]{2,1,0:T(8,128)(2,1)}), bf16[4,192,128]{2,1,0:T(8,128)(2,1)S(1)}, u32[]{:S(2)}, u32[]{:S(2)}) async-start(bf16[4,192,128]{2,1,0:T(8,128)(2,1)} %bitcast.7), calls=%async_computation | async-start | bytes 393216 | tf_op jit(solution)/shard_map/all_to_all | solution.py:1020
  64.3 4.7 %collective-permute-start.23 = (bf16[64,1536]{1,0:T(8,128)(2,1)S(1)}, bf16[64,1536]{1,0:T(8,128)(2,1)S(1)}, u32[]{:S(2)}, u32[]{:S(2)}) collective-permute-start(bf16[64,1536]{1,0:T(8,128)(2,1)S(1)} %collective-permute-done.19.refs_3_), channel_id=1, source_target_pairs={{0,1},{1,0},{2,3},{3,2},{4,5},{5,4},{6,7},{7,6},{8,9},{9,8},{10,11... | collective-permute-start | bytes 589832 | tf_op jit(solution)/shard_map/ppermute | solution.py:253
  67.2 1.4 collective-permute-start.21
  67.6 1.4 collective-permute-start.22
  72.6 8.8 %collective-permute-start.26 = (bf16[64,1536]{1,0:T(8,128)(2,1)S(1)}, bf16[64,1536]{1,0:T(8,128)(2,1)S(1)}, u32[]{:S(2)}, u32[]{:S(2)}) collective-permute-start(bf16[64,1536]{1,0:T(8,128)(2,1)S(1)} %get-tuple-element.144.refs_0_), channel_id=1, source_target_pairs={{0,24},{1,25},{2,26},{3,27},{4,28},{5,29},{6,30},{7,31},{8,16},{9,... | collective-permute-start | bytes 589832 | tf_op jit(solution)/shard_map/ppermute | solution.py:253
  73.7 10.7 %collective-permute-start.24 = (bf16[64,1536]{1,0:T(8,128)(2,1)S(1)}, bf16[64,1536]{1,0:T(8,128)(2,1)S(1)}, u32[]{:S(2)}, u32[]{:S(2)}) collective-permute-start(bf16[64,1536]{1,0:T(8,128)(2,1)S(1)} %get-tuple-element.144.refs_0_), channel_id=1, source_target_pairs={{0,8},{1,9},{2,10},{3,11},{4,12},{5,13},{6,14},{7,15},{8,0},{9,1},... | collective-permute-start | bytes 589832 | tf_op jit(solution)/shard_map/ppermute | solution.py:253
  75.2 9.6 %collective-permute-start.25 = (bf16[64,1536]{1,0:T(8,128)(2,1)S(1)}, bf16[64,1536]{1,0:T(8,128)(2,1)S(1)}, u32[]{:S(2)}, u32[]{:S(2)}) collective-permute-start(bf16[64,1536]{1,0:T(8,128)(2,1)S(1)} %get-tuple-element.144.refs_0_), channel_id=1, source_target_pairs={{0,16},{1,17},{2,18},{3,19},{4,20},{5,21},{6,22},{7,23},{8,24},{9,... | collective-permute-start | bytes 589832 | tf_op jit(solution)/shard_map/ppermute | solution.py:253
  76.2 1.4 collective-permute-start.27
  77.6 7.3 %collective-permute-start.28 = (bf16[64,1536]{1,0:T(8,128)(2,1)S(1)}, bf16[64,1536]{1,0:T(8,128)(2,1)S(1)}, u32[]{:S(2)}, u32[]{:S(2)}) collective-permute-start(bf16[64,1536]{1,0:T(8,128)(2,1)S(1)} %get-tuple-element.144.refs_0_), channel_id=1, source_target_pairs={{0,1},{1,0},{2,3},{3,2},{4,5},{5,4},{6,7},{7,6},{8,9},{9,8},{10,11... | collective-permute-start | bytes 589832 | tf_op jit(solution)/shard_map/ppermute | solution.py:253
  81.4 3.5 %collective-permute-start.31 = (bf16[64,1536]{1,0:T(8,128)(2,1)S(1)}, bf16[64,1536]{1,0:T(8,128)(2,1)S(1)}, u32[]{:S(2)}, u32[]{:S(2)}) collective-permute-start(bf16[64,1536]{1,0:T(8,128)(2,1)S(1)} %collective-permute-done.26.refs_3_), channel_id=1, source_target_pairs={{0,1},{1,0},{2,3},{3,2},{4,5},{5,4},{6,7},{7,6},{8,9},{9,8},{10,11... | collective-permute-start | bytes 589832 | tf_op jit(solution)/shard_map/ppermute | solution.py:253
  84.4 1.4 collective-permute-start.29
  84.8 1.4 collective-permute-start.30
  88.9 1.5 collective-permute-start.32
  94.3 9.5 %collective-permute-start.34 = (bf16[64,1536]{1,0:T(8,128)(2,1)S(1)}, bf16[64,1536]{1,0:T(8,128)(2,1)S(1)}, u32[]{:S(2)}, u32[]{:S(2)}) collective-permute-start(bf16[64,1536]{1,0:T(8,128)(2,1)S(1)} %get-tuple-element.157), channel_id=1, source_target_pairs={{0,8},{1,9},{2,10},{3,11},{4,12},{5,13},{6,14},{7,15},{8,0},{9,1},... | collective-permute-start | bytes 589832 | tf_op jit(solution)/shard_map/ppermute | solution.py:253
  94.9 8.9 %collective-permute-start.35 = (bf16[64,1536]{1,0:T(8,128)(2,1)S(1)}, bf16[64,1536]{1,0:T(8,128)(2,1)S(1)}, u32[]{:S(2)}, u32[]{:S(2)}) collective-permute-start(bf16[64,1536]{1,0:T(8,128)(2,1)S(1)} %get-tuple-element.158), channel_id=1, source_target_pairs={{0,16},{1,17},{2,18},{3,19},{4,20},{5,21},{6,22},{7,23},{8,24},{9,... | collective-permute-start | bytes 589832 | tf_op jit(solution)/shard_map/ppermute | solution.py:253
  96.0 10.1 %collective-permute-start.36 = (bf16[64,1536]{1,0:T(8,128)(2,1)S(1)}, bf16[64,1536]{1,0:T(8,128)(2,1)S(1)}, u32[]{:S(2)}, u32[]{:S(2)}) collective-permute-start(bf16[64,1536]{1,0:T(8,128)(2,1)S(1)} %get-tuple-element.159), channel_id=1, source_target_pairs={{0,24},{1,25},{2,26},{3,27},{4,28},{5,29},{6,30},{7,31},{8,16},{9,... | collective-permute-start | bytes 589832 | tf_op jit(solution)/shard_map/ppermute | solution.py:253
  97.9 20.7 %all-to-all-start.1 = ((bf16[4,592,128]{2,1,0:T(8,128)(2,1)}), bf16[4,592,128]{2,1,0:T(8,128)(2,1)}, u32[]{:S(2)}, u32[]{:S(2)}) async-start(bf16[4,592,128]{2,1,0:T(8,128)(2,1)} %bitcast.35), calls=%async_computation.1 | async-start | bytes 1212416 | tf_op jit(solution)/shard_map/all_to_all | solution.py:1087
  106.6 1.5 collective-permute-start.37
  111.9 12.1 %collective-permute-start.38 = (bf16[64,1536]{1,0:T(8,128)(2,1)S(1)}, bf16[64,1536]{1,0:T(8,128)(2,1)S(1)}, u32[]{:S(2)}, u32[]{:S(2)}) collective-permute-start(bf16[64,1536]{1,0:T(8,128)(2,1)S(1)} %get-tuple-element.171), channel_id=1, source_target_pairs={{0,8},{1,9},{2,10},{3,11},{4,12},{5,13},{6,14},{7,15},{8,0},{9,1},... | collective-permute-start | bytes 589832 | tf_op jit(solution)/shard_map/ppermute | solution.py:253
  113.3 10.9 %collective-permute-start.39 = (bf16[64,1536]{1,0:T(8,128)(2,1)S(1)}, bf16[64,1536]{1,0:T(8,128)(2,1)S(1)}, u32[]{:S(2)}, u32[]{:S(2)}) collective-permute-start(bf16[64,1536]{1,0:T(8,128)(2,1)S(1)} %get-tuple-element.172), channel_id=1, source_target_pairs={{0,16},{1,17},{2,18},{3,19},{4,20},{5,21},{6,22},{7,23},{8,24},{9,... | collective-permute-start | bytes 589832 | tf_op jit(solution)/shard_map/ppermute | solution.py:253
  114.3 9.8 %collective-permute-start.40 = (bf16[64,1536]{1,0:T(8,128)(2,1)S(1)}, bf16[64,1536]{1,0:T(8,128)(2,1)S(1)}, u32[]{:S(2)}, u32[]{:S(2)}) collective-permute-start(bf16[64,1536]{1,0:T(8,128)(2,1)S(1)} %get-tuple-element.173), channel_id=1, source_target_pairs={{0,24},{1,25},{2,26},{3,27},{4,28},{5,29},{6,30},{7,31},{8,16},{9,... | collective-permute-start | bytes 589832 | tf_op jit(solution)/shard_map/ppermute | solution.py:253
  118.6 20.0 %all-to-all-start.2 = ((bf16[4,592,128]{2,1,0:T(8,128)(2,1)}), bf16[4,592,128]{2,1,0:T(8,128)(2,1)}, u32[]{:S(2)}, u32[]{:S(2)}) async-start(bf16[4,592,128]{2,1,0:T(8,128)(2,1)} %bitcast.33), calls=%async_computation.2 | async-start | bytes 1212416 | tf_op jit(solution)/shard_map/all_to_all | solution.py:1087
  126.2 1.5 collective-permute-start.41
  131.6 12.1 %collective-permute-start.42 = (bf16[64,1536]{1,0:T(8,128)(2,1)S(1)}, bf16[64,1536]{1,0:T(8,128)(2,1)S(1)}, u32[]{:S(2)}, u32[]{:S(2)}) collective-permute-start(bf16[64,1536]{1,0:T(8,128)(2,1)S(1)} %get-tuple-element.185), channel_id=1, source_target_pairs={{0,8},{1,9},{2,10},{3,11},{4,12},{5,13},{6,14},{7,15},{8,0},{9,1},... | collective-permute-start | bytes 589832 | tf_op jit(solution)/shard_map/ppermute | solution.py:253
  132.4 11.3 %collective-permute-start.43 = (bf16[64,1536]{1,0:T(8,128)(2,1)S(1)}, bf16[64,1536]{1,0:T(8,128)(2,1)S(1)}, u32[]{:S(2)}, u32[]{:S(2)}) collective-permute-start(bf16[64,1536]{1,0:T(8,128)(2,1)S(1)} %get-tuple-element.186), channel_id=1, source_target_pairs={{0,16},{1,17},{2,18},{3,19},{4,20},{5,21},{6,22},{7,23},{8,24},{9,... | collective-permute-start | bytes 589832 | tf_op jit(solution)/shard_map/ppermute | solution.py:253
  133.4 10.4 %collective-permute-start.44 = (bf16[64,1536]{1,0:T(8,128)(2,1)S(1)}, bf16[64,1536]{1,0:T(8,128)(2,1)S(1)}, u32[]{:S(2)}, u32[]{:S(2)}) collective-permute-start(bf16[64,1536]{1,0:T(8,128)(2,1)S(1)} %get-tuple-element.187), channel_id=1, source_target_pairs={{0,24},{1,25},{2,26},{3,27},{4,28},{5,29},{6,30},{7,31},{8,16},{9,... | collective-permute-start | bytes 589832 | tf_op jit(solution)/shard_map/ppermute | solution.py:253
  138.5 20.0 %all-to-all-start.3 = ((bf16[4,592,128]{2,1,0:T(8,128)(2,1)}), bf16[4,592,128]{2,1,0:T(8,128)(2,1)}, u32[]{:S(2)}, u32[]{:S(2)}) async-start(bf16[4,592,128]{2,1,0:T(8,128)(2,1)} %bitcast.32), calls=%async_computation.3 | async-start | bytes 1212416 | tf_op jit(solution)/shard_map/all_to_all | solution.py:1087
  144.3 1.5 collective-permute-start.45
  149.7 12.3 %collective-permute-start.53 = (bf16[64,1536]{1,0:T(8,128)(2,1)S(1)}, bf16[64,1536]{1,0:T(8,128)(2,1)S(1)}, u32[]{:S(2)}, u32[]{:S(2)}) collective-permute-start(bf16[64,1536]{1,0:T(8,128)(2,1)S(1)} %get-tuple-element.213), channel_id=1, source_target_pairs={{0,8},{1,9},{2,10},{3,11},{4,12},{5,13},{6,14},{7,15},{8,0},{9,1},... | collective-permute-start | bytes 589832 | tf_op jit(solution)/shard_map/ppermute | solution.py:253
  150.5 11.5 %collective-permute-start.54 = (bf16[64,1536]{1,0:T(8,128)(2,1)S(1)}, bf16[64,1536]{1,0:T(8,128)(2,1)S(1)}, u32[]{:S(2)}, u32[]{:S(2)}) collective-permute-start(bf16[64,1536]{1,0:T(8,128)(2,1)S(1)} %get-tuple-element.214), channel_id=1, source_target_pairs={{0,16},{1,17},{2,18},{3,19},{4,20},{5,21},{6,22},{7,23},{8,24},{9,... | collective-permute-start | bytes 589832 | tf_op jit(solution)/shard_map/ppermute | solution.py:253
  151.6 10.5 %collective-permute-start.55 = (bf16[64,1536]{1,0:T(8,128)(2,1)S(1)}, bf16[64,1536]{1,0:T(8,128)(2,1)S(1)}, u32[]{:S(2)}, u32[]{:S(2)}) collective-permute-start(bf16[64,1536]{1,0:T(8,128)(2,1)S(1)} %get-tuple-element.215), channel_id=1, source_target_pairs={{0,24},{1,25},{2,26},{3,27},{4,28},{5,29},{6,30},{7,31},{8,16},{9,... | collective-permute-start | bytes 589832 | tf_op jit(solution)/shard_map/ppermute | solution.py:253
  158.5 23.4 %all-to-all-start.4 = ((bf16[4,592,128]{2,1,0:T(8,128)(2,1)}), bf16[4,592,128]{2,1,0:T(8,128)(2,1)S(1)}, u32[]{:S(2)}, u32[]{:S(2)}) async-start(bf16[4,592,128]{2,1,0:T(8,128)(2,1)} %bitcast.34), calls=%async_computation.4 | async-start | bytes 1212416 | tf_op jit(solution)/shard_map/all_to_all | solution.py:1087
  163.0 1.5 collective-permute-start.56
  164.6 21.2 %collective-permute-start.57 = (bf16[256,384]{1,0:T(8,128)(2,1)S(1)}, bf16[256,384]{1,0:T(8,128)(2,1)S(1)}, u32[]{:S(2)}, u32[]{:S(2)}) collective-permute-start(bf16[256,384]{1,0:T(8,128)(2,1)S(1)} %get-tuple-element.222), channel_id=1, source_target_pairs={{0,0},{1,5},{2,8},{3,13},{4,16},{5,21},{6,24},{7,29},{8,2},{9,7},{... | collective-permute-start | bytes 589832 | tf_op jit(solution)/shard_map/ppermute | solution.py:253
  165.2 20.5 %collective-permute-start.58 = (bf16[256,384]{1,0:T(8,128)(2,1)S(1)}, bf16[256,384]{1,0:T(8,128)(2,1)S(1)}, u32[]{:S(2)}, u32[]{:S(2)}) collective-permute-start(bf16[256,384]{1,0:T(8,128)(2,1)S(1)} %get-tuple-element.223), channel_id=1, source_target_pairs={{0,2},{1,7},{2,10},{3,15},{4,18},{5,23},{6,26},{7,31},{8,0},{9,5},... | collective-permute-start | bytes 589832 | tf_op jit(solution)/shard_map/ppermute | solution.py:253
  182.1 7.3 %collective-permute-start.46 = (bf16[592,128]{1,0:T(8,128)(2,1)S(1)}, bf16[592,128]{1,0:T(8,128)(2,1)S(1)}, u32[]{:S(2)}, u32[]{:S(2)}) collective-permute-start(bf16[592,128]{1,0:T(8,128)(2,1)S(1)} %get-tuple-element.209), channel_id=1, source_target_pairs={{0,8},{1,9},{2,10},{3,11},{4,12},{5,13},{6,14},{7,15},{8,0},{9,1},... | collective-permute-start | bytes 454664 | tf_op jit(solution)/shard_map/ppermute | solution.py:253
  183.7 7.9 %collective-permute-start.47 = (bf16[592,128]{1,0:T(8,128)(2,1)S(1)}, bf16[592,128]{1,0:T(8,128)(2,1)S(1)}, u32[]{:S(2)}, u32[]{:S(2)}) collective-permute-start(bf16[592,128]{1,0:T(8,128)(2,1)S(1)} %get-tuple-element.210), channel_id=1, source_target_pairs={{0,16},{1,17},{2,18},{3,19},{4,20},{5,21},{6,22},{7,23},{8,24},{9,... | collective-permute-start | bytes 454664 | tf_op jit(solution)/shard_map/ppermute | solution.py:253
  184.8 7.0 %collective-permute-start.48 = (bf16[592,128]{1,0:T(8,128)(2,1)S(1)}, bf16[592,128]{1,0:T(8,128)(2,1)S(1)}, u32[]{:S(2)}, u32[]{:S(2)}) collective-permute-start(bf16[592,128]{1,0:T(8,128)(2,1)S(1)} %get-tuple-element.211), channel_id=1, source_target_pairs={{0,24},{1,25},{2,26},{3,27},{4,28},{5,29},{6,30},{7,31},{8,16},{9,... | collective-permute-start | bytes 454664 | tf_op jit(solution)/shard_map/ppermute | solution.py:253
  185.7 6.4 %collective-permute-start.49 = (bf16[592,128]{1,0:T(8,128)(2,1)S(1)}, bf16[592,128]{1,0:T(8,128)(2,1)S(1)}, u32[]{:S(2)}, u32[]{:S(2)}) collective-permute-start(bf16[592,128]{1,0:T(8,128)(2,1)S(1)} %get-tuple-element.208.refs_0_), channel_id=1, source_target_pairs={{0,1},{1,0},{2,3},{3,2},{4,5},{5,4},{6,7},{7,6},{8,9},{9,8},{10,11... | collective-permute-start | bytes 454664 | tf_op jit(solution)/shard_map/ppermute | solution.py:253
  185.8 6.7 %collective-permute-start.59 = (bf16[256,384]{1,0:T(8,128)(2,1)S(1)}, bf16[256,384]{1,0:T(8,128)(2,1)S(1)}, u32[]{:S(2)}, u32[]{:S(2)}) collective-permute-start(bf16[256,384]{1,0:T(8,128)(2,1)S(1)} %collective-permute-done.57.refs_9_), channel_id=1, source_target_pairs={{0,1},{1,0},{2,3},{3,2},{4,5},{5,4},{6,7},{7,6},{8,9},{9,8},{10,11... | collective-permute-start | bytes 589832 | tf_op jit(solution)/shard_map/ppermute | solution.py:253
  189.4 3.1 %collective-permute-start.60 = (bf16[256,384]{1,0:T(8,128)(2,1)S(1)}, bf16[256,384]{1,0:T(8,128)(2,1)S(1)}, u32[]{:S(2)}, u32[]{:S(2)}) collective-permute-start(bf16[256,384]{1,0:T(8,128)(2,1)S(1)} %collective-permute-done.58.refs_10_), channel_id=1, source_target_pairs={{0,1},{1,0},{2,3},{3,2},{4,5},{5,4},{6,7},{7,6},{8,9},{9,8},{10,11... | collective-permute-start | bytes 589832 | tf_op jit(solution)/shard_map/ppermute | solution.py:253
  192.1 1.4 collective-permute-start.52
  (7 other events, 91.9 us)

commit v6 on v5

--- a/solution.py
+++ b/solution.py
@@ -11,7 +11,7 @@
 
 CONVS = 2
 BACK_FLOPS = (6 * 10**9, 6 * 10**9, 6 * 10**9, 0)
-PICK_FLOPS = 4 * 10**9
+PICK_FLOPS = 2 * 10**9
 COT_LAYER = 2
 INPUT_FLOPS = 4000000000
 
@@ -729,7 +729,7 @@
     copies = start_all(
         [
             pltpu.make_async_copy(own_weights.at[rows], weights.at[:, pl.ds(0, size)], sems.at[0]),
-            pltpu.make_async_copy(other_weights.at[rows], weights.at[:, pl.ds(size, size)], sems.at[1]),
+            pltpu.make_async_copy(other_weights, weights.at[:, pl.ds(size, size)], sems.at[1]),
         ]
     )
     full_copy = pltpu.make_async_copy(full_in, full, sems.at[2])
@@ -785,7 +785,7 @@
 
 
 def turn_weights_kernel(layers, *refs):
-    sources, outs, (full, turned, stage, sems) = refs[:4], refs[4:6], refs[6:]
+    sources, own, others, (full, turned, stage, sems) = refs[:4], refs[4], refs[5:-4], refs[-4:]
     section, _, core = place()
     rows, channels = full.shape[1:]
     half = channels // 2
@@ -799,9 +799,11 @@
             for k in range(4):
                 at = pl.multiple_of((core ^ j) * half + (section ^ k) * ch, ch)
                 stage[j, n * half + k * ch : n * half + (k + 1) * ch, :rows] = turned[pl.ds(at, ch), :]
-    wait_all(
-        start_all([pltpu.make_async_copy(stage.at[j], outs[j], sems.at[j]) for j in range(2)])
-    )
+    copies = [pltpu.make_async_copy(stage.at[0], own, sems.at[0])]
+    for n, other in enumerate(others):
+        source = stage.at[1, pl.ds(n * half, half)]
+        copies.append(pltpu.make_async_copy(source, other, sems.at[1 + n]))
+    wait_all(start_all(copies))
 
 
 def input_kernel(*refs):
@@ -976,8 +978,7 @@
     kept, fulls = [normed], [full]
     same_core = [[2 * z + c for z in range(layers)] for c in range(2)]
     for layer in range(1, layers):
-        picks = layer == COT_LAYER
-        weights = slices if picks else call(
+        weights = call(
             partial(pick_kernel, layer),
             [weight_slice],
             [],
@@ -987,11 +988,11 @@
             held=range(4),
             copies=1,
         )
-        beside = [] if picks else [*weights]
+        beside = [*weights]
         if layer == 1:
-            turned = call(
+            turned, *crossing = call(
                 partial(turn_weights_kernel, layers),
-                [((layers * 4 * ch, tap_rows), bf16)] * 2,
+                [((layers * 4 * ch, tap_rows), bf16)] + [((4 * ch, tap_rows), bf16)] * layers,
                 [
                     ((layers, TAPS * ch, channels), bf16),
                     ((channels, TAPS * ch), bf16),
@@ -1000,10 +1001,10 @@
                 after(slices, hidden),
                 "turn_weights",
                 held=range(4),
-                held_outs=(0, 1),
-                copies=layers,
+                held_outs=range(1 + layers),
+                copies=1 + layers,
             )
-            beside.append(turned)
+            beside.append((turned, crossing))
         if layer == COT_LAYER - 1:
             (cot_slots,) = call(
                 cot_slice_kernel,
@@ -1018,9 +1019,8 @@
         if layer == COT_LAYER:
             cot_slots = after(cot_slots, hidden)
             cots = lax.all_to_all(cot_slots, "dp", 0, 0, tiled=True, axis_index_groups=same_core)
-        if layer == 2:
-            turned = [turned[0], to_core(after(turned[1], hidden))]
         if layer == last:
+            crossing[last] = to_core(after(crossing[last], hidden))
             cots = after(cots, hidden)
             (cot,) = call(
                 cot_kernel,
@@ -1036,14 +1036,13 @@
         blocks = with_core(blocks)
         if layer < last:
             hidden, normed, full = call(
-                partial(forward_kernel, dims, layer, False, picks, layer == CONVS - 1),
+                partial(forward_kernel, dims, layer, False, False, layer == CONVS - 1),
                 [map_out, kept_out, full_map],
-                [full_map, tap_scratch, kept_out] + [weight_slice] * picks,
+                [full_map, tap_scratch, kept_out],
                 [*blocks, *weights, inside, facts],
                 "forward",
-                held=range(8, 12) if picks else (),
                 held_outs=(1, 2),
-                loose=(12, 13) if picks else (9, 10),
+                loose=(9, 10),
                 flops=conv_flops,
                 copies=3,
             )
@@ -1073,7 +1072,7 @@
                 ((2 * tap_rows, length), bf16),
                 ((4 * ch, 2 * tap_rows), bf16),
             ],
-            [grad_pre, to_core(grad_pre), *turned, fulls[layer], sums, facts],
+            [grad_pre, to_core(grad_pre), turned, crossing[layer], fulls[layer], sums, facts],
             "conv_back",
             held=(2, 4),
             free=(3,),
@@ -1086,6 +1085,7 @@
             share = after(share, shares[layer + 1])
         shares[layer] = lax.all_to_all(share, "dp", 0, 0, tiled=True, axis_index_groups=same_core)
         if layer:
+            crossing[layer - 1] = to_core(after(crossing[layer - 1], parts))
             held = call(
                 partial(fetch_kernel, layer - 1),
                 [kept_out, ((META_ROWS, channels), bf16)],

time: 196 us -> 196 us (level)
    ppermute x61 -> x64, waiting for transfers between devices: 50.1 us -> 48.3 us  [send(): return lax.ppermute(x, AXES, pairs)]
    ppermute x61 -> x64, starting transfers between devices: 48.4 us -> 49 us  [send(): return lax.ppermute(x, AXES, pairs)]
    pallas_call x26 -> x27, Pallas kernels: 50.3 us -> 50.4 us  [call(): pl.pallas_call(kernel, out_shape=shapes, in_specs=[pl.BlockSpec(memory_sp...]
  transfers between devices with their start and end apart: 66 -> 69, of which waited for: 35 -> 33; matrix products, arithmetic and copies ran while one was open for 0% -> 0% of each run, Pallas kernels for 19% -> 19%
where the time goes in v6:
time: 196 us; the launch traced here: 195 us
  waiting for transfers between devices  73.1 us (37%)
  starting transfers between devices  70.1 us (36%)
  Pallas kernels  50.4 us (26%)
    pallas_call x27, Pallas kernels, call(): pl.pallas_call(kernel, out_shape=shapes, in_specs=[pl.BlockSpec(memory_sp...  50.4 us
    ppermute x64, starting transfers between devices, send(): return lax.ppermute(x, AXES, pairs)  49 us
    ppermute x64, waiting for transfers between devices, send(): return lax.ppermute(x, AXES, pairs)  48.3 us
    all_to_all x4, waiting for transfers between devices, plane_shards(): lax.all_to_all(share, 'dp', 0, 0, tiled=True, axis_index_groups=same_core)  24.8 us
    all_to_all x4, starting transfers between devices, plane_shards(): lax.all_to_all(share, 'dp', 0, 0, tiled=True, axis_index_groups=same_core)  16.2 us
    all_to_all x1, starting transfers between devices, plane_shards(): lax.all_to_all(cot_slots, 'dp', 0, 0, tiled=True, axis_index_groups=same_...  4.87 us
  transfers between devices with their start and end apart: 69, of which 33 were waited for; matrix products, arithmetic and copies ran while one was open for 0% of the time, Pallas kernels for 19%

profile of v6, /device:TPU:0, one launch (start us, length us, event | category | flops | bytes accessed | tf_op | source)
XLA Modules:
  0.0 195.0 jit_solution(14819884124228768740)
XLA Ops:
  0.6 2.5 %weight_pack.1 = (bf16[592,512]{1,0:T(8,128)(2,1)S(1)}, bf16[592,512]{1,0:T(8,128)(2,1)S(1)}, bf16[592,512]{1,0:T(8,128)(2,1)S(1)}, bf16[592,512]{1,0:T(8,128)(2,1)S(1)}) custom-call(f32[1,512]{1,0:T(1,128)} %gain.1, f32[1,512]{1,0:T(1,128)} %bias.1, bf16[9,512,512]{2,1,0:T(8,128)(2,1)} %bitcast.29), custom_call_target="tpu_custom_call" | custom-call | bytes 7147520 | tf_op jit(solution)/shard_map/weight_pack/pallas_call | solution.py:890
  3.1 3.0 %collective-permute-start.7 = (bf16[592,512]{1,0:T(8,128)(2,1)S(1)}, bf16[592,512]{1,0:T(8,128)(2,1)S(1)}, u32[]{:S(2)}, u32[]{:S(2)}) collective-permute-start(bf16[592,512]{1,0:T(8,128)(2,1)S(1)} %get-tuple-element.130), channel_id=1, source_target_pairs={{0,8},{1,9},{2,10},{3,11},{4,12},{5,13},{6,14},{7,15},{8,0},{9,1},... | collective-permute-start | bytes 1818632 | tf_op jit(solution)/shard_map/ppermute | solution.py:253
  6.2 1.5 collective-permute-start.8
  7.7 1.4 frames.1
  9.1 1.6 collective-permute-start
  11.2 2.6 %collective-permute-start.1 = (bf16[208,512]{1,0:T(8,128)(2,1)S(1)}, bf16[208,512]{1,0:T(8,128)(2,1)S(1)}, u32[]{:S(2)}, u32[]{:S(2)}) collective-permute-start(bf16[208,512]{1,0:T(8,128)(2,1)S(1)} %get-tuple-element.136), channel_id=1, source_target_pairs={{0,4},{1,5},{2,6},{3,7},{4,0},{5,1},{6,2},{7,3},{8,12},{9,13},{10,... | collective-permute-start | bytes 638984 | tf_op jit(solution)/shard_map/ppermute | solution.py:253
  13.8 6.1 %collective-permute-done.refs_1_ = bf16[208,512]{1,0:T(8,128)(2,1)S(1)} collective-permute-done((bf16[208,512]{1,0:T(8,128)(2,1)S(1)}, bf16[208,512]{1,0:T(8,128)(2,1)S(1)}, u32[]{:S(2)}, u32[]{:S(2)}) %collective-permute-start) | collective-permute-done | bytes 213024 | tf_op jit(solution)/shard_map/ppermute | solution.py:253
  19.8 2.5 %collective-permute-start.2 = (bf16[208,512]{1,0:T(8,128)(2,1)S(1)}, bf16[208,512]{1,0:T(8,128)(2,1)S(1)}, u32[]{:S(2)}, u32[]{:S(2)}) collective-permute-start(bf16[208,512]{1,0:T(8,128)(2,1)S(1)} %get-tuple-element.137), channel_id=1, source_target_pairs={{0,6},{1,7},{2,4},{3,5},{4,2},{5,3},{6,0},{7,1},{8,14},{9,15},{10,... | collective-permute-start | bytes 638984 | tf_op jit(solution)/shard_map/ppermute | solution.py:253
  22.3 2.8 %collective-permute-done.1.refs_2_ = bf16[208,512]{1,0:T(8,128)(2,1)S(1)} collective-permute-done((bf16[208,512]{1,0:T(8,128)(2,1)S(1)}, bf16[208,512]{1,0:T(8,128)(2,1)S(1)}, u32[]{:S(2)}, u32[]{:S(2)}) %collective-permute-start.1) | collective-permute-done | bytes 213024 | tf_op jit(solution)/shard_map/ppermute | solution.py:253
  25.1 2.5 %collective-permute-done.2.refs_3_ = bf16[208,512]{1,0:T(8,128)(2,1)S(1)} collective-permute-done((bf16[208,512]{1,0:T(8,128)(2,1)S(1)}, bf16[208,512]{1,0:T(8,128)(2,1)S(1)}, u32[]{:S(2)}, u32[]{:S(2)}) %collective-permute-start.2) | collective-permute-done | bytes 213024 | tf_op jit(solution)/shard_map/ppermute | solution.py:253
  28.1 6.2 %collective-permute-done.8.refs_10_.refs_2_ = bf16[592,512]{1,0:T(8,128)(2,1)S(1)} collective-permute-done((bf16[592,512]{1,0:T(8,128)(2,1)S(1)}, bf16[592,512]{1,0:T(8,128)(2,1)S(1)}, u32[]{:S(2)}, u32[]{:S(2)}) %collective-permute-start.8) | collective-permute-done | bytes 606240 | tf_op jit(solution)/shard_map/ppermute | solution.py:253
  34.4 1.4 collective-permute-done.6.refs_7_
  35.8 2.5 %forward.3 = (bf16[64,1536]{1,0:T(8,128)(2,1)S(1)}, f32[64,1664]{1,0:T(8,128)}, bf16[1536,512]{1,0:T(8,128)(2,1)}, f32[1,1536]{1,0:T(1,128)S(1)}) custom-call(bf16[208,512]{1,0:T(8,128)(2,1)S(1)} %get-tuple-element.134.refs_0_, bf16[208,512]{1,0:T(8,128)(2,1)S(1)} %collective-permute-done.refs_1_, bf16[208,512]{1,0:T(8,128)(2,1)S(1)} %collective-permute-done.1.refs_2_, ...), custom_call_target="tpu_custom_call" | custom-call | flops 905969664 | bytes 6428672 | tf_op jit(solution)/shard_map/forward/pallas_call | solution.py:890
  38.4 1.5 collective-permute-start.12
  39.9 1.5 collective-permute-start.10
  41.9 2.0 %cot_slices.1 = bf16[768,128]{1,0:T(8,128)(2,1)} custom-call(bf16[4,192,512]{2,1,0:T(8,128)(2,1)} %bitcast.33), custom_call_target="tpu_custom_call" | custom-call | bytes 983040 | tf_op jit(solution)/shard_map/cot_slices/pallas_call | solution.py:890
  43.9 3.7 %turn_weights.1 = (bf16[1024,640]{1,0:T(8,128)(2,1)}, bf16[256,640]{1,0:T(8,128)(2,1)}, bf16[256,640]{1,0:T(8,128)(2,1)}, bf16[256,640]{1,0:T(8,128)(2,1)}, bf16[256,640]{1,0:T(8,128)(2,1)}) custom-call(bf16[592,512]{1,0:T(8,128)(2,1)} %copy-done, bf16[592,512]{1,0:T(8,128)(2,1)} %copy-done.1, bf16[592,512]{1,0:T(8,128)(2,1)} %copy-done.2, ...), custom_call_target="tpu_custom_call" | custom-call | bytes 5046272 | tf_op jit(solution)/shard_map/turn_weights/pallas_call | solution.py:890
  47.7 1.1 pick.3.refs_8_
  49.4 1.2 collective-permute-done.10.refs_1_
  52.3 3.1 %forward.4 = (bf16[64,1536]{1,0:T(8,128)(2,1)S(1)}, f32[64,1664]{1,0:T(8,128)}, bf16[512,1536]{1,0:T(8,128)(2,1)}) custom-call(bf16[64,1536]{1,0:T(8,128)(2,1)S(1)} %get-tuple-element.144.refs_0_, bf16[64,1536]{1,0:T(8,128)(2,1)S(1)} %collective-permute-done.10.refs_1_, bf16[64,1536]{1,0:T(8,128)(2,1)S(1)} %collective-permute-done.11.refs_2_, ...), custom_call_target="tpu_custom_call" | custom-call | flops 905969664 | bytes 4478976 | tf_op jit(solution)/shard_map/forward/pallas_call | solution.py:890
  55.4 1.2 collective-permute-start.19
  56.5 1.5 collective-permute-start.17
  59.0 4.9 %all-to-all-start = ((bf16[4,192,128]{2,1,0:T(8,128)(2,1)}), bf16[4,192,128]{2,1,0:T(8,128)(2,1)S(1)}, u32[]{:S(2)}, u32[]{:S(2)}) async-start(bf16[4,192,128]{2,1,0:T(8,128)(2,1)} %bitcast.7), calls=%async_computation | async-start | bytes 393216 | tf_op jit(solution)/shard_map/all_to_all | solution.py:1021
  63.8 1.1 pick.4.refs_8_
  65.2 2.0 %collective-permute-done.17.refs_1_ = bf16[64,1536]{1,0:T(8,128)(2,1)S(1)} collective-permute-done((bf16[64,1536]{1,0:T(8,128)(2,1)S(1)}, bf16[64,1536]{1,0:T(8,128)(2,1)S(1)}, u32[]{:S(2)}, u32[]{:S(2)}) %collective-permute-start.17) | collective-permute-done | bytes 196640 | tf_op jit(solution)/shard_map/ppermute | solution.py:253
  69.1 2.4 %forward.5 = (bf16[64,1536]{1,0:T(8,128)(2,1)S(1)}, f32[64,1664]{1,0:T(8,128)}, bf16[512,1536]{1,0:T(8,128)(2,1)}) custom-call(bf16[64,1536]{1,0:T(8,128)(2,1)S(1)} %get-tuple-element.157.refs_0_, bf16[64,1536]{1,0:T(8,128)(2,1)S(1)} %collective-permute-done.17.refs_1_, bf16[64,1536]{1,0:T(8,128)(2,1)S(1)} %collective-permute-done.18.refs_2_, ...), custom_call_target="tpu_custom_call" | custom-call | flops 905969664 | bytes 4478976 | tf_op jit(solution)/shard_map/forward/pallas_call | solution.py:890
  71.5 1.1 collective-permute-start.26
  72.6 1.5 collective-permute-start.24
  75.7 1.1 pick.5.refs_8_
  77.1 3.1 %collective-permute-done.26.refs_3_ = bf16[64,1536]{1,0:T(8,128)(2,1)S(1)} collective-permute-done((bf16[64,1536]{1,0:T(8,128)(2,1)S(1)}, bf16[64,1536]{1,0:T(8,128)(2,1)S(1)}, u32[]{:S(2)}, u32[]{:S(2)}) %collective-permute-start.26) | collective-permute-done | bytes 196640 | tf_op jit(solution)/shard_map/ppermute | solution.py:253
  80.3 3.0 %collective-permute-done.24.refs_1_ = bf16[64,1536]{1,0:T(8,128)(2,1)S(1)} collective-permute-done((bf16[64,1536]{1,0:T(8,128)(2,1)S(1)}, bf16[64,1536]{1,0:T(8,128)(2,1)S(1)}, u32[]{:S(2)}, u32[]{:S(2)}) %collective-permute-start.24) | collective-permute-done | bytes 196640 | tf_op jit(solution)/shard_map/ppermute | solution.py:253
  85.1 2.7 %turn.1 = (bf16[64,1536]{1,0:T(8,128)(2,1)}, bf16[512,1536]{1,0:T(8,128)(2,1)}, bf16[64,1536]{1,0:T(8,128)(2,1)S(1)}, f32[64,256]{1,0:T(8,128)S(1)}) custom-call(bf16[64,1536]{1,0:T(8,128)(2,1)S(1)} %get-tuple-element.163.refs_0_, bf16[64,1536]{1,0:T(8,128)(2,1)S(1)} %collective-permute-done.24.refs_1_, ...), custom_call_target="tpu_custom_call" | custom-call | flops 905969664 | bytes 4511744 | tf_op jit(solution)/shard_map/turn/pallas_call | solution.py:890
  88.0 1.3 collective-permute-done.32.other
  89.3 3.9 %conv_back.4 = (bf16[64,1536]{1,0:T(8,128)(2,1)S(1)}, bf16[64,1536]{1,0:T(8,128)(2,1)S(1)}, bf16[64,1536]{1,0:T(8,128)(2,1)S(1)}, bf16[64,1536]{1,0:T(8,128)(2,1)S(1)}, bf16[2368,128]{1,0:T(8,128)(2,1)}) custom-call(bf16[64,1536]{1,0:T(8,128)(2,1)S(1)} %get-tuple-element.171.own, bf16[64,1536]{1,0:T(8,128)(2,1)S(1)} %collective-permute-done.32.other, ...), custom_call_target="tpu_custom_call" | custom-call | bytes 5160960 | tf_op jit(solution)/shard_map/conv_back/pallas_call | solution.py:890
  94.9 1.9 collective-permute-start.36
  96.8 4.9 %all-to-all-start.1 = ((bf16[4,592,128]{2,1,0:T(8,128)(2,1)}), bf16[4,592,128]{2,1,0:T(8,128)(2,1)S(1)}, u32[]{:S(2)}, u32[]{:S(2)}) async-start(bf16[4,592,128]{2,1,0:T(8,128)(2,1)} %bitcast.36), calls=%async_computation.1 | async-start | bytes 1212416 | tf_op jit(solution)/shard_map/all_to_all | solution.py:1086
  102.7 2.2 %collective-permute-done.36.refs_3_ = bf16[64,1536]{1,0:T(8,128)(2,1)S(1)} collective-permute-done((bf16[64,1536]{1,0:T(8,128)(2,1)S(1)}, bf16[64,1536]{1,0:T(8,128)(2,1)S(1)}, u32[]{:S(2)}, u32[]{:S(2)}) %collective-permute-start.36) | collective-permute-done | bytes 196640 | tf_op jit(solution)/shard_map/ppermute | solution.py:253
  105.6 1.4 collective-permute-done.37.other
  107.0 3.9 %conv_back.5 = (bf16[64,1536]{1,0:T(8,128)(2,1)S(1)}, bf16[64,1536]{1,0:T(8,128)(2,1)S(1)}, bf16[64,1536]{1,0:T(8,128)(2,1)S(1)}, bf16[64,1536]{1,0:T(8,128)(2,1)S(1)}, bf16[2368,128]{1,0:T(8,128)(2,1)}) custom-call(bf16[64,1536]{1,0:T(8,128)(2,1)S(1)} %get-tuple-element.186.own, bf16[64,1536]{1,0:T(8,128)(2,1)S(1)} %collective-permute-done.37.other, ...), custom_call_target="tpu_custom_call" | custom-call | flops 6000000000 | bytes 5160960 | tf_op jit(solution)/shard_map/conv_back/pallas_call | solution.py:890
  110.9 1.3 collective-permute-start.39
  113.3 1.2 collective-permute-start.41
  114.5 4.1 %all-to-all-done.1 = bf16[4,592,128]{2,1,0:T(8,128)(2,1)S(1)} async-done(((bf16[4,592,128]{2,1,0:T(8,128)(2,1)}), bf16[4,592,128]{2,1,0:T(8,128)(2,1)S(1)}, u32[]{:S(2)}, u32[]{:S(2)}) %all-to-all-start.1) | async-done | bytes 606240 | tf_op jit(solution)/shard_map/all_to_all | solution.py:1086
  118.6 4.4 %all-to-all-start.2 = ((bf16[4,592,128]{2,1,0:T(8,128)(2,1)}), bf16[4,592,128]{2,1,0:T(8,128)(2,1)}, u32[]{:S(2)}, u32[]{:S(2)}) async-start(bf16[4,592,128]{2,1,0:T(8,128)(2,1)} %bitcast.35), calls=%async_computation.2 | async-start | bytes 1212416 | tf_op jit(solution)/shard_map/all_to_all | solution.py:1086
  124.1 2.1 %norm_back.4 = (bf16[64,1536]{1,0:T(8,128)(2,1)S(1)}, f32[64,256]{1,0:T(8,128)S(1)}) custom-call(bf16[64,1536]{1,0:T(8,128)(2,1)S(1)} %get-tuple-element.190.refs_0_, bf16[64,1536]{1,0:T(8,128)(2,1)S(1)} %collective-permute-done.39.refs_1_, bf16[64,1536]{1,0:T(8,128)(2,1)S(1)} %collective-permute-done.40.refs_2_, ...), custom_call_target="tpu_custom_call" | custom-call | bytes 1595392 | tf_op jit(solution)/shard_map/norm_back/pallas_call | solution.py:890
  126.3 1.4 collective-permute-done.42.other
  127.7 3.9 %conv_back.6 = (bf16[64,1536]{1,0:T(8,128)(2,1)S(1)}, bf16[64,1536]{1,0:T(8,128)(2,1)S(1)}, bf16[64,1536]{1,0:T(8,128)(2,1)S(1)}, bf16[64,1536]{1,0:T(8,128)(2,1)S(1)}, bf16[2368,128]{1,0:T(8,128)(2,1)}) custom-call(bf16[64,1536]{1,0:T(8,128)(2,1)S(1)} %get-tuple-element.201.own, bf16[64,1536]{1,0:T(8,128)(2,1)S(1)} %collective-permute-done.42.other, ...), custom_call_target="tpu_custom_call" | custom-call | flops 6000000000 | bytes 5160960 | tf_op jit(solution)/shard_map/conv_back/pallas_call | solution.py:890
  133.2 1.9 collective-permute-start.46
  135.2 3.8 %all-to-all-done.2 = bf16[4,592,128]{2,1,0:T(8,128)(2,1)} async-done(((bf16[4,592,128]{2,1,0:T(8,128)(2,1)}), bf16[4,592,128]{2,1,0:T(8,128)(2,1)}, u32[]{:S(2)}, u32[]{:S(2)}) %all-to-all-start.2) | async-done | bytes 606240 | tf_op jit(solution)/shard_map/all_to_all | solution.py:1086
  139.0 3.5 %all-to-all-start.3 = ((bf16[4,592,128]{2,1,0:T(8,128)(2,1)}), bf16[4,592,128]{2,1,0:T(8,128)(2,1)S(1)}, u32[]{:S(2)}, u32[]{:S(2)}) async-start(bf16[4,592,128]{2,1,0:T(8,128)(2,1)} %bitcast.34), calls=%async_computation.3 | async-start | bytes 1212416 | tf_op jit(solution)/shard_map/all_to_all | solution.py:1086
  144.2 1.4 collective-permute-done.47.other
  145.6 3.8 %conv_back.7 = (bf16[64,1536]{1,0:T(8,128)(2,1)S(1)}, bf16[64,1536]{1,0:T(8,128)(2,1)S(1)}, bf16[64,1536]{1,0:T(8,128)(2,1)S(1)}, bf16[64,1536]{1,0:T(8,128)(2,1)S(1)}, bf16[2368,128]{1,0:T(8,128)(2,1)}) custom-call(bf16[64,1536]{1,0:T(8,128)(2,1)S(1)} %get-tuple-element.216.own, bf16[64,1536]{1,0:T(8,128)(2,1)S(1)} %collective-permute-done.47.other, ...), custom_call_target="tpu_custom_call" | custom-call | flops 6000000000 | bytes 5160960 | tf_op jit(solution)/shard_map/conv_back/pallas_call | solution.py:890
  149.4 1.1 collective-permute-start.56
  151.6 1.4 collective-permute-start.58
  153.0 5.2 %all-to-all-done.3 = bf16[4,592,128]{2,1,0:T(8,128)(2,1)S(1)} async-done(((bf16[4,592,128]{2,1,0:T(8,128)(2,1)}), bf16[4,592,128]{2,1,0:T(8,128)(2,1)S(1)}, u32[]{:S(2)}, u32[]{:S(2)}) %all-to-all-start.3) | async-done | bytes 606240 | tf_op jit(solution)/shard_map/all_to_all | solution.py:1086
  158.1 3.5 %all-to-all-start.4 = ((bf16[4,592,128]{2,1,0:T(8,128)(2,1)}), bf16[4,592,128]{2,1,0:T(8,128)(2,1)S(1)}, u32[]{:S(2)}, u32[]{:S(2)}) async-start(bf16[4,592,128]{2,1,0:T(8,128)(2,1)} %bitcast.37), calls=%async_computation.4 | async-start | bytes 1212416 | tf_op jit(solution)/shard_map/all_to_all | solution.py:1086
  162.7 1.4 collective-permute-done.59.got
  164.9 3.5 %collective-permute-start.61 = (bf16[256,384]{1,0:T(8,128)(2,1)S(1)}, bf16[256,384]{1,0:T(8,128)(2,1)S(1)}, u32[]{:S(2)}, u32[]{:S(2)}) collective-permute-start(bf16[256,384]{1,0:T(8,128)(2,1)S(1)} %get-tuple-element.245), channel_id=1, source_target_pairs={{0,2},{1,7},{2,10},{3,15},{4,18},{5,23},{6,26},{7,31},{8,0},{9,5},... | collective-permute-start | bytes 589832 | tf_op jit(solution)/shard_map/ppermute | solution.py:253
  168.3 1.5 fold.1
  169.9 11.7 %all-to-all-done.4 = bf16[4,592,128]{2,1,0:T(8,128)(2,1)S(1)} async-done(((bf16[4,592,128]{2,1,0:T(8,128)(2,1)}), bf16[4,592,128]{2,1,0:T(8,128)(2,1)S(1)}, u32[]{:S(2)}, u32[]{:S(2)}) %all-to-all-start.4) | async-done | bytes 606240 | tf_op jit(solution)/shard_map/all_to_all | solution.py:1086
  181.8 1.5 collective-permute-start.49
  183.3 1.1 collective-permute-start.50
  185.9 3.1 %collective-permute-done.49.refs_1_ = bf16[592,128]{1,0:T(8,128)(2,1)S(1)} collective-permute-done((bf16[592,128]{1,0:T(8,128)(2,1)S(1)}, bf16[592,128]{1,0:T(8,128)(2,1)S(1)}, u32[]{:S(2)}, u32[]{:S(2)}) %collective-permute-start.49) | collective-permute-done | bytes 151584 | tf_op jit(solution)/shard_map/ppermute | solution.py:253
  189.1 2.2 %collective-permute-done.50.refs_2_ = bf16[592,128]{1,0:T(8,128)(2,1)S(1)} collective-permute-done((bf16[592,128]{1,0:T(8,128)(2,1)S(1)}, bf16[592,128]{1,0:T(8,128)(2,1)S(1)}, u32[]{:S(2)}, u32[]{:S(2)}) %collective-permute-start.50) | collective-permute-done | bytes 151584 | tf_op jit(solution)/shard_map/ppermute | solution.py:253
  193.1 1.9 outputs.1
  (127 shorter events, 25.8 us)
Async XLA Ops:
  3.1 24.5 %collective-permute-start.7 = (bf16[592,512]{1,0:T(8,128)(2,1)S(1)}, bf16[592,512]{1,0:T(8,128)(2,1)S(1)}, u32[]{:S(2)}, u32[]{:S(2)}) collective-permute-start(bf16[592,512]{1,0:T(8,128)(2,1)S(1)} %get-tuple-element.130), channel_id=1, source_target_pairs={{0,8},{1,9},{2,10},{3,11},{4,12},{5,13},{6,14},{7,15},{8,0},{9,1},... | collective-permute-start | bytes 1818632 | tf_op jit(solution)/shard_map/ppermute | solution.py:253
  6.2 28.1 %collective-permute-start.8 = (bf16[592,512]{1,0:T(8,128)(2,1)S(1)}, bf16[592,512]{1,0:T(8,128)(2,1)S(1)}, u32[]{:S(2)}, u32[]{:S(2)}) collective-permute-start(bf16[592,512]{1,0:T(8,128)(2,1)S(1)} %get-tuple-element.131), channel_id=1, source_target_pairs={{0,16},{1,17},{2,18},{3,19},{4,20},{5,21},{6,22},{7,23},{8,24},{9,... | collective-permute-start | bytes 1818632 | tf_op jit(solution)/shard_map/ppermute | solution.py:253
  9.1 10.8 %collective-permute-start = (bf16[208,512]{1,0:T(8,128)(2,1)S(1)}, bf16[208,512]{1,0:T(8,128)(2,1)S(1)}, u32[]{:S(2)}, u32[]{:S(2)}) collective-permute-start(bf16[208,512]{1,0:T(8,128)(2,1)S(1)} %get-tuple-element.135), channel_id=1, source_target_pairs={{0,2},{1,3},{2,0},{3,1},{4,6},{5,7},{6,4},{7,5},{8,10},{9,11},{10,... | collective-permute-start | bytes 638984 | tf_op jit(solution)/shard_map/ppermute | solution.py:253
  10.7 23.6 %collective-permute-start.9 = (bf16[592,512]{1,0:T(8,128)(2,1)S(1)}, bf16[592,512]{1,0:T(8,128)(2,1)S(1)}, u32[]{:S(2)}, u32[]{:S(2)}) collective-permute-start(bf16[592,512]{1,0:T(8,128)(2,1)S(1)} %get-tuple-element.132), channel_id=1, source_target_pairs={{0,24},{1,25},{2,26},{3,27},{4,28},{5,29},{6,30},{7,31},{8,16},{9,... | collective-permute-start | bytes 1818632 | tf_op jit(solution)/shard_map/ppermute | solution.py:253
  11.2 13.9 %collective-permute-start.1 = (bf16[208,512]{1,0:T(8,128)(2,1)S(1)}, bf16[208,512]{1,0:T(8,128)(2,1)S(1)}, u32[]{:S(2)}, u32[]{:S(2)}) collective-permute-start(bf16[208,512]{1,0:T(8,128)(2,1)S(1)} %get-tuple-element.136), channel_id=1, source_target_pairs={{0,4},{1,5},{2,6},{3,7},{4,0},{5,1},{6,2},{7,3},{8,12},{9,13},{10,... | collective-permute-start | bytes 638984 | tf_op jit(solution)/shard_map/ppermute | solution.py:253
  19.8 7.8 %collective-permute-start.2 = (bf16[208,512]{1,0:T(8,128)(2,1)S(1)}, bf16[208,512]{1,0:T(8,128)(2,1)S(1)}, u32[]{:S(2)}, u32[]{:S(2)}) collective-permute-start(bf16[208,512]{1,0:T(8,128)(2,1)S(1)} %get-tuple-element.137), channel_id=1, source_target_pairs={{0,6},{1,7},{2,4},{3,5},{4,2},{5,3},{6,0},{7,1},{8,14},{9,15},{10,... | collective-permute-start | bytes 638984 | tf_op jit(solution)/shard_map/ppermute | solution.py:253
  25.1 9.2 %collective-permute-start.3 = (bf16[208,512]{1,0:T(8,128)(2,1)S(1)}, bf16[208,512]{1,0:T(8,128)(2,1)S(1)}, u32[]{:S(2)}, u32[]{:S(2)}) collective-permute-start(bf16[208,512]{1,0:T(8,128)(2,1)S(1)} %get-tuple-element.134.refs_0_), channel_id=1, source_target_pairs={{0,1},{1,0},{2,3},{3,2},{4,5},{5,4},{6,7},{7,6},{8,9},{9,8},{10,11... | collective-permute-start | bytes 638984 | tf_op jit(solution)/shard_map/ppermute | solution.py:253
  27.6 6.8 %collective-permute-start.4 = (bf16[208,512]{1,0:T(8,128)(2,1)S(1)}, bf16[208,512]{1,0:T(8,128)(2,1)S(1)}, u32[]{:S(2)}, u32[]{:S(2)}) collective-permute-start(bf16[208,512]{1,0:T(8,128)(2,1)S(1)} %collective-permute-done.refs_1_), channel_id=1, source_target_pairs={{0,1},{1,0},{2,3},{3,2},{4,5},{5,4},{6,7},{7,6},{8,9},{9,8},{10,11... | collective-permute-start | bytes 638984 | tf_op jit(solution)/shard_map/ppermute | solution.py:253
  27.6 6.8 %collective-permute-start.5 = (bf16[208,512]{1,0:T(8,128)(2,1)S(1)}, bf16[208,512]{1,0:T(8,128)(2,1)S(1)}, u32[]{:S(2)}, u32[]{:S(2)}) collective-permute-start(bf16[208,512]{1,0:T(8,128)(2,1)S(1)} %collective-permute-done.1.refs_2_), channel_id=1, source_target_pairs={{0,1},{1,0},{2,3},{3,2},{4,5},{5,4},{6,7},{7,6},{8,9},{9,8},{10,11... | collective-permute-start | bytes 638984 | tf_op jit(solution)/shard_map/ppermute | solution.py:253
  34.3 1.5 collective-permute-start.6
  38.4 10.4 %collective-permute-start.12 = (bf16[64,1536]{1,0:T(8,128)(2,1)S(1)}, bf16[64,1536]{1,0:T(8,128)(2,1)S(1)}, u32[]{:S(2)}, u32[]{:S(2)}) collective-permute-start(bf16[64,1536]{1,0:T(8,128)(2,1)S(1)} %get-tuple-element.144.refs_0_), channel_id=1, source_target_pairs={{0,24},{1,25},{2,26},{3,27},{4,28},{5,29},{6,30},{7,31},{8,16},{9,... | collective-permute-start | bytes 589832 | tf_op jit(solution)/shard_map/ppermute | solution.py:253
  39.9 10.7 %collective-permute-start.10 = (bf16[64,1536]{1,0:T(8,128)(2,1)S(1)}, bf16[64,1536]{1,0:T(8,128)(2,1)S(1)}, u32[]{:S(2)}, u32[]{:S(2)}) collective-permute-start(bf16[64,1536]{1,0:T(8,128)(2,1)S(1)} %get-tuple-element.144.refs_0_), channel_id=1, source_target_pairs={{0,8},{1,9},{2,10},{3,11},{4,12},{5,13},{6,14},{7,15},{8,0},{9,1},... | collective-permute-start | bytes 589832 | tf_op jit(solution)/shard_map/ppermute | solution.py:253
  41.4 9.2 %collective-permute-start.11 = (bf16[64,1536]{1,0:T(8,128)(2,1)S(1)}, bf16[64,1536]{1,0:T(8,128)(2,1)S(1)}, u32[]{:S(2)}, u32[]{:S(2)}) collective-permute-start(bf16[64,1536]{1,0:T(8,128)(2,1)S(1)} %get-tuple-element.144.refs_0_), channel_id=1, source_target_pairs={{0,16},{1,17},{2,18},{3,19},{4,20},{5,21},{6,22},{7,23},{8,24},{9,... | collective-permute-start | bytes 589832 | tf_op jit(solution)/shard_map/ppermute | solution.py:253
  41.9 9.2 %collective-permute-start.13 = (bf16[64,1536]{1,0:T(8,128)(2,1)S(1)}, bf16[64,1536]{1,0:T(8,128)(2,1)S(1)}, u32[]{:S(2)}, u32[]{:S(2)}) collective-permute-start(bf16[64,1536]{1,0:T(8,128)(2,1)S(1)} %get-tuple-element.144.refs_0_), channel_id=1, source_target_pairs={{0,1},{1,0},{2,3},{3,2},{4,5},{5,4},{6,7},{7,6},{8,9},{9,8},{10,11... | collective-permute-start | bytes 589832 | tf_op jit(solution)/shard_map/ppermute | solution.py:253
  48.8 2.3 %collective-permute-start.16 = (bf16[64,1536]{1,0:T(8,128)(2,1)S(1)}, bf16[64,1536]{1,0:T(8,128)(2,1)S(1)}, u32[]{:S(2)}, u32[]{:S(2)}) collective-permute-start(bf16[64,1536]{1,0:T(8,128)(2,1)S(1)} %collective-permute-done.12.refs_3_), channel_id=1, source_target_pairs={{0,1},{1,0},{2,3},{3,2},{4,5},{5,4},{6,7},{7,6},{8,9},{9,8},{10,11... | collective-permute-start | bytes 589832 | tf_op jit(solution)/shard_map/ppermute | solution.py:253
  50.5 1.4 collective-permute-start.14
  50.6 1.7 collective-permute-start.15
  55.4 9.5 %collective-permute-start.19 = (bf16[64,1536]{1,0:T(8,128)(2,1)S(1)}, bf16[64,1536]{1,0:T(8,128)(2,1)S(1)}, u32[]{:S(2)}, u32[]{:S(2)}) collective-permute-start(bf16[64,1536]{1,0:T(8,128)(2,1)S(1)} %get-tuple-element.157.refs_0_), channel_id=1, source_target_pairs={{0,24},{1,25},{2,26},{3,27},{4,28},{5,29},{6,30},{7,31},{8,16},{9,... | collective-permute-start | bytes 589832 | tf_op jit(solution)/shard_map/ppermute | solution.py:253
  56.5 10.7 %collective-permute-start.17 = (bf16[64,1536]{1,0:T(8,128)(2,1)S(1)}, bf16[64,1536]{1,0:T(8,128)(2,1)S(1)}, u32[]{:S(2)}, u32[]{:S(2)}) collective-permute-start(bf16[64,1536]{1,0:T(8,128)(2,1)S(1)} %get-tuple-element.157.refs_0_), channel_id=1, source_target_pairs={{0,8},{1,9},{2,10},{3,11},{4,12},{5,13},{6,14},{7,15},{8,0},{9,1},... | collective-permute-start | bytes 589832 | tf_op jit(solution)/shard_map/ppermute | solution.py:253
  58.1 9.6 %collective-permute-start.18 = (bf16[64,1536]{1,0:T(8,128)(2,1)S(1)}, bf16[64,1536]{1,0:T(8,128)(2,1)S(1)}, u32[]{:S(2)}, u32[]{:S(2)}) collective-permute-start(bf16[64,1536]{1,0:T(8,128)(2,1)S(1)} %get-tuple-element.157.refs_0_), channel_id=1, source_target_pairs={{0,16},{1,17},{2,18},{3,19},{4,20},{5,21},{6,22},{7,23},{8,24},{9,... | collective-permute-start | bytes 589832 | tf_op jit(solution)/shard_map/ppermute | solution.py:253
  58.9 8.8 %collective-permute-start.20 = (bf16[64,1536]{1,0:T(8,128)(2,1)S(1)}, bf16[64,1536]{1,0:T(8,128)(2,1)S(1)}, u32[]{:S(2)}, u32[]{:S(2)}) collective-permute-start(bf16[64,1536]{1,0:T(8,128)(2,1)S(1)} %get-tuple-element.157.refs_0_), channel_id=1, source_target_pairs={{0,1},{1,0},{2,3},{3,2},{4,5},{5,4},{6,7},{7,6},{8,9},{9,8},{10,11... | collective-permute-start | bytes 589832 | tf_op jit(solution)/shard_map/ppermute | solution.py:253
  59.0 16.1 %all-to-all-start = ((bf16[4,192,128]{2,1,0:T(8,128)(2,1)}), bf16[4,192,128]{2,1,0:T(8,128)(2,1)S(1)}, u32[]{:S(2)}, u32[]{:S(2)}) async-start(bf16[4,192,128]{2,1,0:T(8,128)(2,1)} %bitcast.7), calls=%async_computation | async-start | bytes 393216 | tf_op jit(solution)/shard_map/all_to_all | solution.py:1021
  64.9 2.8 %collective-permute-start.23 = (bf16[64,1536]{1,0:T(8,128)(2,1)S(1)}, bf16[64,1536]{1,0:T(8,128)(2,1)S(1)}, u32[]{:S(2)}, u32[]{:S(2)}) collective-permute-start(bf16[64,1536]{1,0:T(8,128)(2,1)S(1)} %collective-permute-done.19.refs_3_), channel_id=1, source_target_pairs={{0,1},{1,0},{2,3},{3,2},{4,5},{5,4},{6,7},{7,6},{8,9},{9,8},{10,11... | collective-permute-start | bytes 589832 | tf_op jit(solution)/shard_map/ppermute | solution.py:253
  67.6 1.4 collective-permute-start.22
  71.5 8.8 %collective-permute-start.26 = (bf16[64,1536]{1,0:T(8,128)(2,1)S(1)}, bf16[64,1536]{1,0:T(8,128)(2,1)S(1)}, u32[]{:S(2)}, u32[]{:S(2)}) collective-permute-start(bf16[64,1536]{1,0:T(8,128)(2,1)S(1)} %get-tuple-element.163.refs_0_), channel_id=1, source_target_pairs={{0,24},{1,25},{2,26},{3,27},{4,28},{5,29},{6,30},{7,31},{8,16},{9,... | collective-permute-start | bytes 589832 | tf_op jit(solution)/shard_map/ppermute | solution.py:253
  72.6 10.7 %collective-permute-start.24 = (bf16[64,1536]{1,0:T(8,128)(2,1)S(1)}, bf16[64,1536]{1,0:T(8,128)(2,1)S(1)}, u32[]{:S(2)}, u32[]{:S(2)}) collective-permute-start(bf16[64,1536]{1,0:T(8,128)(2,1)S(1)} %get-tuple-element.163.refs_0_), channel_id=1, source_target_pairs={{0,8},{1,9},{2,10},{3,11},{4,12},{5,13},{6,14},{7,15},{8,0},{9,1},... | collective-permute-start | bytes 589832 | tf_op jit(solution)/shard_map/ppermute | solution.py:253
  74.1 9.6 %collective-permute-start.25 = (bf16[64,1536]{1,0:T(8,128)(2,1)S(1)}, bf16[64,1536]{1,0:T(8,128)(2,1)S(1)}, u32[]{:S(2)}, u32[]{:S(2)}) collective-permute-start(bf16[64,1536]{1,0:T(8,128)(2,1)S(1)} %get-tuple-element.163.refs_0_), channel_id=1, source_target_pairs={{0,16},{1,17},{2,18},{3,19},{4,20},{5,21},{6,22},{7,23},{8,24},{9,... | collective-permute-start | bytes 589832 | tf_op jit(solution)/shard_map/ppermute | solution.py:253
  75.1 1.7 collective-permute-start.27
  75.2 9.0 %collective-permute-start.28 = (bf16[64,1536]{1,0:T(8,128)(2,1)S(1)}, bf16[64,1536]{1,0:T(8,128)(2,1)S(1)}, u32[]{:S(2)}, u32[]{:S(2)}) collective-permute-start(bf16[64,1536]{1,0:T(8,128)(2,1)S(1)} %get-tuple-element.163.refs_0_), channel_id=1, source_target_pairs={{0,1},{1,0},{2,3},{3,2},{4,5},{5,4},{6,7},{7,6},{8,9},{9,8},{10,11... | collective-permute-start | bytes 589832 | tf_op jit(solution)/shard_map/ppermute | solution.py:253
  80.3 3.9 %collective-permute-start.31 = (bf16[64,1536]{1,0:T(8,128)(2,1)S(1)}, bf16[64,1536]{1,0:T(8,128)(2,1)S(1)}, u32[]{:S(2)}, u32[]{:S(2)}) collective-permute-start(bf16[64,1536]{1,0:T(8,128)(2,1)S(1)} %collective-permute-done.26.refs_3_), channel_id=1, source_target_pairs={{0,1},{1,0},{2,3},{3,2},{4,5},{5,4},{6,7},{7,6},{8,9},{9,8},{10,11... | collective-permute-start | bytes 589832 | tf_op jit(solution)/shard_map/ppermute | solution.py:253
  83.3 1.4 collective-permute-start.29
  83.8 4.3 %collective-permute-start.33 = (bf16[256,640]{1,0:T(8,128)(2,1)S(1)}, bf16[256,640]{1,0:T(8,128)(2,1)S(1)}, u32[]{:S(2)}, u32[]{:S(2)}) collective-permute-start(bf16[256,640]{1,0:T(8,128)(2,1)S(1)} %copy-done.10), channel_id=1, source_target_pairs={{0,1},{1,0},{2,3},{3,2},{4,5},{5,4},{6,7},{7,6},{8,9},{9,8},{10,11... | collective-permute-start | bytes 983048 | tf_op jit(solution)/shard_map/ppermute | solution.py:253
  87.8 1.5 collective-permute-start.32
  93.2 9.5 %collective-permute-start.34 = (bf16[64,1536]{1,0:T(8,128)(2,1)S(1)}, bf16[64,1536]{1,0:T(8,128)(2,1)S(1)}, u32[]{:S(2)}, u32[]{:S(2)}) collective-permute-start(bf16[64,1536]{1,0:T(8,128)(2,1)S(1)} %get-tuple-element.176), channel_id=1, source_target_pairs={{0,8},{1,9},{2,10},{3,11},{4,12},{5,13},{6,14},{7,15},{8,0},{9,1},... | collective-permute-start | bytes 589832 | tf_op jit(solution)/shard_map/ppermute | solution.py:253
  93.8 8.9 %collective-permute-start.35 = (bf16[64,1536]{1,0:T(8,128)(2,1)S(1)}, bf16[64,1536]{1,0:T(8,128)(2,1)S(1)}, u32[]{:S(2)}, u32[]{:S(2)}) collective-permute-start(bf16[64,1536]{1,0:T(8,128)(2,1)S(1)} %get-tuple-element.177), channel_id=1, source_target_pairs={{0,16},{1,17},{2,18},{3,19},{4,20},{5,21},{6,22},{7,23},{8,24},{9,... | collective-permute-start | bytes 589832 | tf_op jit(solution)/shard_map/ppermute | solution.py:253
  94.9 10.1 %collective-permute-start.36 = (bf16[64,1536]{1,0:T(8,128)(2,1)S(1)}, bf16[64,1536]{1,0:T(8,128)(2,1)S(1)}, u32[]{:S(2)}, u32[]{:S(2)}) collective-permute-start(bf16[64,1536]{1,0:T(8,128)(2,1)S(1)} %get-tuple-element.178), channel_id=1, source_target_pairs={{0,24},{1,25},{2,26},{3,27},{4,28},{5,29},{6,30},{7,31},{8,16},{9,... | collective-permute-start | bytes 589832 | tf_op jit(solution)/shard_map/ppermute | solution.py:253
  96.8 8.8 %collective-permute-start.38 = (bf16[256,640]{1,0:T(8,128)(2,1)S(1)}, bf16[256,640]{1,0:T(8,128)(2,1)S(1)}, u32[]{:S(2)}, u32[]{:S(2)}) collective-permute-start(bf16[256,640]{1,0:T(8,128)(2,1)S(1)} %copy-done.9), channel_id=1, source_target_pairs={{0,1},{1,0},{2,3},{3,2},{4,5},{5,4},{6,7},{7,6},{8,9},{9,8},{10,11... | collective-permute-start | bytes 983048 | tf_op jit(solution)/shard_map/ppermute | solution.py:253
  96.8 21.8 %all-to-all-start.1 = ((bf16[4,592,128]{2,1,0:T(8,128)(2,1)}), bf16[4,592,128]{2,1,0:T(8,128)(2,1)S(1)}, u32[]{:S(2)}, u32[]{:S(2)}) async-start(bf16[4,592,128]{2,1,0:T(8,128)(2,1)} %bitcast.36), calls=%async_computation.1 | async-start | bytes 1212416 | tf_op jit(solution)/shard_map/all_to_all | solution.py:1086
  105.5 1.5 collective-permute-start.37
  110.9 13.1 %collective-permute-start.39 = (bf16[64,1536]{1,0:T(8,128)(2,1)S(1)}, bf16[64,1536]{1,0:T(8,128)(2,1)S(1)}, u32[]{:S(2)}, u32[]{:S(2)}) collective-permute-start(bf16[64,1536]{1,0:T(8,128)(2,1)S(1)} %get-tuple-element.191), channel_id=1, source_target_pairs={{0,8},{1,9},{2,10},{3,11},{4,12},{5,13},{6,14},{7,15},{8,0},{9,1},... | collective-permute-start | bytes 589832 | tf_op jit(solution)/shard_map/ppermute | solution.py:253
  112.3 11.8 %collective-permute-start.40 = (bf16[64,1536]{1,0:T(8,128)(2,1)S(1)}, bf16[64,1536]{1,0:T(8,128)(2,1)S(1)}, u32[]{:S(2)}, u32[]{:S(2)}) collective-permute-start(bf16[64,1536]{1,0:T(8,128)(2,1)S(1)} %get-tuple-element.192), channel_id=1, source_target_pairs={{0,16},{1,17},{2,18},{3,19},{4,20},{5,21},{6,22},{7,23},{8,24},{9,... | collective-permute-start | bytes 589832 | tf_op jit(solution)/shard_map/ppermute | solution.py:253
  113.3 10.8 %collective-permute-start.41 = (bf16[64,1536]{1,0:T(8,128)(2,1)S(1)}, bf16[64,1536]{1,0:T(8,128)(2,1)S(1)}, u32[]{:S(2)}, u32[]{:S(2)}) collective-permute-start(bf16[64,1536]{1,0:T(8,128)(2,1)S(1)} %get-tuple-element.193), channel_id=1, source_target_pairs={{0,24},{1,25},{2,26},{3,27},{4,28},{5,29},{6,30},{7,31},{8,16},{9,... | collective-permute-start | bytes 589832 | tf_op jit(solution)/shard_map/ppermute | solution.py:253
  114.5 11.8 %collective-permute-start.43 = (bf16[256,640]{1,0:T(8,128)(2,1)S(1)}, bf16[256,640]{1,0:T(8,128)(2,1)S(1)}, u32[]{:S(2)}, u32[]{:S(2)}) collective-permute-start(bf16[256,640]{1,0:T(8,128)(2,1)S(1)} %copy-done.8), channel_id=1, source_target_pairs={{0,1},{1,0},{2,3},{3,2},{4,5},{5,4},{6,7},{7,6},{8,9},{9,8},{10,11... | collective-permute-start | bytes 983048 | tf_op jit(solution)/shard_map/ppermute | solution.py:253
  118.6 20.3 %all-to-all-start.2 = ((bf16[4,592,128]{2,1,0:T(8,128)(2,1)}), bf16[4,592,128]{2,1,0:T(8,128)(2,1)}, u32[]{:S(2)}, u32[]{:S(2)}) async-start(bf16[4,592,128]{2,1,0:T(8,128)(2,1)} %bitcast.35), calls=%async_computation.2 | async-start | bytes 1212416 | tf_op jit(solution)/shard_map/all_to_all | solution.py:1086
  126.2 1.5 collective-permute-start.42
  131.6 11.9 %collective-permute-start.44 = (bf16[64,1536]{1,0:T(8,128)(2,1)S(1)}, bf16[64,1536]{1,0:T(8,128)(2,1)S(1)}, u32[]{:S(2)}, u32[]{:S(2)}) collective-permute-start(bf16[64,1536]{1,0:T(8,128)(2,1)S(1)} %get-tuple-element.206), channel_id=1, source_target_pairs={{0,8},{1,9},{2,10},{3,11},{4,12},{5,13},{6,14},{7,15},{8,0},{9,1},... | collective-permute-start | bytes 589832 | tf_op jit(solution)/shard_map/ppermute | solution.py:253
  132.2 11.3 %collective-permute-start.45 = (bf16[64,1536]{1,0:T(8,128)(2,1)S(1)}, bf16[64,1536]{1,0:T(8,128)(2,1)S(1)}, u32[]{:S(2)}, u32[]{:S(2)}) collective-permute-start(bf16[64,1536]{1,0:T(8,128)(2,1)S(1)} %get-tuple-element.207), channel_id=1, source_target_pairs={{0,16},{1,17},{2,18},{3,19},{4,20},{5,21},{6,22},{7,23},{8,24},{9,... | collective-permute-start | bytes 589832 | tf_op jit(solution)/shard_map/ppermute | solution.py:253
  133.2 10.3 %collective-permute-start.46 = (bf16[64,1536]{1,0:T(8,128)(2,1)S(1)}, bf16[64,1536]{1,0:T(8,128)(2,1)S(1)}, u32[]{:S(2)}, u32[]{:S(2)}) collective-permute-start(bf16[64,1536]{1,0:T(8,128)(2,1)S(1)} %get-tuple-element.208), channel_id=1, source_target_pairs={{0,24},{1,25},{2,26},{3,27},{4,28},{5,29},{6,30},{7,31},{8,16},{9,... | collective-permute-start | bytes 589832 | tf_op jit(solution)/shard_map/ppermute | solution.py:253
  135.2 9.0 %collective-permute-start.48 = (bf16[256,640]{1,0:T(8,128)(2,1)S(1)}, bf16[256,640]{1,0:T(8,128)(2,1)S(1)}, u32[]{:S(2)}, u32[]{:S(2)}) collective-permute-start(bf16[256,640]{1,0:T(8,128)(2,1)S(1)} %copy-done.7), channel_id=1, source_target_pairs={{0,1},{1,0},{2,3},{3,2},{4,5},{5,4},{6,7},{7,6},{8,9},{9,8},{10,11... | collective-permute-start | bytes 983048 | tf_op jit(solution)/shard_map/ppermute | solution.py:253
  139.0 19.2 %all-to-all-start.3 = ((bf16[4,592,128]{2,1,0:T(8,128)(2,1)}), bf16[4,592,128]{2,1,0:T(8,128)(2,1)S(1)}, u32[]{:S(2)}, u32[]{:S(2)}) async-start(bf16[4,592,128]{2,1,0:T(8,128)(2,1)} %bitcast.34), calls=%async_computation.3 | async-start | bytes 1212416 | tf_op jit(solution)/shard_map/all_to_all | solution.py:1086
  144.1 1.5 collective-permute-start.47
  149.4 12.2 %collective-permute-start.56 = (bf16[64,1536]{1,0:T(8,128)(2,1)S(1)}, bf16[64,1536]{1,0:T(8,128)(2,1)S(1)}, u32[]{:S(2)}, u32[]{:S(2)}) collective-permute-start(bf16[64,1536]{1,0:T(8,128)(2,1)S(1)} %get-tuple-element.235), channel_id=1, source_target_pairs={{0,8},{1,9},{2,10},{3,11},{4,12},{5,13},{6,14},{7,15},{8,0},{9,1},... | collective-permute-start | bytes 589832 | tf_op jit(solution)/shard_map/ppermute | solution.py:253
  150.5 11.1 %collective-permute-start.57 = (bf16[64,1536]{1,0:T(8,128)(2,1)S(1)}, bf16[64,1536]{1,0:T(8,128)(2,1)S(1)}, u32[]{:S(2)}, u32[]{:S(2)}) collective-permute-start(bf16[64,1536]{1,0:T(8,128)(2,1)S(1)} %get-tuple-element.236), channel_id=1, source_target_pairs={{0,16},{1,17},{2,18},{3,19},{4,20},{5,21},{6,22},{7,23},{8,24},{9,... | collective-permute-start | bytes 589832 | tf_op jit(solution)/shard_map/ppermute | solution.py:253
  151.6 10.1 %collective-permute-start.58 = (bf16[64,1536]{1,0:T(8,128)(2,1)S(1)}, bf16[64,1536]{1,0:T(8,128)(2,1)S(1)}, u32[]{:S(2)}, u32[]{:S(2)}) collective-permute-start(bf16[64,1536]{1,0:T(8,128)(2,1)S(1)} %get-tuple-element.237), channel_id=1, source_target_pairs={{0,24},{1,25},{2,26},{3,27},{4,28},{5,29},{6,30},{7,31},{8,16},{9,... | collective-permute-start | bytes 589832 | tf_op jit(solution)/shard_map/ppermute | solution.py:253
  158.1 23.4 %all-to-all-start.4 = ((bf16[4,592,128]{2,1,0:T(8,128)(2,1)}), bf16[4,592,128]{2,1,0:T(8,128)(2,1)S(1)}, u32[]{:S(2)}, u32[]{:S(2)}) async-start(bf16[4,592,128]{2,1,0:T(8,128)(2,1)} %bitcast.37), calls=%async_computation.4 | async-start | bytes 1212416 | tf_op jit(solution)/shard_map/all_to_all | solution.py:1086
  162.7 1.5 collective-permute-start.59
  164.2 21.2 %collective-permute-start.60 = (bf16[256,384]{1,0:T(8,128)(2,1)S(1)}, bf16[256,384]{1,0:T(8,128)(2,1)S(1)}, u32[]{:S(2)}, u32[]{:S(2)}) collective-permute-start(bf16[256,384]{1,0:T(8,128)(2,1)S(1)} %get-tuple-element.244), channel_id=1, source_target_pairs={{0,0},{1,5},{2,8},{3,13},{4,16},{5,21},{6,24},{7,29},{8,2},{9,7},{... | collective-permute-start | bytes 589832 | tf_op jit(solution)/shard_map/ppermute | solution.py:253
  164.9 20.5 %collective-permute-start.61 = (bf16[256,384]{1,0:T(8,128)(2,1)S(1)}, bf16[256,384]{1,0:T(8,128)(2,1)S(1)}, u32[]{:S(2)}, u32[]{:S(2)}) collective-permute-start(bf16[256,384]{1,0:T(8,128)(2,1)S(1)} %get-tuple-element.245), channel_id=1, source_target_pairs={{0,2},{1,7},{2,10},{3,15},{4,18},{5,23},{6,26},{7,31},{8,0},{9,5},... | collective-permute-start | bytes 589832 | tf_op jit(solution)/shard_map/ppermute | solution.py:253
  181.8 7.3 %collective-permute-start.49 = (bf16[592,128]{1,0:T(8,128)(2,1)S(1)}, bf16[592,128]{1,0:T(8,128)(2,1)S(1)}, u32[]{:S(2)}, u32[]{:S(2)}) collective-permute-start(bf16[592,128]{1,0:T(8,128)(2,1)S(1)} %get-tuple-element.231), channel_id=1, source_target_pairs={{0,8},{1,9},{2,10},{3,11},{4,12},{5,13},{6,14},{7,15},{8,0},{9,1},... | collective-permute-start | bytes 454664 | tf_op jit(solution)/shard_map/ppermute | solution.py:253
  183.3 7.9 %collective-permute-start.50 = (bf16[592,128]{1,0:T(8,128)(2,1)S(1)}, bf16[592,128]{1,0:T(8,128)(2,1)S(1)}, u32[]{:S(2)}, u32[]{:S(2)}) collective-permute-start(bf16[592,128]{1,0:T(8,128)(2,1)S(1)} %get-tuple-element.232), channel_id=1, source_target_pairs={{0,16},{1,17},{2,18},{3,19},{4,20},{5,21},{6,22},{7,23},{8,24},{9,... | collective-permute-start | bytes 454664 | tf_op jit(solution)/shard_map/ppermute | solution.py:253
  184.4 7.1 %collective-permute-start.51 = (bf16[592,128]{1,0:T(8,128)(2,1)S(1)}, bf16[592,128]{1,0:T(8,128)(2,1)S(1)}, u32[]{:S(2)}, u32[]{:S(2)}) collective-permute-start(bf16[592,128]{1,0:T(8,128)(2,1)S(1)} %get-tuple-element.233), channel_id=1, source_target_pairs={{0,24},{1,25},{2,26},{3,27},{4,28},{5,29},{6,30},{7,31},{8,16},{9,... | collective-permute-start | bytes 454664 | tf_op jit(solution)/shard_map/ppermute | solution.py:253
  185.4 6.4 %collective-permute-start.52 = (bf16[592,128]{1,0:T(8,128)(2,1)S(1)}, bf16[592,128]{1,0:T(8,128)(2,1)S(1)}, u32[]{:S(2)}, u32[]{:S(2)}) collective-permute-start(bf16[592,128]{1,0:T(8,128)(2,1)S(1)} %get-tuple-element.230.refs_0_), channel_id=1, source_target_pairs={{0,1},{1,0},{2,3},{3,2},{4,5},{5,4},{6,7},{7,6},{8,9},{9,8},{10,11... | collective-permute-start | bytes 454664 | tf_op jit(solution)/shard_map/ppermute | solution.py:253
  185.4 6.7 %collective-permute-start.62 = (bf16[256,384]{1,0:T(8,128)(2,1)S(1)}, bf16[256,384]{1,0:T(8,128)(2,1)S(1)}, u32[]{:S(2)}, u32[]{:S(2)}) collective-permute-start(bf16[256,384]{1,0:T(8,128)(2,1)S(1)} %collective-permute-done.60.refs_9_), channel_id=1, source_target_pairs={{0,1},{1,0},{2,3},{3,2},{4,5},{5,4},{6,7},{7,6},{8,9},{9,8},{10,11... | collective-permute-start | bytes 589832 | tf_op jit(solution)/shard_map/ppermute | solution.py:253
  189.1 3.1 %collective-permute-start.63 = (bf16[256,384]{1,0:T(8,128)(2,1)S(1)}, bf16[256,384]{1,0:T(8,128)(2,1)S(1)}, u32[]{:S(2)}, u32[]{:S(2)}) collective-permute-start(bf16[256,384]{1,0:T(8,128)(2,1)S(1)} %collective-permute-done.61.refs_10_), channel_id=1, source_target_pairs={{0,1},{1,0},{2,3},{3,2},{4,5},{5,4},{6,7},{7,6},{8,9},{9,8},{10,11... | collective-permute-start | bytes 589832 | tf_op jit(solution)/shard_map/ppermute | solution.py:253
  (16 other events, 137.2 us)

commit v7 on v6

--- a/solution.py
+++ b/solution.py
@@ -10,7 +10,7 @@
 from jax.sharding import PartitionSpec as P
 
 CONVS = 2
-BACK_FLOPS = (6 * 10**9, 6 * 10**9, 6 * 10**9, 0)
+BACK_FLOPS = (6 * 10**9, 52 * 10**8, 52 * 10**8, 0)
 PICK_FLOPS = 2 * 10**9
 COT_LAYER = 2
 INPUT_FLOPS = 4000000000
@@ -645,15 +645,14 @@
     grad_pre[...], shift_sum, slope_sum = norm_back(
         cot_in[...].astype(jnp.float32), normed, scale, gain, bias, inside_now, facts_now, cols, pooling
     )
-    keep_sums(sums, shift_sum, slope_sum)
+    sums[...] = with_sums(layer, shift_sum, slope_sum, 0.0)
     full_copy.wait()
     hidden_copy.wait()
 
 
-def keep_sums(sums, shift_sum, slope_sum):
-    ch = shift_sum.shape[0]
-    sums[:, :LANES] = jnp.broadcast_to(shift_sum, (ch, LANES))
-    sums[:, LANES:] = jnp.broadcast_to(slope_sum, (ch, LANES))
+def with_sums(layer, shift_sum, slope_sum, others):
+    at = lax.broadcasted_iota(jnp.int32, (shift_sum.shape[0], LANES), 1)
+    return jnp.where(at == 2 * layer, shift_sum, jnp.where(at == 2 * layer + 1, slope_sum, others))
 
 
 def add_blocks(blocks):
@@ -672,8 +671,8 @@
     copy.wait()
 
 
-def norm_back_kernel(dims, pooling, *refs):
-    blocks, (kept, meta, inside, facts, grad_pre, sums) = refs[:4], refs[4:]
+def norm_back_kernel(dims, layer, pooling, *refs):
+    blocks, (kept, meta, inside, facts, sums_in, grad_pre, sums) = refs[:4], refs[4:]
     ch, length = grad_pre.shape
     grad = add_blocks(blocks).astype(jnp.bfloat16).astype(jnp.float32)
     gain, bias = affine(meta[...], ch)
@@ -688,7 +687,7 @@
         dims[1],
         pooling,
     )
-    keep_sums(sums, shift_sum, slope_sum)
+    sums[...] = with_sums(layer, shift_sum, slope_sum, sums_in[...])
 
 
 def weight_product(moved, full, first):
@@ -697,32 +696,25 @@
     return lax.dot_general(moved, full, NT, preferred_element_type=jnp.float32)
 
 
-def sums_rows(sums, ch, width):
-    lines = []
-    for at in (0, LANES):
-        turned = sums[:, at : at + LANES].T
-        lines.append(jnp.concatenate([turned, jnp.zeros((LANES, width - ch), jnp.float32)], axis=1)[0:1])
-    lines.append(jnp.zeros((META_ROWS - 2, width), jnp.float32))
-    return jnp.concatenate(lines, axis=0).astype(jnp.bfloat16)
-
-
-def store_share(value, sums, pieces):
-    rows = value.shape[0]
-    width = pieces[0].shape[1]
-    below = sums_rows(sums, rows // TAPS, width)
-    for n, piece in enumerate(pieces):
-        piece[:rows, :] = value[:, n * width : (n + 1) * width].astype(jnp.bfloat16)
-        piece[rows:, :] = below
+def sums_rows(sums, width):
+    ch = sums.shape[0]
+    turned = jnp.concatenate([sums[...].T, jnp.zeros((LANES, width - ch), jnp.float32)], axis=1)
+    return turned[:META_ROWS].astype(jnp.bfloat16)
 
 
 def form_share(layer, moved, full, sums, product):
     piece = product.shape[0] // 4
-    value = weight_product(moved[: piece - META_ROWS, :], full[...], layer == 0)
-    store_share(value, sums, [product.at[pl.ds(n * piece, piece)] for n in range(4)])
-
-
-def conv_back_kernel(dims, layer, own, other, own_weights, other_weights, full_in, sums, facts, *refs):
-    *outs, share, product, full, moved, weights, sems = refs
+    rows = piece - META_ROWS * len(sums)
+    width = product.shape[1]
+    value = weight_product(moved[:rows, :], full[...], layer == 0)
+    for n in range(4):
+        product[n * piece : n * piece + rows, :] = value[:, n * width : (n + 1) * width].astype(jnp.bfloat16)
+        for ref in sums:
+            product[n * piece + rows : (n + 1) * piece, :] = sums_rows(ref, width)
+
+
+def conv_back_kernel(dims, layer, own, other, own_weights, other_weights, full_in, facts, *refs):
+    sums, outs, (share, product, full, moved, weights, sems) = refs[:-10], refs[-10:-6], refs[-6:]
     ch = own.shape[0]
     size = moved.shape[0] // 2
     rows = pl.ds(layer * 4 * ch, 4 * ch)
@@ -781,7 +773,8 @@
 
             @pl.when((section ^ k) == layer)
             def _():
-                out[...] = other[...]
+                out[: other.shape[0], :] = other[...]
+                out[other.shape[0] :, :] = value[other.shape[0] :, :]
 
 
 def turn_weights_kernel(layers, *refs):
@@ -859,10 +852,11 @@
     slope_row = jnp.zeros((1, rows), jnp.float32)
     slot = plane * 2 + core
     for (k, j), block in zip(peer_order(), blocks):
-        tail = block[taps * rows :, :].astype(jnp.float32)
+        tail = block[taps * rows :, :rows].astype(jnp.float32)
+        at = lax.broadcasted_iota(jnp.int32, tail.shape, 0)
         mine = slice_at(section, core, k, j) == slot
-        shift_row = shift_row + jnp.where(mine, tail[0:1, :rows], 0.0)
-        slope_row = slope_row + jnp.where(mine, tail[1:2, :rows], 0.0)
+        shift_row = shift_row + jnp.sum(jnp.where(mine & (at == 2 * section), tail, 0.0), axis=0, keepdims=True)
+        slope_row = slope_row + jnp.sum(jnp.where(mine & (at == 2 * section + 1), tail, 0.0), axis=0, keepdims=True)
     shift_out[...] = shift_row
     slope_out[...] = slope_row
 
@@ -920,10 +914,9 @@
     tap_scratch = ((TAPS * ch, length), f32)
     weight_slice = ((slice_rows, channels), bf16)
     map_out = ((ch, length), bf16)
-    sums_out = ((ch, 2 * LANES), f32)
+    sums_out = ((ch, LANES), f32)
     kept_out = ((ch, length + LANES), f32)
-    share_out = ((4 * slice_rows, 2 * ch), bf16)
-    share_piece = ((slice_rows, 2 * ch), bf16)
+    piece_rows = [slice_rows] + [TAPS * ch] * last
 
     taps_first = conv_weight[0].transpose(1, 2, 0, 3).reshape(TAPS, channels, channels)
     packed = call(
@@ -1063,6 +1056,7 @@
 
     shares = [None] * layers
     for layer in range(last, -1, -1):
+        share_out = ((4 * piece_rows[layer], 2 * ch), bf16)
         *parts, share = call(
             partial(conv_back_kernel, dims, layer),
             [map_out] * 4 + [share_out],
@@ -1072,12 +1066,13 @@
                 ((2 * tap_rows, length), bf16),
                 ((4 * ch, 2 * tap_rows), bf16),
             ],
-            [grad_pre, to_core(grad_pre), turned, crossing[layer], fulls[layer], sums, facts],
+            [grad_pre, to_core(grad_pre), turned, crossing[layer], fulls[layer], facts]
+            + ([] if layer else [sums]),
             "conv_back",
             held=(2, 4),
             free=(3,),
             held_outs=(4,),
-            loose=(5, 6),
+            loose=(5,) if layer else (5, 6),
             flops=BACK_FLOPS[layer],
             copies=4,
         )
@@ -1097,12 +1092,12 @@
             )
             blocks = spread(parts, to_section, held)
             grad_pre, sums = call(
-                partial(norm_back_kernel, dims, layer - 1 == CONVS - 1),
+                partial(norm_back_kernel, dims, layer - 1, layer - 1 == CONVS - 1),
                 [map_out, sums_out],
                 [],
-                [*blocks, *held, inside, facts],
+                [*blocks, *held, inside, facts, sums],
                 "norm_back",
-                loose=(6, 7),
+                loose=(6, 7, 8),
             )
     blocks = spread(parts, to_section)
     keep, give = call(
@@ -1120,8 +1115,8 @@
     maps = [send(x, lambda s, z, c, n=n: (z, s ^ (2 * c + n), c)) for n, x in enumerate(maps)]
     folded = call(
         fold_kernel,
-        [share_piece] * last,
-        [((last, 4 * slice_rows, 2 * ch), bf16)],
+        [((rows, 2 * ch), bf16) for rows in piece_rows[1:]],
+        [((last, 4 * TAPS * ch, 2 * ch), bf16)],
         shares[1:],
         "fold",
         held=range(last),
@@ -1129,7 +1124,7 @@
     )
     chosen = call(
         choose_kernel,
-        [share_piece] * 4,
+        [((slice_rows, 2 * ch), bf16)] * 4,
         [],
         [shares[0], *folded],
         "choose",

time: 196 us -> 195 us (level)
  transfers between devices with their start and end apart: 69 -> 69, of which waited for: 33 -> 35; matrix products, arithmetic and copies ran while one was open for 0% -> 0% of each run, Pallas kernels for 19% -> 19%
where the time goes in v7:
time: 195 us; the launch traced here: 194 us
  waiting for transfers between devices  72 us (37%)
  starting transfers between devices  70.1 us (36%)
  Pallas kernels  50.2 us (26%)
    pallas_call x27, Pallas kernels, call(): pl.pallas_call(kernel, out_shape=shapes, in_specs=[pl.BlockSpec(memory_sp...  50.2 us
    ppermute x64, starting transfers between devices, send(): return lax.ppermute(x, AXES, pairs)  49.1 us
    ppermute x64, waiting for transfers between devices, send(): return lax.ppermute(x, AXES, pairs)  48.9 us
    all_to_all x4, waiting for transfers between devices, plane_shards(): lax.all_to_all(share, 'dp', 0, 0, tiled=True, axis_index_groups=same_core)  23.1 us
    all_to_all x4, starting transfers between devices, plane_shards(): lax.all_to_all(share, 'dp', 0, 0, tiled=True, axis_index_groups=same_core)  16.2 us
    all_to_all x1, starting transfers between devices, plane_shards(): lax.all_to_all(cot_slots, 'dp', 0, 0, tiled=True, axis_index_groups=same_...  4.87 us
  transfers between devices with their start and end apart: 69, of which 35 were waited for; matrix products, arithmetic and copies ran while one was open for 0% of the time, Pallas kernels for 19%

profile of v7, /device:TPU:0, one launch (start us, length us, event | category | flops | bytes accessed | tf_op | source)
XLA Modules:
  0.0 193.8 jit_solution(13909595592777417657)
XLA Ops:
  0.6 2.5 %weight_pack.1 = (bf16[592,512]{1,0:T(8,128)(2,1)S(1)}, bf16[592,512]{1,0:T(8,128)(2,1)S(1)}, bf16[592,512]{1,0:T(8,128)(2,1)S(1)}, bf16[592,512]{1,0:T(8,128)(2,1)S(1)}) custom-call(f32[1,512]{1,0:T(1,128)} %gain.1, f32[1,512]{1,0:T(1,128)} %bias.1, bf16[9,512,512]{2,1,0:T(8,128)(2,1)} %bitcast.29), custom_call_target="tpu_custom_call" | custom-call | bytes 7147520 | tf_op jit(solution)/shard_map/weight_pack/pallas_call | solution.py:884
  3.1 3.0 %collective-permute-start.7 = (bf16[592,512]{1,0:T(8,128)(2,1)S(1)}, bf16[592,512]{1,0:T(8,128)(2,1)S(1)}, u32[]{:S(2)}, u32[]{:S(2)}) collective-permute-start(bf16[592,512]{1,0:T(8,128)(2,1)S(1)} %get-tuple-element.130), channel_id=1, source_target_pairs={{0,8},{1,9},{2,10},{3,11},{4,12},{5,13},{6,14},{7,15},{8,0},{9,1},... | collective-permute-start | bytes 1818632 | tf_op jit(solution)/shard_map/ppermute | solution.py:253
  6.2 1.5 collective-permute-start.8
  7.7 1.4 frames.1
  9.1 1.6 collective-permute-start
  11.2 2.6 %collective-permute-start.1 = (bf16[208,512]{1,0:T(8,128)(2,1)S(1)}, bf16[208,512]{1,0:T(8,128)(2,1)S(1)}, u32[]{:S(2)}, u32[]{:S(2)}) collective-permute-start(bf16[208,512]{1,0:T(8,128)(2,1)S(1)} %get-tuple-element.136), channel_id=1, source_target_pairs={{0,4},{1,5},{2,6},{3,7},{4,0},{5,1},{6,2},{7,3},{8,12},{9,13},{10,... | collective-permute-start | bytes 638984 | tf_op jit(solution)/shard_map/ppermute | solution.py:253
  13.8 6.1 %collective-permute-done.refs_1_ = bf16[208,512]{1,0:T(8,128)(2,1)S(1)} collective-permute-done((bf16[208,512]{1,0:T(8,128)(2,1)S(1)}, bf16[208,512]{1,0:T(8,128)(2,1)S(1)}, u32[]{:S(2)}, u32[]{:S(2)}) %collective-permute-start) | collective-permute-done | bytes 213024 | tf_op jit(solution)/shard_map/ppermute | solution.py:253
  19.8 2.5 %collective-permute-start.2 = (bf16[208,512]{1,0:T(8,128)(2,1)S(1)}, bf16[208,512]{1,0:T(8,128)(2,1)S(1)}, u32[]{:S(2)}, u32[]{:S(2)}) collective-permute-start(bf16[208,512]{1,0:T(8,128)(2,1)S(1)} %get-tuple-element.137), channel_id=1, source_target_pairs={{0,6},{1,7},{2,4},{3,5},{4,2},{5,3},{6,0},{7,1},{8,14},{9,15},{10,... | collective-permute-start | bytes 638984 | tf_op jit(solution)/shard_map/ppermute | solution.py:253
  22.3 2.8 %collective-permute-done.1.refs_2_ = bf16[208,512]{1,0:T(8,128)(2,1)S(1)} collective-permute-done((bf16[208,512]{1,0:T(8,128)(2,1)S(1)}, bf16[208,512]{1,0:T(8,128)(2,1)S(1)}, u32[]{:S(2)}, u32[]{:S(2)}) %collective-permute-start.1) | collective-permute-done | bytes 213024 | tf_op jit(solution)/shard_map/ppermute | solution.py:253
  25.1 2.5 %collective-permute-done.2.refs_3_ = bf16[208,512]{1,0:T(8,128)(2,1)S(1)} collective-permute-done((bf16[208,512]{1,0:T(8,128)(2,1)S(1)}, bf16[208,512]{1,0:T(8,128)(2,1)S(1)}, u32[]{:S(2)}, u32[]{:S(2)}) %collective-permute-start.2) | collective-permute-done | bytes 213024 | tf_op jit(solution)/shard_map/ppermute | solution.py:253
  28.1 6.2 %collective-permute-done.8.refs_10_.refs_2_ = bf16[592,512]{1,0:T(8,128)(2,1)S(1)} collective-permute-done((bf16[592,512]{1,0:T(8,128)(2,1)S(1)}, bf16[592,512]{1,0:T(8,128)(2,1)S(1)}, u32[]{:S(2)}, u32[]{:S(2)}) %collective-permute-start.8) | collective-permute-done | bytes 606240 | tf_op jit(solution)/shard_map/ppermute | solution.py:253
  34.4 1.4 collective-permute-done.6.refs_7_
  35.8 2.5 %forward.3 = (bf16[64,1536]{1,0:T(8,128)(2,1)S(1)}, f32[64,1664]{1,0:T(8,128)}, bf16[1536,512]{1,0:T(8,128)(2,1)}, f32[1,1536]{1,0:T(1,128)S(1)}) custom-call(bf16[208,512]{1,0:T(8,128)(2,1)S(1)} %get-tuple-element.134.refs_0_, bf16[208,512]{1,0:T(8,128)(2,1)S(1)} %collective-permute-done.refs_1_, bf16[208,512]{1,0:T(8,128)(2,1)S(1)} %collective-permute-done.1.refs_2_, ...), custom_call_target="tpu_custom_call" | custom-call | flops 905969664 | bytes 6428672 | tf_op jit(solution)/shard_map/forward/pallas_call | solution.py:884
  38.3 1.5 collective-permute-start.12
  39.9 1.5 collective-permute-start.10
  41.9 2.0 %cot_slices.1 = bf16[768,128]{1,0:T(8,128)(2,1)} custom-call(bf16[4,192,512]{2,1,0:T(8,128)(2,1)} %bitcast.33), custom_call_target="tpu_custom_call" | custom-call | bytes 983040 | tf_op jit(solution)/shard_map/cot_slices/pallas_call | solution.py:884
  43.9 3.7 %turn_weights.1 = (bf16[1024,640]{1,0:T(8,128)(2,1)}, bf16[256,640]{1,0:T(8,128)(2,1)}, bf16[256,640]{1,0:T(8,128)(2,1)}, bf16[256,640]{1,0:T(8,128)(2,1)}, bf16[256,640]{1,0:T(8,128)(2,1)}) custom-call(bf16[592,512]{1,0:T(8,128)(2,1)} %copy-done, bf16[592,512]{1,0:T(8,128)(2,1)} %copy-done.1, bf16[592,512]{1,0:T(8,128)(2,1)} %copy-done.2, ...), custom_call_target="tpu_custom_call" | custom-call | bytes 5046272 | tf_op jit(solution)/shard_map/turn_weights/pallas_call | solution.py:884
  47.7 1.1 pick.3.refs_8_
  49.3 1.2 collective-permute-done.10.refs_1_
  52.3 3.1 %forward.4 = (bf16[64,1536]{1,0:T(8,128)(2,1)S(1)}, f32[64,1664]{1,0:T(8,128)}, bf16[512,1536]{1,0:T(8,128)(2,1)}) custom-call(bf16[64,1536]{1,0:T(8,128)(2,1)S(1)} %get-tuple-element.144.refs_0_, bf16[64,1536]{1,0:T(8,128)(2,1)S(1)} %collective-permute-done.10.refs_1_, bf16[64,1536]{1,0:T(8,128)(2,1)S(1)} %collective-permute-done.11.refs_2_, ...), custom_call_target="tpu_custom_call" | custom-call | flops 905969664 | bytes 4478976 | tf_op jit(solution)/shard_map/forward/pallas_call | solution.py:884
  55.4 1.2 collective-permute-start.19
  56.5 1.5 collective-permute-start.17
  58.9 4.9 %all-to-all-start = ((bf16[4,192,128]{2,1,0:T(8,128)(2,1)}), bf16[4,192,128]{2,1,0:T(8,128)(2,1)S(1)}, u32[]{:S(2)}, u32[]{:S(2)}) async-start(bf16[4,192,128]{2,1,0:T(8,128)(2,1)} %bitcast.7), calls=%async_computation | async-start | bytes 393216 | tf_op jit(solution)/shard_map/all_to_all | solution.py:1014
  63.8 1.1 pick.4.refs_8_
  65.2 2.0 %collective-permute-done.17.refs_1_ = bf16[64,1536]{1,0:T(8,128)(2,1)S(1)} collective-permute-done((bf16[64,1536]{1,0:T(8,128)(2,1)S(1)}, bf16[64,1536]{1,0:T(8,128)(2,1)S(1)}, u32[]{:S(2)}, u32[]{:S(2)}) %collective-permute-start.17) | collective-permute-done | bytes 196640 | tf_op jit(solution)/shard_map/ppermute | solution.py:253
  69.0 2.5 %forward.5 = (bf16[64,1536]{1,0:T(8,128)(2,1)S(1)}, f32[64,1664]{1,0:T(8,128)}, bf16[512,1536]{1,0:T(8,128)(2,1)}) custom-call(bf16[64,1536]{1,0:T(8,128)(2,1)S(1)} %get-tuple-element.157.refs_0_, bf16[64,1536]{1,0:T(8,128)(2,1)S(1)} %collective-permute-done.17.refs_1_, bf16[64,1536]{1,0:T(8,128)(2,1)S(1)} %collective-permute-done.18.refs_2_, ...), custom_call_target="tpu_custom_call" | custom-call | flops 905969664 | bytes 4478976 | tf_op jit(solution)/shard_map/forward/pallas_call | solution.py:884
  71.5 1.1 collective-permute-start.26
  72.6 1.5 collective-permute-start.24
  75.7 1.1 pick.5.refs_8_
  77.1 3.1 %collective-permute-done.26.refs_3_ = bf16[64,1536]{1,0:T(8,128)(2,1)S(1)} collective-permute-done((bf16[64,1536]{1,0:T(8,128)(2,1)S(1)}, bf16[64,1536]{1,0:T(8,128)(2,1)S(1)}, u32[]{:S(2)}, u32[]{:S(2)}) %collective-permute-start.26) | collective-permute-done | bytes 196640 | tf_op jit(solution)/shard_map/ppermute | solution.py:253
  80.3 3.0 %collective-permute-done.24.refs_1_ = bf16[64,1536]{1,0:T(8,128)(2,1)S(1)} collective-permute-done((bf16[64,1536]{1,0:T(8,128)(2,1)S(1)}, bf16[64,1536]{1,0:T(8,128)(2,1)S(1)}, u32[]{:S(2)}, u32[]{:S(2)}) %collective-permute-start.24) | collective-permute-done | bytes 196640 | tf_op jit(solution)/shard_map/ppermute | solution.py:253
  85.1 2.5 %turn.1 = (bf16[64,1536]{1,0:T(8,128)(2,1)}, bf16[512,1536]{1,0:T(8,128)(2,1)}, bf16[64,1536]{1,0:T(8,128)(2,1)S(1)}, f32[64,128]{1,0:T(8,128)S(1)}) custom-call(bf16[64,1536]{1,0:T(8,128)(2,1)S(1)} %get-tuple-element.163.refs_0_, bf16[64,1536]{1,0:T(8,128)(2,1)S(1)} %collective-permute-done.24.refs_1_, ...), custom_call_target="tpu_custom_call" | custom-call | flops 905969664 | bytes 4478976 | tf_op jit(solution)/shard_map/turn/pallas_call | solution.py:884
  87.8 1.3 collective-permute-done.32.other
  89.1 3.9 %conv_back.4 = (bf16[64,1536]{1,0:T(8,128)(2,1)S(1)}, bf16[64,1536]{1,0:T(8,128)(2,1)S(1)}, bf16[64,1536]{1,0:T(8,128)(2,1)S(1)}, bf16[64,1536]{1,0:T(8,128)(2,1)S(1)}, bf16[2304,128]{1,0:T(8,128)(2,1)}) custom-call(bf16[64,1536]{1,0:T(8,128)(2,1)S(1)} %get-tuple-element.171.own, bf16[64,1536]{1,0:T(8,128)(2,1)S(1)} %collective-permute-done.32.other, ...), custom_call_target="tpu_custom_call" | custom-call | bytes 5079040 | tf_op jit(solution)/shard_map/conv_back/pallas_call | solution.py:884
  94.7 1.9 collective-permute-start.36
  96.6 4.9 %all-to-all-start.1 = ((bf16[4,576,128]{2,1,0:T(8,128)(2,1)}), bf16[4,576,128]{2,1,0:T(8,128)(2,1)S(1)}, u32[]{:S(2)}, u32[]{:S(2)}) async-start(bf16[4,576,128]{2,1,0:T(8,128)(2,1)} %bitcast.37), calls=%async_computation.1 | async-start | bytes 1179648 | tf_op jit(solution)/shard_map/all_to_all | solution.py:1081
  102.5 2.2 %collective-permute-done.36.refs_3_ = bf16[64,1536]{1,0:T(8,128)(2,1)S(1)} collective-permute-done((bf16[64,1536]{1,0:T(8,128)(2,1)S(1)}, bf16[64,1536]{1,0:T(8,128)(2,1)S(1)}, u32[]{:S(2)}, u32[]{:S(2)}) %collective-permute-start.36) | collective-permute-done | bytes 196640 | tf_op jit(solution)/shard_map/ppermute | solution.py:253
  105.4 1.4 collective-permute-done.37.other
  106.8 3.9 %conv_back.5 = (bf16[64,1536]{1,0:T(8,128)(2,1)S(1)}, bf16[64,1536]{1,0:T(8,128)(2,1)S(1)}, bf16[64,1536]{1,0:T(8,128)(2,1)S(1)}, bf16[64,1536]{1,0:T(8,128)(2,1)S(1)}, bf16[2304,128]{1,0:T(8,128)(2,1)}) custom-call(bf16[64,1536]{1,0:T(8,128)(2,1)S(1)} %get-tuple-element.186.own, bf16[64,1536]{1,0:T(8,128)(2,1)S(1)} %collective-permute-done.37.other, ...), custom_call_target="tpu_custom_call" | custom-call | flops 5200000000 | bytes 5079040 | tf_op jit(solution)/shard_map/conv_back/pallas_call | solution.py:884
  110.7 1.3 collective-permute-start.39
  113.1 1.2 collective-permute-start.41
  114.3 3.8 %all-to-all-done.1 = bf16[4,576,128]{2,1,0:T(8,128)(2,1)S(1)} async-done(((bf16[4,576,128]{2,1,0:T(8,128)(2,1)}), bf16[4,576,128]{2,1,0:T(8,128)(2,1)S(1)}, u32[]{:S(2)}, u32[]{:S(2)}) %all-to-all-start.1) | async-done | bytes 589856 | tf_op jit(solution)/shard_map/all_to_all | solution.py:1081
  118.1 4.4 %all-to-all-start.2 = ((bf16[4,576,128]{2,1,0:T(8,128)(2,1)}), bf16[4,576,128]{2,1,0:T(8,128)(2,1)}, u32[]{:S(2)}, u32[]{:S(2)}) async-start(bf16[4,576,128]{2,1,0:T(8,128)(2,1)} %bitcast.36), calls=%async_computation.2 | async-start | bytes 1179648 | tf_op jit(solution)/shard_map/all_to_all | solution.py:1081
  123.5 2.1 %norm_back.4 = (bf16[64,1536]{1,0:T(8,128)(2,1)S(1)}, f32[64,128]{1,0:T(8,128)S(1)}) custom-call(bf16[64,1536]{1,0:T(8,128)(2,1)S(1)} %get-tuple-element.189.refs_0_, bf16[64,1536]{1,0:T(8,128)(2,1)S(1)} %collective-permute-done.39.refs_1_, bf16[64,1536]{1,0:T(8,128)(2,1)S(1)} %collective-permute-done.40.refs_2_, ...), custom_call_target="tpu_custom_call" | custom-call | bytes 1595392 | tf_op jit(solution)/shard_map/norm_back/pallas_call | solution.py:884
  125.7 1.4 collective-permute-done.42.other
  127.1 3.9 %conv_back.6 = (bf16[64,1536]{1,0:T(8,128)(2,1)S(1)}, bf16[64,1536]{1,0:T(8,128)(2,1)S(1)}, bf16[64,1536]{1,0:T(8,128)(2,1)S(1)}, bf16[64,1536]{1,0:T(8,128)(2,1)S(1)}, bf16[2304,128]{1,0:T(8,128)(2,1)}) custom-call(bf16[64,1536]{1,0:T(8,128)(2,1)S(1)} %get-tuple-element.201.own, bf16[64,1536]{1,0:T(8,128)(2,1)S(1)} %collective-permute-done.42.other, ...), custom_call_target="tpu_custom_call" | custom-call | flops 5200000000 | bytes 5079040 | tf_op jit(solution)/shard_map/conv_back/pallas_call | solution.py:884
  132.7 1.9 collective-permute-start.46
  134.6 3.5 %all-to-all-done.2 = bf16[4,576,128]{2,1,0:T(8,128)(2,1)} async-done(((bf16[4,576,128]{2,1,0:T(8,128)(2,1)}), bf16[4,576,128]{2,1,0:T(8,128)(2,1)}, u32[]{:S(2)}, u32[]{:S(2)}) %all-to-all-start.2) | async-done | bytes 589856 | tf_op jit(solution)/shard_map/all_to_all | solution.py:1081
  138.0 3.5 %all-to-all-start.3 = ((bf16[4,576,128]{2,1,0:T(8,128)(2,1)}), bf16[4,576,128]{2,1,0:T(8,128)(2,1)S(1)}, u32[]{:S(2)}, u32[]{:S(2)}) async-start(bf16[4,576,128]{2,1,0:T(8,128)(2,1)} %bitcast.35), calls=%async_computation.3 | async-start | bytes 1179648 | tf_op jit(solution)/shard_map/all_to_all | solution.py:1081
  143.4 1.4 collective-permute-done.47.other
  144.8 3.8 %conv_back.7 = (bf16[64,1536]{1,0:T(8,128)(2,1)S(1)}, bf16[64,1536]{1,0:T(8,128)(2,1)S(1)}, bf16[64,1536]{1,0:T(8,128)(2,1)S(1)}, bf16[64,1536]{1,0:T(8,128)(2,1)S(1)}, bf16[2368,128]{1,0:T(8,128)(2,1)}) custom-call(bf16[64,1536]{1,0:T(8,128)(2,1)S(1)} %get-tuple-element.216.own, bf16[64,1536]{1,0:T(8,128)(2,1)S(1)} %collective-permute-done.47.other, ...), custom_call_target="tpu_custom_call" | custom-call | flops 6000000000 | bytes 5128192 | tf_op jit(solution)/shard_map/conv_back/pallas_call | solution.py:884
  148.6 1.3 collective-permute-start.56
  151.0 1.2 collective-permute-start.58
  152.2 4.7 %all-to-all-done.3 = bf16[4,576,128]{2,1,0:T(8,128)(2,1)S(1)} async-done(((bf16[4,576,128]{2,1,0:T(8,128)(2,1)}), bf16[4,576,128]{2,1,0:T(8,128)(2,1)S(1)}, u32[]{:S(2)}, u32[]{:S(2)}) %all-to-all-start.3) | async-done | bytes 589856 | tf_op jit(solution)/shard_map/all_to_all | solution.py:1081
  156.9 3.5 %all-to-all-start.4 = ((bf16[4,592,128]{2,1,0:T(8,128)(2,1)}), bf16[4,592,128]{2,1,0:T(8,128)(2,1)S(1)}, u32[]{:S(2)}, u32[]{:S(2)}) async-start(bf16[4,592,128]{2,1,0:T(8,128)(2,1)} %bitcast.34), calls=%async_computation.4 | async-start | bytes 1212416 | tf_op jit(solution)/shard_map/all_to_all | solution.py:1081
  161.9 1.4 collective-permute-done.59.got
  164.1 3.5 %collective-permute-start.61 = (bf16[256,384]{1,0:T(8,128)(2,1)S(1)}, bf16[256,384]{1,0:T(8,128)(2,1)S(1)}, u32[]{:S(2)}, u32[]{:S(2)}) collective-permute-start(bf16[256,384]{1,0:T(8,128)(2,1)S(1)} %get-tuple-element.245), channel_id=1, source_target_pairs={{0,2},{1,7},{2,10},{3,15},{4,18},{5,23},{6,26},{7,31},{8,0},{9,5},... | collective-permute-start | bytes 589832 | tf_op jit(solution)/shard_map/ppermute | solution.py:253
  167.6 1.5 fold.1
  169.1 11.2 %all-to-all-done.4 = bf16[4,592,128]{2,1,0:T(8,128)(2,1)S(1)} async-done(((bf16[4,592,128]{2,1,0:T(8,128)(2,1)}), bf16[4,592,128]{2,1,0:T(8,128)(2,1)S(1)}, u32[]{:S(2)}, u32[]{:S(2)}) %all-to-all-start.4) | async-done | bytes 606240 | tf_op jit(solution)/shard_map/all_to_all | solution.py:1081
  180.5 1.5 collective-permute-start.49
  182.0 1.2 collective-permute-start.50
  184.6 3.1 %collective-permute-done.49.refs_1_ = bf16[592,128]{1,0:T(8,128)(2,1)S(1)} collective-permute-done((bf16[592,128]{1,0:T(8,128)(2,1)S(1)}, bf16[592,128]{1,0:T(8,128)(2,1)S(1)}, u32[]{:S(2)}, u32[]{:S(2)}) %collective-permute-start.49) | collective-permute-done | bytes 151584 | tf_op jit(solution)/shard_map/ppermute | solution.py:253
  187.8 2.2 %collective-permute-done.50.refs_2_ = bf16[592,128]{1,0:T(8,128)(2,1)S(1)} collective-permute-done((bf16[592,128]{1,0:T(8,128)(2,1)S(1)}, bf16[592,128]{1,0:T(8,128)(2,1)S(1)}, u32[]{:S(2)}, u32[]{:S(2)}) %collective-permute-start.50) | collective-permute-done | bytes 151584 | tf_op jit(solution)/shard_map/ppermute | solution.py:253
  191.9 1.9 outputs.1
  (127 shorter events, 26.5 us)
Async XLA Ops:
  3.1 24.5 %collective-permute-start.7 = (bf16[592,512]{1,0:T(8,128)(2,1)S(1)}, bf16[592,512]{1,0:T(8,128)(2,1)S(1)}, u32[]{:S(2)}, u32[]{:S(2)}) collective-permute-start(bf16[592,512]{1,0:T(8,128)(2,1)S(1)} %get-tuple-element.130), channel_id=1, source_target_pairs={{0,8},{1,9},{2,10},{3,11},{4,12},{5,13},{6,14},{7,15},{8,0},{9,1},... | collective-permute-start | bytes 1818632 | tf_op jit(solution)/shard_map/ppermute | solution.py:253
  6.2 28.1 %collective-permute-start.8 = (bf16[592,512]{1,0:T(8,128)(2,1)S(1)}, bf16[592,512]{1,0:T(8,128)(2,1)S(1)}, u32[]{:S(2)}, u32[]{:S(2)}) collective-permute-start(bf16[592,512]{1,0:T(8,128)(2,1)S(1)} %get-tuple-element.131), channel_id=1, source_target_pairs={{0,16},{1,17},{2,18},{3,19},{4,20},{5,21},{6,22},{7,23},{8,24},{9,... | collective-permute-start | bytes 1818632 | tf_op jit(solution)/shard_map/ppermute | solution.py:253
  9.1 10.8 %collective-permute-start = (bf16[208,512]{1,0:T(8,128)(2,1)S(1)}, bf16[208,512]{1,0:T(8,128)(2,1)S(1)}, u32[]{:S(2)}, u32[]{:S(2)}) collective-permute-start(bf16[208,512]{1,0:T(8,128)(2,1)S(1)} %get-tuple-element.135), channel_id=1, source_target_pairs={{0,2},{1,3},{2,0},{3,1},{4,6},{5,7},{6,4},{7,5},{8,10},{9,11},{10,... | collective-permute-start | bytes 638984 | tf_op jit(solution)/shard_map/ppermute | solution.py:253
  10.7 23.6 %collective-permute-start.9 = (bf16[592,512]{1,0:T(8,128)(2,1)S(1)}, bf16[592,512]{1,0:T(8,128)(2,1)S(1)}, u32[]{:S(2)}, u32[]{:S(2)}) collective-permute-start(bf16[592,512]{1,0:T(8,128)(2,1)S(1)} %get-tuple-element.132), channel_id=1, source_target_pairs={{0,24},{1,25},{2,26},{3,27},{4,28},{5,29},{6,30},{7,31},{8,16},{9,... | collective-permute-start | bytes 1818632 | tf_op jit(solution)/shard_map/ppermute | solution.py:253
  11.2 13.9 %collective-permute-start.1 = (bf16[208,512]{1,0:T(8,128)(2,1)S(1)}, bf16[208,512]{1,0:T(8,128)(2,1)S(1)}, u32[]{:S(2)}, u32[]{:S(2)}) collective-permute-start(bf16[208,512]{1,0:T(8,128)(2,1)S(1)} %get-tuple-element.136), channel_id=1, source_target_pairs={{0,4},{1,5},{2,6},{3,7},{4,0},{5,1},{6,2},{7,3},{8,12},{9,13},{10,... | collective-permute-start | bytes 638984 | tf_op jit(solution)/shard_map/ppermute | solution.py:253
  19.8 7.8 %collective-permute-start.2 = (bf16[208,512]{1,0:T(8,128)(2,1)S(1)}, bf16[208,512]{1,0:T(8,128)(2,1)S(1)}, u32[]{:S(2)}, u32[]{:S(2)}) collective-permute-start(bf16[208,512]{1,0:T(8,128)(2,1)S(1)} %get-tuple-element.137), channel_id=1, source_target_pairs={{0,6},{1,7},{2,4},{3,5},{4,2},{5,3},{6,0},{7,1},{8,14},{9,15},{10,... | collective-permute-start | bytes 638984 | tf_op jit(solution)/shard_map/ppermute | solution.py:253
  25.1 9.2 %collective-permute-start.3 = (bf16[208,512]{1,0:T(8,128)(2,1)S(1)}, bf16[208,512]{1,0:T(8,128)(2,1)S(1)}, u32[]{:S(2)}, u32[]{:S(2)}) collective-permute-start(bf16[208,512]{1,0:T(8,128)(2,1)S(1)} %get-tuple-element.134.refs_0_), channel_id=1, source_target_pairs={{0,1},{1,0},{2,3},{3,2},{4,5},{5,4},{6,7},{7,6},{8,9},{9,8},{10,11... | collective-permute-start | bytes 638984 | tf_op jit(solution)/shard_map/ppermute | solution.py:253
  27.6 6.8 %collective-permute-start.4 = (bf16[208,512]{1,0:T(8,128)(2,1)S(1)}, bf16[208,512]{1,0:T(8,128)(2,1)S(1)}, u32[]{:S(2)}, u32[]{:S(2)}) collective-permute-start(bf16[208,512]{1,0:T(8,128)(2,1)S(1)} %collective-permute-done.refs_1_), channel_id=1, source_target_pairs={{0,1},{1,0},{2,3},{3,2},{4,5},{5,4},{6,7},{7,6},{8,9},{9,8},{10,11... | collective-permute-start | bytes 638984 | tf_op jit(solution)/shard_map/ppermute | solution.py:253
  27.6 6.8 %collective-permute-start.5 = (bf16[208,512]{1,0:T(8,128)(2,1)S(1)}, bf16[208,512]{1,0:T(8,128)(2,1)S(1)}, u32[]{:S(2)}, u32[]{:S(2)}) collective-permute-start(bf16[208,512]{1,0:T(8,128)(2,1)S(1)} %collective-permute-done.1.refs_2_), channel_id=1, source_target_pairs={{0,1},{1,0},{2,3},{3,2},{4,5},{5,4},{6,7},{7,6},{8,9},{9,8},{10,11... | collective-permute-start | bytes 638984 | tf_op jit(solution)/shard_map/ppermute | solution.py:253
  34.3 1.5 collective-permute-start.6
  38.3 10.4 %collective-permute-start.12 = (bf16[64,1536]{1,0:T(8,128)(2,1)S(1)}, bf16[64,1536]{1,0:T(8,128)(2,1)S(1)}, u32[]{:S(2)}, u32[]{:S(2)}) collective-permute-start(bf16[64,1536]{1,0:T(8,128)(2,1)S(1)} %get-tuple-element.144.refs_0_), channel_id=1, source_target_pairs={{0,24},{1,25},{2,26},{3,27},{4,28},{5,29},{6,30},{7,31},{8,16},{9,... | collective-permute-start | bytes 589832 | tf_op jit(solution)/shard_map/ppermute | solution.py:253
  39.9 10.7 %collective-permute-start.10 = (bf16[64,1536]{1,0:T(8,128)(2,1)S(1)}, bf16[64,1536]{1,0:T(8,128)(2,1)S(1)}, u32[]{:S(2)}, u32[]{:S(2)}) collective-permute-start(bf16[64,1536]{1,0:T(8,128)(2,1)S(1)} %get-tuple-element.144.refs_0_), channel_id=1, source_target_pairs={{0,8},{1,9},{2,10},{3,11},{4,12},{5,13},{6,14},{7,15},{8,0},{9,1},... | collective-permute-start | bytes 589832 | tf_op jit(solution)/shard_map/ppermute | solution.py:253
  41.4 9.2 %collective-permute-start.11 = (bf16[64,1536]{1,0:T(8,128)(2,1)S(1)}, bf16[64,1536]{1,0:T(8,128)(2,1)S(1)}, u32[]{:S(2)}, u32[]{:S(2)}) collective-permute-start(bf16[64,1536]{1,0:T(8,128)(2,1)S(1)} %get-tuple-element.144.refs_0_), channel_id=1, source_target_pairs={{0,16},{1,17},{2,18},{3,19},{4,20},{5,21},{6,22},{7,23},{8,24},{9,... | collective-permute-start | bytes 589832 | tf_op jit(solution)/shard_map/ppermute | solution.py:253
  41.9 9.2 %collective-permute-start.13 = (bf16[64,1536]{1,0:T(8,128)(2,1)S(1)}, bf16[64,1536]{1,0:T(8,128)(2,1)S(1)}, u32[]{:S(2)}, u32[]{:S(2)}) collective-permute-start(bf16[64,1536]{1,0:T(8,128)(2,1)S(1)} %get-tuple-element.144.refs_0_), channel_id=1, source_target_pairs={{0,1},{1,0},{2,3},{3,2},{4,5},{5,4},{6,7},{7,6},{8,9},{9,8},{10,11... | collective-permute-start | bytes 589832 | tf_op jit(solution)/shard_map/ppermute | solution.py:253
  48.8 2.3 %collective-permute-start.16 = (bf16[64,1536]{1,0:T(8,128)(2,1)S(1)}, bf16[64,1536]{1,0:T(8,128)(2,1)S(1)}, u32[]{:S(2)}, u32[]{:S(2)}) collective-permute-start(bf16[64,1536]{1,0:T(8,128)(2,1)S(1)} %collective-permute-done.12.refs_3_), channel_id=1, source_target_pairs={{0,1},{1,0},{2,3},{3,2},{4,5},{5,4},{6,7},{7,6},{8,9},{9,8},{10,11... | collective-permute-start | bytes 589832 | tf_op jit(solution)/shard_map/ppermute | solution.py:253
  50.5 1.4 collective-permute-start.14
  50.5 1.7 collective-permute-start.15
  55.4 9.5 %collective-permute-start.19 = (bf16[64,1536]{1,0:T(8,128)(2,1)S(1)}, bf16[64,1536]{1,0:T(8,128)(2,1)S(1)}, u32[]{:S(2)}, u32[]{:S(2)}) collective-permute-start(bf16[64,1536]{1,0:T(8,128)(2,1)S(1)} %get-tuple-element.157.refs_0_), channel_id=1, source_target_pairs={{0,24},{1,25},{2,26},{3,27},{4,28},{5,29},{6,30},{7,31},{8,16},{9,... | collective-permute-start | bytes 589832 | tf_op jit(solution)/shard_map/ppermute | solution.py:253
  56.5 10.7 %collective-permute-start.17 = (bf16[64,1536]{1,0:T(8,128)(2,1)S(1)}, bf16[64,1536]{1,0:T(8,128)(2,1)S(1)}, u32[]{:S(2)}, u32[]{:S(2)}) collective-permute-start(bf16[64,1536]{1,0:T(8,128)(2,1)S(1)} %get-tuple-element.157.refs_0_), channel_id=1, source_target_pairs={{0,8},{1,9},{2,10},{3,11},{4,12},{5,13},{6,14},{7,15},{8,0},{9,1},... | collective-permute-start | bytes 589832 | tf_op jit(solution)/shard_map/ppermute | solution.py:253
  58.0 9.6 %collective-permute-start.18 = (bf16[64,1536]{1,0:T(8,128)(2,1)S(1)}, bf16[64,1536]{1,0:T(8,128)(2,1)S(1)}, u32[]{:S(2)}, u32[]{:S(2)}) collective-permute-start(bf16[64,1536]{1,0:T(8,128)(2,1)S(1)} %get-tuple-element.157.refs_0_), channel_id=1, source_target_pairs={{0,16},{1,17},{2,18},{3,19},{4,20},{5,21},{6,22},{7,23},{8,24},{9,... | collective-permute-start | bytes 589832 | tf_op jit(solution)/shard_map/ppermute | solution.py:253
  58.9 8.8 %collective-permute-start.20 = (bf16[64,1536]{1,0:T(8,128)(2,1)S(1)}, bf16[64,1536]{1,0:T(8,128)(2,1)S(1)}, u32[]{:S(2)}, u32[]{:S(2)}) collective-permute-start(bf16[64,1536]{1,0:T(8,128)(2,1)S(1)} %get-tuple-element.157.refs_0_), channel_id=1, source_target_pairs={{0,1},{1,0},{2,3},{3,2},{4,5},{5,4},{6,7},{7,6},{8,9},{9,8},{10,11... | collective-permute-start | bytes 589832 | tf_op jit(solution)/shard_map/ppermute | solution.py:253
  58.9 16.1 %all-to-all-start = ((bf16[4,192,128]{2,1,0:T(8,128)(2,1)}), bf16[4,192,128]{2,1,0:T(8,128)(2,1)S(1)}, u32[]{:S(2)}, u32[]{:S(2)}) async-start(bf16[4,192,128]{2,1,0:T(8,128)(2,1)} %bitcast.7), calls=%async_computation | async-start | bytes 393216 | tf_op jit(solution)/shard_map/all_to_all | solution.py:1014
  64.9 2.8 %collective-permute-start.23 = (bf16[64,1536]{1,0:T(8,128)(2,1)S(1)}, bf16[64,1536]{1,0:T(8,128)(2,1)S(1)}, u32[]{:S(2)}, u32[]{:S(2)}) collective-permute-start(bf16[64,1536]{1,0:T(8,128)(2,1)S(1)} %collective-permute-done.19.refs_3_), channel_id=1, source_target_pairs={{0,1},{1,0},{2,3},{3,2},{4,5},{5,4},{6,7},{7,6},{8,9},{9,8},{10,11... | collective-permute-start | bytes 589832 | tf_op jit(solution)/shard_map/ppermute | solution.py:253
  67.2 1.4 collective-permute-start.21
  71.5 8.8 %collective-permute-start.26 = (bf16[64,1536]{1,0:T(8,128)(2,1)S(1)}, bf16[64,1536]{1,0:T(8,128)(2,1)S(1)}, u32[]{:S(2)}, u32[]{:S(2)}) collective-permute-start(bf16[64,1536]{1,0:T(8,128)(2,1)S(1)} %get-tuple-element.163.refs_0_), channel_id=1, source_target_pairs={{0,24},{1,25},{2,26},{3,27},{4,28},{5,29},{6,30},{7,31},{8,16},{9,... | collective-permute-start | bytes 589832 | tf_op jit(solution)/shard_map/ppermute | solution.py:253
  72.6 10.7 %collective-permute-start.24 = (bf16[64,1536]{1,0:T(8,128)(2,1)S(1)}, bf16[64,1536]{1,0:T(8,128)(2,1)S(1)}, u32[]{:S(2)}, u32[]{:S(2)}) collective-permute-start(bf16[64,1536]{1,0:T(8,128)(2,1)S(1)} %get-tuple-element.163.refs_0_), channel_id=1, source_target_pairs={{0,8},{1,9},{2,10},{3,11},{4,12},{5,13},{6,14},{7,15},{8,0},{9,1},... | collective-permute-start | bytes 589832 | tf_op jit(solution)/shard_map/ppermute | solution.py:253
  74.1 9.6 %collective-permute-start.25 = (bf16[64,1536]{1,0:T(8,128)(2,1)S(1)}, bf16[64,1536]{1,0:T(8,128)(2,1)S(1)}, u32[]{:S(2)}, u32[]{:S(2)}) collective-permute-start(bf16[64,1536]{1,0:T(8,128)(2,1)S(1)} %get-tuple-element.163.refs_0_), channel_id=1, source_target_pairs={{0,16},{1,17},{2,18},{3,19},{4,20},{5,21},{6,22},{7,23},{8,24},{9,... | collective-permute-start | bytes 589832 | tf_op jit(solution)/shard_map/ppermute | solution.py:253
  75.1 1.7 collective-permute-start.27
  75.2 9.0 %collective-permute-start.28 = (bf16[64,1536]{1,0:T(8,128)(2,1)S(1)}, bf16[64,1536]{1,0:T(8,128)(2,1)S(1)}, u32[]{:S(2)}, u32[]{:S(2)}) collective-permute-start(bf16[64,1536]{1,0:T(8,128)(2,1)S(1)} %get-tuple-element.163.refs_0_), channel_id=1, source_target_pairs={{0,1},{1,0},{2,3},{3,2},{4,5},{5,4},{6,7},{7,6},{8,9},{9,8},{10,11... | collective-permute-start | bytes 589832 | tf_op jit(solution)/shard_map/ppermute | solution.py:253
  80.3 3.9 %collective-permute-start.31 = (bf16[64,1536]{1,0:T(8,128)(2,1)S(1)}, bf16[64,1536]{1,0:T(8,128)(2,1)S(1)}, u32[]{:S(2)}, u32[]{:S(2)}) collective-permute-start(bf16[64,1536]{1,0:T(8,128)(2,1)S(1)} %collective-permute-done.26.refs_3_), channel_id=1, source_target_pairs={{0,1},{1,0},{2,3},{3,2},{4,5},{5,4},{6,7},{7,6},{8,9},{9,8},{10,11... | collective-permute-start | bytes 589832 | tf_op jit(solution)/shard_map/ppermute | solution.py:253
  83.3 1.4 collective-permute-start.29
  83.8 4.1 %collective-permute-start.33 = (bf16[256,640]{1,0:T(8,128)(2,1)S(1)}, bf16[256,640]{1,0:T(8,128)(2,1)S(1)}, u32[]{:S(2)}, u32[]{:S(2)}) collective-permute-start(bf16[256,640]{1,0:T(8,128)(2,1)S(1)} %copy-done.10), channel_id=1, source_target_pairs={{0,1},{1,0},{2,3},{3,2},{4,5},{5,4},{6,7},{7,6},{8,9},{9,8},{10,11... | collective-permute-start | bytes 983048 | tf_op jit(solution)/shard_map/ppermute | solution.py:253
  87.6 1.5 collective-permute-start.32
  93.0 9.5 %collective-permute-start.34 = (bf16[64,1536]{1,0:T(8,128)(2,1)S(1)}, bf16[64,1536]{1,0:T(8,128)(2,1)S(1)}, u32[]{:S(2)}, u32[]{:S(2)}) collective-permute-start(bf16[64,1536]{1,0:T(8,128)(2,1)S(1)} %get-tuple-element.175), channel_id=1, source_target_pairs={{0,8},{1,9},{2,10},{3,11},{4,12},{5,13},{6,14},{7,15},{8,0},{9,1},... | collective-permute-start | bytes 589832 | tf_op jit(solution)/shard_map/ppermute | solution.py:253
  93.6 8.9 %collective-permute-start.35 = (bf16[64,1536]{1,0:T(8,128)(2,1)S(1)}, bf16[64,1536]{1,0:T(8,128)(2,1)S(1)}, u32[]{:S(2)}, u32[]{:S(2)}) collective-permute-start(bf16[64,1536]{1,0:T(8,128)(2,1)S(1)} %get-tuple-element.176), channel_id=1, source_target_pairs={{0,16},{1,17},{2,18},{3,19},{4,20},{5,21},{6,22},{7,23},{8,24},{9,... | collective-permute-start | bytes 589832 | tf_op jit(solution)/shard_map/ppermute | solution.py:253
  94.7 10.1 %collective-permute-start.36 = (bf16[64,1536]{1,0:T(8,128)(2,1)S(1)}, bf16[64,1536]{1,0:T(8,128)(2,1)S(1)}, u32[]{:S(2)}, u32[]{:S(2)}) collective-permute-start(bf16[64,1536]{1,0:T(8,128)(2,1)S(1)} %get-tuple-element.177), channel_id=1, source_target_pairs={{0,24},{1,25},{2,26},{3,27},{4,28},{5,29},{6,30},{7,31},{8,16},{9,... | collective-permute-start | bytes 589832 | tf_op jit(solution)/shard_map/ppermute | solution.py:253
  96.6 8.8 %collective-permute-start.38 = (bf16[256,640]{1,0:T(8,128)(2,1)S(1)}, bf16[256,640]{1,0:T(8,128)(2,1)S(1)}, u32[]{:S(2)}, u32[]{:S(2)}) collective-permute-start(bf16[256,640]{1,0:T(8,128)(2,1)S(1)} %copy-done.9), channel_id=1, source_target_pairs={{0,1},{1,0},{2,3},{3,2},{4,5},{5,4},{6,7},{7,6},{8,9},{9,8},{10,11... | collective-permute-start | bytes 983048 | tf_op jit(solution)/shard_map/ppermute | solution.py:253
  96.6 21.4 %all-to-all-start.1 = ((bf16[4,576,128]{2,1,0:T(8,128)(2,1)}), bf16[4,576,128]{2,1,0:T(8,128)(2,1)S(1)}, u32[]{:S(2)}, u32[]{:S(2)}) async-start(bf16[4,576,128]{2,1,0:T(8,128)(2,1)} %bitcast.37), calls=%async_computation.1 | async-start | bytes 1179648 | tf_op jit(solution)/shard_map/all_to_all | solution.py:1081
  105.3 1.5 collective-permute-start.37
  110.7 12.8 %collective-permute-start.39 = (bf16[64,1536]{1,0:T(8,128)(2,1)S(1)}, bf16[64,1536]{1,0:T(8,128)(2,1)S(1)}, u32[]{:S(2)}, u32[]{:S(2)}) collective-permute-start(bf16[64,1536]{1,0:T(8,128)(2,1)S(1)} %get-tuple-element.190), channel_id=1, source_target_pairs={{0,8},{1,9},{2,10},{3,11},{4,12},{5,13},{6,14},{7,15},{8,0},{9,1},... | collective-permute-start | bytes 589832 | tf_op jit(solution)/shard_map/ppermute | solution.py:253
  112.1 11.4 %collective-permute-start.40 = (bf16[64,1536]{1,0:T(8,128)(2,1)S(1)}, bf16[64,1536]{1,0:T(8,128)(2,1)S(1)}, u32[]{:S(2)}, u32[]{:S(2)}) collective-permute-start(bf16[64,1536]{1,0:T(8,128)(2,1)S(1)} %get-tuple-element.191), channel_id=1, source_target_pairs={{0,16},{1,17},{2,18},{3,19},{4,20},{5,21},{6,22},{7,23},{8,24},{9,... | collective-permute-start | bytes 589832 | tf_op jit(solution)/shard_map/ppermute | solution.py:253
  113.1 10.4 %collective-permute-start.41 = (bf16[64,1536]{1,0:T(8,128)(2,1)S(1)}, bf16[64,1536]{1,0:T(8,128)(2,1)S(1)}, u32[]{:S(2)}, u32[]{:S(2)}) collective-permute-start(bf16[64,1536]{1,0:T(8,128)(2,1)S(1)} %get-tuple-element.192), channel_id=1, source_target_pairs={{0,24},{1,25},{2,26},{3,27},{4,28},{5,29},{6,30},{7,31},{8,16},{9,... | collective-permute-start | bytes 589832 | tf_op jit(solution)/shard_map/ppermute | solution.py:253
  114.3 11.4 %collective-permute-start.43 = (bf16[256,640]{1,0:T(8,128)(2,1)S(1)}, bf16[256,640]{1,0:T(8,128)(2,1)S(1)}, u32[]{:S(2)}, u32[]{:S(2)}) collective-permute-start(bf16[256,640]{1,0:T(8,128)(2,1)S(1)} %copy-done.8), channel_id=1, source_target_pairs={{0,1},{1,0},{2,3},{3,2},{4,5},{5,4},{6,7},{7,6},{8,9},{9,8},{10,11... | collective-permute-start | bytes 983048 | tf_op jit(solution)/shard_map/ppermute | solution.py:253
  118.1 20.0 %all-to-all-start.2 = ((bf16[4,576,128]{2,1,0:T(8,128)(2,1)}), bf16[4,576,128]{2,1,0:T(8,128)(2,1)}, u32[]{:S(2)}, u32[]{:S(2)}) async-start(bf16[4,576,128]{2,1,0:T(8,128)(2,1)} %bitcast.36), calls=%async_computation.2 | async-start | bytes 1179648 | tf_op jit(solution)/shard_map/all_to_all | solution.py:1081
  125.6 1.5 collective-permute-start.42
  131.0 11.5 %collective-permute-start.44 = (bf16[64,1536]{1,0:T(8,128)(2,1)S(1)}, bf16[64,1536]{1,0:T(8,128)(2,1)S(1)}, u32[]{:S(2)}, u32[]{:S(2)}) collective-permute-start(bf16[64,1536]{1,0:T(8,128)(2,1)S(1)} %get-tuple-element.205), channel_id=1, source_target_pairs={{0,8},{1,9},{2,10},{3,11},{4,12},{5,13},{6,14},{7,15},{8,0},{9,1},... | collective-permute-start | bytes 589832 | tf_op jit(solution)/shard_map/ppermute | solution.py:253
  131.6 11.0 %collective-permute-start.45 = (bf16[64,1536]{1,0:T(8,128)(2,1)S(1)}, bf16[64,1536]{1,0:T(8,128)(2,1)S(1)}, u32[]{:S(2)}, u32[]{:S(2)}) collective-permute-start(bf16[64,1536]{1,0:T(8,128)(2,1)S(1)} %get-tuple-element.206), channel_id=1, source_target_pairs={{0,16},{1,17},{2,18},{3,19},{4,20},{5,21},{6,22},{7,23},{8,24},{9,... | collective-permute-start | bytes 589832 | tf_op jit(solution)/shard_map/ppermute | solution.py:253
  132.7 10.1 %collective-permute-start.46 = (bf16[64,1536]{1,0:T(8,128)(2,1)S(1)}, bf16[64,1536]{1,0:T(8,128)(2,1)S(1)}, u32[]{:S(2)}, u32[]{:S(2)}) collective-permute-start(bf16[64,1536]{1,0:T(8,128)(2,1)S(1)} %get-tuple-element.207), channel_id=1, source_target_pairs={{0,24},{1,25},{2,26},{3,27},{4,28},{5,29},{6,30},{7,31},{8,16},{9,... | collective-permute-start | bytes 589832 | tf_op jit(solution)/shard_map/ppermute | solution.py:253
  134.6 8.8 %collective-permute-start.48 = (bf16[256,640]{1,0:T(8,128)(2,1)S(1)}, bf16[256,640]{1,0:T(8,128)(2,1)S(1)}, u32[]{:S(2)}, u32[]{:S(2)}) collective-permute-start(bf16[256,640]{1,0:T(8,128)(2,1)S(1)} %copy-done.7), channel_id=1, source_target_pairs={{0,1},{1,0},{2,3},{3,2},{4,5},{5,4},{6,7},{7,6},{8,9},{9,8},{10,11... | collective-permute-start | bytes 983048 | tf_op jit(solution)/shard_map/ppermute | solution.py:253
  138.0 18.8 %all-to-all-start.3 = ((bf16[4,576,128]{2,1,0:T(8,128)(2,1)}), bf16[4,576,128]{2,1,0:T(8,128)(2,1)S(1)}, u32[]{:S(2)}, u32[]{:S(2)}) async-start(bf16[4,576,128]{2,1,0:T(8,128)(2,1)} %bitcast.35), calls=%async_computation.3 | async-start | bytes 1179648 | tf_op jit(solution)/shard_map/all_to_all | solution.py:1081
  143.3 1.5 collective-permute-start.47
  148.6 11.7 %collective-permute-start.56 = (bf16[64,1536]{1,0:T(8,128)(2,1)S(1)}, bf16[64,1536]{1,0:T(8,128)(2,1)S(1)}, u32[]{:S(2)}, u32[]{:S(2)}) collective-permute-start(bf16[64,1536]{1,0:T(8,128)(2,1)S(1)} %get-tuple-element.235), channel_id=1, source_target_pairs={{0,8},{1,9},{2,10},{3,11},{4,12},{5,13},{6,14},{7,15},{8,0},{9,1},... | collective-permute-start | bytes 589832 | tf_op jit(solution)/shard_map/ppermute | solution.py:253
  150.0 10.9 %collective-permute-start.57 = (bf16[64,1536]{1,0:T(8,128)(2,1)S(1)}, bf16[64,1536]{1,0:T(8,128)(2,1)S(1)}, u32[]{:S(2)}, u32[]{:S(2)}) collective-permute-start(bf16[64,1536]{1,0:T(8,128)(2,1)S(1)} %get-tuple-element.236), channel_id=1, source_target_pairs={{0,16},{1,17},{2,18},{3,19},{4,20},{5,21},{6,22},{7,23},{8,24},{9,... | collective-permute-start | bytes 589832 | tf_op jit(solution)/shard_map/ppermute | solution.py:253
  151.0 9.8 %collective-permute-start.58 = (bf16[64,1536]{1,0:T(8,128)(2,1)S(1)}, bf16[64,1536]{1,0:T(8,128)(2,1)S(1)}, u32[]{:S(2)}, u32[]{:S(2)}) collective-permute-start(bf16[64,1536]{1,0:T(8,128)(2,1)S(1)} %get-tuple-element.237), channel_id=1, source_target_pairs={{0,24},{1,25},{2,26},{3,27},{4,28},{5,29},{6,30},{7,31},{8,16},{9,... | collective-permute-start | bytes 589832 | tf_op jit(solution)/shard_map/ppermute | solution.py:253
  156.9 23.4 %all-to-all-start.4 = ((bf16[4,592,128]{2,1,0:T(8,128)(2,1)}), bf16[4,592,128]{2,1,0:T(8,128)(2,1)S(1)}, u32[]{:S(2)}, u32[]{:S(2)}) async-start(bf16[4,592,128]{2,1,0:T(8,128)(2,1)} %bitcast.34), calls=%async_computation.4 | async-start | bytes 1212416 | tf_op jit(solution)/shard_map/all_to_all | solution.py:1081
  161.8 1.5 collective-permute-start.59
  163.4 20.7 %collective-permute-start.60 = (bf16[256,384]{1,0:T(8,128)(2,1)S(1)}, bf16[256,384]{1,0:T(8,128)(2,1)S(1)}, u32[]{:S(2)}, u32[]{:S(2)}) collective-permute-start(bf16[256,384]{1,0:T(8,128)(2,1)S(1)} %get-tuple-element.244), channel_id=1, source_target_pairs={{0,0},{1,5},{2,8},{3,13},{4,16},{5,21},{6,24},{7,29},{8,2},{9,7},{... | collective-permute-start | bytes 589832 | tf_op jit(solution)/shard_map/ppermute | solution.py:253
  164.1 20.1 %collective-permute-start.61 = (bf16[256,384]{1,0:T(8,128)(2,1)S(1)}, bf16[256,384]{1,0:T(8,128)(2,1)S(1)}, u32[]{:S(2)}, u32[]{:S(2)}) collective-permute-start(bf16[256,384]{1,0:T(8,128)(2,1)S(1)} %get-tuple-element.245), channel_id=1, source_target_pairs={{0,2},{1,7},{2,10},{3,15},{4,18},{5,23},{6,26},{7,31},{8,0},{9,5},... | collective-permute-start | bytes 589832 | tf_op jit(solution)/shard_map/ppermute | solution.py:253
  180.5 7.3 %collective-permute-start.49 = (bf16[592,128]{1,0:T(8,128)(2,1)S(1)}, bf16[592,128]{1,0:T(8,128)(2,1)S(1)}, u32[]{:S(2)}, u32[]{:S(2)}) collective-permute-start(bf16[592,128]{1,0:T(8,128)(2,1)S(1)} %get-tuple-element.231), channel_id=1, source_target_pairs={{0,8},{1,9},{2,10},{3,11},{4,12},{5,13},{6,14},{7,15},{8,0},{9,1},... | collective-permute-start | bytes 454664 | tf_op jit(solution)/shard_map/ppermute | solution.py:253
  182.0 7.9 %collective-permute-start.50 = (bf16[592,128]{1,0:T(8,128)(2,1)S(1)}, bf16[592,128]{1,0:T(8,128)(2,1)S(1)}, u32[]{:S(2)}, u32[]{:S(2)}) collective-permute-start(bf16[592,128]{1,0:T(8,128)(2,1)S(1)} %get-tuple-element.232), channel_id=1, source_target_pairs={{0,16},{1,17},{2,18},{3,19},{4,20},{5,21},{6,22},{7,23},{8,24},{9,... | collective-permute-start | bytes 454664 | tf_op jit(solution)/shard_map/ppermute | solution.py:253
  183.2 7.0 %collective-permute-start.51 = (bf16[592,128]{1,0:T(8,128)(2,1)S(1)}, bf16[592,128]{1,0:T(8,128)(2,1)S(1)}, u32[]{:S(2)}, u32[]{:S(2)}) collective-permute-start(bf16[592,128]{1,0:T(8,128)(2,1)S(1)} %get-tuple-element.233), channel_id=1, source_target_pairs={{0,24},{1,25},{2,26},{3,27},{4,28},{5,29},{6,30},{7,31},{8,16},{9,... | collective-permute-start | bytes 454664 | tf_op jit(solution)/shard_map/ppermute | solution.py:253
  184.1 6.4 %collective-permute-start.52 = (bf16[592,128]{1,0:T(8,128)(2,1)S(1)}, bf16[592,128]{1,0:T(8,128)(2,1)S(1)}, u32[]{:S(2)}, u32[]{:S(2)}) collective-permute-start(bf16[592,128]{1,0:T(8,128)(2,1)S(1)} %get-tuple-element.230.refs_0_), channel_id=1, source_target_pairs={{0,1},{1,0},{2,3},{3,2},{4,5},{5,4},{6,7},{7,6},{8,9},{9,8},{10,11... | collective-permute-start | bytes 454664 | tf_op jit(solution)/shard_map/ppermute | solution.py:253
  184.1 6.7 %collective-permute-start.62 = (bf16[256,384]{1,0:T(8,128)(2,1)S(1)}, bf16[256,384]{1,0:T(8,128)(2,1)S(1)}, u32[]{:S(2)}, u32[]{:S(2)}) collective-permute-start(bf16[256,384]{1,0:T(8,128)(2,1)S(1)} %collective-permute-done.60.refs_9_), channel_id=1, source_target_pairs={{0,1},{1,0},{2,3},{3,2},{4,5},{5,4},{6,7},{7,6},{8,9},{9,8},{10,11... | collective-permute-start | bytes 589832 | tf_op jit(solution)/shard_map/ppermute | solution.py:253
  187.8 3.1 %collective-permute-start.63 = (bf16[256,384]{1,0:T(8,128)(2,1)S(1)}, bf16[256,384]{1,0:T(8,128)(2,1)S(1)}, u32[]{:S(2)}, u32[]{:S(2)}) collective-permute-start(bf16[256,384]{1,0:T(8,128)(2,1)S(1)} %collective-permute-done.61.refs_10_), channel_id=1, source_target_pairs={{0,1},{1,0},{2,3},{3,2},{4,5},{5,4},{6,7},{7,6},{8,9},{9,8},{10,11... | collective-permute-start | bytes 589832 | tf_op jit(solution)/shard_map/ppermute | solution.py:253
  (16 other events, 137.5 us)

commit v8 on v7

--- a/solution.py
+++ b/solution.py
@@ -10,10 +10,10 @@
 from jax.sharding import PartitionSpec as P
 
 CONVS = 2
-BACK_FLOPS = (6 * 10**9, 52 * 10**8, 52 * 10**8, 0)
+BACK_FLOPS = (3 * 10**9, 52 * 10**8, 52 * 10**8, 0)
 PICK_FLOPS = 2 * 10**9
 COT_LAYER = 2
-INPUT_FLOPS = 4000000000
+INPUT_FLOPS = 0 * 10**9
 
 
 eps = 1e-05
@@ -713,8 +713,21 @@
             product[n * piece + rows : (n + 1) * piece, :] = sums_rows(ref, width)
 
 
+def copy_pieces(product, shares, sems):
+    if len(shares) == 1:
+        return start_all([pltpu.make_async_copy(product, shares[0], sems.at[3])])
+    _, plane, _ = place()
+    piece = shares[0].shape[0]
+    copies = []
+    for k, share in enumerate(shares):
+        at = pl.multiple_of((plane ^ k) * piece, META_ROWS)
+        copies.append(pltpu.make_async_copy(product.at[pl.ds(at, piece)], share, sems.at[3 + k]))
+    return start_all(copies)
+
+
 def conv_back_kernel(dims, layer, own, other, own_weights, other_weights, full_in, facts, *refs):
-    sums, outs, (share, product, full, moved, weights, sems) = refs[:-10], refs[-10:-6], refs[-6:]
+    refs, (product, full, moved, weights, sems) = refs[:-5], refs[-5:]
+    sums, outs, shares = (refs[:1], refs[1:5], refs[5:]) if layer == 0 else ((), refs[:4], refs[4:])
     ch = own.shape[0]
     size = moved.shape[0] // 2
     rows = pl.ds(layer * 4 * ch, 4 * ch)
@@ -730,8 +743,7 @@
     spread_taps(own[...], moved, 0, facts_now, dims[1])
     full_copy.wait()
     form_share(layer, moved, full, sums, product)
-    share_copy = pltpu.make_async_copy(product, share, sems.at[3])
-    share_copy.start()
+    share_copies = copy_pieces(product, shares, sems)
     spread_taps(other[...], moved, size, facts_now, dims[1])
     for n in range(2):
         moved[n * size + TAPS * ch : (n + 1) * size, :] = jnp.zeros(
@@ -741,7 +753,7 @@
     value = jnp.dot(weights[...], moved[...], preferred_element_type=jnp.float32)
     for k, out in enumerate(outs):
         out[...] = value[k * ch : (k + 1) * ch, :].astype(jnp.bfloat16)
-    share_copy.wait()
+    wait_all(share_copies)
 
 
 def fold_kernel(*refs):
@@ -758,10 +770,9 @@
 
 
 def choose_kernel(*refs):
-    last, others, outs = refs[0], refs[1:-4], refs[-4:]
+    lasts, others, outs = refs[:4], refs[4:-4], refs[-4:]
     section, _, _ = place()
-    rows = outs[0].shape[0]
-    value = add_blocks([last.at[pl.ds(n * rows, rows)] for n in range(last.shape[0] // rows)])
+    value = add_blocks(lasts)
     value = value.astype(jnp.bfloat16)
     for k, out in enumerate(outs):
 
@@ -1057,9 +1068,10 @@
     shares = [None] * layers
     for layer in range(last, -1, -1):
         share_out = ((4 * piece_rows[layer], 2 * ch), bf16)
-        *parts, share = call(
+        pieces = [share_out] if layer else [((slice_rows, 2 * ch), bf16)] * 4
+        outs = call(
             partial(conv_back_kernel, dims, layer),
-            [map_out] * 4 + [share_out],
+            [map_out] * 4 + pieces,
             [
                 share_out,
                 full_map if layer else full_frames,
@@ -1071,14 +1083,18 @@
             "conv_back",
             held=(2, 4),
             free=(3,),
-            held_outs=(4,),
+            held_outs=range(4, 8),
             loose=(5,) if layer else (5, 6),
             flops=BACK_FLOPS[layer],
-            copies=4,
+            copies=7,
         )
+        parts, share = outs[:4], outs[4:]
+        if layer == 0:
+            shares[0] = [share[0]] + [None] + [to_plane(share[k], k) for k in (2, 3)]
+            break
         if layer < last:
             share = after(share, shares[layer + 1])
-        shares[layer] = lax.all_to_all(share, "dp", 0, 0, tiled=True, axis_index_groups=same_core)
+        shares[layer] = lax.all_to_all(share[0], "dp", 0, 0, tiled=True, axis_index_groups=same_core)
         if layer:
             crossing[layer - 1] = to_core(after(crossing[layer - 1], parts))
             held = call(
@@ -1099,7 +1115,9 @@
                 "norm_back",
                 loose=(6, 7, 8),
             )
-    blocks = spread(parts, to_section)
+    blocks = [parts[0]] + [to_section(parts[k], k) for k in (1, 2, 3)]
+    shares[0][1] = to_plane(after(share[1], blocks[1]), 1)
+    blocks = after(blocks, shares[1])
     keep, give = call(
         input_kernel,
         [((4 * ch, 2 * cells), bf16)] * 2,
@@ -1126,9 +1144,9 @@
         choose_kernel,
         [((slice_rows, 2 * ch), bf16)] * 4,
         [],
-        [shares[0], *folded],
+        [*shares[0], *folded],
         "choose",
-        loose=(0,),
+        loose=range(4),
     )
     pick = (core * cells + np.arange(cells))[:, None] == np.arange(2 * cells)[None, :]
     map_pick = pick.astype(bf16)

time: 195 us -> 191 us (0.979)
  waiting for transfers between devices: 72 us -> 63.8 us
  starting transfers between devices: 70.1 us -> 74.2 us
    all_to_all x4 -> x3, waiting for transfers between devices: 23.1 us -> 6.04 us  [plane_shards(): lax.all_to_all(share[0], 'dp', 0, 0, tiled=True, axis_index_groups=same_c...]
    ppermute x64 -> x67, waiting for transfers between devices: 48.9 us -> 57.8 us  [send(): return lax.ppermute(x, AXES, pairs)]
    ppermute x64 -> x67, starting transfers between devices: 49.1 us -> 56.6 us  [send(): return lax.ppermute(x, AXES, pairs)]
    all_to_all x4 -> x3, starting transfers between devices: 16.2 us -> 12.7 us  [plane_shards(): lax.all_to_all(share[0], 'dp', 0, 0, tiled=True, axis_index_groups=same_c...]
  transfers between devices with their start and end apart: 69 -> 71, of which waited for: 35 -> 37; matrix products, arithmetic and copies ran while one was open for 0% -> 0% of each run, Pallas kernels for 19% -> 19%
where the time goes in v8:
time: 191 us; the launch traced here: 190 us
  starting transfers between devices  74.2 us (39%)
  waiting for transfers between devices  63.8 us (33%)
  Pallas kernels  50.4 us (26%)
    ppermute x67, waiting for transfers between devices, send(): return lax.ppermute(x, AXES, pairs)  57.8 us
    ppermute x67, starting transfers between devices, send(): return lax.ppermute(x, AXES, pairs)  56.6 us
    pallas_call x27, Pallas kernels, call(): pl.pallas_call(kernel, out_shape=shapes, in_specs=[pl.BlockSpec(memory_sp...  50.4 us
    all_to_all x3, starting transfers between devices, plane_shards(): lax.all_to_all(share[0], 'dp', 0, 0, tiled=True, axis_index_groups=same_c...  12.7 us
    all_to_all x3, waiting for transfers between devices, plane_shards(): lax.all_to_all(share[0], 'dp', 0, 0, tiled=True, axis_index_groups=same_c...  6.04 us
    all_to_all x1, starting transfers between devices, plane_shards(): lax.all_to_all(cot_slots, 'dp', 0, 0, tiled=True, axis_index_groups=same_...  4.87 us
  transfers between devices with their start and end apart: 71, of which 37 were waited for; matrix products, arithmetic and copies ran while one was open for 0% of the time, Pallas kernels for 19%

profile of v8, /device:TPU:0, one launch (start us, length us, event | category | flops | bytes accessed | tf_op | source)
XLA Modules:
  0.0 189.9 jit_solution(273177858983008320)
XLA Ops:
  0.6 2.5 %weight_pack.1 = (bf16[592,512]{1,0:T(8,128)(2,1)S(1)}, bf16[592,512]{1,0:T(8,128)(2,1)S(1)}, bf16[592,512]{1,0:T(8,128)(2,1)S(1)}, bf16[592,512]{1,0:T(8,128)(2,1)S(1)}) custom-call(f32[1,512]{1,0:T(1,128)} %gain.1, f32[1,512]{1,0:T(1,128)} %bias.1, bf16[9,512,512]{2,1,0:T(8,128)(2,1)} %bitcast.26), custom_call_target="tpu_custom_call" | custom-call | bytes 7147520 | tf_op jit(solution)/shard_map/weight_pack/pallas_call | solution.py:895
  3.1 3.0 %collective-permute-start.7 = (bf16[592,512]{1,0:T(8,128)(2,1)S(1)}, bf16[592,512]{1,0:T(8,128)(2,1)S(1)}, u32[]{:S(2)}, u32[]{:S(2)}) collective-permute-start(bf16[592,512]{1,0:T(8,128)(2,1)S(1)} %get-tuple-element.134), channel_id=1, source_target_pairs={{0,8},{1,9},{2,10},{3,11},{4,12},{5,13},{6,14},{7,15},{8,0},{9,1},... | collective-permute-start | bytes 1818632 | tf_op jit(solution)/shard_map/ppermute | solution.py:253
  6.2 1.5 collective-permute-start.8
  7.7 1.4 frames.1
  9.1 1.6 collective-permute-start
  11.2 2.6 %collective-permute-start.1 = (bf16[208,512]{1,0:T(8,128)(2,1)S(1)}, bf16[208,512]{1,0:T(8,128)(2,1)S(1)}, u32[]{:S(2)}, u32[]{:S(2)}) collective-permute-start(bf16[208,512]{1,0:T(8,128)(2,1)S(1)} %get-tuple-element.140), channel_id=1, source_target_pairs={{0,4},{1,5},{2,6},{3,7},{4,0},{5,1},{6,2},{7,3},{8,12},{9,13},{10,... | collective-permute-start | bytes 638984 | tf_op jit(solution)/shard_map/ppermute | solution.py:253
  13.8 6.1 %collective-permute-done.refs_1_ = bf16[208,512]{1,0:T(8,128)(2,1)S(1)} collective-permute-done((bf16[208,512]{1,0:T(8,128)(2,1)S(1)}, bf16[208,512]{1,0:T(8,128)(2,1)S(1)}, u32[]{:S(2)}, u32[]{:S(2)}) %collective-permute-start) | collective-permute-done | bytes 213024 | tf_op jit(solution)/shard_map/ppermute | solution.py:253
  19.8 2.5 %collective-permute-start.2 = (bf16[208,512]{1,0:T(8,128)(2,1)S(1)}, bf16[208,512]{1,0:T(8,128)(2,1)S(1)}, u32[]{:S(2)}, u32[]{:S(2)}) collective-permute-start(bf16[208,512]{1,0:T(8,128)(2,1)S(1)} %get-tuple-element.141), channel_id=1, source_target_pairs={{0,6},{1,7},{2,4},{3,5},{4,2},{5,3},{6,0},{7,1},{8,14},{9,15},{10,... | collective-permute-start | bytes 638984 | tf_op jit(solution)/shard_map/ppermute | solution.py:253
  22.3 2.8 %collective-permute-done.1.refs_2_ = bf16[208,512]{1,0:T(8,128)(2,1)S(1)} collective-permute-done((bf16[208,512]{1,0:T(8,128)(2,1)S(1)}, bf16[208,512]{1,0:T(8,128)(2,1)S(1)}, u32[]{:S(2)}, u32[]{:S(2)}) %collective-permute-start.1) | collective-permute-done | bytes 213024 | tf_op jit(solution)/shard_map/ppermute | solution.py:253
  25.1 2.5 %collective-permute-done.2.refs_3_ = bf16[208,512]{1,0:T(8,128)(2,1)S(1)} collective-permute-done((bf16[208,512]{1,0:T(8,128)(2,1)S(1)}, bf16[208,512]{1,0:T(8,128)(2,1)S(1)}, u32[]{:S(2)}, u32[]{:S(2)}) %collective-permute-start.2) | collective-permute-done | bytes 213024 | tf_op jit(solution)/shard_map/ppermute | solution.py:253
  28.1 6.2 %collective-permute-done.8.refs_10_.refs_2_ = bf16[592,512]{1,0:T(8,128)(2,1)S(1)} collective-permute-done((bf16[592,512]{1,0:T(8,128)(2,1)S(1)}, bf16[592,512]{1,0:T(8,128)(2,1)S(1)}, u32[]{:S(2)}, u32[]{:S(2)}) %collective-permute-start.8) | collective-permute-done | bytes 606240 | tf_op jit(solution)/shard_map/ppermute | solution.py:253
  34.4 1.4 collective-permute-done.6.refs_7_
  35.8 2.5 %forward.3 = (bf16[64,1536]{1,0:T(8,128)(2,1)S(1)}, f32[64,1664]{1,0:T(8,128)}, bf16[1536,512]{1,0:T(8,128)(2,1)}, f32[1,1536]{1,0:T(1,128)S(1)}) custom-call(bf16[208,512]{1,0:T(8,128)(2,1)S(1)} %get-tuple-element.138.refs_0_, bf16[208,512]{1,0:T(8,128)(2,1)S(1)} %collective-permute-done.refs_1_, bf16[208,512]{1,0:T(8,128)(2,1)S(1)} %collective-permute-done.1.refs_2_, ...), custom_call_target="tpu_custom_call" | custom-call | flops 905969664 | bytes 6428672 | tf_op jit(solution)/shard_map/forward/pallas_call | solution.py:895
  38.4 1.5 collective-permute-start.12
  39.9 1.5 collective-permute-start.10
  41.9 2.0 %cot_slices.1 = bf16[768,128]{1,0:T(8,128)(2,1)} custom-call(bf16[4,192,512]{2,1,0:T(8,128)(2,1)} %bitcast.30), custom_call_target="tpu_custom_call" | custom-call | bytes 983040 | tf_op jit(solution)/shard_map/cot_slices/pallas_call | solution.py:895
  43.9 3.7 %turn_weights.1 = (bf16[1024,640]{1,0:T(8,128)(2,1)}, bf16[256,640]{1,0:T(8,128)(2,1)}, bf16[256,640]{1,0:T(8,128)(2,1)}, bf16[256,640]{1,0:T(8,128)(2,1)}, bf16[256,640]{1,0:T(8,128)(2,1)}) custom-call(bf16[592,512]{1,0:T(8,128)(2,1)} %copy-done, bf16[592,512]{1,0:T(8,128)(2,1)} %copy-done.1, bf16[592,512]{1,0:T(8,128)(2,1)} %copy-done.2, ...), custom_call_target="tpu_custom_call" | custom-call | bytes 5046272 | tf_op jit(solution)/shard_map/turn_weights/pallas_call | solution.py:895
  47.6 1.1 pick.3.refs_8_
  49.3 1.2 collective-permute-done.10.refs_1_
  52.3 3.1 %forward.4 = (bf16[64,1536]{1,0:T(8,128)(2,1)S(1)}, f32[64,1664]{1,0:T(8,128)}, bf16[512,1536]{1,0:T(8,128)(2,1)}) custom-call(bf16[64,1536]{1,0:T(8,128)(2,1)S(1)} %get-tuple-element.148.refs_0_, bf16[64,1536]{1,0:T(8,128)(2,1)S(1)} %collective-permute-done.10.refs_1_, bf16[64,1536]{1,0:T(8,128)(2,1)S(1)} %collective-permute-done.11.refs_2_, ...), custom_call_target="tpu_custom_call" | custom-call | flops 905969664 | bytes 4478976 | tf_op jit(solution)/shard_map/forward/pallas_call | solution.py:895
  55.4 1.2 collective-permute-start.19
  56.5 1.5 collective-permute-start.17
  58.9 4.9 %all-to-all-start = ((bf16[4,192,128]{2,1,0:T(8,128)(2,1)}), bf16[4,192,128]{2,1,0:T(8,128)(2,1)S(1)}, u32[]{:S(2)}, u32[]{:S(2)}) async-start(bf16[4,192,128]{2,1,0:T(8,128)(2,1)} %bitcast.7), calls=%async_computation | async-start | bytes 393216 | tf_op jit(solution)/shard_map/all_to_all | solution.py:1025
  63.8 1.1 pick.4.refs_8_
  65.2 2.0 %collective-permute-done.17.refs_1_ = bf16[64,1536]{1,0:T(8,128)(2,1)S(1)} collective-permute-done((bf16[64,1536]{1,0:T(8,128)(2,1)S(1)}, bf16[64,1536]{1,0:T(8,128)(2,1)S(1)}, u32[]{:S(2)}, u32[]{:S(2)}) %collective-permute-start.17) | collective-permute-done | bytes 196640 | tf_op jit(solution)/shard_map/ppermute | solution.py:253
  69.0 2.5 %forward.5 = (bf16[64,1536]{1,0:T(8,128)(2,1)S(1)}, f32[64,1664]{1,0:T(8,128)}, bf16[512,1536]{1,0:T(8,128)(2,1)}) custom-call(bf16[64,1536]{1,0:T(8,128)(2,1)S(1)} %get-tuple-element.161.refs_0_, bf16[64,1536]{1,0:T(8,128)(2,1)S(1)} %collective-permute-done.17.refs_1_, bf16[64,1536]{1,0:T(8,128)(2,1)S(1)} %collective-permute-done.18.refs_2_, ...), custom_call_target="tpu_custom_call" | custom-call | flops 905969664 | bytes 4478976 | tf_op jit(solution)/shard_map/forward/pallas_call | solution.py:895
  72.6 1.5 collective-permute-start.24
  75.7 1.1 pick.5.refs_8_
  77.1 3.1 %collective-permute-done.26.refs_3_ = bf16[64,1536]{1,0:T(8,128)(2,1)S(1)} collective-permute-done((bf16[64,1536]{1,0:T(8,128)(2,1)S(1)}, bf16[64,1536]{1,0:T(8,128)(2,1)S(1)}, u32[]{:S(2)}, u32[]{:S(2)}) %collective-permute-start.26) | collective-permute-done | bytes 196640 | tf_op jit(solution)/shard_map/ppermute | solution.py:253
  80.3 3.0 %collective-permute-done.24.refs_1_ = bf16[64,1536]{1,0:T(8,128)(2,1)S(1)} collective-permute-done((bf16[64,1536]{1,0:T(8,128)(2,1)S(1)}, bf16[64,1536]{1,0:T(8,128)(2,1)S(1)}, u32[]{:S(2)}, u32[]{:S(2)}) %collective-permute-start.24) | collective-permute-done | bytes 196640 | tf_op jit(solution)/shard_map/ppermute | solution.py:253
  85.1 2.5 %turn.1 = (bf16[64,1536]{1,0:T(8,128)(2,1)}, bf16[512,1536]{1,0:T(8,128)(2,1)}, bf16[64,1536]{1,0:T(8,128)(2,1)S(1)}, f32[64,128]{1,0:T(8,128)S(1)}) custom-call(bf16[64,1536]{1,0:T(8,128)(2,1)S(1)} %get-tuple-element.167.refs_0_, bf16[64,1536]{1,0:T(8,128)(2,1)S(1)} %collective-permute-done.24.refs_1_, ...), custom_call_target="tpu_custom_call" | custom-call | flops 905969664 | bytes 4478976 | tf_op jit(solution)/shard_map/turn/pallas_call | solution.py:895
  87.8 1.3 collective-permute-done.32.other
  89.1 3.9 %conv_back.4 = (bf16[64,1536]{1,0:T(8,128)(2,1)S(1)}, bf16[64,1536]{1,0:T(8,128)(2,1)S(1)}, bf16[64,1536]{1,0:T(8,128)(2,1)S(1)}, bf16[64,1536]{1,0:T(8,128)(2,1)S(1)}, bf16[2304,128]{1,0:T(8,128)(2,1)}) custom-call(bf16[64,1536]{1,0:T(8,128)(2,1)S(1)} %get-tuple-element.175.own, bf16[64,1536]{1,0:T(8,128)(2,1)S(1)} %collective-permute-done.32.other, ...), custom_call_target="tpu_custom_call" | custom-call | bytes 5079040 | tf_op jit(solution)/shard_map/conv_back/pallas_call | solution.py:895
  94.7 1.9 %collective-permute-start.36 = (bf16[64,1536]{1,0:T(8,128)(2,1)S(1)}, bf16[64,1536]{1,0:T(8,128)(2,1)S(1)}, u32[]{:S(2)}, u32[]{:S(2)}) collective-permute-start(bf16[64,1536]{1,0:T(8,128)(2,1)S(1)} %get-tuple-element.181), channel_id=1, source_target_pairs={{0,24},{1,25},{2,26},{3,27},{4,28},{5,29},{6,30},{7,31},{8,16},{9,... | collective-permute-start | bytes 589832 | tf_op jit(solution)/shard_map/ppermute | solution.py:253
  96.6 4.9 %all-to-all-start.1 = ((bf16[4,576,128]{2,1,0:T(8,128)(2,1)}), bf16[4,576,128]{2,1,0:T(8,128)(2,1)S(1)}, u32[]{:S(2)}, u32[]{:S(2)}) async-start(bf16[4,576,128]{2,1,0:T(8,128)(2,1)} %bitcast.33), calls=%async_computation.1 | async-start | bytes 1179648 | tf_op jit(solution)/shard_map/all_to_all | solution.py:1097
  102.6 2.2 %collective-permute-done.36.refs_3_ = bf16[64,1536]{1,0:T(8,128)(2,1)S(1)} collective-permute-done((bf16[64,1536]{1,0:T(8,128)(2,1)S(1)}, bf16[64,1536]{1,0:T(8,128)(2,1)S(1)}, u32[]{:S(2)}, u32[]{:S(2)}) %collective-permute-start.36) | collective-permute-done | bytes 196640 | tf_op jit(solution)/shard_map/ppermute | solution.py:253
  105.4 1.4 collective-permute-done.37.other
  106.8 3.9 %conv_back.5 = (bf16[64,1536]{1,0:T(8,128)(2,1)S(1)}, bf16[64,1536]{1,0:T(8,128)(2,1)S(1)}, bf16[64,1536]{1,0:T(8,128)(2,1)S(1)}, bf16[64,1536]{1,0:T(8,128)(2,1)S(1)}, bf16[2304,128]{1,0:T(8,128)(2,1)}) custom-call(bf16[64,1536]{1,0:T(8,128)(2,1)S(1)} %get-tuple-element.190.own, bf16[64,1536]{1,0:T(8,128)(2,1)S(1)} %collective-permute-done.37.other, ...), custom_call_target="tpu_custom_call" | custom-call | flops 5200000000 | bytes 5079040 | tf_op jit(solution)/shard_map/conv_back/pallas_call | solution.py:895
  110.8 1.3 collective-permute-start.39
  113.2 1.2 collective-permute-start.41
  114.3 2.5 %all-to-all-done.1 = bf16[4,576,128]{2,1,0:T(8,128)(2,1)S(1)} async-done(((bf16[4,576,128]{2,1,0:T(8,128)(2,1)}), bf16[4,576,128]{2,1,0:T(8,128)(2,1)S(1)}, u32[]{:S(2)}, u32[]{:S(2)}) %all-to-all-start.1) | async-done | bytes 589856 | tf_op jit(solution)/shard_map/all_to_all | solution.py:1097
  116.9 4.4 %all-to-all-start.2 = ((bf16[4,576,128]{2,1,0:T(8,128)(2,1)}), bf16[4,576,128]{2,1,0:T(8,128)(2,1)}, u32[]{:S(2)}, u32[]{:S(2)}) async-start(bf16[4,576,128]{2,1,0:T(8,128)(2,1)} %bitcast.32), calls=%async_computation.2 | async-start | bytes 1179648 | tf_op jit(solution)/shard_map/all_to_all | solution.py:1097
  123.0 2.0 %norm_back.4 = (bf16[64,1536]{1,0:T(8,128)(2,1)S(1)}, f32[64,128]{1,0:T(8,128)S(1)}) custom-call(bf16[64,1536]{1,0:T(8,128)(2,1)S(1)} %get-tuple-element.193.refs_0_, bf16[64,1536]{1,0:T(8,128)(2,1)S(1)} %collective-permute-done.39.refs_1_, bf16[64,1536]{1,0:T(8,128)(2,1)S(1)} %collective-permute-done.40.refs_2_, ...), custom_call_target="tpu_custom_call" | custom-call | bytes 1595392 | tf_op jit(solution)/shard_map/norm_back/pallas_call | solution.py:895
  125.1 1.4 collective-permute-done.42.other
  126.5 3.9 %conv_back.6 = (bf16[64,1536]{1,0:T(8,128)(2,1)S(1)}, bf16[64,1536]{1,0:T(8,128)(2,1)S(1)}, bf16[64,1536]{1,0:T(8,128)(2,1)S(1)}, bf16[64,1536]{1,0:T(8,128)(2,1)S(1)}, bf16[2304,128]{1,0:T(8,128)(2,1)}) custom-call(bf16[64,1536]{1,0:T(8,128)(2,1)S(1)} %get-tuple-element.205.own, bf16[64,1536]{1,0:T(8,128)(2,1)S(1)} %collective-permute-done.42.other, ...), custom_call_target="tpu_custom_call" | custom-call | flops 5200000000 | bytes 5079040 | tf_op jit(solution)/shard_map/conv_back/pallas_call | solution.py:895
  132.3 1.7 collective-permute-start.46
  134.0 2.4 %all-to-all-done.2 = bf16[4,576,128]{2,1,0:T(8,128)(2,1)} async-done(((bf16[4,576,128]{2,1,0:T(8,128)(2,1)}), bf16[4,576,128]{2,1,0:T(8,128)(2,1)}, u32[]{:S(2)}, u32[]{:S(2)}) %all-to-all-start.2) | async-done | bytes 589856 | tf_op jit(solution)/shard_map/all_to_all | solution.py:1097
  136.5 3.5 %all-to-all-start.3 = ((bf16[4,576,128]{2,1,0:T(8,128)(2,1)}), bf16[4,576,128]{2,1,0:T(8,128)(2,1)S(1)}, u32[]{:S(2)}, u32[]{:S(2)}) async-start(bf16[4,576,128]{2,1,0:T(8,128)(2,1)} %bitcast.31), calls=%async_computation.3 | async-start | bytes 1179648 | tf_op jit(solution)/shard_map/all_to_all | solution.py:1097
  141.1 1.1 collective-permute-done.46.refs_3_
  142.8 1.4 collective-permute-done.47.other
  144.3 3.9 %conv_back.7 = (bf16[64,1536]{1,0:T(8,128)(2,1)S(1)}, bf16[64,1536]{1,0:T(8,128)(2,1)S(1)}, bf16[64,1536]{1,0:T(8,128)(2,1)S(1)}, bf16[64,1536]{1,0:T(8,128)(2,1...) custom-call(bf16[64,1536]{1,0:T(8,128)(2,1)S(1)} %get-tuple-element., ...), custom_call_target="tpu_custom_call" | custom-call | flops 3000000000 | bytes 5128192 | tf_op jit(solution)/shard_map/conv_back/pallas_call | solution.py:895
  148.1 1.3 collective-permute-start.49
  150.5 1.2 collective-permute-start.61
  151.7 2.6 %collective-permute-start.51 = (bf16[592,128]{1,0:T(8,128)(2,1)}, bf16[592,128]{1,0:T(8,128)(2,1)S(1)}, u32[]{:S(2)}, u32[]{:S(2)}) collective-permute-start(bf16[592,128]{1,0:T(8,128)(2,1)} %get-tuple-element.228), channel_id=1, source_target_pairs={{0,4},{1,5},{2,6},{3,7},{4,0},{5,1},{6,2},{7,3},{8,12},{9,13},{10,... | collective-permute-start | bytes 454664 | tf_op jit(solution)/shard_map/ppermute | solution.py:253
  154.3 1.4 collective-permute-start.52
  155.9 1.6 collective-permute-start.50
  157.5 2.8 %collective-permute-done.60.refs_2_ = bf16[64,1536]{1,0:T(8,128)(2,1)S(1)} collective-permute-done((bf16[64,1536]{1,0:T(8,128)(2,1)S(1)}, bf16[64,1536]{1,0:T(8,128)(2,1)S(1)}, u32[]{:S(2)}, u32[]{:S(2)}) %collective-permute-start.60) | collective-permute-done | bytes 196640 | tf_op jit(solution)/shard_map/ppermute | solution.py:253
  161.4 1.2 input.1
  162.6 1.5 fold.1
  164.2 1.5 collective-permute-done.51.refs_2_
  168.1 4.2 %collective-permute-start.64 = (bf16[256,384]{1,0:T(8,128)(2,1)S(1)}, bf16[256,384]{1,0:T(8,128)(2,1)S(1)}, u32[]{:S(2)}, u32[]{:S(2)}) collective-permute-start(bf16[256,384]{1,0:T(8,128)(2,1)S(1)} %get-tuple-element.253), channel_id=1, source_target_pairs={{0,2},{1,7},{2,10},{3,15},{4,18},{5,23},{6,26},{7,31},{8,0},{9,5},... | collective-permute-start | bytes 589832 | tf_op jit(solution)/shard_map/ppermute | solution.py:253
  172.3 3.7 %collective-permute-start.54 = (bf16[592,128]{1,0:T(8,128)(2,1)S(1)}, bf16[592,128]{1,0:T(8,128)(2,1)S(1)}, u32[]{:S(2)}, u32[]{:S(2)}) collective-permute-start(bf16[592,128]{1,0:T(8,128)(2,1)S(1)} %get-tuple-element.240), channel_id=1, source_target_pairs={{0,16},{1,17},{2,18},{3,19},{4,20},{5,21},{6,22},{7,23},{8,24},{9,... | collective-permute-start | bytes 454664 | tf_op jit(solution)/shard_map/ppermute | solution.py:253
  176.4 9.0 %collective-permute-done.54.refs_2_ = bf16[592,128]{1,0:T(8,128)(2,1)S(1)} collective-permute-done((bf16[592,128]{1,0:T(8,128)(2,1)S(1)}, bf16[592,128]{1,0:T(8,128)(2,1)S(1)}, u32[]{:S(2)}, u32[]{:S(2)}) %collective-permute-start.54) | collective-permute-done | bytes 151584 | tf_op jit(solution)/shard_map/ppermute | solution.py:253
  188.0 1.9 %outputs.1 = (f32[9,64,512]{2,1,0:T(8,128)}, f32[1,64]{1,0:T(1,128)}, f32[1,64]{1,0:T(1,128)}, bf16[192,512]{1,0:T(8,128)(2,1)}, bf16[192,512]{1,0:T(8,128)(2,1)}) custom-call(bf16[592,128]{1,0:T(8,128)(2,1)S(1)} %get-tuple-element.238.refs_0_, bf16[592,128]{1,0:T(8,128)(2,1)S(1)} %collective-permute-done.53.refs_1_, ...), custom_call_target="tpu_custom_call" | custom-call | bytes 3736064 | tf_op jit(solution)/shard_map/outputs/pallas_call | solution.py:895
  (133 shorter events, 29.3 us)
Async XLA Ops:
  3.1 24.4 %collective-permute-start.7 = (bf16[592,512]{1,0:T(8,128)(2,1)S(1)}, bf16[592,512]{1,0:T(8,128)(2,1)S(1)}, u32[]{:S(2)}, u32[]{:S(2)}) collective-permute-start(bf16[592,512]{1,0:T(8,128)(2,1)S(1)} %get-tuple-element.134), channel_id=1, source_target_pairs={{0,8},{1,9},{2,10},{3,11},{4,12},{5,13},{6,14},{7,15},{8,0},{9,1},... | collective-permute-start | bytes 1818632 | tf_op jit(solution)/shard_map/ppermute | solution.py:253
  6.2 28.1 %collective-permute-start.8 = (bf16[592,512]{1,0:T(8,128)(2,1)S(1)}, bf16[592,512]{1,0:T(8,128)(2,1)S(1)}, u32[]{:S(2)}, u32[]{:S(2)}) collective-permute-start(bf16[592,512]{1,0:T(8,128)(2,1)S(1)} %get-tuple-element.135), channel_id=1, source_target_pairs={{0,16},{1,17},{2,18},{3,19},{4,20},{5,21},{6,22},{7,23},{8,24},{9,... | collective-permute-start | bytes 1818632 | tf_op jit(solution)/shard_map/ppermute | solution.py:253
  9.1 10.8 %collective-permute-start = (bf16[208,512]{1,0:T(8,128)(2,1)S(1)}, bf16[208,512]{1,0:T(8,128)(2,1)S(1)}, u32[]{:S(2)}, u32[]{:S(2)}) collective-permute-start(bf16[208,512]{1,0:T(8,128)(2,1)S(1)} %get-tuple-element.139), channel_id=1, source_target_pairs={{0,2},{1,3},{2,0},{3,1},{4,6},{5,7},{6,4},{7,5},{8,10},{9,11},{10,... | collective-permute-start | bytes 638984 | tf_op jit(solution)/shard_map/ppermute | solution.py:253
  10.7 23.6 %collective-permute-start.9 = (bf16[592,512]{1,0:T(8,128)(2,1)S(1)}, bf16[592,512]{1,0:T(8,128)(2,1)S(1)}, u32[]{:S(2)}, u32[]{:S(2)}) collective-permute-start(bf16[592,512]{1,0:T(8,128)(2,1)S(1)} %get-tuple-element.136), channel_id=1, source_target_pairs={{0,24},{1,25},{2,26},{3,27},{4,28},{5,29},{6,30},{7,31},{8,16},{9,... | collective-permute-start | bytes 1818632 | tf_op jit(solution)/shard_map/ppermute | solution.py:253
  11.2 13.9 %collective-permute-start.1 = (bf16[208,512]{1,0:T(8,128)(2,1)S(1)}, bf16[208,512]{1,0:T(8,128)(2,1)S(1)}, u32[]{:S(2)}, u32[]{:S(2)}) collective-permute-start(bf16[208,512]{1,0:T(8,128)(2,1)S(1)} %get-tuple-element.140), channel_id=1, source_target_pairs={{0,4},{1,5},{2,6},{3,7},{4,0},{5,1},{6,2},{7,3},{8,12},{9,13},{10,... | collective-permute-start | bytes 638984 | tf_op jit(solution)/shard_map/ppermute | solution.py:253
  19.8 7.8 %collective-permute-start.2 = (bf16[208,512]{1,0:T(8,128)(2,1)S(1)}, bf16[208,512]{1,0:T(8,128)(2,1)S(1)}, u32[]{:S(2)}, u32[]{:S(2)}) collective-permute-start(bf16[208,512]{1,0:T(8,128)(2,1)S(1)} %get-tuple-element.141), channel_id=1, source_target_pairs={{0,6},{1,7},{2,4},{3,5},{4,2},{5,3},{6,0},{7,1},{8,14},{9,15},{10,... | collective-permute-start | bytes 638984 | tf_op jit(solution)/shard_map/ppermute | solution.py:253
  25.1 9.2 %collective-permute-start.3 = (bf16[208,512]{1,0:T(8,128)(2,1)S(1)}, bf16[208,512]{1,0:T(8,128)(2,1)S(1)}, u32[]{:S(2)}, u32[]{:S(2)}) collective-permute-start(bf16[208,512]{1,0:T(8,128)(2,1)S(1)} %get-tuple-element.138.refs_0_), channel_id=1, source_target_pairs={{0,1},{1,0},{2,3},{3,2},{4,5},{5,4},{6,7},{7,6},{8,9},{9,8},{10,11... | collective-permute-start | bytes 638984 | tf_op jit(solution)/shard_map/ppermute | solution.py:253
  27.6 6.8 %collective-permute-start.4 = (bf16[208,512]{1,0:T(8,128)(2,1)S(1)}, bf16[208,512]{1,0:T(8,128)(2,1)S(1)}, u32[]{:S(2)}, u32[]{:S(2)}) collective-permute-start(bf16[208,512]{1,0:T(8,128)(2,1)S(1)} %collective-permute-done.refs_1_), channel_id=1, source_target_pairs={{0,1},{1,0},{2,3},{3,2},{4,5},{5,4},{6,7},{7,6},{8,9},{9,8},{10,11... | collective-permute-start | bytes 638984 | tf_op jit(solution)/shard_map/ppermute | solution.py:253
  27.6 6.8 %collective-permute-start.5 = (bf16[208,512]{1,0:T(8,128)(2,1)S(1)}, bf16[208,512]{1,0:T(8,128)(2,1)S(1)}, u32[]{:S(2)}, u32[]{:S(2)}) collective-permute-start(bf16[208,512]{1,0:T(8,128)(2,1)S(1)} %collective-permute-done.1.refs_2_), channel_id=1, source_target_pairs={{0,1},{1,0},{2,3},{3,2},{4,5},{5,4},{6,7},{7,6},{8,9},{9,8},{10,11... | collective-permute-start | bytes 638984 | tf_op jit(solution)/shard_map/ppermute | solution.py:253
  34.3 1.5 collective-permute-start.6
  38.4 10.4 %collective-permute-start.12 = (bf16[64,1536]{1,0:T(8,128)(2,1)S(1)}, bf16[64,1536]{1,0:T(8,128)(2,1)S(1)}, u32[]{:S(2)}, u32[]{:S(2)}) collective-permute-start(bf16[64,1536]{1,0:T(8,128)(2,1)S(1)} %get-tuple-element.148.refs_0_), channel_id=1, source_target_pairs={{0,24},{1,25},{2,26},{3,27},{4,28},{5,29},{6,30},{7,31},{8,16},{9,... | collective-permute-start | bytes 589832 | tf_op jit(solution)/shard_map/ppermute | solution.py:253
  39.9 10.7 %collective-permute-start.10 = (bf16[64,1536]{1,0:T(8,128)(2,1)S(1)}, bf16[64,1536]{1,0:T(8,128)(2,1)S(1)}, u32[]{:S(2)}, u32[]{:S(2)}) collective-permute-start(bf16[64,1536]{1,0:T(8,128)(2,1)S(1)} %get-tuple-element.148.refs_0_), channel_id=1, source_target_pairs={{0,8},{1,9},{2,10},{3,11},{4,12},{5,13},{6,14},{7,15},{8,0},{9,1},... | collective-permute-start | bytes 589832 | tf_op jit(solution)/shard_map/ppermute | solution.py:253
  41.4 9.2 %collective-permute-start.11 = (bf16[64,1536]{1,0:T(8,128)(2,1)S(1)}, bf16[64,1536]{1,0:T(8,128)(2,1)S(1)}, u32[]{:S(2)}, u32[]{:S(2)}) collective-permute-start(bf16[64,1536]{1,0:T(8,128)(2,1)S(1)} %get-tuple-element.148.refs_0_), channel_id=1, source_target_pairs={{0,16},{1,17},{2,18},{3,19},{4,20},{5,21},{6,22},{7,23},{8,24},{9,... | collective-permute-start | bytes 589832 | tf_op jit(solution)/shard_map/ppermute | solution.py:253
  41.9 9.2 %collective-permute-start.13 = (bf16[64,1536]{1,0:T(8,128)(2,1)S(1)}, bf16[64,1536]{1,0:T(8,128)(2,1)S(1)}, u32[]{:S(2)}, u32[]{:S(2)}) collective-permute-start(bf16[64,1536]{1,0:T(8,128)(2,1)S(1)} %get-tuple-element.148.refs_0_), channel_id=1, source_target_pairs={{0,1},{1,0},{2,3},{3,2},{4,5},{5,4},{6,7},{7,6},{8,9},{9,8},{10,11... | collective-permute-start | bytes 589832 | tf_op jit(solution)/shard_map/ppermute | solution.py:253
  48.8 2.3 %collective-permute-start.16 = (bf16[64,1536]{1,0:T(8,128)(2,1)S(1)}, bf16[64,1536]{1,0:T(8,128)(2,1)S(1)}, u32[]{:S(2)}, u32[]{:S(2)}) collective-permute-start(bf16[64,1536]{1,0:T(8,128)(2,1)S(1)} %collective-permute-done.12.refs_3_), channel_id=1, source_target_pairs={{0,1},{1,0},{2,3},{3,2},{4,5},{5,4},{6,7},{7,6},{8,9},{9,8},{10,11... | collective-permute-start | bytes 589832 | tf_op jit(solution)/shard_map/ppermute | solution.py:253
  50.6 1.7 collective-permute-start.15
  55.4 9.5 %collective-permute-start.19 = (bf16[64,1536]{1,0:T(8,128)(2,1)S(1)}, bf16[64,1536]{1,0:T(8,128)(2,1)S(1)}, u32[]{:S(2)}, u32[]{:S(2)}) collective-permute-start(bf16[64,1536]{1,0:T(8,128)(2,1)S(1)} %get-tuple-element.161.refs_0_), channel_id=1, source_target_pairs={{0,24},{1,25},{2,26},{3,27},{4,28},{5,29},{6,30},{7,31},{8,16},{9,... | collective-permute-start | bytes 589832 | tf_op jit(solution)/shard_map/ppermute | solution.py:253
  56.5 10.7 %collective-permute-start.17 = (bf16[64,1536]{1,0:T(8,128)(2,1)S(1)}, bf16[64,1536]{1,0:T(8,128)(2,1)S(1)}, u32[]{:S(2)}, u32[]{:S(2)}) collective-permute-start(bf16[64,1536]{1,0:T(8,128)(2,1)S(1)} %get-tuple-element.161.refs_0_), channel_id=1, source_target_pairs={{0,8},{1,9},{2,10},{3,11},{4,12},{5,13},{6,14},{7,15},{8,0},{9,1},... | collective-permute-start | bytes 589832 | tf_op jit(solution)/shard_map/ppermute | solution.py:253
  58.0 9.6 %collective-permute-start.18 = (bf16[64,1536]{1,0:T(8,128)(2,1)S(1)}, bf16[64,1536]{1,0:T(8,128)(2,1)S(1)}, u32[]{:S(2)}, u32[]{:S(2)}) collective-permute-start(bf16[64,1536]{1,0:T(8,128)(2,1)S(1)} %get-tuple-element.161.refs_0_), channel_id=1, source_target_pairs={{0,16},{1,17},{2,18},{3,19},{4,20},{5,21},{6,22},{7,23},{8,24},{9,... | collective-permute-start | bytes 589832 | tf_op jit(solution)/shard_map/ppermute | solution.py:253
  58.9 8.8 %collective-permute-start.20 = (bf16[64,1536]{1,0:T(8,128)(2,1)S(1)}, bf16[64,1536]{1,0:T(8,128)(2,1)S(1)}, u32[]{:S(2)}, u32[]{:S(2)}) collective-permute-start(bf16[64,1536]{1,0:T(8,128)(2,1)S(1)} %get-tuple-element.161.refs_0_), channel_id=1, source_target_pairs={{0,1},{1,0},{2,3},{3,2},{4,5},{5,4},{6,7},{7,6},{8,9},{9,8},{10,11... | collective-permute-start | bytes 589832 | tf_op jit(solution)/shard_map/ppermute | solution.py:253
  58.9 16.1 %all-to-all-start = ((bf16[4,192,128]{2,1,0:T(8,128)(2,1)}), bf16[4,192,128]{2,1,0:T(8,128)(2,1)S(1)}, u32[]{:S(2)}, u32[]{:S(2)}) async-start(bf16[4,192,128]{2,1,0:T(8,128)(2,1)} %bitcast.7), calls=%async_computation | async-start | bytes 393216 | tf_op jit(solution)/shard_map/all_to_all | solution.py:1025
  64.9 2.8 %collective-permute-start.23 = (bf16[64,1536]{1,0:T(8,128)(2,1)S(1)}, bf16[64,1536]{1,0:T(8,128)(2,1)S(1)}, u32[]{:S(2)}, u32[]{:S(2)}) collective-permute-start(bf16[64,1536]{1,0:T(8,128)(2,1)S(1)} %collective-permute-done.19.refs_3_), channel_id=1, source_target_pairs={{0,1},{1,0},{2,3},{3,2},{4,5},{5,4},{6,7},{7,6},{8,9},{9,8},{10,11... | collective-permute-start | bytes 589832 | tf_op jit(solution)/shard_map/ppermute | solution.py:253
  71.5 8.8 %collective-permute-start.26 = (bf16[64,1536]{1,0:T(8,128)(2,1)S(1)}, bf16[64,1536]{1,0:T(8,128)(2,1)S(1)}, u32[]{:S(2)}, u32[]{:S(2)}) collective-permute-start(bf16[64,1536]{1,0:T(8,128)(2,1)S(1)} %get-tuple-element.167.refs_0_), channel_id=1, source_target_pairs={{0,24},{1,25},{2,26},{3,27},{4,28},{5,29},{6,30},{7,31},{8,16},{9,... | collective-permute-start | bytes 589832 | tf_op jit(solution)/shard_map/ppermute | solution.py:253
  72.6 10.7 %collective-permute-start.24 = (bf16[64,1536]{1,0:T(8,128)(2,1)S(1)}, bf16[64,1536]{1,0:T(8,128)(2,1)S(1)}, u32[]{:S(2)}, u32[]{:S(2)}) collective-permute-start(bf16[64,1536]{1,0:T(8,128)(2,1)S(1)} %get-tuple-element.167.refs_0_), channel_id=1, source_target_pairs={{0,8},{1,9},{2,10},{3,11},{4,12},{5,13},{6,14},{7,15},{8,0},{9,1},... | collective-permute-start | bytes 589832 | tf_op jit(solution)/shard_map/ppermute | solution.py:253
  74.1 9.6 %collective-permute-start.25 = (bf16[64,1536]{1,0:T(8,128)(2,1)S(1)}, bf16[64,1536]{1,0:T(8,128)(2,1)S(1)}, u32[]{:S(2)}, u32[]{:S(2)}) collective-permute-start(bf16[64,1536]{1,0:T(8,128)(2,1)S(1)} %get-tuple-element.167.refs_0_), channel_id=1, source_target_pairs={{0,16},{1,17},{2,18},{3,19},{4,20},{5,21},{6,22},{7,23},{8,24},{9,... | collective-permute-start | bytes 589832 | tf_op jit(solution)/shard_map/ppermute | solution.py:253
  75.1 1.7 collective-permute-start.27
  75.2 9.0 %collective-permute-start.28 = (bf16[64,1536]{1,0:T(8,128)(2,1)S(1)}, bf16[64,1536]{1,0:T(8,128)(2,1)S(1)}, u32[]{:S(2)}, u32[]{:S(2)}) collective-permute-start(bf16[64,1536]{1,0:T(8,128)(2,1)S(1)} %get-tuple-element.167.refs_0_), channel_id=1, source_target_pairs={{0,1},{1,0},{2,3},{3,2},{4,5},{5,4},{6,7},{7,6},{8,9},{9,8},{10,11... | collective-permute-start | bytes 589832 | tf_op jit(solution)/shard_map/ppermute | solution.py:253
  80.3 3.9 %collective-permute-start.31 = (bf16[64,1536]{1,0:T(8,128)(2,1)S(1)}, bf16[64,1536]{1,0:T(8,128)(2,1)S(1)}, u32[]{:S(2)}, u32[]{:S(2)}) collective-permute-start(bf16[64,1536]{1,0:T(8,128)(2,1)S(1)} %collective-permute-done.26.refs_3_), channel_id=1, source_target_pairs={{0,1},{1,0},{2,3},{3,2},{4,5},{5,4},{6,7},{7,6},{8,9},{9,8},{10,11... | collective-permute-start | bytes 589832 | tf_op jit(solution)/shard_map/ppermute | solution.py:253
  83.8 4.1 %collective-permute-start.33 = (bf16[256,640]{1,0:T(8,128)(2,1)S(1)}, bf16[256,640]{1,0:T(8,128)(2,1)S(1)}, u32[]{:S(2)}, u32[]{:S(2)}) collective-permute-start(bf16[256,640]{1,0:T(8,128)(2,1)S(1)} %copy-done.11), channel_id=1, source_target_pairs={{0,1},{1,0},{2,3},{3,2},{4,5},{5,4},{6,7},{7,6},{8,9},{9,8},{10,11... | collective-permute-start | bytes 983048 | tf_op jit(solution)/shard_map/ppermute | solution.py:253
  87.6 1.5 collective-permute-start.32
  93.1 9.5 %collective-permute-start.34 = (bf16[64,1536]{1,0:T(8,128)(2,1)S(1)}, bf16[64,1536]{1,0:T(8,128)(2,1)S(1)}, u32[]{:S(2)}, u32[]{:S(2)}) collective-permute-start(bf16[64,1536]{1,0:T(8,128)(2,1)S(1)} %get-tuple-element.179), channel_id=1, source_target_pairs={{0,8},{1,9},{2,10},{3,11},{4,12},{5,13},{6,14},{7,15},{8,0},{9,1},... | collective-permute-start | bytes 589832 | tf_op jit(solution)/shard_map/ppermute | solution.py:253
  93.7 8.9 %collective-permute-start.35 = (bf16[64,1536]{1,0:T(8,128)(2,1)S(1)}, bf16[64,1536]{1,0:T(8,128)(2,1)S(1)}, u32[]{:S(2)}, u32[]{:S(2)}) collective-permute-start(bf16[64,1536]{1,0:T(8,128)(2,1)S(1)} %get-tuple-element.180), channel_id=1, source_target_pairs={{0,16},{1,17},{2,18},{3,19},{4,20},{5,21},{6,22},{7,23},{8,24},{9,... | collective-permute-start | bytes 589832 | tf_op jit(solution)/shard_map/ppermute | solution.py:253
  94.7 10.1 %collective-permute-start.36 = (bf16[64,1536]{1,0:T(8,128)(2,1)S(1)}, bf16[64,1536]{1,0:T(8,128)(2,1)S(1)}, u32[]{:S(2)}, u32[]{:S(2)}) collective-permute-start(bf16[64,1536]{1,0:T(8,128)(2,1)S(1)} %get-tuple-element.181), channel_id=1, source_target_pairs={{0,24},{1,25},{2,26},{3,27},{4,28},{5,29},{6,30},{7,31},{8,16},{9,... | collective-permute-start | bytes 589832 | tf_op jit(solution)/shard_map/ppermute | solution.py:253
  96.6 20.2 %all-to-all-start.1 = ((bf16[4,576,128]{2,1,0:T(8,128)(2,1)}), bf16[4,576,128]{2,1,0:T(8,128)(2,1)S(1)}, u32[]{:S(2)}, u32[]{:S(2)}) async-start(bf16[4,576,128]{2,1,0:T(8,128)(2,1)} %bitcast.33), calls=%async_computation.1 | async-start | bytes 1179648 | tf_op jit(solution)/shard_map/all_to_all | solution.py:1097
  101.5 3.9 %collective-permute-start.38 = (bf16[256,640]{1,0:T(8,128)(2,1)S(1)}, bf16[256,640]{1,0:T(8,128)(2,1)S(1)}, u32[]{:S(2)}, u32[]{:S(2)}) collective-permute-start(bf16[256,640]{1,0:T(8,128)(2,1)S(1)} %copy-done.10), channel_id=1, source_target_pairs={{0,1},{1,0},{2,3},{3,2},{4,5},{5,4},{6,7},{7,6},{8,9},{9,8},{10,11... | collective-permute-start | bytes 983048 | tf_op jit(solution)/shard_map/ppermute | solution.py:253
  105.3 1.5 collective-permute-start.37
  110.8 11.6 %collective-permute-start.39 = (bf16[64,1536]{1,0:T(8,128)(2,1)S(1)}, bf16[64,1536]{1,0:T(8,128)(2,1)S(1)}, u32[]{:S(2)}, u32[]{:S(2)}) collective-permute-start(bf16[64,1536]{1,0:T(8,128)(2,1)S(1)} %get-tuple-element.194), channel_id=1, source_target_pairs={{0,8},{1,9},{2,10},{3,11},{4,12},{5,13},{6,14},{7,15},{8,0},{9,1},... | collective-permute-start | bytes 589832 | tf_op jit(solution)/shard_map/ppermute | solution.py:253
  112.1 10.9 %collective-permute-start.40 = (bf16[64,1536]{1,0:T(8,128)(2,1)S(1)}, bf16[64,1536]{1,0:T(8,128)(2,1)S(1)}, u32[]{:S(2)}, u32[]{:S(2)}) collective-permute-start(bf16[64,1536]{1,0:T(8,128)(2,1)S(1)} %get-tuple-element.195), channel_id=1, source_target_pairs={{0,16},{1,17},{2,18},{3,19},{4,20},{5,21},{6,22},{7,23},{8,24},{9,... | collective-permute-start | bytes 589832 | tf_op jit(solution)/shard_map/ppermute | solution.py:253
  113.2 9.8 %collective-permute-start.41 = (bf16[64,1536]{1,0:T(8,128)(2,1)S(1)}, bf16[64,1536]{1,0:T(8,128)(2,1)S(1)}, u32[]{:S(2)}, u32[]{:S(2)}) collective-permute-start(bf16[64,1536]{1,0:T(8,128)(2,1)S(1)} %get-tuple-element.196), channel_id=1, source_target_pairs={{0,24},{1,25},{2,26},{3,27},{4,28},{5,29},{6,30},{7,31},{8,16},{9,... | collective-permute-start | bytes 589832 | tf_op jit(solution)/shard_map/ppermute | solution.py:253
  116.9 19.6 %all-to-all-start.2 = ((bf16[4,576,128]{2,1,0:T(8,128)(2,1)}), bf16[4,576,128]{2,1,0:T(8,128)(2,1)}, u32[]{:S(2)}, u32[]{:S(2)}) async-start(bf16[4,576,128]{2,1,0:T(8,128)(2,1)} %bitcast.32), calls=%async_computation.2 | async-start | bytes 1179648 | tf_op jit(solution)/shard_map/all_to_all | solution.py:1097
  121.3 3.9 %collective-permute-start.43 = (bf16[256,640]{1,0:T(8,128)(2,1)S(1)}, bf16[256,640]{1,0:T(8,128)(2,1)S(1)}, u32[]{:S(2)}, u32[]{:S(2)}) collective-permute-start(bf16[256,640]{1,0:T(8,128)(2,1)S(1)} %copy-done.9), channel_id=1, source_target_pairs={{0,1},{1,0},{2,3},{3,2},{4,5},{5,4},{6,7},{7,6},{8,9},{9,8},{10,11... | collective-permute-start | bytes 983048 | tf_op jit(solution)/shard_map/ppermute | solution.py:253
  125.0 1.5 collective-permute-start.42
  130.5 10.6 %collective-permute-start.44 = (bf16[64,1536]{1,0:T(8,128)(2,1)S(1)}, bf16[64,1536]{1,0:T(8,128)(2,1)S(1)}, u32[]{:S(2)}, u32[]{:S(2)}) collective-permute-start(bf16[64,1536]{1,0:T(8,128)(2,1)S(1)} %get-tuple-element.209), channel_id=1, source_target_pairs={{0,8},{1,9},{2,10},{3,11},{4,12},{5,13},{6,14},{7,15},{8,0},{9,1},... | collective-permute-start | bytes 589832 | tf_op jit(solution)/shard_map/ppermute | solution.py:253
  131.3 9.8 %collective-permute-start.45 = (bf16[64,1536]{1,0:T(8,128)(2,1)S(1)}, bf16[64,1536]{1,0:T(8,128)(2,1)S(1)}, u32[]{:S(2)}, u32[]{:S(2)}) collective-permute-start(bf16[64,1536]{1,0:T(8,128)(2,1)S(1)} %get-tuple-element.210), channel_id=1, source_target_pairs={{0,16},{1,17},{2,18},{3,19},{4,20},{5,21},{6,22},{7,23},{8,24},{9,... | collective-permute-start | bytes 589832 | tf_op jit(solution)/shard_map/ppermute | solution.py:253
  132.3 9.9 %collective-permute-start.46 = (bf16[64,1536]{1,0:T(8,128)(2,1)S(1)}, bf16[64,1536]{1,0:T(8,128)(2,1)S(1)}, u32[]{:S(2)}, u32[]{:S(2)}) collective-permute-start(bf16[64,1536]{1,0:T(8,128)(2,1)S(1)} %get-tuple-element.211), channel_id=1, source_target_pairs={{0,24},{1,25},{2,26},{3,27},{4,28},{5,29},{6,30},{7,31},{8,16},{9,... | collective-permute-start | bytes 589832 | tf_op jit(solution)/shard_map/ppermute | solution.py:253
  136.5 24.9 %all-to-all-start.3 = ((bf16[4,576,128]{2,1,0:T(8,128)(2,1)}), bf16[4,576,128]{2,1,0:T(8,128)(2,1)S(1)}, u32[]{:S(2)}, u32[]{:S(2)}) async-start(bf16[4,576,128]{2,1,0:T(8,128)(2,1)} %bitcast.31), calls=%async_computation.3 | async-start | bytes 1179648 | tf_op jit(solution)/shard_map/all_to_all | solution.py:1097
  140.0 2.8 %collective-permute-start.48 = (bf16[256,640]{1,0:T(8,128)(2,1)S(1)}, bf16[256,640]{1,0:T(8,128)(2,1)S(1)}, u32[]{:S(2)}, u32[]{:S(2)}) collective-permute-start(bf16[256,640]{1,0:T(8,128)(2,1)S(1)} %copy-done.8), channel_id=1, source_target_pairs={{0,1},{1,0},{2,3},{3,2},{4,5},{5,4},{6,7},{7,6},{8,9},{9,8},{10,11... | collective-permute-start | bytes 983048 | tf_op jit(solution)/shard_map/ppermute | solution.py:253
  142.7 1.5 collective-permute-start.47
  148.1 7.8 %collective-permute-start.49 = (bf16[64,1536]{1,0:T(8,128)(2,1)S(1)}, bf16[64,1536]{1,0:T(8,128)(2,1)S(1)}, u32[]{:S(2)}, u32[]{:S(2)}) collective-permute-start(bf16[64,1536]{1,0:T(8,128)(2,1)S(1)} %get-tuple-element.226), channel_id=1, source_target_pairs={{0,8},{1,9},{2,10},{3,11},{4,12},{5,13},{6,14},{7,15},{8,0},{9,1},... | collective-permute-start | bytes 589832 | tf_op jit(solution)/shard_map/ppermute | solution.py:253
  149.5 10.9 %collective-permute-start.60 = (bf16[64,1536]{1,0:T(8,128)(2,1)S(1)}, bf16[64,1536]{1,0:T(8,128)(2,1)S(1)}, u32[]{:S(2)}, u32[]{:S(2)}) collective-permute-start(bf16[64,1536]{1,0:T(8,128)(2,1)S(1)} %get-tuple-element.243), channel_id=1, source_target_pairs={{0,16},{1,17},{2,18},{3,19},{4,20},{5,21},{6,22},{7,23},{8,24},{9,... | collective-permute-start | bytes 589832 | tf_op jit(solution)/shard_map/ppermute | solution.py:253
  150.5 9.8 %collective-permute-start.61 = (bf16[64,1536]{1,0:T(8,128)(2,1)S(1)}, bf16[64,1536]{1,0:T(8,128)(2,1)S(1)}, u32[]{:S(2)}, u32[]{:S(2)}) collective-permute-start(bf16[64,1536]{1,0:T(8,128)(2,1)S(1)} %get-tuple-element.244), channel_id=1, source_target_pairs={{0,24},{1,25},{2,26},{3,27},{4,28},{5,29},{6,30},{7,31},{8,16},{9,... | collective-permute-start | bytes 589832 | tf_op jit(solution)/shard_map/ppermute | solution.py:253
  151.7 13.9 %collective-permute-start.51 = (bf16[592,128]{1,0:T(8,128)(2,1)}, bf16[592,128]{1,0:T(8,128)(2,1)S(1)}, u32[]{:S(2)}, u32[]{:S(2)}) collective-permute-start(bf16[592,128]{1,0:T(8,128)(2,1)} %get-tuple-element.228), channel_id=1, source_target_pairs={{0,4},{1,5},{2,6},{3,7},{4,0},{5,1},{6,2},{7,3},{8,12},{9,13},{10,... | collective-permute-start | bytes 454664 | tf_op jit(solution)/shard_map/ppermute | solution.py:253
  154.3 11.4 %collective-permute-start.52 = (bf16[592,128]{1,0:T(8,128)(2,1)}, bf16[592,128]{1,0:T(8,128)(2,1)S(1)}, u32[]{:S(2)}, u32[]{:S(2)}) collective-permute-start(bf16[592,128]{1,0:T(8,128)(2,1)} %get-tuple-element.229), channel_id=1, source_target_pairs={{0,6},{1,7},{2,4},{3,5},{4,2},{5,3},{6,0},{7,1},{8,14},{9,15},{10,... | collective-permute-start | bytes 454664 | tf_op jit(solution)/shard_map/ppermute | solution.py:253
  155.9 10.6 %collective-permute-start.50 = (bf16[592,128]{1,0:T(8,128)(2,1)}, bf16[592,128]{1,0:T(8,128)(2,1)S(1)}, u32[]{:S(2)}, u32[]{:S(2)}) collective-permute-start(bf16[592,128]{1,0:T(8,128)(2,1)} %get-tuple-element.227), channel_id=1, source_target_pairs={{0,2},{1,3},{2,0},{3,1},{4,6},{5,7},{6,4},{7,5},{8,10},{9,11},{10,... | collective-permute-start | bytes 454664 | tf_op jit(solution)/shard_map/ppermute | solution.py:253
  162.6 4.9 %collective-permute-start.62 = (bf16[256,384]{1,0:T(8,128)(2,1)S(1)}, bf16[256,384]{1,0:T(8,128)(2,1)S(1)}, u32[]{:S(2)}, u32[]{:S(2)}) collective-permute-start(bf16[256,384]{1,0:T(8,128)(2,1)S(1)} %get-tuple-element.251), channel_id=1, source_target_pairs={{0,1},{1,0},{2,3},{3,2},{4,5},{5,4},{6,7},{7,6},{8,9},{9,8},{10,11... | collective-permute-start | bytes 589832 | tf_op jit(solution)/shard_map/ppermute | solution.py:253
  166.7 9.5 %collective-permute-start.53 = (bf16[592,128]{1,0:T(8,128)(2,1)S(1)}, bf16[592,128]{1,0:T(8,128)(2,1)S(1)}, u32[]{:S(2)}, u32[]{:S(2)}) collective-permute-start(bf16[592,128]{1,0:T(8,128)(2,1)S(1)} %get-tuple-element.239), channel_id=1, source_target_pairs={{0,8},{1,9},{2,10},{3,11},{4,12},{5,13},{6,14},{7,15},{8,0},{9,1},... | collective-permute-start | bytes 454664 | tf_op jit(solution)/shard_map/ppermute | solution.py:253
  167.4 18.5 %collective-permute-start.63 = (bf16[256,384]{1,0:T(8,128)(2,1)S(1)}, bf16[256,384]{1,0:T(8,128)(2,1)S(1)}, u32[]{:S(2)}, u32[]{:S(2)}) collective-permute-start(bf16[256,384]{1,0:T(8,128)(2,1)S(1)} %get-tuple-element.252), channel_id=1, source_target_pairs={{0,0},{1,5},{2,8},{3,13},{4,16},{5,21},{6,24},{7,29},{8,2},{9,7},{... | collective-permute-start | bytes 589832 | tf_op jit(solution)/shard_map/ppermute | solution.py:253
  168.1 17.9 %collective-permute-start.64 = (bf16[256,384]{1,0:T(8,128)(2,1)S(1)}, bf16[256,384]{1,0:T(8,128)(2,1)S(1)}, u32[]{:S(2)}, u32[]{:S(2)}) collective-permute-start(bf16[256,384]{1,0:T(8,128)(2,1)S(1)} %get-tuple-element.253), channel_id=1, source_target_pairs={{0,2},{1,7},{2,10},{3,15},{4,18},{5,23},{6,26},{7,31},{8,0},{9,5},... | collective-permute-start | bytes 589832 | tf_op jit(solution)/shard_map/ppermute | solution.py:253
  172.3 13.2 %collective-permute-start.54 = (bf16[592,128]{1,0:T(8,128)(2,1)S(1)}, bf16[592,128]{1,0:T(8,128)(2,1)S(1)}, u32[]{:S(2)}, u32[]{:S(2)}) collective-permute-start(bf16[592,128]{1,0:T(8,128)(2,1)S(1)} %get-tuple-element.240), channel_id=1, source_target_pairs={{0,16},{1,17},{2,18},{3,19},{4,20},{5,21},{6,22},{7,23},{8,24},{9,... | collective-permute-start | bytes 454664 | tf_op jit(solution)/shard_map/ppermute | solution.py:253
  176.0 9.5 %collective-permute-start.55 = (bf16[592,128]{1,0:T(8,128)(2,1)S(1)}, bf16[592,128]{1,0:T(8,128)(2,1)S(1)}, u32[]{:S(2)}, u32[]{:S(2)}) collective-permute-start(bf16[592,128]{1,0:T(8,128)(2,1)S(1)} %get-tuple-element.241), channel_id=1, source_target_pairs={{0,24},{1,25},{2,26},{3,27},{4,28},{5,29},{6,30},{7,31},{8,16},{9,... | collective-permute-start | bytes 454664 | tf_op jit(solution)/shard_map/ppermute | solution.py:253
  176.3 10.3 %collective-permute-start.56 = (bf16[592,128]{1,0:T(8,128)(2,1)S(1)}, bf16[592,128]{1,0:T(8,128)(2,1)S(1)}, u32[]{:S(2)}, u32[]{:S(2)}) collective-permute-start(bf16[592,128]{1,0:T(8,128)(2,1)S(1)} %get-tuple-element.238.refs_0_), channel_id=1, source_target_pairs={{0,1},{1,0},{2,3},{3,2},{4,5},{5,4},{6,7},{7,6},{8,9},{9,8},{10,11... | collective-permute-start | bytes 454664 | tf_op jit(solution)/shard_map/ppermute | solution.py:253
  185.5 1.5 collective-permute-start.58
  186.1 1.6 collective-permute-start.65
  186.5 1.4 collective-permute-start.66
  (19 other events, 173.1 us)

commit v9 on v8

--- a/solution.py
+++ b/solution.py
@@ -10,7 +10,7 @@
 from jax.sharding import PartitionSpec as P
 
 CONVS = 2
-BACK_FLOPS = (3 * 10**9, 52 * 10**8, 52 * 10**8, 0)
+BACK_FLOPS = (4 * 10**9, 52 * 10**8, 52 * 10**8, 0)
 PICK_FLOPS = 2 * 10**9
 COT_LAYER = 2
 INPUT_FLOPS = 0 * 10**9
@@ -811,7 +811,7 @@
 
 
 def input_kernel(*refs):
-    blocks, (hidden, inside, keep, give, full, sems) = refs[:4], refs[4:]
+    blocks, (hidden, inside, keep, *gives, full, sems) = refs[:4], refs[4:]
     section, _, core = place()
     ch = hidden.shape[0]
     copy = pltpu.make_async_copy(hidden, full.at[pl.ds(0, ch)], sems.at[0])
@@ -820,17 +820,17 @@
     copy.wait()
     rows = 2 * ch
     width = keep.shape[1]
-    for j, out in enumerate((keep, give)):
-        for n in range(2):
-            at = pl.multiple_of((section ^ (2 * (core ^ j) + n)) * width, width)
-            out[n * rows : (n + 1) * rows, :] = full[:, pl.ds(at, width)]
-
-
-def pair_kernel(keep, got, *outs):
+    outs = [keep.at[pl.ds(n * rows, rows)] for n in range(2)] + gives
+    for m, out in enumerate(outs):
+        at = pl.multiple_of((section ^ (2 * (core ^ (m // 2)) + m % 2)) * width, width)
+        out[...] = full[:, pl.ds(at, width)]
+
+
+def pair_kernel(keep, *refs):
     rows = keep.shape[0] // 2
-    for n, out in enumerate(outs):
+    for n, (got, out) in enumerate(zip(refs[:2], refs[2:])):
         out[:rows, :] = keep[n * rows : (n + 1) * rows, :]
-        out[rows:, :] = got[n * rows : (n + 1) * rows, :]
+        out[rows:, :] = got[...]
 
 
 def store_maps(blocks, pick, outs, full):
@@ -1117,20 +1117,6 @@
             )
     blocks = [parts[0]] + [to_section(parts[k], k) for k in (1, 2, 3)]
     shares[0][1] = to_plane(after(share[1], blocks[1]), 1)
-    blocks = after(blocks, shares[1])
-    keep, give = call(
-        input_kernel,
-        [((4 * ch, 2 * cells), bf16)] * 2,
-        [((2 * ch, length), bf16)],
-        [*blocks, activation, inside],
-        "input",
-        flops=INPUT_FLOPS,
-        held=(4,),
-        loose=(5,),
-        copies=1,
-    )
-    maps = call(pair_kernel, [((4 * ch, 2 * cells), bf16)] * 2, [], [keep, to_core(give)], "pair")
-    maps = [send(x, lambda s, z, c, n=n: (z, s ^ (2 * c + n), c)) for n, x in enumerate(maps)]
     folded = call(
         fold_kernel,
         [((rows, 2 * ch), bf16) for rows in piece_rows[1:]],
@@ -1140,6 +1126,20 @@
         held=range(last),
         copies=last,
     )
+    blocks = after(blocks, folded)
+    keep, *gives = call(
+        input_kernel,
+        [((4 * ch, 2 * cells), bf16)] + [((2 * ch, 2 * cells), bf16)] * 2,
+        [((2 * ch, length), bf16)],
+        [*blocks, activation, inside],
+        "input",
+        flops=INPUT_FLOPS,
+        held=(4,),
+        loose=(5,),
+        copies=1,
+    )
+    maps = call(pair_kernel, [((4 * ch, 2 * cells), bf16)] * 2, [], [keep, *map(to_core, gives)], "pair")
+    maps = [send(x, lambda s, z, c, n=n: (z, s ^ (2 * c + n), c)) for n, x in enumerate(maps)]
     chosen = call(
         choose_kernel,
         [((slice_rows, 2 * ch), bf16)] * 4,
@@ -1148,6 +1148,8 @@
         "choose",
         loose=range(4),
     )
+    landed = [chosen[0]] + [to_section(chosen[k], k) for k in (1, 2, 3)]
+    landed, maps = lax.optimization_barrier((landed, maps))
     pick = (core * cells + np.arange(cells))[:, None] == np.arange(2 * cells)[None, :]
     map_pick = pick.astype(bf16)
     pick = (core * ch + np.arange(ch))[:, None] == np.arange(2 * ch)[None, :]
@@ -1156,9 +1158,9 @@
         [((TAPS, ch, channels), f32), ((1, ch), f32), ((1, ch), f32)] + [((cells, channels), bf16)] * 2,
         [((TAPS, channels, 2 * ch), bf16), ((2, channels, 2 * cells), bf16)],
         [
-            *with_core([chosen[0]] + [to_section(chosen[k], k) for k in (1, 2, 3)]),
+            *with_core(landed),
             pick.astype(bf16),
-            *with_core(after(maps, chosen)),
+            *with_core(maps),
             map_pick,
         ],
         "outputs",

time: 191 us -> 192 us (level)
    all_to_all x3, waiting for transfers between devices: 6.04 us -> 13.3 us  [plane_shards(): lax.all_to_all(share[0], 'dp', 0, 0, tiled=True, axis_index_groups=same_c...]
    ppermute x67 -> x68, waiting for transfers between devices: 57.8 us -> 51.2 us  [send(): return lax.ppermute(x, AXES, pairs)]
    ppermute x67 -> x68, starting transfers between devices: 56.6 us -> 56.3 us  [send(): return lax.ppermute(x, AXES, pairs)]
  transfers between devices with their start and end apart: 71 -> 72, of which waited for: 37 -> 35; matrix products, arithmetic and copies ran while one was open for 0% -> 0% of each run, Pallas kernels for 19% -> 19%
where the time goes in v9:
time: 192 us; the launch traced here: 191 us
  starting transfers between devices  74 us (39%)
  waiting for transfers between devices  64.6 us (34%)
  Pallas kernels  50.3 us (26%)
    ppermute x68, starting transfers between devices, send(): return lax.ppermute(x, AXES, pairs)  56.3 us
    ppermute x68, waiting for transfers between devices, send(): return lax.ppermute(x, AXES, pairs)  51.2 us
    pallas_call x27, Pallas kernels, call(): pl.pallas_call(kernel, out_shape=shapes, in_specs=[pl.BlockSpec(memory_sp...  50.3 us
    all_to_all x3, waiting for transfers between devices, plane_shards(): lax.all_to_all(share[0], 'dp', 0, 0, tiled=True, axis_index_groups=same_c...  13.3 us
    all_to_all x3, starting transfers between devices, plane_shards(): lax.all_to_all(share[0], 'dp', 0, 0, tiled=True, axis_index_groups=same_c...  12.7 us
    all_to_all x1, starting transfers between devices, plane_shards(): lax.all_to_all(cot_slots, 'dp', 0, 0, tiled=True, axis_index_groups=same_...  4.87 us
  transfers between devices with their start and end apart: 72, of which 35 were waited for; matrix products, arithmetic and copies ran while one was open for 0% of the time, Pallas kernels for 19%

profile of v9, /device:TPU:0, one launch (start us, length us, event | category | flops | bytes accessed | tf_op | source)
XLA Modules:
  0.0 191.1 jit_solution(10693300283655666362)
XLA Ops:
  0.6 2.5 %weight_pack.1 = (bf16[592,512]{1,0:T(8,128)(2,1)S(1)}, bf16[592,512]{1,0:T(8,128)(2,1)S(1)}, bf16[592,512]{1,0:T(8,128)(2,1)S(1)}, bf16[592,512]{1,0:T(8,128)(2,1)S(1)}) custom-call(f32[1,512]{1,0:T(1,128)} %gain.1, f32[1,512]{1,0:T(1,128)} %bias.1, bf16[9,512,512]{2,1,0:T(8,128)(2,1)} %bitcast.26), custom_call_target="tpu_custom_call" | custom-call | bytes 7147520 | tf_op jit(solution)/shard_map/weight_pack/pallas_call | solution.py:895
  3.1 3.0 %collective-permute-start.7 = (bf16[592,512]{1,0:T(8,128)(2,1)S(1)}, bf16[592,512]{1,0:T(8,128)(2,1)S(1)}, u32[]{:S(2)}, u32[]{:S(2)}) collective-permute-start(bf16[592,512]{1,0:T(8,128)(2,1)S(1)} %get-tuple-element.139), channel_id=1, source_target_pairs={{0,8},{1,9},{2,10},{3,11},{4,12},{5,13},{6,14},{7,15},{8,0},{9,1},... | collective-permute-start | bytes 1818632 | tf_op jit(solution)/shard_map/ppermute | solution.py:253
  6.2 1.5 collective-permute-start.8
  7.7 1.4 frames.1
  9.1 1.6 collective-permute-start
  11.2 2.6 %collective-permute-start.1 = (bf16[208,512]{1,0:T(8,128)(2,1)S(1)}, bf16[208,512]{1,0:T(8,128)(2,1)S(1)}, u32[]{:S(2)}, u32[]{:S(2)}) collective-permute-start(bf16[208,512]{1,0:T(8,128)(2,1)S(1)} %get-tuple-element.145), channel_id=1, source_target_pairs={{0,4},{1,5},{2,6},{3,7},{4,0},{5,1},{6,2},{7,3},{8,12},{9,13},{10,... | collective-permute-start | bytes 638984 | tf_op jit(solution)/shard_map/ppermute | solution.py:253
  13.8 6.1 %collective-permute-done.refs_1_ = bf16[208,512]{1,0:T(8,128)(2,1)S(1)} collective-permute-done((bf16[208,512]{1,0:T(8,128)(2,1)S(1)}, bf16[208,512]{1,0:T(8,128)(2,1)S(1)}, u32[]{:S(2)}, u32[]{:S(2)}) %collective-permute-start) | collective-permute-done | bytes 213024 | tf_op jit(solution)/shard_map/ppermute | solution.py:253
  19.8 2.5 %collective-permute-start.2 = (bf16[208,512]{1,0:T(8,128)(2,1)S(1)}, bf16[208,512]{1,0:T(8,128)(2,1)S(1)}, u32[]{:S(2)}, u32[]{:S(2)}) collective-permute-start(bf16[208,512]{1,0:T(8,128)(2,1)S(1)} %get-tuple-element.146), channel_id=1, source_target_pairs={{0,6},{1,7},{2,4},{3,5},{4,2},{5,3},{6,0},{7,1},{8,14},{9,15},{10,... | collective-permute-start | bytes 638984 | tf_op jit(solution)/shard_map/ppermute | solution.py:253
  22.3 2.8 %collective-permute-done.1.refs_2_ = bf16[208,512]{1,0:T(8,128)(2,1)S(1)} collective-permute-done((bf16[208,512]{1,0:T(8,128)(2,1)S(1)}, bf16[208,512]{1,0:T(8,128)(2,1)S(1)}, u32[]{:S(2)}, u32[]{:S(2)}) %collective-permute-start.1) | collective-permute-done | bytes 213024 | tf_op jit(solution)/shard_map/ppermute | solution.py:253
  25.1 2.5 %collective-permute-done.2.refs_3_ = bf16[208,512]{1,0:T(8,128)(2,1)S(1)} collective-permute-done((bf16[208,512]{1,0:T(8,128)(2,1)S(1)}, bf16[208,512]{1,0:T(8,128)(2,1)S(1)}, u32[]{:S(2)}, u32[]{:S(2)}) %collective-permute-start.2) | collective-permute-done | bytes 213024 | tf_op jit(solution)/shard_map/ppermute | solution.py:253
  28.1 6.2 %collective-permute-done.8.refs_10_.refs_2_ = bf16[592,512]{1,0:T(8,128)(2,1)S(1)} collective-permute-done((bf16[592,512]{1,0:T(8,128)(2,1)S(1)}, bf16[592,512]{1,0:T(8,128)(2,1)S(1)}, u32[]{:S(2)}, u32[]{:S(2)}) %collective-permute-start.8) | collective-permute-done | bytes 606240 | tf_op jit(solution)/shard_map/ppermute | solution.py:253
  34.4 1.4 collective-permute-done.6.refs_7_
  35.8 2.5 %forward.3 = (bf16[64,1536]{1,0:T(8,128)(2,1)S(1)}, f32[64,1664]{1,0:T(8,128)}, bf16[1536,512]{1,0:T(8,128)(2,1)}, f32[1,1536]{1,0:T(1,128)S(1)}) custom-call(bf16[208,512]{1,0:T(8,128)(2,1)S(1)} %get-tuple-element.143.refs_0_, bf16[208,512]{1,0:T(8,128)(2,1)S(1)} %collective-permute-done.refs_1_, bf16[208,512]{1,0:T(8,128)(2,1)S(1)} %collective-permute-done.1.refs_2_, ...), custom_call_target="tpu_custom_call" | custom-call | flops 905969664 | bytes 6428672 | tf_op jit(solution)/shard_map/forward/pallas_call | solution.py:895
  38.3 1.5 collective-permute-start.12
  39.9 1.5 collective-permute-start.10
  41.9 2.0 %cot_slices.1 = bf16[768,128]{1,0:T(8,128)(2,1)} custom-call(bf16[4,192,512]{2,1,0:T(8,128)(2,1)} %bitcast.30), custom_call_target="tpu_custom_call" | custom-call | bytes 983040 | tf_op jit(solution)/shard_map/cot_slices/pallas_call | solution.py:895
  43.9 3.7 %turn_weights.1 = (bf16[1024,640]{1,0:T(8,128)(2,1)}, bf16[256,640]{1,0:T(8,128)(2,1)}, bf16[256,640]{1,0:T(8,128)(2,1)}, bf16[256,640]{1,0:T(8,128)(2,1)}, bf16[256,640]{1,0:T(8,128)(2,1)}) custom-call(bf16[592,512]{1,0:T(8,128)(2,1)} %copy-done, bf16[592,512]{1,0:T(8,128)(2,1)} %copy-done.1, bf16[592,512]{1,0:T(8,128)(2,1)} %copy-done.2, ...), custom_call_target="tpu_custom_call" | custom-call | bytes 5046272 | tf_op jit(solution)/shard_map/turn_weights/pallas_call | solution.py:895
  47.6 1.1 pick.3.refs_8_
  49.3 1.2 collective-permute-done.10.refs_1_
  52.3 3.1 %forward.4 = (bf16[64,1536]{1,0:T(8,128)(2,1)S(1)}, f32[64,1664]{1,0:T(8,128)}, bf16[512,1536]{1,0:T(8,128)(2,1)}) custom-call(bf16[64,1536]{1,0:T(8,128)(2,1)S(1)} %get-tuple-element.153.refs_0_, bf16[64,1536]{1,0:T(8,128)(2,1)S(1)} %collective-permute-done.10.refs_1_, bf16[64,1536]{1,0:T(8,128)(2,1)S(1)} %collective-permute-done.11.refs_2_, ...), custom_call_target="tpu_custom_call" | custom-call | flops 905969664 | bytes 4478976 | tf_op jit(solution)/shard_map/forward/pallas_call | solution.py:895
  55.4 1.2 collective-permute-start.19
  56.5 1.5 collective-permute-start.17
  58.9 4.9 %all-to-all-start = ((bf16[4,192,128]{2,1,0:T(8,128)(2,1)}), bf16[4,192,128]{2,1,0:T(8,128)(2,1)S(1)}, u32[]{:S(2)}, u32[]{:S(2)}) async-start(bf16[4,192,128]{2,1,0:T(8,128)(2,1)} %bitcast.7), calls=%async_computation | async-start | bytes 393216 | tf_op jit(solution)/shard_map/all_to_all | solution.py:1025
  63.8 1.1 pick.4.refs_8_
  65.2 2.0 %collective-permute-done.17.refs_1_ = bf16[64,1536]{1,0:T(8,128)(2,1)S(1)} collective-permute-done((bf16[64,1536]{1,0:T(8,128)(2,1)S(1)}, bf16[64,1536]{1,0:T(8,128)(2,1)S(1)}, u32[]{:S(2)}, u32[]{:S(2)}) %collective-permute-start.17) | collective-permute-done | bytes 196640 | tf_op jit(solution)/shard_map/ppermute | solution.py:253
  69.0 2.5 %forward.5 = (bf16[64,1536]{1,0:T(8,128)(2,1)S(1)}, f32[64,1664]{1,0:T(8,128)}, bf16[512,1536]{1,0:T(8,128)(2,1)}) custom-call(bf16[64,1536]{1,0:T(8,128)(2,1)S(1)} %get-tuple-element.166.refs_0_, bf16[64,1536]{1,0:T(8,128)(2,1)S(1)} %collective-permute-done.17.refs_1_, bf16[64,1536]{1,0:T(8,128)(2,1)S(1)} %collective-permute-done.18.refs_2_, ...), custom_call_target="tpu_custom_call" | custom-call | flops 905969664 | bytes 4478976 | tf_op jit(solution)/shard_map/forward/pallas_call | solution.py:895
  71.5 1.1 collective-permute-start.26
  72.6 1.5 collective-permute-start.24
  75.7 1.1 pick.5.refs_8_
  77.1 3.1 %collective-permute-done.26.refs_3_ = bf16[64,1536]{1,0:T(8,128)(2,1)S(1)} collective-permute-done((bf16[64,1536]{1,0:T(8,128)(2,1)S(1)}, bf16[64,1536]{1,0:T(8,128)(2,1)S(1)}, u32[]{:S(2)}, u32[]{:S(2)}) %collective-permute-start.26) | collective-permute-done | bytes 196640 | tf_op jit(solution)/shard_map/ppermute | solution.py:253
  80.3 3.0 %collective-permute-done.24.refs_1_ = bf16[64,1536]{1,0:T(8,128)(2,1)S(1)} collective-permute-done((bf16[64,1536]{1,0:T(8,128)(2,1)S(1)}, bf16[64,1536]{1,0:T(8,128)(2,1)S(1)}, u32[]{:S(2)}, u32[]{:S(2)}) %collective-permute-start.24) | collective-permute-done | bytes 196640 | tf_op jit(solution)/shard_map/ppermute | solution.py:253
  85.1 2.5 %turn.1 = (bf16[64,1536]{1,0:T(8,128)(2,1)}, bf16[512,1536]{1,0:T(8,128)(2,1)}, bf16[64,1536]{1,0:T(8,128)(2,1)S(1)}, f32[64,128]{1,0:T(8,128)S(1)}) custom-call(bf16[64,1536]{1,0:T(8,128)(2,1)S(1)} %get-tuple-element.172.refs_0_, bf16[64,1536]{1,0:T(8,128)(2,1)S(1)} %collective-permute-done.24.refs_1_, ...), custom_call_target="tpu_custom_call" | custom-call | flops 905969664 | bytes 4478976 | tf_op jit(solution)/shard_map/turn/pallas_call | solution.py:895
  87.8 1.3 collective-permute-done.32.other
  89.1 3.9 %conv_back.4 = (bf16[64,1536]{1,0:T(8,128)(2,1)S(1)}, bf16[64,1536]{1,0:T(8,128)(2,1)S(1)}, bf16[64,1536]{1,0:T(8,128)(2,1)S(1)}, bf16[64,1536]{1,0:T(8,128)(2,1)S(1)}, bf16[2304,128]{1,0:T(8,128)(2,1)}) custom-call(bf16[64,1536]{1,0:T(8,128)(2,1)S(1)} %get-tuple-element.180.own, bf16[64,1536]{1,0:T(8,128)(2,1)S(1)} %collective-permute-done.32.other, ...), custom_call_target="tpu_custom_call" | custom-call | bytes 5079040 | tf_op jit(solution)/shard_map/conv_back/pallas_call | solution.py:895
  93.6 1.1 collective-permute-start.35
  94.7 1.9 %collective-permute-start.36 = (bf16[64,1536]{1,0:T(8,128)(2,1)S(1)}, bf16[64,1536]{1,0:T(8,128)(2,1)S(1)}, u32[]{:S(2)}, u32[]{:S(2)}) collective-permute-start(bf16[64,1536]{1,0:T(8,128)(2,1)S(1)} %get-tuple-element.186), channel_id=1, source_target_pairs={{0,24},{1,25},{2,26},{3,27},{4,28},{5,29},{6,30},{7,31},{8,16},{9,... | collective-permute-start | bytes 589832 | tf_op jit(solution)/shard_map/ppermute | solution.py:253
  96.6 4.9 %all-to-all-start.1 = ((bf16[4,576,128]{2,1,0:T(8,128)(2,1)}), bf16[4,576,128]{2,1,0:T(8,128)(2,1)S(1)}, u32[]{:S(2)}, u32[]{:S(2)}) async-start(bf16[4,576,128]{2,1,0:T(8,128)(2,1)} %bitcast.33), calls=%async_computation.1 | async-start | bytes 1179648 | tf_op jit(solution)/shard_map/all_to_all | solution.py:1097
  102.6 2.2 %collective-permute-done.36.refs_3_ = bf16[64,1536]{1,0:T(8,128)(2,1)S(1)} collective-permute-done((bf16[64,1536]{1,0:T(8,128)(2,1)S(1)}, bf16[64,1536]{1,0:T(8,128)(2,1)S(1)}, u32[]{:S(2)}, u32[]{:S(2)}) %collective-permute-start.36) | collective-permute-done | bytes 196640 | tf_op jit(solution)/shard_map/ppermute | solution.py:253
  105.4 1.4 collective-permute-done.37.other
  106.8 3.9 %conv_back.5 = (bf16[64,1536]{1,0:T(8,128)(2,1)S(1)}, bf16[64,1536]{1,0:T(8,128)(2,1)S(1)}, bf16[64,1536]{1,0:T(8,128)(2,1)S(1)}, bf16[64,1536]{1,0:T(8,128)(2,1)S(1)}, bf16[2304,128]{1,0:T(8,128)(2,1)}) custom-call(bf16[64,1536]{1,0:T(8,128)(2,1)S(1)} %get-tuple-element.195.own, bf16[64,1536]{1,0:T(8,128)(2,1)S(1)} %collective-permute-done.37.other, ...), custom_call_target="tpu_custom_call" | custom-call | flops 5200000000 | bytes 5079040 | tf_op jit(solution)/shard_map/conv_back/pallas_call | solution.py:895
  110.8 1.3 collective-permute-start.39
  113.1 1.2 collective-permute-start.41
  114.3 3.7 %all-to-all-done.1 = bf16[4,576,128]{2,1,0:T(8,128)(2,1)S(1)} async-done(((bf16[4,576,128]{2,1,0:T(8,128)(2,1)}), bf16[4,576,128]{2,1,0:T(8,128)(2,1)S(1)}, u32[]{:S(2)}, u32[]{:S(2)}) %all-to-all-start.1) | async-done | bytes 589856 | tf_op jit(solution)/shard_map/all_to_all | solution.py:1097
  118.1 4.4 %all-to-all-start.2 = ((bf16[4,576,128]{2,1,0:T(8,128)(2,1)}), bf16[4,576,128]{2,1,0:T(8,128)(2,1)}, u32[]{:S(2)}, u32[]{:S(2)}) async-start(bf16[4,576,128]{2,1,0:T(8,128)(2,1)} %bitcast.32), calls=%async_computation.2 | async-start | bytes 1179648 | tf_op jit(solution)/shard_map/all_to_all | solution.py:1097
  123.5 2.1 %norm_back.4 = (bf16[64,1536]{1,0:T(8,128)(2,1)S(1)}, f32[64,128]{1,0:T(8,128)S(1)}) custom-call(bf16[64,1536]{1,0:T(8,128)(2,1)S(1)} %get-tuple-element.198.refs_0_, bf16[64,1536]{1,0:T(8,128)(2,1)S(1)} %collective-permute-done.39.refs_1_, bf16[64,1536]{1,0:T(8,128)(2,1)S(1)} %collective-permute-done.40.refs_2_, ...), custom_call_target="tpu_custom_call" | custom-call | bytes 1595392 | tf_op jit(solution)/shard_map/norm_back/pallas_call | solution.py:895
  125.7 1.4 collective-permute-done.42.other
  127.1 3.9 %conv_back.6 = (bf16[64,1536]{1,0:T(8,128)(2,1)S(1)}, bf16[64,1536]{1,0:T(8,128)(2,1)S(1)}, bf16[64,1536]{1,0:T(8,128)(2,1)S(1)}, bf16[64,1536]{1,0:T(8,128)(2,1)S(1)}, bf16[2304,128]{1,0:T(8,128)(2,1)}) custom-call(bf16[64,1536]{1,0:T(8,128)(2,1)S(1)} %get-tuple-element.210.own, bf16[64,1536]{1,0:T(8,128)(2,1)S(1)} %collective-permute-done.42.other, ...), custom_call_target="tpu_custom_call" | custom-call | flops 5200000000 | bytes 5079040 | tf_op jit(solution)/shard_map/conv_back/pallas_call | solution.py:895
  132.7 1.9 %collective-permute-start.46 = (bf16[64,1536]{1,0:T(8,128)(2,1)S(1)}, bf16[64,1536]{1,0:T(8,128)(2,1)S(1)}, u32[]{:S(2)}, u32[]{:S(2)}) collective-permute-start(bf16[64,1536]{1,0:T(8,128)(2,1)S(1)} %get-tuple-element.216), channel_id=1, source_target_pairs={{0,24},{1,25},{2,26},{3,27},{4,28},{5,29},{6,30},{7,31},{8,16},{9,... | collective-permute-start | bytes 589832 | tf_op jit(solution)/shard_map/ppermute | solution.py:253
  134.6 3.4 %all-to-all-done.2 = bf16[4,576,128]{2,1,0:T(8,128)(2,1)} async-done(((bf16[4,576,128]{2,1,0:T(8,128)(2,1)}), bf16[4,576,128]{2,1,0:T(8,128)(2,1)}, u32[]{:S(2)}, u32[]{:S(2)}) %all-to-all-start.2) | async-done | bytes 589856 | tf_op jit(solution)/shard_map/all_to_all | solution.py:1097
  138.0 3.5 %all-to-all-start.3 = ((bf16[4,576,128]{2,1,0:T(8,128)(2,1)}), bf16[4,576,128]{2,1,0:T(8,128)(2,1)S(1)}, u32[]{:S(2)}, u32[]{:S(2)}) async-start(bf16[4,576,128]{2,1,0:T(8,128)(2,1)} %bitcast.31), calls=%async_computation.3 | async-start | bytes 1179648 | tf_op jit(solution)/shard_map/all_to_all | solution.py:1097
  143.4 1.4 collective-permute-done.47.other
  144.8 3.9 %conv_back.7 = (bf16[64,1536]{1,0:T(8,128)(2,1)S(1)}, bf16[64,1536]{1,0:T(8,128)(2,1)S(1)}, bf16[64,1536]{1,0:T(8,128)(2,1)S(1)}, bf16[64,1536]{1,0:T(8,128)(2,1...) custom-call(bf16[64,1536]{1,0:T(8,128)(2,1)S(1)} %get-tuple-element., ...), custom_call_target="tpu_custom_call" | custom-call | flops 4000000000 | bytes 5128192 | tf_op jit(solution)/shard_map/conv_back/pallas_call | solution.py:895
  148.7 1.3 collective-permute-start.49
  151.1 1.2 collective-permute-start.57
  152.2 2.7 %collective-permute-start.51 = (bf16[592,128]{1,0:T(8,128)(2,1)}, bf16[592,128]{1,0:T(8,128)(2,1)S(1)}, u32[]{:S(2)}, u32[]{:S(2)}) collective-permute-start(bf16[592,128]{1,0:T(8,128)(2,1)} %get-tuple-element.233), channel_id=1, source_target_pairs={{0,4},{1,5},{2,6},{3,7},{4,0},{5,1},{6,2},{7,3},{8,12},{9,13},{10,... | collective-permute-start | bytes 454664 | tf_op jit(solution)/shard_map/ppermute | solution.py:253
  155.0 1.5 collective-permute-start.52
  156.5 1.8 collective-permute-start.50
  158.3 6.2 %all-to-all-done.3 = bf16[4,576,128]{2,1,0:T(8,128)(2,1)S(1)} async-done(((bf16[4,576,128]{2,1,0:T(8,128)(2,1)}), bf16[4,576,128]{2,1,0:T(8,128)(2,1)S(1)}, u32[]{:S(2)}, u32[]{:S(2)}) %all-to-all-start.3) | async-done | bytes 589856 | tf_op jit(solution)/shard_map/all_to_all | solution.py:1097
  165.3 1.6 fold.1
  170.1 2.1 %collective-permute-start.61 = (bf16[256,384]{1,0:T(8,128)(2,1)S(1)}, bf16[256,384]{1,0:T(8,128)(2,1)S(1)}, u32[]{:S(2)}, u32[]{:S(2)}) collective-permute-start(bf16[256,384]{1,0:T(8,128)(2,1)S(1)} %get-tuple-element.259), channel_id=1, source_target_pairs={{0,2},{1,7},{2,10},{3,15},{4,18},{5,23},{6,26},{7,31},{8,0},{9,5},... | collective-permute-start | bytes 589832 | tf_op jit(solution)/shard_map/ppermute | solution.py:253
  172.5 5.5 %collective-permute-start.54 = (bf16[592,128]{1,0:T(8,128)(2,1)S(1)}, bf16[592,128]{1,0:T(8,128)(2,1)S(1)}, u32[]{:S(2)}, u32[]{:S(2)}) collective-permute-start(bf16[592,128]{1,0:T(8,128)(2,1)S(1)} %get-tuple-element.245), channel_id=1, source_target_pairs={{0,16},{1,17},{2,18},{3,19},{4,20},{5,21},{6,22},{7,23},{8,24},{9,... | collective-permute-start | bytes 454664 | tf_op jit(solution)/shard_map/ppermute | solution.py:253
  178.0 4.3 %collective-permute-done.53.refs_1_ = bf16[592,128]{1,0:T(8,128)(2,1)S(1)} collective-permute-done((bf16[592,128]{1,0:T(8,128)(2,1)S(1)}, bf16[592,128]{1,0:T(8,128)(2,1)S(1)}, u32[]{:S(2)}, u32[]{:S(2)}) %collective-permute-start.53) | collective-permute-done | bytes 151584 | tf_op jit(solution)/shard_map/ppermute | solution.py:253
  182.3 4.0 %collective-permute-done.54.refs_2_ = bf16[592,128]{1,0:T(8,128)(2,1)S(1)} collective-permute-done((bf16[592,128]{1,0:T(8,128)(2,1)S(1)}, bf16[592,128]{1,0:T(8,128)(2,1)S(1)}, u32[]{:S(2)}, u32[]{:S(2)}) %collective-permute-start.54) | collective-permute-done | bytes 151584 | tf_op jit(solution)/shard_map/ppermute | solution.py:253
  189.1 1.9 %outputs.1 = (f32[9,64,512]{2,1,0:T(8,128)}, f32[1,64]{1,0:T(1,128)}, f32[1,64]{1,0:T(1,128)}, bf16[192,512]{1,0:T(8,128)(2,1)}, bf16[192,512]{1,0:T(8,128)(2,1)}) custom-call(bf16[592,128]{1,0:T(8,128)(2,1)S(1)} %get-tuple-element.260.refs_0_, bf16[592,128]{1,0:T(8,128)(2,1)S(1)} %collective-permute-done.53.refs_1_, ...), custom_call_target="tpu_custom_call" | custom-call | bytes 3736064 | tf_op jit(solution)/shard_map/outputs/pallas_call | solution.py:895
  (135 shorter events, 26.9 us)
Async XLA Ops:
  3.1 24.5 %collective-permute-start.7 = (bf16[592,512]{1,0:T(8,128)(2,1)S(1)}, bf16[592,512]{1,0:T(8,128)(2,1)S(1)}, u32[]{:S(2)}, u32[]{:S(2)}) collective-permute-start(bf16[592,512]{1,0:T(8,128)(2,1)S(1)} %get-tuple-element.139), channel_id=1, source_target_pairs={{0,8},{1,9},{2,10},{3,11},{4,12},{5,13},{6,14},{7,15},{8,0},{9,1},... | collective-permute-start | bytes 1818632 | tf_op jit(solution)/shard_map/ppermute | solution.py:253
  6.2 28.1 %collective-permute-start.8 = (bf16[592,512]{1,0:T(8,128)(2,1)S(1)}, bf16[592,512]{1,0:T(8,128)(2,1)S(1)}, u32[]{:S(2)}, u32[]{:S(2)}) collective-permute-start(bf16[592,512]{1,0:T(8,128)(2,1)S(1)} %get-tuple-element.140), channel_id=1, source_target_pairs={{0,16},{1,17},{2,18},{3,19},{4,20},{5,21},{6,22},{7,23},{8,24},{9,... | collective-permute-start | bytes 1818632 | tf_op jit(solution)/shard_map/ppermute | solution.py:253
  9.1 10.8 %collective-permute-start = (bf16[208,512]{1,0:T(8,128)(2,1)S(1)}, bf16[208,512]{1,0:T(8,128)(2,1)S(1)}, u32[]{:S(2)}, u32[]{:S(2)}) collective-permute-start(bf16[208,512]{1,0:T(8,128)(2,1)S(1)} %get-tuple-element.144), channel_id=1, source_target_pairs={{0,2},{1,3},{2,0},{3,1},{4,6},{5,7},{6,4},{7,5},{8,10},{9,11},{10,... | collective-permute-start | bytes 638984 | tf_op jit(solution)/shard_map/ppermute | solution.py:253
  10.7 23.6 %collective-permute-start.9 = (bf16[592,512]{1,0:T(8,128)(2,1)S(1)}, bf16[592,512]{1,0:T(8,128)(2,1)S(1)}, u32[]{:S(2)}, u32[]{:S(2)}) collective-permute-start(bf16[592,512]{1,0:T(8,128)(2,1)S(1)} %get-tuple-element.141), channel_id=1, source_target_pairs={{0,24},{1,25},{2,26},{3,27},{4,28},{5,29},{6,30},{7,31},{8,16},{9,... | collective-permute-start | bytes 1818632 | tf_op jit(solution)/shard_map/ppermute | solution.py:253
  11.2 13.9 %collective-permute-start.1 = (bf16[208,512]{1,0:T(8,128)(2,1)S(1)}, bf16[208,512]{1,0:T(8,128)(2,1)S(1)}, u32[]{:S(2)}, u32[]{:S(2)}) collective-permute-start(bf16[208,512]{1,0:T(8,128)(2,1)S(1)} %get-tuple-element.145), channel_id=1, source_target_pairs={{0,4},{1,5},{2,6},{3,7},{4,0},{5,1},{6,2},{7,3},{8,12},{9,13},{10,... | collective-permute-start | bytes 638984 | tf_op jit(solution)/shard_map/ppermute | solution.py:253
  19.8 7.8 %collective-permute-start.2 = (bf16[208,512]{1,0:T(8,128)(2,1)S(1)}, bf16[208,512]{1,0:T(8,128)(2,1)S(1)}, u32[]{:S(2)}, u32[]{:S(2)}) collective-permute-start(bf16[208,512]{1,0:T(8,128)(2,1)S(1)} %get-tuple-element.146), channel_id=1, source_target_pairs={{0,6},{1,7},{2,4},{3,5},{4,2},{5,3},{6,0},{7,1},{8,14},{9,15},{10,... | collective-permute-start | bytes 638984 | tf_op jit(solution)/shard_map/ppermute | solution.py:253
  25.1 9.2 %collective-permute-start.3 = (bf16[208,512]{1,0:T(8,128)(2,1)S(1)}, bf16[208,512]{1,0:T(8,128)(2,1)S(1)}, u32[]{:S(2)}, u32[]{:S(2)}) collective-permute-start(bf16[208,512]{1,0:T(8,128)(2,1)S(1)} %get-tuple-element.143.refs_0_), channel_id=1, source_target_pairs={{0,1},{1,0},{2,3},{3,2},{4,5},{5,4},{6,7},{7,6},{8,9},{9,8},{10,11... | collective-permute-start | bytes 638984 | tf_op jit(solution)/shard_map/ppermute | solution.py:253
  27.6 6.8 %collective-permute-start.4 = (bf16[208,512]{1,0:T(8,128)(2,1)S(1)}, bf16[208,512]{1,0:T(8,128)(2,1)S(1)}, u32[]{:S(2)}, u32[]{:S(2)}) collective-permute-start(bf16[208,512]{1,0:T(8,128)(2,1)S(1)} %collective-permute-done.refs_1_), channel_id=1, source_target_pairs={{0,1},{1,0},{2,3},{3,2},{4,5},{5,4},{6,7},{7,6},{8,9},{9,8},{10,11... | collective-permute-start | bytes 638984 | tf_op jit(solution)/shard_map/ppermute | solution.py:253
  27.6 6.8 %collective-permute-start.5 = (bf16[208,512]{1,0:T(8,128)(2,1)S(1)}, bf16[208,512]{1,0:T(8,128)(2,1)S(1)}, u32[]{:S(2)}, u32[]{:S(2)}) collective-permute-start(bf16[208,512]{1,0:T(8,128)(2,1)S(1)} %collective-permute-done.1.refs_2_), channel_id=1, source_target_pairs={{0,1},{1,0},{2,3},{3,2},{4,5},{5,4},{6,7},{7,6},{8,9},{9,8},{10,11... | collective-permute-start | bytes 638984 | tf_op jit(solution)/shard_map/ppermute | solution.py:253
  34.3 1.5 collective-permute-start.6
  38.3 10.4 %collective-permute-start.12 = (bf16[64,1536]{1,0:T(8,128)(2,1)S(1)}, bf16[64,1536]{1,0:T(8,128)(2,1)S(1)}, u32[]{:S(2)}, u32[]{:S(2)}) collective-permute-start(bf16[64,1536]{1,0:T(8,128)(2,1)S(1)} %get-tuple-element.153.refs_0_), channel_id=1, source_target_pairs={{0,24},{1,25},{2,26},{3,27},{4,28},{5,29},{6,30},{7,31},{8,16},{9,... | collective-permute-start | bytes 589832 | tf_op jit(solution)/shard_map/ppermute | solution.py:253
  39.9 10.7 %collective-permute-start.10 = (bf16[64,1536]{1,0:T(8,128)(2,1)S(1)}, bf16[64,1536]{1,0:T(8,128)(2,1)S(1)}, u32[]{:S(2)}, u32[]{:S(2)}) collective-permute-start(bf16[64,1536]{1,0:T(8,128)(2,1)S(1)} %get-tuple-element.153.refs_0_), channel_id=1, source_target_pairs={{0,8},{1,9},{2,10},{3,11},{4,12},{5,13},{6,14},{7,15},{8,0},{9,1},... | collective-permute-start | bytes 589832 | tf_op jit(solution)/shard_map/ppermute | solution.py:253
  41.4 9.2 %collective-permute-start.11 = (bf16[64,1536]{1,0:T(8,128)(2,1)S(1)}, bf16[64,1536]{1,0:T(8,128)(2,1)S(1)}, u32[]{:S(2)}, u32[]{:S(2)}) collective-permute-start(bf16[64,1536]{1,0:T(8,128)(2,1)S(1)} %get-tuple-element.153.refs_0_), channel_id=1, source_target_pairs={{0,16},{1,17},{2,18},{3,19},{4,20},{5,21},{6,22},{7,23},{8,24},{9,... | collective-permute-start | bytes 589832 | tf_op jit(solution)/shard_map/ppermute | solution.py:253
  41.9 9.2 %collective-permute-start.13 = (bf16[64,1536]{1,0:T(8,128)(2,1)S(1)}, bf16[64,1536]{1,0:T(8,128)(2,1)S(1)}, u32[]{:S(2)}, u32[]{:S(2)}) collective-permute-start(bf16[64,1536]{1,0:T(8,128)(2,1)S(1)} %get-tuple-element.153.refs_0_), channel_id=1, source_target_pairs={{0,1},{1,0},{2,3},{3,2},{4,5},{5,4},{6,7},{7,6},{8,9},{9,8},{10,11... | collective-permute-start | bytes 589832 | tf_op jit(solution)/shard_map/ppermute | solution.py:253
  48.7 2.3 %collective-permute-start.16 = (bf16[64,1536]{1,0:T(8,128)(2,1)S(1)}, bf16[64,1536]{1,0:T(8,128)(2,1)S(1)}, u32[]{:S(2)}, u32[]{:S(2)}) collective-permute-start(bf16[64,1536]{1,0:T(8,128)(2,1)S(1)} %collective-permute-done.12.refs_3_), channel_id=1, source_target_pairs={{0,1},{1,0},{2,3},{3,2},{4,5},{5,4},{6,7},{7,6},{8,9},{9,8},{10,11... | collective-permute-start | bytes 589832 | tf_op jit(solution)/shard_map/ppermute | solution.py:253
  50.5 1.4 collective-permute-start.14
  50.5 1.7 collective-permute-start.15
  55.4 9.5 %collective-permute-start.19 = (bf16[64,1536]{1,0:T(8,128)(2,1)S(1)}, bf16[64,1536]{1,0:T(8,128)(2,1)S(1)}, u32[]{:S(2)}, u32[]{:S(2)}) collective-permute-start(bf16[64,1536]{1,0:T(8,128)(2,1)S(1)} %get-tuple-element.166.refs_0_), channel_id=1, source_target_pairs={{0,24},{1,25},{2,26},{3,27},{4,28},{5,29},{6,30},{7,31},{8,16},{9,... | collective-permute-start | bytes 589832 | tf_op jit(solution)/shard_map/ppermute | solution.py:253
  56.5 10.7 %collective-permute-start.17 = (bf16[64,1536]{1,0:T(8,128)(2,1)S(1)}, bf16[64,1536]{1,0:T(8,128)(2,1)S(1)}, u32[]{:S(2)}, u32[]{:S(2)}) collective-permute-start(bf16[64,1536]{1,0:T(8,128)(2,1)S(1)} %get-tuple-element.166.refs_0_), channel_id=1, source_target_pairs={{0,8},{1,9},{2,10},{3,11},{4,12},{5,13},{6,14},{7,15},{8,0},{9,1},... | collective-permute-start | bytes 589832 | tf_op jit(solution)/shard_map/ppermute | solution.py:253
  58.0 9.6 %collective-permute-start.18 = (bf16[64,1536]{1,0:T(8,128)(2,1)S(1)}, bf16[64,1536]{1,0:T(8,128)(2,1)S(1)}, u32[]{:S(2)}, u32[]{:S(2)}) collective-permute-start(bf16[64,1536]{1,0:T(8,128)(2,1)S(1)} %get-tuple-element.166.refs_0_), channel_id=1, source_target_pairs={{0,16},{1,17},{2,18},{3,19},{4,20},{5,21},{6,22},{7,23},{8,24},{9,... | collective-permute-start | bytes 589832 | tf_op jit(solution)/shard_map/ppermute | solution.py:253
  58.9 8.8 %collective-permute-start.20 = (bf16[64,1536]{1,0:T(8,128)(2,1)S(1)}, bf16[64,1536]{1,0:T(8,128)(2,1)S(1)}, u32[]{:S(2)}, u32[]{:S(2)}) collective-permute-start(bf16[64,1536]{1,0:T(8,128)(2,1)S(1)} %get-tuple-element.166.refs_0_), channel_id=1, source_target_pairs={{0,1},{1,0},{2,3},{3,2},{4,5},{5,4},{6,7},{7,6},{8,9},{9,8},{10,11... | collective-permute-start | bytes 589832 | tf_op jit(solution)/shard_map/ppermute | solution.py:253
  58.9 16.1 %all-to-all-start = ((bf16[4,192,128]{2,1,0:T(8,128)(2,1)}), bf16[4,192,128]{2,1,0:T(8,128)(2,1)S(1)}, u32[]{:S(2)}, u32[]{:S(2)}) async-start(bf16[4,192,128]{2,1,0:T(8,128)(2,1)} %bitcast.7), calls=%async_computation | async-start | bytes 393216 | tf_op jit(solution)/shard_map/all_to_all | solution.py:1025
  64.9 2.8 %collective-permute-start.23 = (bf16[64,1536]{1,0:T(8,128)(2,1)S(1)}, bf16[64,1536]{1,0:T(8,128)(2,1)S(1)}, u32[]{:S(2)}, u32[]{:S(2)}) collective-permute-start(bf16[64,1536]{1,0:T(8,128)(2,1)S(1)} %collective-permute-done.19.refs_3_), channel_id=1, source_target_pairs={{0,1},{1,0},{2,3},{3,2},{4,5},{5,4},{6,7},{7,6},{8,9},{9,8},{10,11... | collective-permute-start | bytes 589832 | tf_op jit(solution)/shard_map/ppermute | solution.py:253
  71.5 8.8 %collective-permute-start.26 = (bf16[64,1536]{1,0:T(8,128)(2,1)S(1)}, bf16[64,1536]{1,0:T(8,128)(2,1)S(1)}, u32[]{:S(2)}, u32[]{:S(2)}) collective-permute-start(bf16[64,1536]{1,0:T(8,128)(2,1)S(1)} %get-tuple-element.172.refs_0_), channel_id=1, source_target_pairs={{0,24},{1,25},{2,26},{3,27},{4,28},{5,29},{6,30},{7,31},{8,16},{9,... | collective-permute-start | bytes 589832 | tf_op jit(solution)/shard_map/ppermute | solution.py:253
  72.6 10.7 %collective-permute-start.24 = (bf16[64,1536]{1,0:T(8,128)(2,1)S(1)}, bf16[64,1536]{1,0:T(8,128)(2,1)S(1)}, u32[]{:S(2)}, u32[]{:S(2)}) collective-permute-start(bf16[64,1536]{1,0:T(8,128)(2,1)S(1)} %get-tuple-element.172.refs_0_), channel_id=1, source_target_pairs={{0,8},{1,9},{2,10},{3,11},{4,12},{5,13},{6,14},{7,15},{8,0},{9,1},... | collective-permute-start | bytes 589832 | tf_op jit(solution)/shard_map/ppermute | solution.py:253
  74.1 9.6 %collective-permute-start.25 = (bf16[64,1536]{1,0:T(8,128)(2,1)S(1)}, bf16[64,1536]{1,0:T(8,128)(2,1)S(1)}, u32[]{:S(2)}, u32[]{:S(2)}) collective-permute-start(bf16[64,1536]{1,0:T(8,128)(2,1)S(1)} %get-tuple-element.172.refs_0_), channel_id=1, source_target_pairs={{0,16},{1,17},{2,18},{3,19},{4,20},{5,21},{6,22},{7,23},{8,24},{9,... | collective-permute-start | bytes 589832 | tf_op jit(solution)/shard_map/ppermute | solution.py:253
  75.1 1.7 collective-permute-start.27
  75.1 9.0 %collective-permute-start.28 = (bf16[64,1536]{1,0:T(8,128)(2,1)S(1)}, bf16[64,1536]{1,0:T(8,128)(2,1)S(1)}, u32[]{:S(2)}, u32[]{:S(2)}) collective-permute-start(bf16[64,1536]{1,0:T(8,128)(2,1)S(1)} %get-tuple-element.172.refs_0_), channel_id=1, source_target_pairs={{0,1},{1,0},{2,3},{3,2},{4,5},{5,4},{6,7},{7,6},{8,9},{9,8},{10,11... | collective-permute-start | bytes 589832 | tf_op jit(solution)/shard_map/ppermute | solution.py:253
  80.3 3.9 %collective-permute-start.31 = (bf16[64,1536]{1,0:T(8,128)(2,1)S(1)}, bf16[64,1536]{1,0:T(8,128)(2,1)S(1)}, u32[]{:S(2)}, u32[]{:S(2)}) collective-permute-start(bf16[64,1536]{1,0:T(8,128)(2,1)S(1)} %collective-permute-done.26.refs_3_), channel_id=1, source_target_pairs={{0,1},{1,0},{2,3},{3,2},{4,5},{5,4},{6,7},{7,6},{8,9},{9,8},{10,11... | collective-permute-start | bytes 589832 | tf_op jit(solution)/shard_map/ppermute | solution.py:253
  83.8 4.1 %collective-permute-start.33 = (bf16[256,640]{1,0:T(8,128)(2,1)S(1)}, bf16[256,640]{1,0:T(8,128)(2,1)S(1)}, u32[]{:S(2)}, u32[]{:S(2)}) collective-permute-start(bf16[256,640]{1,0:T(8,128)(2,1)S(1)} %copy-done.11), channel_id=1, source_target_pairs={{0,1},{1,0},{2,3},{3,2},{4,5},{5,4},{6,7},{7,6},{8,9},{9,8},{10,11... | collective-permute-start | bytes 983048 | tf_op jit(solution)/shard_map/ppermute | solution.py:253
  87.6 1.5 collective-permute-start.32
  93.1 9.5 %collective-permute-start.34 = (bf16[64,1536]{1,0:T(8,128)(2,1)S(1)}, bf16[64,1536]{1,0:T(8,128)(2,1)S(1)}, u32[]{:S(2)}, u32[]{:S(2)}) collective-permute-start(bf16[64,1536]{1,0:T(8,128)(2,1)S(1)} %get-tuple-element.184), channel_id=1, source_target_pairs={{0,8},{1,9},{2,10},{3,11},{4,12},{5,13},{6,14},{7,15},{8,0},{9,1},... | collective-permute-start | bytes 589832 | tf_op jit(solution)/shard_map/ppermute | solution.py:253
  93.6 8.9 %collective-permute-start.35 = (bf16[64,1536]{1,0:T(8,128)(2,1)S(1)}, bf16[64,1536]{1,0:T(8,128)(2,1)S(1)}, u32[]{:S(2)}, u32[]{:S(2)}) collective-permute-start(bf16[64,1536]{1,0:T(8,128)(2,1)S(1)} %get-tuple-element.185), channel_id=1, source_target_pairs={{0,16},{1,17},{2,18},{3,19},{4,20},{5,21},{6,22},{7,23},{8,24},{9,... | collective-permute-start | bytes 589832 | tf_op jit(solution)/shard_map/ppermute | solution.py:253
  94.7 10.1 %collective-permute-start.36 = (bf16[64,1536]{1,0:T(8,128)(2,1)S(1)}, bf16[64,1536]{1,0:T(8,128)(2,1)S(1)}, u32[]{:S(2)}, u32[]{:S(2)}) collective-permute-start(bf16[64,1536]{1,0:T(8,128)(2,1)S(1)} %get-tuple-element.186), channel_id=1, source_target_pairs={{0,24},{1,25},{2,26},{3,27},{4,28},{5,29},{6,30},{7,31},{8,16},{9,... | collective-permute-start | bytes 589832 | tf_op jit(solution)/shard_map/ppermute | solution.py:253
  96.6 8.8 %collective-permute-start.38 = (bf16[256,640]{1,0:T(8,128)(2,1)S(1)}, bf16[256,640]{1,0:T(8,128)(2,1)S(1)}, u32[]{:S(2)}, u32[]{:S(2)}) collective-permute-start(bf16[256,640]{1,0:T(8,128)(2,1)S(1)} %copy-done.10), channel_id=1, source_target_pairs={{0,1},{1,0},{2,3},{3,2},{4,5},{5,4},{6,7},{7,6},{8,9},{9,8},{10,11... | collective-permute-start | bytes 983048 | tf_op jit(solution)/shard_map/ppermute | solution.py:253
  96.6 21.4 %all-to-all-start.1 = ((bf16[4,576,128]{2,1,0:T(8,128)(2,1)}), bf16[4,576,128]{2,1,0:T(8,128)(2,1)S(1)}, u32[]{:S(2)}, u32[]{:S(2)}) async-start(bf16[4,576,128]{2,1,0:T(8,128)(2,1)} %bitcast.33), calls=%async_computation.1 | async-start | bytes 1179648 | tf_op jit(solution)/shard_map/all_to_all | solution.py:1097
  105.3 1.5 collective-permute-start.37
  110.8 12.7 %collective-permute-start.39 = (bf16[64,1536]{1,0:T(8,128)(2,1)S(1)}, bf16[64,1536]{1,0:T(8,128)(2,1)S(1)}, u32[]{:S(2)}, u32[]{:S(2)}) collective-permute-start(bf16[64,1536]{1,0:T(8,128)(2,1)S(1)} %get-tuple-element.199), channel_id=1, source_target_pairs={{0,8},{1,9},{2,10},{3,11},{4,12},{5,13},{6,14},{7,15},{8,0},{9,1},... | collective-permute-start | bytes 589832 | tf_op jit(solution)/shard_map/ppermute | solution.py:253
  112.1 11.4 %collective-permute-start.40 = (bf16[64,1536]{1,0:T(8,128)(2,1)S(1)}, bf16[64,1536]{1,0:T(8,128)(2,1)S(1)}, u32[]{:S(2)}, u32[]{:S(2)}) collective-permute-start(bf16[64,1536]{1,0:T(8,128)(2,1)S(1)} %get-tuple-element.200), channel_id=1, source_target_pairs={{0,16},{1,17},{2,18},{3,19},{4,20},{5,21},{6,22},{7,23},{8,24},{9,... | collective-permute-start | bytes 589832 | tf_op jit(solution)/shard_map/ppermute | solution.py:253
  113.1 10.4 %collective-permute-start.41 = (bf16[64,1536]{1,0:T(8,128)(2,1)S(1)}, bf16[64,1536]{1,0:T(8,128)(2,1)S(1)}, u32[]{:S(2)}, u32[]{:S(2)}) collective-permute-start(bf16[64,1536]{1,0:T(8,128)(2,1)S(1)} %get-tuple-element.201), channel_id=1, source_target_pairs={{0,24},{1,25},{2,26},{3,27},{4,28},{5,29},{6,30},{7,31},{8,16},{9,... | collective-permute-start | bytes 589832 | tf_op jit(solution)/shard_map/ppermute | solution.py:253
  114.3 11.4 %collective-permute-start.43 = (bf16[256,640]{1,0:T(8,128)(2,1)S(1)}, bf16[256,640]{1,0:T(8,128)(2,1)S(1)}, u32[]{:S(2)}, u32[]{:S(2)}) collective-permute-start(bf16[256,640]{1,0:T(8,128)(2,1)S(1)} %copy-done.9), channel_id=1, source_target_pairs={{0,1},{1,0},{2,3},{3,2},{4,5},{5,4},{6,7},{7,6},{8,9},{9,8},{10,11... | collective-permute-start | bytes 983048 | tf_op jit(solution)/shard_map/ppermute | solution.py:253
  118.1 20.0 %all-to-all-start.2 = ((bf16[4,576,128]{2,1,0:T(8,128)(2,1)}), bf16[4,576,128]{2,1,0:T(8,128)(2,1)}, u32[]{:S(2)}, u32[]{:S(2)}) async-start(bf16[4,576,128]{2,1,0:T(8,128)(2,1)} %bitcast.32), calls=%async_computation.2 | async-start | bytes 1179648 | tf_op jit(solution)/shard_map/all_to_all | solution.py:1097
  125.6 1.5 collective-permute-start.42
  131.1 11.5 %collective-permute-start.44 = (bf16[64,1536]{1,0:T(8,128)(2,1)S(1)}, bf16[64,1536]{1,0:T(8,128)(2,1)S(1)}, u32[]{:S(2)}, u32[]{:S(2)}) collective-permute-start(bf16[64,1536]{1,0:T(8,128)(2,1)S(1)} %get-tuple-element.214), channel_id=1, source_target_pairs={{0,8},{1,9},{2,10},{3,11},{4,12},{5,13},{6,14},{7,15},{8,0},{9,1},... | collective-permute-start | bytes 589832 | tf_op jit(solution)/shard_map/ppermute | solution.py:253
  131.7 10.9 %collective-permute-start.45 = (bf16[64,1536]{1,0:T(8,128)(2,1)S(1)}, bf16[64,1536]{1,0:T(8,128)(2,1)S(1)}, u32[]{:S(2)}, u32[]{:S(2)}) collective-permute-start(bf16[64,1536]{1,0:T(8,128)(2,1)S(1)} %get-tuple-element.215), channel_id=1, source_target_pairs={{0,16},{1,17},{2,18},{3,19},{4,20},{5,21},{6,22},{7,23},{8,24},{9,... | collective-permute-start | bytes 589832 | tf_op jit(solution)/shard_map/ppermute | solution.py:253
  132.7 10.1 %collective-permute-start.46 = (bf16[64,1536]{1,0:T(8,128)(2,1)S(1)}, bf16[64,1536]{1,0:T(8,128)(2,1)S(1)}, u32[]{:S(2)}, u32[]{:S(2)}) collective-permute-start(bf16[64,1536]{1,0:T(8,128)(2,1)S(1)} %get-tuple-element.216), channel_id=1, source_target_pairs={{0,24},{1,25},{2,26},{3,27},{4,28},{5,29},{6,30},{7,31},{8,16},{9,... | collective-permute-start | bytes 589832 | tf_op jit(solution)/shard_map/ppermute | solution.py:253
  134.6 8.8 %collective-permute-start.48 = (bf16[256,640]{1,0:T(8,128)(2,1)S(1)}, bf16[256,640]{1,0:T(8,128)(2,1)S(1)}, u32[]{:S(2)}, u32[]{:S(2)}) collective-permute-start(bf16[256,640]{1,0:T(8,128)(2,1)S(1)} %copy-done.8), channel_id=1, source_target_pairs={{0,1},{1,0},{2,3},{3,2},{4,5},{5,4},{6,7},{7,6},{8,9},{9,8},{10,11... | collective-permute-start | bytes 983048 | tf_op jit(solution)/shard_map/ppermute | solution.py:253
  138.0 26.4 %all-to-all-start.3 = ((bf16[4,576,128]{2,1,0:T(8,128)(2,1)}), bf16[4,576,128]{2,1,0:T(8,128)(2,1)S(1)}, u32[]{:S(2)}, u32[]{:S(2)}) async-start(bf16[4,576,128]{2,1,0:T(8,128)(2,1)} %bitcast.31), calls=%async_computation.3 | async-start | bytes 1179648 | tf_op jit(solution)/shard_map/all_to_all | solution.py:1097
  143.3 1.5 collective-permute-start.47
  148.7 7.8 %collective-permute-start.49 = (bf16[64,1536]{1,0:T(8,128)(2,1)S(1)}, bf16[64,1536]{1,0:T(8,128)(2,1)S(1)}, u32[]{:S(2)}, u32[]{:S(2)}) collective-permute-start(bf16[64,1536]{1,0:T(8,128)(2,1)S(1)} %get-tuple-element.231), channel_id=1, source_target_pairs={{0,8},{1,9},{2,10},{3,11},{4,12},{5,13},{6,14},{7,15},{8,0},{9,1},... | collective-permute-start | bytes 589832 | tf_op jit(solution)/shard_map/ppermute | solution.py:253
  150.0 16.8 %collective-permute-start.56 = (bf16[64,1536]{1,0:T(8,128)(2,1)S(1)}, bf16[64,1536]{1,0:T(8,128)(2,1)S(1)}, u32[]{:S(2)}, u32[]{:S(2)}) collective-permute-start(bf16[64,1536]{1,0:T(8,128)(2,1)S(1)} %get-tuple-element.248), channel_id=1, source_target_pairs={{0,16},{1,17},{2,18},{3,19},{4,20},{5,21},{6,22},{7,23},{8,24},{9,... | collective-permute-start | bytes 589832 | tf_op jit(solution)/shard_map/ppermute | solution.py:253
  151.1 15.8 %collective-permute-start.57 = (bf16[64,1536]{1,0:T(8,128)(2,1)S(1)}, bf16[64,1536]{1,0:T(8,128)(2,1)S(1)}, u32[]{:S(2)}, u32[]{:S(2)}) collective-permute-start(bf16[64,1536]{1,0:T(8,128)(2,1)S(1)} %get-tuple-element.249), channel_id=1, source_target_pairs={{0,24},{1,25},{2,26},{3,27},{4,28},{5,29},{6,30},{7,31},{8,16},{9,... | collective-permute-start | bytes 589832 | tf_op jit(solution)/shard_map/ppermute | solution.py:253
  152.2 19.9 %collective-permute-start.51 = (bf16[592,128]{1,0:T(8,128)(2,1)}, bf16[592,128]{1,0:T(8,128)(2,1)S(1)}, u32[]{:S(2)}, u32[]{:S(2)}) collective-permute-start(bf16[592,128]{1,0:T(8,128)(2,1)} %get-tuple-element.233), channel_id=1, source_target_pairs={{0,4},{1,5},{2,6},{3,7},{4,0},{5,1},{6,2},{7,3},{8,12},{9,13},{10,... | collective-permute-start | bytes 454664 | tf_op jit(solution)/shard_map/ppermute | solution.py:253
  155.0 17.2 %collective-permute-start.52 = (bf16[592,128]{1,0:T(8,128)(2,1)}, bf16[592,128]{1,0:T(8,128)(2,1)S(1)}, u32[]{:S(2)}, u32[]{:S(2)}) collective-permute-start(bf16[592,128]{1,0:T(8,128)(2,1)} %get-tuple-element.234), channel_id=1, source_target_pairs={{0,6},{1,7},{2,4},{3,5},{4,2},{5,3},{6,0},{7,1},{8,14},{9,15},{10,... | collective-permute-start | bytes 454664 | tf_op jit(solution)/shard_map/ppermute | solution.py:253
  156.5 15.7 %collective-permute-start.50 = (bf16[592,128]{1,0:T(8,128)(2,1)}, bf16[592,128]{1,0:T(8,128)(2,1)S(1)}, u32[]{:S(2)}, u32[]{:S(2)}) collective-permute-start(bf16[592,128]{1,0:T(8,128)(2,1)} %get-tuple-element.232), channel_id=1, source_target_pairs={{0,2},{1,3},{2,0},{3,1},{4,6},{5,7},{6,4},{7,5},{8,10},{9,11},{10,... | collective-permute-start | bytes 454664 | tf_op jit(solution)/shard_map/ppermute | solution.py:253
  169.4 16.9 %collective-permute-start.60 = (bf16[256,384]{1,0:T(8,128)(2,1)S(1)}, bf16[256,384]{1,0:T(8,128)(2,1)S(1)}, u32[]{:S(2)}, u32[]{:S(2)}) collective-permute-start(bf16[256,384]{1,0:T(8,128)(2,1)S(1)} %get-tuple-element.258), channel_id=1, source_target_pairs={{0,0},{1,5},{2,8},{3,13},{4,16},{5,21},{6,24},{7,29},{8,2},{9,7},{... | collective-permute-start | bytes 589832 | tf_op jit(solution)/shard_map/ppermute | solution.py:253
  170.1 16.2 %collective-permute-start.61 = (bf16[256,384]{1,0:T(8,128)(2,1)S(1)}, bf16[256,384]{1,0:T(8,128)(2,1)S(1)}, u32[]{:S(2)}, u32[]{:S(2)}) collective-permute-start(bf16[256,384]{1,0:T(8,128)(2,1)S(1)} %get-tuple-element.259), channel_id=1, source_target_pairs={{0,2},{1,7},{2,10},{3,15},{4,18},{5,23},{6,26},{7,31},{8,0},{9,5},... | collective-permute-start | bytes 589832 | tf_op jit(solution)/shard_map/ppermute | solution.py:253
  172.4 9.9 %collective-permute-start.53 = (bf16[592,128]{1,0:T(8,128)(2,1)S(1)}, bf16[592,128]{1,0:T(8,128)(2,1)S(1)}, u32[]{:S(2)}, u32[]{:S(2)}) collective-permute-start(bf16[592,128]{1,0:T(8,128)(2,1)S(1)} %get-tuple-element.244), channel_id=1, source_target_pairs={{0,8},{1,9},{2,10},{3,11},{4,12},{5,13},{6,14},{7,15},{8,0},{9,1},... | collective-permute-start | bytes 454664 | tf_op jit(solution)/shard_map/ppermute | solution.py:253
  172.5 13.8 %collective-permute-start.54 = (bf16[592,128]{1,0:T(8,128)(2,1)S(1)}, bf16[592,128]{1,0:T(8,128)(2,1)S(1)}, u32[]{:S(2)}, u32[]{:S(2)}) collective-permute-start(bf16[592,128]{1,0:T(8,128)(2,1)S(1)} %get-tuple-element.245), channel_id=1, source_target_pairs={{0,16},{1,17},{2,18},{3,19},{4,20},{5,21},{6,22},{7,23},{8,24},{9,... | collective-permute-start | bytes 454664 | tf_op jit(solution)/shard_map/ppermute | solution.py:253
  178.0 8.3 %collective-permute-start.55 = (bf16[592,128]{1,0:T(8,128)(2,1)S(1)}, bf16[592,128]{1,0:T(8,128)(2,1)S(1)}, u32[]{:S(2)}, u32[]{:S(2)}) collective-permute-start(bf16[592,128]{1,0:T(8,128)(2,1)S(1)} %get-tuple-element.246), channel_id=1, source_target_pairs={{0,24},{1,25},{2,26},{3,27},{4,28},{5,29},{6,30},{7,31},{8,16},{9,... | collective-permute-start | bytes 454664 | tf_op jit(solution)/shard_map/ppermute | solution.py:253
  186.3 1.4 collective-permute-start.62
  186.4 2.7 %collective-permute-start.66 = (bf16[256,384]{1,0:T(8,128)(2,1)S(1)}, bf16[256,384]{1,0:T(8,128)(2,1)S(1)}, u32[]{:S(2)}, u32[]{:S(2)}) collective-permute-start(bf16[256,384]{1,0:T(8,128)(2,1)S(1)} %collective-permute-done.60.refs_9_), channel_id=1, source_target_pairs={{0,1},{1,0},{2,3},{3,2},{4,5},{5,4},{6,7},{7,6},{8,9},{9,8},{10,11... | collective-permute-start | bytes 589832 | tf_op jit(solution)/shard_map/ppermute | solution.py:253
  186.9 2.2 %collective-permute-start.67 = (bf16[256,384]{1,0:T(8,128)(2,1)S(1)}, bf16[256,384]{1,0:T(8,128)(2,1)S(1)}, u32[]{:S(2)}, u32[]{:S(2)}) collective-permute-start(bf16[256,384]{1,0:T(8,128)(2,1)S(1)} %collective-permute-done.61.refs_10_), channel_id=1, source_target_pairs={{0,1},{1,0},{2,3},{3,2},{4,5},{5,4},{6,7},{7,6},{8,9},{9,8},{10,11... | collective-permute-start | bytes 589832 | tf_op jit(solution)/shard_map/ppermute | solution.py:253
  187.0 1.6 collective-permute-start.63
  (20 other events, 144.7 us)

commit v10 on v8

--- a/solution.py
+++ b/solution.py
@@ -1068,6 +1068,18 @@
     shares = [None] * layers
     for layer in range(last, -1, -1):
         share_out = ((4 * piece_rows[layer], 2 * ch), bf16)
+        other = to_core(grad_pre)
+        if layer:
+            held = call(
+                partial(fetch_kernel, layer - 1),
+                [kept_out, ((META_ROWS, channels), bf16)],
+                [],
+                [after(kept[layer - 1], grad_pre), *slices],
+                "fetch",
+                held=range(5),
+                copies=2,
+            )
+            other, held = lax.optimization_barrier((other, held))
         pieces = [share_out] if layer else [((slice_rows, 2 * ch), bf16)] * 4
         outs = call(
             partial(conv_back_kernel, dims, layer),
@@ -1078,7 +1090,7 @@
                 ((2 * tap_rows, length), bf16),
                 ((4 * ch, 2 * tap_rows), bf16),
             ],
-            [grad_pre, to_core(grad_pre), turned, crossing[layer], fulls[layer], facts]
+            [grad_pre, other, turned, crossing[layer], fulls[layer], facts]
             + ([] if layer else [sums]),
             "conv_back",
             held=(2, 4),
@@ -1097,16 +1109,7 @@
         shares[layer] = lax.all_to_all(share[0], "dp", 0, 0, tiled=True, axis_index_groups=same_core)
         if layer:
             crossing[layer - 1] = to_core(after(crossing[layer - 1], parts))
-            held = call(
-                partial(fetch_kernel, layer - 1),
-                [kept_out, ((META_ROWS, channels), bf16)],
-                [],
-                [after(kept[layer - 1], parts), *slices],
-                "fetch",
-                held=range(5),
-                copies=2,
-            )
-            blocks = spread(parts, to_section, held)
+            blocks = spread(parts, to_section)
             grad_pre, sums = call(
                 partial(norm_back_kernel, dims, layer - 1, layer - 1 == CONVS - 1),
                 [map_out, sums_out],

time: 191 us -> 191 us (level)
  no operation moved by 1% of the time
where the time goes in v10:
time: 191 us; the launch traced here: 190 us
  starting transfers between devices  74.3 us (39%)
  waiting for transfers between devices  63.8 us (33%)
  Pallas kernels  50.4 us (26%)
    ppermute x67, waiting for transfers between devices, send(): return lax.ppermute(x, AXES, pairs)  57.9 us
    ppermute x67, starting transfers between devices, send(): return lax.ppermute(x, AXES, pairs)  56.7 us
    pallas_call x27, Pallas kernels, call(): pl.pallas_call(kernel, out_shape=shapes, in_specs=[pl.BlockSpec(memory_sp...  50.4 us
    all_to_all x3, starting transfers between devices, plane_shards(): lax.all_to_all(share[0], 'dp', 0, 0, tiled=True, axis_index_groups=same_c...  12.7 us
    all_to_all x3, waiting for transfers between devices, plane_shards(): lax.all_to_all(share[0], 'dp', 0, 0, tiled=True, axis_index_groups=same_c...  5.9 us
    all_to_all x1, starting transfers between devices, plane_shards(): lax.all_to_all(cot_slots, 'dp', 0, 0, tiled=True, axis_index_groups=same_...  4.87 us
  transfers between devices with their start and end apart: 71, of which 37 were waited for; matrix products, arithmetic and copies ran while one was open for 0% of the time, Pallas kernels for 19%

profile of v10, /device:TPU:0, one launch (start us, length us, event | category | flops | bytes accessed | tf_op | source)
XLA Modules:
  0.0 189.9 jit_solution(5333349937734241872)
XLA Ops:
  0.6 2.5 %weight_pack.1 = (bf16[592,512]{1,0:T(8,128)(2,1)S(1)}, bf16[592,512]{1,0:T(8,128)(2,1)S(1)}, bf16[592,512]{1,0:T(8,128)(2,1)S(1)}, bf16[592,512]{1,0:T(8,128)(2,1)S(1)}) custom-call(f32[1,512]{1,0:T(1,128)} %gain.1, f32[1,512]{1,0:T(1,128)} %bias.1, bf16[9,512,512]{2,1,0:T(8,128)(2,1)} %bitcast.26), custom_call_target="tpu_custom_call" | custom-call | bytes 7147520 | tf_op jit(solution)/shard_map/weight_pack/pallas_call | solution.py:895
  3.1 3.0 %collective-permute-start.7 = (bf16[592,512]{1,0:T(8,128)(2,1)S(1)}, bf16[592,512]{1,0:T(8,128)(2,1)S(1)}, u32[]{:S(2)}, u32[]{:S(2)}) collective-permute-start(bf16[592,512]{1,0:T(8,128)(2,1)S(1)} %get-tuple-element.143), channel_id=1, source_target_pairs={{0,8},{1,9},{2,10},{3,11},{4,12},{5,13},{6,14},{7,15},{8,0},{9,1},... | collective-permute-start | bytes 1818632 | tf_op jit(solution)/shard_map/ppermute | solution.py:253
  6.2 1.5 collective-permute-start.8
  7.7 1.4 frames.1
  9.1 1.6 collective-permute-start
  11.2 2.6 %collective-permute-start.1 = (bf16[208,512]{1,0:T(8,128)(2,1)S(1)}, bf16[208,512]{1,0:T(8,128)(2,1)S(1)}, u32[]{:S(2)}, u32[]{:S(2)}) collective-permute-start(bf16[208,512]{1,0:T(8,128)(2,1)S(1)} %get-tuple-element.149), channel_id=1, source_target_pairs={{0,4},{1,5},{2,6},{3,7},{4,0},{5,1},{6,2},{7,3},{8,12},{9,13},{10,... | collective-permute-start | bytes 638984 | tf_op jit(solution)/shard_map/ppermute | solution.py:253
  13.8 6.1 %collective-permute-done.refs_1_ = bf16[208,512]{1,0:T(8,128)(2,1)S(1)} collective-permute-done((bf16[208,512]{1,0:T(8,128)(2,1)S(1)}, bf16[208,512]{1,0:T(8,128)(2,1)S(1)}, u32[]{:S(2)}, u32[]{:S(2)}) %collective-permute-start) | collective-permute-done | bytes 213024 | tf_op jit(solution)/shard_map/ppermute | solution.py:253
  19.8 2.5 %collective-permute-start.2 = (bf16[208,512]{1,0:T(8,128)(2,1)S(1)}, bf16[208,512]{1,0:T(8,128)(2,1)S(1)}, u32[]{:S(2)}, u32[]{:S(2)}) collective-permute-start(bf16[208,512]{1,0:T(8,128)(2,1)S(1)} %get-tuple-element.150), channel_id=1, source_target_pairs={{0,6},{1,7},{2,4},{3,5},{4,2},{5,3},{6,0},{7,1},{8,14},{9,15},{10,... | collective-permute-start | bytes 638984 | tf_op jit(solution)/shard_map/ppermute | solution.py:253
  22.3 2.8 %collective-permute-done.1.refs_2_ = bf16[208,512]{1,0:T(8,128)(2,1)S(1)} collective-permute-done((bf16[208,512]{1,0:T(8,128)(2,1)S(1)}, bf16[208,512]{1,0:T(8,128)(2,1)S(1)}, u32[]{:S(2)}, u32[]{:S(2)}) %collective-permute-start.1) | collective-permute-done | bytes 213024 | tf_op jit(solution)/shard_map/ppermute | solution.py:253
  25.1 2.5 %collective-permute-done.2.refs_3_ = bf16[208,512]{1,0:T(8,128)(2,1)S(1)} collective-permute-done((bf16[208,512]{1,0:T(8,128)(2,1)S(1)}, bf16[208,512]{1,0:T(8,128)(2,1)S(1)}, u32[]{:S(2)}, u32[]{:S(2)}) %collective-permute-start.2) | collective-permute-done | bytes 213024 | tf_op jit(solution)/shard_map/ppermute | solution.py:253
  28.1 6.2 %collective-permute-done.8.refs_10_.refs_2_ = bf16[592,512]{1,0:T(8,128)(2,1)S(1)} collective-permute-done((bf16[592,512]{1,0:T(8,128)(2,1)S(1)}, bf16[592,512]{1,0:T(8,128)(2,1)S(1)}, u32[]{:S(2)}, u32[]{:S(2)}) %collective-permute-start.8) | collective-permute-done | bytes 606240 | tf_op jit(solution)/shard_map/ppermute | solution.py:253
  34.4 1.4 collective-permute-done.6.refs_7_
  35.8 2.5 %forward.3 = (bf16[64,1536]{1,0:T(8,128)(2,1)S(1)}, f32[64,1664]{1,0:T(8,128)}, bf16[1536,512]{1,0:T(8,128)(2,1)}, f32[1,1536]{1,0:T(1,128)S(1)}) custom-call(bf16[208,512]{1,0:T(8,128)(2,1)S(1)} %get-tuple-element.147.refs_0_, bf16[208,512]{1,0:T(8,128)(2,1)S(1)} %collective-permute-done.refs_1_, bf16[208,512]{1,0:T(8,128)(2,1)S(1)} %collective-permute-done.1.refs_2_, ...), custom_call_target="tpu_custom_call" | custom-call | flops 905969664 | bytes 6428672 | tf_op jit(solution)/shard_map/forward/pallas_call | solution.py:895
  38.4 1.5 collective-permute-start.12
  39.9 1.5 collective-permute-start.10
  41.9 2.0 %cot_slices.1 = bf16[768,128]{1,0:T(8,128)(2,1)} custom-call(bf16[4,192,512]{2,1,0:T(8,128)(2,1)} %bitcast.30), custom_call_target="tpu_custom_call" | custom-call | bytes 983040 | tf_op jit(solution)/shard_map/cot_slices/pallas_call | solution.py:895
  43.9 3.7 %turn_weights.1 = (bf16[1024,640]{1,0:T(8,128)(2,1)}, bf16[256,640]{1,0:T(8,128)(2,1)}, bf16[256,640]{1,0:T(8,128)(2,1)}, bf16[256,640]{1,0:T(8,128)(2,1)}, bf16[256,640]{1,0:T(8,128)(2,1)}) custom-call(bf16[592,512]{1,0:T(8,128)(2,1)} %copy-done, bf16[592,512]{1,0:T(8,128)(2,1)} %copy-done.1, bf16[592,512]{1,0:T(8,128)(2,1)} %copy-done.2, ...), custom_call_target="tpu_custom_call" | custom-call | bytes 5046272 | tf_op jit(solution)/shard_map/turn_weights/pallas_call | solution.py:895
  47.7 1.1 pick.3.refs_8_
  49.3 1.2 collective-permute-done.10.refs_1_
  52.3 3.1 %forward.4 = (bf16[64,1536]{1,0:T(8,128)(2,1)S(1)}, f32[64,1664]{1,0:T(8,128)}, bf16[512,1536]{1,0:T(8,128)(2,1)}) custom-call(bf16[64,1536]{1,0:T(8,128)(2,1)S(1)} %get-tuple-element.157.refs_0_, bf16[64,1536]{1,0:T(8,128)(2,1)S(1)} %collective-permute-done.10.refs_1_, bf16[64,1536]{1,0:T(8,128)(2,1)S(1)} %collective-permute-done.11.refs_2_, ...), custom_call_target="tpu_custom_call" | custom-call | flops 905969664 | bytes 4478976 | tf_op jit(solution)/shard_map/forward/pallas_call | solution.py:895
  55.4 1.2 collective-permute-start.19
  56.5 1.5 collective-permute-start.17
  58.9 4.9 %all-to-all-start = ((bf16[4,192,128]{2,1,0:T(8,128)(2,1)}), bf16[4,192,128]{2,1,0:T(8,128)(2,1)S(1)}, u32[]{:S(2)}, u32[]{:S(2)}) async-start(bf16[4,192,128]{2,1,0:T(8,128)(2,1)} %bitcast.7), calls=%async_computation | async-start | bytes 393216 | tf_op jit(solution)/shard_map/all_to_all | solution.py:1025
  63.8 1.1 pick.4.refs_8_
  65.2 2.0 %collective-permute-done.17.refs_1_ = bf16[64,1536]{1,0:T(8,128)(2,1)S(1)} collective-permute-done((bf16[64,1536]{1,0:T(8,128)(2,1)S(1)}, bf16[64,1536]{1,0:T(8,128)(2,1)S(1)}, u32[]{:S(2)}, u32[]{:S(2)}) %collective-permute-start.17) | collective-permute-done | bytes 196640 | tf_op jit(solution)/shard_map/ppermute | solution.py:253
  69.0 2.4 %forward.5 = (bf16[64,1536]{1,0:T(8,128)(2,1)S(1)}, f32[64,1664]{1,0:T(8,128)}, bf16[512,1536]{1,0:T(8,128)(2,1)}) custom-call(bf16[64,1536]{1,0:T(8,128)(2,1)S(1)} %get-tuple-element.170.refs_0_, bf16[64,1536]{1,0:T(8,128)(2,1)S(1)} %collective-permute-done.17.refs_1_, bf16[64,1536]{1,0:T(8,128)(2,1)S(1)} %collective-permute-done.18.refs_2_, ...), custom_call_target="tpu_custom_call" | custom-call | flops 905969664 | bytes 4478976 | tf_op jit(solution)/shard_map/forward/pallas_call | solution.py:895
  71.5 1.1 collective-permute-start.26
  72.6 1.5 collective-permute-start.24
  75.7 1.1 pick.5.refs_8_
  77.1 3.1 %collective-permute-done.26.refs_3_ = bf16[64,1536]{1,0:T(8,128)(2,1)S(1)} collective-permute-done((bf16[64,1536]{1,0:T(8,128)(2,1)S(1)}, bf16[64,1536]{1,0:T(8,128)(2,1)S(1)}, u32[]{:S(2)}, u32[]{:S(2)}) %collective-permute-start.26) | collective-permute-done | bytes 196640 | tf_op jit(solution)/shard_map/ppermute | solution.py:253
  80.2 3.0 %collective-permute-done.24.refs_1_ = bf16[64,1536]{1,0:T(8,128)(2,1)S(1)} collective-permute-done((bf16[64,1536]{1,0:T(8,128)(2,1)S(1)}, bf16[64,1536]{1,0:T(8,128)(2,1)S(1)}, u32[]{:S(2)}, u32[]{:S(2)}) %collective-permute-start.24) | collective-permute-done | bytes 196640 | tf_op jit(solution)/shard_map/ppermute | solution.py:253
  85.1 2.5 %turn.1 = (bf16[64,1536]{1,0:T(8,128)(2,1)}, bf16[512,1536]{1,0:T(8,128)(2,1)}, bf16[64,1536]{1,0:T(8,128)(2,1)S(1)}, f32[64,128]{1,0:T(8,128)S(1)}) custom-call(bf16[64,1536]{1,0:T(8,128)(2,1)S(1)} %get-tuple-element.176.refs_0_, bf16[64,1536]{1,0:T(8,128)(2,1)S(1)} %collective-permute-done.24.refs_1_, ...), custom_call_target="tpu_custom_call" | custom-call | flops 905969664 | bytes 4478976 | tf_op jit(solution)/shard_map/turn/pallas_call | solution.py:895
  89.1 3.9 %conv_back.4 = (bf16[64,1536]{1,0:T(8,128)(2,1)S(1)}, bf16[64,1536]{1,0:T(8,128)(2,1)S(1)}, bf16[64,1536]{1,0:T(8,128)(2,1)S(1)}, bf16[64,1536]{1,0:T(8,128)(2,1)S(1)}, bf16[2304,128]{1,0:T(8,128)(2,1)}) custom-call(bf16[64,1536]{1,0:T(8,128)(2,1)S(1)} %get-tuple-element.184.own, bf16[64,1536]{1,0:T(8,128)(2,1)S(1)} %collective-permute-done.32.other, ...), custom_call_target="tpu_custom_call" | custom-call | bytes 5079040 | tf_op jit(solution)/shard_map/conv_back/pallas_call | solution.py:895
  93.6 1.0 collective-permute-start.35
  94.7 1.9 %collective-permute-start.36 = (bf16[64,1536]{1,0:T(8,128)(2,1)S(1)}, bf16[64,1536]{1,0:T(8,128)(2,1)S(1)}, u32[]{:S(2)}, u32[]{:S(2)}) collective-permute-start(bf16[64,1536]{1,0:T(8,128)(2,1)S(1)} %get-tuple-element.195), channel_id=1, source_target_pairs={{0,24},{1,25},{2,26},{3,27},{4,28},{5,29},{6,30},{7,31},{8,16},{9,... | collective-permute-start | bytes 589832 | tf_op jit(solution)/shard_map/ppermute | solution.py:253
  96.6 4.9 %all-to-all-start.1 = ((bf16[4,576,128]{2,1,0:T(8,128)(2,1)}), bf16[4,576,128]{2,1,0:T(8,128)(2,1)S(1)}, u32[]{:S(2)}, u32[]{:S(2)}) async-start(bf16[4,576,128]{2,1,0:T(8,128)(2,1)} %bitcast.33), calls=%async_computation.1 | async-start | bytes 1179648 | tf_op jit(solution)/shard_map/all_to_all | solution.py:1109
  101.5 3.2 %collective-permute-done.36.refs_3_ = bf16[64,1536]{1,0:T(8,128)(2,1)S(1)} collective-permute-done((bf16[64,1536]{1,0:T(8,128)(2,1)S(1)}, bf16[64,1536]{1,0:T(8,128)(2,1)S(1)}, u32[]{:S(2)}, u32[]{:S(2)}) %collective-permute-start.36) | collective-permute-done | bytes 196640 | tf_op jit(solution)/shard_map/ppermute | solution.py:253
  106.8 3.9 %conv_back.5 = (bf16[64,1536]{1,0:T(8,128)(2,1)S(1)}, bf16[64,1536]{1,0:T(8,128)(2,1)S(1)}, bf16[64,1536]{1,0:T(8,128)(2,1)S(1)}, bf16[64,1536]{1,0:T(8,128)(2,1)S(1)}, bf16[2304,128]{1,0:T(8,128)(2,1)}) custom-call(bf16[64,1536]{1,0:T(8,128)(2,1)S(1)} %get-tuple-element.202.own, bf16[64,1536]{1,0:T(8,128)(2,1)S(1)} %collective-permute-done.37.other, ...), custom_call_target="tpu_custom_call" | custom-call | flops 5200000000 | bytes 5079040 | tf_op jit(solution)/shard_map/conv_back/pallas_call | solution.py:895
  110.7 1.4 collective-permute-start.39
  113.1 1.2 collective-permute-start.41
  114.3 2.5 %all-to-all-done.1 = bf16[4,576,128]{2,1,0:T(8,128)(2,1)S(1)} async-done(((bf16[4,576,128]{2,1,0:T(8,128)(2,1)}), bf16[4,576,128]{2,1,0:T(8,128)(2,1)S(1)}, u32[]{:S(2)}, u32[]{:S(2)}) %all-to-all-start.1) | async-done | bytes 589856 | tf_op jit(solution)/shard_map/all_to_all | solution.py:1109
  116.9 4.4 %all-to-all-start.2 = ((bf16[4,576,128]{2,1,0:T(8,128)(2,1)}), bf16[4,576,128]{2,1,0:T(8,128)(2,1)}, u32[]{:S(2)}, u32[]{:S(2)}) async-start(bf16[4,576,128]{2,1,0:T(8,128)(2,1)} %bitcast.32), calls=%async_computation.2 | async-start | bytes 1179648 | tf_op jit(solution)/shard_map/all_to_all | solution.py:1109
  121.3 1.6 collective-permute-done.40.refs_2_
  123.0 2.1 %norm_back.4 = (bf16[64,1536]{1,0:T(8,128)(2,1)S(1)}, f32[64,128]{1,0:T(8,128)S(1)}) custom-call(bf16[64,1536]{1,0:T(8,128)(2,1)S(1)} %get-tuple-element.210.refs_0_, bf16[64,1536]{1,0:T(8,128)(2,1)S(1)} %collective-permute-done.39.refs_1_, bf16[64,1536]{1,0:T(8,128)(2,1)S(1)} %collective-permute-done.40.refs_2_, ...), custom_call_target="tpu_custom_call" | custom-call | bytes 1595392 | tf_op jit(solution)/shard_map/norm_back/pallas_call | solution.py:895
  126.6 3.9 %conv_back.6 = (bf16[64,1536]{1,0:T(8,128)(2,1)S(1)}, bf16[64,1536]{1,0:T(8,128)(2,1)S(1)}, bf16[64,1536]{1,0:T(8,128)(2,1)S(1)}, bf16[64,1536]{1,0:T(8,128)(2,1)S(1)}, bf16[2304,128]{1,0:T(8,128)(2,1)}) custom-call(bf16[64,1536]{1,0:T(8,128)(2,1)S(1)} %get-tuple-element.220.own, bf16[64,1536]{1,0:T(8,128)(2,1)S(1)} %collective-permute-done.42.other, ...), custom_call_target="tpu_custom_call" | custom-call | flops 5200000000 | bytes 5079040 | tf_op jit(solution)/shard_map/conv_back/pallas_call | solution.py:895
  132.3 1.7 collective-permute-start.46
  134.1 2.4 %all-to-all-done.2 = bf16[4,576,128]{2,1,0:T(8,128)(2,1)} async-done(((bf16[4,576,128]{2,1,0:T(8,128)(2,1)}), bf16[4,576,128]{2,1,0:T(8,128)(2,1)}, u32[]{:S(2)}, u32[]{:S(2)}) %all-to-all-start.2) | async-done | bytes 589856 | tf_op jit(solution)/shard_map/all_to_all | solution.py:1109
  136.5 3.5 %all-to-all-start.3 = ((bf16[4,576,128]{2,1,0:T(8,128)(2,1)}), bf16[4,576,128]{2,1,0:T(8,128)(2,1)S(1)}, u32[]{:S(2)}, u32[]{:S(2)}) async-start(bf16[4,576,128]{2,1,0:T(8,128)(2,1)} %bitcast.31), calls=%async_computation.3 | async-start | bytes 1179648 | tf_op jit(solution)/shard_map/all_to_all | solution.py:1109
  140.1 2.1 %collective-permute-done.46.refs_3_ = bf16[64,1536]{1,0:T(8,128)(2,1)S(1)} collective-permute-done((bf16[64,1536]{1,0:T(8,128)(2,1)S(1)}, bf16[64,1536]{1,0:T(8,128)(2,1)S(1)}, u32[]{:S(2)}, u32[]{:S(2)}) %collective-permute-start.46) | collective-permute-done | bytes 196640 | tf_op jit(solution)/shard_map/ppermute | solution.py:253
  142.8 1.4 collective-permute-done.47.other
  144.3 3.9 %conv_back.7 = (bf16[64,1536]{1,0:T(8,128)(2,1)S(1)}, bf16[64,1536]{1,0:T(8,128)(2,1)S(1)}, bf16[64,1536]{1,0:T(8,128)(2,1)S(1)}, bf16[64,1536]{1,0:T(8,128)(2,1...) custom-call(bf16[64,1536]{1,0:T(8,128)(2,1)S(1)} %get-tuple-element., ...), custom_call_target="tpu_custom_call" | custom-call | flops 3000000000 | bytes 5128192 | tf_op jit(solution)/shard_map/conv_back/pallas_call | solution.py:895
  148.1 1.4 collective-permute-start.49
  150.5 1.2 collective-permute-start.61
  151.7 2.6 %collective-permute-start.51 = (bf16[592,128]{1,0:T(8,128)(2,1)}, bf16[592,128]{1,0:T(8,128)(2,1)S(1)}, u32[]{:S(2)}, u32[]{:S(2)}) collective-permute-start(bf16[592,128]{1,0:T(8,128)(2,1)} %get-tuple-element.246), channel_id=1, source_target_pairs={{0,4},{1,5},{2,6},{3,7},{4,0},{5,1},{6,2},{7,3},{8,12},{9,13},{10,... | collective-permute-start | bytes 454664 | tf_op jit(solution)/shard_map/ppermute | solution.py:253
  154.3 1.3 collective-permute-start.52
  156.0 1.6 collective-permute-start.50
  157.5 2.8 %collective-permute-done.60.refs_2_ = bf16[64,1536]{1,0:T(8,128)(2,1)S(1)} collective-permute-done((bf16[64,1536]{1,0:T(8,128)(2,1)S(1)}, bf16[64,1536]{1,0:T(8,128)(2,1)S(1)}, u32[]{:S(2)}, u32[]{:S(2)}) %collective-permute-start.60) | collective-permute-done | bytes 196640 | tf_op jit(solution)/shard_map/ppermute | solution.py:253
  161.3 1.2 input.1
  162.6 1.5 fold.1
  164.1 1.5 collective-permute-done.51.refs_2_
  168.2 4.1 %collective-permute-start.64 = (bf16[256,384]{1,0:T(8,128)(2,1)S(1)}, bf16[256,384]{1,0:T(8,128)(2,1)S(1)}, u32[]{:S(2)}, u32[]{:S(2)}) collective-permute-start(bf16[256,384]{1,0:T(8,128)(2,1)S(1)} %get-tuple-element.271), channel_id=1, source_target_pairs={{0,2},{1,7},{2,10},{3,15},{4,18},{5,23},{6,26},{7,31},{8,0},{9,5},... | collective-permute-start | bytes 589832 | tf_op jit(solution)/shard_map/ppermute | solution.py:253
  172.3 3.7 %collective-permute-start.54 = (bf16[592,128]{1,0:T(8,128)(2,1)S(1)}, bf16[592,128]{1,0:T(8,128)(2,1)S(1)}, u32[]{:S(2)}, u32[]{:S(2)}) collective-permute-start(bf16[592,128]{1,0:T(8,128)(2,1)S(1)} %get-tuple-element.258), channel_id=1, source_target_pairs={{0,16},{1,17},{2,18},{3,19},{4,20},{5,21},{6,22},{7,23},{8,24},{9,... | collective-permute-start | bytes 454664 | tf_op jit(solution)/shard_map/ppermute | solution.py:253
  176.5 9.0 %collective-permute-done.54.refs_2_ = bf16[592,128]{1,0:T(8,128)(2,1)S(1)} collective-permute-done((bf16[592,128]{1,0:T(8,128)(2,1)S(1)}, bf16[592,128]{1,0:T(8,128)(2,1)S(1)}, u32[]{:S(2)}, u32[]{:S(2)}) %collective-permute-start.54) | collective-permute-done | bytes 151584 | tf_op jit(solution)/shard_map/ppermute | solution.py:253
  188.0 1.9 %outputs.1 = (f32[9,64,512]{2,1,0:T(8,128)}, f32[1,64]{1,0:T(1,128)}, f32[1,64]{1,0:T(1,128)}, bf16[192,512]{1,0:T(8,128)(2,1)}, bf16[192,512]{1,0:T(8,128)(2,1)}) custom-call(bf16[592,128]{1,0:T(8,128)(2,1)S(1)} %get-tuple-element.256.refs_0_, bf16[592,128]{1,0:T(8,128)(2,1)S(1)} %collective-permute-done.53.refs_1_, ...), custom_call_target="tpu_custom_call" | custom-call | bytes 3736064 | tf_op jit(solution)/shard_map/outputs/pallas_call | solution.py:895
  (133 shorter events, 27.7 us)
Async XLA Ops:
  3.1 24.4 %collective-permute-start.7 = (bf16[592,512]{1,0:T(8,128)(2,1)S(1)}, bf16[592,512]{1,0:T(8,128)(2,1)S(1)}, u32[]{:S(2)}, u32[]{:S(2)}) collective-permute-start(bf16[592,512]{1,0:T(8,128)(2,1)S(1)} %get-tuple-element.143), channel_id=1, source_target_pairs={{0,8},{1,9},{2,10},{3,11},{4,12},{5,13},{6,14},{7,15},{8,0},{9,1},... | collective-permute-start | bytes 1818632 | tf_op jit(solution)/shard_map/ppermute | solution.py:253
  6.2 28.1 %collective-permute-start.8 = (bf16[592,512]{1,0:T(8,128)(2,1)S(1)}, bf16[592,512]{1,0:T(8,128)(2,1)S(1)}, u32[]{:S(2)}, u32[]{:S(2)}) collective-permute-start(bf16[592,512]{1,0:T(8,128)(2,1)S(1)} %get-tuple-element.144), channel_id=1, source_target_pairs={{0,16},{1,17},{2,18},{3,19},{4,20},{5,21},{6,22},{7,23},{8,24},{9,... | collective-permute-start | bytes 1818632 | tf_op jit(solution)/shard_map/ppermute | solution.py:253
  9.1 10.8 %collective-permute-start = (bf16[208,512]{1,0:T(8,128)(2,1)S(1)}, bf16[208,512]{1,0:T(8,128)(2,1)S(1)}, u32[]{:S(2)}, u32[]{:S(2)}) collective-permute-start(bf16[208,512]{1,0:T(8,128)(2,1)S(1)} %get-tuple-element.148), channel_id=1, source_target_pairs={{0,2},{1,3},{2,0},{3,1},{4,6},{5,7},{6,4},{7,5},{8,10},{9,11},{10,... | collective-permute-start | bytes 638984 | tf_op jit(solution)/shard_map/ppermute | solution.py:253
  10.7 23.6 %collective-permute-start.9 = (bf16[592,512]{1,0:T(8,128)(2,1)S(1)}, bf16[592,512]{1,0:T(8,128)(2,1)S(1)}, u32[]{:S(2)}, u32[]{:S(2)}) collective-permute-start(bf16[592,512]{1,0:T(8,128)(2,1)S(1)} %get-tuple-element.145), channel_id=1, source_target_pairs={{0,24},{1,25},{2,26},{3,27},{4,28},{5,29},{6,30},{7,31},{8,16},{9,... | collective-permute-start | bytes 1818632 | tf_op jit(solution)/shard_map/ppermute | solution.py:253
  11.2 13.9 %collective-permute-start.1 = (bf16[208,512]{1,0:T(8,128)(2,1)S(1)}, bf16[208,512]{1,0:T(8,128)(2,1)S(1)}, u32[]{:S(2)}, u32[]{:S(2)}) collective-permute-start(bf16[208,512]{1,0:T(8,128)(2,1)S(1)} %get-tuple-element.149), channel_id=1, source_target_pairs={{0,4},{1,5},{2,6},{3,7},{4,0},{5,1},{6,2},{7,3},{8,12},{9,13},{10,... | collective-permute-start | bytes 638984 | tf_op jit(solution)/shard_map/ppermute | solution.py:253
  19.8 7.8 %collective-permute-start.2 = (bf16[208,512]{1,0:T(8,128)(2,1)S(1)}, bf16[208,512]{1,0:T(8,128)(2,1)S(1)}, u32[]{:S(2)}, u32[]{:S(2)}) collective-permute-start(bf16[208,512]{1,0:T(8,128)(2,1)S(1)} %get-tuple-element.150), channel_id=1, source_target_pairs={{0,6},{1,7},{2,4},{3,5},{4,2},{5,3},{6,0},{7,1},{8,14},{9,15},{10,... | collective-permute-start | bytes 638984 | tf_op jit(solution)/shard_map/ppermute | solution.py:253
  25.1 9.2 %collective-permute-start.3 = (bf16[208,512]{1,0:T(8,128)(2,1)S(1)}, bf16[208,512]{1,0:T(8,128)(2,1)S(1)}, u32[]{:S(2)}, u32[]{:S(2)}) collective-permute-start(bf16[208,512]{1,0:T(8,128)(2,1)S(1)} %get-tuple-element.147.refs_0_), channel_id=1, source_target_pairs={{0,1},{1,0},{2,3},{3,2},{4,5},{5,4},{6,7},{7,6},{8,9},{9,8},{10,11... | collective-permute-start | bytes 638984 | tf_op jit(solution)/shard_map/ppermute | solution.py:253
  27.6 6.8 %collective-permute-start.4 = (bf16[208,512]{1,0:T(8,128)(2,1)S(1)}, bf16[208,512]{1,0:T(8,128)(2,1)S(1)}, u32[]{:S(2)}, u32[]{:S(2)}) collective-permute-start(bf16[208,512]{1,0:T(8,128)(2,1)S(1)} %collective-permute-done.refs_1_), channel_id=1, source_target_pairs={{0,1},{1,0},{2,3},{3,2},{4,5},{5,4},{6,7},{7,6},{8,9},{9,8},{10,11... | collective-permute-start | bytes 638984 | tf_op jit(solution)/shard_map/ppermute | solution.py:253
  27.6 6.8 %collective-permute-start.5 = (bf16[208,512]{1,0:T(8,128)(2,1)S(1)}, bf16[208,512]{1,0:T(8,128)(2,1)S(1)}, u32[]{:S(2)}, u32[]{:S(2)}) collective-permute-start(bf16[208,512]{1,0:T(8,128)(2,1)S(1)} %collective-permute-done.1.refs_2_), channel_id=1, source_target_pairs={{0,1},{1,0},{2,3},{3,2},{4,5},{5,4},{6,7},{7,6},{8,9},{9,8},{10,11... | collective-permute-start | bytes 638984 | tf_op jit(solution)/shard_map/ppermute | solution.py:253
  34.3 1.5 collective-permute-start.6
  38.4 10.4 %collective-permute-start.12 = (bf16[64,1536]{1,0:T(8,128)(2,1)S(1)}, bf16[64,1536]{1,0:T(8,128)(2,1)S(1)}, u32[]{:S(2)}, u32[]{:S(2)}) collective-permute-start(bf16[64,1536]{1,0:T(8,128)(2,1)S(1)} %get-tuple-element.157.refs_0_), channel_id=1, source_target_pairs={{0,24},{1,25},{2,26},{3,27},{4,28},{5,29},{6,30},{7,31},{8,16},{9,... | collective-permute-start | bytes 589832 | tf_op jit(solution)/shard_map/ppermute | solution.py:253
  39.9 10.7 %collective-permute-start.10 = (bf16[64,1536]{1,0:T(8,128)(2,1)S(1)}, bf16[64,1536]{1,0:T(8,128)(2,1)S(1)}, u32[]{:S(2)}, u32[]{:S(2)}) collective-permute-start(bf16[64,1536]{1,0:T(8,128)(2,1)S(1)} %get-tuple-element.157.refs_0_), channel_id=1, source_target_pairs={{0,8},{1,9},{2,10},{3,11},{4,12},{5,13},{6,14},{7,15},{8,0},{9,1},... | collective-permute-start | bytes 589832 | tf_op jit(solution)/shard_map/ppermute | solution.py:253
  41.4 9.2 %collective-permute-start.11 = (bf16[64,1536]{1,0:T(8,128)(2,1)S(1)}, bf16[64,1536]{1,0:T(8,128)(2,1)S(1)}, u32[]{:S(2)}, u32[]{:S(2)}) collective-permute-start(bf16[64,1536]{1,0:T(8,128)(2,1)S(1)} %get-tuple-element.157.refs_0_), channel_id=1, source_target_pairs={{0,16},{1,17},{2,18},{3,19},{4,20},{5,21},{6,22},{7,23},{8,24},{9,... | collective-permute-start | bytes 589832 | tf_op jit(solution)/shard_map/ppermute | solution.py:253
  41.9 9.2 %collective-permute-start.13 = (bf16[64,1536]{1,0:T(8,128)(2,1)S(1)}, bf16[64,1536]{1,0:T(8,128)(2,1)S(1)}, u32[]{:S(2)}, u32[]{:S(2)}) collective-permute-start(bf16[64,1536]{1,0:T(8,128)(2,1)S(1)} %get-tuple-element.157.refs_0_), channel_id=1, source_target_pairs={{0,1},{1,0},{2,3},{3,2},{4,5},{5,4},{6,7},{7,6},{8,9},{9,8},{10,11... | collective-permute-start | bytes 589832 | tf_op jit(solution)/shard_map/ppermute | solution.py:253
  48.8 2.3 %collective-permute-start.16 = (bf16[64,1536]{1,0:T(8,128)(2,1)S(1)}, bf16[64,1536]{1,0:T(8,128)(2,1)S(1)}, u32[]{:S(2)}, u32[]{:S(2)}) collective-permute-start(bf16[64,1536]{1,0:T(8,128)(2,1)S(1)} %collective-permute-done.12.refs_3_), channel_id=1, source_target_pairs={{0,1},{1,0},{2,3},{3,2},{4,5},{5,4},{6,7},{7,6},{8,9},{9,8},{10,11... | collective-permute-start | bytes 589832 | tf_op jit(solution)/shard_map/ppermute | solution.py:253
  50.6 1.7 collective-permute-start.15
  55.4 9.5 %collective-permute-start.19 = (bf16[64,1536]{1,0:T(8,128)(2,1)S(1)}, bf16[64,1536]{1,0:T(8,128)(2,1)S(1)}, u32[]{:S(2)}, u32[]{:S(2)}) collective-permute-start(bf16[64,1536]{1,0:T(8,128)(2,1)S(1)} %get-tuple-element.170.refs_0_), channel_id=1, source_target_pairs={{0,24},{1,25},{2,26},{3,27},{4,28},{5,29},{6,30},{7,31},{8,16},{9,... | collective-permute-start | bytes 589832 | tf_op jit(solution)/shard_map/ppermute | solution.py:253
  56.5 10.7 %collective-permute-start.17 = (bf16[64,1536]{1,0:T(8,128)(2,1)S(1)}, bf16[64,1536]{1,0:T(8,128)(2,1)S(1)}, u32[]{:S(2)}, u32[]{:S(2)}) collective-permute-start(bf16[64,1536]{1,0:T(8,128)(2,1)S(1)} %get-tuple-element.170.refs_0_), channel_id=1, source_target_pairs={{0,8},{1,9},{2,10},{3,11},{4,12},{5,13},{6,14},{7,15},{8,0},{9,1},... | collective-permute-start | bytes 589832 | tf_op jit(solution)/shard_map/ppermute | solution.py:253
  58.0 9.6 %collective-permute-start.18 = (bf16[64,1536]{1,0:T(8,128)(2,1)S(1)}, bf16[64,1536]{1,0:T(8,128)(2,1)S(1)}, u32[]{:S(2)}, u32[]{:S(2)}) collective-permute-start(bf16[64,1536]{1,0:T(8,128)(2,1)S(1)} %get-tuple-element.170.refs_0_), channel_id=1, source_target_pairs={{0,16},{1,17},{2,18},{3,19},{4,20},{5,21},{6,22},{7,23},{8,24},{9,... | collective-permute-start | bytes 589832 | tf_op jit(solution)/shard_map/ppermute | solution.py:253
  58.9 8.8 %collective-permute-start.20 = (bf16[64,1536]{1,0:T(8,128)(2,1)S(1)}, bf16[64,1536]{1,0:T(8,128)(2,1)S(1)}, u32[]{:S(2)}, u32[]{:S(2)}) collective-permute-start(bf16[64,1536]{1,0:T(8,128)(2,1)S(1)} %get-tuple-element.170.refs_0_), channel_id=1, source_target_pairs={{0,1},{1,0},{2,3},{3,2},{4,5},{5,4},{6,7},{7,6},{8,9},{9,8},{10,11... | collective-permute-start | bytes 589832 | tf_op jit(solution)/shard_map/ppermute | solution.py:253
  58.9 16.1 %all-to-all-start = ((bf16[4,192,128]{2,1,0:T(8,128)(2,1)}), bf16[4,192,128]{2,1,0:T(8,128)(2,1)S(1)}, u32[]{:S(2)}, u32[]{:S(2)}) async-start(bf16[4,192,128]{2,1,0:T(8,128)(2,1)} %bitcast.7), calls=%async_computation | async-start | bytes 393216 | tf_op jit(solution)/shard_map/all_to_all | solution.py:1025
  64.9 2.8 %collective-permute-start.23 = (bf16[64,1536]{1,0:T(8,128)(2,1)S(1)}, bf16[64,1536]{1,0:T(8,128)(2,1)S(1)}, u32[]{:S(2)}, u32[]{:S(2)}) collective-permute-start(bf16[64,1536]{1,0:T(8,128)(2,1)S(1)} %collective-permute-done.19.refs_3_), channel_id=1, source_target_pairs={{0,1},{1,0},{2,3},{3,2},{4,5},{5,4},{6,7},{7,6},{8,9},{9,8},{10,11... | collective-permute-start | bytes 589832 | tf_op jit(solution)/shard_map/ppermute | solution.py:253
  71.5 8.8 %collective-permute-start.26 = (bf16[64,1536]{1,0:T(8,128)(2,1)S(1)}, bf16[64,1536]{1,0:T(8,128)(2,1)S(1)}, u32[]{:S(2)}, u32[]{:S(2)}) collective-permute-start(bf16[64,1536]{1,0:T(8,128)(2,1)S(1)} %get-tuple-element.176.refs_0_), channel_id=1, source_target_pairs={{0,24},{1,25},{2,26},{3,27},{4,28},{5,29},{6,30},{7,31},{8,16},{9,... | collective-permute-start | bytes 589832 | tf_op jit(solution)/shard_map/ppermute | solution.py:253
  72.6 10.7 %collective-permute-start.24 = (bf16[64,1536]{1,0:T(8,128)(2,1)S(1)}, bf16[64,1536]{1,0:T(8,128)(2,1)S(1)}, u32[]{:S(2)}, u32[]{:S(2)}) collective-permute-start(bf16[64,1536]{1,0:T(8,128)(2,1)S(1)} %get-tuple-element.176.refs_0_), channel_id=1, source_target_pairs={{0,8},{1,9},{2,10},{3,11},{4,12},{5,13},{6,14},{7,15},{8,0},{9,1},... | collective-permute-start | bytes 589832 | tf_op jit(solution)/shard_map/ppermute | solution.py:253
  74.1 9.6 %collective-permute-start.25 = (bf16[64,1536]{1,0:T(8,128)(2,1)S(1)}, bf16[64,1536]{1,0:T(8,128)(2,1)S(1)}, u32[]{:S(2)}, u32[]{:S(2)}) collective-permute-start(bf16[64,1536]{1,0:T(8,128)(2,1)S(1)} %get-tuple-element.176.refs_0_), channel_id=1, source_target_pairs={{0,16},{1,17},{2,18},{3,19},{4,20},{5,21},{6,22},{7,23},{8,24},{9,... | collective-permute-start | bytes 589832 | tf_op jit(solution)/shard_map/ppermute | solution.py:253
  75.0 1.7 collective-permute-start.27
  75.1 9.0 %collective-permute-start.28 = (bf16[64,1536]{1,0:T(8,128)(2,1)S(1)}, bf16[64,1536]{1,0:T(8,128)(2,1)S(1)}, u32[]{:S(2)}, u32[]{:S(2)}) collective-permute-start(bf16[64,1536]{1,0:T(8,128)(2,1)S(1)} %get-tuple-element.176.refs_0_), channel_id=1, source_target_pairs={{0,1},{1,0},{2,3},{3,2},{4,5},{5,4},{6,7},{7,6},{8,9},{9,8},{10,11... | collective-permute-start | bytes 589832 | tf_op jit(solution)/shard_map/ppermute | solution.py:253
  80.2 3.9 %collective-permute-start.31 = (bf16[64,1536]{1,0:T(8,128)(2,1)S(1)}, bf16[64,1536]{1,0:T(8,128)(2,1)S(1)}, u32[]{:S(2)}, u32[]{:S(2)}) collective-permute-start(bf16[64,1536]{1,0:T(8,128)(2,1)S(1)} %collective-permute-done.26.refs_3_), channel_id=1, source_target_pairs={{0,1},{1,0},{2,3},{3,2},{4,5},{5,4},{6,7},{7,6},{8,9},{9,8},{10,11... | collective-permute-start | bytes 589832 | tf_op jit(solution)/shard_map/ppermute | solution.py:253
  83.8 5.4 %collective-permute-start.33 = (bf16[256,640]{1,0:T(8,128)(2,1)S(1)}, bf16[256,640]{1,0:T(8,128)(2,1)S(1)}, u32[]{:S(2)}, u32[]{:S(2)}) collective-permute-start(bf16[256,640]{1,0:T(8,128)(2,1)S(1)} %copy-done.11), channel_id=1, source_target_pairs={{0,1},{1,0},{2,3},{3,2},{4,5},{5,4},{6,7},{7,6},{8,9},{9,8},{10,11... | collective-permute-start | bytes 983048 | tf_op jit(solution)/shard_map/ppermute | solution.py:253
  87.6 1.5 collective-permute-start.32
  93.1 8.4 %collective-permute-start.34 = (bf16[64,1536]{1,0:T(8,128)(2,1)S(1)}, bf16[64,1536]{1,0:T(8,128)(2,1)S(1)}, u32[]{:S(2)}, u32[]{:S(2)}) collective-permute-start(bf16[64,1536]{1,0:T(8,128)(2,1)S(1)} %get-tuple-element.193), channel_id=1, source_target_pairs={{0,8},{1,9},{2,10},{3,11},{4,12},{5,13},{6,14},{7,15},{8,0},{9,1},... | collective-permute-start | bytes 589832 | tf_op jit(solution)/shard_map/ppermute | solution.py:253
  93.6 7.9 %collective-permute-start.35 = (bf16[64,1536]{1,0:T(8,128)(2,1)S(1)}, bf16[64,1536]{1,0:T(8,128)(2,1)S(1)}, u32[]{:S(2)}, u32[]{:S(2)}) collective-permute-start(bf16[64,1536]{1,0:T(8,128)(2,1)S(1)} %get-tuple-element.194), channel_id=1, source_target_pairs={{0,16},{1,17},{2,18},{3,19},{4,20},{5,21},{6,22},{7,23},{8,24},{9,... | collective-permute-start | bytes 589832 | tf_op jit(solution)/shard_map/ppermute | solution.py:253
  94.7 10.1 %collective-permute-start.36 = (bf16[64,1536]{1,0:T(8,128)(2,1)S(1)}, bf16[64,1536]{1,0:T(8,128)(2,1)S(1)}, u32[]{:S(2)}, u32[]{:S(2)}) collective-permute-start(bf16[64,1536]{1,0:T(8,128)(2,1)S(1)} %get-tuple-element.195), channel_id=1, source_target_pairs={{0,24},{1,25},{2,26},{3,27},{4,28},{5,29},{6,30},{7,31},{8,16},{9,... | collective-permute-start | bytes 589832 | tf_op jit(solution)/shard_map/ppermute | solution.py:253
  96.6 20.2 %all-to-all-start.1 = ((bf16[4,576,128]{2,1,0:T(8,128)(2,1)}), bf16[4,576,128]{2,1,0:T(8,128)(2,1)S(1)}, u32[]{:S(2)}, u32[]{:S(2)}) async-start(bf16[4,576,128]{2,1,0:T(8,128)(2,1)} %bitcast.33), calls=%async_computation.1 | async-start | bytes 1179648 | tf_op jit(solution)/shard_map/all_to_all | solution.py:1109
  101.5 5.3 %collective-permute-start.38 = (bf16[256,640]{1,0:T(8,128)(2,1)S(1)}, bf16[256,640]{1,0:T(8,128)(2,1)S(1)}, u32[]{:S(2)}, u32[]{:S(2)}) collective-permute-start(bf16[256,640]{1,0:T(8,128)(2,1)S(1)} %copy-done.10), channel_id=1, source_target_pairs={{0,1},{1,0},{2,3},{3,2},{4,5},{5,4},{6,7},{7,6},{8,9},{9,8},{10,11... | collective-permute-start | bytes 983048 | tf_op jit(solution)/shard_map/ppermute | solution.py:253
  105.3 1.5 collective-permute-start.37
  110.7 10.6 %collective-permute-start.39 = (bf16[64,1536]{1,0:T(8,128)(2,1)S(1)}, bf16[64,1536]{1,0:T(8,128)(2,1)S(1)}, u32[]{:S(2)}, u32[]{:S(2)}) collective-permute-start(bf16[64,1536]{1,0:T(8,128)(2,1)S(1)} %get-tuple-element.211), channel_id=1, source_target_pairs={{0,8},{1,9},{2,10},{3,11},{4,12},{5,13},{6,14},{7,15},{8,0},{9,1},... | collective-permute-start | bytes 589832 | tf_op jit(solution)/shard_map/ppermute | solution.py:253
  112.1 10.9 %collective-permute-start.40 = (bf16[64,1536]{1,0:T(8,128)(2,1)S(1)}, bf16[64,1536]{1,0:T(8,128)(2,1)S(1)}, u32[]{:S(2)}, u32[]{:S(2)}) collective-permute-start(bf16[64,1536]{1,0:T(8,128)(2,1)S(1)} %get-tuple-element.212), channel_id=1, source_target_pairs={{0,16},{1,17},{2,18},{3,19},{4,20},{5,21},{6,22},{7,23},{8,24},{9,... | collective-permute-start | bytes 589832 | tf_op jit(solution)/shard_map/ppermute | solution.py:253
  113.1 9.8 %collective-permute-start.41 = (bf16[64,1536]{1,0:T(8,128)(2,1)S(1)}, bf16[64,1536]{1,0:T(8,128)(2,1)S(1)}, u32[]{:S(2)}, u32[]{:S(2)}) collective-permute-start(bf16[64,1536]{1,0:T(8,128)(2,1)S(1)} %get-tuple-element.213), channel_id=1, source_target_pairs={{0,24},{1,25},{2,26},{3,27},{4,28},{5,29},{6,30},{7,31},{8,16},{9,... | collective-permute-start | bytes 589832 | tf_op jit(solution)/shard_map/ppermute | solution.py:253
  116.9 19.6 %all-to-all-start.2 = ((bf16[4,576,128]{2,1,0:T(8,128)(2,1)}), bf16[4,576,128]{2,1,0:T(8,128)(2,1)}, u32[]{:S(2)}, u32[]{:S(2)}) async-start(bf16[4,576,128]{2,1,0:T(8,128)(2,1)} %bitcast.32), calls=%async_computation.2 | async-start | bytes 1179648 | tf_op jit(solution)/shard_map/all_to_all | solution.py:1109
  121.3 5.3 %collective-permute-start.43 = (bf16[256,640]{1,0:T(8,128)(2,1)S(1)}, bf16[256,640]{1,0:T(8,128)(2,1)S(1)}, u32[]{:S(2)}, u32[]{:S(2)}) collective-permute-start(bf16[256,640]{1,0:T(8,128)(2,1)S(1)} %copy-done.9), channel_id=1, source_target_pairs={{0,1},{1,0},{2,3},{3,2},{4,5},{5,4},{6,7},{7,6},{8,9},{9,8},{10,11... | collective-permute-start | bytes 983048 | tf_op jit(solution)/shard_map/ppermute | solution.py:253
  125.1 1.5 collective-permute-start.42
  130.5 9.5 %collective-permute-start.44 = (bf16[64,1536]{1,0:T(8,128)(2,1)S(1)}, bf16[64,1536]{1,0:T(8,128)(2,1)S(1)}, u32[]{:S(2)}, u32[]{:S(2)}) collective-permute-start(bf16[64,1536]{1,0:T(8,128)(2,1)S(1)} %get-tuple-element.229), channel_id=1, source_target_pairs={{0,8},{1,9},{2,10},{3,11},{4,12},{5,13},{6,14},{7,15},{8,0},{9,1},... | collective-permute-start | bytes 589832 | tf_op jit(solution)/shard_map/ppermute | solution.py:253
  131.3 8.7 %collective-permute-start.45 = (bf16[64,1536]{1,0:T(8,128)(2,1)S(1)}, bf16[64,1536]{1,0:T(8,128)(2,1)S(1)}, u32[]{:S(2)}, u32[]{:S(2)}) collective-permute-start(bf16[64,1536]{1,0:T(8,128)(2,1)S(1)} %get-tuple-element.230), channel_id=1, source_target_pairs={{0,16},{1,17},{2,18},{3,19},{4,20},{5,21},{6,22},{7,23},{8,24},{9,... | collective-permute-start | bytes 589832 | tf_op jit(solution)/shard_map/ppermute | solution.py:253
  132.3 9.9 %collective-permute-start.46 = (bf16[64,1536]{1,0:T(8,128)(2,1)S(1)}, bf16[64,1536]{1,0:T(8,128)(2,1)S(1)}, u32[]{:S(2)}, u32[]{:S(2)}) collective-permute-start(bf16[64,1536]{1,0:T(8,128)(2,1)S(1)} %get-tuple-element.231), channel_id=1, source_target_pairs={{0,24},{1,25},{2,26},{3,27},{4,28},{5,29},{6,30},{7,31},{8,16},{9,... | collective-permute-start | bytes 589832 | tf_op jit(solution)/shard_map/ppermute | solution.py:253
  136.5 24.9 %all-to-all-start.3 = ((bf16[4,576,128]{2,1,0:T(8,128)(2,1)}), bf16[4,576,128]{2,1,0:T(8,128)(2,1)S(1)}, u32[]{:S(2)}, u32[]{:S(2)}) async-start(bf16[4,576,128]{2,1,0:T(8,128)(2,1)} %bitcast.31), calls=%async_computation.3 | async-start | bytes 1179648 | tf_op jit(solution)/shard_map/all_to_all | solution.py:1109
  140.0 2.9 %collective-permute-start.48 = (bf16[256,640]{1,0:T(8,128)(2,1)S(1)}, bf16[256,640]{1,0:T(8,128)(2,1)S(1)}, u32[]{:S(2)}, u32[]{:S(2)}) collective-permute-start(bf16[256,640]{1,0:T(8,128)(2,1)S(1)} %copy-done.8), channel_id=1, source_target_pairs={{0,1},{1,0},{2,3},{3,2},{4,5},{5,4},{6,7},{7,6},{8,9},{9,8},{10,11... | collective-permute-start | bytes 983048 | tf_op jit(solution)/shard_map/ppermute | solution.py:253
  142.7 1.5 collective-permute-start.47
  148.1 7.8 %collective-permute-start.49 = (bf16[64,1536]{1,0:T(8,128)(2,1)S(1)}, bf16[64,1536]{1,0:T(8,128)(2,1)S(1)}, u32[]{:S(2)}, u32[]{:S(2)}) collective-permute-start(bf16[64,1536]{1,0:T(8,128)(2,1)S(1)} %get-tuple-element.244), channel_id=1, source_target_pairs={{0,8},{1,9},{2,10},{3,11},{4,12},{5,13},{6,14},{7,15},{8,0},{9,1},... | collective-permute-start | bytes 589832 | tf_op jit(solution)/shard_map/ppermute | solution.py:253
  149.5 10.9 %collective-permute-start.60 = (bf16[64,1536]{1,0:T(8,128)(2,1)S(1)}, bf16[64,1536]{1,0:T(8,128)(2,1)S(1)}, u32[]{:S(2)}, u32[]{:S(2)}) collective-permute-start(bf16[64,1536]{1,0:T(8,128)(2,1)S(1)} %get-tuple-element.261), channel_id=1, source_target_pairs={{0,16},{1,17},{2,18},{3,19},{4,20},{5,21},{6,22},{7,23},{8,24},{9,... | collective-permute-start | bytes 589832 | tf_op jit(solution)/shard_map/ppermute | solution.py:253
  150.5 9.9 %collective-permute-start.61 = (bf16[64,1536]{1,0:T(8,128)(2,1)S(1)}, bf16[64,1536]{1,0:T(8,128)(2,1)S(1)}, u32[]{:S(2)}, u32[]{:S(2)}) collective-permute-start(bf16[64,1536]{1,0:T(8,128)(2,1)S(1)} %get-tuple-element.262), channel_id=1, source_target_pairs={{0,24},{1,25},{2,26},{3,27},{4,28},{5,29},{6,30},{7,31},{8,16},{9,... | collective-permute-start | bytes 589832 | tf_op jit(solution)/shard_map/ppermute | solution.py:253
  151.7 13.9 %collective-permute-start.51 = (bf16[592,128]{1,0:T(8,128)(2,1)}, bf16[592,128]{1,0:T(8,128)(2,1)S(1)}, u32[]{:S(2)}, u32[]{:S(2)}) collective-permute-start(bf16[592,128]{1,0:T(8,128)(2,1)} %get-tuple-element.246), channel_id=1, source_target_pairs={{0,4},{1,5},{2,6},{3,7},{4,0},{5,1},{6,2},{7,3},{8,12},{9,13},{10,... | collective-permute-start | bytes 454664 | tf_op jit(solution)/shard_map/ppermute | solution.py:253
  154.3 11.3 %collective-permute-start.52 = (bf16[592,128]{1,0:T(8,128)(2,1)}, bf16[592,128]{1,0:T(8,128)(2,1)S(1)}, u32[]{:S(2)}, u32[]{:S(2)}) collective-permute-start(bf16[592,128]{1,0:T(8,128)(2,1)} %get-tuple-element.247), channel_id=1, source_target_pairs={{0,6},{1,7},{2,4},{3,5},{4,2},{5,3},{6,0},{7,1},{8,14},{9,15},{10,... | collective-permute-start | bytes 454664 | tf_op jit(solution)/shard_map/ppermute | solution.py:253
  156.0 10.6 %collective-permute-start.50 = (bf16[592,128]{1,0:T(8,128)(2,1)}, bf16[592,128]{1,0:T(8,128)(2,1)S(1)}, u32[]{:S(2)}, u32[]{:S(2)}) collective-permute-start(bf16[592,128]{1,0:T(8,128)(2,1)} %get-tuple-element.245), channel_id=1, source_target_pairs={{0,2},{1,3},{2,0},{3,1},{4,6},{5,7},{6,4},{7,5},{8,10},{9,11},{10,... | collective-permute-start | bytes 454664 | tf_op jit(solution)/shard_map/ppermute | solution.py:253
  162.5 4.9 %collective-permute-start.62 = (bf16[256,384]{1,0:T(8,128)(2,1)S(1)}, bf16[256,384]{1,0:T(8,128)(2,1)S(1)}, u32[]{:S(2)}, u32[]{:S(2)}) collective-permute-start(bf16[256,384]{1,0:T(8,128)(2,1)S(1)} %get-tuple-element.269), channel_id=1, source_target_pairs={{0,1},{1,0},{2,3},{3,2},{4,5},{5,4},{6,7},{7,6},{8,9},{9,8},{10,11... | collective-permute-start | bytes 589832 | tf_op jit(solution)/shard_map/ppermute | solution.py:253
  166.7 9.6 %collective-permute-start.53 = (bf16[592,128]{1,0:T(8,128)(2,1)S(1)}, bf16[592,128]{1,0:T(8,128)(2,1)S(1)}, u32[]{:S(2)}, u32[]{:S(2)}) collective-permute-start(bf16[592,128]{1,0:T(8,128)(2,1)S(1)} %get-tuple-element.257), channel_id=1, source_target_pairs={{0,8},{1,9},{2,10},{3,11},{4,12},{5,13},{6,14},{7,15},{8,0},{9,1},... | collective-permute-start | bytes 454664 | tf_op jit(solution)/shard_map/ppermute | solution.py:253
  167.5 18.5 %collective-permute-start.63 = (bf16[256,384]{1,0:T(8,128)(2,1)S(1)}, bf16[256,384]{1,0:T(8,128)(2,1)S(1)}, u32[]{:S(2)}, u32[]{:S(2)}) collective-permute-start(bf16[256,384]{1,0:T(8,128)(2,1)S(1)} %get-tuple-element.270), channel_id=1, source_target_pairs={{0,0},{1,5},{2,8},{3,13},{4,16},{5,21},{6,24},{7,29},{8,2},{9,7},{... | collective-permute-start | bytes 589832 | tf_op jit(solution)/shard_map/ppermute | solution.py:253
  168.2 17.9 %collective-permute-start.64 = (bf16[256,384]{1,0:T(8,128)(2,1)S(1)}, bf16[256,384]{1,0:T(8,128)(2,1)S(1)}, u32[]{:S(2)}, u32[]{:S(2)}) collective-permute-start(bf16[256,384]{1,0:T(8,128)(2,1)S(1)} %get-tuple-element.271), channel_id=1, source_target_pairs={{0,2},{1,7},{2,10},{3,15},{4,18},{5,23},{6,26},{7,31},{8,0},{9,5},... | collective-permute-start | bytes 589832 | tf_op jit(solution)/shard_map/ppermute | solution.py:253
  172.3 13.2 %collective-permute-start.54 = (bf16[592,128]{1,0:T(8,128)(2,1)S(1)}, bf16[592,128]{1,0:T(8,128)(2,1)S(1)}, u32[]{:S(2)}, u32[]{:S(2)}) collective-permute-start(bf16[592,128]{1,0:T(8,128)(2,1)S(1)} %get-tuple-element.258), channel_id=1, source_target_pairs={{0,16},{1,17},{2,18},{3,19},{4,20},{5,21},{6,22},{7,23},{8,24},{9,... | collective-permute-start | bytes 454664 | tf_op jit(solution)/shard_map/ppermute | solution.py:253
  176.0 9.5 %collective-permute-start.55 = (bf16[592,128]{1,0:T(8,128)(2,1)S(1)}, bf16[592,128]{1,0:T(8,128)(2,1)S(1)}, u32[]{:S(2)}, u32[]{:S(2)}) collective-permute-start(bf16[592,128]{1,0:T(8,128)(2,1)S(1)} %get-tuple-element.259), channel_id=1, source_target_pairs={{0,24},{1,25},{2,26},{3,27},{4,28},{5,29},{6,30},{7,31},{8,16},{9,... | collective-permute-start | bytes 454664 | tf_op jit(solution)/shard_map/ppermute | solution.py:253
  176.3 10.3 %collective-permute-start.56 = (bf16[592,128]{1,0:T(8,128)(2,1)S(1)}, bf16[592,128]{1,0:T(8,128)(2,1)S(1)}, u32[]{:S(2)}, u32[]{:S(2)}) collective-permute-start(bf16[592,128]{1,0:T(8,128)(2,1)S(1)} %get-tuple-element.256.refs_0_), channel_id=1, source_target_pairs={{0,1},{1,0},{2,3},{3,2},{4,5},{5,4},{6,7},{7,6},{8,9},{9,8},{10,11... | collective-permute-start | bytes 454664 | tf_op jit(solution)/shard_map/ppermute | solution.py:253
  185.5 1.5 collective-permute-start.58
  186.1 1.6 collective-permute-start.65
  186.5 1.4 collective-permute-start.66
  (19 other events, 176.9 us)

commit v11 on v10

--- a/solution.py
+++ b/solution.py
@@ -10,7 +10,7 @@
 from jax.sharding import PartitionSpec as P
 
 CONVS = 2
-BACK_FLOPS = (3 * 10**9, 52 * 10**8, 52 * 10**8, 0)
+BACK_FLOPS = (3 * 10**9, 56 * 10**8, 56 * 10**8, 0)
 PICK_FLOPS = 2 * 10**9
 COT_LAYER = 2
 INPUT_FLOPS = 0 * 10**9

time: 191 us -> 191 us (level)
    all_to_all x3, waiting for transfers between devices: 5.9 us -> 11.8 us  [plane_shards(): lax.all_to_all(share[0], 'dp', 0, 0, tiled=True, axis_index_groups=same_c...]
    ppermute x67, waiting for transfers between devices: 57.9 us -> 52.4 us  [send(): return lax.ppermute(x, AXES, pairs)]
  transfers between devices with their start and end apart: 71 -> 71, of which waited for: 37 -> 38; matrix products, arithmetic and copies ran while one was open for 0% -> 0% of each run, Pallas kernels for 19% -> 19%
where the time goes in v11:
time: 191 us; the launch traced here: 190 us
  starting transfers between devices  73.8 us (39%)
  waiting for transfers between devices  64.2 us (34%)
  Pallas kernels  50.5 us (26%)
    ppermute x67, starting transfers between devices, send(): return lax.ppermute(x, AXES, pairs)  56.2 us
    ppermute x67, waiting for transfers between devices, send(): return lax.ppermute(x, AXES, pairs)  52.4 us
    pallas_call x27, Pallas kernels, call(): pl.pallas_call(kernel, out_shape=shapes, in_specs=[pl.BlockSpec(memory_sp...  50.5 us
    all_to_all x3, starting transfers between devices, plane_shards(): lax.all_to_all(share[0], 'dp', 0, 0, tiled=True, axis_index_groups=same_c...  12.7 us
    all_to_all x3, waiting for transfers between devices, plane_shards(): lax.all_to_all(share[0], 'dp', 0, 0, tiled=True, axis_index_groups=same_c...  11.8 us
    all_to_all x1, starting transfers between devices, plane_shards(): lax.all_to_all(cot_slots, 'dp', 0, 0, tiled=True, axis_index_groups=same_...  4.87 us
  transfers between devices with their start and end apart: 71, of which 38 were waited for; matrix products, arithmetic and copies ran while one was open for 0% of the time, Pallas kernels for 19%

profile of v11, /device:TPU:0, one launch (start us, length us, event | category | flops | bytes accessed | tf_op | source)
XLA Modules:
  0.0 189.8 jit_solution(17114007660644926031)
XLA Ops:
  0.6 2.5 %weight_pack.1 = (bf16[592,512]{1,0:T(8,128)(2,1)S(1)}, bf16[592,512]{1,0:T(8,128)(2,1)S(1)}, bf16[592,512]{1,0:T(8,128)(2,1)S(1)}, bf16[592,512]{1,0:T(8,128)(2,1)S(1)}) custom-call(f32[1,512]{1,0:T(1,128)} %gain.1, f32[1,512]{1,0:T(1,128)} %bias.1, bf16[9,512,512]{2,1,0:T(8,128)(2,1)} %bitcast.26), custom_call_target="tpu_custom_call" | custom-call | bytes 7147520 | tf_op jit(solution)/shard_map/weight_pack/pallas_call | solution.py:895
  3.1 3.0 %collective-permute-start.7 = (bf16[592,512]{1,0:T(8,128)(2,1)S(1)}, bf16[592,512]{1,0:T(8,128)(2,1)S(1)}, u32[]{:S(2)}, u32[]{:S(2)}) collective-permute-start(bf16[592,512]{1,0:T(8,128)(2,1)S(1)} %get-tuple-element.143), channel_id=1, source_target_pairs={{0,8},{1,9},{2,10},{3,11},{4,12},{5,13},{6,14},{7,15},{8,0},{9,1},... | collective-permute-start | bytes 1818632 | tf_op jit(solution)/shard_map/ppermute | solution.py:253
  6.2 1.5 collective-permute-start.8
  7.7 1.4 frames.1
  9.1 1.6 collective-permute-start
  11.2 2.6 %collective-permute-start.1 = (bf16[208,512]{1,0:T(8,128)(2,1)S(1)}, bf16[208,512]{1,0:T(8,128)(2,1)S(1)}, u32[]{:S(2)}, u32[]{:S(2)}) collective-permute-start(bf16[208,512]{1,0:T(8,128)(2,1)S(1)} %get-tuple-element.149), channel_id=1, source_target_pairs={{0,4},{1,5},{2,6},{3,7},{4,0},{5,1},{6,2},{7,3},{8,12},{9,13},{10,... | collective-permute-start | bytes 638984 | tf_op jit(solution)/shard_map/ppermute | solution.py:253
  13.8 6.1 %collective-permute-done.refs_1_ = bf16[208,512]{1,0:T(8,128)(2,1)S(1)} collective-permute-done((bf16[208,512]{1,0:T(8,128)(2,1)S(1)}, bf16[208,512]{1,0:T(8,128)(2,1)S(1)}, u32[]{:S(2)}, u32[]{:S(2)}) %collective-permute-start) | collective-permute-done | bytes 213024 | tf_op jit(solution)/shard_map/ppermute | solution.py:253
  19.8 2.5 %collective-permute-start.2 = (bf16[208,512]{1,0:T(8,128)(2,1)S(1)}, bf16[208,512]{1,0:T(8,128)(2,1)S(1)}, u32[]{:S(2)}, u32[]{:S(2)}) collective-permute-start(bf16[208,512]{1,0:T(8,128)(2,1)S(1)} %get-tuple-element.150), channel_id=1, source_target_pairs={{0,6},{1,7},{2,4},{3,5},{4,2},{5,3},{6,0},{7,1},{8,14},{9,15},{10,... | collective-permute-start | bytes 638984 | tf_op jit(solution)/shard_map/ppermute | solution.py:253
  22.3 2.8 %collective-permute-done.1.refs_2_ = bf16[208,512]{1,0:T(8,128)(2,1)S(1)} collective-permute-done((bf16[208,512]{1,0:T(8,128)(2,1)S(1)}, bf16[208,512]{1,0:T(8,128)(2,1)S(1)}, u32[]{:S(2)}, u32[]{:S(2)}) %collective-permute-start.1) | collective-permute-done | bytes 213024 | tf_op jit(solution)/shard_map/ppermute | solution.py:253
  25.1 2.5 %collective-permute-done.2.refs_3_ = bf16[208,512]{1,0:T(8,128)(2,1)S(1)} collective-permute-done((bf16[208,512]{1,0:T(8,128)(2,1)S(1)}, bf16[208,512]{1,0:T(8,128)(2,1)S(1)}, u32[]{:S(2)}, u32[]{:S(2)}) %collective-permute-start.2) | collective-permute-done | bytes 213024 | tf_op jit(solution)/shard_map/ppermute | solution.py:253
  28.1 6.2 %collective-permute-done.8.refs_10_.refs_2_ = bf16[592,512]{1,0:T(8,128)(2,1)S(1)} collective-permute-done((bf16[592,512]{1,0:T(8,128)(2,1)S(1)}, bf16[592,512]{1,0:T(8,128)(2,1)S(1)}, u32[]{:S(2)}, u32[]{:S(2)}) %collective-permute-start.8) | collective-permute-done | bytes 606240 | tf_op jit(solution)/shard_map/ppermute | solution.py:253
  34.4 1.4 collective-permute-done.6.refs_7_
  35.8 2.5 %forward.3 = (bf16[64,1536]{1,0:T(8,128)(2,1)S(1)}, f32[64,1664]{1,0:T(8,128)}, bf16[1536,512]{1,0:T(8,128)(2,1)}, f32[1,1536]{1,0:T(1,128)S(1)}) custom-call(bf16[208,512]{1,0:T(8,128)(2,1)S(1)} %get-tuple-element.147.refs_0_, bf16[208,512]{1,0:T(8,128)(2,1)S(1)} %collective-permute-done.refs_1_, bf16[208,512]{1,0:T(8,128)(2,1)S(1)} %collective-permute-done.1.refs_2_, ...), custom_call_target="tpu_custom_call" | custom-call | flops 905969664 | bytes 6428672 | tf_op jit(solution)/shard_map/forward/pallas_call | solution.py:895
  38.4 1.5 collective-permute-start.12
  39.9 1.5 collective-permute-start.10
  41.9 2.0 %cot_slices.1 = bf16[768,128]{1,0:T(8,128)(2,1)} custom-call(bf16[4,192,512]{2,1,0:T(8,128)(2,1)} %bitcast.30), custom_call_target="tpu_custom_call" | custom-call | bytes 983040 | tf_op jit(solution)/shard_map/cot_slices/pallas_call | solution.py:895
  43.9 3.7 %turn_weights.1 = (bf16[1024,640]{1,0:T(8,128)(2,1)}, bf16[256,640]{1,0:T(8,128)(2,1)}, bf16[256,640]{1,0:T(8,128)(2,1)}, bf16[256,640]{1,0:T(8,128)(2,1)}, bf16[256,640]{1,0:T(8,128)(2,1)}) custom-call(bf16[592,512]{1,0:T(8,128)(2,1)} %copy-done, bf16[592,512]{1,0:T(8,128)(2,1)} %copy-done.1, bf16[592,512]{1,0:T(8,128)(2,1)} %copy-done.2, ...), custom_call_target="tpu_custom_call" | custom-call | bytes 5046272 | tf_op jit(solution)/shard_map/turn_weights/pallas_call | solution.py:895
  47.7 1.1 pick.3.refs_8_
  49.3 1.2 collective-permute-done.10.refs_1_
  52.3 3.1 %forward.4 = (bf16[64,1536]{1,0:T(8,128)(2,1)S(1)}, f32[64,1664]{1,0:T(8,128)}, bf16[512,1536]{1,0:T(8,128)(2,1)}) custom-call(bf16[64,1536]{1,0:T(8,128)(2,1)S(1)} %get-tuple-element.157.refs_0_, bf16[64,1536]{1,0:T(8,128)(2,1)S(1)} %collective-permute-done.10.refs_1_, bf16[64,1536]{1,0:T(8,128)(2,1)S(1)} %collective-permute-done.11.refs_2_, ...), custom_call_target="tpu_custom_call" | custom-call | flops 905969664 | bytes 4478976 | tf_op jit(solution)/shard_map/forward/pallas_call | solution.py:895
  55.4 1.2 collective-permute-start.19
  56.5 1.5 collective-permute-start.17
  58.9 4.9 %all-to-all-start = ((bf16[4,192,128]{2,1,0:T(8,128)(2,1)}), bf16[4,192,128]{2,1,0:T(8,128)(2,1)S(1)}, u32[]{:S(2)}, u32[]{:S(2)}) async-start(bf16[4,192,128]{2,1,0:T(8,128)(2,1)} %bitcast.7), calls=%async_computation | async-start | bytes 393216 | tf_op jit(solution)/shard_map/all_to_all | solution.py:1025
  63.8 1.1 pick.4.refs_8_
  65.2 2.0 %collective-permute-done.17.refs_1_ = bf16[64,1536]{1,0:T(8,128)(2,1)S(1)} collective-permute-done((bf16[64,1536]{1,0:T(8,128)(2,1)S(1)}, bf16[64,1536]{1,0:T(8,128)(2,1)S(1)}, u32[]{:S(2)}, u32[]{:S(2)}) %collective-permute-start.17) | collective-permute-done | bytes 196640 | tf_op jit(solution)/shard_map/ppermute | solution.py:253
  69.0 2.4 %forward.5 = (bf16[64,1536]{1,0:T(8,128)(2,1)S(1)}, f32[64,1664]{1,0:T(8,128)}, bf16[512,1536]{1,0:T(8,128)(2,1)}) custom-call(bf16[64,1536]{1,0:T(8,128)(2,1)S(1)} %get-tuple-element.170.refs_0_, bf16[64,1536]{1,0:T(8,128)(2,1)S(1)} %collective-permute-done.17.refs_1_, bf16[64,1536]{1,0:T(8,128)(2,1)S(1)} %collective-permute-done.18.refs_2_, ...), custom_call_target="tpu_custom_call" | custom-call | flops 905969664 | bytes 4478976 | tf_op jit(solution)/shard_map/forward/pallas_call | solution.py:895
  71.5 1.1 collective-permute-start.26
  72.6 1.5 collective-permute-start.24
  75.7 1.1 pick.5.refs_8_
  77.1 3.1 %collective-permute-done.26.refs_3_ = bf16[64,1536]{1,0:T(8,128)(2,1)S(1)} collective-permute-done((bf16[64,1536]{1,0:T(8,128)(2,1)S(1)}, bf16[64,1536]{1,0:T(8,128)(2,1)S(1)}, u32[]{:S(2)}, u32[]{:S(2)}) %collective-permute-start.26) | collective-permute-done | bytes 196640 | tf_op jit(solution)/shard_map/ppermute | solution.py:253
  80.2 3.0 %collective-permute-done.24.refs_1_ = bf16[64,1536]{1,0:T(8,128)(2,1)S(1)} collective-permute-done((bf16[64,1536]{1,0:T(8,128)(2,1)S(1)}, bf16[64,1536]{1,0:T(8,128)(2,1)S(1)}, u32[]{:S(2)}, u32[]{:S(2)}) %collective-permute-start.24) | collective-permute-done | bytes 196640 | tf_op jit(solution)/shard_map/ppermute | solution.py:253
  85.1 2.5 %turn.1 = (bf16[64,1536]{1,0:T(8,128)(2,1)}, bf16[512,1536]{1,0:T(8,128)(2,1)}, bf16[64,1536]{1,0:T(8,128)(2,1)S(1)}, f32[64,128]{1,0:T(8,128)S(1)}) custom-call(bf16[64,1536]{1,0:T(8,128)(2,1)S(1)} %get-tuple-element.176.refs_0_, bf16[64,1536]{1,0:T(8,128)(2,1)S(1)} %collective-permute-done.24.refs_1_, ...), custom_call_target="tpu_custom_call" | custom-call | flops 905969664 | bytes 4478976 | tf_op jit(solution)/shard_map/turn/pallas_call | solution.py:895
  89.1 3.9 %conv_back.4 = (bf16[64,1536]{1,0:T(8,128)(2,1)S(1)}, bf16[64,1536]{1,0:T(8,128)(2,1)S(1)}, bf16[64,1536]{1,0:T(8,128)(2,1)S(1)}, bf16[64,1536]{1,0:T(8,128)(2,1)S(1)}, bf16[2304,128]{1,0:T(8,128)(2,1)}) custom-call(bf16[64,1536]{1,0:T(8,128)(2,1)S(1)} %get-tuple-element.184.own, bf16[64,1536]{1,0:T(8,128)(2,1)S(1)} %collective-permute-done.32.other, ...), custom_call_target="tpu_custom_call" | custom-call | bytes 5079040 | tf_op jit(solution)/shard_map/conv_back/pallas_call | solution.py:895
  93.6 1.0 collective-permute-start.35
  94.7 1.9 %collective-permute-start.36 = (bf16[64,1536]{1,0:T(8,128)(2,1)S(1)}, bf16[64,1536]{1,0:T(8,128)(2,1)S(1)}, u32[]{:S(2)}, u32[]{:S(2)}) collective-permute-start(bf16[64,1536]{1,0:T(8,128)(2,1)S(1)} %get-tuple-element.195), channel_id=1, source_target_pairs={{0,24},{1,25},{2,26},{3,27},{4,28},{5,29},{6,30},{7,31},{8,16},{9,... | collective-permute-start | bytes 589832 | tf_op jit(solution)/shard_map/ppermute | solution.py:253
  96.6 4.9 %all-to-all-start.1 = ((bf16[4,576,128]{2,1,0:T(8,128)(2,1)}), bf16[4,576,128]{2,1,0:T(8,128)(2,1)S(1)}, u32[]{:S(2)}, u32[]{:S(2)}) async-start(bf16[4,576,128]{2,1,0:T(8,128)(2,1)} %bitcast.33), calls=%async_computation.1 | async-start | bytes 1179648 | tf_op jit(solution)/shard_map/all_to_all | solution.py:1109
  101.5 3.2 %collective-permute-done.36.refs_3_ = bf16[64,1536]{1,0:T(8,128)(2,1)S(1)} collective-permute-done((bf16[64,1536]{1,0:T(8,128)(2,1)S(1)}, bf16[64,1536]{1,0:T(8,128)(2,1)S(1)}, u32[]{:S(2)}, u32[]{:S(2)}) %collective-permute-start.36) | collective-permute-done | bytes 196640 | tf_op jit(solution)/shard_map/ppermute | solution.py:253
  105.4 1.0 fetch.4
  106.8 3.9 %conv_back.5 = (bf16[64,1536]{1,0:T(8,128)(2,1)S(1)}, bf16[64,1536]{1,0:T(8,128)(2,1)S(1)}, bf16[64,1536]{1,0:T(8,128)(2,1)S(1)}, bf16[64,1536]{1,0:T(8,128)(2,1)S(1)}, bf16[2304,128]{1,0:T(8,128)(2,1)}) custom-call(bf16[64,1536]{1,0:T(8,128)(2,1)S(1)} %get-tuple-element.202.own, bf16[64,1536]{1,0:T(8,128)(2,1)S(1)} %collective-permute-done.37.other, ...), custom_call_target="tpu_custom_call" | custom-call | flops 5600000000 | bytes 5079040 | tf_op jit(solution)/shard_map/conv_back/pallas_call | solution.py:895
  110.8 1.4 collective-permute-start.39
  113.1 1.2 collective-permute-start.41
  114.3 3.7 %all-to-all-done.1 = bf16[4,576,128]{2,1,0:T(8,128)(2,1)S(1)} async-done(((bf16[4,576,128]{2,1,0:T(8,128)(2,1)}), bf16[4,576,128]{2,1,0:T(8,128)(2,1)S(1)}, u32[]{:S(2)}, u32[]{:S(2)}) %all-to-all-start.1) | async-done | bytes 589856 | tf_op jit(solution)/shard_map/all_to_all | solution.py:1109
  118.1 4.4 %all-to-all-start.2 = ((bf16[4,576,128]{2,1,0:T(8,128)(2,1)}), bf16[4,576,128]{2,1,0:T(8,128)(2,1)}, u32[]{:S(2)}, u32[]{:S(2)}) async-start(bf16[4,576,128]{2,1,0:T(8,128)(2,1)} %bitcast.32), calls=%async_computation.2 | async-start | bytes 1179648 | tf_op jit(solution)/shard_map/all_to_all | solution.py:1109
  123.0 2.1 %norm_back.4 = (bf16[64,1536]{1,0:T(8,128)(2,1)S(1)}, f32[64,128]{1,0:T(8,128)S(1)}) custom-call(bf16[64,1536]{1,0:T(8,128)(2,1)S(1)} %get-tuple-element.210.refs_0_, bf16[64,1536]{1,0:T(8,128)(2,1)S(1)} %collective-permute-done.39.refs_1_, bf16[64,1536]{1,0:T(8,128)(2,1)S(1)} %collective-permute-done.40.refs_2_, ...), custom_call_target="tpu_custom_call" | custom-call | bytes 1595392 | tf_op jit(solution)/shard_map/norm_back/pallas_call | solution.py:895
  126.6 3.9 %conv_back.6 = (bf16[64,1536]{1,0:T(8,128)(2,1)S(1)}, bf16[64,1536]{1,0:T(8,128)(2,1)S(1)}, bf16[64,1536]{1,0:T(8,128)(2,1)S(1)}, bf16[64,1536]{1,0:T(8,128)(2,1)S(1)}, bf16[2304,128]{1,0:T(8,128)(2,1)}) custom-call(bf16[64,1536]{1,0:T(8,128)(2,1)S(1)} %get-tuple-element.220.own, bf16[64,1536]{1,0:T(8,128)(2,1)S(1)} %collective-permute-done.42.other, ...), custom_call_target="tpu_custom_call" | custom-call | flops 5600000000 | bytes 5079040 | tf_op jit(solution)/shard_map/conv_back/pallas_call | solution.py:895
  132.3 1.7 collective-permute-start.46
  134.1 4.0 %all-to-all-done.2 = bf16[4,576,128]{2,1,0:T(8,128)(2,1)} async-done(((bf16[4,576,128]{2,1,0:T(8,128)(2,1)}), bf16[4,576,128]{2,1,0:T(8,128)(2,1)}, u32[]{:S(2)}, u32[]{:S(2)}) %all-to-all-start.2) | async-done | bytes 589856 | tf_op jit(solution)/shard_map/all_to_all | solution.py:1109
  138.0 3.5 %all-to-all-start.3 = ((bf16[4,576,128]{2,1,0:T(8,128)(2,1)}), bf16[4,576,128]{2,1,0:T(8,128)(2,1)S(1)}, u32[]{:S(2)}, u32[]{:S(2)}) async-start(bf16[4,576,128]{2,1,0:T(8,128)(2,1)} %bitcast.31), calls=%async_computation.3 | async-start | bytes 1179648 | tf_op jit(solution)/shard_map/all_to_all | solution.py:1109
  143.2 1.0 collective-permute-done.47.other
  144.3 3.9 %conv_back.7 = (bf16[64,1536]{1,0:T(8,128)(2,1)S(1)}, bf16[64,1536]{1,0:T(8,128)(2,1)S(1)}, bf16[64,1536]{1,0:T(8,128)(2,1)S(1)}, bf16[64,1536]{1,0:T(8,128)(2,1...) custom-call(bf16[64,1536]{1,0:T(8,128)(2,1)S(1)} %get-tuple-element., ...), custom_call_target="tpu_custom_call" | custom-call | flops 3000000000 | bytes 5128192 | tf_op jit(solution)/shard_map/conv_back/pallas_call | solution.py:895
  148.2 1.3 collective-permute-start.49
  149.5 1.0 collective-permute-start.60
  150.5 1.2 collective-permute-start.61
  151.7 2.6 %collective-permute-start.51 = (bf16[592,128]{1,0:T(8,128)(2,1)}, bf16[592,128]{1,0:T(8,128)(2,1)S(1)}, u32[]{:S(2)}, u32[]{:S(2)}) collective-permute-start(bf16[592,128]{1,0:T(8,128)(2,1)} %get-tuple-element.246), channel_id=1, source_target_pairs={{0,4},{1,5},{2,6},{3,7},{4,0},{5,1},{6,2},{7,3},{8,12},{9,13},{10,... | collective-permute-start | bytes 454664 | tf_op jit(solution)/shard_map/ppermute | solution.py:253
  154.3 1.3 collective-permute-start.52
  156.0 1.6 collective-permute-start.50
  157.5 2.8 %collective-permute-done.60.refs_2_ = bf16[64,1536]{1,0:T(8,128)(2,1)S(1)} collective-permute-done((bf16[64,1536]{1,0:T(8,128)(2,1)S(1)}, bf16[64,1536]{1,0:T(8,128)(2,1)S(1)}, u32[]{:S(2)}, u32[]{:S(2)}) %collective-permute-start.60) | collective-permute-done | bytes 196640 | tf_op jit(solution)/shard_map/ppermute | solution.py:253
  160.4 4.1 %all-to-all-done.3 = bf16[4,576,128]{2,1,0:T(8,128)(2,1)S(1)} async-done(((bf16[4,576,128]{2,1,0:T(8,128)(2,1)}), bf16[4,576,128]{2,1,0:T(8,128)(2,1)S(1)}, u32[]{:S(2)}, u32[]{:S(2)}) %all-to-all-start.3) | async-done | bytes 589856 | tf_op jit(solution)/shard_map/all_to_all | solution.py:1109
  164.5 1.2 input.1
  165.7 1.5 fold.1
  169.6 4.2 %collective-permute-start.64 = (bf16[256,384]{1,0:T(8,128)(2,1)S(1)}, bf16[256,384]{1,0:T(8,128)(2,1)S(1)}, u32[]{:S(2)}, u32[]{:S(2)}) collective-permute-start(bf16[256,384]{1,0:T(8,128)(2,1)S(1)} %get-tuple-element.271), channel_id=1, source_target_pairs={{0,2},{1,7},{2,10},{3,15},{4,18},{5,23},{6,26},{7,31},{8,0},{9,5},... | collective-permute-start | bytes 589832 | tf_op jit(solution)/shard_map/ppermute | solution.py:253
  173.8 3.8 %collective-permute-start.54 = (bf16[592,128]{1,0:T(8,128)(2,1)S(1)}, bf16[592,128]{1,0:T(8,128)(2,1)S(1)}, u32[]{:S(2)}, u32[]{:S(2)}) collective-permute-start(bf16[592,128]{1,0:T(8,128)(2,1)S(1)} %get-tuple-element.258), channel_id=1, source_target_pairs={{0,16},{1,17},{2,18},{3,19},{4,20},{5,21},{6,22},{7,23},{8,24},{9,... | collective-permute-start | bytes 454664 | tf_op jit(solution)/shard_map/ppermute | solution.py:253
  177.6 7.8 %collective-permute-done.54.refs_2_ = bf16[592,128]{1,0:T(8,128)(2,1)S(1)} collective-permute-done((bf16[592,128]{1,0:T(8,128)(2,1)S(1)}, bf16[592,128]{1,0:T(8,128)(2,1)S(1)}, u32[]{:S(2)}, u32[]{:S(2)}) %collective-permute-start.54) | collective-permute-done | bytes 151584 | tf_op jit(solution)/shard_map/ppermute | solution.py:253
  187.9 1.9 %outputs.1 = (f32[9,64,512]{2,1,0:T(8,128)}, f32[1,64]{1,0:T(1,128)}, f32[1,64]{1,0:T(1,128)}, bf16[192,512]{1,0:T(8,128)(2,1)}, bf16[192,512]{1,0:T(8,128)(2,1)}) custom-call(bf16[592,128]{1,0:T(8,128)(2,1)S(1)} %get-tuple-element.256.refs_0_, bf16[592,128]{1,0:T(8,128)(2,1)S(1)} %collective-permute-done.53.refs_1_, ...), custom_call_target="tpu_custom_call" | custom-call | bytes 3736064 | tf_op jit(solution)/shard_map/outputs/pallas_call | solution.py:895
  (133 shorter events, 25.3 us)
Async XLA Ops:
  3.1 24.5 %collective-permute-start.7 = (bf16[592,512]{1,0:T(8,128)(2,1)S(1)}, bf16[592,512]{1,0:T(8,128)(2,1)S(1)}, u32[]{:S(2)}, u32[]{:S(2)}) collective-permute-start(bf16[592,512]{1,0:T(8,128)(2,1)S(1)} %get-tuple-element.143), channel_id=1, source_target_pairs={{0,8},{1,9},{2,10},{3,11},{4,12},{5,13},{6,14},{7,15},{8,0},{9,1},... | collective-permute-start | bytes 1818632 | tf_op jit(solution)/shard_map/ppermute | solution.py:253
  6.2 28.1 %collective-permute-start.8 = (bf16[592,512]{1,0:T(8,128)(2,1)S(1)}, bf16[592,512]{1,0:T(8,128)(2,1)S(1)}, u32[]{:S(2)}, u32[]{:S(2)}) collective-permute-start(bf16[592,512]{1,0:T(8,128)(2,1)S(1)} %get-tuple-element.144), channel_id=1, source_target_pairs={{0,16},{1,17},{2,18},{3,19},{4,20},{5,21},{6,22},{7,23},{8,24},{9,... | collective-permute-start | bytes 1818632 | tf_op jit(solution)/shard_map/ppermute | solution.py:253
  9.1 10.8 %collective-permute-start = (bf16[208,512]{1,0:T(8,128)(2,1)S(1)}, bf16[208,512]{1,0:T(8,128)(2,1)S(1)}, u32[]{:S(2)}, u32[]{:S(2)}) collective-permute-start(bf16[208,512]{1,0:T(8,128)(2,1)S(1)} %get-tuple-element.148), channel_id=1, source_target_pairs={{0,2},{1,3},{2,0},{3,1},{4,6},{5,7},{6,4},{7,5},{8,10},{9,11},{10,... | collective-permute-start | bytes 638984 | tf_op jit(solution)/shard_map/ppermute | solution.py:253
  10.7 23.6 %collective-permute-start.9 = (bf16[592,512]{1,0:T(8,128)(2,1)S(1)}, bf16[592,512]{1,0:T(8,128)(2,1)S(1)}, u32[]{:S(2)}, u32[]{:S(2)}) collective-permute-start(bf16[592,512]{1,0:T(8,128)(2,1)S(1)} %get-tuple-element.145), channel_id=1, source_target_pairs={{0,24},{1,25},{2,26},{3,27},{4,28},{5,29},{6,30},{7,31},{8,16},{9,... | collective-permute-start | bytes 1818632 | tf_op jit(solution)/shard_map/ppermute | solution.py:253
  11.2 13.9 %collective-permute-start.1 = (bf16[208,512]{1,0:T(8,128)(2,1)S(1)}, bf16[208,512]{1,0:T(8,128)(2,1)S(1)}, u32[]{:S(2)}, u32[]{:S(2)}) collective-permute-start(bf16[208,512]{1,0:T(8,128)(2,1)S(1)} %get-tuple-element.149), channel_id=1, source_target_pairs={{0,4},{1,5},{2,6},{3,7},{4,0},{5,1},{6,2},{7,3},{8,12},{9,13},{10,... | collective-permute-start | bytes 638984 | tf_op jit(solution)/shard_map/ppermute | solution.py:253
  19.8 7.8 %collective-permute-start.2 = (bf16[208,512]{1,0:T(8,128)(2,1)S(1)}, bf16[208,512]{1,0:T(8,128)(2,1)S(1)}, u32[]{:S(2)}, u32[]{:S(2)}) collective-permute-start(bf16[208,512]{1,0:T(8,128)(2,1)S(1)} %get-tuple-element.150), channel_id=1, source_target_pairs={{0,6},{1,7},{2,4},{3,5},{4,2},{5,3},{6,0},{7,1},{8,14},{9,15},{10,... | collective-permute-start | bytes 638984 | tf_op jit(solution)/shard_map/ppermute | solution.py:253
  25.1 9.2 %collective-permute-start.3 = (bf16[208,512]{1,0:T(8,128)(2,1)S(1)}, bf16[208,512]{1,0:T(8,128)(2,1)S(1)}, u32[]{:S(2)}, u32[]{:S(2)}) collective-permute-start(bf16[208,512]{1,0:T(8,128)(2,1)S(1)} %get-tuple-element.147.refs_0_), channel_id=1, source_target_pairs={{0,1},{1,0},{2,3},{3,2},{4,5},{5,4},{6,7},{7,6},{8,9},{9,8},{10,11... | collective-permute-start | bytes 638984 | tf_op jit(solution)/shard_map/ppermute | solution.py:253
  27.6 6.8 %collective-permute-start.4 = (bf16[208,512]{1,0:T(8,128)(2,1)S(1)}, bf16[208,512]{1,0:T(8,128)(2,1)S(1)}, u32[]{:S(2)}, u32[]{:S(2)}) collective-permute-start(bf16[208,512]{1,0:T(8,128)(2,1)S(1)} %collective-permute-done.refs_1_), channel_id=1, source_target_pairs={{0,1},{1,0},{2,3},{3,2},{4,5},{5,4},{6,7},{7,6},{8,9},{9,8},{10,11... | collective-permute-start | bytes 638984 | tf_op jit(solution)/shard_map/ppermute | solution.py:253
  27.6 6.8 %collective-permute-start.5 = (bf16[208,512]{1,0:T(8,128)(2,1)S(1)}, bf16[208,512]{1,0:T(8,128)(2,1)S(1)}, u32[]{:S(2)}, u32[]{:S(2)}) collective-permute-start(bf16[208,512]{1,0:T(8,128)(2,1)S(1)} %collective-permute-done.1.refs_2_), channel_id=1, source_target_pairs={{0,1},{1,0},{2,3},{3,2},{4,5},{5,4},{6,7},{7,6},{8,9},{9,8},{10,11... | collective-permute-start | bytes 638984 | tf_op jit(solution)/shard_map/ppermute | solution.py:253
  34.3 1.5 collective-permute-start.6
  38.4 10.4 %collective-permute-start.12 = (bf16[64,1536]{1,0:T(8,128)(2,1)S(1)}, bf16[64,1536]{1,0:T(8,128)(2,1)S(1)}, u32[]{:S(2)}, u32[]{:S(2)}) collective-permute-start(bf16[64,1536]{1,0:T(8,128)(2,1)S(1)} %get-tuple-element.157.refs_0_), channel_id=1, source_target_pairs={{0,24},{1,25},{2,26},{3,27},{4,28},{5,29},{6,30},{7,31},{8,16},{9,... | collective-permute-start | bytes 589832 | tf_op jit(solution)/shard_map/ppermute | solution.py:253
  39.9 10.7 %collective-permute-start.10 = (bf16[64,1536]{1,0:T(8,128)(2,1)S(1)}, bf16[64,1536]{1,0:T(8,128)(2,1)S(1)}, u32[]{:S(2)}, u32[]{:S(2)}) collective-permute-start(bf16[64,1536]{1,0:T(8,128)(2,1)S(1)} %get-tuple-element.157.refs_0_), channel_id=1, source_target_pairs={{0,8},{1,9},{2,10},{3,11},{4,12},{5,13},{6,14},{7,15},{8,0},{9,1},... | collective-permute-start | bytes 589832 | tf_op jit(solution)/shard_map/ppermute | solution.py:253
  41.4 9.2 %collective-permute-start.11 = (bf16[64,1536]{1,0:T(8,128)(2,1)S(1)}, bf16[64,1536]{1,0:T(8,128)(2,1)S(1)}, u32[]{:S(2)}, u32[]{:S(2)}) collective-permute-start(bf16[64,1536]{1,0:T(8,128)(2,1)S(1)} %get-tuple-element.157.refs_0_), channel_id=1, source_target_pairs={{0,16},{1,17},{2,18},{3,19},{4,20},{5,21},{6,22},{7,23},{8,24},{9,... | collective-permute-start | bytes 589832 | tf_op jit(solution)/shard_map/ppermute | solution.py:253
  41.9 9.2 %collective-permute-start.13 = (bf16[64,1536]{1,0:T(8,128)(2,1)S(1)}, bf16[64,1536]{1,0:T(8,128)(2,1)S(1)}, u32[]{:S(2)}, u32[]{:S(2)}) collective-permute-start(bf16[64,1536]{1,0:T(8,128)(2,1)S(1)} %get-tuple-element.157.refs_0_), channel_id=1, source_target_pairs={{0,1},{1,0},{2,3},{3,2},{4,5},{5,4},{6,7},{7,6},{8,9},{9,8},{10,11... | collective-permute-start | bytes 589832 | tf_op jit(solution)/shard_map/ppermute | solution.py:253
  48.8 2.3 %collective-permute-start.16 = (bf16[64,1536]{1,0:T(8,128)(2,1)S(1)}, bf16[64,1536]{1,0:T(8,128)(2,1)S(1)}, u32[]{:S(2)}, u32[]{:S(2)}) collective-permute-start(bf16[64,1536]{1,0:T(8,128)(2,1)S(1)} %collective-permute-done.12.refs_3_), channel_id=1, source_target_pairs={{0,1},{1,0},{2,3},{3,2},{4,5},{5,4},{6,7},{7,6},{8,9},{9,8},{10,11... | collective-permute-start | bytes 589832 | tf_op jit(solution)/shard_map/ppermute | solution.py:253
  50.6 1.7 collective-permute-start.15
  55.4 9.5 %collective-permute-start.19 = (bf16[64,1536]{1,0:T(8,128)(2,1)S(1)}, bf16[64,1536]{1,0:T(8,128)(2,1)S(1)}, u32[]{:S(2)}, u32[]{:S(2)}) collective-permute-start(bf16[64,1536]{1,0:T(8,128)(2,1)S(1)} %get-tuple-element.170.refs_0_), channel_id=1, source_target_pairs={{0,24},{1,25},{2,26},{3,27},{4,28},{5,29},{6,30},{7,31},{8,16},{9,... | collective-permute-start | bytes 589832 | tf_op jit(solution)/shard_map/ppermute | solution.py:253
  56.5 10.7 %collective-permute-start.17 = (bf16[64,1536]{1,0:T(8,128)(2,1)S(1)}, bf16[64,1536]{1,0:T(8,128)(2,1)S(1)}, u32[]{:S(2)}, u32[]{:S(2)}) collective-permute-start(bf16[64,1536]{1,0:T(8,128)(2,1)S(1)} %get-tuple-element.170.refs_0_), channel_id=1, source_target_pairs={{0,8},{1,9},{2,10},{3,11},{4,12},{5,13},{6,14},{7,15},{8,0},{9,1},... | collective-permute-start | bytes 589832 | tf_op jit(solution)/shard_map/ppermute | solution.py:253
  58.0 9.6 %collective-permute-start.18 = (bf16[64,1536]{1,0:T(8,128)(2,1)S(1)}, bf16[64,1536]{1,0:T(8,128)(2,1)S(1)}, u32[]{:S(2)}, u32[]{:S(2)}) collective-permute-start(bf16[64,1536]{1,0:T(8,128)(2,1)S(1)} %get-tuple-element.170.refs_0_), channel_id=1, source_target_pairs={{0,16},{1,17},{2,18},{3,19},{4,20},{5,21},{6,22},{7,23},{8,24},{9,... | collective-permute-start | bytes 589832 | tf_op jit(solution)/shard_map/ppermute | solution.py:253
  58.9 8.8 %collective-permute-start.20 = (bf16[64,1536]{1,0:T(8,128)(2,1)S(1)}, bf16[64,1536]{1,0:T(8,128)(2,1)S(1)}, u32[]{:S(2)}, u32[]{:S(2)}) collective-permute-start(bf16[64,1536]{1,0:T(8,128)(2,1)S(1)} %get-tuple-element.170.refs_0_), channel_id=1, source_target_pairs={{0,1},{1,0},{2,3},{3,2},{4,5},{5,4},{6,7},{7,6},{8,9},{9,8},{10,11... | collective-permute-start | bytes 589832 | tf_op jit(solution)/shard_map/ppermute | solution.py:253
  58.9 16.1 %all-to-all-start = ((bf16[4,192,128]{2,1,0:T(8,128)(2,1)}), bf16[4,192,128]{2,1,0:T(8,128)(2,1)S(1)}, u32[]{:S(2)}, u32[]{:S(2)}) async-start(bf16[4,192,128]{2,1,0:T(8,128)(2,1)} %bitcast.7), calls=%async_computation | async-start | bytes 393216 | tf_op jit(solution)/shard_map/all_to_all | solution.py:1025
  64.9 2.8 %collective-permute-start.23 = (bf16[64,1536]{1,0:T(8,128)(2,1)S(1)}, bf16[64,1536]{1,0:T(8,128)(2,1)S(1)}, u32[]{:S(2)}, u32[]{:S(2)}) collective-permute-start(bf16[64,1536]{1,0:T(8,128)(2,1)S(1)} %collective-permute-done.19.refs_3_), channel_id=1, source_target_pairs={{0,1},{1,0},{2,3},{3,2},{4,5},{5,4},{6,7},{7,6},{8,9},{9,8},{10,11... | collective-permute-start | bytes 589832 | tf_op jit(solution)/shard_map/ppermute | solution.py:253
  71.5 8.8 %collective-permute-start.26 = (bf16[64,1536]{1,0:T(8,128)(2,1)S(1)}, bf16[64,1536]{1,0:T(8,128)(2,1)S(1)}, u32[]{:S(2)}, u32[]{:S(2)}) collective-permute-start(bf16[64,1536]{1,0:T(8,128)(2,1)S(1)} %get-tuple-element.176.refs_0_), channel_id=1, source_target_pairs={{0,24},{1,25},{2,26},{3,27},{4,28},{5,29},{6,30},{7,31},{8,16},{9,... | collective-permute-start | bytes 589832 | tf_op jit(solution)/shard_map/ppermute | solution.py:253
  72.6 10.7 %collective-permute-start.24 = (bf16[64,1536]{1,0:T(8,128)(2,1)S(1)}, bf16[64,1536]{1,0:T(8,128)(2,1)S(1)}, u32[]{:S(2)}, u32[]{:S(2)}) collective-permute-start(bf16[64,1536]{1,0:T(8,128)(2,1)S(1)} %get-tuple-element.176.refs_0_), channel_id=1, source_target_pairs={{0,8},{1,9},{2,10},{3,11},{4,12},{5,13},{6,14},{7,15},{8,0},{9,1},... | collective-permute-start | bytes 589832 | tf_op jit(solution)/shard_map/ppermute | solution.py:253
  74.1 9.6 %collective-permute-start.25 = (bf16[64,1536]{1,0:T(8,128)(2,1)S(1)}, bf16[64,1536]{1,0:T(8,128)(2,1)S(1)}, u32[]{:S(2)}, u32[]{:S(2)}) collective-permute-start(bf16[64,1536]{1,0:T(8,128)(2,1)S(1)} %get-tuple-element.176.refs_0_), channel_id=1, source_target_pairs={{0,16},{1,17},{2,18},{3,19},{4,20},{5,21},{6,22},{7,23},{8,24},{9,... | collective-permute-start | bytes 589832 | tf_op jit(solution)/shard_map/ppermute | solution.py:253
  75.0 1.7 collective-permute-start.27
  75.1 9.0 %collective-permute-start.28 = (bf16[64,1536]{1,0:T(8,128)(2,1)S(1)}, bf16[64,1536]{1,0:T(8,128)(2,1)S(1)}, u32[]{:S(2)}, u32[]{:S(2)}) collective-permute-start(bf16[64,1536]{1,0:T(8,128)(2,1)S(1)} %get-tuple-element.176.refs_0_), channel_id=1, source_target_pairs={{0,1},{1,0},{2,3},{3,2},{4,5},{5,4},{6,7},{7,6},{8,9},{9,8},{10,11... | collective-permute-start | bytes 589832 | tf_op jit(solution)/shard_map/ppermute | solution.py:253
  80.2 3.9 %collective-permute-start.31 = (bf16[64,1536]{1,0:T(8,128)(2,1)S(1)}, bf16[64,1536]{1,0:T(8,128)(2,1)S(1)}, u32[]{:S(2)}, u32[]{:S(2)}) collective-permute-start(bf16[64,1536]{1,0:T(8,128)(2,1)S(1)} %collective-permute-done.26.refs_3_), channel_id=1, source_target_pairs={{0,1},{1,0},{2,3},{3,2},{4,5},{5,4},{6,7},{7,6},{8,9},{9,8},{10,11... | collective-permute-start | bytes 589832 | tf_op jit(solution)/shard_map/ppermute | solution.py:253
  83.8 5.4 %collective-permute-start.33 = (bf16[256,640]{1,0:T(8,128)(2,1)S(1)}, bf16[256,640]{1,0:T(8,128)(2,1)S(1)}, u32[]{:S(2)}, u32[]{:S(2)}) collective-permute-start(bf16[256,640]{1,0:T(8,128)(2,1)S(1)} %copy-done.11), channel_id=1, source_target_pairs={{0,1},{1,0},{2,3},{3,2},{4,5},{5,4},{6,7},{7,6},{8,9},{9,8},{10,11... | collective-permute-start | bytes 983048 | tf_op jit(solution)/shard_map/ppermute | solution.py:253
  87.6 1.5 collective-permute-start.32
  93.1 8.4 %collective-permute-start.34 = (bf16[64,1536]{1,0:T(8,128)(2,1)S(1)}, bf16[64,1536]{1,0:T(8,128)(2,1)S(1)}, u32[]{:S(2)}, u32[]{:S(2)}) collective-permute-start(bf16[64,1536]{1,0:T(8,128)(2,1)S(1)} %get-tuple-element.193), channel_id=1, source_target_pairs={{0,8},{1,9},{2,10},{3,11},{4,12},{5,13},{6,14},{7,15},{8,0},{9,1},... | collective-permute-start | bytes 589832 | tf_op jit(solution)/shard_map/ppermute | solution.py:253
  93.6 7.9 %collective-permute-start.35 = (bf16[64,1536]{1,0:T(8,128)(2,1)S(1)}, bf16[64,1536]{1,0:T(8,128)(2,1)S(1)}, u32[]{:S(2)}, u32[]{:S(2)}) collective-permute-start(bf16[64,1536]{1,0:T(8,128)(2,1)S(1)} %get-tuple-element.194), channel_id=1, source_target_pairs={{0,16},{1,17},{2,18},{3,19},{4,20},{5,21},{6,22},{7,23},{8,24},{9,... | collective-permute-start | bytes 589832 | tf_op jit(solution)/shard_map/ppermute | solution.py:253
  94.7 10.1 %collective-permute-start.36 = (bf16[64,1536]{1,0:T(8,128)(2,1)S(1)}, bf16[64,1536]{1,0:T(8,128)(2,1)S(1)}, u32[]{:S(2)}, u32[]{:S(2)}) collective-permute-start(bf16[64,1536]{1,0:T(8,128)(2,1)S(1)} %get-tuple-element.195), channel_id=1, source_target_pairs={{0,24},{1,25},{2,26},{3,27},{4,28},{5,29},{6,30},{7,31},{8,16},{9,... | collective-permute-start | bytes 589832 | tf_op jit(solution)/shard_map/ppermute | solution.py:253
  96.6 10.2 %collective-permute-start.38 = (bf16[256,640]{1,0:T(8,128)(2,1)S(1)}, bf16[256,640]{1,0:T(8,128)(2,1)S(1)}, u32[]{:S(2)}, u32[]{:S(2)}) collective-permute-start(bf16[256,640]{1,0:T(8,128)(2,1)S(1)} %copy-done.10), channel_id=1, source_target_pairs={{0,1},{1,0},{2,3},{3,2},{4,5},{5,4},{6,7},{7,6},{8,9},{9,8},{10,11... | collective-permute-start | bytes 983048 | tf_op jit(solution)/shard_map/ppermute | solution.py:253
  96.6 21.4 %all-to-all-start.1 = ((bf16[4,576,128]{2,1,0:T(8,128)(2,1)}), bf16[4,576,128]{2,1,0:T(8,128)(2,1)S(1)}, u32[]{:S(2)}, u32[]{:S(2)}) async-start(bf16[4,576,128]{2,1,0:T(8,128)(2,1)} %bitcast.33), calls=%async_computation.1 | async-start | bytes 1179648 | tf_op jit(solution)/shard_map/all_to_all | solution.py:1109
  105.3 1.5 collective-permute-start.37
  110.8 11.7 %collective-permute-start.39 = (bf16[64,1536]{1,0:T(8,128)(2,1)S(1)}, bf16[64,1536]{1,0:T(8,128)(2,1)S(1)}, u32[]{:S(2)}, u32[]{:S(2)}) collective-permute-start(bf16[64,1536]{1,0:T(8,128)(2,1)S(1)} %get-tuple-element.211), channel_id=1, source_target_pairs={{0,8},{1,9},{2,10},{3,11},{4,12},{5,13},{6,14},{7,15},{8,0},{9,1},... | collective-permute-start | bytes 589832 | tf_op jit(solution)/shard_map/ppermute | solution.py:253
  112.1 10.9 %collective-permute-start.40 = (bf16[64,1536]{1,0:T(8,128)(2,1)S(1)}, bf16[64,1536]{1,0:T(8,128)(2,1)S(1)}, u32[]{:S(2)}, u32[]{:S(2)}) collective-permute-start(bf16[64,1536]{1,0:T(8,128)(2,1)S(1)} %get-tuple-element.212), channel_id=1, source_target_pairs={{0,16},{1,17},{2,18},{3,19},{4,20},{5,21},{6,22},{7,23},{8,24},{9,... | collective-permute-start | bytes 589832 | tf_op jit(solution)/shard_map/ppermute | solution.py:253
  113.1 9.9 %collective-permute-start.41 = (bf16[64,1536]{1,0:T(8,128)(2,1)S(1)}, bf16[64,1536]{1,0:T(8,128)(2,1)S(1)}, u32[]{:S(2)}, u32[]{:S(2)}) collective-permute-start(bf16[64,1536]{1,0:T(8,128)(2,1)S(1)} %get-tuple-element.213), channel_id=1, source_target_pairs={{0,24},{1,25},{2,26},{3,27},{4,28},{5,29},{6,30},{7,31},{8,16},{9,... | collective-permute-start | bytes 589832 | tf_op jit(solution)/shard_map/ppermute | solution.py:253
  114.3 12.3 %collective-permute-start.43 = (bf16[256,640]{1,0:T(8,128)(2,1)S(1)}, bf16[256,640]{1,0:T(8,128)(2,1)S(1)}, u32[]{:S(2)}, u32[]{:S(2)}) collective-permute-start(bf16[256,640]{1,0:T(8,128)(2,1)S(1)} %copy-done.9), channel_id=1, source_target_pairs={{0,1},{1,0},{2,3},{3,2},{4,5},{5,4},{6,7},{7,6},{8,9},{9,8},{10,11... | collective-permute-start | bytes 983048 | tf_op jit(solution)/shard_map/ppermute | solution.py:253
  118.1 20.0 %all-to-all-start.2 = ((bf16[4,576,128]{2,1,0:T(8,128)(2,1)}), bf16[4,576,128]{2,1,0:T(8,128)(2,1)}, u32[]{:S(2)}, u32[]{:S(2)}) async-start(bf16[4,576,128]{2,1,0:T(8,128)(2,1)} %bitcast.32), calls=%async_computation.2 | async-start | bytes 1179648 | tf_op jit(solution)/shard_map/all_to_all | solution.py:1109
  125.1 1.5 collective-permute-start.42
  130.5 11.1 %collective-permute-start.44 = (bf16[64,1536]{1,0:T(8,128)(2,1)S(1)}, bf16[64,1536]{1,0:T(8,128)(2,1)S(1)}, u32[]{:S(2)}, u32[]{:S(2)}) collective-permute-start(bf16[64,1536]{1,0:T(8,128)(2,1)S(1)} %get-tuple-element.229), channel_id=1, source_target_pairs={{0,8},{1,9},{2,10},{3,11},{4,12},{5,13},{6,14},{7,15},{8,0},{9,1},... | collective-permute-start | bytes 589832 | tf_op jit(solution)/shard_map/ppermute | solution.py:253
  131.3 10.3 %collective-permute-start.45 = (bf16[64,1536]{1,0:T(8,128)(2,1)S(1)}, bf16[64,1536]{1,0:T(8,128)(2,1)S(1)}, u32[]{:S(2)}, u32[]{:S(2)}) collective-permute-start(bf16[64,1536]{1,0:T(8,128)(2,1)S(1)} %get-tuple-element.230), channel_id=1, source_target_pairs={{0,16},{1,17},{2,18},{3,19},{4,20},{5,21},{6,22},{7,23},{8,24},{9,... | collective-permute-start | bytes 589832 | tf_op jit(solution)/shard_map/ppermute | solution.py:253
  132.3 9.9 %collective-permute-start.46 = (bf16[64,1536]{1,0:T(8,128)(2,1)S(1)}, bf16[64,1536]{1,0:T(8,128)(2,1)S(1)}, u32[]{:S(2)}, u32[]{:S(2)}) collective-permute-start(bf16[64,1536]{1,0:T(8,128)(2,1)S(1)} %get-tuple-element.231), channel_id=1, source_target_pairs={{0,24},{1,25},{2,26},{3,27},{4,28},{5,29},{6,30},{7,31},{8,16},{9,... | collective-permute-start | bytes 589832 | tf_op jit(solution)/shard_map/ppermute | solution.py:253
  138.0 26.4 %all-to-all-start.3 = ((bf16[4,576,128]{2,1,0:T(8,128)(2,1)}), bf16[4,576,128]{2,1,0:T(8,128)(2,1)S(1)}, u32[]{:S(2)}, u32[]{:S(2)}) async-start(bf16[4,576,128]{2,1,0:T(8,128)(2,1)} %bitcast.31), calls=%async_computation.3 | async-start | bytes 1179648 | tf_op jit(solution)/shard_map/all_to_all | solution.py:1109
  141.5 1.7 collective-permute-start.48
  142.8 1.5 collective-permute-start.47
  148.2 7.8 %collective-permute-start.49 = (bf16[64,1536]{1,0:T(8,128)(2,1)S(1)}, bf16[64,1536]{1,0:T(8,128)(2,1)S(1)}, u32[]{:S(2)}, u32[]{:S(2)}) collective-permute-start(bf16[64,1536]{1,0:T(8,128)(2,1)S(1)} %get-tuple-element.244), channel_id=1, source_target_pairs={{0,8},{1,9},{2,10},{3,11},{4,12},{5,13},{6,14},{7,15},{8,0},{9,1},... | collective-permute-start | bytes 589832 | tf_op jit(solution)/shard_map/ppermute | solution.py:253
  149.5 10.9 %collective-permute-start.60 = (bf16[64,1536]{1,0:T(8,128)(2,1)S(1)}, bf16[64,1536]{1,0:T(8,128)(2,1)S(1)}, u32[]{:S(2)}, u32[]{:S(2)}) collective-permute-start(bf16[64,1536]{1,0:T(8,128)(2,1)S(1)} %get-tuple-element.261), channel_id=1, source_target_pairs={{0,16},{1,17},{2,18},{3,19},{4,20},{5,21},{6,22},{7,23},{8,24},{9,... | collective-permute-start | bytes 589832 | tf_op jit(solution)/shard_map/ppermute | solution.py:253
  150.5 9.9 %collective-permute-start.61 = (bf16[64,1536]{1,0:T(8,128)(2,1)S(1)}, bf16[64,1536]{1,0:T(8,128)(2,1)S(1)}, u32[]{:S(2)}, u32[]{:S(2)}) collective-permute-start(bf16[64,1536]{1,0:T(8,128)(2,1)S(1)} %get-tuple-element.262), channel_id=1, source_target_pairs={{0,24},{1,25},{2,26},{3,27},{4,28},{5,29},{6,30},{7,31},{8,16},{9,... | collective-permute-start | bytes 589832 | tf_op jit(solution)/shard_map/ppermute | solution.py:253
  151.7 16.0 %collective-permute-start.51 = (bf16[592,128]{1,0:T(8,128)(2,1)}, bf16[592,128]{1,0:T(8,128)(2,1)S(1)}, u32[]{:S(2)}, u32[]{:S(2)}) collective-permute-start(bf16[592,128]{1,0:T(8,128)(2,1)} %get-tuple-element.246), channel_id=1, source_target_pairs={{0,4},{1,5},{2,6},{3,7},{4,0},{5,1},{6,2},{7,3},{8,12},{9,13},{10,... | collective-permute-start | bytes 454664 | tf_op jit(solution)/shard_map/ppermute | solution.py:253
  154.3 13.4 %collective-permute-start.52 = (bf16[592,128]{1,0:T(8,128)(2,1)}, bf16[592,128]{1,0:T(8,128)(2,1)S(1)}, u32[]{:S(2)}, u32[]{:S(2)}) collective-permute-start(bf16[592,128]{1,0:T(8,128)(2,1)} %get-tuple-element.247), channel_id=1, source_target_pairs={{0,6},{1,7},{2,4},{3,5},{4,2},{5,3},{6,0},{7,1},{8,14},{9,15},{10,... | collective-permute-start | bytes 454664 | tf_op jit(solution)/shard_map/ppermute | solution.py:253
  156.0 12.1 %collective-permute-start.50 = (bf16[592,128]{1,0:T(8,128)(2,1)}, bf16[592,128]{1,0:T(8,128)(2,1)S(1)}, u32[]{:S(2)}, u32[]{:S(2)}) collective-permute-start(bf16[592,128]{1,0:T(8,128)(2,1)} %get-tuple-element.245), channel_id=1, source_target_pairs={{0,2},{1,3},{2,0},{3,1},{4,6},{5,7},{6,4},{7,5},{8,10},{9,11},{10,... | collective-permute-start | bytes 454664 | tf_op jit(solution)/shard_map/ppermute | solution.py:253
  165.7 3.2 %collective-permute-start.62 = (bf16[256,384]{1,0:T(8,128)(2,1)S(1)}, bf16[256,384]{1,0:T(8,128)(2,1)S(1)}, u32[]{:S(2)}, u32[]{:S(2)}) collective-permute-start(bf16[256,384]{1,0:T(8,128)(2,1)S(1)} %get-tuple-element.269), channel_id=1, source_target_pairs={{0,1},{1,0},{2,3},{3,2},{4,5},{5,4},{6,7},{7,6},{8,9},{9,8},{10,11... | collective-permute-start | bytes 589832 | tf_op jit(solution)/shard_map/ppermute | solution.py:253
  168.2 9.4 %collective-permute-start.53 = (bf16[592,128]{1,0:T(8,128)(2,1)S(1)}, bf16[592,128]{1,0:T(8,128)(2,1)S(1)}, u32[]{:S(2)}, u32[]{:S(2)}) collective-permute-start(bf16[592,128]{1,0:T(8,128)(2,1)S(1)} %get-tuple-element.257), channel_id=1, source_target_pairs={{0,8},{1,9},{2,10},{3,11},{4,12},{5,13},{6,14},{7,15},{8,0},{9,1},... | collective-permute-start | bytes 454664 | tf_op jit(solution)/shard_map/ppermute | solution.py:253
  168.9 17.1 %collective-permute-start.63 = (bf16[256,384]{1,0:T(8,128)(2,1)S(1)}, bf16[256,384]{1,0:T(8,128)(2,1)S(1)}, u32[]{:S(2)}, u32[]{:S(2)}) collective-permute-start(bf16[256,384]{1,0:T(8,128)(2,1)S(1)} %get-tuple-element.270), channel_id=1, source_target_pairs={{0,0},{1,5},{2,8},{3,13},{4,16},{5,21},{6,24},{7,29},{8,2},{9,7},{... | collective-permute-start | bytes 589832 | tf_op jit(solution)/shard_map/ppermute | solution.py:253
  169.6 16.4 %collective-permute-start.64 = (bf16[256,384]{1,0:T(8,128)(2,1)S(1)}, bf16[256,384]{1,0:T(8,128)(2,1)S(1)}, u32[]{:S(2)}, u32[]{:S(2)}) collective-permute-start(bf16[256,384]{1,0:T(8,128)(2,1)S(1)} %get-tuple-element.271), channel_id=1, source_target_pairs={{0,2},{1,7},{2,10},{3,15},{4,18},{5,23},{6,26},{7,31},{8,0},{9,5},... | collective-permute-start | bytes 589832 | tf_op jit(solution)/shard_map/ppermute | solution.py:253
  173.8 11.6 %collective-permute-start.54 = (bf16[592,128]{1,0:T(8,128)(2,1)S(1)}, bf16[592,128]{1,0:T(8,128)(2,1)S(1)}, u32[]{:S(2)}, u32[]{:S(2)}) collective-permute-start(bf16[592,128]{1,0:T(8,128)(2,1)S(1)} %get-tuple-element.258), channel_id=1, source_target_pairs={{0,16},{1,17},{2,18},{3,19},{4,20},{5,21},{6,22},{7,23},{8,24},{9,... | collective-permute-start | bytes 454664 | tf_op jit(solution)/shard_map/ppermute | solution.py:253
  177.6 7.9 %collective-permute-start.55 = (bf16[592,128]{1,0:T(8,128)(2,1)S(1)}, bf16[592,128]{1,0:T(8,128)(2,1)S(1)}, u32[]{:S(2)}, u32[]{:S(2)}) collective-permute-start(bf16[592,128]{1,0:T(8,128)(2,1)S(1)} %get-tuple-element.259), channel_id=1, source_target_pairs={{0,24},{1,25},{2,26},{3,27},{4,28},{5,29},{6,30},{7,31},{8,16},{9,... | collective-permute-start | bytes 454664 | tf_op jit(solution)/shard_map/ppermute | solution.py:253
  177.6 8.9 %collective-permute-start.56 = (bf16[592,128]{1,0:T(8,128)(2,1)S(1)}, bf16[592,128]{1,0:T(8,128)(2,1)S(1)}, u32[]{:S(2)}, u32[]{:S(2)}) collective-permute-start(bf16[592,128]{1,0:T(8,128)(2,1)S(1)} %get-tuple-element.256.refs_0_), channel_id=1, source_target_pairs={{0,1},{1,0},{2,3},{3,2},{4,5},{5,4},{6,7},{7,6},{8,9},{9,8},{10,11... | collective-permute-start | bytes 454664 | tf_op jit(solution)/shard_map/ppermute | solution.py:253
  185.5 1.6 collective-permute-start.58
  186.0 1.6 collective-permute-start.65
  186.5 1.4 collective-permute-start.66
  (19 other events, 166.9 us)
